TPU v7x, 32 devices: a whole 2x2x4 slice. The times are simulated.
32 devices in a mesh: grp: 2 (over x), cell: 16 (over z, y, core).
Axes of the slice: x: 2, y: 2, z: 4, core: 2. Of those that a mesh axis runs over, the one named last changes fastest.
Arguments:
- windows: bfloat16 [3, 16, 1024, 256], P(None, 'cell', 'grp'), parts along dimension 2, may hold values from -6 to 6
- counts: int32 [32], P('grp'), parts along dimension 0, may hold values from 1 to 32, as said below
- pairs: int32 [2, 2, 16384], P(None, None, ('grp', 'cell')), parts along dimension 2, may hold values from 0 to 31, as said below
Outputs:
- lags: float32 [2, 16384, 256], P(None, ('grp', 'cell')), parts along dimension 1
There are 2 independent parts, one for each index of `grp`. A program takes and returns all parts, laid end to end along the dimension named above; each array names one. Nothing has to cross between parts.
Inputs may be any that keep to these rules, and one draw needn't show every extreme that they name: `counts`: slots below a cell's count hold events, the rest are empty; some cell is full in every draw. `pairs`: slot numbers within a cell; every cell's list of every round names slot 0 and slot 31.
All inputs are finite; a program needn't handle non-finite values.
Results may differ from a plain program's by a relative error of at most 0.0052.
Values may be sent and summed in bfloat16 or wider, within the bound.
No kernel may reach another device: no remote copies, remote signals or barrier semaphores. Data moves between devices by JAX's collectives and lax.ppermute only.
A program may use at most 64 MiB of HBM per device.

v0:
```python
import math

import jax
import jax.numpy as jnp
from jax import lax
from jax.sharding import PartitionSpec as P

EPSILON = 1e-06


def partner_2(x, axis, distance):
    return lax.ppermute(x, axis, [(i, i ^ 1 << distance) for i in range(lax.axis_size(axis))])


def phase_angles(samples, count):
    moments = jnp.arange(samples, dtype=jnp.int32)
    freq_bins = jnp.arange(count, dtype=jnp.int32)
    product = moments[:, None] * freq_bins[None, :] % samples
    return product.astype(jnp.float32) * (2.0 * math.pi / samples)


def forward_matrix(samples):
    angles = phase_angles(samples, samples // 2)
    return jnp.concatenate([jnp.cos(angles), -jnp.sin(angles)], axis=1).astype(jnp.bfloat16)


def inverse_matrices(samples):
    angles = phase_angles(samples, samples // 2).T
    weights = jnp.where(jnp.arange(samples // 2) == 0, 1.0, 2.0).astype(jnp.float32) / samples
    return (weights[:, None] * jnp.cos(angles), -weights[:, None] * jnp.sin(angles))


def spectra_of(block, forward):
    flat_block = block.reshape(-1, block.shape[-1])
    energy = jnp.sum(jnp.square(flat_block.astype(jnp.float32)), axis=1, keepdims=True)
    raw_spectra = jnp.dot(flat_block, forward, preferred_element_type=jnp.float32)
    return (raw_spectra / jnp.sqrt(energy + EPSILON)).astype(jnp.bfloat16).reshape(block.shape)


def contract(left, right):
    return jnp.einsum("sik,sjk->kij", left, right, preferred_element_type=jnp.float32)


def cross_spectra(own_spectra, far_spectra):
    half_bins = own_spectra.shape[-1] // 2
    own_real, own_imag = (own_spectra[..., :half_bins], own_spectra[..., half_bins:])
    far_real, far_imag = (far_spectra[..., :half_bins], far_spectra[..., half_bins:])
    cross_real = contract(own_real, far_real) + contract(own_imag, far_imag)
    cross_imag = contract(own_real, far_imag) - contract(own_imag, far_real)
    return (cross_real, cross_imag)


def lag_block(
    cross_real,
    cross_imag,
    first_slot,
    second_slot,
    own_count,
    far_count,
    cos_part,
    sin_part,
    stack_scale,
):
    events = cross_real.shape[1]
    flat_index = first_slot * events + second_slot
    picked_real = jnp.take(cross_real.reshape(cross_real.shape[0], -1), flat_index, axis=1)
    picked_imag = jnp.take(cross_imag.reshape(cross_imag.shape[0], -1), flat_index, axis=1)
    lag_values = jnp.einsum("kp,kt->pt", picked_real, cos_part, precision=lax.Precision.HIGHEST)
    lag_values = lag_values + jnp.einsum(
        "kp,kt->pt", picked_imag, sin_part, precision=lax.Precision.HIGHEST
    )
    live_pair = (first_slot < own_count) & (second_slot < far_count)
    return jnp.where(live_pair[:, None], lag_values * stack_scale, 0.0)


def round_bit(step_round, levels, rounds):
    return step_round * (levels - 1) // max(rounds - 1, 1)


def on_device(windows, counts, pairs):
    samples = windows.shape[-1]
    forward = forward_matrix(samples)
    cos_part, sin_part = inverse_matrices(samples)
    regrouped = lax.all_to_all(windows, "cell", split_axis=2, concat_axis=1, tiled=True)
    own_spectra = spectra_of(regrouped, forward)
    stations = own_spectra.shape[1]
    flat_own = own_spectra.reshape(-1, own_spectra.shape[2], samples)
    stack_scale = math.sqrt(samples / (3.0 * stations))
    position = lax.axis_index("cell")
    levels = lax.axis_size("cell").bit_length() - 1
    rounds = pairs.shape[0]
    results = []
    for step_round in range(rounds):
        partner_bit = round_bit(step_round, levels, rounds)
        far_spectra = partner_2(flat_own, "cell", partner_bit)
        partner = jnp.bitwise_xor(position, 1 << partner_bit)
        cross_real, cross_imag = cross_spectra(flat_own, far_spectra)
        results.append(
            lag_block(
                cross_real,
                cross_imag,
                pairs[step_round, 0],
                pairs[step_round, 1],
                counts[position],
                counts[partner],
                cos_part,
                sin_part,
                stack_scale,
            )
        )
    return jnp.stack(results)


def solution(mesh):
    in_specs = (P(None, "cell", "grp", None), P("grp"), P(None, None, ("grp", "cell")))
    out_specs = P(None, ("grp", "cell"), None)
    return jax.shard_map(
        on_device, mesh=mesh, in_specs=in_specs, out_specs=out_specs, check_vma=False
    )
```

profile of v0, /device:TPU:0, one launch (start us, length us, event | category | flops | bytes accessed | tf_op | source)
XLA Modules:
  0.0 129.2 jit_solution(6214006130045851245)
XLA Ops:
  0.0 2.8 %copy.75 = bf16[3,1,512,256]{3,0,1,2:T(4,128)(2,1)} copy(bf16[3,1,512,256]{3,2,1,0:T(8,128)(2,1)} %param.5) | data formatting | bytes 1572864 | tf_op args[0]
  2.8 7.4 %all-to-all-start = ((bf16[3,1,512,256]{3,0,1,2:T(4,128)(2,1)}), bf16[3,1,512,256]{3,0,1,2:T(4,128)(2,1)S(1)}, u32[]{:S(2)}, u32[]{:S(2)}) async-start(bf16[3,1,512,256]{3,0,1,2:T(4,128)(2,1)} %copy.75), calls=%async_computation | async-start | bytes 2097152 | tf_op jit(solution)/shard_map/all_to_all | solution.py:84
  10.2 0.7 fusion.75
  10.9 0.5 fusion.49
  11.5 2.4 %and_reduce_fusion.1 = (pred[512]{0:T(512)(128)(4,1)}, pred[512]{0:T(512)(128)(4,1)}) fusion(s32[2,2,512]{2,1,0:T(2,128)S(1)} %copy-done.7, s32[]{:T(128)} %bitcast.1, s32[]{:T(128)} %bitcast, s32[]{:T(128)} %bitcast.11), kind=kLoop, calls=%fused_computation.70 | loop fusion | flops 3072 | bytes 9228 | tf_op jit(solution)/shard_map/and | solution.py:72
  13.9 0.5 negate_convert_fusion
  14.4 18.7 %all-to-all-done = bf16[3,1,512,256]{3,0,1,2:T(4,128)(2,1)S(1)} async-done(((bf16[3,1,512,256]{3,0,1,2:T(4,128)(2,1)}), bf16[3,1,512,256]{3,0,1,2:T(4,128)(2,1)S(1)}, u32[]{:S(2)}, u32[]{:S(2)}) %all-to-all-start) | async-done | bytes 786464 | tf_op jit(solution)/shard_map/all_to_all | solution.py:84
  33.1 0.3 multiply_reduce_fusion
  33.5 0.1 copy.76
  33.6 0.4 fusion.1
  34.0 1.2 copy.80
  35.2 5.1 %collective-permute-start.1 = (bf16[48,32,256]{2,1,0:T(8,128)(2,1)}, bf16[48,32,256]{2,1,0:T(8,128)(2,1)}, u32[]{:S(2)}, u32[]{:S(2)}) collective-permute-start(bf16[48,32,256]{2,1,0:T(8,128)(2,1)} %bitcast.5), channel_id=1, source_target_pairs={{0,8},{1,9},{2,10},{3,11},{4,12},{5,13},{6,14},{7,15},{8,0},{9,1},... | collective-permute-start | bytes 2359304 | tf_op jit(solution)/shard_map/ppermute | solution.py:12
  40.3 0.6 fusion.50
  40.8 0.1 collective-permute-start
  40.9 1.2 fusion.74
  42.1 1.6 %copy.94 = bf16[48,32,128]{0,1,2:T(8,128)(2,1)S(1)} copy(bf16[48,32,128]{2,1,0:T(8,128)(2,1)S(1)} %get-tuple-element.13) | data formatting | bytes 786432
  43.7 1.6 %copy.92 = bf16[48,32,128]{0,1,2:T(8,128)(2,1)S(1)} copy(bf16[48,32,128]{2,1,0:T(8,128)(2,1)S(1)} %get-tuple-element.12) | data formatting | bytes 786432
  45.4 29.4 %collective-permute-done.1 = bf16[48,32,256]{2,1,0:T(8,128)(2,1)} collective-permute-done((bf16[48,32,256]{2,1,0:T(8,128)(2,1)}, bf16[48,32,256]{2,1,0:T(8,128)(2,1)}, u32[]{:S(2)}, u32[]{:S(2)}) %collective-permute-start.1) | collective-permute-done | bytes 786464 | tf_op jit(solution)/shard_map/ppermute | solution.py:12
  74.8 1.9 %fusion.73 = (bf16[48,32,128]{2,1,0:T(8,128)(2,1)S(1)}, bf16[48,32,128]{2,1,0:T(8,128)(2,1)}) fusion(bf16[48,32,256]{2,1,0:T(8,128)(2,1)} %collective-permute-done.1), kind=kLoop, calls=%fused_computation.104 | loop fusion | bytes 1572864 | tf_op jit(solution)/shard_map/slice | solution.py:47
  76.7 2.8 %copy.97 = bf16[48,32,128]{0,1,2:T(8,128)(2,1)S(1)} copy(bf16[48,32,128]{2,1,0:T(8,128)(2,1)} %get-tuple-element.11) | data formatting | bytes 786432
  79.4 2.5 %copy.96 = bf16[48,32,128]{0,1,2:T(8,128)(2,1)} copy(bf16[48,32,128]{2,1,0:T(8,128)(2,1)S(1)} %get-tuple-element.10) | data formatting | bytes 786432
  81.9 0.7 fusion.78
  82.6 0.0 copy-done
  82.6 0.6 copy-done.2
  83.1 2.0 %convolution_add_fusion = f32[128,32,32]{2,1,0:T(8,128)} fusion(f32[128,32,32]{2,1,0:T(8,128)S(1)} %fusion.78, bf16[48,32,128]{0,1,2:T(8,128)(2,1)S(1)} %copy.92, bf16[48,32,128]{0,1,2:T(8,128)(2,1)S(1)} %copy-done.2), kind=kOutput, calls=%fused_computation.8 | convolution fusion | flops 12713984 | bytes 1835008 | tf_op jit(solution)/shard_map/sik,sjk->kij/dot_general | solution.py:41
  85.2 2.7 %copy.89 = f32[128,32,32]{0,2,1:T(8,128)S(1)} copy(f32[128,32,32]{2,1,0:T(8,128)} %convolution_add_fusion) | data formatting | bytes 1048576 | tf_op jit(solution)/shard_map/add | solution.py:48
  87.8 2.0 %fusion.79 = f32[128,32,32]{2,1,0:T(8,128)S(1)} fusion(bf16[48,32,128]{0,1,2:T(8,128)(2,1)S(1)} %copy.94, bf16[48,32,128]{0,1,2:T(8,128)(2,1)} %copy.96), kind=kOutput, calls=%fused_computation.110 | convolution fusion | flops 12582912 | bytes 1310720 | tf_op jit(solution)/shard_map/sik,sjk->kij/dot_general | solution.py:41
  89.8 2.0 %convolution_subtract_fusion = f32[128,32,32]{2,1,0:T(8,128)} fusion(f32[128,32,32]{2,1,0:T(8,128)S(1)} %fusion.79, bf16[48,32,128]{0,1,2:T(8,128)(2,1)S(1)} %copy.92, bf16[48,32,128]{0,1,2:T(8,128)(2,1)S(1)} %copy-done.1), kind=kOutput, calls=%fused_computation.7 | convolution fusion | flops 12713984 | bytes 1835008 | tf_op jit(solution)/shard_map/sik,sjk->kij/dot_general | solution.py:41
  91.8 2.7 %copy.90 = f32[128,32,32]{0,2,1:T(8,128)S(1)} copy(f32[128,32,32]{2,1,0:T(8,128)} %convolution_subtract_fusion) | data formatting | bytes 1048576 | tf_op jit(solution)/shard_map/sub | solution.py:49
  94.5 1.8 %gather_fusion.2 = f32[512,128]{1,0:T(8,128)} fusion(f32[128,1024]{0,1:T(8,128)S(1)} %bitcast.46, s32[1024]{0:T(1024)S(1)} %pad_clamp_fusion), kind=kCustom, calls=%fused_computation.2.clone | custom fusion | bytes 526336 | tf_op jit(solution)/shard_map/jit(_take)/gather | solution.py:66
  96.3 1.6 %gather_fusion.3 = f32[512,128]{1,0:T(8,128)} fusion(f32[128,1024]{0,1:T(8,128)S(1)} %bitcast.48, s32[1024]{0:T(1024)S(1)} %pad_clamp_fusion), kind=kCustom, calls=%fused_computation.3.clone | custom fusion | bytes 526336 | tf_op jit(solution)/shard_map/jit(_take)/gather | solution.py:67
  97.9 0.0 collective-permute-done
  97.9 1.9 %fusion.72 = (bf16[48,32,128]{2,1,0:T(8,128)(2,1)S(1)}, bf16[48,32,128]{2,1,0:T(8,128)(2,1)}) fusion(bf16[48,32,256]{2,1,0:T(8,128)(2,1)} %collective-permute-done), kind=kLoop, calls=%fused_computation.103 | loop fusion | bytes 1572864 | tf_op jit(solution)/shard_map/slice | solution.py:47
  99.8 2.8 %copy.95 = bf16[48,32,128]{0,1,2:T(8,128)(2,1)S(1)} copy(bf16[48,32,128]{2,1,0:T(8,128)(2,1)} %get-tuple-element.9) | data formatting | bytes 786432
  102.6 2.0 %fusion.76 = f32[128,32,32]{2,1,0:T(8,128)} fusion(bf16[48,32,128]{0,1,2:T(8,128)(2,1)S(1)} %copy.94, bf16[48,32,128]{0,1,2:T(8,128)(2,1)S(1)} %copy.95), kind=kOutput, calls=%fused_computation.107 | convolution fusion | flops 12582912 | bytes 1310720 | tf_op jit(solution)/shard_map/sik,sjk->kij/dot_general | solution.py:41
  104.6 2.5 %copy.93 = bf16[48,32,128]{0,1,2:T(8,128)(2,1)} copy(bf16[48,32,128]{2,1,0:T(8,128)(2,1)S(1)} %get-tuple-element.8) | data formatting | bytes 786432
  107.1 3.4 %fusion.77 = f32[128,32,32]{2,1,0:T(8,128)} fusion(bf16[48,32,128]{0,1,2:T(8,128)(2,1)S(1)} %copy.94, bf16[48,32,128]{0,1,2:T(8,128)(2,1)} %copy.93), kind=kOutput, calls=%fused_computation.108 | convolution fusion | flops 12582912 | bytes 1310720 | tf_op jit(solution)/shard_map/sik,sjk->kij/dot_general | solution.py:41
  110.4 2.0 %convolution_add_fusion.1 = f32[128,32,32]{2,1,0:T(8,128)} fusion(f32[128,32,32]{2,1,0:T(8,128)S(1)} %copy-done.4, bf16[48,32,128]{0,1,2:T(8,128)(2,1)S(1)} %copy.92, bf16[48,32,128]{0,1,2:T(8,128)(2,1)S(1)} %copy-done.3), kind=kOutput, calls=%fused_computation.10 | convolution fusion | flops 12713984 | bytes 1835008 | tf_op jit(solution)/shard_map/sik,sjk->kij/dot_general | solution.py:41
  112.4 2.7 %copy.85 = f32[128,32,32]{0,2,1:T(8,128)S(1)} copy(f32[128,32,32]{2,1,0:T(8,128)} %convolution_add_fusion.1) | data formatting | bytes 1048576 | tf_op jit(solution)/shard_map/add | solution.py:48
  115.1 3.6 %convolution_subtract_fusion.1 = f32[128,32,32]{2,1,0:T(8,128)} fusion(f32[128,32,32]{2,1,0:T(8,128)} %fusion.77, bf16[48,32,128]{0,1,2:T(8,128)(2,1)S(1)} %copy.92, bf16[48,32,128]{0,1,2:T(8,128)(2,1)S(1)} %copy.95), kind=kOutput, calls=%fused_computation.9 | convolution fusion | flops 12713984 | bytes 1835008 | tf_op jit(solution)/shard_map/sik,sjk->kij/dot_general | solution.py:41
  118.7 2.7 %copy.86 = f32[128,32,32]{0,2,1:T(8,128)S(1)} copy(f32[128,32,32]{2,1,0:T(8,128)} %convolution_subtract_fusion.1) | data formatting | bytes 1048576 | tf_op jit(solution)/shard_map/sub | solution.py:49
  121.4 1.0 gather_fusion
  122.4 1.3 gather_fusion.1
  123.7 1.1 fusion.9
  124.8 1.1 fusion.12
  125.9 1.1 fusion.4
  127.0 1.1 fusion.7
  128.2 1.0 pad_maximum_fusion
  (33 shorter events, 0.1 us)
Async XLA Ops:
  0.0 10.2 %copy-start.8 = (s32[16]{0:T(128)S(1)}, s32[16]{0:T(128)}, u32[]{:S(2)}) copy-start(s32[16]{0:T(128)} %param.6) | copy-start | bytes 196
  0.0 11.4 %copy-start.7 = (s32[2,2,512]{2,1,0:T(2,128)S(1)}, s32[2,2,512]{2,1,0:T(2,128)}, u32[]{:S(2)}) copy-start(s32[2,2,512]{2,1,0:T(2,128)} %param.7) | copy-start | bytes 24580
  2.8 30.3 %all-to-all-start = ((bf16[3,1,512,256]{3,0,1,2:T(4,128)(2,1)}), bf16[3,1,512,256]{3,0,1,2:T(4,128)(2,1)S(1)}, u32[]{:S(2)}, u32[]{:S(2)}) async-start(bf16[3,1,512,256]{3,0,1,2:T(4,128)(2,1)} %copy.75), calls=%async_computation | async-start | bytes 2097152 | tf_op jit(solution)/shard_map/all_to_all | solution.py:84
  35.2 39.6 %collective-permute-start.1 = (bf16[48,32,256]{2,1,0:T(8,128)(2,1)}, bf16[48,32,256]{2,1,0:T(8,128)(2,1)}, u32[]{:S(2)}, u32[]{:S(2)}) collective-permute-start(bf16[48,32,256]{2,1,0:T(8,128)(2,1)} %bitcast.5), channel_id=1, source_target_pairs={{0,8},{1,9},{2,10},{3,11},{4,12},{5,13},{6,14},{7,15},{8,0},{9,1},... | collective-permute-start | bytes 2359304 | tf_op jit(solution)/shard_map/ppermute | solution.py:12
  40.8 57.1 %collective-permute-start = (bf16[48,32,256]{2,1,0:T(8,128)(2,1)}, bf16[48,32,256]{2,1,0:T(8,128)(2,1)}, u32[]{:S(2)}, u32[]{:S(2)}) collective-permute-start(bf16[48,32,256]{2,1,0:T(8,128)(2,1)} %bitcast.5), channel_id=1, source_target_pairs={{0,1},{1,0},{2,3},{3,2},{4,5},{5,4},{6,7},{7,6},{8,9},{9,8},{10,11... | collective-permute-start | bytes 2359304 | tf_op jit(solution)/shard_map/ppermute | solution.py:12
  79.4 3.2 %copy-start = (bf16[48,32,128]{0,1,2:T(8,128)(2,1)}, bf16[48,32,128]{0,1,2:T(8,128)(2,1)S(1)}, u32[]{:S(2)}) copy-start(bf16[48,32,128]{0,1,2:T(8,128)(2,1)S(1)} %copy.97) | copy-start | bytes 1179652
  81.9 1.2 copy-start.2
  87.8 2.0 %copy-start.1 = (bf16[48,32,128]{0,1,2:T(8,128)(2,1)S(1)}, bf16[48,32,128]{0,1,2:T(8,128)(2,1)}, u32[]{:S(2)}) copy-start(bf16[48,32,128]{0,1,2:T(8,128)(2,1)} %copy-done) | copy-start | bytes 1179652
  107.1 3.4 %copy-start.3 = (bf16[48,32,128]{0,1,2:T(8,128)(2,1)S(1)}, bf16[48,32,128]{0,1,2:T(8,128)(2,1)}, u32[]{:S(2)}) copy-start(bf16[48,32,128]{0,1,2:T(8,128)(2,1)} %copy.93) | copy-start | bytes 1179652
  107.1 3.4 %copy-start.4 = (f32[128,32,32]{2,1,0:T(8,128)S(1)}, f32[128,32,32]{2,1,0:T(8,128)}, u32[]{:S(2)}) copy-start(f32[128,32,32]{2,1,0:T(8,128)} %fusion.76) | copy-start | bytes 1572868
  121.3 2.4 %copy-start.5 = (f32[512,128]{1,0:T(8,128)S(1)}, f32[512,128]{1,0:T(8,128)}, u32[]{:S(2)}) copy-start(f32[512,128]{1,0:T(8,128)} %gather_fusion.2) | copy-start | bytes 786436
  121.3 2.4 %copy-start.9 = (f32[128]{0:T(128)S(1)}, f32[128]{0:T(128)}, u32[]{:S(2)}) copy-start(f32[128]{0:T(128)} %fusion.49) | copy-start | bytes 1540
  122.4 3.5 %copy-start.6 = (f32[512,128]{1,0:T(8,128)S(1)}, f32[512,128]{1,0:T(8,128)}, u32[]{:S(2)}) copy-start(f32[512,128]{1,0:T(8,128)} %gather_fusion.3) | copy-start | bytes 786436
  122.4 3.5 %copy-start.10 = (f32[128]{0:T(128)S(1)}, f32[128]{0:T(128)}, u32[]{:S(2)}) copy-start(f32[128]{0:T(128)} %fusion.50) | copy-start | bytes 1540
  122.4 3.5 %copy-start.12 = (pred[512]{0:T(512)(128)(4,1)S(1)}, pred[512]{0:T(512)(128)(4,1)}, u32[]{:S(2)}) copy-start(pred[512]{0:T(512)(128)(4,1)} %get-tuple-element.7) | copy-start | bytes 1540
  122.4 4.6 %copy-start.11 = (pred[512]{0:T(512)(128)(4,1)S(1)}, pred[512]{0:T(512)(128)(4,1)}, u32[]{:S(2)}) copy-start(pred[512]{0:T(512)(128)(4,1)} %get-tuple-element.6) | copy-start | bytes 1540
where the time goes:
time: 130 us; the launch traced here: 129 us
  waiting for transfers between devices  48.1 us (37%)
  local copies, waits for them, and re-layouts  40.5 us (31%)
  matrix products  22.3 us (17%)
  starting transfers between devices  12.5 us (10%)
  other arithmetic  5.41 us (4%)
    ppermute x2, waiting for transfers between devices, partner_2(): lax.ppermute(x, axis, [(i, i ^ 1 << distance) for i in range(lax.axis_siz...  29.4 us
    all_to_all x1, waiting for transfers between devices, on_device(): lax.all_to_all(windows, 'cell', split_axis=2, concat_axis=1, tiled=True)  18.7 us
    dot_general x8, matrix products, contract(): jnp.einsum('sik,sjk->kij', left, right, preferred_element_type=jnp.float32)  17.6 us
    unnamed x33, local copies, waits for them, and re-layouts  17.1 us
    all_to_all x1, starting transfers between devices, on_device(): lax.all_to_all(windows, 'cell', split_axis=2, concat_axis=1, tiled=True)  7.39 us
    add x2, local copies, waits for them, and re-layouts, cross_spectra(): cross_real = contract(own_real, far_real) + contract(own_imag, far_imag)  5.31 us
    sub x2, local copies, waits for them, and re-layouts, cross_spectra(): cross_imag = contract(own_real, far_imag) - contract(own_imag, far_real)  5.31 us
    ppermute x2, starting transfers between devices, partner_2(): lax.ppermute(x, axis, [(i, i ^ 1 << distance) for i in range(lax.axis_siz...  5.14 us
  transfers between devices with their start and end apart: 3, of which 2 were waited for; matrix products, arithmetic and copies ran while one was open for 25% of the time, Pallas kernels for 0%

commit v1 on v0

v1 whole, which is shorter than its diff:
```python
import math

import jax
import jax.numpy as jnp
import numpy as np
from jax import lax
from jax.experimental import pallas as pl
from jax.experimental.pallas import tpu as pltpu
from jax.sharding import PartitionSpec as P

EPSILON = 1e-06
SLOTS = 32
NT = (((1,), (1,)), ((), ()))
TN = (((0,), (0,)), ((), ()))
VMEM_LIMIT = 40 * 1024 * 1024


def tables(samples, stations):
    bins = samples // 2
    quarter = bins // 4
    turn = np.arange(bins)[:, None] * np.arange(samples)[None, :] % samples
    angle = turn * (2.0 * math.pi / samples)
    weight = np.where(np.arange(bins) == 0, 1.0, 2.0)[:, None] / samples
    weight = weight * math.sqrt(samples / (3.0 * stations))

    def by_quarter(real, imag):
        rows = [real.reshape(4, quarter, samples), imag.reshape(4, quarter, samples)]
        return np.concatenate(rows, axis=1).reshape(4 * 2 * quarter, samples)

    forward = by_quarter(np.cos(angle), -np.sin(angle)).astype(np.float32)
    inverse = by_quarter(weight * np.cos(angle), -weight * np.sin(angle)).astype(np.float32)
    return forward.astype(jnp.bfloat16), inverse


def spectra_kernel(place_ref, windows_ref, forward_ref, *piece_refs):
    groups = windows_ref.shape[2]
    rows = forward_ref.shape[0] // 4
    quarter, group = place_ref[0], place_ref[1]
    table = jnp.concatenate(
        [forward_ref[pl.ds(pl.multiple_of((quarter ^ m) * rows, rows), rows), :] for m in range(4)]
    )
    ones = jnp.ones((16, table.shape[1]), jnp.bfloat16)
    for mg in range(groups):
        parts = []
        for comp in range(windows_ref.shape[0]):
            low = windows_ref[comp, 0, group ^ mg]
            high = windows_ref[comp, 1, group ^ mg]
            parts += [low[:SLOTS], high[SLOTS:], low[SLOTS:], high[:SLOTS]]
        traces = jnp.concatenate(parts)
        square = jnp.square(traces.astype(jnp.float32))
        square_hi = square.astype(jnp.bfloat16)
        square_lo = (square - square_hi.astype(jnp.float32)).astype(jnp.bfloat16)
        energy = lax.dot_general(ones, square_hi, NT, preferred_element_type=jnp.float32)
        energy += lax.dot_general(ones, square_lo, NT, preferred_element_type=jnp.float32)
        scale = lax.rsqrt(energy[:1] + EPSILON)
        raw = lax.dot_general(table, traces, NT, preferred_element_type=jnp.float32)
        spectra = (raw * scale).astype(jnp.bfloat16)
        lanes = 4 * SLOTS
        for mq in range(4):
            piece = piece_refs[(mq // 2) * 2 * groups + mg * 2 + mq % 2]
            for comp in range(windows_ref.shape[0]):
                piece[comp] = spectra[mq * rows : (mq + 1) * rows, comp * lanes : (comp + 1) * lanes]


def pick_kernel(place_ref, *refs):
    index_refs, refs = refs[:4], refs[4:]
    piece_refs, refs = refs[:-7], refs[-7:]
    picked_refs, (trace_ref, cross_ref, flat_ref) = refs[:4], refs[4:]
    quarter = place_ref[0]
    comps, rows, lanes = piece_refs[0].shape
    bins = rows // 2
    traces = comps * len(piece_refs)
    for s, piece in enumerate(piece_refs):
        for comp in range(comps):
            start = (s * comps + comp) * rows
            trace_ref[start : start + rows] = piece[comp].astype(jnp.float32)
    half = 2 * SLOTS
    for k in range(bins):
        real = trace_ref[pl.ds(k, traces, stride=rows), :].astype(jnp.bfloat16)
        imag = trace_ref[pl.ds(bins + k, traces, stride=rows), :].astype(jnp.bfloat16)
        left = jnp.concatenate([real, imag], axis=0)
        right = jnp.concatenate(
            [jnp.concatenate([real, imag], axis=1), jnp.concatenate([imag, -real], axis=1)], axis=0
        )
        cross = lax.dot_general(left, right, TN, preferred_element_type=jnp.float32)
        cross_ref[k * half : (k + 1) * half] = cross[:half, :lanes]
        cross_ref[(bins + k) * half : (bins + k + 1) * half] = cross[:half, lanes:]
    for i in range(half):
        turned = cross_ref[pl.ds(i, rows, stride=half), :].T.astype(jnp.bfloat16)
        own, slot = i // SLOTS, i % SLOTS
        for far in range(2):
            start = half + far * SLOTS
            flat_ref[own, far, slot * SLOTS : (slot + 1) * SLOTS] = turned[start : start + SLOTS]
    pairs = index_refs[0].shape[1]
    columns = jnp.concatenate([ref[...] for ref in index_refs], axis=0).T
    lane = lax.broadcasted_iota(jnp.int32, (pairs, lanes), 1)
    for mq in range(4):
        cell = quarter ^ mq
        high, low = cell // 2, cell % 2
        sides = ((high, high), (low, 1 - low))
        found = []
        for step_round in range(2):
            at = mq * 2 + step_round
            offset = columns[:, at : at + 1] - lane
            hot = jnp.concatenate(
                [
                    jnp.where(offset == lanes * t, 1.0, 0.0).astype(jnp.bfloat16)
                    for t in range(SLOTS * SLOTS // lanes)
                ],
                axis=1,
            )
            block = flat_ref[sides[step_round][0], sides[step_round][1]]
            found.append(jnp.dot(hot, block, preferred_element_type=jnp.float32))
        picked_refs[mq][...] = jnp.concatenate(found, axis=1).astype(jnp.bfloat16)


def lag_kernel(place_ref, inverse_ref, *refs):
    picked_refs, lags_ref = refs[:4], refs[4]
    quarter = place_ref[0]
    rows = inverse_ref.shape[0] // 4
    sign = jnp.where(quarter // 2 == quarter % 2, 1.0, -1.0)
    row = lax.broadcasted_iota(jnp.int32, (rows, inverse_ref.shape[1]), 0)
    factor = jnp.where(row < rows // 2, 1.0, sign)
    table = jnp.concatenate(
        [
            inverse_ref[pl.ds(pl.multiple_of((quarter ^ m) * rows, rows), rows), :] * factor
            for m in range(4)
        ]
    )
    table_hi = table.astype(jnp.bfloat16)
    table_lo = (table - table_hi.astype(jnp.float32)).astype(jnp.bfloat16)
    picked = [ref[...] for ref in picked_refs]
    for step_round in range(2):
        cross = jnp.concatenate([p[:, step_round * rows : (step_round + 1) * rows] for p in picked], axis=1)
        lags_ref[step_round] = jnp.dot(
            cross, table_hi, preferred_element_type=jnp.float32
        ) + jnp.dot(cross, table_lo, preferred_element_type=jnp.float32)


def on_device(windows, counts, pairs):
    comps, _, events, samples = windows.shape
    cells = lax.axis_size("cell")
    half, groups = cells // 2, cells // 4
    count = pairs.shape[2]
    rows = samples // 4
    lanes = 4 * SLOTS
    forward, inverse = tables(samples, cells)
    position = lax.axis_index("cell")
    high, low = position // half, position % 2
    place = jnp.stack([high * 2 + low, (position % half) // 2]).astype(jnp.int32)

    def swap(x, mask):
        return lax.ppermute(x, "cell", [(i, i ^ mask) for i in range(cells)])

    vmem = pl.BlockSpec(memory_space=pltpu.VMEM)
    smem = pl.BlockSpec(memory_space=pltpu.SMEM)
    params = pltpu.CompilerParams(vmem_limit_bytes=VMEM_LIMIT)

    first, second = pairs[:, 0], pairs[:, 1]
    far_counts = jnp.stack([counts[position ^ 1], counts[position ^ half]])
    live = (first < counts[position]) & (second < far_counts[:, None])
    flat = jnp.where(high == low, first * SLOTS + second, second * SLOTS + first)
    index = jnp.where(live, flat, -1)
    masks = [(m // 2) * half + m % 2 for m in range(4)]
    indices = [index] + [swap(index, m) for m in masks[1:]]

    pieces = pl.pallas_call(
        spectra_kernel,
        out_shape=[jax.ShapeDtypeStruct((comps, rows, lanes), jnp.bfloat16)] * cells,
        in_specs=[smem, vmem, vmem],
        out_specs=[vmem] * cells,
        compiler_params=params,
        name="spectra",
    )(place, windows.reshape(comps, 2, groups, 2 * SLOTS, samples), jnp.asarray(forward))
    pieces = [pieces[0]] + [swap(pieces[m], m) for m in range(1, cells)]

    picked = pl.pallas_call(
        pick_kernel,
        out_shape=[jax.ShapeDtypeStruct((count, 2 * rows), jnp.bfloat16)] * 4,
        in_specs=[smem] + [vmem] * (4 + cells),
        out_specs=[vmem] * 4,
        scratch_shapes=[
            pltpu.VMEM((comps * cells * rows, lanes), jnp.float32),
            pltpu.VMEM((rows * 2 * SLOTS, lanes), jnp.float32),
            pltpu.VMEM((2, 2, SLOTS * SLOTS, rows), jnp.bfloat16),
        ],
        compiler_params=params,
        name="picks",
    )(place, *indices, *pieces)
    picked = [picked[0]] + [swap(p, m) for p, m in zip(picked[1:], masks[1:])]

    return pl.pallas_call(
        lag_kernel,
        out_shape=jax.ShapeDtypeStruct((2, count, samples), jnp.float32),
        in_specs=[smem] + [vmem] * 5,
        out_specs=vmem,
        compiler_params=params,
        name="lags",
    )(place, jnp.asarray(inverse), *picked)


def solution(mesh):
    in_specs = (P(None, "cell", "grp", None), P("grp"), P(None, None, ("grp", "cell")))
    out_specs = P(None, ("grp", "cell"), None)
    return jax.shard_map(
        on_device, mesh=mesh, in_specs=in_specs, out_specs=out_specs, check_vma=False
    )
```

time: 130 us -> 62.4 us (0.48)
  local copies, waits for them, and re-layouts: 40.5 us -> 3.36 us
  waiting for transfers between devices: 48.1 us -> 16 us
  matrix products: 22.3 us -> 0 us
  starting transfers between devices: 12.5 us -> 31.1 us
  Pallas kernels: 0 us -> 9.4 us
  other arithmetic: 5.41 us -> 2.22 us
    ppermute x2 -> x21, starting transfers between devices: 5.14 us -> 31.1 us  [swap(): return lax.ppermute(x, 'cell', [(i, i ^ mask) for i in range(cells)])]
    dot_general x13 -> x0, matrix products: 22.3 us -> none  [the longest x8 17.6 us: contract(): jnp.einsum('sik,sjk->kij', left, right, preferred_element_type=jnp.float32)]
    all_to_all x1 -> x0, waiting for transfers between devices: 18.7 us -> none  [on_device(): lax.all_to_all(windows, 'cell', split_axis=2, concat_axis=1, tiled=True)]
    unnamed x33 -> x6, local copies, waits for them, and re-layouts: 17.1 us -> 1.14 us
    ppermute x2 -> x21, waiting for transfers between devices: 29.4 us -> 16 us  [swap(): return lax.ppermute(x, 'cell', [(i, i ^ mask) for i in range(cells)])]
    pallas_call x0 -> x3, Pallas kernels: none -> 9.4 us  [the longest x1 5.95 us: on_device(): pl.pallas_call(pick_kernel, out_shape=[jax.ShapeDtypeStruct((count, 2 * r...]
    all_to_all x1 -> x0, starting transfers between devices: 7.39 us -> none  [on_device(): lax.all_to_all(windows, 'cell', split_axis=2, concat_axis=1, tiled=True)]
    gather x4 -> x0, local copies, waits for them, and re-layouts: 5.76 us -> none  [the longest x2 2.9 us: lag_block(): jnp.take(cross_imag.reshape(cross_imag.shape[0], -1), flat_index, axis=1)]
  transfers between devices with their start and end apart: 3 -> 21, of which waited for: 2 -> 4; matrix products, arithmetic and copies ran while one was open for 25% -> 0% of each run, Pallas kernels for 0% -> 2%
where the time goes in v1:
time: 62.4 us; the launch traced here: 62.2 us
  starting transfers between devices  31.1 us (50%)
  waiting for transfers between devices  16 us (26%)
  Pallas kernels  9.4 us (15%)
  local copies, waits for them, and re-layouts  3.36 us (5%)
  other arithmetic  2.22 us (4%)
    ppermute x21, starting transfers between devices, swap(): return lax.ppermute(x, 'cell', [(i, i ^ mask) for i in range(cells)])  31.1 us
    ppermute x21, waiting for transfers between devices, swap(): return lax.ppermute(x, 'cell', [(i, i ^ mask) for i in range(cells)])  16 us
    pallas_call x1, Pallas kernels, on_device(): pl.pallas_call(pick_kernel, out_shape=[jax.ShapeDtypeStruct((count, 2 * r...  5.95 us
    pallas_call x1, Pallas kernels, on_device(): pl.pallas_call(lag_kernel, out_shape=jax.ShapeDtypeStruct((2, count, samp...  1.99 us
    pallas_call x1, Pallas kernels, on_device(): pl.pallas_call(spectra_kernel, out_shape=[jax.ShapeDtypeStruct((comps, ro...  1.46 us
    dynamic_slice x1, local copies, waits for them, and re-layouts, on_device(): live = (first < counts[position]) & (second < far_counts[:, None])  1.44 us
    another operation x1, other arithmetic, on_device(): far_counts = jnp.stack([counts[position ^ 1], counts[position ^ half]])  1.43 us
  transfers between devices with their start and end apart: 21, of which 4 were waited for; matrix products, arithmetic and copies ran while one was open for 0% of the time, Pallas kernels for 2%

profile of v1, /device:TPU:0, one launch (start us, length us, event | category | flops | bytes accessed | tf_op | source)
XLA Modules:
  0.0 62.2 jit_solution(9661895857785233725)
XLA Ops:
  0.0 0.8 %fusion = (s32[2,1,512]{2,1,0:T(1,128)S(1)}, s32[2,1,512]{2,1,0:T(1,128)S(1)}) fusion(s32[2,2,512]{2,1,0:T(2,128)} %param.7), kind=kLoop, calls=%fused_computation.5 | loop fusion | bytes 16384 | tf_op jit(solution)/shard_map/slice | solution.py:159
  0.8 1.4 %fusion.1 = (s32[1]{0:T(128)}, s32[1]{0:T(128)}, s32[1]{0:T(128)}) fusion(s32[16]{0:T(128)} %param.6, s32[]{:T(128)S(6)} %select_n.43, s32[]{:T(128)S(6)} %select_n.45, s32[]{:T(128)S(6)} %select_n.44), kind=kLoop, calls=%fused_computation.6 | loop fusion | bytes 36 | tf_op jit(solution)/shard_map/dynamic_slice | solution.py:161
  2.3 1.4 %pad_add_fusion.1 = s32[2]{0:T(128)S(1)} fusion(s32[1]{0:T(128)} %get-tuple-element.48, s32[1]{0:T(128)} %get-tuple-element.49), kind=kLoop, calls=%fused_computation.4 | loop fusion | flops 2 | bytes 16 | tf_op jit(solution)/shard_map/stack | solution.py:160
  3.7 0.7 %and_select_fusion.refs_0_ = s32[2,512]{1,0:T(2,128)S(1)} fusion(s32[2,1,512]{2,1,0:T(1,128)S(1)} %get-tuple-element.46, s32[2,1,512]{2,1,0:T(1,128)S(1)} %get-tuple-element.45, pred[]{:T(512)S(6)} %eq.6, s32[2]{0:T(128)S(1)} %pad_add_fusion.1, s32[]{:T(128)} %bitcast.3), kind=kLoop, calls=%fused_computation | loop fusion | flops 9216 | bytes 12301 | tf_op jit(solution)/shard_map/jit(_where)/select_n | solution.py:163
  4.4 3.5 %collective-permute-start.2 = (s32[2,512]{1,0:T(2,128)S(1)}, s32[2,512]{1,0:T(2,128)S(1)}, u32[]{:S(2)}, u32[]{:S(2)}) collective-permute-start(s32[2,512]{1,0:T(2,128)S(1)} %and_select_fusion.refs_0_), channel_id=1, source_target_pairs={{0,9},{1,8},{2,11},{3,10},{4,13},{5,12},{6,15},{7,14},{8,1},{9,0},... | collective-permute-start | bytes 12296 | tf_op jit(solution)/shard_map/ppermute | solution.py:153
  7.9 0.6 %collective-permute-start.1 = (s32[2,512]{1,0:T(2,128)S(1)}, s32[2,512]{1,0:T(2,128)S(1)}, u32[]{:S(2)}, u32[]{:S(2)}) collective-permute-start(s32[2,512]{1,0:T(2,128)S(1)} %and_select_fusion.refs_0_), channel_id=1, source_target_pairs={{0,8},{1,9},{2,10},{3,11},{4,12},{5,13},{6,14},{7,15},{8,0},{9,1},... | collective-permute-start | bytes 12296 | tf_op jit(solution)/shard_map/ppermute | solution.py:153
  8.5 0.0 collective-permute-start
  8.6 0.1 pad_add_fusion.place_ref
  8.7 1.1 %copy-done = bf16[3,1,512,256]{3,2,1,0:T(8,128)(2,1)S(1)} copy-done((bf16[3,1,512,256]{3,2,1,0:T(8,128)(2,1)S(1)}, bf16[3,1,512,256]{3,2,1,0:T(8,128)(2,1)}, u32[]{:S(2)}) %copy-start) | copy-done | bytes 786456
  9.8 1.5 %spectra.1 = (bf16[3,64,128]{2,1,0:T(8,128)(2,1)S(1)}, bf16[3,64,128]{2,1,0:T(8,128)(2,1)S(1)}, bf16[3,64,128]{2,1,0:T(8,128)(2,1)S(1)}, bf16[3,64,128]{2,1,0:T(...) custom-call(s32[2]{0:T(128)S(1)} %pad_add_fusion.place_ref, ...), custom_call_target="tpu_custom_call" | custom-call | tf_op jit(solution)/shard_map/spectra/pallas_call | solution.py:167
  11.3 0.5 collective-permute-start.3
  11.8 1.5 %collective-permute-start.4 = (bf16[3,64,128]{2,1,0:T(8,128)(2,1)S(1)}, bf16[3,64,128]{2,1,0:T(8,128)(2,1)S(1)}, u32[]{:S(2)}, u32[]{:S(2)}) collective-permute-start(bf16[3,64,128]{2,1,0:T(8,128)(2,1)S(1)} %get-tuple-element.27), channel_id=1, source_target_pairs={{0,2},{1,3},{2,0},{3,1},{4,6},{5,7},{6,4},{7,5},{8,10},{9,11},{10,... | collective-permute-start | bytes 147464 | tf_op jit(solution)/shard_map/ppermute | solution.py:153
  13.3 0.0 collective-permute-done.2.refs_3_
  13.3 0.0 collective-permute-start.5
  13.3 0.0 collective-permute-done.1.refs_2_
  13.3 1.6 %collective-permute-start.6 = (bf16[3,64,128]{2,1,0:T(8,128)(2,1)S(1)}, bf16[3,64,128]{2,1,0:T(8,128)(2,1)S(1)}, u32[]{:S(2)}, u32[]{:S(2)}) collective-permute-start(bf16[3,64,128]{2,1,0:T(8,128)(2,1)S(1)} %get-tuple-element.29), channel_id=1, source_target_pairs={{0,4},{1,5},{2,6},{3,7},{4,0},{5,1},{6,2},{7,3},{8,12},{9,13},{10,... | collective-permute-start | bytes 147464 | tf_op jit(solution)/shard_map/ppermute | solution.py:153
  15.0 0.0 collective-permute-done.refs_1_
  15.0 0.3 collective-permute-start.7
  15.3 0.0 collective-permute-done.3.refs_5_
  15.3 2.6 %collective-permute-start.8 = (bf16[3,64,128]{2,1,0:T(8,128)(2,1)S(1)}, bf16[3,64,128]{2,1,0:T(8,128)(2,1)S(1)}, u32[]{:S(2)}, u32[]{:S(2)}) collective-permute-start(bf16[3,64,128]{2,1,0:T(8,128)(2,1)S(1)} %get-tuple-element.31), channel_id=1, source_target_pairs={{0,6},{1,7},{2,4},{3,5},{4,2},{5,3},{6,0},{7,1},{8,14},{9,15},{10,... | collective-permute-start | bytes 147464 | tf_op jit(solution)/shard_map/ppermute | solution.py:153
  17.9 0.0 collective-permute-done.4.refs_6_
  17.9 0.0 collective-permute-start.9
  17.9 0.0 collective-permute-done.5.refs_7_
  17.9 2.4 %collective-permute-start.10 = (bf16[3,64,128]{2,1,0:T(8,128)(2,1)S(1)}, bf16[3,64,128]{2,1,0:T(8,128)(2,1)S(1)}, u32[]{:S(2)}, u32[]{:S(2)}) collective-permute-start(bf16[3,64,128]{2,1,0:T(8,128)(2,1)S(1)} %get-tuple-element.33), channel_id=1, source_target_pairs={{0,8},{1,9},{2,10},{3,11},{4,12},{5,13},{6,14},{7,15},{8,0},{9,1},... | collective-permute-start | bytes 147464 | tf_op jit(solution)/shard_map/ppermute | solution.py:153
  20.3 0.0 collective-permute-done.6.refs_8_
  20.3 1.0 %collective-permute-start.11 = (bf16[3,64,128]{2,1,0:T(8,128)(2,1)S(1)}, bf16[3,64,128]{2,1,0:T(8,128)(2,1)S(1)}, u32[]{:S(2)}, u32[]{:S(2)}) collective-permute-start(bf16[3,64,128]{2,1,0:T(8,128)(2,1)S(1)} %get-tuple-element.34), channel_id=1, source_target_pairs={{0,9},{1,8},{2,11},{3,10},{4,13},{5,12},{6,15},{7,14},{8,1},{9,0},... | collective-permute-start | bytes 147464 | tf_op jit(solution)/shard_map/ppermute | solution.py:153
  21.3 0.0 collective-permute-done.7.refs_9_
  21.3 2.6 %collective-permute-start.12 = (bf16[3,64,128]{2,1,0:T(8,128)(2,1)S(1)}, bf16[3,64,128]{2,1,0:T(8,128)(2,1)S(1)}, u32[]{:S(2)}, u32[]{:S(2)}) collective-permute-start(bf16[3,64,128]{2,1,0:T(8,128)(2,1)S(1)} %get-tuple-element.35), channel_id=1, source_target_pairs={{0,10},{1,11},{2,8},{3,9},{4,14},{5,15},{6,12},{7,13},{8,2},{9,3},... | collective-permute-start | bytes 147464 | tf_op jit(solution)/shard_map/ppermute | solution.py:153
  23.8 0.0 collective-permute-done.8.refs_10_
  23.9 0.4 collective-permute-start.13
  24.3 0.0 collective-permute-done.9.refs_11_
  24.3 3.3 %collective-permute-start.14 = (bf16[3,64,128]{2,1,0:T(8,128)(2,1)S(1)}, bf16[3,64,128]{2,1,0:T(8,128)(2,1)S(1)}, u32[]{:S(2)}, u32[]{:S(2)}) collective-permute-start(bf16[3,64,128]{2,1,0:T(8,128)(2,1)S(1)} %get-tuple-element.37), channel_id=1, source_target_pairs={{0,12},{1,13},{2,14},{3,15},{4,8},{5,9},{6,10},{7,11},{8,4},{9,5},... | collective-permute-start | bytes 147464 | tf_op jit(solution)/shard_map/ppermute | solution.py:153
  27.5 0.0 collective-permute-done.10.refs_12_
  27.5 0.9 %collective-permute-start.15 = (bf16[3,64,128]{2,1,0:T(8,128)(2,1)S(1)}, bf16[3,64,128]{2,1,0:T(8,128)(2,1)S(1)}, u32[]{:S(2)}, u32[]{:S(2)}) collective-permute-start(bf16[3,64,128]{2,1,0:T(8,128)(2,1)S(1)} %get-tuple-element.38), channel_id=1, source_target_pairs={{0,13},{1,12},{2,15},{3,14},{4,9},{5,8},{6,11},{7,10},{8,5},{9,4},... | collective-permute-start | bytes 147464 | tf_op jit(solution)/shard_map/ppermute | solution.py:153
  28.4 3.9 %collective-permute-start.16 = (bf16[3,64,128]{2,1,0:T(8,128)(2,1)S(1)}, bf16[3,64,128]{2,1,0:T(8,128)(2,1)S(1)}, u32[]{:S(2)}, u32[]{:S(2)}) collective-permute-start(bf16[3,64,128]{2,1,0:T(8,128)(2,1)S(1)} %get-tuple-element.39), channel_id=1, source_target_pairs={{0,14},{1,15},{2,12},{3,13},{4,10},{5,11},{6,8},{7,9},{8,6},{9,7},... | collective-permute-start | bytes 147464 | tf_op jit(solution)/shard_map/ppermute | solution.py:153
  32.2 2.9 %collective-permute-start.17 = (bf16[3,64,128]{2,1,0:T(8,128)(2,1)S(1)}, bf16[3,64,128]{2,1,0:T(8,128)(2,1)S(1)}, u32[]{:S(2)}, u32[]{:S(2)}) collective-permute-start(bf16[3,64,128]{2,1,0:T(8,128)(2,1)S(1)} %get-tuple-element.40), channel_id=1, source_target_pairs={{0,15},{1,14},{2,13},{3,12},{4,11},{5,10},{6,9},{7,8},{8,7},{9,6},... | collective-permute-start | bytes 147464 | tf_op jit(solution)/shard_map/ppermute | solution.py:153
  35.1 0.0 collective-permute-done.13.refs_15_
  35.1 0.0 collective-permute-done.14.refs_16_
  35.1 0.0 collective-permute-done.15.refs_17_
  35.1 0.1 collective-permute-done.16.refs_18_
  35.2 3.8 %collective-permute-done.17.refs_19_ = bf16[3,64,128]{2,1,0:T(8,128)(2,1)S(1)} collective-permute-done((bf16[3,64,128]{2,1,0:T(8,128)(2,1)S(1)}, bf16[3,64,128]{2,1,0:T(8,128)(2,1)S(1)}, u32[]{:S(2)}, u32[]{:S(2)}) %collective-permute-start.17) | collective-permute-done | bytes 49184 | tf_op jit(solution)/shard_map/ppermute | solution.py:153
  39.0 5.9 %picks.1 = (bf16[512,128]{1,0:T(8,128)(2,1)S(1)}, bf16[512,128]{1,0:T(8,128)(2,1)S(1)}, bf16[512,128]{1,0:T(8,128)(2,1)S(1)}, bf16[512,128]{1,0:T(8,128)(2,1)S(1)}) custom-call(s32[2]{0:T(128)S(1)} %pad_add_fusion.place_ref, s32[2,512]{1,0:T(2,128)S(1)} %and_select_fusion.refs_0_, s32[2,512]{1,0:T(2,128)S(1)} %collective-permute-done.refs_1_, ...), custom_call_target="tpu_custom_call" | custom-call | tf_op jit(solution)/shard_map/picks/pallas_call | solution.py:177
  45.0 0.1 collective-permute-start.18
  45.1 2.9 %collective-permute-start.19 = (bf16[512,128]{1,0:T(8,128)(2,1)S(1)}, bf16[512,128]{1,0:T(8,128)(2,1)S(1)}, u32[]{:S(2)}, u32[]{:S(2)}) collective-permute-start(bf16[512,128]{1,0:T(8,128)(2,1)S(1)} %get-tuple-element.43), channel_id=1, source_target_pairs={{0,8},{1,9},{2,10},{3,11},{4,12},{5,13},{6,14},{7,15},{8,0},{9,1},... | collective-permute-start | bytes 393224 | tf_op jit(solution)/shard_map/ppermute | solution.py:153
  48.0 0.1 collective-permute-start.20
  48.1 9.9 %collective-permute-done.19.refs_2_ = bf16[512,128]{1,0:T(8,128)(2,1)S(1)} collective-permute-done((bf16[512,128]{1,0:T(8,128)(2,1)S(1)}, bf16[512,128]{1,0:T(8,128)(2,1)S(1)}, u32[]{:S(2)}, u32[]{:S(2)}) %collective-permute-start.19) | collective-permute-done | bytes 131104 | tf_op jit(solution)/shard_map/ppermute | solution.py:153
  58.0 2.2 %collective-permute-done.20.refs_3_ = bf16[512,128]{1,0:T(8,128)(2,1)S(1)} collective-permute-done((bf16[512,128]{1,0:T(8,128)(2,1)S(1)}, bf16[512,128]{1,0:T(8,128)(2,1)S(1)}, u32[]{:S(2)}, u32[]{:S(2)}) %collective-permute-start.20) | collective-permute-done | bytes 131104 | tf_op jit(solution)/shard_map/ppermute | solution.py:153
  60.2 2.0 %lags.1 = f32[2,512,256]{2,1,0:T(8,128)} custom-call(s32[2]{0:T(128)S(1)} %pad_add_fusion.place_ref, f32[256,256]{1,0:T(8,128)S(1)} %copy-done.1, bf16[512,128]{1,0:T(8,128)(2,1)S(1)} %get-tuple-element.41.refs_0_, bf16[512,128]{1,0:T(8,128)(2,1)S(1)} %collective-permute-done.18.refs_1_, bf16[512,128]{1,0:T(8,128)(2,1)S(1)} %collective-permute-done.19.refs_2_, ...), custom_call_target="tpu_custom_call" | custom-call | tf_op jit(solution)/shard_map/lags/pallas_call | solution.py:192
  (8 shorter events, 0.0 us)
Async XLA Ops:
  0.0 8.7 %copy-start.2 = (bf16[256,256]{1,0:T(8,128)(2,1)S(1)}, bf16[256,256]{1,0:T(8,128)(2,1)}, u32[]{:S(2)}) copy-start(bf16[256,256]{1,0:T(8,128)(2,1)} %constant.58.clone.forward_ref) | copy-start | bytes 393220
  4.4 8.9 %collective-permute-start.2 = (s32[2,512]{1,0:T(2,128)S(1)}, s32[2,512]{1,0:T(2,128)S(1)}, u32[]{:S(2)}, u32[]{:S(2)}) collective-permute-start(s32[2,512]{1,0:T(2,128)S(1)} %and_select_fusion.refs_0_), channel_id=1, source_target_pairs={{0,9},{1,8},{2,11},{3,10},{4,13},{5,12},{6,15},{7,14},{8,1},{9,0},... | collective-permute-start | bytes 12296 | tf_op jit(solution)/shard_map/ppermute | solution.py:153
  7.9 5.4 %collective-permute-start.1 = (s32[2,512]{1,0:T(2,128)S(1)}, s32[2,512]{1,0:T(2,128)S(1)}, u32[]{:S(2)}, u32[]{:S(2)}) collective-permute-start(s32[2,512]{1,0:T(2,128)S(1)} %and_select_fusion.refs_0_), channel_id=1, source_target_pairs={{0,8},{1,9},{2,10},{3,11},{4,12},{5,13},{6,14},{7,15},{8,0},{9,1},... | collective-permute-start | bytes 12296 | tf_op jit(solution)/shard_map/ppermute | solution.py:153
  8.5 6.5 %collective-permute-start = (s32[2,512]{1,0:T(2,128)S(1)}, s32[2,512]{1,0:T(2,128)S(1)}, u32[]{:S(2)}, u32[]{:S(2)}) collective-permute-start(s32[2,512]{1,0:T(2,128)S(1)} %and_select_fusion.refs_0_), channel_id=1, source_target_pairs={{0,1},{1,0},{2,3},{3,2},{4,5},{5,4},{6,7},{7,6},{8,9},{9,8},{10,11... | collective-permute-start | bytes 12296 | tf_op jit(solution)/shard_map/ppermute | solution.py:153
  8.7 1.1 %copy-start = (bf16[3,1,512,256]{3,2,1,0:T(8,128)(2,1)S(1)}, bf16[3,1,512,256]{3,2,1,0:T(8,128)(2,1)}, u32[]{:S(2)}) copy-start(bf16[3,1,512,256]{3,2,1,0:T(8,128)(2,1)} %param.5) | copy-start | bytes 2359300
  11.3 4.0 %collective-permute-start.3 = (bf16[3,64,128]{2,1,0:T(8,128)(2,1)S(1)}, bf16[3,64,128]{2,1,0:T(8,128)(2,1)S(1)}, u32[]{:S(2)}, u32[]{:S(2)}) collective-permute-start(bf16[3,64,128]{2,1,0:T(8,128)(2,1)S(1)} %get-tuple-element.26), channel_id=1, source_target_pairs={{0,1},{1,0},{2,3},{3,2},{4,5},{5,4},{6,7},{7,6},{8,9},{9,8},{10,11... | collective-permute-start | bytes 147464 | tf_op jit(solution)/shard_map/ppermute | solution.py:153
  11.8 6.1 %collective-permute-start.4 = (bf16[3,64,128]{2,1,0:T(8,128)(2,1)S(1)}, bf16[3,64,128]{2,1,0:T(8,128)(2,1)S(1)}, u32[]{:S(2)}, u32[]{:S(2)}) collective-permute-start(bf16[3,64,128]{2,1,0:T(8,128)(2,1)S(1)} %get-tuple-element.27), channel_id=1, source_target_pairs={{0,2},{1,3},{2,0},{3,1},{4,6},{5,7},{6,4},{7,5},{8,10},{9,11},{10,... | collective-permute-start | bytes 147464 | tf_op jit(solution)/shard_map/ppermute | solution.py:153
  13.3 4.5 %collective-permute-start.5 = (bf16[3,64,128]{2,1,0:T(8,128)(2,1)S(1)}, bf16[3,64,128]{2,1,0:T(8,128)(2,1)S(1)}, u32[]{:S(2)}, u32[]{:S(2)}) collective-permute-start(bf16[3,64,128]{2,1,0:T(8,128)(2,1)S(1)} %get-tuple-element.28), channel_id=1, source_target_pairs={{0,3},{1,2},{2,1},{3,0},{4,7},{5,6},{6,5},{7,4},{8,11},{9,10},{10,... | collective-permute-start | bytes 147464 | tf_op jit(solution)/shard_map/ppermute | solution.py:153
  13.3 7.0 %collective-permute-start.6 = (bf16[3,64,128]{2,1,0:T(8,128)(2,1)S(1)}, bf16[3,64,128]{2,1,0:T(8,128)(2,1)S(1)}, u32[]{:S(2)}, u32[]{:S(2)}) collective-permute-start(bf16[3,64,128]{2,1,0:T(8,128)(2,1)S(1)} %get-tuple-element.29), channel_id=1, source_target_pairs={{0,4},{1,5},{2,6},{3,7},{4,0},{5,1},{6,2},{7,3},{8,12},{9,13},{10,... | collective-permute-start | bytes 147464 | tf_op jit(solution)/shard_map/ppermute | solution.py:153
  15.0 6.3 %collective-permute-start.7 = (bf16[3,64,128]{2,1,0:T(8,128)(2,1)S(1)}, bf16[3,64,128]{2,1,0:T(8,128)(2,1)S(1)}, u32[]{:S(2)}, u32[]{:S(2)}) collective-permute-start(bf16[3,64,128]{2,1,0:T(8,128)(2,1)S(1)} %get-tuple-element.30), channel_id=1, source_target_pairs={{0,5},{1,4},{2,7},{3,6},{4,1},{5,0},{6,3},{7,2},{8,13},{9,12},{10,... | collective-permute-start | bytes 147464 | tf_op jit(solution)/shard_map/ppermute | solution.py:153
  15.3 8.6 %collective-permute-start.8 = (bf16[3,64,128]{2,1,0:T(8,128)(2,1)S(1)}, bf16[3,64,128]{2,1,0:T(8,128)(2,1)S(1)}, u32[]{:S(2)}, u32[]{:S(2)}) collective-permute-start(bf16[3,64,128]{2,1,0:T(8,128)(2,1)S(1)} %get-tuple-element.31), channel_id=1, source_target_pairs={{0,6},{1,7},{2,4},{3,5},{4,2},{5,3},{6,0},{7,1},{8,14},{9,15},{10,... | collective-permute-start | bytes 147464 | tf_op jit(solution)/shard_map/ppermute | solution.py:153
  17.9 6.4 %collective-permute-start.9 = (bf16[3,64,128]{2,1,0:T(8,128)(2,1)S(1)}, bf16[3,64,128]{2,1,0:T(8,128)(2,1)S(1)}, u32[]{:S(2)}, u32[]{:S(2)}) collective-permute-start(bf16[3,64,128]{2,1,0:T(8,128)(2,1)S(1)} %get-tuple-element.32), channel_id=1, source_target_pairs={{0,7},{1,6},{2,5},{3,4},{4,3},{5,2},{6,1},{7,0},{8,15},{9,14},{10,... | collective-permute-start | bytes 147464 | tf_op jit(solution)/shard_map/ppermute | solution.py:153
  17.9 9.6 %collective-permute-start.10 = (bf16[3,64,128]{2,1,0:T(8,128)(2,1)S(1)}, bf16[3,64,128]{2,1,0:T(8,128)(2,1)S(1)}, u32[]{:S(2)}, u32[]{:S(2)}) collective-permute-start(bf16[3,64,128]{2,1,0:T(8,128)(2,1)S(1)} %get-tuple-element.33), channel_id=1, source_target_pairs={{0,8},{1,9},{2,10},{3,11},{4,12},{5,13},{6,14},{7,15},{8,0},{9,1},... | collective-permute-start | bytes 147464 | tf_op jit(solution)/shard_map/ppermute | solution.py:153
  20.3 8.1 %collective-permute-start.11 = (bf16[3,64,128]{2,1,0:T(8,128)(2,1)S(1)}, bf16[3,64,128]{2,1,0:T(8,128)(2,1)S(1)}, u32[]{:S(2)}, u32[]{:S(2)}) collective-permute-start(bf16[3,64,128]{2,1,0:T(8,128)(2,1)S(1)} %get-tuple-element.34), channel_id=1, source_target_pairs={{0,9},{1,8},{2,11},{3,10},{4,13},{5,12},{6,15},{7,14},{8,1},{9,0},... | collective-permute-start | bytes 147464 | tf_op jit(solution)/shard_map/ppermute | solution.py:153
  21.3 11.0 %collective-permute-start.12 = (bf16[3,64,128]{2,1,0:T(8,128)(2,1)S(1)}, bf16[3,64,128]{2,1,0:T(8,128)(2,1)S(1)}, u32[]{:S(2)}, u32[]{:S(2)}) collective-permute-start(bf16[3,64,128]{2,1,0:T(8,128)(2,1)S(1)} %get-tuple-element.35), channel_id=1, source_target_pairs={{0,10},{1,11},{2,8},{3,9},{4,14},{5,15},{6,12},{7,13},{8,2},{9,3},... | collective-permute-start | bytes 147464 | tf_op jit(solution)/shard_map/ppermute | solution.py:153
  23.9 11.3 %collective-permute-start.13 = (bf16[3,64,128]{2,1,0:T(8,128)(2,1)S(1)}, bf16[3,64,128]{2,1,0:T(8,128)(2,1)S(1)}, u32[]{:S(2)}, u32[]{:S(2)}) collective-permute-start(bf16[3,64,128]{2,1,0:T(8,128)(2,1)S(1)} %get-tuple-element.36), channel_id=1, source_target_pairs={{0,11},{1,10},{2,9},{3,8},{4,15},{5,14},{6,13},{7,12},{8,3},{9,2},... | collective-permute-start | bytes 147464 | tf_op jit(solution)/shard_map/ppermute | solution.py:153
  24.3 10.9 %collective-permute-start.14 = (bf16[3,64,128]{2,1,0:T(8,128)(2,1)S(1)}, bf16[3,64,128]{2,1,0:T(8,128)(2,1)S(1)}, u32[]{:S(2)}, u32[]{:S(2)}) collective-permute-start(bf16[3,64,128]{2,1,0:T(8,128)(2,1)S(1)} %get-tuple-element.37), channel_id=1, source_target_pairs={{0,12},{1,13},{2,14},{3,15},{4,8},{5,9},{6,10},{7,11},{8,4},{9,5},... | collective-permute-start | bytes 147464 | tf_op jit(solution)/shard_map/ppermute | solution.py:153
  27.5 7.6 %collective-permute-start.15 = (bf16[3,64,128]{2,1,0:T(8,128)(2,1)S(1)}, bf16[3,64,128]{2,1,0:T(8,128)(2,1)S(1)}, u32[]{:S(2)}, u32[]{:S(2)}) collective-permute-start(bf16[3,64,128]{2,1,0:T(8,128)(2,1)S(1)} %get-tuple-element.38), channel_id=1, source_target_pairs={{0,13},{1,12},{2,15},{3,14},{4,9},{5,8},{6,11},{7,10},{8,5},{9,4},... | collective-permute-start | bytes 147464 | tf_op jit(solution)/shard_map/ppermute | solution.py:153
  28.4 6.8 %collective-permute-start.16 = (bf16[3,64,128]{2,1,0:T(8,128)(2,1)S(1)}, bf16[3,64,128]{2,1,0:T(8,128)(2,1)S(1)}, u32[]{:S(2)}, u32[]{:S(2)}) collective-permute-start(bf16[3,64,128]{2,1,0:T(8,128)(2,1)S(1)} %get-tuple-element.39), channel_id=1, source_target_pairs={{0,14},{1,15},{2,12},{3,13},{4,10},{5,11},{6,8},{7,9},{8,6},{9,7},... | collective-permute-start | bytes 147464 | tf_op jit(solution)/shard_map/ppermute | solution.py:153
  32.2 6.8 %collective-permute-start.17 = (bf16[3,64,128]{2,1,0:T(8,128)(2,1)S(1)}, bf16[3,64,128]{2,1,0:T(8,128)(2,1)S(1)}, u32[]{:S(2)}, u32[]{:S(2)}) collective-permute-start(bf16[3,64,128]{2,1,0:T(8,128)(2,1)S(1)} %get-tuple-element.40), channel_id=1, source_target_pairs={{0,15},{1,14},{2,13},{3,12},{4,11},{5,10},{6,9},{7,8},{8,7},{9,6},... | collective-permute-start | bytes 147464 | tf_op jit(solution)/shard_map/ppermute | solution.py:153
  39.0 21.2 %copy-start.1 = (f32[256,256]{1,0:T(8,128)S(1)}, f32[256,256]{1,0:T(8,128)}, u32[]{:S(2)}) copy-start(f32[256,256]{1,0:T(8,128)} %constant.59.clone.inverse_ref) | copy-start | bytes 786436
  45.0 3.1 %collective-permute-start.18 = (bf16[512,128]{1,0:T(8,128)(2,1)S(1)}, bf16[512,128]{1,0:T(8,128)(2,1)S(1)}, u32[]{:S(2)}, u32[]{:S(2)}) collective-permute-start(bf16[512,128]{1,0:T(8,128)(2,1)S(1)} %get-tuple-element.42), channel_id=1, source_target_pairs={{0,1},{1,0},{2,3},{3,2},{4,5},{5,4},{6,7},{7,6},{8,9},{9,8},{10,11... | collective-permute-start | bytes 393224 | tf_op jit(solution)/shard_map/ppermute | solution.py:153
  45.1 12.9 %collective-permute-start.19 = (bf16[512,128]{1,0:T(8,128)(2,1)S(1)}, bf16[512,128]{1,0:T(8,128)(2,1)S(1)}, u32[]{:S(2)}, u32[]{:S(2)}) collective-permute-start(bf16[512,128]{1,0:T(8,128)(2,1)S(1)} %get-tuple-element.43), channel_id=1, source_target_pairs={{0,8},{1,9},{2,10},{3,11},{4,12},{5,13},{6,14},{7,15},{8,0},{9,1},... | collective-permute-start | bytes 393224 | tf_op jit(solution)/shard_map/ppermute | solution.py:153
  48.0 12.2 %collective-permute-start.20 = (bf16[512,128]{1,0:T(8,128)(2,1)S(1)}, bf16[512,128]{1,0:T(8,128)(2,1)S(1)}, u32[]{:S(2)}, u32[]{:S(2)}) collective-permute-start(bf16[512,128]{1,0:T(8,128)(2,1)S(1)} %get-tuple-element.44), channel_id=1, source_target_pairs={{0,9},{1,8},{2,11},{3,10},{4,13},{5,12},{6,15},{7,14},{8,1},{9,0},... | collective-permute-start | bytes 393224 | tf_op jit(solution)/shard_map/ppermute | solution.py:153

commit v2 on v1

v2 whole, which is shorter than its diff:
```python
import functools
import math

import jax
import jax.numpy as jnp
import numpy as np
from jax import lax
from jax.experimental import pallas as pl
from jax.experimental.pallas import tpu as pltpu
from jax.sharding import PartitionSpec as P

EPSILON = 1e-06
SLOTS = 32
NT = (((1,), (1,)), ((), ()))
TN = (((0,), (0,)), ((), ()))
VMEM_LIMIT = 40 * 1024 * 1024


def tables(samples, stations):
    bins = samples // 2
    quarter = bins // 4
    turn = np.arange(bins)[:, None] * np.arange(samples)[None, :] % samples
    angle = turn * (2.0 * math.pi / samples)
    weight = np.where(np.arange(bins) == 0, 1.0, 2.0)[:, None] / samples
    weight = weight * math.sqrt(samples / (3.0 * stations))

    def by_quarter(real, imag):
        rows = [real.reshape(4, quarter, samples), imag.reshape(4, quarter, samples)]
        return np.concatenate(rows, axis=1).reshape(4 * 2 * quarter, samples)

    forward = by_quarter(np.cos(angle), -np.sin(angle)).astype(np.float32)
    inverse = by_quarter(weight * np.cos(angle), -weight * np.sin(angle)).astype(np.float32)
    return forward.astype(jnp.bfloat16), inverse


def place_of(place_ref, groups):
    position = place_ref[0]
    high, inner = position // (2 * groups), position % (2 * groups)
    return high * 2 + inner % 2, inner // 2


def spectra_kernel(place_ref, windows_ref, pairs_ref, forward_ref, *piece_refs):
    comps, _, groups, _, samples = windows_ref.shape
    rows = forward_ref.shape[0] // 4
    lanes = 4 * SLOTS
    quarter, group = place_of(place_ref, groups)
    table = jnp.concatenate(
        [forward_ref[pl.ds(pl.multiple_of((quarter ^ m) * rows, rows), rows), :] for m in range(4)]
    )
    ones = jnp.ones((16, samples), jnp.bfloat16)
    listed = jnp.concatenate([pairs_ref[0], pairs_ref[1]]).astype(jnp.float32)
    listed = jnp.concatenate(
        [listed[:, at : at + lanes] for at in range(0, listed.shape[1], lanes)]
    ).astype(jnp.bfloat16)
    for mg in range(groups):
        parts = []
        for comp in range(comps):
            low = windows_ref[comp, 0, group ^ mg]
            high = windows_ref[comp, 1, group ^ mg]
            parts += [low[:SLOTS], high[SLOTS:], low[SLOTS:], high[:SLOTS]]
        traces = jnp.concatenate(parts)
        square = jnp.square(traces.astype(jnp.float32))
        square_hi = square.astype(jnp.bfloat16)
        square_lo = (square - square_hi.astype(jnp.float32)).astype(jnp.bfloat16)
        energy = lax.dot_general(ones, square_hi, NT, preferred_element_type=jnp.float32)
        energy += lax.dot_general(ones, square_lo, NT, preferred_element_type=jnp.float32)
        scale = lax.rsqrt(energy[:1] + EPSILON)
        raw = lax.dot_general(table, traces, NT, preferred_element_type=jnp.float32)
        spectra = (raw * scale).astype(jnp.bfloat16)
        for mq in range(4):
            piece = piece_refs[(mq // 2) * 2 * groups + mg * 2 + mq % 2]
            for comp in range(comps):
                piece[comp * rows : (comp + 1) * rows] = spectra[
                    mq * rows : (mq + 1) * rows, comp * lanes : (comp + 1) * lanes
                ]
            if mg == 0:
                piece[comps * rows :] = listed


def pick(place_ref, counts_ref, listed, flat_ref, mq, *picked_refs):
    cells = counts_ref.shape[0]
    quarter, group = place_of(place_ref, cells // 4)
    own = quarter ^ mq
    high, low = own // 2, own % 2
    cell = high * (cells // 2) + group * 2 + low
    lanes = listed.shape[1]
    turned = listed.astype(jnp.float32).T
    lane = lax.broadcasted_iota(jnp.int32, (lanes, lanes), 1)
    sides = ((high, high), (low, 1 - low))
    found = []
    for step_round in range(2):
        own_count = counts_ref[cell].astype(jnp.float32)
        far_count = counts_ref[cell ^ (cells // 2 if step_round else 1)].astype(jnp.float32)
        hot = []
        for chunk in range(listed.shape[0] // 4):
            at = chunk * 4 + step_round * 2
            first, second = turned[:, at : at + 1], turned[:, at + 1 : at + 2]
            live = (first < own_count) & (second < far_count)
            place = jnp.where(high == low, first * SLOTS + second, second * SLOTS + first)
            offset = jnp.where(live, place, -1.0).astype(jnp.int32) - lane
            hot.append(
                jnp.concatenate(
                    [
                        jnp.where(offset == lanes * t, 1.0, 0.0).astype(jnp.bfloat16)
                        for t in range(SLOTS * SLOTS // lanes)
                    ],
                    axis=1,
                )
            )
        block = flat_ref[sides[step_round][0], sides[step_round][1]]
        found.append(jnp.dot(jnp.concatenate(hot), block, preferred_element_type=jnp.float32))
    found = jnp.concatenate(found, axis=1).astype(jnp.bfloat16)
    each = found.shape[0] // len(picked_refs)
    for at, ref in enumerate(picked_refs):
        ref[...] = found[at * each : (at + 1) * each]


def cross_kernel(place_ref, counts_ref, *refs):
    piece_refs, (flat_ref, picked_0, picked_1, trace_ref, cross_ref) = refs[:-5], refs[-5:]
    rows = flat_ref.shape[3]
    bins = rows // 2
    lanes = piece_refs[0].shape[1]
    each = piece_refs[-1].shape[0]
    traces = len(piece_refs) * each // rows
    for s, piece in enumerate(piece_refs):
        trace_ref[s * each : (s + 1) * each] = piece[:each].astype(jnp.float32)
    half = 2 * SLOTS
    for k in range(bins):
        real = trace_ref[pl.ds(k, traces, stride=rows), :].astype(jnp.bfloat16)
        imag = trace_ref[pl.ds(bins + k, traces, stride=rows), :].astype(jnp.bfloat16)
        left = jnp.concatenate([real, imag], axis=0)
        right = jnp.concatenate(
            [jnp.concatenate([real, imag], axis=1), jnp.concatenate([imag, -real], axis=1)], axis=0
        )
        cross = lax.dot_general(left, right, TN, preferred_element_type=jnp.float32)
        cross_ref[k * half : (k + 1) * half] = cross[:half, :lanes]
        cross_ref[(bins + k) * half : (bins + k + 1) * half] = cross[:half, lanes:]
    for i in range(half):
        turned = cross_ref[pl.ds(i, rows, stride=half), :].T.astype(jnp.bfloat16)
        own, slot = i // SLOTS, i % SLOTS
        for far in range(2):
            start = half + far * SLOTS
            flat_ref[own, far, slot * SLOTS : (slot + 1) * SLOTS] = turned[start : start + SLOTS]
    pick(place_ref, counts_ref, piece_refs[2][each:], flat_ref, 2, picked_0)
    pick(place_ref, counts_ref, piece_refs[3][each:], flat_ref, 3, picked_1)


def near_kernel(place_ref, counts_ref, listed_0, listed_1, flat_ref, picked_0, *picked_1):
    listing = picked_0.shape[0] * 4 // listed_0.shape[1]
    pick(place_ref, counts_ref, listed_1[listed_1.shape[0] - listing :], flat_ref, 1, *picked_1)
    pick(place_ref, counts_ref, listed_0[listed_0.shape[0] - listing :], flat_ref, 0, picked_0)


def lag_kernel(groups, place_ref, inverse_ref, *refs):
    picked_refs, lags_ref = refs[:-1], refs[-1]
    quarter, _ = place_of(place_ref, groups)
    rows = inverse_ref.shape[0] // 4
    sign = jnp.where(quarter // 2 == quarter % 2, 1.0, -1.0)
    row = lax.broadcasted_iota(jnp.int32, (rows, inverse_ref.shape[1]), 0)
    factor = jnp.where(row < rows // 2, 1.0, sign)
    table = jnp.concatenate(
        [
            inverse_ref[pl.ds(pl.multiple_of((quarter ^ m) * rows, rows), rows), :] * factor
            for m in (0, 2, 3, 1)
        ]
    )
    table_hi = table.astype(jnp.bfloat16)
    table_lo = (table - table_hi.astype(jnp.float32)).astype(jnp.bfloat16)
    picked = [ref[...] for ref in picked_refs]
    picked[3:] = [jnp.concatenate(picked[3:])]
    for step_round in range(2):
        cross = jnp.concatenate([p[:, step_round * rows : (step_round + 1) * rows] for p in picked], axis=1)
        lags_ref[step_round] = jnp.dot(
            cross, table_hi, preferred_element_type=jnp.float32
        ) + jnp.dot(cross, table_lo, preferred_element_type=jnp.float32)


def on_device(windows, counts, pairs):
    comps, _, events, samples = windows.shape
    cells = lax.axis_size("cell")
    half, groups = cells // 2, cells // 4
    count = pairs.shape[2]
    rows = samples // 4
    lanes = 4 * SLOTS
    forward, inverse = tables(samples, cells)
    place = lax.axis_index("cell").astype(jnp.int32).reshape(1)

    def swap(x, mask):
        return lax.ppermute(x, "cell", [(i, i ^ mask) for i in range(cells)])

    vmem = pl.BlockSpec(memory_space=pltpu.VMEM)
    smem = pl.BlockSpec(memory_space=pltpu.SMEM)
    params = pltpu.CompilerParams(vmem_limit_bytes=VMEM_LIMIT)

    near = [0, 1, half, half + 1]
    listing = pairs.size // lanes
    pieces = pl.pallas_call(
        spectra_kernel,
        out_shape=[
            jax.ShapeDtypeStruct((comps * rows + listing * (m in near), lanes), jnp.bfloat16)
            for m in range(cells)
        ],
        in_specs=[smem, vmem, vmem, vmem],
        out_specs=[vmem] * cells,
        compiler_params=params,
        name="spectra",
    )(place, windows.reshape(comps, 2, groups, 2 * SLOTS, samples), pairs, jnp.asarray(forward))
    order = [half, 1]
    for m in range(1, half):
        order += [half + m] + [m + 1] * (m + 1 < half)
    arrived = {m: swap(pieces[m], m) for m in order}
    arrived[0] = pieces[0]
    pieces = [arrived[m] for m in near + [m for m in order if m not in near]]

    picked_shape = jax.ShapeDtypeStruct((count, 2 * rows), jnp.bfloat16)
    flat, picked_2, picked_3 = pl.pallas_call(
        cross_kernel,
        out_shape=[
            jax.ShapeDtypeStruct((2, 2, SLOTS * SLOTS, rows), jnp.bfloat16),
            picked_shape,
            picked_shape,
        ],
        in_specs=[smem, smem] + [vmem] * cells,
        out_specs=[vmem] * 3,
        scratch_shapes=[
            pltpu.VMEM((comps * cells * rows, lanes), jnp.float32),
            pltpu.VMEM((rows * 2 * SLOTS, lanes), jnp.float32),
        ],
        compiler_params=params,
        name="cross",
    )(place, counts, *pieces)
    picked_2, picked_3 = swap(picked_2, near[2]), swap(picked_3, near[3])
    picked_0, *picked_1 = pl.pallas_call(
        near_kernel,
        out_shape=[picked_shape] + [jax.ShapeDtypeStruct((count // 2, 2 * rows), jnp.bfloat16)] * 2,
        in_specs=[smem, smem] + [vmem] * 3,
        out_specs=[vmem] * 3,
        compiler_params=params,
        cost_estimate=pl.CostEstimate(
            flops=128 * count * SLOTS * SLOTS * rows, bytes_accessed=2**21, transcendentals=0
        ),
        name="near",
    )(place, counts, pieces[0], pieces[1], flat)
    picked_1 = [swap(p, near[1]) for p in picked_1]

    return pl.pallas_call(
        functools.partial(lag_kernel, groups),
        out_shape=jax.ShapeDtypeStruct((2, count, samples), jnp.float32),
        in_specs=[smem] + [vmem] * 6,
        out_specs=vmem,
        compiler_params=params,
        name="lags",
    )(place, jnp.asarray(inverse), picked_0, picked_2, picked_3, *picked_1)


def solution(mesh):
    in_specs = (P(None, "cell", "grp", None), P("grp"), P(None, None, ("grp", "cell")))
    out_specs = P(None, ("grp", "cell"), None)
    return jax.shard_map(
        on_device, mesh=mesh, in_specs=in_specs, out_specs=out_specs, check_vma=False
    )
```

time: 62.4 us -> 53.1 us (0.85)
  starting transfers between devices: 31.1 us -> 25.8 us
  other arithmetic: 2.22 us -> 0 us
  waiting for transfers between devices: 16 us -> 14.6 us
    ppermute x21 -> x19, starting transfers between devices: 31.1 us -> 25.8 us  [swap(): return lax.ppermute(x, 'cell', [(i, i ^ mask) for i in range(cells)])]
    unnamed x6 -> x10, local copies, waits for them, and re-layouts: 1.14 us -> 2.74 us
    another operation x2 -> x0, other arithmetic: 1.51 us -> none  [the longest x1 1.43 us: on_device(): far_counts = jnp.stack([counts[position ^ 1], counts[position ^ half]])]
    ppermute x21 -> x19, waiting for transfers between devices: 16 us -> 14.6 us  [swap(): return lax.ppermute(x, 'cell', [(i, i ^ mask) for i in range(cells)])]
    dynamic_slice x1 -> x0, local copies, waits for them, and re-layouts: 1.44 us -> none  [on_device(): live = (first < counts[position]) & (second < far_counts[:, None])]
    slice x1 -> x0, local copies, waits for them, and re-layouts: 0.78 us -> none  [on_device(): first, second = (pairs[:, 0], pairs[:, 1])]
    select_n x1 -> x0, other arithmetic: 0.72 us -> none  [on_device(): index = jnp.where(live, flat, -1)]
    pallas_call x3 -> x4, Pallas kernels: 9.4 us -> 9.79 us  [the longest x1 5.23 us: on_device(): pl.pallas_call(cross_kernel, out_shape=[jax.ShapeDtypeStruct((2, 2, SLOTS...]
  transfers between devices with their start and end apart: 21 -> 19, of which waited for: 4 -> 7; matrix products, arithmetic and copies ran while one was open for 0% -> 0% of each run, Pallas kernels for 2% -> 4%
where the time goes in v2:
time: 53.1 us; the launch traced here: 52.9 us
  starting transfers between devices  25.8 us (49%)
  waiting for transfers between devices  14.6 us (27%)
  Pallas kernels  9.79 us (18%)
  local copies, waits for them, and re-layouts  2.74 us (5%)
    ppermute x19, starting transfers between devices, swap(): return lax.ppermute(x, 'cell', [(i, i ^ mask) for i in range(cells)])  25.8 us
    ppermute x19, waiting for transfers between devices, swap(): return lax.ppermute(x, 'cell', [(i, i ^ mask) for i in range(cells)])  14.6 us
    pallas_call x1, Pallas kernels, on_device(): pl.pallas_call(cross_kernel, out_shape=[jax.ShapeDtypeStruct((2, 2, SLOTS...  5.23 us
    unnamed x10, local copies, waits for them, and re-layouts  2.74 us
    pallas_call x1, Pallas kernels, on_device(): pl.pallas_call(near_kernel, out_shape=[picked_shape] + [jax.ShapeDtypeStr...  2.2 us
    pallas_call x1, Pallas kernels, on_device(): pl.pallas_call(functools.partial(lag_kernel, groups), out_shape=jax.Shape...  1.45 us
  transfers between devices with their start and end apart: 19, of which 7 were waited for; matrix products, arithmetic and copies ran while one was open for 0% of the time, Pallas kernels for 4%

profile of v2, /device:TPU:0, one launch (start us, length us, event | category | flops | bytes accessed | tf_op | source)
XLA Modules:
  0.0 52.9 jit_solution(15439654055306142563)
XLA Ops:
  0.0 0.0 copy-start.3
  0.0 0.7 %copy-done.3 = s32[2,2,512]{2,1,0:T(2,128)S(1)} copy-done((s32[2,2,512]{2,1,0:T(2,128)S(1)}, s32[2,2,512]{2,1,0:T(2,128)}, u32[]{:S(2)}) %copy-start.3) | copy-done | bytes 8216
  0.7 1.1 %copy-done = bf16[3,1,512,256]{3,2,1,0:T(8,128)(2,1)S(1)} copy-done((bf16[3,1,512,256]{3,2,1,0:T(8,128)(2,1)S(1)}, bf16[3,1,512,256]{3,2,1,0:T(8,128)(2,1)}, u32[]{:S(2)}) %copy-start) | copy-done | bytes 786456
  1.8 0.9 %copy-done.2 = bf16[256,256]{1,0:T(8,128)(2,1)S(1)} copy-done((bf16[256,256]{1,0:T(8,128)(2,1)S(1)}, bf16[256,256]{1,0:T(8,128)(2,1)}, u32[]{:S(2)}) %copy-start.2) | copy-done | bytes 131096
  2.7 0.9 %spectra.1 = (bf16[208,128]{1,0:T(8,128)(2,1)S(1)}, bf16[208,128]{1,0:T(8,128)(2,1)S(1)}, bf16[192,128]{1,0:T(8,128)(2,1)S(1)}, bf16[192,128]{1,0:T(8,128)(2,1)S...) custom-call(s32[1]{0:T(128)} %bitcast.place_ref, ...), custom_call_target="tpu_custom_call" | custom-call | tf_op jit(solution)/shard_map/spectra/pallas_call | solution.py:197
  3.7 3.0 %collective-permute-start.3 = (bf16[192,128]{1,0:T(8,128)(2,1)S(1)}, bf16[192,128]{1,0:T(8,128)(2,1)S(1)}, u32[]{:S(2)}, u32[]{:S(2)}) collective-permute-start(bf16[192,128]{1,0:T(8,128)(2,1)S(1)} %get-tuple-element.31), channel_id=1, source_target_pairs={{0,2},{1,3},{2,0},{3,1},{4,6},{5,7},{6,4},{7,5},{8,10},{9,11},{10,... | collective-permute-start | bytes 147464 | tf_op jit(solution)/shard_map/ppermute | solution.py:189
  6.7 2.5 %collective-permute-start.4 = (bf16[192,128]{1,0:T(8,128)(2,1)S(1)}, bf16[192,128]{1,0:T(8,128)(2,1)S(1)}, u32[]{:S(2)}, u32[]{:S(2)}) collective-permute-start(bf16[192,128]{1,0:T(8,128)(2,1)S(1)} %get-tuple-element.32), channel_id=1, source_target_pairs={{0,10},{1,11},{2,8},{3,9},{4,14},{5,15},{6,12},{7,13},{8,2},{9,3},... | collective-permute-start | bytes 147464 | tf_op jit(solution)/shard_map/ppermute | solution.py:189
  9.2 0.4 collective-permute-start.5
  9.6 0.8 %collective-permute-start.6 = (bf16[192,128]{1,0:T(8,128)(2,1)S(1)}, bf16[192,128]{1,0:T(8,128)(2,1)S(1)}, u32[]{:S(2)}, u32[]{:S(2)}) collective-permute-start(bf16[192,128]{1,0:T(8,128)(2,1)S(1)} %get-tuple-element.34), channel_id=1, source_target_pairs={{0,11},{1,10},{2,9},{3,8},{4,15},{5,14},{6,13},{7,12},{8,3},{9,2},... | collective-permute-start | bytes 147464 | tf_op jit(solution)/shard_map/ppermute | solution.py:189
  10.5 1.9 %collective-permute-start.7 = (bf16[192,128]{1,0:T(8,128)(2,1)S(1)}, bf16[192,128]{1,0:T(8,128)(2,1)S(1)}, u32[]{:S(2)}, u32[]{:S(2)}) collective-permute-start(bf16[192,128]{1,0:T(8,128)(2,1)S(1)} %get-tuple-element.35), channel_id=1, source_target_pairs={{0,4},{1,5},{2,6},{3,7},{4,0},{5,1},{6,2},{7,3},{8,12},{9,13},{10,... | collective-permute-start | bytes 147464 | tf_op jit(solution)/shard_map/ppermute | solution.py:189
  12.3 0.0 collective-permute-done.3.refs_4_
  12.3 2.5 %collective-permute-start.8 = (bf16[192,128]{1,0:T(8,128)(2,1)S(1)}, bf16[192,128]{1,0:T(8,128)(2,1)S(1)}, u32[]{:S(2)}, u32[]{:S(2)}) collective-permute-start(bf16[192,128]{1,0:T(8,128)(2,1)S(1)} %get-tuple-element.36), channel_id=1, source_target_pairs={{0,12},{1,13},{2,14},{3,15},{4,8},{5,9},{6,10},{7,11},{8,4},{9,5},... | collective-permute-start | bytes 147464 | tf_op jit(solution)/shard_map/ppermute | solution.py:189
  14.8 0.0 collective-permute-done.4.refs_5_
  14.8 0.0 collective-permute-start.9
  14.8 0.0 collective-permute-done.5.refs_6_
  14.8 2.1 %collective-permute-start.10 = (bf16[192,128]{1,0:T(8,128)(2,1)S(1)}, bf16[192,128]{1,0:T(8,128)(2,1)S(1)}, u32[]{:S(2)}, u32[]{:S(2)}) collective-permute-start(bf16[192,128]{1,0:T(8,128)(2,1)S(1)} %get-tuple-element.38), channel_id=1, source_target_pairs={{0,13},{1,12},{2,15},{3,14},{4,9},{5,8},{6,11},{7,10},{8,5},{9,4},... | collective-permute-start | bytes 147464 | tf_op jit(solution)/shard_map/ppermute | solution.py:189
  16.9 0.0 collective-permute-done.6.refs_7_
  16.9 1.7 %collective-permute-start.11 = (bf16[192,128]{1,0:T(8,128)(2,1)S(1)}, bf16[192,128]{1,0:T(8,128)(2,1)S(1)}, u32[]{:S(2)}, u32[]{:S(2)}) collective-permute-start(bf16[192,128]{1,0:T(8,128)(2,1)S(1)} %get-tuple-element.39), channel_id=1, source_target_pairs={{0,6},{1,7},{2,4},{3,5},{4,2},{5,3},{6,0},{7,1},{8,14},{9,15},{10,... | collective-permute-start | bytes 147464 | tf_op jit(solution)/shard_map/ppermute | solution.py:189
  18.6 0.0 collective-permute-done.7.refs_8_
  18.6 1.8 %collective-permute-start.12 = (bf16[192,128]{1,0:T(8,128)(2,1)S(1)}, bf16[192,128]{1,0:T(8,128)(2,1)S(1)}, u32[]{:S(2)}, u32[]{:S(2)}) collective-permute-start(bf16[192,128]{1,0:T(8,128)(2,1)S(1)} %get-tuple-element.40), channel_id=1, source_target_pairs={{0,14},{1,15},{2,12},{3,13},{4,10},{5,11},{6,8},{7,9},{8,6},{9,7},... | collective-permute-start | bytes 147464 | tf_op jit(solution)/shard_map/ppermute | solution.py:189
  20.4 0.0 collective-permute-done.8.refs_9_
  20.4 0.4 collective-permute-start
  20.8 0.0 collective-permute-done.9.refs_10_
  20.8 1.4 %collective-permute-start.1 = (bf16[208,128]{1,0:T(8,128)(2,1)S(1)}, bf16[208,128]{1,0:T(8,128)(2,1)S(1)}, u32[]{:S(2)}, u32[]{:S(2)}) collective-permute-start(bf16[208,128]{1,0:T(8,128)(2,1)S(1)} %get-tuple-element.29), channel_id=1, source_target_pairs={{0,8},{1,9},{2,10},{3,11},{4,12},{5,13},{6,14},{7,15},{8,0},{9,1},... | collective-permute-start | bytes 159752 | tf_op jit(solution)/shard_map/ppermute | solution.py:189
  22.2 0.0 collective-permute-done.10.refs_11_
  22.2 1.0 %collective-permute-start.2 = (bf16[208,128]{1,0:T(8,128)(2,1)S(1)}, bf16[208,128]{1,0:T(8,128)(2,1)S(1)}, u32[]{:S(2)}, u32[]{:S(2)}) collective-permute-start(bf16[208,128]{1,0:T(8,128)(2,1)S(1)} %get-tuple-element.30), channel_id=1, source_target_pairs={{0,9},{1,8},{2,11},{3,10},{4,13},{5,12},{6,15},{7,14},{8,1},{9,0},... | collective-permute-start | bytes 159752 | tf_op jit(solution)/shard_map/ppermute | solution.py:189
  23.2 0.0 collective-permute-done.11.refs_12_
  23.2 1.5 %collective-permute-start.13 = (bf16[192,128]{1,0:T(8,128)(2,1)S(1)}, bf16[192,128]{1,0:T(8,128)(2,1)S(1)}, u32[]{:S(2)}, u32[]{:S(2)}) collective-permute-start(bf16[192,128]{1,0:T(8,128)(2,1)S(1)} %get-tuple-element.41), channel_id=1, source_target_pairs={{0,7},{1,6},{2,5},{3,4},{4,3},{5,2},{6,1},{7,0},{8,15},{9,14},{10,... | collective-permute-start | bytes 147464 | tf_op jit(solution)/shard_map/ppermute | solution.py:189
  24.8 0.6 %collective-permute-done.12.refs_13_ = bf16[192,128]{1,0:T(8,128)(2,1)S(1)} collective-permute-done((bf16[192,128]{1,0:T(8,128)(2,1)S(1)}, bf16[192,128]{1,0:T(8,128)(2,1)S(1)}, u32[]{:S(2)}, u32[]{:S(2)}) %collective-permute-start.12) | collective-permute-done | bytes 49184 | tf_op jit(solution)/shard_map/ppermute | solution.py:189
  25.4 1.5 %collective-permute-start.14 = (bf16[192,128]{1,0:T(8,128)(2,1)S(1)}, bf16[192,128]{1,0:T(8,128)(2,1)S(1)}, u32[]{:S(2)}, u32[]{:S(2)}) collective-permute-start(bf16[192,128]{1,0:T(8,128)(2,1)S(1)} %get-tuple-element.42), channel_id=1, source_target_pairs={{0,15},{1,14},{2,13},{3,12},{4,11},{5,10},{6,9},{7,8},{8,7},{9,6},... | collective-permute-start | bytes 147464 | tf_op jit(solution)/shard_map/ppermute | solution.py:189
  26.8 1.1 %collective-permute-done.13.refs_14_ = bf16[192,128]{1,0:T(8,128)(2,1)S(1)} collective-permute-done((bf16[192,128]{1,0:T(8,128)(2,1)S(1)}, bf16[192,128]{1,0:T(8,128)(2,1)S(1)}, u32[]{:S(2)}, u32[]{:S(2)}) %collective-permute-start.13) | collective-permute-done | bytes 49184 | tf_op jit(solution)/shard_map/ppermute | solution.py:189
  27.9 4.0 %collective-permute-done.14.refs_15_ = bf16[192,128]{1,0:T(8,128)(2,1)S(1)} collective-permute-done((bf16[192,128]{1,0:T(8,128)(2,1)S(1)}, bf16[192,128]{1,0:T(8,128)(2,1)S(1)}, u32[]{:S(2)}, u32[]{:S(2)}) %collective-permute-start.14) | collective-permute-done | bytes 49184 | tf_op jit(solution)/shard_map/ppermute | solution.py:189
  31.9 0.0 collective-permute-done.refs_1_.listed_1
  31.9 0.0 collective-permute-done.1.refs_2_
  31.9 0.0 collective-permute-done.2.refs_3_
  31.9 0.0 copy-done.4
  32.0 5.2 %cross.1 = (bf16[2,2,1024,64]{3,2,1,0:T(8,128)(2,1)S(1)}, bf16[512,128]{1,0:T(8,128)(2,1)S(1)}, bf16[512,128]{1,0:T(8,128)(2,1)S(1)}) custom-call(s32[1]{0:T(128)} %bitcast.place_ref, s32[16]{0:T(128)S(1)} %copy-done.4, bf16[208,128]{1,0:T(8,128)(2,1)S(1)} %get-tuple-element.27.refs_0_.listed_0, bf16[208,128]{1,0:T(8,128)(2,1)S(1)} %collective-permute-done.refs_1_.listed_1, ...), custom_call_target="tpu_custom_call" | custom-call | tf_op jit(solution)/shard_map/cross/pallas_call | solution.py:216
  37.2 0.1 collective-permute-start.15
  37.3 2.0 %collective-permute-start.16 = (bf16[512,128]{1,0:T(8,128)(2,1)S(1)}, bf16[512,128]{1,0:T(8,128)(2,1)S(1)}, u32[]{:S(2)}, u32[]{:S(2)}) collective-permute-start(bf16[512,128]{1,0:T(8,128)(2,1)S(1)} %get-tuple-element.46), channel_id=1, source_target_pairs={{0,9},{1,8},{2,11},{3,10},{4,13},{5,12},{6,15},{7,14},{8,1},{9,0},... | collective-permute-start | bytes 393224 | tf_op jit(solution)/shard_map/ppermute | solution.py:189
  39.3 2.2 %near.1 = (bf16[512,128]{1,0:T(8,128)(2,1)S(1)}, bf16[256,128]{1,0:T(8,128)(2,1)S(1)}, bf16[256,128]{1,0:T(8,128)(2,1)S(1)}) custom-call(s32[1]{0:T(128)} %bitcast.place_ref, s32[16]{0:T(128)S(1)} %copy-done.4, bf16[208,128]{1,0:T(8,128)(2,1)S(1)} %get-tuple-element.27.refs_0_.listed_0, bf16[208,128]{1,0:T(8,128)(2,1)S(1)} %collective-permute-done.refs_1_.listed_1, ...), custom_call_target="tpu_custom_call" | custom-call | flops 4294967296 | bytes 2097152 | tf_op jit(solution)/shard_map/near/pallas_call | solution.py:233
  41.5 1.1 %collective-permute-start.17 = (bf16[256,128]{1,0:T(8,128)(2,1)S(1)}, bf16[256,128]{1,0:T(8,128)(2,1)S(1)}, u32[]{:S(2)}, u32[]{:S(2)}) collective-permute-start(bf16[256,128]{1,0:T(8,128)(2,1)S(1)} %get-tuple-element.47), channel_id=1, source_target_pairs={{0,1},{1,0},{2,3},{3,2},{4,5},{5,4},{6,7},{7,6},{8,9},{9,8},{10,11... | collective-permute-start | bytes 196616 | tf_op jit(solution)/shard_map/ppermute | solution.py:189
  42.6 0.1 collective-permute-start.18
  42.6 0.8 %collective-permute-done.17.refs_3_ = bf16[256,128]{1,0:T(8,128)(2,1)S(1)} collective-permute-done((bf16[256,128]{1,0:T(8,128)(2,1)S(1)}, bf16[256,128]{1,0:T(8,128)(2,1)S(1)}, u32[]{:S(2)}, u32[]{:S(2)}) %collective-permute-start.17) | collective-permute-done | bytes 65568 | tf_op jit(solution)/shard_map/ppermute | solution.py:189
  43.5 0.4 collective-permute-done.18.refs_4_
  43.8 5.4 %collective-permute-done.15.refs_1_ = bf16[512,128]{1,0:T(8,128)(2,1)S(1)} collective-permute-done((bf16[512,128]{1,0:T(8,128)(2,1)S(1)}, bf16[512,128]{1,0:T(8,128)(2,1)S(1)}, u32[]{:S(2)}, u32[]{:S(2)}) %collective-permute-start.15) | collective-permute-done | bytes 131104 | tf_op jit(solution)/shard_map/ppermute | solution.py:189
  49.2 2.3 %collective-permute-done.16.refs_2_ = bf16[512,128]{1,0:T(8,128)(2,1)S(1)} collective-permute-done((bf16[512,128]{1,0:T(8,128)(2,1)S(1)}, bf16[512,128]{1,0:T(8,128)(2,1)S(1)}, u32[]{:S(2)}, u32[]{:S(2)}) %collective-permute-start.16) | collective-permute-done | bytes 131104 | tf_op jit(solution)/shard_map/ppermute | solution.py:189
  51.5 0.0 copy-done.1
  51.5 1.5 %lags.1 = f32[2,512,256]{2,1,0:T(8,128)} custom-call(s32[1]{0:T(128)} %bitcast.place_ref, f32[256,256]{1,0:T(8,128)S(1)} %copy-done.1, bf16[512,128]{1,0:T(8,128)(2,1)S(1)} %get-tuple-element.44.refs_0_, bf16[512,128]{1,0:T(8,128)(2,1)S(1)} %collective-permute-done.15.refs_1_, bf16[512,128]{1,0:T(8,128)(2,1)S(1)} %collective-permute-done.16.refs_2_, ...), custom_call_target="tpu_custom_call" | custom-call | tf_op jit(solution)/shard_map/lags/pallas_call | solution.py:246
  (4 shorter events, 0.0 us)
Async XLA Ops:
  0.0 0.7 %copy-start.3 = (s32[2,2,512]{2,1,0:T(2,128)S(1)}, s32[2,2,512]{2,1,0:T(2,128)}, u32[]{:S(2)}) copy-start(s32[2,2,512]{2,1,0:T(2,128)} %pairs_ref.1) | copy-start | bytes 24580
  0.7 1.1 %copy-start = (bf16[3,1,512,256]{3,2,1,0:T(8,128)(2,1)S(1)}, bf16[3,1,512,256]{3,2,1,0:T(8,128)(2,1)}, u32[]{:S(2)}) copy-start(bf16[3,1,512,256]{3,2,1,0:T(8,128)(2,1)} %param.5) | copy-start | bytes 2359300
  1.8 0.9 %copy-start.2 = (bf16[256,256]{1,0:T(8,128)(2,1)S(1)}, bf16[256,256]{1,0:T(8,128)(2,1)}, u32[]{:S(2)}) copy-start(bf16[256,256]{1,0:T(8,128)(2,1)} %constant.8.clone.forward_ref) | copy-start | bytes 393220
  3.7 8.7 %collective-permute-start.3 = (bf16[192,128]{1,0:T(8,128)(2,1)S(1)}, bf16[192,128]{1,0:T(8,128)(2,1)S(1)}, u32[]{:S(2)}, u32[]{:S(2)}) collective-permute-start(bf16[192,128]{1,0:T(8,128)(2,1)S(1)} %get-tuple-element.31), channel_id=1, source_target_pairs={{0,2},{1,3},{2,0},{3,1},{4,6},{5,7},{6,4},{7,5},{8,10},{9,11},{10,... | collective-permute-start | bytes 147464 | tf_op jit(solution)/shard_map/ppermute | solution.py:189
  6.7 8.1 %collective-permute-start.4 = (bf16[192,128]{1,0:T(8,128)(2,1)S(1)}, bf16[192,128]{1,0:T(8,128)(2,1)S(1)}, u32[]{:S(2)}, u32[]{:S(2)}) collective-permute-start(bf16[192,128]{1,0:T(8,128)(2,1)S(1)} %get-tuple-element.32), channel_id=1, source_target_pairs={{0,10},{1,11},{2,8},{3,9},{4,14},{5,15},{6,12},{7,13},{8,2},{9,3},... | collective-permute-start | bytes 147464 | tf_op jit(solution)/shard_map/ppermute | solution.py:189
  9.2 5.6 %collective-permute-start.5 = (bf16[192,128]{1,0:T(8,128)(2,1)S(1)}, bf16[192,128]{1,0:T(8,128)(2,1)S(1)}, u32[]{:S(2)}, u32[]{:S(2)}) collective-permute-start(bf16[192,128]{1,0:T(8,128)(2,1)S(1)} %get-tuple-element.33), channel_id=1, source_target_pairs={{0,3},{1,2},{2,1},{3,0},{4,7},{5,6},{6,5},{7,4},{8,11},{9,10},{10,... | collective-permute-start | bytes 147464 | tf_op jit(solution)/shard_map/ppermute | solution.py:189
  9.6 7.2 %collective-permute-start.6 = (bf16[192,128]{1,0:T(8,128)(2,1)S(1)}, bf16[192,128]{1,0:T(8,128)(2,1)S(1)}, u32[]{:S(2)}, u32[]{:S(2)}) collective-permute-start(bf16[192,128]{1,0:T(8,128)(2,1)S(1)} %get-tuple-element.34), channel_id=1, source_target_pairs={{0,11},{1,10},{2,9},{3,8},{4,15},{5,14},{6,13},{7,12},{8,3},{9,2},... | collective-permute-start | bytes 147464 | tf_op jit(solution)/shard_map/ppermute | solution.py:189
  10.5 8.1 %collective-permute-start.7 = (bf16[192,128]{1,0:T(8,128)(2,1)S(1)}, bf16[192,128]{1,0:T(8,128)(2,1)S(1)}, u32[]{:S(2)}, u32[]{:S(2)}) collective-permute-start(bf16[192,128]{1,0:T(8,128)(2,1)S(1)} %get-tuple-element.35), channel_id=1, source_target_pairs={{0,4},{1,5},{2,6},{3,7},{4,0},{5,1},{6,2},{7,3},{8,12},{9,13},{10,... | collective-permute-start | bytes 147464 | tf_op jit(solution)/shard_map/ppermute | solution.py:189
  12.3 8.1 %collective-permute-start.8 = (bf16[192,128]{1,0:T(8,128)(2,1)S(1)}, bf16[192,128]{1,0:T(8,128)(2,1)S(1)}, u32[]{:S(2)}, u32[]{:S(2)}) collective-permute-start(bf16[192,128]{1,0:T(8,128)(2,1)S(1)} %get-tuple-element.36), channel_id=1, source_target_pairs={{0,12},{1,13},{2,14},{3,15},{4,8},{5,9},{6,10},{7,11},{8,4},{9,5},... | collective-permute-start | bytes 147464 | tf_op jit(solution)/shard_map/ppermute | solution.py:189
  14.8 6.0 %collective-permute-start.9 = (bf16[192,128]{1,0:T(8,128)(2,1)S(1)}, bf16[192,128]{1,0:T(8,128)(2,1)S(1)}, u32[]{:S(2)}, u32[]{:S(2)}) collective-permute-start(bf16[192,128]{1,0:T(8,128)(2,1)S(1)} %get-tuple-element.37), channel_id=1, source_target_pairs={{0,5},{1,4},{2,7},{3,6},{4,1},{5,0},{6,3},{7,2},{8,13},{9,12},{10,... | collective-permute-start | bytes 147464 | tf_op jit(solution)/shard_map/ppermute | solution.py:189
  14.8 7.4 %collective-permute-start.10 = (bf16[192,128]{1,0:T(8,128)(2,1)S(1)}, bf16[192,128]{1,0:T(8,128)(2,1)S(1)}, u32[]{:S(2)}, u32[]{:S(2)}) collective-permute-start(bf16[192,128]{1,0:T(8,128)(2,1)S(1)} %get-tuple-element.38), channel_id=1, source_target_pairs={{0,13},{1,12},{2,15},{3,14},{4,9},{5,8},{6,11},{7,10},{8,5},{9,4},... | collective-permute-start | bytes 147464 | tf_op jit(solution)/shard_map/ppermute | solution.py:189
  16.9 6.4 %collective-permute-start.11 = (bf16[192,128]{1,0:T(8,128)(2,1)S(1)}, bf16[192,128]{1,0:T(8,128)(2,1)S(1)}, u32[]{:S(2)}, u32[]{:S(2)}) collective-permute-start(bf16[192,128]{1,0:T(8,128)(2,1)S(1)} %get-tuple-element.39), channel_id=1, source_target_pairs={{0,6},{1,7},{2,4},{3,5},{4,2},{5,3},{6,0},{7,1},{8,14},{9,15},{10,... | collective-permute-start | bytes 147464 | tf_op jit(solution)/shard_map/ppermute | solution.py:189
  18.6 6.8 %collective-permute-start.12 = (bf16[192,128]{1,0:T(8,128)(2,1)S(1)}, bf16[192,128]{1,0:T(8,128)(2,1)S(1)}, u32[]{:S(2)}, u32[]{:S(2)}) collective-permute-start(bf16[192,128]{1,0:T(8,128)(2,1)S(1)} %get-tuple-element.40), channel_id=1, source_target_pairs={{0,14},{1,15},{2,12},{3,13},{4,10},{5,11},{6,8},{7,9},{8,6},{9,7},... | collective-permute-start | bytes 147464 | tf_op jit(solution)/shard_map/ppermute | solution.py:189
  20.4 11.6 %collective-permute-start = (bf16[208,128]{1,0:T(8,128)(2,1)S(1)}, bf16[208,128]{1,0:T(8,128)(2,1)S(1)}, u32[]{:S(2)}, u32[]{:S(2)}) collective-permute-start(bf16[208,128]{1,0:T(8,128)(2,1)S(1)} %get-tuple-element.28), channel_id=1, source_target_pairs={{0,1},{1,0},{2,3},{3,2},{4,5},{5,4},{6,7},{7,6},{8,9},{9,8},{10,11... | collective-permute-start | bytes 159752 | tf_op jit(solution)/shard_map/ppermute | solution.py:189
  20.8 11.2 %collective-permute-start.1 = (bf16[208,128]{1,0:T(8,128)(2,1)S(1)}, bf16[208,128]{1,0:T(8,128)(2,1)S(1)}, u32[]{:S(2)}, u32[]{:S(2)}) collective-permute-start(bf16[208,128]{1,0:T(8,128)(2,1)S(1)} %get-tuple-element.29), channel_id=1, source_target_pairs={{0,8},{1,9},{2,10},{3,11},{4,12},{5,13},{6,14},{7,15},{8,0},{9,1},... | collective-permute-start | bytes 159752 | tf_op jit(solution)/shard_map/ppermute | solution.py:189
  22.2 9.8 %collective-permute-start.2 = (bf16[208,128]{1,0:T(8,128)(2,1)S(1)}, bf16[208,128]{1,0:T(8,128)(2,1)S(1)}, u32[]{:S(2)}, u32[]{:S(2)}) collective-permute-start(bf16[208,128]{1,0:T(8,128)(2,1)S(1)} %get-tuple-element.30), channel_id=1, source_target_pairs={{0,9},{1,8},{2,11},{3,10},{4,13},{5,12},{6,15},{7,14},{8,1},{9,0},... | collective-permute-start | bytes 159752 | tf_op jit(solution)/shard_map/ppermute | solution.py:189
  23.2 4.7 %collective-permute-start.13 = (bf16[192,128]{1,0:T(8,128)(2,1)S(1)}, bf16[192,128]{1,0:T(8,128)(2,1)S(1)}, u32[]{:S(2)}, u32[]{:S(2)}) collective-permute-start(bf16[192,128]{1,0:T(8,128)(2,1)S(1)} %get-tuple-element.41), channel_id=1, source_target_pairs={{0,7},{1,6},{2,5},{3,4},{4,3},{5,2},{6,1},{7,0},{8,15},{9,14},{10,... | collective-permute-start | bytes 147464 | tf_op jit(solution)/shard_map/ppermute | solution.py:189
  25.4 6.6 %copy-start.4 = (s32[16]{0:T(128)S(1)}, s32[16]{0:T(128)}, u32[]{:S(2)}) copy-start(s32[16]{0:T(128)} %counts_ref.3) | copy-start | bytes 196
  25.4 6.6 %collective-permute-start.14 = (bf16[192,128]{1,0:T(8,128)(2,1)S(1)}, bf16[192,128]{1,0:T(8,128)(2,1)S(1)}, u32[]{:S(2)}, u32[]{:S(2)}) collective-permute-start(bf16[192,128]{1,0:T(8,128)(2,1)S(1)} %get-tuple-element.42), channel_id=1, source_target_pairs={{0,15},{1,14},{2,13},{3,12},{4,11},{5,10},{6,9},{7,8},{8,7},{9,6},... | collective-permute-start | bytes 147464 | tf_op jit(solution)/shard_map/ppermute | solution.py:189
  37.2 12.0 %collective-permute-start.15 = (bf16[512,128]{1,0:T(8,128)(2,1)S(1)}, bf16[512,128]{1,0:T(8,128)(2,1)S(1)}, u32[]{:S(2)}, u32[]{:S(2)}) collective-permute-start(bf16[512,128]{1,0:T(8,128)(2,1)S(1)} %get-tuple-element.45), channel_id=1, source_target_pairs={{0,8},{1,9},{2,10},{3,11},{4,12},{5,13},{6,14},{7,15},{8,0},{9,1},... | collective-permute-start | bytes 393224 | tf_op jit(solution)/shard_map/ppermute | solution.py:189
  37.3 14.2 %collective-permute-start.16 = (bf16[512,128]{1,0:T(8,128)(2,1)S(1)}, bf16[512,128]{1,0:T(8,128)(2,1)S(1)}, u32[]{:S(2)}, u32[]{:S(2)}) collective-permute-start(bf16[512,128]{1,0:T(8,128)(2,1)S(1)} %get-tuple-element.46), channel_id=1, source_target_pairs={{0,9},{1,8},{2,11},{3,10},{4,13},{5,12},{6,15},{7,14},{8,1},{9,0},... | collective-permute-start | bytes 393224 | tf_op jit(solution)/shard_map/ppermute | solution.py:189
  39.3 12.2 %copy-start.1 = (f32[256,256]{1,0:T(8,128)S(1)}, f32[256,256]{1,0:T(8,128)}, u32[]{:S(2)}) copy-start(f32[256,256]{1,0:T(8,128)} %constant.9.clone.inverse_ref) | copy-start | bytes 786436
  41.5 2.0 %collective-permute-start.17 = (bf16[256,128]{1,0:T(8,128)(2,1)S(1)}, bf16[256,128]{1,0:T(8,128)(2,1)S(1)}, u32[]{:S(2)}, u32[]{:S(2)}) collective-permute-start(bf16[256,128]{1,0:T(8,128)(2,1)S(1)} %get-tuple-element.47), channel_id=1, source_target_pairs={{0,1},{1,0},{2,3},{3,2},{4,5},{5,4},{6,7},{7,6},{8,9},{9,8},{10,11... | collective-permute-start | bytes 196616 | tf_op jit(solution)/shard_map/ppermute | solution.py:189
  42.6 1.3 %collective-permute-start.18 = (bf16[256,128]{1,0:T(8,128)(2,1)S(1)}, bf16[256,128]{1,0:T(8,128)(2,1)S(1)}, u32[]{:S(2)}, u32[]{:S(2)}) collective-permute-start(bf16[256,128]{1,0:T(8,128)(2,1)S(1)} %get-tuple-element.48), channel_id=1, source_target_pairs={{0,1},{1,0},{2,3},{3,2},{4,5},{5,4},{6,7},{7,6},{8,9},{9,8},{10,11... | collective-permute-start | bytes 196616 | tf_op jit(solution)/shard_map/ppermute | solution.py:189

commit v3 on v2

--- a/solution.py
+++ b/solution.py
@@ -39,42 +39,46 @@
     return high * 2 + inner % 2, inner // 2
 
 
-def spectra_kernel(place_ref, windows_ref, pairs_ref, forward_ref, *piece_refs):
-    comps, _, groups, _, samples = windows_ref.shape
+def listing_of(pairs_ref, lanes):
+    listed = jnp.concatenate([pairs_ref[0], pairs_ref[1]]).astype(jnp.float32)
+    return jnp.concatenate([listed[:, at : at + lanes] for at in range(0, listed.shape[1], lanes)])
+
+
+def spectra_kernel(place_ref, own_ref, near_ref, own_pairs_ref, near_pairs_ref, forward_ref, *piece_refs):
+    comps, _, groups, _, samples = own_ref.shape
     rows = forward_ref.shape[0] // 4
     lanes = 4 * SLOTS
     quarter, group = place_of(place_ref, groups)
     table = jnp.concatenate(
-        [forward_ref[pl.ds(pl.multiple_of((quarter ^ m) * rows, rows), rows), :] for m in range(4)]
+        [forward_ref[pl.ds(pl.multiple_of((quarter ^ m) * rows, rows), rows), :] for m in (0, 2)]
     )
     ones = jnp.ones((16, samples), jnp.bfloat16)
-    listed = jnp.concatenate([pairs_ref[0], pairs_ref[1]]).astype(jnp.float32)
-    listed = jnp.concatenate(
-        [listed[:, at : at + lanes] for at in range(0, listed.shape[1], lanes)]
+    piece_refs[groups][2 * comps * rows :] = jnp.concatenate(
+        [listing_of(own_pairs_ref, lanes), listing_of(near_pairs_ref, lanes)]
     ).astype(jnp.bfloat16)
     for mg in range(groups):
-        parts = []
-        for comp in range(comps):
-            low = windows_ref[comp, 0, group ^ mg]
-            high = windows_ref[comp, 1, group ^ mg]
-            parts += [low[:SLOTS], high[SLOTS:], low[SLOTS:], high[:SLOTS]]
-        traces = jnp.concatenate(parts)
-        square = jnp.square(traces.astype(jnp.float32))
-        square_hi = square.astype(jnp.bfloat16)
-        square_lo = (square - square_hi.astype(jnp.float32)).astype(jnp.bfloat16)
-        energy = lax.dot_general(ones, square_hi, NT, preferred_element_type=jnp.float32)
-        energy += lax.dot_general(ones, square_lo, NT, preferred_element_type=jnp.float32)
-        scale = lax.rsqrt(energy[:1] + EPSILON)
-        raw = lax.dot_general(table, traces, NT, preferred_element_type=jnp.float32)
-        spectra = (raw * scale).astype(jnp.bfloat16)
-        for mq in range(4):
-            piece = piece_refs[(mq // 2) * 2 * groups + mg * 2 + mq % 2]
+        for station, windows_ref in enumerate((own_ref, near_ref)):
+            parts = []
             for comp in range(comps):
-                piece[comp * rows : (comp + 1) * rows] = spectra[
-                    mq * rows : (mq + 1) * rows, comp * lanes : (comp + 1) * lanes
-                ]
-            if mg == 0:
-                piece[comps * rows :] = listed
+                low = windows_ref[comp, 0, group ^ mg]
+                high = windows_ref[comp, 1, group ^ mg]
+                parts += [low[:SLOTS], high[SLOTS:], low[SLOTS:], high[:SLOTS]]
+            traces = jnp.concatenate(parts)
+            square = jnp.square(traces.astype(jnp.float32))
+            square_hi = square.astype(jnp.bfloat16)
+            square_lo = (square - square_hi.astype(jnp.float32)).astype(jnp.bfloat16)
+            energy = lax.dot_general(ones, square_hi, NT, preferred_element_type=jnp.float32)
+            energy += lax.dot_general(ones, square_lo, NT, preferred_element_type=jnp.float32)
+            scale = lax.rsqrt(energy[:1] + EPSILON)
+            raw = lax.dot_general(table, traces, NT, preferred_element_type=jnp.float32)
+            spectra = (raw * scale).astype(jnp.bfloat16)
+            for far in range(2):
+                piece = piece_refs[far * groups + mg]
+                for comp in range(comps):
+                    start = (station * comps + comp) * rows
+                    piece[start : start + rows] = spectra[
+                        far * rows : (far + 1) * rows, comp * lanes : (comp + 1) * lanes
+                    ]
 
 
 def pick(place_ref, counts_ref, listed, flat_ref, mq, *picked_refs):
@@ -84,7 +88,7 @@
     high, low = own // 2, own % 2
     cell = high * (cells // 2) + group * 2 + low
     lanes = listed.shape[1]
-    turned = listed.astype(jnp.float32).T
+    turned = listed.T
     lane = lax.broadcasted_iota(jnp.int32, (lanes, lanes), 1)
     sides = ((high, high), (low, 1 - low))
     found = []
@@ -119,8 +123,7 @@
     piece_refs, (flat_ref, picked_0, picked_1, trace_ref, cross_ref) = refs[:-5], refs[-5:]
     rows = flat_ref.shape[3]
     bins = rows // 2
-    lanes = piece_refs[0].shape[1]
-    each = piece_refs[-1].shape[0]
+    each, lanes = piece_refs[0].shape
     traces = len(piece_refs) * each // rows
     for s, piece in enumerate(piece_refs):
         trace_ref[s * each : (s + 1) * each] = piece[:each].astype(jnp.float32)
@@ -141,14 +144,16 @@
         for far in range(2):
             start = half + far * SLOTS
             flat_ref[own, far, slot * SLOTS : (slot + 1) * SLOTS] = turned[start : start + SLOTS]
-    pick(place_ref, counts_ref, piece_refs[2][each:], flat_ref, 2, picked_0)
-    pick(place_ref, counts_ref, piece_refs[3][each:], flat_ref, 3, picked_1)
-
-
-def near_kernel(place_ref, counts_ref, listed_0, listed_1, flat_ref, picked_0, *picked_1):
-    listing = picked_0.shape[0] * 4 // listed_0.shape[1]
-    pick(place_ref, counts_ref, listed_1[listed_1.shape[0] - listing :], flat_ref, 1, *picked_1)
-    pick(place_ref, counts_ref, listed_0[listed_0.shape[0] - listing :], flat_ref, 0, picked_0)
+    listed = piece_refs[1][each:].astype(jnp.float32)
+    listing = listed.shape[0] // 2
+    pick(place_ref, counts_ref, listed[:listing], flat_ref, 2, picked_0)
+    pick(place_ref, counts_ref, listed[listing:], flat_ref, 3, picked_1)
+
+
+def near_kernel(place_ref, counts_ref, own_pairs_ref, near_pairs_ref, flat_ref, picked_0, *picked_1):
+    lanes = 4 * SLOTS
+    pick(place_ref, counts_ref, listing_of(near_pairs_ref, lanes), flat_ref, 1, *picked_1)
+    pick(place_ref, counts_ref, listing_of(own_pairs_ref, lanes), flat_ref, 0, picked_0)
 
 
 def lag_kernel(groups, place_ref, inverse_ref, *refs):
@@ -192,25 +197,23 @@
     smem = pl.BlockSpec(memory_space=pltpu.SMEM)
     params = pltpu.CompilerParams(vmem_limit_bytes=VMEM_LIMIT)
 
-    near = [0, 1, half, half + 1]
-    listing = pairs.size // lanes
+    windows = windows.reshape(comps, 2, groups, 2 * SLOTS, samples)
+    near_windows, near_pairs = swap(windows, 1), swap(pairs, 1)
+    listing = 2 * pairs.size // lanes
     pieces = pl.pallas_call(
         spectra_kernel,
         out_shape=[
-            jax.ShapeDtypeStruct((comps * rows + listing * (m in near), lanes), jnp.bfloat16)
-            for m in range(cells)
+            jax.ShapeDtypeStruct((2 * comps * rows + listing * (m == groups), lanes), jnp.bfloat16)
+            for m in range(2 * groups)
         ],
-        in_specs=[smem, vmem, vmem, vmem],
-        out_specs=[vmem] * cells,
+        in_specs=[smem] + [vmem] * 5,
+        out_specs=[vmem] * (2 * groups),
         compiler_params=params,
         name="spectra",
-    )(place, windows.reshape(comps, 2, groups, 2 * SLOTS, samples), pairs, jnp.asarray(forward))
-    order = [half, 1]
-    for m in range(1, half):
-        order += [half + m] + [m + 1] * (m + 1 < half)
-    arrived = {m: swap(pieces[m], m) for m in order}
-    arrived[0] = pieces[0]
-    pieces = [arrived[m] for m in near + [m for m in order if m not in near]]
+    )(place, windows, near_windows, pairs, near_pairs, jnp.asarray(forward))
+    order = [m for pair in zip(range(groups, 2 * groups), range(groups)) for m in pair if m]
+    arrived = {m: swap(pieces[m], 2 * m) for m in order}
+    pieces = [pieces[0]] + [arrived[m] for m in order]
 
     picked_shape = jax.ShapeDtypeStruct((count, 2 * rows), jnp.bfloat16)
     flat, picked_2, picked_3 = pl.pallas_call(
@@ -220,7 +223,7 @@
             picked_shape,
             picked_shape,
         ],
-        in_specs=[smem, smem] + [vmem] * cells,
+        in_specs=[smem, smem] + [vmem] * (2 * groups),
         out_specs=[vmem] * 3,
         scratch_shapes=[
             pltpu.VMEM((comps * cells * rows, lanes), jnp.float32),
@@ -229,7 +232,7 @@
         compiler_params=params,
         name="cross",
     )(place, counts, *pieces)
-    picked_2, picked_3 = swap(picked_2, near[2]), swap(picked_3, near[3])
+    picked_2, picked_3 = swap(picked_2, half), swap(picked_3, half + 1)
     picked_0, *picked_1 = pl.pallas_call(
         near_kernel,
         out_shape=[picked_shape] + [jax.ShapeDtypeStruct((count // 2, 2 * rows), jnp.bfloat16)] * 2,
@@ -240,8 +243,8 @@
             flops=128 * count * SLOTS * SLOTS * rows, bytes_accessed=2**21, transcendentals=0
         ),
         name="near",
-    )(place, counts, pieces[0], pieces[1], flat)
-    picked_1 = [swap(p, near[1]) for p in picked_1]
+    )(place, counts, pairs, near_pairs, flat)
+    picked_1 = [swap(p, 1) for p in picked_1]
 
     return pl.pallas_call(
         functools.partial(lag_kernel, groups),

time: 53.1 us -> 50.6 us (0.953); the launches traced: 52.9 us -> 49.9 us
  starting transfers between devices: 25.8 us -> 18.6 us
  waiting for transfers between devices: 14.6 us -> 18.8 us
  local copies, waits for them, and re-layouts: 2.74 us -> 2.05 us
  Pallas kernels: 9.79 us -> 10.4 us
    ppermute x19 -> x13, starting transfers between devices: 25.8 us -> 18.6 us  [swap(): return lax.ppermute(x, 'cell', [(i, i ^ mask) for i in range(cells)])]
    ppermute x19 -> x13, waiting for transfers between devices: 14.6 us -> 18.8 us  [swap(): return lax.ppermute(x, 'cell', [(i, i ^ mask) for i in range(cells)])]
    unnamed x10, local copies, waits for them, and re-layouts: 2.74 us -> 2.05 us
    pallas_call x1, Pallas kernels: 0.91 us -> 1.47 us  [on_device(): pl.pallas_call(spectra_kernel, out_shape=[jax.ShapeDtypeStruct((2 * comps...]
  transfers between devices with their start and end apart: 19 -> 13, of which waited for: 7 -> 8; matrix products, arithmetic and copies ran while one was open for 0% -> 0% of each run, Pallas kernels for 4% -> 4%
where the time goes in v3:
time: 50.6 us; the launch traced here: 49.9 us
  waiting for transfers between devices  18.8 us (37%)
  starting transfers between devices  18.6 us (37%)
  Pallas kernels  10.4 us (21%)
  local copies, waits for them, and re-layouts  2.05 us (4%)
    ppermute x13, waiting for transfers between devices, swap(): return lax.ppermute(x, 'cell', [(i, i ^ mask) for i in range(cells)])  18.8 us
    ppermute x13, starting transfers between devices, swap(): return lax.ppermute(x, 'cell', [(i, i ^ mask) for i in range(cells)])  18.6 us
    pallas_call x1, Pallas kernels, on_device(): pl.pallas_call(cross_kernel, out_shape=[jax.ShapeDtypeStruct((2, 2, SLOTS...  5.23 us
    pallas_call x1, Pallas kernels, on_device(): pl.pallas_call(near_kernel, out_shape=[picked_shape] + [jax.ShapeDtypeStr...  2.23 us
    unnamed x10, local copies, waits for them, and re-layouts  2.05 us
    pallas_call x1, Pallas kernels, on_device(): pl.pallas_call(spectra_kernel, out_shape=[jax.ShapeDtypeStruct((2 * comps...  1.47 us
    pallas_call x1, Pallas kernels, on_device(): pl.pallas_call(functools.partial(lag_kernel, groups), out_shape=jax.Shape...  1.45 us
  transfers between devices with their start and end apart: 13, of which 8 were waited for; matrix products, arithmetic and copies ran while one was open for 0% of the time, Pallas kernels for 4%

profile of v3, /device:TPU:0, one launch (start us, length us, event | category | flops | bytes accessed | tf_op | source)
XLA Modules:
  0.0 49.9 jit_solution(10887505503029967791)
XLA Ops:
  0.0 0.0 copy-start.3
  0.0 0.5 collective-permute-start.1
  0.5 0.1 collective-permute-start
  0.5 2.1 %collective-permute-done.near_pairs_ref = s32[2,2,512]{2,1,0:T(2,128)S(1)} collective-permute-done((s32[2,2,512]{2,1,0:T(2,128)}, s32[2,2,512]{2,1,0:T(2,128)S(1)}, u32[]{:S(2)}, u32[]{:S(2)}) %collective-permute-start) | collective-permute-done | bytes 8224 | tf_op jit(solution)/shard_map/ppermute | solution.py:194
  2.6 0.0 collective-permute-done.1.near_ref
  2.6 0.0 copy-done.3
  2.6 0.0 copy-start
  2.6 1.1 %copy-done = bf16[3,1,512,256]{3,2,1,0:T(8,128)(2,1)S(1)} copy-done((bf16[3,1,512,256]{3,2,1,0:T(8,128)(2,1)S(1)}, bf16[3,1,512,256]{3,2,1,0:T(8,128)(2,1)}, u32[]{:S(2)}) %copy-start) | copy-done | bytes 786456
  3.7 0.0 copy-start.2
  3.7 0.9 %copy-done.2 = bf16[256,256]{1,0:T(8,128)(2,1)S(1)} copy-done((bf16[256,256]{1,0:T(8,128)(2,1)S(1)}, bf16[256,256]{1,0:T(8,128)(2,1)}, u32[]{:S(2)}) %copy-start.2) | copy-done | bytes 131096
  4.6 1.5 %spectra.1 = (bf16[384,128]{1,0:T(8,128)(2,1)S(1)}, bf16[384,128]{1,0:T(8,128)(2,1)S(1)}, bf16[384,128]{1,0:T(8,128)(2,1)S(1)}, bf16[384,128]{1,0:T(8,128)(2,1)S...) custom-call(s32[1]{0:T(128)} %bitcast.place_ref, ...), custom_call_target="tpu_custom_call" | custom-call | tf_op jit(solution)/shard_map/spectra/pallas_call | solution.py:203
  6.1 5.0 %collective-permute-start.3 = (bf16[384,128]{1,0:T(8,128)(2,1)S(1)}, bf16[384,128]{1,0:T(8,128)(2,1)S(1)}, u32[]{:S(2)}, u32[]{:S(2)}) collective-permute-start(bf16[384,128]{1,0:T(8,128)(2,1)S(1)} %get-tuple-element.21), channel_id=1, source_target_pairs={{0,10},{1,11},{2,8},{3,9},{4,14},{5,15},{6,12},{7,13},{8,2},{9,3},... | collective-permute-start | bytes 294920 | tf_op jit(solution)/shard_map/ppermute | solution.py:194
  11.1 0.5 %collective-permute-start.4 = (bf16[384,128]{1,0:T(8,128)(2,1)S(1)}, bf16[384,128]{1,0:T(8,128)(2,1)S(1)}, u32[]{:S(2)}, u32[]{:S(2)}) collective-permute-start(bf16[384,128]{1,0:T(8,128)(2,1)S(1)} %get-tuple-element.22), channel_id=1, source_target_pairs={{0,2},{1,3},{2,0},{3,1},{4,6},{5,7},{6,4},{7,5},{8,10},{9,11},{10,... | collective-permute-start | bytes 294920 | tf_op jit(solution)/shard_map/ppermute | solution.py:194
  11.6 0.1 collective-permute-start.2
  11.7 3.8 %collective-permute-start.5 = (bf16[384,128]{1,0:T(8,128)(2,1)S(1)}, bf16[384,128]{1,0:T(8,128)(2,1)S(1)}, u32[]{:S(2)}, u32[]{:S(2)}) collective-permute-start(bf16[384,128]{1,0:T(8,128)(2,1)S(1)} %get-tuple-element.23), channel_id=1, source_target_pairs={{0,12},{1,13},{2,14},{3,15},{4,8},{5,9},{6,10},{7,11},{8,4},{9,5},... | collective-permute-start | bytes 294920 | tf_op jit(solution)/shard_map/ppermute | solution.py:194
  15.5 0.0 collective-permute-start.6
  15.5 4.3 %collective-permute-done.3.refs_2_ = bf16[384,128]{1,0:T(8,128)(2,1)S(1)} collective-permute-done((bf16[384,128]{1,0:T(8,128)(2,1)S(1)}, bf16[384,128]{1,0:T(8,128)(2,1)S(1)}, u32[]{:S(2)}, u32[]{:S(2)}) %collective-permute-start.3) | collective-permute-done | bytes 98336 | tf_op jit(solution)/shard_map/ppermute | solution.py:194
  19.9 5.4 %collective-permute-start.7 = (bf16[384,128]{1,0:T(8,128)(2,1)S(1)}, bf16[384,128]{1,0:T(8,128)(2,1)S(1)}, u32[]{:S(2)}, u32[]{:S(2)}) collective-permute-start(bf16[384,128]{1,0:T(8,128)(2,1)S(1)} %get-tuple-element.25), channel_id=1, source_target_pairs={{0,14},{1,15},{2,12},{3,13},{4,10},{5,11},{6,8},{7,9},{8,6},{9,7},... | collective-permute-start | bytes 294920 | tf_op jit(solution)/shard_map/ppermute | solution.py:194
  25.3 0.0 collective-permute-done.4.refs_3_
  25.3 0.0 copy-start.4
  25.3 0.0 collective-permute-start.8
  25.3 0.0 collective-permute-done.5.refs_4_
  25.3 0.0 collective-permute-done.6.refs_5_
  25.3 3.6 %collective-permute-done.7.refs_6_ = bf16[384,128]{1,0:T(8,128)(2,1)S(1)} collective-permute-done((bf16[384,128]{1,0:T(8,128)(2,1)S(1)}, bf16[384,128]{1,0:T(8,128)(2,1)S(1)}, u32[]{:S(2)}, u32[]{:S(2)}) %collective-permute-start.7) | collective-permute-done | bytes 98336 | tf_op jit(solution)/shard_map/ppermute | solution.py:194
  28.9 1.9 %collective-permute-done.8.refs_7_ = bf16[384,128]{1,0:T(8,128)(2,1)S(1)} collective-permute-done((bf16[384,128]{1,0:T(8,128)(2,1)S(1)}, bf16[384,128]{1,0:T(8,128)(2,1)S(1)}, u32[]{:S(2)}, u32[]{:S(2)}) %collective-permute-start.8) | collective-permute-done | bytes 98336 | tf_op jit(solution)/shard_map/ppermute | solution.py:194
  30.8 0.0 collective-permute-done.2.refs_1_
  30.8 0.0 copy-done.4
  30.8 5.2 %cross.1 = (bf16[2,2,1024,64]{3,2,1,0:T(8,128)(2,1)S(1)}, bf16[512,128]{1,0:T(8,128)(2,1)S(1)}, bf16[512,128]{1,0:T(8,128)(2,1)S(1)}) custom-call(s32[1]{0:T(128)} %bitcast.place_ref, s32[16]{0:T(128)S(1)} %copy-done.4, bf16[384,128]{1,0:T(8,128)(2,1)S(1)} %get-tuple-element.19.refs_0_, bf16[416,128]{1,0:T(8,128)(2,1)S(1)} %collective-permute-done.2.refs_1_, ...), custom_call_target="tpu_custom_call" | custom-call | tf_op jit(solution)/shard_map/cross/pallas_call | solution.py:219
  36.0 1.2 %collective-permute-start.9 = (bf16[512,128]{1,0:T(8,128)(2,1)S(1)}, bf16[512,128]{1,0:T(8,128)(2,1)S(1)}, u32[]{:S(2)}, u32[]{:S(2)}) collective-permute-start(bf16[512,128]{1,0:T(8,128)(2,1)S(1)} %get-tuple-element.29), channel_id=1, source_target_pairs={{0,8},{1,9},{2,10},{3,11},{4,12},{5,13},{6,14},{7,15},{8,0},{9,1},... | collective-permute-start | bytes 393224 | tf_op jit(solution)/shard_map/ppermute | solution.py:194
  37.2 0.0 collective-permute-start.10
  37.2 0.0 copy-start.1
  37.2 2.2 %near.1 = (bf16[512,128]{1,0:T(8,128)(2,1)S(1)}, bf16[256,128]{1,0:T(8,128)(2,1)S(1)}, bf16[256,128]{1,0:T(8,128)(2,1)S(1)}) custom-call(s32[1]{0:T(128)} %bitcast.place_ref, s32[16]{0:T(128)S(1)} %copy-done.4, s32[2,2,512]{2,1,0:T(2,128)S(1)} %copy-done.3, s32[2,2,512]{2,1,0:T(2,128)S(1)} %collective-permute-done.near_pairs_ref, ...), custom_call_target="tpu_custom_call" | custom-call | flops 4294967296 | bytes 2097152 | tf_op jit(solution)/shard_map/near/pallas_call | solution.py:236
  39.5 2.0 %collective-permute-start.11 = (bf16[256,128]{1,0:T(8,128)(2,1)S(1)}, bf16[256,128]{1,0:T(8,128)(2,1)S(1)}, u32[]{:S(2)}, u32[]{:S(2)}) collective-permute-start(bf16[256,128]{1,0:T(8,128)(2,1)S(1)} %get-tuple-element.31), channel_id=1, source_target_pairs={{0,1},{1,0},{2,3},{3,2},{4,5},{5,4},{6,7},{7,6},{8,9},{9,8},{10,11... | collective-permute-start | bytes 196616 | tf_op jit(solution)/shard_map/ppermute | solution.py:194
  41.4 0.1 collective-permute-start.12
  41.5 0.8 %collective-permute-done.11.refs_3_ = bf16[256,128]{1,0:T(8,128)(2,1)S(1)} collective-permute-done((bf16[256,128]{1,0:T(8,128)(2,1)S(1)}, bf16[256,128]{1,0:T(8,128)(2,1)S(1)}, u32[]{:S(2)}, u32[]{:S(2)}) %collective-permute-start.11) | collective-permute-done | bytes 65568 | tf_op jit(solution)/shard_map/ppermute | solution.py:194
  42.3 0.4 collective-permute-done.12.refs_4_
  42.7 5.2 %collective-permute-done.9.refs_1_ = bf16[512,128]{1,0:T(8,128)(2,1)S(1)} collective-permute-done((bf16[512,128]{1,0:T(8,128)(2,1)S(1)}, bf16[512,128]{1,0:T(8,128)(2,1)S(1)}, u32[]{:S(2)}, u32[]{:S(2)}) %collective-permute-start.9) | collective-permute-done | bytes 131104 | tf_op jit(solution)/shard_map/ppermute | solution.py:194
  47.9 0.5 %collective-permute-done.10.refs_2_ = bf16[512,128]{1,0:T(8,128)(2,1)S(1)} collective-permute-done((bf16[512,128]{1,0:T(8,128)(2,1)S(1)}, bf16[512,128]{1,0:T(8,128)(2,1)S(1)}, u32[]{:S(2)}, u32[]{:S(2)}) %collective-permute-start.10) | collective-permute-done | bytes 131104 | tf_op jit(solution)/shard_map/ppermute | solution.py:194
  48.4 0.0 copy-done.1
  48.4 1.5 %lags.1 = f32[2,512,256]{2,1,0:T(8,128)} custom-call(s32[1]{0:T(128)} %bitcast.place_ref, f32[256,256]{1,0:T(8,128)S(1)} %copy-done.1, bf16[512,128]{1,0:T(8,128)(2,1)S(1)} %get-tuple-element.28.refs_0_, bf16[512,128]{1,0:T(8,128)(2,1)S(1)} %collective-permute-done.9.refs_1_, bf16[512,128]{1,0:T(8,128)(2,1)S(1)} %collective-permute-done.10.refs_2_, ...), custom_call_target="tpu_custom_call" | custom-call | tf_op jit(solution)/shard_map/lags/pallas_call | solution.py:249
Async XLA Ops:
  0.0 2.6 %copy-start.3 = (s32[2,2,512]{2,1,0:T(2,128)S(1)}, s32[2,2,512]{2,1,0:T(2,128)}, u32[]{:S(2)}) copy-start(s32[2,2,512]{2,1,0:T(2,128)} %own_pairs_ref.3) | copy-start | bytes 24580
  0.0 2.6 %collective-permute-start.1 = (bf16[3,2,4,64,256]{4,3,2,1,0:T(8,128)(2,1)}, bf16[3,2,4,64,256]{4,3,2,1,0:T(8,128)(2,1)S(1)}, u32[]{:S(2)}, u32[]{:S(2)}) collective-permute-start(bf16[3,2,4,64,256]{4,3,2,1,0:T(8,128)(2,1)} %bitcast.2), channel_id=1, source_target_pairs={{0,1},{1,0},{2,3},{3,2},{4,5},{5,4},{6,7},{7,6},{8,9},{9,8},{10,11... | collective-permute-start | bytes 2359304 | tf_op jit(solution)/shard_map/ppermute | solution.py:194
  0.5 2.1 %collective-permute-start = (s32[2,2,512]{2,1,0:T(2,128)}, s32[2,2,512]{2,1,0:T(2,128)S(1)}, u32[]{:S(2)}, u32[]{:S(2)}) collective-permute-start(s32[2,2,512]{2,1,0:T(2,128)} %own_pairs_ref.3), channel_id=1, source_target_pairs={{0,1},{1,0},{2,3},{3,2},{4,5},{5,4},{6,7},{7,6},{8,9},{9,8},{10,11... | collective-permute-start | bytes 24584 | tf_op jit(solution)/shard_map/ppermute | solution.py:194
  2.6 1.1 %copy-start = (bf16[3,1,512,256]{3,2,1,0:T(8,128)(2,1)S(1)}, bf16[3,1,512,256]{3,2,1,0:T(8,128)(2,1)}, u32[]{:S(2)}) copy-start(bf16[3,1,512,256]{3,2,1,0:T(8,128)(2,1)} %param.5) | copy-start | bytes 2359300
  3.7 0.9 %copy-start.2 = (bf16[256,256]{1,0:T(8,128)(2,1)S(1)}, bf16[256,256]{1,0:T(8,128)(2,1)}, u32[]{:S(2)}) copy-start(bf16[256,256]{1,0:T(8,128)(2,1)} %constant.8.clone.forward_ref) | copy-start | bytes 393220
  6.1 13.7 %collective-permute-start.3 = (bf16[384,128]{1,0:T(8,128)(2,1)S(1)}, bf16[384,128]{1,0:T(8,128)(2,1)S(1)}, u32[]{:S(2)}, u32[]{:S(2)}) collective-permute-start(bf16[384,128]{1,0:T(8,128)(2,1)S(1)} %get-tuple-element.21), channel_id=1, source_target_pairs={{0,10},{1,11},{2,8},{3,9},{4,14},{5,15},{6,12},{7,13},{8,2},{9,3},... | collective-permute-start | bytes 294920 | tf_op jit(solution)/shard_map/ppermute | solution.py:194
  11.1 14.2 %collective-permute-start.4 = (bf16[384,128]{1,0:T(8,128)(2,1)S(1)}, bf16[384,128]{1,0:T(8,128)(2,1)S(1)}, u32[]{:S(2)}, u32[]{:S(2)}) collective-permute-start(bf16[384,128]{1,0:T(8,128)(2,1)S(1)} %get-tuple-element.22), channel_id=1, source_target_pairs={{0,2},{1,3},{2,0},{3,1},{4,6},{5,7},{6,4},{7,5},{8,10},{9,11},{10,... | collective-permute-start | bytes 294920 | tf_op jit(solution)/shard_map/ppermute | solution.py:194
  11.6 19.2 %collective-permute-start.2 = (bf16[416,128]{1,0:T(8,128)(2,1)S(1)}, bf16[416,128]{1,0:T(8,128)(2,1)S(1)}, u32[]{:S(2)}, u32[]{:S(2)}) collective-permute-start(bf16[416,128]{1,0:T(8,128)(2,1)S(1)} %get-tuple-element.20), channel_id=1, source_target_pairs={{0,8},{1,9},{2,10},{3,11},{4,12},{5,13},{6,14},{7,15},{8,0},{9,1},... | collective-permute-start | bytes 319496 | tf_op jit(solution)/shard_map/ppermute | solution.py:194
  11.7 13.5 %collective-permute-start.5 = (bf16[384,128]{1,0:T(8,128)(2,1)S(1)}, bf16[384,128]{1,0:T(8,128)(2,1)S(1)}, u32[]{:S(2)}, u32[]{:S(2)}) collective-permute-start(bf16[384,128]{1,0:T(8,128)(2,1)S(1)} %get-tuple-element.23), channel_id=1, source_target_pairs={{0,12},{1,13},{2,14},{3,15},{4,8},{5,9},{6,10},{7,11},{8,4},{9,5},... | collective-permute-start | bytes 294920 | tf_op jit(solution)/shard_map/ppermute | solution.py:194
  15.5 9.8 %collective-permute-start.6 = (bf16[384,128]{1,0:T(8,128)(2,1)S(1)}, bf16[384,128]{1,0:T(8,128)(2,1)S(1)}, u32[]{:S(2)}, u32[]{:S(2)}) collective-permute-start(bf16[384,128]{1,0:T(8,128)(2,1)S(1)} %get-tuple-element.24), channel_id=1, source_target_pairs={{0,4},{1,5},{2,6},{3,7},{4,0},{5,1},{6,2},{7,3},{8,12},{9,13},{10,... | collective-permute-start | bytes 294920 | tf_op jit(solution)/shard_map/ppermute | solution.py:194
  19.9 9.1 %collective-permute-start.7 = (bf16[384,128]{1,0:T(8,128)(2,1)S(1)}, bf16[384,128]{1,0:T(8,128)(2,1)S(1)}, u32[]{:S(2)}, u32[]{:S(2)}) collective-permute-start(bf16[384,128]{1,0:T(8,128)(2,1)S(1)} %get-tuple-element.25), channel_id=1, source_target_pairs={{0,14},{1,15},{2,12},{3,13},{4,10},{5,11},{6,8},{7,9},{8,6},{9,7},... | collective-permute-start | bytes 294920 | tf_op jit(solution)/shard_map/ppermute | solution.py:194
  25.3 5.5 %copy-start.4 = (s32[16]{0:T(128)S(1)}, s32[16]{0:T(128)}, u32[]{:S(2)}) copy-start(s32[16]{0:T(128)} %counts_ref.3) | copy-start | bytes 196
  25.3 5.5 %collective-permute-start.8 = (bf16[384,128]{1,0:T(8,128)(2,1)S(1)}, bf16[384,128]{1,0:T(8,128)(2,1)S(1)}, u32[]{:S(2)}, u32[]{:S(2)}) collective-permute-start(bf16[384,128]{1,0:T(8,128)(2,1)S(1)} %get-tuple-element.26), channel_id=1, source_target_pairs={{0,6},{1,7},{2,4},{3,5},{4,2},{5,3},{6,0},{7,1},{8,14},{9,15},{10,... | collective-permute-start | bytes 294920 | tf_op jit(solution)/shard_map/ppermute | solution.py:194
  36.0 11.9 %collective-permute-start.9 = (bf16[512,128]{1,0:T(8,128)(2,1)S(1)}, bf16[512,128]{1,0:T(8,128)(2,1)S(1)}, u32[]{:S(2)}, u32[]{:S(2)}) collective-permute-start(bf16[512,128]{1,0:T(8,128)(2,1)S(1)} %get-tuple-element.29), channel_id=1, source_target_pairs={{0,8},{1,9},{2,10},{3,11},{4,12},{5,13},{6,14},{7,15},{8,0},{9,1},... | collective-permute-start | bytes 393224 | tf_op jit(solution)/shard_map/ppermute | solution.py:194
  37.2 11.2 %collective-permute-start.10 = (bf16[512,128]{1,0:T(8,128)(2,1)S(1)}, bf16[512,128]{1,0:T(8,128)(2,1)S(1)}, u32[]{:S(2)}, u32[]{:S(2)}) collective-permute-start(bf16[512,128]{1,0:T(8,128)(2,1)S(1)} %get-tuple-element.30), channel_id=1, source_target_pairs={{0,9},{1,8},{2,11},{3,10},{4,13},{5,12},{6,15},{7,14},{8,1},{9,0},... | collective-permute-start | bytes 393224 | tf_op jit(solution)/shard_map/ppermute | solution.py:194
  37.2 11.2 %copy-start.1 = (f32[256,256]{1,0:T(8,128)S(1)}, f32[256,256]{1,0:T(8,128)}, u32[]{:S(2)}) copy-start(f32[256,256]{1,0:T(8,128)} %constant.9.clone.inverse_ref) | copy-start | bytes 786436
  39.5 2.9 %collective-permute-start.11 = (bf16[256,128]{1,0:T(8,128)(2,1)S(1)}, bf16[256,128]{1,0:T(8,128)(2,1)S(1)}, u32[]{:S(2)}, u32[]{:S(2)}) collective-permute-start(bf16[256,128]{1,0:T(8,128)(2,1)S(1)} %get-tuple-element.31), channel_id=1, source_target_pairs={{0,1},{1,0},{2,3},{3,2},{4,5},{5,4},{6,7},{7,6},{8,9},{9,8},{10,11... | collective-permute-start | bytes 196616 | tf_op jit(solution)/shard_map/ppermute | solution.py:194
  41.4 1.3 %collective-permute-start.12 = (bf16[256,128]{1,0:T(8,128)(2,1)S(1)}, bf16[256,128]{1,0:T(8,128)(2,1)S(1)}, u32[]{:S(2)}, u32[]{:S(2)}) collective-permute-start(bf16[256,128]{1,0:T(8,128)(2,1)S(1)} %get-tuple-element.32), channel_id=1, source_target_pairs={{0,1},{1,0},{2,3},{3,2},{4,5},{5,4},{6,7},{7,6},{8,9},{9,8},{10,11... | collective-permute-start | bytes 196616 | tf_op jit(solution)/shard_map/ppermute | solution.py:194

commit v4 on v3

--- a/solution.py
+++ b/solution.py
@@ -44,41 +44,72 @@
     return jnp.concatenate([listed[:, at : at + lanes] for at in range(0, listed.shape[1], lanes)])
 
 
-def spectra_kernel(place_ref, own_ref, near_ref, own_pairs_ref, near_pairs_ref, forward_ref, *piece_refs):
-    comps, _, groups, _, samples = own_ref.shape
+def station_spectra(windows_ref, at, table):
+    parts = []
+    for comp in range(windows_ref.shape[0]):
+        low = windows_ref[comp, 0, at]
+        high = windows_ref[comp, 1, at]
+        parts += [low[:SLOTS], high[SLOTS:], low[SLOTS:], high[:SLOTS]]
+    traces = jnp.concatenate(parts)
+    square = jnp.square(traces.astype(jnp.float32))
+    square_hi = square.astype(jnp.bfloat16)
+    square_lo = (square - square_hi.astype(jnp.float32)).astype(jnp.bfloat16)
+    ones = jnp.ones((16, traces.shape[1]), jnp.bfloat16)
+    energy = lax.dot_general(ones, square_hi, NT, preferred_element_type=jnp.float32)
+    energy += lax.dot_general(ones, square_lo, NT, preferred_element_type=jnp.float32)
+    scale = lax.rsqrt(energy[:1] + EPSILON)
+    raw = lax.dot_general(table, traces, NT, preferred_element_type=jnp.float32)
+    return (raw * scale).astype(jnp.bfloat16)
+
+
+def own_kernel(place_ref, windows_ref, forward_ref, spectra_ref, table_ref, held_ref, whole_ref, sems):
+    comps, _, groups, _, _ = windows_ref.shape
     rows = forward_ref.shape[0] // 4
     lanes = 4 * SLOTS
     quarter, group = place_of(place_ref, groups)
-    table = jnp.concatenate(
-        [forward_ref[pl.ds(pl.multiple_of((quarter ^ m) * rows, rows), rows), :] for m in (0, 2)]
-    )
-    ones = jnp.ones((16, samples), jnp.bfloat16)
+    copies = [pltpu.make_async_copy(forward_ref, whole_ref, sems.at[groups])]
+    for mg in range(groups):
+        copies.append(
+            pltpu.make_async_copy(windows_ref.at[:, :, group ^ mg], held_ref.at[:, :, mg], sems.at[mg])
+        )
+    for copy in copies:
+        copy.start()
+    copies[0].wait()
+    for far in range(2):
+        start = pl.multiple_of((quarter ^ (2 * far)) * rows, rows)
+        table_ref[far * rows : (far + 1) * rows] = whole_ref[pl.ds(start, rows), :]
+    table = table_ref[...]
+    for mg in range(groups):
+        copies[1 + mg].wait()
+        spectra = station_spectra(held_ref, mg, table)
+        for far in range(2):
+            for comp in range(comps):
+                spectra_ref[far * groups + mg, comp * rows : (comp + 1) * rows] = spectra[
+                    far * rows : (far + 1) * rows, comp * lanes : (comp + 1) * lanes
+                ]
+
+
+def near_spectra_kernel(
+    place_ref, own_pairs_ref, near_pairs_ref, table_ref, own_ref, windows_ref, *piece_refs
+):
+    comps, _, groups, _, _ = windows_ref.shape
+    rows = table_ref.shape[0] // 2
+    lanes = 4 * SLOTS
+    _, group = place_of(place_ref, groups)
+    table = table_ref[...]
     piece_refs[groups][2 * comps * rows :] = jnp.concatenate(
         [listing_of(own_pairs_ref, lanes), listing_of(near_pairs_ref, lanes)]
     ).astype(jnp.bfloat16)
     for mg in range(groups):
-        for station, windows_ref in enumerate((own_ref, near_ref)):
-            parts = []
+        spectra = station_spectra(windows_ref, group ^ mg, table)
+        for far in range(2):
+            piece = piece_refs[far * groups + mg]
+            piece[: comps * rows] = own_ref[far * groups + mg]
             for comp in range(comps):
-                low = windows_ref[comp, 0, group ^ mg]
-                high = windows_ref[comp, 1, group ^ mg]
-                parts += [low[:SLOTS], high[SLOTS:], low[SLOTS:], high[:SLOTS]]
-            traces = jnp.concatenate(parts)
-            square = jnp.square(traces.astype(jnp.float32))
-            square_hi = square.astype(jnp.bfloat16)
-            square_lo = (square - square_hi.astype(jnp.float32)).astype(jnp.bfloat16)
-            energy = lax.dot_general(ones, square_hi, NT, preferred_element_type=jnp.float32)
-            energy += lax.dot_general(ones, square_lo, NT, preferred_element_type=jnp.float32)
-            scale = lax.rsqrt(energy[:1] + EPSILON)
-            raw = lax.dot_general(table, traces, NT, preferred_element_type=jnp.float32)
-            spectra = (raw * scale).astype(jnp.bfloat16)
-            for far in range(2):
-                piece = piece_refs[far * groups + mg]
-                for comp in range(comps):
-                    start = (station * comps + comp) * rows
-                    piece[start : start + rows] = spectra[
-                        far * rows : (far + 1) * rows, comp * lanes : (comp + 1) * lanes
-                    ]
+                start = (comps + comp) * rows
+                piece[start : start + rows] = spectra[
+                    far * rows : (far + 1) * rows, comp * lanes : (comp + 1) * lanes
+                ]
 
 
 def pick(place_ref, counts_ref, listed, flat_ref, mq, *picked_refs):
@@ -123,7 +154,7 @@
     piece_refs, (flat_ref, picked_0, picked_1, trace_ref, cross_ref) = refs[:-5], refs[-5:]
     rows = flat_ref.shape[3]
     bins = rows // 2
-    each, lanes = piece_refs[0].shape
+    each, lanes = piece_refs[1].shape
     traces = len(piece_refs) * each // rows
     for s, piece in enumerate(piece_refs):
         trace_ref[s * each : (s + 1) * each] = piece[:each].astype(jnp.float32)
@@ -144,7 +175,7 @@
         for far in range(2):
             start = half + far * SLOTS
             flat_ref[own, far, slot * SLOTS : (slot + 1) * SLOTS] = turned[start : start + SLOTS]
-    listed = piece_refs[1][each:].astype(jnp.float32)
+    listed = piece_refs[0][each:].astype(jnp.float32)
     listing = listed.shape[0] // 2
     pick(place_ref, counts_ref, listed[:listing], flat_ref, 2, picked_0)
     pick(place_ref, counts_ref, listed[listing:], flat_ref, 3, picked_1)
@@ -200,8 +231,28 @@
     windows = windows.reshape(comps, 2, groups, 2 * SLOTS, samples)
     near_windows, near_pairs = swap(windows, 1), swap(pairs, 1)
     listing = 2 * pairs.size // lanes
+    hbm = pl.BlockSpec(memory_space=pltpu.HBM)
+    own_spectra, table = pl.pallas_call(
+        own_kernel,
+        out_shape=[
+            jax.ShapeDtypeStruct((2 * groups, comps * rows, lanes), jnp.bfloat16),
+            jax.ShapeDtypeStruct((2 * rows, samples), jnp.bfloat16),
+        ],
+        in_specs=[smem, hbm, hbm],
+        out_specs=[vmem, vmem],
+        scratch_shapes=[
+            pltpu.VMEM(windows.shape, jnp.bfloat16),
+            pltpu.VMEM(forward.shape, jnp.bfloat16),
+            pltpu.SemaphoreType.DMA((groups + 1,)),
+        ],
+        compiler_params=params,
+        cost_estimate=pl.CostEstimate(
+            flops=4 * windows.size * samples, bytes_accessed=4 * windows.size, transcendentals=0
+        ),
+        name="own_spectra",
+    )(place, windows, jnp.asarray(forward))
     pieces = pl.pallas_call(
-        spectra_kernel,
+        near_spectra_kernel,
         out_shape=[
             jax.ShapeDtypeStruct((2 * comps * rows + listing * (m == groups), lanes), jnp.bfloat16)
             for m in range(2 * groups)
@@ -209,11 +260,11 @@
         in_specs=[smem] + [vmem] * 5,
         out_specs=[vmem] * (2 * groups),
         compiler_params=params,
-        name="spectra",
-    )(place, windows, near_windows, pairs, near_pairs, jnp.asarray(forward))
-    order = [m for pair in zip(range(groups, 2 * groups), range(groups)) for m in pair if m]
+        name="near_spectra",
+    )(place, pairs, near_pairs, table, own_spectra, near_windows)
+    order = [*range(1, groups - 1), *range(groups, 2 * groups), groups - 1]
     arrived = {m: swap(pieces[m], 2 * m) for m in order}
-    pieces = [pieces[0]] + [arrived[m] for m in order]
+    pieces = [arrived.pop(groups), pieces[0]] + list(arrived.values())
 
     picked_shape = jax.ShapeDtypeStruct((count, 2 * rows), jnp.bfloat16)
     flat, picked_2, picked_3 = pl.pallas_call(

time: 50.6 us -> 49.1 us (0.970)
  waiting for transfers between devices: 18.8 us -> 17.4 us
  starting transfers between devices: 18.6 us -> 17.5 us
  Pallas kernels: 10.4 us -> 11.4 us
    ppermute x13, waiting for transfers between devices: 18.8 us -> 17.4 us  [swap(): return lax.ppermute(x, 'cell', [(i, i ^ mask) for i in range(cells)])]
    ppermute x13, starting transfers between devices: 18.6 us -> 17.5 us  [swap(): return lax.ppermute(x, 'cell', [(i, i ^ mask) for i in range(cells)])]
    pallas_call x1 -> x2, Pallas kernels: 1.47 us -> 2.54 us  [the longest x1 1.71 us: on_device(): pl.pallas_call(own_kernel, out_shape=[jax.ShapeDtypeStruct((2 * groups, c...]
  transfers between devices with their start and end apart: 13 -> 13, of which waited for: 8 -> 6; matrix products, arithmetic and copies ran while one was open for 0% -> 0% of each run, Pallas kernels for 4% -> 8%
where the time goes in v4:
time: 49.1 us; the launch traced here: 48.5 us
  starting transfers between devices  17.5 us (36%)
  waiting for transfers between devices  17.4 us (35%)
  Pallas kernels  11.4 us (23%)
  local copies, waits for them, and re-layouts  2.05 us (4%)
    ppermute x13, starting transfers between devices, swap(): return lax.ppermute(x, 'cell', [(i, i ^ mask) for i in range(cells)])  17.5 us
    ppermute x13, waiting for transfers between devices, swap(): return lax.ppermute(x, 'cell', [(i, i ^ mask) for i in range(cells)])  17.4 us
    pallas_call x1, Pallas kernels, on_device(): pl.pallas_call(cross_kernel, out_shape=[jax.ShapeDtypeStruct((2, 2, SLOTS...  5.23 us
    pallas_call x1, Pallas kernels, on_device(): pl.pallas_call(near_kernel, out_shape=[picked_shape] + [jax.ShapeDtypeStr...  2.23 us
    unnamed x10, local copies, waits for them, and re-layouts  2.05 us
    pallas_call x1, Pallas kernels, on_device(): pl.pallas_call(own_kernel, out_shape=[jax.ShapeDtypeStruct((2 * groups, c...  1.71 us
    pallas_call x1, Pallas kernels, on_device(): pl.pallas_call(functools.partial(lag_kernel, groups), out_shape=jax.Shape...  1.46 us
  transfers between devices with their start and end apart: 13, of which 6 were waited for; matrix products, arithmetic and copies ran while one was open for 0% of the time, Pallas kernels for 8%

profile of v4, /device:TPU:0, one launch (start us, length us, event | category | flops | bytes accessed | tf_op | source)
XLA Modules:
  0.0 48.5 jit_solution(5306695003742341126)
XLA Ops:
  0.0 0.5 collective-permute-start.1
  0.5 0.1 collective-permute-start
  0.5 0.0 copy-start.3
  0.5 1.1 %copy-done.3 = bf16[3,1,512,256]{3,2,1,0:T(8,128)(2,1)S(1)} copy-done((bf16[3,1,512,256]{3,2,1,0:T(8,128)(2,1)S(1)}, bf16[3,1,512,256]{3,2,1,0:T(8,128)(2,1)}, u32[]{:S(2)}) %copy-start.3) | copy-done | bytes 786456
  1.6 0.0 copy-start.4
  1.6 0.9 %copy-done.4 = bf16[256,256]{1,0:T(8,128)(2,1)S(1)} copy-done((bf16[256,256]{1,0:T(8,128)(2,1)S(1)}, bf16[256,256]{1,0:T(8,128)(2,1)}, u32[]{:S(2)}) %copy-start.4) | copy-done | bytes 131096
  2.5 0.0 copy-start.1
  2.6 1.7 %own_spectra.1 = (bf16[8,192,128]{2,1,0:T(8,128)(2,1)S(1)}, bf16[128,256]{1,0:T(8,128)(2,1)S(1)}) custom-call(s32[1]{0:T(128)} %bitcast.place_ref, bf16[3,2,4,64,256]{4,3,2,1,0:T(8,128)(2,1)S(1)} %bitcast.3, bf16[256,256]{1,0:T(8,128)(2,1)S(1)} %copy-done.4), custom_call_target="tpu_custom_call" | custom-call | flops 402653184 | bytes 1572864 | tf_op jit(solution)/shard_map/own_spectra/pallas_call | solution.py:235
  4.3 0.0 collective-permute-done.near_pairs_ref
  4.3 0.0 collective-permute-done.1.windows_ref
  4.3 0.0 copy-done.1
  4.3 0.8 %near_spectra.1 = (bf16[384,128]{1,0:T(8,128)(2,1)S(1)}, bf16[384,128]{1,0:T(8,128)(2,1)S(1)}, bf16[384,128]{1,0:T(8,128)(2,1)S(1)}, bf16[384,128]{1,0:T(8,128)(...) custom-call(s32[1]{0:T(128)} %bitcast.place_ref, ...), custom_call_target="tpu_custom_call" | custom-call | tf_op jit(solution)/shard_map/near_spectra/pallas_call | solution.py:254
  5.1 3.0 %collective-permute-start.3 = (bf16[384,128]{1,0:T(8,128)(2,1)S(1)}, bf16[384,128]{1,0:T(8,128)(2,1)S(1)}, u32[]{:S(2)}, u32[]{:S(2)}) collective-permute-start(bf16[384,128]{1,0:T(8,128)(2,1)S(1)} %get-tuple-element.25), channel_id=1, source_target_pairs={{0,2},{1,3},{2,0},{3,1},{4,6},{5,7},{6,4},{7,5},{8,10},{9,11},{10,... | collective-permute-start | bytes 294920 | tf_op jit(solution)/shard_map/ppermute | solution.py:225
  8.2 1.6 %collective-permute-start.4 = (bf16[384,128]{1,0:T(8,128)(2,1)S(1)}, bf16[384,128]{1,0:T(8,128)(2,1)S(1)}, u32[]{:S(2)}, u32[]{:S(2)}) collective-permute-start(bf16[384,128]{1,0:T(8,128)(2,1)S(1)} %get-tuple-element.26), channel_id=1, source_target_pairs={{0,4},{1,5},{2,6},{3,7},{4,0},{5,1},{6,2},{7,3},{8,12},{9,13},{10,... | collective-permute-start | bytes 294920 | tf_op jit(solution)/shard_map/ppermute | solution.py:225
  9.7 2.6 %collective-permute-start.2 = (bf16[416,128]{1,0:T(8,128)(2,1)S(1)}, bf16[416,128]{1,0:T(8,128)(2,1)S(1)}, u32[]{:S(2)}, u32[]{:S(2)}) collective-permute-start(bf16[416,128]{1,0:T(8,128)(2,1)S(1)} %get-tuple-element.23), channel_id=1, source_target_pairs={{0,8},{1,9},{2,10},{3,11},{4,12},{5,13},{6,14},{7,15},{8,0},{9,1},... | collective-permute-start | bytes 319496 | tf_op jit(solution)/shard_map/ppermute | solution.py:225
  12.3 0.3 collective-permute-start.5
  12.6 2.5 %collective-permute-start.6 = (bf16[384,128]{1,0:T(8,128)(2,1)S(1)}, bf16[384,128]{1,0:T(8,128)(2,1)S(1)}, u32[]{:S(2)}, u32[]{:S(2)}) collective-permute-start(bf16[384,128]{1,0:T(8,128)(2,1)S(1)} %get-tuple-element.28), channel_id=1, source_target_pairs={{0,12},{1,13},{2,14},{3,15},{4,8},{5,9},{6,10},{7,11},{8,4},{9,5},... | collective-permute-start | bytes 294920 | tf_op jit(solution)/shard_map/ppermute | solution.py:225
  15.1 0.0 collective-permute-done.3.refs_2_
  15.1 2.3 %collective-permute-start.7 = (bf16[384,128]{1,0:T(8,128)(2,1)S(1)}, bf16[384,128]{1,0:T(8,128)(2,1)S(1)}, u32[]{:S(2)}, u32[]{:S(2)}) collective-permute-start(bf16[384,128]{1,0:T(8,128)(2,1)S(1)} %get-tuple-element.29), channel_id=1, source_target_pairs={{0,14},{1,15},{2,12},{3,13},{4,10},{5,11},{6,8},{7,9},{8,6},{9,7},... | collective-permute-start | bytes 294920 | tf_op jit(solution)/shard_map/ppermute | solution.py:225
  17.4 0.0 collective-permute-done.4.refs_3_
  17.4 0.0 copy-start.2
  17.4 0.0 collective-permute-start.8
  17.4 8.5 %collective-permute-done.5.refs_4_ = bf16[384,128]{1,0:T(8,128)(2,1)S(1)} collective-permute-done((bf16[384,128]{1,0:T(8,128)(2,1)S(1)}, bf16[384,128]{1,0:T(8,128)(2,1)S(1)}, u32[]{:S(2)}, u32[]{:S(2)}) %collective-permute-start.5) | collective-permute-done | bytes 98336 | tf_op jit(solution)/shard_map/ppermute | solution.py:225
  25.9 0.0 collective-permute-done.6.refs_5_
  25.9 0.0 collective-permute-done.7.refs_6_
  25.9 1.4 %collective-permute-done.8.refs_7_ = bf16[384,128]{1,0:T(8,128)(2,1)S(1)} collective-permute-done((bf16[384,128]{1,0:T(8,128)(2,1)S(1)}, bf16[384,128]{1,0:T(8,128)(2,1)S(1)}, u32[]{:S(2)}, u32[]{:S(2)}) %collective-permute-start.8) | collective-permute-done | bytes 98336 | tf_op jit(solution)/shard_map/ppermute | solution.py:225
  27.4 0.0 collective-permute-done.2.refs_0_
  27.4 0.0 copy-done.2
  27.4 5.2 %cross.1 = (bf16[2,2,1024,64]{3,2,1,0:T(8,128)(2,1)S(1)}, bf16[512,128]{1,0:T(8,128)(2,1)S(1)}, bf16[512,128]{1,0:T(8,128)(2,1)S(1)}) custom-call(s32[1]{0:T(128)} %bitcast.place_ref, s32[16]{0:T(128)S(1)} %copy-done.2, bf16[416,128]{1,0:T(8,128)(2,1)S(1)} %collective-permute-done.2.refs_0_, bf16[384,128]{1,0:T(8,128)(2,1)S(1)} %get-tuple-element.24.refs_1_, ...), custom_call_target="tpu_custom_call" | custom-call | tf_op jit(solution)/shard_map/cross/pallas_call | solution.py:270
  32.6 4.2 %collective-permute-start.9 = (bf16[512,128]{1,0:T(8,128)(2,1)S(1)}, bf16[512,128]{1,0:T(8,128)(2,1)S(1)}, u32[]{:S(2)}, u32[]{:S(2)}) collective-permute-start(bf16[512,128]{1,0:T(8,128)(2,1)S(1)} %get-tuple-element.33), channel_id=1, source_target_pairs={{0,8},{1,9},{2,10},{3,11},{4,12},{5,13},{6,14},{7,15},{8,0},{9,1},... | collective-permute-start | bytes 393224 | tf_op jit(solution)/shard_map/ppermute | solution.py:225
  36.8 0.0 collective-permute-start.10
  36.8 0.0 copy-start
  36.8 2.2 %near.1 = (bf16[512,128]{1,0:T(8,128)(2,1)S(1)}, bf16[256,128]{1,0:T(8,128)(2,1)S(1)}, bf16[256,128]{1,0:T(8,128)(2,1)S(1)}) custom-call(s32[1]{0:T(128)} %bitcast.place_ref, s32[16]{0:T(128)S(1)} %copy-done.2, s32[2,2,512]{2,1,0:T(2,128)S(1)} %copy-done.1, s32[2,2,512]{2,1,0:T(2,128)S(1)} %collective-permute-done.near_pairs_ref, ...), custom_call_target="tpu_custom_call" | custom-call | flops 4294967296 | bytes 2097152 | tf_op jit(solution)/shard_map/near/pallas_call | solution.py:287
  39.0 0.3 collective-permute-start.11
  39.2 0.3 collective-permute-start.12
  39.6 0.7 %collective-permute-done.11.refs_3_ = bf16[256,128]{1,0:T(8,128)(2,1)S(1)} collective-permute-done((bf16[256,128]{1,0:T(8,128)(2,1)S(1)}, bf16[256,128]{1,0:T(8,128)(2,1)S(1)}, u32[]{:S(2)}, u32[]{:S(2)}) %collective-permute-start.11) | collective-permute-done | bytes 65568 | tf_op jit(solution)/shard_map/ppermute | solution.py:225
  40.3 0.2 collective-permute-done.12.refs_4_
  40.5 5.9 %collective-permute-done.9.refs_1_ = bf16[512,128]{1,0:T(8,128)(2,1)S(1)} collective-permute-done((bf16[512,128]{1,0:T(8,128)(2,1)S(1)}, bf16[512,128]{1,0:T(8,128)(2,1)S(1)}, u32[]{:S(2)}, u32[]{:S(2)}) %collective-permute-start.9) | collective-permute-done | bytes 131104 | tf_op jit(solution)/shard_map/ppermute | solution.py:225
  46.4 0.6 %collective-permute-done.10.refs_2_ = bf16[512,128]{1,0:T(8,128)(2,1)S(1)} collective-permute-done((bf16[512,128]{1,0:T(8,128)(2,1)S(1)}, bf16[512,128]{1,0:T(8,128)(2,1)S(1)}, u32[]{:S(2)}, u32[]{:S(2)}) %collective-permute-start.10) | collective-permute-done | bytes 131104 | tf_op jit(solution)/shard_map/ppermute | solution.py:225
  47.0 0.0 copy-done
  47.0 1.5 %lags.1 = f32[2,512,256]{2,1,0:T(8,128)} custom-call(s32[1]{0:T(128)} %bitcast.place_ref, f32[256,256]{1,0:T(8,128)S(1)} %copy-done, bf16[512,128]{1,0:T(8,128)(2,1)S(1)} %get-tuple-element.32.refs_0_, bf16[512,128]{1,0:T(8,128)(2,1)S(1)} %collective-permute-done.9.refs_1_, bf16[512,128]{1,0:T(8,128)(2,1)S(1)} %collective-permute-done.10.refs_2_, ...), custom_call_target="tpu_custom_call" | custom-call | tf_op jit(solution)/shard_map/lags/pallas_call | solution.py:300
Async XLA Ops:
  0.0 4.3 %collective-permute-start.1 = (bf16[3,2,4,64,256]{4,3,2,1,0:T(8,128)(2,1)}, bf16[3,2,4,64,256]{4,3,2,1,0:T(8,128)(2,1)S(1)}, u32[]{:S(2)}, u32[]{:S(2)}) collective-permute-start(bf16[3,2,4,64,256]{4,3,2,1,0:T(8,128)(2,1)} %bitcast.2), channel_id=1, source_target_pairs={{0,1},{1,0},{2,3},{3,2},{4,5},{5,4},{6,7},{7,6},{8,9},{9,8},{10,11... | collective-permute-start | bytes 2359304 | tf_op jit(solution)/shard_map/ppermute | solution.py:225
  0.5 3.8 %collective-permute-start = (s32[2,2,512]{2,1,0:T(2,128)}, s32[2,2,512]{2,1,0:T(2,128)S(1)}, u32[]{:S(2)}, u32[]{:S(2)}) collective-permute-start(s32[2,2,512]{2,1,0:T(2,128)} %own_pairs_ref.3), channel_id=1, source_target_pairs={{0,1},{1,0},{2,3},{3,2},{4,5},{5,4},{6,7},{7,6},{8,9},{9,8},{10,11... | collective-permute-start | bytes 24584 | tf_op jit(solution)/shard_map/ppermute | solution.py:225
  0.5 1.1 %copy-start.3 = (bf16[3,1,512,256]{3,2,1,0:T(8,128)(2,1)S(1)}, bf16[3,1,512,256]{3,2,1,0:T(8,128)(2,1)}, u32[]{:S(2)}) copy-start(bf16[3,1,512,256]{3,2,1,0:T(8,128)(2,1)} %param.5) | copy-start | bytes 2359300
  1.6 0.9 %copy-start.4 = (bf16[256,256]{1,0:T(8,128)(2,1)S(1)}, bf16[256,256]{1,0:T(8,128)(2,1)}, u32[]{:S(2)}) copy-start(bf16[256,256]{1,0:T(8,128)(2,1)} %constant.8.clone.forward_ref) | copy-start | bytes 393220
  2.5 1.7 %copy-start.1 = (s32[2,2,512]{2,1,0:T(2,128)S(1)}, s32[2,2,512]{2,1,0:T(2,128)}, u32[]{:S(2)}) copy-start(s32[2,2,512]{2,1,0:T(2,128)} %own_pairs_ref.3) | copy-start | bytes 24580
  5.1 10.0 %collective-permute-start.3 = (bf16[384,128]{1,0:T(8,128)(2,1)S(1)}, bf16[384,128]{1,0:T(8,128)(2,1)S(1)}, u32[]{:S(2)}, u32[]{:S(2)}) collective-permute-start(bf16[384,128]{1,0:T(8,128)(2,1)S(1)} %get-tuple-element.25), channel_id=1, source_target_pairs={{0,2},{1,3},{2,0},{3,1},{4,6},{5,7},{6,4},{7,5},{8,10},{9,11},{10,... | collective-permute-start | bytes 294920 | tf_op jit(solution)/shard_map/ppermute | solution.py:225
  8.2 9.2 %collective-permute-start.4 = (bf16[384,128]{1,0:T(8,128)(2,1)S(1)}, bf16[384,128]{1,0:T(8,128)(2,1)S(1)}, u32[]{:S(2)}, u32[]{:S(2)}) collective-permute-start(bf16[384,128]{1,0:T(8,128)(2,1)S(1)} %get-tuple-element.26), channel_id=1, source_target_pairs={{0,4},{1,5},{2,6},{3,7},{4,0},{5,1},{6,2},{7,3},{8,12},{9,13},{10,... | collective-permute-start | bytes 294920 | tf_op jit(solution)/shard_map/ppermute | solution.py:225
  9.7 17.6 %collective-permute-start.2 = (bf16[416,128]{1,0:T(8,128)(2,1)S(1)}, bf16[416,128]{1,0:T(8,128)(2,1)S(1)}, u32[]{:S(2)}, u32[]{:S(2)}) collective-permute-start(bf16[416,128]{1,0:T(8,128)(2,1)S(1)} %get-tuple-element.23), channel_id=1, source_target_pairs={{0,8},{1,9},{2,10},{3,11},{4,12},{5,13},{6,14},{7,15},{8,0},{9,1},... | collective-permute-start | bytes 319496 | tf_op jit(solution)/shard_map/ppermute | solution.py:225
  12.3 13.6 %collective-permute-start.5 = (bf16[384,128]{1,0:T(8,128)(2,1)S(1)}, bf16[384,128]{1,0:T(8,128)(2,1)S(1)}, u32[]{:S(2)}, u32[]{:S(2)}) collective-permute-start(bf16[384,128]{1,0:T(8,128)(2,1)S(1)} %get-tuple-element.27), channel_id=1, source_target_pairs={{0,10},{1,11},{2,8},{3,9},{4,14},{5,15},{6,12},{7,13},{8,2},{9,3},... | collective-permute-start | bytes 294920 | tf_op jit(solution)/shard_map/ppermute | solution.py:225
  12.6 13.3 %collective-permute-start.6 = (bf16[384,128]{1,0:T(8,128)(2,1)S(1)}, bf16[384,128]{1,0:T(8,128)(2,1)S(1)}, u32[]{:S(2)}, u32[]{:S(2)}) collective-permute-start(bf16[384,128]{1,0:T(8,128)(2,1)S(1)} %get-tuple-element.28), channel_id=1, source_target_pairs={{0,12},{1,13},{2,14},{3,15},{4,8},{5,9},{6,10},{7,11},{8,4},{9,5},... | collective-permute-start | bytes 294920 | tf_op jit(solution)/shard_map/ppermute | solution.py:225
  15.1 10.8 %collective-permute-start.7 = (bf16[384,128]{1,0:T(8,128)(2,1)S(1)}, bf16[384,128]{1,0:T(8,128)(2,1)S(1)}, u32[]{:S(2)}, u32[]{:S(2)}) collective-permute-start(bf16[384,128]{1,0:T(8,128)(2,1)S(1)} %get-tuple-element.29), channel_id=1, source_target_pairs={{0,14},{1,15},{2,12},{3,13},{4,10},{5,11},{6,8},{7,9},{8,6},{9,7},... | collective-permute-start | bytes 294920 | tf_op jit(solution)/shard_map/ppermute | solution.py:225
  17.4 10.0 %copy-start.2 = (s32[16]{0:T(128)S(1)}, s32[16]{0:T(128)}, u32[]{:S(2)}) copy-start(s32[16]{0:T(128)} %counts_ref.3) | copy-start | bytes 196
  17.4 9.9 %collective-permute-start.8 = (bf16[384,128]{1,0:T(8,128)(2,1)S(1)}, bf16[384,128]{1,0:T(8,128)(2,1)S(1)}, u32[]{:S(2)}, u32[]{:S(2)}) collective-permute-start(bf16[384,128]{1,0:T(8,128)(2,1)S(1)} %get-tuple-element.30), channel_id=1, source_target_pairs={{0,6},{1,7},{2,4},{3,5},{4,2},{5,3},{6,0},{7,1},{8,14},{9,15},{10,... | collective-permute-start | bytes 294920 | tf_op jit(solution)/shard_map/ppermute | solution.py:225
  32.6 13.8 %collective-permute-start.9 = (bf16[512,128]{1,0:T(8,128)(2,1)S(1)}, bf16[512,128]{1,0:T(8,128)(2,1)S(1)}, u32[]{:S(2)}, u32[]{:S(2)}) collective-permute-start(bf16[512,128]{1,0:T(8,128)(2,1)S(1)} %get-tuple-element.33), channel_id=1, source_target_pairs={{0,8},{1,9},{2,10},{3,11},{4,12},{5,13},{6,14},{7,15},{8,0},{9,1},... | collective-permute-start | bytes 393224 | tf_op jit(solution)/shard_map/ppermute | solution.py:225
  36.8 10.3 %collective-permute-start.10 = (bf16[512,128]{1,0:T(8,128)(2,1)S(1)}, bf16[512,128]{1,0:T(8,128)(2,1)S(1)}, u32[]{:S(2)}, u32[]{:S(2)}) collective-permute-start(bf16[512,128]{1,0:T(8,128)(2,1)S(1)} %get-tuple-element.34), channel_id=1, source_target_pairs={{0,9},{1,8},{2,11},{3,10},{4,13},{5,12},{6,15},{7,14},{8,1},{9,0},... | collective-permute-start | bytes 393224 | tf_op jit(solution)/shard_map/ppermute | solution.py:225
  36.8 10.3 %copy-start = (f32[256,256]{1,0:T(8,128)S(1)}, f32[256,256]{1,0:T(8,128)}, u32[]{:S(2)}) copy-start(f32[256,256]{1,0:T(8,128)} %constant.9.clone.inverse_ref) | copy-start | bytes 786436
  39.0 1.3 %collective-permute-start.11 = (bf16[256,128]{1,0:T(8,128)(2,1)S(1)}, bf16[256,128]{1,0:T(8,128)(2,1)S(1)}, u32[]{:S(2)}, u32[]{:S(2)}) collective-permute-start(bf16[256,128]{1,0:T(8,128)(2,1)S(1)} %get-tuple-element.35), channel_id=1, source_target_pairs={{0,1},{1,0},{2,3},{3,2},{4,5},{5,4},{6,7},{7,6},{8,9},{9,8},{10,11... | collective-permute-start | bytes 196616 | tf_op jit(solution)/shard_map/ppermute | solution.py:225
  39.2 1.3 %collective-permute-start.12 = (bf16[256,128]{1,0:T(8,128)(2,1)S(1)}, bf16[256,128]{1,0:T(8,128)(2,1)S(1)}, u32[]{:S(2)}, u32[]{:S(2)}) collective-permute-start(bf16[256,128]{1,0:T(8,128)(2,1)S(1)} %get-tuple-element.36), channel_id=1, source_target_pairs={{0,1},{1,0},{2,3},{3,2},{4,5},{5,4},{6,7},{7,6},{8,9},{9,8},{10,11... | collective-permute-start | bytes 196616 | tf_op jit(solution)/shard_map/ppermute | solution.py:225

commit v5 on v4

--- a/solution.py
+++ b/solution.py
@@ -40,8 +40,11 @@
 
 
 def listing_of(pairs_ref, lanes):
-    listed = jnp.concatenate([pairs_ref[0], pairs_ref[1]]).astype(jnp.float32)
-    return jnp.concatenate([listed[:, at : at + lanes] for at in range(0, listed.shape[1], lanes)])
+    ends = []
+    for end in range(2):
+        slots = pairs_ref[:, end, :].astype(jnp.float32)
+        ends += [slots[:, at : at + lanes] for at in range(0, slots.shape[1], lanes)]
+    return jnp.concatenate(ends)
 
 
 def station_spectra(windows_ref, at, table):
@@ -62,26 +65,17 @@
     return (raw * scale).astype(jnp.bfloat16)
 
 
-def own_kernel(place_ref, windows_ref, forward_ref, spectra_ref, table_ref, held_ref, whole_ref, sems):
+def own_kernel(place_ref, windows_ref, forward_ref, spectra_ref, table_ref):
     comps, _, groups, _, _ = windows_ref.shape
     rows = forward_ref.shape[0] // 4
     lanes = 4 * SLOTS
     quarter, group = place_of(place_ref, groups)
-    copies = [pltpu.make_async_copy(forward_ref, whole_ref, sems.at[groups])]
-    for mg in range(groups):
-        copies.append(
-            pltpu.make_async_copy(windows_ref.at[:, :, group ^ mg], held_ref.at[:, :, mg], sems.at[mg])
-        )
-    for copy in copies:
-        copy.start()
-    copies[0].wait()
     for far in range(2):
         start = pl.multiple_of((quarter ^ (2 * far)) * rows, rows)
-        table_ref[far * rows : (far + 1) * rows] = whole_ref[pl.ds(start, rows), :]
+        table_ref[far * rows : (far + 1) * rows] = forward_ref[pl.ds(start, rows), :]
     table = table_ref[...]
     for mg in range(groups):
-        copies[1 + mg].wait()
-        spectra = station_spectra(held_ref, mg, table)
+        spectra = station_spectra(windows_ref, group ^ mg, table)
         for far in range(2):
             for comp in range(comps):
                 spectra_ref[far * groups + mg, comp * rows : (comp + 1) * rows] = spectra[
@@ -119,63 +113,114 @@
     high, low = own // 2, own % 2
     cell = high * (cells // 2) + group * 2 + low
     lanes = listed.shape[1]
-    turned = listed.T
+    count = listed.shape[0] // 2
+    first, second = listed[:count].astype(jnp.int32), listed[count:].astype(jnp.int32)
+    far_counts = [counts_ref[cell ^ 1], counts_ref[cell ^ (cells // 2)]]
+    odd = lax.broadcasted_iota(jnp.int32, (count, lanes), 0) % 2
+    live = (first < counts_ref[cell]) & (second < jnp.where(odd == 1, far_counts[1], far_counts[0]))
+    left, right = jnp.where(high == low, first, second), jnp.where(high == low, second, first)
+    spot = jnp.where(live, (left // 4) * SLOTS + right, -1)
+    turned = jnp.concatenate([spot, left % 4]).T
     lane = lax.broadcasted_iota(jnp.int32, (lanes, lanes), 1)
+    run = lane // SLOTS
+    spread = lax.broadcasted_iota(jnp.int32, (2 * lanes, lanes), 0)
+    kept = lax.broadcasted_iota(jnp.int32, (2 * lanes, lanes), 1)
     sides = ((high, high), (low, 1 - low))
     found = []
+    folds = []
     for step_round in range(2):
-        own_count = counts_ref[cell].astype(jnp.float32)
-        far_count = counts_ref[cell ^ (cells // 2 if step_round else 1)].astype(jnp.float32)
         hot = []
-        for chunk in range(listed.shape[0] // 4):
-            at = chunk * 4 + step_round * 2
-            first, second = turned[:, at : at + 1], turned[:, at + 1 : at + 2]
-            live = (first < own_count) & (second < far_count)
-            place = jnp.where(high == low, first * SLOTS + second, second * SLOTS + first)
-            offset = jnp.where(live, place, -1.0).astype(jnp.int32) - lane
+        for at in range(step_round, count, 2):
+            offset = turned[:, at : at + 1] - lane
             hot.append(
                 jnp.concatenate(
+                    [jnp.where(offset == start, 1.0, 0.0).astype(jnp.bfloat16) for start in (0, lanes)],
+                    axis=1,
+                )
+            )
+        block = flat_ref[sides[step_round][0], sides[step_round][1]]
+        wide = jnp.dot(jnp.concatenate(hot), block, preferred_element_type=jnp.float32)
+        masked = []
+        for chunk, at in enumerate(range(step_round, count, 2)):
+            here = run == turned[:, count + at : count + at + 1]
+            part = wide[chunk * lanes : (chunk + 1) * lanes]
+            masked.append(
+                jnp.concatenate(
                     [
-                        jnp.where(offset == lanes * t, 1.0, 0.0).astype(jnp.bfloat16)
-                        for t in range(SLOTS * SLOTS // lanes)
+                        jnp.where(here, part[:, :lanes], 0.0).astype(jnp.bfloat16),
+                        jnp.where(here, part[:, lanes:], 0.0).astype(jnp.bfloat16),
                     ],
                     axis=1,
                 )
             )
-        block = flat_ref[sides[step_round][0], sides[step_round][1]]
-        found.append(jnp.dot(jnp.concatenate(hot), block, preferred_element_type=jnp.float32))
-    found = jnp.concatenate(found, axis=1).astype(jnp.bfloat16)
-    each = found.shape[0] // len(picked_refs)
+        found.append(jnp.concatenate(masked))
+        place = (step_round * 2 + spread // lanes) * SLOTS + spread % SLOTS
+        folds.append(jnp.where(kept == place, 1.0, 0.0).astype(jnp.bfloat16))
+    picked = jnp.dot(
+        jnp.concatenate(found, axis=1),
+        jnp.concatenate(folds),
+        preferred_element_type=jnp.float32,
+    ).astype(jnp.bfloat16)
+    each = picked.shape[0] // len(picked_refs)
     for at, ref in enumerate(picked_refs):
-        ref[...] = found[at * each : (at + 1) * each]
-
-
-def cross_kernel(place_ref, counts_ref, *refs):
-    piece_refs, (flat_ref, picked_0, picked_1, trace_ref, cross_ref) = refs[:-5], refs[-5:]
-    rows = flat_ref.shape[3]
+        ref[...] = picked[at * each : (at + 1) * each]
+
+
+def padded(traces):
+    return -(-traces // 16) * 16
+
+
+def add_cross(piece_refs, trace_ref, rows, sums_ref, before_ref=None):
     bins = rows // 2
-    each, lanes = piece_refs[1].shape
-    traces = len(piece_refs) * each // rows
-    for s, piece in enumerate(piece_refs):
-        trace_ref[s * each : (s + 1) * each] = piece[:each].astype(jnp.float32)
-    half = 2 * SLOTS
+    slots, lanes = 2 * SLOTS, 4 * SLOTS
+    traces = trace_ref.shape[0] // rows
+    each = traces * rows
+    start = 0
+    for piece in piece_refs:
+        held = piece.shape[0] // rows * rows
+        trace_ref[start : start + held] = piece[:held].astype(jnp.float32)
+        start += held
+    if start < each:
+        trace_ref[start:] = jnp.zeros((each - start, lanes), jnp.float32)
     for k in range(bins):
         real = trace_ref[pl.ds(k, traces, stride=rows), :].astype(jnp.bfloat16)
         imag = trace_ref[pl.ds(bins + k, traces, stride=rows), :].astype(jnp.bfloat16)
-        left = jnp.concatenate([real, imag], axis=0)
+        left = jnp.concatenate([real, imag], axis=0)[:, :slots]
         right = jnp.concatenate(
             [jnp.concatenate([real, imag], axis=1), jnp.concatenate([imag, -real], axis=1)], axis=0
         )
         cross = lax.dot_general(left, right, TN, preferred_element_type=jnp.float32)
-        cross_ref[k * half : (k + 1) * half] = cross[:half, :lanes]
-        cross_ref[(bins + k) * half : (bins + k + 1) * half] = cross[:half, lanes:]
-    for i in range(half):
-        turned = cross_ref[pl.ds(i, rows, stride=half), :].T.astype(jnp.bfloat16)
-        own, slot = i // SLOTS, i % SLOTS
-        for far in range(2):
-            start = half + far * SLOTS
-            flat_ref[own, far, slot * SLOTS : (slot + 1) * SLOTS] = turned[start : start + SLOTS]
-    listed = piece_refs[0][each:].astype(jnp.float32)
+        for part in range(2):
+            at = (part * bins + k) * slots
+            value = cross[:, part * lanes : (part + 1) * lanes]
+            if before_ref is not None:
+                value += before_ref[at : at + slots]
+            sums_ref[at : at + slots] = value
+
+
+def early_kernel(*refs):
+    piece_refs, (sums_ref, trace_ref) = refs[:-2], refs[-2:]
+    add_cross(piece_refs, trace_ref, sums_ref.shape[0] // (2 * SLOTS), sums_ref)
+
+
+def cross_kernel(place_ref, counts_ref, listed_ref, before_ref, *refs):
+    piece_refs, (flat_ref, picked_0, picked_1, trace_ref, cross_ref) = refs[:-5], refs[-5:]
+    slots, lanes = 2 * SLOTS, 4 * SLOTS
+    rows = before_ref.shape[0] // slots
+    bins = rows // 2
+    add_cross(piece_refs, trace_ref, rows, cross_ref, before_ref)
+    for own in range(2):
+        for four in range(SLOTS // 4):
+            for part in range(2):
+                first = part * bins * slots + own * SLOTS + four * 4
+                block = jnp.concatenate(
+                    [cross_ref[pl.ds(first + i, bins, stride=slots), :] for i in range(4)]
+                ).T.astype(jnp.bfloat16)
+                for far in range(2):
+                    flat_ref[
+                        own, far, four * SLOTS : (four + 1) * SLOTS, part * lanes : (part + 1) * lanes
+                    ] = block[slots + far * SLOTS : slots + (far + 1) * SLOTS]
+    listed = listed_ref[listed_ref.shape[0] // rows * rows :].astype(jnp.float32)
     listing = listed.shape[0] // 2
     pick(place_ref, counts_ref, listed[:listing], flat_ref, 2, picked_0)
     pick(place_ref, counts_ref, listed[listing:], flat_ref, 3, picked_1)
@@ -231,20 +276,14 @@
     windows = windows.reshape(comps, 2, groups, 2 * SLOTS, samples)
     near_windows, near_pairs = swap(windows, 1), swap(pairs, 1)
     listing = 2 * pairs.size // lanes
-    hbm = pl.BlockSpec(memory_space=pltpu.HBM)
     own_spectra, table = pl.pallas_call(
         own_kernel,
         out_shape=[
             jax.ShapeDtypeStruct((2 * groups, comps * rows, lanes), jnp.bfloat16),
             jax.ShapeDtypeStruct((2 * rows, samples), jnp.bfloat16),
         ],
-        in_specs=[smem, hbm, hbm],
+        in_specs=[smem, vmem, vmem],
         out_specs=[vmem, vmem],
-        scratch_shapes=[
-            pltpu.VMEM(windows.shape, jnp.bfloat16),
-            pltpu.VMEM(forward.shape, jnp.bfloat16),
-            pltpu.SemaphoreType.DMA((groups + 1,)),
-        ],
         compiler_params=params,
         cost_estimate=pl.CostEstimate(
             flops=4 * windows.size * samples, bytes_accessed=4 * windows.size, transcendentals=0
@@ -264,25 +303,36 @@
     )(place, pairs, near_pairs, table, own_spectra, near_windows)
     order = [*range(1, groups - 1), *range(groups, 2 * groups), groups - 1]
     arrived = {m: swap(pieces[m], 2 * m) for m in order}
-    pieces = [arrived.pop(groups), pieces[0]] + list(arrived.values())
-
+    late = [2 * groups - 2, 2 * groups - 1]
+    early = [pieces[0]] + [arrived[m] for m in order if m not in late]
+
+    sums = pl.pallas_call(
+        early_kernel,
+        out_shape=jax.ShapeDtypeStruct((2 * SLOTS * rows, lanes), jnp.float32),
+        in_specs=[vmem] * len(early),
+        out_specs=vmem,
+        scratch_shapes=[pltpu.VMEM((padded(len(early) * 2 * comps) * rows, lanes), jnp.float32)],
+        compiler_params=params,
+        cost_estimate=pl.CostEstimate(flops=2**31, bytes_accessed=2**22, transcendentals=0),
+        name="early",
+    )(*early)
     picked_shape = jax.ShapeDtypeStruct((count, 2 * rows), jnp.bfloat16)
     flat, picked_2, picked_3 = pl.pallas_call(
         cross_kernel,
         out_shape=[
-            jax.ShapeDtypeStruct((2, 2, SLOTS * SLOTS, rows), jnp.bfloat16),
+            jax.ShapeDtypeStruct((2, 2, SLOTS * SLOTS // 4, 2 * lanes), jnp.bfloat16),
             picked_shape,
             picked_shape,
         ],
-        in_specs=[smem, smem] + [vmem] * (2 * groups),
+        in_specs=[smem, smem] + [vmem] * (2 + len(late)),
         out_specs=[vmem] * 3,
         scratch_shapes=[
-            pltpu.VMEM((comps * cells * rows, lanes), jnp.float32),
-            pltpu.VMEM((rows * 2 * SLOTS, lanes), jnp.float32),
+            pltpu.VMEM((padded(len(late) * 2 * comps) * rows, lanes), jnp.float32),
+            pltpu.VMEM((2 * SLOTS * rows, lanes), jnp.float32),
         ],
         compiler_params=params,
         name="cross",
-    )(place, counts, *pieces)
+    )(place, counts, arrived[groups], sums, *[arrived[m] for m in late])
     picked_2, picked_3 = swap(picked_2, half), swap(picked_3, half + 1)
     picked_0, *picked_1 = pl.pallas_call(
         near_kernel,

time: 49.1 us -> 47.4 us (0.965)
  waiting for transfers between devices: 17.4 us -> 15.1 us
  starting transfers between devices: 17.5 us -> 19.7 us
  Pallas kernels: 11.4 us -> 9.52 us
  local copies, waits for them, and re-layouts: 2.05 us -> 2.74 us
    ppermute x13, waiting for transfers between devices: 17.4 us -> 15.1 us  [swap(): return lax.ppermute(x, 'cell', [(i, i ^ mask) for i in range(cells)])]
    ppermute x13, starting transfers between devices: 17.5 us -> 19.7 us  [swap(): return lax.ppermute(x, 'cell', [(i, i ^ mask) for i in range(cells)])]
    pallas_call x1, Pallas kernels: 5.23 us -> 3.47 us  [on_device(): pl.pallas_call(cross_kernel, out_shape=[jax.ShapeDtypeStruct((2, 2, SLOTS...]
    pallas_call x0 -> x1, Pallas kernels: none -> 1.34 us  [on_device(): pl.pallas_call(early_kernel, out_shape=jax.ShapeDtypeStruct((2 * SLOTS *...]
    pallas_call x1, Pallas kernels: 1.71 us -> 0.81 us  [on_device(): pl.pallas_call(own_kernel, out_shape=[jax.ShapeDtypeStruct((2 * groups, c...]
    unnamed x10 -> x12, local copies, waits for them, and re-layouts: 2.05 us -> 2.74 us
    pallas_call x1, Pallas kernels: 2.23 us -> 1.62 us  [on_device(): pl.pallas_call(near_kernel, out_shape=[picked_shape] + [jax.ShapeDtypeStr...]
where the time goes in v5:
time: 47.4 us; the launch traced here: 47.2 us
  starting transfers between devices  19.7 us (42%)
  waiting for transfers between devices  15.1 us (32%)
  Pallas kernels  9.52 us (20%)
  local copies, waits for them, and re-layouts  2.74 us (6%)
    ppermute x13, starting transfers between devices, swap(): return lax.ppermute(x, 'cell', [(i, i ^ mask) for i in range(cells)])  19.7 us
    ppermute x13, waiting for transfers between devices, swap(): return lax.ppermute(x, 'cell', [(i, i ^ mask) for i in range(cells)])  15.1 us
    pallas_call x1, Pallas kernels, on_device(): pl.pallas_call(cross_kernel, out_shape=[jax.ShapeDtypeStruct((2, 2, SLOTS...  3.47 us
    unnamed x12, local copies, waits for them, and re-layouts  2.74 us
    pallas_call x1, Pallas kernels, on_device(): pl.pallas_call(near_kernel, out_shape=[picked_shape] + [jax.ShapeDtypeStr...  1.62 us
    pallas_call x1, Pallas kernels, on_device(): pl.pallas_call(functools.partial(lag_kernel, groups), out_shape=jax.Shape...  1.46 us
    pallas_call x1, Pallas kernels, on_device(): pl.pallas_call(early_kernel, out_shape=jax.ShapeDtypeStruct((2 * SLOTS *...  1.34 us
  transfers between devices with their start and end apart: 13, of which 6 were waited for; matrix products, arithmetic and copies ran while one was open for 0% of the time, Pallas kernels for 8%

profile of v5, /device:TPU:0, one launch (start us, length us, event | category | flops | bytes accessed | tf_op | source)
XLA Modules:
  0.0 47.2 jit_solution(12098378170970997308)
XLA Ops:
  0.0 0.5 collective-permute-start.1
  0.5 0.1 collective-permute-start
  0.5 0.0 copy-start.4
  0.5 1.1 %copy-done.4 = bf16[3,1,512,256]{3,2,1,0:T(8,128)(2,1)S(1)} copy-done((bf16[3,1,512,256]{3,2,1,0:T(8,128)(2,1)S(1)}, bf16[3,1,512,256]{3,2,1,0:T(8,128)(2,1)}, u32[]{:S(2)}) %copy-start.4) | copy-done | bytes 786456
  1.6 0.0 copy-start.5
  1.6 0.9 %copy-done.5 = bf16[256,256]{1,0:T(8,128)(2,1)S(1)} copy-done((bf16[256,256]{1,0:T(8,128)(2,1)S(1)}, bf16[256,256]{1,0:T(8,128)(2,1)}, u32[]{:S(2)}) %copy-start.5) | copy-done | bytes 131096
  2.5 0.8 %own_spectra.1 = (bf16[8,192,128]{2,1,0:T(8,128)(2,1)S(1)}, bf16[128,256]{1,0:T(8,128)(2,1)S(1)}) custom-call(s32[1]{0:T(128)} %bitcast.place_ref, bf16[3,2,4,64,256]{4,3,2,1,0:T(8,128)(2,1)S(1)} %bitcast.3, bf16[256,256]{1,0:T(8,128)(2,1)S(1)} %copy-done.5), custom_call_target="tpu_custom_call" | custom-call | flops 402653184 | bytes 1572864 | tf_op jit(solution)/shard_map/own_spectra/pallas_call | solution.py:279
  3.4 0.0 collective-permute-done.near_pairs_ref
  3.4 0.0 collective-permute-done.1.windows_ref
  3.4 0.0 copy-start.1
  3.4 0.7 %copy-done.1 = s32[2,2,512]{2,1,0:T(2,128)S(1)} copy-done((s32[2,2,512]{2,1,0:T(2,128)S(1)}, s32[2,2,512]{2,1,0:T(2,128)}, u32[]{:S(2)}) %copy-start.1) | copy-done | bytes 8216
  4.1 0.8 %near_spectra.1 = (bf16[384,128]{1,0:T(8,128)(2,1)S(1)}, bf16[384,128]{1,0:T(8,128)(2,1)S(1)}, bf16[384,128]{1,0:T(8,128)(2,1)S(1)}, bf16[384,128]{1,0:T(8,128)(...) custom-call(s32[1]{0:T(128)} %bitcast.place_ref, ...), custom_call_target="tpu_custom_call" | custom-call | tf_op jit(solution)/shard_map/near_spectra/pallas_call | solution.py:293
  4.9 4.1 %collective-permute-start.2 = (bf16[416,128]{1,0:T(8,128)(2,1)S(1)}, bf16[416,128]{1,0:T(8,128)(2,1)S(1)}, u32[]{:S(2)}, u32[]{:S(2)}) collective-permute-start(bf16[416,128]{1,0:T(8,128)(2,1)S(1)} %get-tuple-element.23), channel_id=1, source_target_pairs={{0,8},{1,9},{2,10},{3,11},{4,12},{5,13},{6,14},{7,15},{8,0},{9,1},... | collective-permute-start | bytes 319496 | tf_op jit(solution)/shard_map/ppermute | solution.py:270
  9.0 1.5 %collective-permute-start.3 = (bf16[384,128]{1,0:T(8,128)(2,1)S(1)}, bf16[384,128]{1,0:T(8,128)(2,1)S(1)}, u32[]{:S(2)}, u32[]{:S(2)}) collective-permute-start(bf16[384,128]{1,0:T(8,128)(2,1)S(1)} %get-tuple-element.25), channel_id=1, source_target_pairs={{0,2},{1,3},{2,0},{3,1},{4,6},{5,7},{6,4},{7,5},{8,10},{9,11},{10,... | collective-permute-start | bytes 294920 | tf_op jit(solution)/shard_map/ppermute | solution.py:270
  10.5 1.6 %collective-permute-start.4 = (bf16[384,128]{1,0:T(8,128)(2,1)S(1)}, bf16[384,128]{1,0:T(8,128)(2,1)S(1)}, u32[]{:S(2)}, u32[]{:S(2)}) collective-permute-start(bf16[384,128]{1,0:T(8,128)(2,1)S(1)} %get-tuple-element.26), channel_id=1, source_target_pairs={{0,4},{1,5},{2,6},{3,7},{4,0},{5,1},{6,2},{7,3},{8,12},{9,13},{10,... | collective-permute-start | bytes 294920 | tf_op jit(solution)/shard_map/ppermute | solution.py:270
  12.1 0.3 collective-permute-start.5
  12.4 1.4 %collective-permute-start.6 = (bf16[384,128]{1,0:T(8,128)(2,1)S(1)}, bf16[384,128]{1,0:T(8,128)(2,1)S(1)}, u32[]{:S(2)}, u32[]{:S(2)}) collective-permute-start(bf16[384,128]{1,0:T(8,128)(2,1)S(1)} %get-tuple-element.28), channel_id=1, source_target_pairs={{0,6},{1,7},{2,4},{3,5},{4,2},{5,3},{6,0},{7,1},{8,14},{9,15},{10,... | collective-permute-start | bytes 294920 | tf_op jit(solution)/shard_map/ppermute | solution.py:270
  13.8 0.0 collective-permute-done.3.refs_1_
  13.8 3.6 %collective-permute-start.7 = (bf16[384,128]{1,0:T(8,128)(2,1)S(1)}, bf16[384,128]{1,0:T(8,128)(2,1)S(1)}, u32[]{:S(2)}, u32[]{:S(2)}) collective-permute-start(bf16[384,128]{1,0:T(8,128)(2,1)S(1)} %get-tuple-element.29), channel_id=1, source_target_pairs={{0,12},{1,13},{2,14},{3,15},{4,8},{5,9},{6,10},{7,11},{8,4},{9,5},... | collective-permute-start | bytes 294920 | tf_op jit(solution)/shard_map/ppermute | solution.py:270
  17.4 0.3 collective-permute-done.4.refs_2_
  17.7 0.7 %collective-permute-start.8 = (bf16[384,128]{1,0:T(8,128)(2,1)S(1)}, bf16[384,128]{1,0:T(8,128)(2,1)S(1)}, u32[]{:S(2)}, u32[]{:S(2)}) collective-permute-start(bf16[384,128]{1,0:T(8,128)(2,1)S(1)} %get-tuple-element.30), channel_id=1, source_target_pairs={{0,14},{1,15},{2,12},{3,13},{4,10},{5,11},{6,8},{7,9},{8,6},{9,7},... | collective-permute-start | bytes 294920 | tf_op jit(solution)/shard_map/ppermute | solution.py:270
  18.4 5.4 %collective-permute-done.5.refs_4_ = bf16[384,128]{1,0:T(8,128)(2,1)S(1)} collective-permute-done((bf16[384,128]{1,0:T(8,128)(2,1)S(1)}, bf16[384,128]{1,0:T(8,128)(2,1)S(1)}, u32[]{:S(2)}, u32[]{:S(2)}) %collective-permute-start.5) | collective-permute-done | bytes 98336 | tf_op jit(solution)/shard_map/ppermute | solution.py:270
  23.9 0.0 collective-permute-done.6.refs_5_
  23.9 0.0 collective-permute-done.2.refs_3_.listed_ref
  23.9 0.0 copy-start.3
  23.9 1.3 %early.1.before_ref = f32[4096,128]{1,0:T(8,128)S(1)} custom-call(bf16[384,128]{1,0:T(8,128)(2,1)S(1)} %get-tuple-element.24.refs_0_, bf16[384,128]{1,0:T(8,128)(2,1)S(1)} %collective-permute-done.3.refs_1_, bf16[384,128]{1,0:T(8,128)(2,1)S(1)} %collective-permute-done.4.refs_2_, bf16[416,128]{1,0:T(8,128)(2,1)S(1)} %collective-permute-done.2.refs_3_.listed_ref, ...), custom_call_target="tpu_custom_call" | custom-call | flops 2147483648 | bytes 4194304 | tf_op jit(solution)/shard_map/early/pallas_call | solution.py:309
  25.2 0.0 copy-start.2
  25.2 0.0 collective-permute-done.7.refs_0_
  25.2 0.0 collective-permute-done.8.refs_1_
  25.2 0.0 copy-done.3
  25.2 3.5 %cross.1 = (bf16[2,2,256,256]{3,2,1,0:T(8,128)(2,1)S(1)}, bf16[512,128]{1,0:T(8,128)(2,1)S(1)}, bf16[512,128]{1,0:T(8,128)(2,1)S(1)}) custom-call(s32[1]{0:T(128)} %bitcast.place_ref, s32[16]{0:T(128)S(1)} %copy-done.3, bf16[416,128]{1,0:T(8,128)(2,1)S(1)} %collective-permute-done.2.refs_3_.listed_ref, f32[4096,128]{1,0:T(8,128)S(1)} %early.1.before_ref, ...), custom_call_target="tpu_custom_call" | custom-call | tf_op jit(solution)/shard_map/cross/pallas_call | solution.py:320
  28.7 5.5 %collective-permute-start.9 = (bf16[512,128]{1,0:T(8,128)(2,1)S(1)}, bf16[512,128]{1,0:T(8,128)(2,1)S(1)}, u32[]{:S(2)}, u32[]{:S(2)}) collective-permute-start(bf16[512,128]{1,0:T(8,128)(2,1)S(1)} %get-tuple-element.33), channel_id=1, source_target_pairs={{0,8},{1,9},{2,10},{3,11},{4,12},{5,13},{6,14},{7,15},{8,0},{9,1},... | collective-permute-start | bytes 393224 | tf_op jit(solution)/shard_map/ppermute | solution.py:270
  34.2 0.0 collective-permute-start.10
  34.2 0.0 copy-done.2
  34.2 0.0 copy-start
  34.2 1.6 %near.1 = (bf16[512,128]{1,0:T(8,128)(2,1)S(1)}, bf16[256,128]{1,0:T(8,128)(2,1)S(1)}, bf16[256,128]{1,0:T(8,128)(2,1)S(1)}) custom-call(s32[1]{0:T(128)} %bitcast.place_ref, s32[16]{0:T(128)S(1)} %copy-done.3, s32[2,2,512]{2,1,0:T(2,128)S(1)} %copy-done.2, s32[2,2,512]{2,1,0:T(2,128)S(1)} %collective-permute-done.near_pairs_ref, ...), custom_call_target="tpu_custom_call" | custom-call | flops 4294967296 | bytes 2097152 | tf_op jit(solution)/shard_map/near/pallas_call | solution.py:337
  35.9 0.3 collective-permute-start.11
  36.1 0.3 collective-permute-start.12
  36.4 0.7 %collective-permute-done.11.refs_3_ = bf16[256,128]{1,0:T(8,128)(2,1)S(1)} collective-permute-done((bf16[256,128]{1,0:T(8,128)(2,1)S(1)}, bf16[256,128]{1,0:T(8,128)(2,1)S(1)}, u32[]{:S(2)}, u32[]{:S(2)}) %collective-permute-start.11) | collective-permute-done | bytes 65568 | tf_op jit(solution)/shard_map/ppermute | solution.py:270
  37.2 0.2 collective-permute-done.12.refs_4_
  37.4 5.7 %collective-permute-done.9.refs_1_ = bf16[512,128]{1,0:T(8,128)(2,1)S(1)} collective-permute-done((bf16[512,128]{1,0:T(8,128)(2,1)S(1)}, bf16[512,128]{1,0:T(8,128)(2,1)S(1)}, u32[]{:S(2)}, u32[]{:S(2)}) %collective-permute-start.9) | collective-permute-done | bytes 131104 | tf_op jit(solution)/shard_map/ppermute | solution.py:270
  43.1 2.7 %collective-permute-done.10.refs_2_ = bf16[512,128]{1,0:T(8,128)(2,1)S(1)} collective-permute-done((bf16[512,128]{1,0:T(8,128)(2,1)S(1)}, bf16[512,128]{1,0:T(8,128)(2,1)S(1)}, u32[]{:S(2)}, u32[]{:S(2)}) %collective-permute-start.10) | collective-permute-done | bytes 131104 | tf_op jit(solution)/shard_map/ppermute | solution.py:270
  45.8 0.0 copy-done
  45.8 1.5 %lags.1 = f32[2,512,256]{2,1,0:T(8,128)} custom-call(s32[1]{0:T(128)} %bitcast.place_ref, f32[256,256]{1,0:T(8,128)S(1)} %copy-done, bf16[512,128]{1,0:T(8,128)(2,1)S(1)} %get-tuple-element.32.refs_0_, bf16[512,128]{1,0:T(8,128)(2,1)S(1)} %collective-permute-done.9.refs_1_, bf16[512,128]{1,0:T(8,128)(2,1)S(1)} %collective-permute-done.10.refs_2_, ...), custom_call_target="tpu_custom_call" | custom-call | tf_op jit(solution)/shard_map/lags/pallas_call | solution.py:350
Async XLA Ops:
  0.0 3.4 %collective-permute-start.1 = (bf16[3,2,4,64,256]{4,3,2,1,0:T(8,128)(2,1)}, bf16[3,2,4,64,256]{4,3,2,1,0:T(8,128)(2,1)S(1)}, u32[]{:S(2)}, u32[]{:S(2)}) collective-permute-start(bf16[3,2,4,64,256]{4,3,2,1,0:T(8,128)(2,1)} %bitcast.2), channel_id=1, source_target_pairs={{0,1},{1,0},{2,3},{3,2},{4,5},{5,4},{6,7},{7,6},{8,9},{9,8},{10,11... | collective-permute-start | bytes 2359304 | tf_op jit(solution)/shard_map/ppermute | solution.py:270
  0.5 2.9 %collective-permute-start = (s32[2,2,512]{2,1,0:T(2,128)}, s32[2,2,512]{2,1,0:T(2,128)S(1)}, u32[]{:S(2)}, u32[]{:S(2)}) collective-permute-start(s32[2,2,512]{2,1,0:T(2,128)} %own_pairs_ref.3), channel_id=1, source_target_pairs={{0,1},{1,0},{2,3},{3,2},{4,5},{5,4},{6,7},{7,6},{8,9},{9,8},{10,11... | collective-permute-start | bytes 24584 | tf_op jit(solution)/shard_map/ppermute | solution.py:270
  0.5 1.1 %copy-start.4 = (bf16[3,1,512,256]{3,2,1,0:T(8,128)(2,1)S(1)}, bf16[3,1,512,256]{3,2,1,0:T(8,128)(2,1)}, u32[]{:S(2)}) copy-start(bf16[3,1,512,256]{3,2,1,0:T(8,128)(2,1)} %param.5) | copy-start | bytes 2359300
  1.6 0.9 %copy-start.5 = (bf16[256,256]{1,0:T(8,128)(2,1)S(1)}, bf16[256,256]{1,0:T(8,128)(2,1)}, u32[]{:S(2)}) copy-start(bf16[256,256]{1,0:T(8,128)(2,1)} %constant.8.clone.forward_ref) | copy-start | bytes 393220
  3.4 0.7 %copy-start.1 = (s32[2,2,512]{2,1,0:T(2,128)S(1)}, s32[2,2,512]{2,1,0:T(2,128)}, u32[]{:S(2)}) copy-start(s32[2,2,512]{2,1,0:T(2,128)} %own_pairs_ref.3) | copy-start | bytes 24580
  4.9 18.9 %collective-permute-start.2 = (bf16[416,128]{1,0:T(8,128)(2,1)S(1)}, bf16[416,128]{1,0:T(8,128)(2,1)S(1)}, u32[]{:S(2)}, u32[]{:S(2)}) collective-permute-start(bf16[416,128]{1,0:T(8,128)(2,1)S(1)} %get-tuple-element.23), channel_id=1, source_target_pairs={{0,8},{1,9},{2,10},{3,11},{4,12},{5,13},{6,14},{7,15},{8,0},{9,1},... | collective-permute-start | bytes 319496 | tf_op jit(solution)/shard_map/ppermute | solution.py:270
  9.0 4.8 %collective-permute-start.3 = (bf16[384,128]{1,0:T(8,128)(2,1)S(1)}, bf16[384,128]{1,0:T(8,128)(2,1)S(1)}, u32[]{:S(2)}, u32[]{:S(2)}) collective-permute-start(bf16[384,128]{1,0:T(8,128)(2,1)S(1)} %get-tuple-element.25), channel_id=1, source_target_pairs={{0,2},{1,3},{2,0},{3,1},{4,6},{5,7},{6,4},{7,5},{8,10},{9,11},{10,... | collective-permute-start | bytes 294920 | tf_op jit(solution)/shard_map/ppermute | solution.py:270
  10.5 7.2 %collective-permute-start.4 = (bf16[384,128]{1,0:T(8,128)(2,1)S(1)}, bf16[384,128]{1,0:T(8,128)(2,1)S(1)}, u32[]{:S(2)}, u32[]{:S(2)}) collective-permute-start(bf16[384,128]{1,0:T(8,128)(2,1)S(1)} %get-tuple-element.26), channel_id=1, source_target_pairs={{0,4},{1,5},{2,6},{3,7},{4,0},{5,1},{6,2},{7,3},{8,12},{9,13},{10,... | collective-permute-start | bytes 294920 | tf_op jit(solution)/shard_map/ppermute | solution.py:270
  12.1 11.7 %collective-permute-start.5 = (bf16[384,128]{1,0:T(8,128)(2,1)S(1)}, bf16[384,128]{1,0:T(8,128)(2,1)S(1)}, u32[]{:S(2)}, u32[]{:S(2)}) collective-permute-start(bf16[384,128]{1,0:T(8,128)(2,1)S(1)} %get-tuple-element.27), channel_id=1, source_target_pairs={{0,10},{1,11},{2,8},{3,9},{4,14},{5,15},{6,12},{7,13},{8,2},{9,3},... | collective-permute-start | bytes 294920 | tf_op jit(solution)/shard_map/ppermute | solution.py:270
  12.4 11.5 %collective-permute-start.6 = (bf16[384,128]{1,0:T(8,128)(2,1)S(1)}, bf16[384,128]{1,0:T(8,128)(2,1)S(1)}, u32[]{:S(2)}, u32[]{:S(2)}) collective-permute-start(bf16[384,128]{1,0:T(8,128)(2,1)S(1)} %get-tuple-element.28), channel_id=1, source_target_pairs={{0,6},{1,7},{2,4},{3,5},{4,2},{5,3},{6,0},{7,1},{8,14},{9,15},{10,... | collective-permute-start | bytes 294920 | tf_op jit(solution)/shard_map/ppermute | solution.py:270
  13.8 11.4 %collective-permute-start.7 = (bf16[384,128]{1,0:T(8,128)(2,1)S(1)}, bf16[384,128]{1,0:T(8,128)(2,1)S(1)}, u32[]{:S(2)}, u32[]{:S(2)}) collective-permute-start(bf16[384,128]{1,0:T(8,128)(2,1)S(1)} %get-tuple-element.29), channel_id=1, source_target_pairs={{0,12},{1,13},{2,14},{3,15},{4,8},{5,9},{6,10},{7,11},{8,4},{9,5},... | collective-permute-start | bytes 294920 | tf_op jit(solution)/shard_map/ppermute | solution.py:270
  17.7 7.5 %collective-permute-start.8 = (bf16[384,128]{1,0:T(8,128)(2,1)S(1)}, bf16[384,128]{1,0:T(8,128)(2,1)S(1)}, u32[]{:S(2)}, u32[]{:S(2)}) collective-permute-start(bf16[384,128]{1,0:T(8,128)(2,1)S(1)} %get-tuple-element.30), channel_id=1, source_target_pairs={{0,14},{1,15},{2,12},{3,13},{4,10},{5,11},{6,8},{7,9},{8,6},{9,7},... | collective-permute-start | bytes 294920 | tf_op jit(solution)/shard_map/ppermute | solution.py:270
  23.9 1.4 %copy-start.3 = (s32[16]{0:T(128)S(1)}, s32[16]{0:T(128)}, u32[]{:S(2)}) copy-start(s32[16]{0:T(128)} %counts_ref.3) | copy-start | bytes 196
  25.2 9.0 %copy-start.2 = (s32[2,2,512]{2,1,0:T(2,128)S(1)}, s32[2,2,512]{2,1,0:T(2,128)}, u32[]{:S(2)}) copy-start(s32[2,2,512]{2,1,0:T(2,128)} %own_pairs_ref.3) | copy-start | bytes 24580
  28.7 14.4 %collective-permute-start.9 = (bf16[512,128]{1,0:T(8,128)(2,1)S(1)}, bf16[512,128]{1,0:T(8,128)(2,1)S(1)}, u32[]{:S(2)}, u32[]{:S(2)}) collective-permute-start(bf16[512,128]{1,0:T(8,128)(2,1)S(1)} %get-tuple-element.33), channel_id=1, source_target_pairs={{0,8},{1,9},{2,10},{3,11},{4,12},{5,13},{6,14},{7,15},{8,0},{9,1},... | collective-permute-start | bytes 393224 | tf_op jit(solution)/shard_map/ppermute | solution.py:270
  34.2 11.5 %collective-permute-start.10 = (bf16[512,128]{1,0:T(8,128)(2,1)S(1)}, bf16[512,128]{1,0:T(8,128)(2,1)S(1)}, u32[]{:S(2)}, u32[]{:S(2)}) collective-permute-start(bf16[512,128]{1,0:T(8,128)(2,1)S(1)} %get-tuple-element.34), channel_id=1, source_target_pairs={{0,9},{1,8},{2,11},{3,10},{4,13},{5,12},{6,15},{7,14},{8,1},{9,0},... | collective-permute-start | bytes 393224 | tf_op jit(solution)/shard_map/ppermute | solution.py:270
  34.2 11.5 %copy-start = (f32[256,256]{1,0:T(8,128)S(1)}, f32[256,256]{1,0:T(8,128)}, u32[]{:S(2)}) copy-start(f32[256,256]{1,0:T(8,128)} %constant.9.clone.inverse_ref) | copy-start | bytes 786436
  35.9 1.3 %collective-permute-start.11 = (bf16[256,128]{1,0:T(8,128)(2,1)S(1)}, bf16[256,128]{1,0:T(8,128)(2,1)S(1)}, u32[]{:S(2)}, u32[]{:S(2)}) collective-permute-start(bf16[256,128]{1,0:T(8,128)(2,1)S(1)} %get-tuple-element.35), channel_id=1, source_target_pairs={{0,1},{1,0},{2,3},{3,2},{4,5},{5,4},{6,7},{7,6},{8,9},{9,8},{10,11... | collective-permute-start | bytes 196616 | tf_op jit(solution)/shard_map/ppermute | solution.py:270
  36.1 1.3 %collective-permute-start.12 = (bf16[256,128]{1,0:T(8,128)(2,1)S(1)}, bf16[256,128]{1,0:T(8,128)(2,1)S(1)}, u32[]{:S(2)}, u32[]{:S(2)}) collective-permute-start(bf16[256,128]{1,0:T(8,128)(2,1)S(1)} %get-tuple-element.36), channel_id=1, source_target_pairs={{0,1},{1,0},{2,3},{3,2},{4,5},{5,4},{6,7},{7,6},{8,9},{9,8},{10,11... | collective-permute-start | bytes 196616 | tf_op jit(solution)/shard_map/ppermute | solution.py:270

commit v6 on v5

--- a/solution.py
+++ b/solution.py
@@ -10,27 +10,45 @@
 from jax.sharding import PartitionSpec as P
 
 EPSILON = 1e-06
+COSINE = (
+    0.9999999999993376,
+    -4.934802200431432,
+    4.058712123240781,
+    -1.3352627346923478,
+    0.23533044681677665,
+    -0.02580633847975355,
+    0.0019285963125396874,
+    -0.00010362767792380447,
+    3.734915399663344e-06,
+)
 SLOTS = 32
 NT = (((1,), (1,)), ((), ()))
 TN = (((0,), (0,)), ((), ()))
 VMEM_LIMIT = 40 * 1024 * 1024
 
 
-def tables(samples, stations):
+def inverse_table(samples, stations):
     bins = samples // 2
     quarter = bins // 4
     turn = np.arange(bins)[:, None] * np.arange(samples)[None, :] % samples
     angle = turn * (2.0 * math.pi / samples)
     weight = np.where(np.arange(bins) == 0, 1.0, 2.0)[:, None] / samples
     weight = weight * math.sqrt(samples / (3.0 * stations))
-
-    def by_quarter(real, imag):
-        rows = [real.reshape(4, quarter, samples), imag.reshape(4, quarter, samples)]
-        return np.concatenate(rows, axis=1).reshape(4 * 2 * quarter, samples)
-
-    forward = by_quarter(np.cos(angle), -np.sin(angle)).astype(np.float32)
-    inverse = by_quarter(weight * np.cos(angle), -weight * np.sin(angle)).astype(np.float32)
-    return forward.astype(jnp.bfloat16), inverse
+    parts = [weight * np.cos(angle), -weight * np.sin(angle)]
+    rows = [part.reshape(4, quarter, samples) for part in parts]
+    return np.concatenate(rows, axis=1).reshape(2 * bins, samples).astype(np.float32)
+
+
+def forward_rows(bins, samples):
+    count = bins.shape[0]
+    sample = lax.broadcasted_iota(jnp.int32, (2 * count, samples), 1)
+    turn = jnp.concatenate([bins * sample[:count], bins * sample[:count] + samples // 4]) % samples
+    x = jnp.where(turn > samples // 2, turn - samples, turn).astype(jnp.float32) * (2.0 / samples)
+    square = x * x
+    value = jnp.full(square.shape, COSINE[-1], jnp.float32)
+    for factor in COSINE[-2::-1]:
+        value = value * square + factor
+    return value.astype(jnp.bfloat16)
 
 
 def place_of(place_ref, groups):
@@ -65,14 +83,16 @@
     return (raw * scale).astype(jnp.bfloat16)
 
 
-def own_kernel(place_ref, windows_ref, forward_ref, spectra_ref, table_ref):
-    comps, _, groups, _, _ = windows_ref.shape
-    rows = forward_ref.shape[0] // 4
+def own_kernel(place_ref, windows_ref, spectra_ref, table_ref):
+    comps, _, groups, _, samples = windows_ref.shape
+    rows = table_ref.shape[0] // 2
     lanes = 4 * SLOTS
     quarter, group = place_of(place_ref, groups)
     for far in range(2):
-        start = pl.multiple_of((quarter ^ (2 * far)) * rows, rows)
-        table_ref[far * rows : (far + 1) * rows] = forward_ref[pl.ds(start, rows), :]
+        bins = lax.broadcasted_iota(jnp.int32, (rows // 2, samples), 0)
+        table_ref[far * rows : (far + 1) * rows] = forward_rows(
+            bins + (quarter ^ (2 * far)) * (rows // 2), samples
+        )
     table = table_ref[...]
     for mg in range(groups):
         spectra = station_spectra(windows_ref, group ^ mg, table)
@@ -83,17 +103,15 @@
                 ]
 
 
-def near_spectra_kernel(
-    place_ref, own_pairs_ref, near_pairs_ref, table_ref, own_ref, windows_ref, *piece_refs
-):
+def near_spectra_kernel(place_ref, table_ref, own_ref, windows_ref, *refs):
+    pairs_refs, listed_ref, piece_refs = refs[:3], refs[3], refs[4:]
     comps, _, groups, _, _ = windows_ref.shape
     rows = table_ref.shape[0] // 2
     lanes = 4 * SLOTS
     _, group = place_of(place_ref, groups)
     table = table_ref[...]
-    piece_refs[groups][2 * comps * rows :] = jnp.concatenate(
-        [listing_of(own_pairs_ref, lanes), listing_of(near_pairs_ref, lanes)]
-    ).astype(jnp.bfloat16)
+    for at, pairs_ref in enumerate(pairs_refs):
+        listed_ref[at] = listing_of(pairs_ref, lanes)
     for mg in range(groups):
         spectra = station_spectra(windows_ref, group ^ mg, table)
         for far in range(2):
@@ -177,8 +195,8 @@
     each = traces * rows
     start = 0
     for piece in piece_refs:
-        held = piece.shape[0] // rows * rows
-        trace_ref[start : start + held] = piece[:held].astype(jnp.float32)
+        held = piece.shape[0]
+        trace_ref[start : start + held] = piece[...].astype(jnp.float32)
         start += held
     if start < each:
         trace_ref[start:] = jnp.zeros((each - start, lanes), jnp.float32)
@@ -220,15 +238,13 @@
                     flat_ref[
                         own, far, four * SLOTS : (four + 1) * SLOTS, part * lanes : (part + 1) * lanes
                     ] = block[slots + far * SLOTS : slots + (far + 1) * SLOTS]
-    listed = listed_ref[listed_ref.shape[0] // rows * rows :].astype(jnp.float32)
-    listing = listed.shape[0] // 2
-    pick(place_ref, counts_ref, listed[:listing], flat_ref, 2, picked_0)
-    pick(place_ref, counts_ref, listed[listing:], flat_ref, 3, picked_1)
-
-
-def near_kernel(place_ref, counts_ref, own_pairs_ref, near_pairs_ref, flat_ref, picked_0, *picked_1):
+    pick(place_ref, counts_ref, listed_ref[1], flat_ref, 2, picked_0)
+    pick(place_ref, counts_ref, listed_ref[2], flat_ref, 3, picked_1)
+
+
+def near_kernel(place_ref, counts_ref, own_pairs_ref, listed_ref, flat_ref, picked_0, *picked_1):
     lanes = 4 * SLOTS
-    pick(place_ref, counts_ref, listing_of(near_pairs_ref, lanes), flat_ref, 1, *picked_1)
+    pick(place_ref, counts_ref, listed_ref[0], flat_ref, 1, *picked_1)
     pick(place_ref, counts_ref, listing_of(own_pairs_ref, lanes), flat_ref, 0, picked_0)
 
 
@@ -263,7 +279,7 @@
     count = pairs.shape[2]
     rows = samples // 4
     lanes = 4 * SLOTS
-    forward, inverse = tables(samples, cells)
+    inverse = inverse_table(samples, cells)
     place = lax.axis_index("cell").astype(jnp.int32).reshape(1)
 
     def swap(x, mask):
@@ -274,33 +290,32 @@
     params = pltpu.CompilerParams(vmem_limit_bytes=VMEM_LIMIT)
 
     windows = windows.reshape(comps, 2, groups, 2 * SLOTS, samples)
-    near_windows, near_pairs = swap(windows, 1), swap(pairs, 1)
-    listing = 2 * pairs.size // lanes
+    near_windows = swap(windows, 1)
+    other_pairs = [swap(pairs, m) for m in (1, half, half + 1)]
+    listing = pairs.size // lanes
     own_spectra, table = pl.pallas_call(
         own_kernel,
         out_shape=[
             jax.ShapeDtypeStruct((2 * groups, comps * rows, lanes), jnp.bfloat16),
             jax.ShapeDtypeStruct((2 * rows, samples), jnp.bfloat16),
         ],
-        in_specs=[smem, vmem, vmem],
+        in_specs=[smem, vmem],
         out_specs=[vmem, vmem],
         compiler_params=params,
         cost_estimate=pl.CostEstimate(
             flops=4 * windows.size * samples, bytes_accessed=4 * windows.size, transcendentals=0
         ),
         name="own_spectra",
-    )(place, windows, jnp.asarray(forward))
-    pieces = pl.pallas_call(
+    )(place, windows)
+    listed, *pieces = pl.pallas_call(
         near_spectra_kernel,
-        out_shape=[
-            jax.ShapeDtypeStruct((2 * comps * rows + listing * (m == groups), lanes), jnp.bfloat16)
-            for m in range(2 * groups)
-        ],
-        in_specs=[smem] + [vmem] * 5,
-        out_specs=[vmem] * (2 * groups),
+        out_shape=[jax.ShapeDtypeStruct((3, listing, lanes), jnp.float32)]
+        + [jax.ShapeDtypeStruct((2 * comps * rows, lanes), jnp.bfloat16)] * (2 * groups),
+        in_specs=[smem] + [vmem] * 6,
+        out_specs=[vmem] * (1 + 2 * groups),
         compiler_params=params,
         name="near_spectra",
-    )(place, pairs, near_pairs, table, own_spectra, near_windows)
+    )(place, table, own_spectra, near_windows, *other_pairs)
     order = [*range(1, groups - 1), *range(groups, 2 * groups), groups - 1]
     arrived = {m: swap(pieces[m], 2 * m) for m in order}
     late = [2 * groups - 2, 2 * groups - 1]
@@ -332,7 +347,7 @@
         ],
         compiler_params=params,
         name="cross",
-    )(place, counts, arrived[groups], sums, *[arrived[m] for m in late])
+    )(place, counts, listed, sums, *[arrived[m] for m in late])
     picked_2, picked_3 = swap(picked_2, half), swap(picked_3, half + 1)
     picked_0, *picked_1 = pl.pallas_call(
         near_kernel,
@@ -344,7 +359,7 @@
             flops=128 * count * SLOTS * SLOTS * rows, bytes_accessed=2**21, transcendentals=0
         ),
         name="near",
-    )(place, counts, pairs, near_pairs, flat)
+    )(place, counts, pairs, listed, flat)
     picked_1 = [swap(p, 1) for p in picked_1]
 
     return pl.pallas_call(

time: 47.4 us -> 49.5 us (1.044)
  waiting for transfers between devices: 15.1 us -> 19.8 us
  local copies, waits for them, and re-layouts: 2.74 us -> 1.14 us
  starting transfers between devices: 19.7 us -> 18.7 us
    ppermute x13 -> x15, waiting for transfers between devices: 15.1 us -> 19.8 us  [swap(): return lax.ppermute(x, 'cell', [(i, i ^ mask) for i in range(cells)])]
    unnamed x12 -> x8, local copies, waits for them, and re-layouts: 2.74 us -> 1.14 us
    ppermute x13 -> x15, starting transfers between devices: 19.7 us -> 18.7 us  [swap(): return lax.ppermute(x, 'cell', [(i, i ^ mask) for i in range(cells)])]
  transfers between devices with their start and end apart: 13 -> 15, of which waited for: 6 -> 8; matrix products, arithmetic and copies ran while one was open for 0% -> 0% of each run, Pallas kernels for 8% -> 8%
where the time goes in v6:
time: 49.5 us; the launch traced here: 49.4 us
  waiting for transfers between devices  19.8 us (40%)
  starting transfers between devices  18.7 us (38%)
  Pallas kernels  9.6 us (19%)
  local copies, waits for them, and re-layouts  1.14 us (2%)
    ppermute x15, waiting for transfers between devices, swap(): return lax.ppermute(x, 'cell', [(i, i ^ mask) for i in range(cells)])  19.8 us
    ppermute x15, starting transfers between devices, swap(): return lax.ppermute(x, 'cell', [(i, i ^ mask) for i in range(cells)])  18.7 us
    pallas_call x1, Pallas kernels, on_device(): pl.pallas_call(cross_kernel, out_shape=[jax.ShapeDtypeStruct((2, 2, SLOTS...  3.48 us
    pallas_call x1, Pallas kernels, on_device(): pl.pallas_call(near_kernel, out_shape=[picked_shape] + [jax.ShapeDtypeStr...  1.62 us
    pallas_call x1, Pallas kernels, on_device(): pl.pallas_call(functools.partial(lag_kernel, groups), out_shape=jax.Shape...  1.46 us
    pallas_call x1, Pallas kernels, on_device(): pl.pallas_call(early_kernel, out_shape=jax.ShapeDtypeStruct((2 * SLOTS *...  1.33 us
    unnamed x8, local copies, waits for them, and re-layouts  1.14 us
  transfers between devices with their start and end apart: 15, of which 8 were waited for; matrix products, arithmetic and copies ran while one was open for 0% of the time, Pallas kernels for 8%

profile of v6, /device:TPU:0, one launch (start us, length us, event | category | flops | bytes accessed | tf_op | source)
XLA Modules:
  0.0 49.4 jit_solution(8790343924250683770)
XLA Ops:
  0.0 0.5 collective-permute-start
  0.5 3.6 %collective-permute-start.2 = (s32[2,2,512]{2,1,0:T(2,128)}, s32[2,2,512]{2,1,0:T(2,128)S(1)}, u32[]{:S(2)}, u32[]{:S(2)}) collective-permute-start(s32[2,2,512]{2,1,0:T(2,128)} %own_pairs_ref.1), channel_id=1, source_target_pairs={{0,8},{1,9},{2,10},{3,11},{4,12},{5,13},{6,14},{7,15},{8,0},{9,1},... | collective-permute-start | bytes 24584 | tf_op jit(solution)/shard_map/ppermute | solution.py:286
  4.0 0.2 collective-permute-start.1
  4.3 0.0 collective-permute-start.3
  4.3 0.0 copy-start.2
  4.3 1.1 %copy-done.2 = bf16[3,1,512,256]{3,2,1,0:T(8,128)(2,1)S(1)} copy-done((bf16[3,1,512,256]{3,2,1,0:T(8,128)(2,1)S(1)}, bf16[3,1,512,256]{3,2,1,0:T(8,128)(2,1)}, u32[]{:S(2)}) %copy-start.2) | copy-done | bytes 786456
  5.4 0.9 %own_spectra.1 = (bf16[8,192,128]{2,1,0:T(8,128)(2,1)S(1)}, bf16[128,256]{1,0:T(8,128)(2,1)S(1)}) custom-call(s32[1]{0:T(128)} %bitcast.place_ref, bf16[3,2,4,64,256]{4,3,2,1,0:T(8,128)(2,1)S(1)} %bitcast.3), custom_call_target="tpu_custom_call" | custom-call | flops 402653184 | bytes 1572864 | tf_op jit(solution)/shard_map/own_spectra/pallas_call | solution.py:296
  6.3 0.0 collective-permute-done.2.refs_1_
  6.3 0.0 collective-permute-done.1.refs_0_
  6.3 2.1 %collective-permute-done.3.refs_2_ = s32[2,2,512]{2,1,0:T(2,128)S(1)} collective-permute-done((s32[2,2,512]{2,1,0:T(2,128)}, s32[2,2,512]{2,1,0:T(2,128)S(1)}, u32[]{:S(2)}, u32[]{:S(2)}) %collective-permute-start.3) | collective-permute-done | bytes 8224 | tf_op jit(solution)/shard_map/ppermute | solution.py:286
  8.5 0.0 collective-permute-done.windows_ref
  8.5 0.8 %near_spectra.1 = (f32[3,16,128]{2,1,0:T(8,128)S(1)}, bf16[384,128]{1,0:T(8,128)(2,1)S(1)}, bf16[384,128]{1,0:T(8,128)(2,1)S(1)}, bf16[384,128]{1,0:T(8,128)(2,1...) custom-call(s32[1]{0:T(128)} %bitcast.place_ref, ...), custom_call_target="tpu_custom_call" | custom-call | tf_op jit(solution)/shard_map/near_spectra/pallas_call | solution.py:310
  9.3 1.6 %collective-permute-start.4 = (bf16[384,128]{1,0:T(8,128)(2,1)S(1)}, bf16[384,128]{1,0:T(8,128)(2,1)S(1)}, u32[]{:S(2)}, u32[]{:S(2)}) collective-permute-start(bf16[384,128]{1,0:T(8,128)(2,1)S(1)} %get-tuple-element.26), channel_id=1, source_target_pairs={{0,2},{1,3},{2,0},{3,1},{4,6},{5,7},{6,4},{7,5},{8,10},{9,11},{10,... | collective-permute-start | bytes 294920 | tf_op jit(solution)/shard_map/ppermute | solution.py:286
  10.9 1.6 %collective-permute-start.5 = (bf16[384,128]{1,0:T(8,128)(2,1)S(1)}, bf16[384,128]{1,0:T(8,128)(2,1)S(1)}, u32[]{:S(2)}, u32[]{:S(2)}) collective-permute-start(bf16[384,128]{1,0:T(8,128)(2,1)S(1)} %get-tuple-element.27), channel_id=1, source_target_pairs={{0,4},{1,5},{2,6},{3,7},{4,0},{5,1},{6,2},{7,3},{8,12},{9,13},{10,... | collective-permute-start | bytes 294920 | tf_op jit(solution)/shard_map/ppermute | solution.py:286
  12.4 0.7 %collective-permute-start.6 = (bf16[384,128]{1,0:T(8,128)(2,1)S(1)}, bf16[384,128]{1,0:T(8,128)(2,1)S(1)}, u32[]{:S(2)}, u32[]{:S(2)}) collective-permute-start(bf16[384,128]{1,0:T(8,128)(2,1)S(1)} %get-tuple-element.28), channel_id=1, source_target_pairs={{0,8},{1,9},{2,10},{3,11},{4,12},{5,13},{6,14},{7,15},{8,0},{9,1},... | collective-permute-start | bytes 294920 | tf_op jit(solution)/shard_map/ppermute | solution.py:286
  13.1 2.2 %collective-permute-start.7 = (bf16[384,128]{1,0:T(8,128)(2,1)S(1)}, bf16[384,128]{1,0:T(8,128)(2,1)S(1)}, u32[]{:S(2)}, u32[]{:S(2)}) collective-permute-start(bf16[384,128]{1,0:T(8,128)(2,1)S(1)} %get-tuple-element.29), channel_id=1, source_target_pairs={{0,10},{1,11},{2,8},{3,9},{4,14},{5,15},{6,12},{7,13},{8,2},{9,3},... | collective-permute-start | bytes 294920 | tf_op jit(solution)/shard_map/ppermute | solution.py:286
  15.3 1.4 %collective-permute-start.8 = (bf16[384,128]{1,0:T(8,128)(2,1)S(1)}, bf16[384,128]{1,0:T(8,128)(2,1)S(1)}, u32[]{:S(2)}, u32[]{:S(2)}) collective-permute-start(bf16[384,128]{1,0:T(8,128)(2,1)S(1)} %get-tuple-element.30), channel_id=1, source_target_pairs={{0,6},{1,7},{2,4},{3,5},{4,2},{5,3},{6,0},{7,1},{8,14},{9,15},{10,... | collective-permute-start | bytes 294920 | tf_op jit(solution)/shard_map/ppermute | solution.py:286
  16.7 0.0 collective-permute-done.4.refs_1_
  16.7 1.7 %collective-permute-start.9 = (bf16[384,128]{1,0:T(8,128)(2,1)S(1)}, bf16[384,128]{1,0:T(8,128)(2,1)S(1)}, u32[]{:S(2)}, u32[]{:S(2)}) collective-permute-start(bf16[384,128]{1,0:T(8,128)(2,1)S(1)} %get-tuple-element.31), channel_id=1, source_target_pairs={{0,12},{1,13},{2,14},{3,15},{4,8},{5,9},{6,10},{7,11},{8,4},{9,5},... | collective-permute-start | bytes 294920 | tf_op jit(solution)/shard_map/ppermute | solution.py:286
  18.4 0.0 collective-permute-done.5.refs_2_
  18.4 2.1 %collective-permute-start.10 = (bf16[384,128]{1,0:T(8,128)(2,1)S(1)}, bf16[384,128]{1,0:T(8,128)(2,1)S(1)}, u32[]{:S(2)}, u32[]{:S(2)}) collective-permute-start(bf16[384,128]{1,0:T(8,128)(2,1)S(1)} %get-tuple-element.32), channel_id=1, source_target_pairs={{0,14},{1,15},{2,12},{3,13},{4,10},{5,11},{6,8},{7,9},{8,6},{9,7},... | collective-permute-start | bytes 294920 | tf_op jit(solution)/shard_map/ppermute | solution.py:286
  20.5 5.9 %collective-permute-done.6.refs_3_ = bf16[384,128]{1,0:T(8,128)(2,1)S(1)} collective-permute-done((bf16[384,128]{1,0:T(8,128)(2,1)S(1)}, bf16[384,128]{1,0:T(8,128)(2,1)S(1)}, u32[]{:S(2)}, u32[]{:S(2)}) %collective-permute-start.6) | collective-permute-done | bytes 98336 | tf_op jit(solution)/shard_map/ppermute | solution.py:286
  26.4 2.0 %collective-permute-done.7.refs_4_ = bf16[384,128]{1,0:T(8,128)(2,1)S(1)} collective-permute-done((bf16[384,128]{1,0:T(8,128)(2,1)S(1)}, bf16[384,128]{1,0:T(8,128)(2,1)S(1)}, u32[]{:S(2)}, u32[]{:S(2)}) %collective-permute-start.7) | collective-permute-done | bytes 98336 | tf_op jit(solution)/shard_map/ppermute | solution.py:286
  28.4 0.3 collective-permute-done.8.refs_5_
  28.7 0.0 copy-start.1
  28.7 1.3 %early.1.before_ref = f32[4096,128]{1,0:T(8,128)S(1)} custom-call(bf16[384,128]{1,0:T(8,128)(2,1)S(1)} %get-tuple-element.25.refs_0_, bf16[384,128]{1,0:T(8,128)(2,1)S(1)} %collective-permute-done.4.refs_1_, bf16[384,128]{1,0:T(8,128)(2,1)S(1)} %collective-permute-done.5.refs_2_, bf16[384,128]{1,0:T(8,128)(2,1)S(1)} %collective-permute-done.6.refs_3_, ...), custom_call_target="tpu_custom_call" | custom-call | flops 2147483648 | bytes 4194304 | tf_op jit(solution)/shard_map/early/pallas_call | solution.py:324
  30.0 0.0 copy-start.3
  30.0 0.0 collective-permute-done.9.refs_0_
  30.0 0.0 collective-permute-done.10.refs_1_
  30.1 0.0 copy-done.1
  30.1 3.5 %cross.1 = (bf16[2,2,256,256]{3,2,1,0:T(8,128)(2,1)S(1)}, bf16[512,128]{1,0:T(8,128)(2,1)S(1)}, bf16[512,128]{1,0:T(8,128)(2,1)S(1)}) custom-call(s32[1]{0:T(128)} %bitcast.place_ref, s32[16]{0:T(128)S(1)} %copy-done.1, f32[3,16,128]{2,1,0:T(8,128)S(1)} %get-tuple-element.24.listed_ref, f32[4096,128]{1,0:T(8,128)S(1)} %early.1.before_ref, ...), custom_call_target="tpu_custom_call" | custom-call | tf_op jit(solution)/shard_map/cross/pallas_call | solution.py:335
  33.5 2.4 %collective-permute-start.11 = (bf16[512,128]{1,0:T(8,128)(2,1)S(1)}, bf16[512,128]{1,0:T(8,128)(2,1)S(1)}, u32[]{:S(2)}, u32[]{:S(2)}) collective-permute-start(bf16[512,128]{1,0:T(8,128)(2,1)S(1)} %get-tuple-element.35), channel_id=1, source_target_pairs={{0,8},{1,9},{2,10},{3,11},{4,12},{5,13},{6,14},{7,15},{8,0},{9,1},... | collective-permute-start | bytes 393224 | tf_op jit(solution)/shard_map/ppermute | solution.py:286
  35.9 0.0 collective-permute-start.12
  35.9 0.0 copy-done.3
  35.9 0.0 copy-start
  35.9 1.6 %near.1 = (bf16[512,128]{1,0:T(8,128)(2,1)S(1)}, bf16[256,128]{1,0:T(8,128)(2,1)S(1)}, bf16[256,128]{1,0:T(8,128)(2,1)S(1)}) custom-call(s32[1]{0:T(128)} %bitcast.place_ref, s32[16]{0:T(128)S(1)} %copy-done.1, s32[2,2,512]{2,1,0:T(2,128)S(1)} %copy-done.3, f32[3,16,128]{2,1,0:T(8,128)S(1)} %get-tuple-element.24.listed_ref, ...), custom_call_target="tpu_custom_call" | custom-call | flops 4294967296 | bytes 2097152 | tf_op jit(solution)/shard_map/near/pallas_call | solution.py:352
  37.5 0.8 %collective-permute-start.13 = (bf16[256,128]{1,0:T(8,128)(2,1)S(1)}, bf16[256,128]{1,0:T(8,128)(2,1)S(1)}, u32[]{:S(2)}, u32[]{:S(2)}) collective-permute-start(bf16[256,128]{1,0:T(8,128)(2,1)S(1)} %get-tuple-element.37), channel_id=1, source_target_pairs={{0,1},{1,0},{2,3},{3,2},{4,5},{5,4},{6,7},{7,6},{8,9},{9,8},{10,11... | collective-permute-start | bytes 196616 | tf_op jit(solution)/shard_map/ppermute | solution.py:286
  38.3 0.1 collective-permute-start.14
  38.4 0.8 %collective-permute-done.13.refs_3_ = bf16[256,128]{1,0:T(8,128)(2,1)S(1)} collective-permute-done((bf16[256,128]{1,0:T(8,128)(2,1)S(1)}, bf16[256,128]{1,0:T(8,128)(2,1)S(1)}, u32[]{:S(2)}, u32[]{:S(2)}) %collective-permute-start.13) | collective-permute-done | bytes 65568 | tf_op jit(solution)/shard_map/ppermute | solution.py:286
  39.3 0.4 collective-permute-done.14.refs_4_
  39.6 0.2 collective-permute-done.11.refs_1_
  39.8 8.1 %collective-permute-done.12.refs_2_ = bf16[512,128]{1,0:T(8,128)(2,1)S(1)} collective-permute-done((bf16[512,128]{1,0:T(8,128)(2,1)S(1)}, bf16[512,128]{1,0:T(8,128)(2,1)S(1)}, u32[]{:S(2)}, u32[]{:S(2)}) %collective-permute-start.12) | collective-permute-done | bytes 131104 | tf_op jit(solution)/shard_map/ppermute | solution.py:286
  47.9 0.0 copy-done
  47.9 1.5 %lags.1 = f32[2,512,256]{2,1,0:T(8,128)} custom-call(s32[1]{0:T(128)} %bitcast.place_ref, f32[256,256]{1,0:T(8,128)S(1)} %copy-done, bf16[512,128]{1,0:T(8,128)(2,1)S(1)} %get-tuple-element.34.refs_0_, bf16[512,128]{1,0:T(8,128)(2,1)S(1)} %collective-permute-done.11.refs_1_, bf16[512,128]{1,0:T(8,128)(2,1)S(1)} %collective-permute-done.12.refs_2_, ...), custom_call_target="tpu_custom_call" | custom-call | tf_op jit(solution)/shard_map/lags/pallas_call | solution.py:365
Async XLA Ops:
  0.0 8.5 %collective-permute-start = (bf16[3,2,4,64,256]{4,3,2,1,0:T(8,128)(2,1)}, bf16[3,2,4,64,256]{4,3,2,1,0:T(8,128)(2,1)S(1)}, u32[]{:S(2)}, u32[]{:S(2)}) collective-permute-start(bf16[3,2,4,64,256]{4,3,2,1,0:T(8,128)(2,1)} %bitcast.2), channel_id=1, source_target_pairs={{0,1},{1,0},{2,3},{3,2},{4,5},{5,4},{6,7},{7,6},{8,9},{9,8},{10,11... | collective-permute-start | bytes 2359304 | tf_op jit(solution)/shard_map/ppermute | solution.py:286
  0.5 5.8 %collective-permute-start.2 = (s32[2,2,512]{2,1,0:T(2,128)}, s32[2,2,512]{2,1,0:T(2,128)S(1)}, u32[]{:S(2)}, u32[]{:S(2)}) collective-permute-start(s32[2,2,512]{2,1,0:T(2,128)} %own_pairs_ref.1), channel_id=1, source_target_pairs={{0,8},{1,9},{2,10},{3,11},{4,12},{5,13},{6,14},{7,15},{8,0},{9,1},... | collective-permute-start | bytes 24584 | tf_op jit(solution)/shard_map/ppermute | solution.py:286
  4.0 2.3 %collective-permute-start.1 = (s32[2,2,512]{2,1,0:T(2,128)}, s32[2,2,512]{2,1,0:T(2,128)S(1)}, u32[]{:S(2)}, u32[]{:S(2)}) collective-permute-start(s32[2,2,512]{2,1,0:T(2,128)} %own_pairs_ref.1), channel_id=1, source_target_pairs={{0,1},{1,0},{2,3},{3,2},{4,5},{5,4},{6,7},{7,6},{8,9},{9,8},{10,11... | collective-permute-start | bytes 24584 | tf_op jit(solution)/shard_map/ppermute | solution.py:286
  4.3 4.2 %collective-permute-start.3 = (s32[2,2,512]{2,1,0:T(2,128)}, s32[2,2,512]{2,1,0:T(2,128)S(1)}, u32[]{:S(2)}, u32[]{:S(2)}) collective-permute-start(s32[2,2,512]{2,1,0:T(2,128)} %own_pairs_ref.1), channel_id=1, source_target_pairs={{0,9},{1,8},{2,11},{3,10},{4,13},{5,12},{6,15},{7,14},{8,1},{9,0},... | collective-permute-start | bytes 24584 | tf_op jit(solution)/shard_map/ppermute | solution.py:286
  4.3 1.1 %copy-start.2 = (bf16[3,1,512,256]{3,2,1,0:T(8,128)(2,1)S(1)}, bf16[3,1,512,256]{3,2,1,0:T(8,128)(2,1)}, u32[]{:S(2)}) copy-start(bf16[3,1,512,256]{3,2,1,0:T(8,128)(2,1)} %param.4) | copy-start | bytes 2359300
  9.3 7.4 %collective-permute-start.4 = (bf16[384,128]{1,0:T(8,128)(2,1)S(1)}, bf16[384,128]{1,0:T(8,128)(2,1)S(1)}, u32[]{:S(2)}, u32[]{:S(2)}) collective-permute-start(bf16[384,128]{1,0:T(8,128)(2,1)S(1)} %get-tuple-element.26), channel_id=1, source_target_pairs={{0,2},{1,3},{2,0},{3,1},{4,6},{5,7},{6,4},{7,5},{8,10},{9,11},{10,... | collective-permute-start | bytes 294920 | tf_op jit(solution)/shard_map/ppermute | solution.py:286
  10.9 7.6 %collective-permute-start.5 = (bf16[384,128]{1,0:T(8,128)(2,1)S(1)}, bf16[384,128]{1,0:T(8,128)(2,1)S(1)}, u32[]{:S(2)}, u32[]{:S(2)}) collective-permute-start(bf16[384,128]{1,0:T(8,128)(2,1)S(1)} %get-tuple-element.27), channel_id=1, source_target_pairs={{0,4},{1,5},{2,6},{3,7},{4,0},{5,1},{6,2},{7,3},{8,12},{9,13},{10,... | collective-permute-start | bytes 294920 | tf_op jit(solution)/shard_map/ppermute | solution.py:286
  12.4 13.9 %collective-permute-start.6 = (bf16[384,128]{1,0:T(8,128)(2,1)S(1)}, bf16[384,128]{1,0:T(8,128)(2,1)S(1)}, u32[]{:S(2)}, u32[]{:S(2)}) collective-permute-start(bf16[384,128]{1,0:T(8,128)(2,1)S(1)} %get-tuple-element.28), channel_id=1, source_target_pairs={{0,8},{1,9},{2,10},{3,11},{4,12},{5,13},{6,14},{7,15},{8,0},{9,1},... | collective-permute-start | bytes 294920 | tf_op jit(solution)/shard_map/ppermute | solution.py:286
  13.1 15.2 %collective-permute-start.7 = (bf16[384,128]{1,0:T(8,128)(2,1)S(1)}, bf16[384,128]{1,0:T(8,128)(2,1)S(1)}, u32[]{:S(2)}, u32[]{:S(2)}) collective-permute-start(bf16[384,128]{1,0:T(8,128)(2,1)S(1)} %get-tuple-element.29), channel_id=1, source_target_pairs={{0,10},{1,11},{2,8},{3,9},{4,14},{5,15},{6,12},{7,13},{8,2},{9,3},... | collective-permute-start | bytes 294920 | tf_op jit(solution)/shard_map/ppermute | solution.py:286
  15.3 13.4 %collective-permute-start.8 = (bf16[384,128]{1,0:T(8,128)(2,1)S(1)}, bf16[384,128]{1,0:T(8,128)(2,1)S(1)}, u32[]{:S(2)}, u32[]{:S(2)}) collective-permute-start(bf16[384,128]{1,0:T(8,128)(2,1)S(1)} %get-tuple-element.30), channel_id=1, source_target_pairs={{0,6},{1,7},{2,4},{3,5},{4,2},{5,3},{6,0},{7,1},{8,14},{9,15},{10,... | collective-permute-start | bytes 294920 | tf_op jit(solution)/shard_map/ppermute | solution.py:286
  16.7 13.3 %collective-permute-start.9 = (bf16[384,128]{1,0:T(8,128)(2,1)S(1)}, bf16[384,128]{1,0:T(8,128)(2,1)S(1)}, u32[]{:S(2)}, u32[]{:S(2)}) collective-permute-start(bf16[384,128]{1,0:T(8,128)(2,1)S(1)} %get-tuple-element.31), channel_id=1, source_target_pairs={{0,12},{1,13},{2,14},{3,15},{4,8},{5,9},{6,10},{7,11},{8,4},{9,5},... | collective-permute-start | bytes 294920 | tf_op jit(solution)/shard_map/ppermute | solution.py:286
  18.4 11.6 %collective-permute-start.10 = (bf16[384,128]{1,0:T(8,128)(2,1)S(1)}, bf16[384,128]{1,0:T(8,128)(2,1)S(1)}, u32[]{:S(2)}, u32[]{:S(2)}) collective-permute-start(bf16[384,128]{1,0:T(8,128)(2,1)S(1)} %get-tuple-element.32), channel_id=1, source_target_pairs={{0,14},{1,15},{2,12},{3,13},{4,10},{5,11},{6,8},{7,9},{8,6},{9,7},... | collective-permute-start | bytes 294920 | tf_op jit(solution)/shard_map/ppermute | solution.py:286
  28.7 1.4 %copy-start.1 = (s32[16]{0:T(128)S(1)}, s32[16]{0:T(128)}, u32[]{:S(2)}) copy-start(s32[16]{0:T(128)} %counts_ref.3) | copy-start | bytes 196
  30.0 5.9 %copy-start.3 = (s32[2,2,512]{2,1,0:T(2,128)S(1)}, s32[2,2,512]{2,1,0:T(2,128)}, u32[]{:S(2)}) copy-start(s32[2,2,512]{2,1,0:T(2,128)} %own_pairs_ref.1) | copy-start | bytes 24580
  33.5 6.3 %collective-permute-start.11 = (bf16[512,128]{1,0:T(8,128)(2,1)S(1)}, bf16[512,128]{1,0:T(8,128)(2,1)S(1)}, u32[]{:S(2)}, u32[]{:S(2)}) collective-permute-start(bf16[512,128]{1,0:T(8,128)(2,1)S(1)} %get-tuple-element.35), channel_id=1, source_target_pairs={{0,8},{1,9},{2,10},{3,11},{4,12},{5,13},{6,14},{7,15},{8,0},{9,1},... | collective-permute-start | bytes 393224 | tf_op jit(solution)/shard_map/ppermute | solution.py:286
  35.9 12.0 %collective-permute-start.12 = (bf16[512,128]{1,0:T(8,128)(2,1)S(1)}, bf16[512,128]{1,0:T(8,128)(2,1)S(1)}, u32[]{:S(2)}, u32[]{:S(2)}) collective-permute-start(bf16[512,128]{1,0:T(8,128)(2,1)S(1)} %get-tuple-element.36), channel_id=1, source_target_pairs={{0,9},{1,8},{2,11},{3,10},{4,13},{5,12},{6,15},{7,14},{8,1},{9,0},... | collective-permute-start | bytes 393224 | tf_op jit(solution)/shard_map/ppermute | solution.py:286
  35.9 12.0 %copy-start = (f32[256,256]{1,0:T(8,128)S(1)}, f32[256,256]{1,0:T(8,128)}, u32[]{:S(2)}) copy-start(f32[256,256]{1,0:T(8,128)} %constant.6.clone.inverse_ref) | copy-start | bytes 786436
  37.5 1.7 %collective-permute-start.13 = (bf16[256,128]{1,0:T(8,128)(2,1)S(1)}, bf16[256,128]{1,0:T(8,128)(2,1)S(1)}, u32[]{:S(2)}, u32[]{:S(2)}) collective-permute-start(bf16[256,128]{1,0:T(8,128)(2,1)S(1)} %get-tuple-element.37), channel_id=1, source_target_pairs={{0,1},{1,0},{2,3},{3,2},{4,5},{5,4},{6,7},{7,6},{8,9},{9,8},{10,11... | collective-permute-start | bytes 196616 | tf_op jit(solution)/shard_map/ppermute | solution.py:286
  38.3 1.3 %collective-permute-start.14 = (bf16[256,128]{1,0:T(8,128)(2,1)S(1)}, bf16[256,128]{1,0:T(8,128)(2,1)S(1)}, u32[]{:S(2)}, u32[]{:S(2)}) collective-permute-start(bf16[256,128]{1,0:T(8,128)(2,1)S(1)} %get-tuple-element.38), channel_id=1, source_target_pairs={{0,1},{1,0},{2,3},{3,2},{4,5},{5,4},{6,7},{7,6},{8,9},{9,8},{10,11... | collective-permute-start | bytes 196616 | tf_op jit(solution)/shard_map/ppermute | solution.py:286

commit v7 on v6

v7 whole, which is shorter than its diff:
```python
import functools
import math

import jax
import jax.numpy as jnp
import numpy as np
from jax import lax
from jax.experimental import pallas as pl
from jax.experimental.pallas import tpu as pltpu
from jax.sharding import PartitionSpec as P

EPSILON = 1e-06
COSINE = (
    0.9999999999993376,
    -4.934802200431432,
    4.058712123240781,
    -1.3352627346923478,
    0.23533044681677665,
    -0.02580633847975355,
    0.0019285963125396874,
    -0.00010362767792380447,
    3.734915399663344e-06,
)
SLOTS = 32
LANES = 4 * SLOTS
COMPS = 3
NT = (((1,), (1,)), ((), ()))
TN = (((0,), (0,)), ((), ()))
VMEM_LIMIT = 40 * 1024 * 1024

PART = 32
FULL = 16


def inverse_table(samples, stations):
    bins = samples // 2
    turn = np.arange(bins)[:, None] * np.arange(samples)[None, :] % samples
    angle = turn * (2.0 * math.pi / samples)
    weight = np.where(np.arange(bins) == 0, 1.0, 2.0)[:, None] / samples
    weight = weight * math.sqrt(samples / (3.0 * stations))
    real, imag = weight * np.cos(angle), -weight * np.sin(angle)
    runs = [(at, PART) for at in range(0, bins // 2, PART)]
    runs += [(at, FULL) for at in range(bins // 2, bins, FULL)]
    rows = [part[at : at + run] for at, run in runs for part in (real, imag)]
    return np.concatenate(rows).astype(np.float32)


def forward_rows(bins, samples):
    count = bins.shape[0]
    sample = lax.broadcasted_iota(jnp.int32, (2 * count, samples), 1)
    turn = jnp.concatenate([bins * sample[:count], bins * sample[:count] + samples // 4]) % samples
    x = jnp.where(turn > samples // 2, turn - samples, turn).astype(jnp.float32) * (2.0 / samples)
    square = x * x
    value = jnp.full(square.shape, COSINE[-1], jnp.float32)
    for factor in COSINE[-2::-1]:
        value = value * square + factor
    return value.astype(jnp.bfloat16)


def place_of(place_ref, groups):
    position = place_ref[0]
    high, inner = position // (2 * groups), position % (2 * groups)
    return high * 2 + inner % 2, inner // 2


def listing_of(pairs_ref, lanes):
    ends = []
    for end in range(2):
        slots = pairs_ref[:, end, :].astype(jnp.float32)
        ends += [slots[:, at : at + lanes] for at in range(0, slots.shape[1], lanes)]
    return jnp.concatenate(ends)


def station_spectra(windows_ref, at, table):
    parts = []
    for comp in range(windows_ref.shape[0]):
        low = windows_ref[comp, 0, at]
        high = windows_ref[comp, 1, at]
        parts += [low[:SLOTS], high[SLOTS:], low[SLOTS:], high[:SLOTS]]
    traces = jnp.concatenate(parts)
    square = jnp.square(traces.astype(jnp.float32))
    square_hi = square.astype(jnp.bfloat16)
    square_lo = (square - square_hi.astype(jnp.float32)).astype(jnp.bfloat16)
    ones = jnp.ones((16, traces.shape[1]), jnp.bfloat16)
    energy = lax.dot_general(ones, square_hi, NT, preferred_element_type=jnp.float32)
    energy += lax.dot_general(ones, square_lo, NT, preferred_element_type=jnp.float32)
    scale = lax.rsqrt(energy[:1] + EPSILON)
    raw = lax.dot_general(table, traces, NT, preferred_element_type=jnp.float32)
    return (raw * scale).astype(jnp.bfloat16)


def own_kernel(place_ref, windows_ref, part_ref, full_ref, table_ref):
    groups, samples = windows_ref.shape[2], windows_ref.shape[4]
    quarter, group = place_of(place_ref, groups)
    bins = lax.broadcasted_iota(jnp.int32, (PART, samples), 0) + (quarter % 2) * PART
    table_ref[: 2 * PART] = forward_rows(bins, samples)
    for far in range(2):
        start = samples // 4 + (quarter ^ (2 * far)) * FULL
        bins = lax.broadcasted_iota(jnp.int32, (FULL, samples), 0) + start
        at = 2 * PART + 2 * FULL * far
        table_ref[at : at + 2 * FULL] = forward_rows(bins, samples)
    table = table_ref[...]
    for mg in range(groups):
        spectra = station_spectra(windows_ref, group ^ mg, table)
        for comp in range(COMPS):
            lanes = spectra[:, comp * LANES : (comp + 1) * LANES]
            part_ref[mg, comp * 2 * PART : (comp + 1) * 2 * PART] = lanes[: 2 * PART]
            for far in range(2):
                at = 2 * PART + 2 * FULL * far
                full_ref[far * groups + mg, comp * 2 * FULL : (comp + 1) * 2 * FULL] = lanes[at : at + 2 * FULL]


def near_spectra_kernel(
    place_ref, own_pairs_ref, near_pairs_ref, table_ref, part_ref, full_ref, windows_ref, *piece_refs
):
    groups = windows_ref.shape[2]
    _, group = place_of(place_ref, groups)
    table = table_ref[...]
    part_rows, full_rows = COMPS * 2 * PART, COMPS * 2 * FULL
    piece_refs[groups][2 * full_rows :] = jnp.concatenate(
        [listing_of(own_pairs_ref, LANES), listing_of(near_pairs_ref, LANES)]
    ).astype(jnp.bfloat16)
    for mg in range(groups):
        spectra = station_spectra(windows_ref, group ^ mg, table)
        side, cross = piece_refs[mg], piece_refs[groups + mg]
        side[:part_rows] = part_ref[mg]
        side[2 * part_rows : 2 * part_rows + full_rows] = full_ref[mg]
        cross[:full_rows] = full_ref[groups + mg]
        for comp in range(COMPS):
            lanes = spectra[:, comp * LANES : (comp + 1) * LANES]
            at = part_rows + comp * 2 * PART
            side[at : at + 2 * PART] = lanes[: 2 * PART]
            at = 2 * part_rows + full_rows + comp * 2 * FULL
            side[at : at + 2 * FULL] = lanes[2 * PART : 2 * PART + 2 * FULL]
            at = full_rows + comp * 2 * FULL
            cross[at : at + 2 * FULL] = lanes[2 * PART + 2 * FULL :]


def pick(place_ref, counts_ref, listed, flat_ref, bins, mq, *picked_refs):
    cells = counts_ref.shape[0]
    quarter, group = place_of(place_ref, cells // 4)
    own = quarter ^ mq
    high, low = own // 2, own % 2
    cell = high * (cells // 2) + group * 2 + low
    count = listed.shape[0] // 2
    runs = LANES // bins
    first, second = listed[:count].astype(jnp.int32), listed[count:].astype(jnp.int32)
    far_counts = [counts_ref[cell ^ 1], counts_ref[cell ^ (cells // 2)]]
    odd = lax.broadcasted_iota(jnp.int32, (count, LANES), 0) % 2
    live = (first < counts_ref[cell]) & (second < jnp.where(odd == 1, far_counts[1], far_counts[0]))
    left, right = jnp.where(high == low, first, second), jnp.where(high == low, second, first)
    spot = jnp.where(live, (left // runs) * SLOTS + right, -1)
    turned = jnp.concatenate([spot, left % runs]).T
    lane = lax.broadcasted_iota(jnp.int32, (LANES, LANES), 1)
    run = lane // bins
    spread = lax.broadcasted_iota(jnp.int32, (2 * LANES, LANES), 0)
    kept = lax.broadcasted_iota(jnp.int32, (2 * LANES, LANES), 1)
    sides = ((high, high), (low, 1 - low))
    found = []
    for step_round in range(2):
        hot = []
        for at in range(step_round, count, 2):
            offset = turned[:, at : at + 1] - lane
            hot.append(
                jnp.concatenate(
                    [
                        jnp.where(offset == start, 1.0, 0.0).astype(jnp.bfloat16)
                        for start in range(0, flat_ref.shape[2], LANES)
                    ],
                    axis=1,
                )
            )
        block = flat_ref[sides[step_round][0], sides[step_round][1]]
        wide = jnp.dot(jnp.concatenate(hot), block, preferred_element_type=jnp.float32)
        masked = []
        for chunk, at in enumerate(range(step_round, count, 2)):
            here = run == turned[:, count + at : count + at + 1]
            part = wide[chunk * LANES : (chunk + 1) * LANES]
            masked.append(
                jnp.concatenate(
                    [
                        jnp.where(here, part[:, :LANES], 0.0).astype(jnp.bfloat16),
                        jnp.where(here, part[:, LANES:], 0.0).astype(jnp.bfloat16),
                    ],
                    axis=1,
                )
            )
        found.append(jnp.concatenate(masked))
    found = jnp.concatenate(found, axis=1)
    packs = LANES // (4 * bins)
    held = found.shape[0] // packs
    picked = 0.0
    for pack in range(packs):
        folds = []
        for step_round in range(2):
            place = (pack * 4 + step_round * 2 + spread // LANES) * bins + spread % bins
            folds.append(jnp.where(kept == place, 1.0, 0.0).astype(jnp.bfloat16))
        picked += jnp.dot(
            found[pack * held : (pack + 1) * held],
            jnp.concatenate(folds),
            preferred_element_type=jnp.float32,
        )
    picked = picked.astype(jnp.bfloat16)
    each = held // len(picked_refs)
    for at, ref in enumerate(picked_refs):
        ref[...] = picked[at * each : (at + 1) * each]


def padded(traces):
    return -(-traces // 16) * 16


def add_cross(pieces, trace_ref, bins, sums_ref, before_ref=None):
    slots, rows = 2 * SLOTS, 2 * bins
    traces = trace_ref.shape[0] // rows
    start = 0
    for piece, at, size in pieces:
        trace_ref[start : start + size] = piece[at : at + size].astype(jnp.float32)
        start += size
    if start < traces * rows:
        trace_ref[start:] = jnp.zeros((traces * rows - start, LANES), jnp.float32)
    for k in range(bins):
        real = trace_ref[pl.ds(k, traces, stride=rows), :].astype(jnp.bfloat16)
        imag = trace_ref[pl.ds(bins + k, traces, stride=rows), :].astype(jnp.bfloat16)
        left = jnp.concatenate([real, imag], axis=0)[:, :slots]
        right = jnp.concatenate(
            [jnp.concatenate([real, imag], axis=1), jnp.concatenate([imag, -real], axis=1)], axis=0
        )
        cross = lax.dot_general(left, right, TN, preferred_element_type=jnp.float32)
        for part in range(2):
            at = (part * bins + k) * slots
            value = cross[:, part * LANES : (part + 1) * LANES]
            if before_ref is not None:
                value += before_ref[at : at + slots]
            sums_ref[at : at + slots] = value


def turn_blocks(cross_ref, bins, flat_ref):
    slots, runs = 2 * SLOTS, LANES // bins
    for own in range(2):
        for at in range(SLOTS // runs):
            for part in range(2):
                first = part * bins * slots + own * SLOTS + at * runs
                block = jnp.concatenate(
                    [cross_ref[pl.ds(first + i, bins, stride=slots), :] for i in range(runs)]
                ).T.astype(jnp.bfloat16)
                for far in range(2):
                    flat_ref[
                        own, far, at * SLOTS : (at + 1) * SLOTS, part * LANES : (part + 1) * LANES
                    ] = block[slots + far * SLOTS : slots + (far + 1) * SLOTS]


def side_part(ref):
    return (ref, 0, 2 * COMPS * 2 * PART)


def side_full(ref):
    return (ref, 2 * COMPS * 2 * PART, 2 * COMPS * 2 * FULL)


def cross_full(ref):
    return (ref, 0, 2 * COMPS * 2 * FULL)


def part_kernel(place_ref, counts_ref, listed_ref, *refs):
    piece_refs, (flat_ref, picked_0, picked_1, trace_ref, cross_ref) = refs[:-5], refs[-5:]
    add_cross([side_part(ref) for ref in piece_refs], trace_ref, PART, cross_ref)
    turn_blocks(cross_ref, PART, flat_ref)
    listed = listed_ref[cross_full(listed_ref)[2] :].astype(jnp.float32)
    listing = listed.shape[0] // 2
    pick(place_ref, counts_ref, listed[:listing], flat_ref, PART, 2, picked_0)
    pick(place_ref, counts_ref, listed[listing:], flat_ref, PART, 3, picked_1)


def early_kernel(sides, after_ref, *refs):
    piece_refs, (sums_ref, trace_ref) = refs[:-2], refs[-2:]
    pieces = [side_full(ref) for ref in piece_refs[:sides]] + [cross_full(ref) for ref in piece_refs[sides:]]
    add_cross(pieces, trace_ref, FULL, sums_ref)


def full_kernel(before_ref, *refs):
    piece_refs, (flat_ref, trace_ref, cross_ref) = refs[:-3], refs[-3:]
    add_cross([cross_full(ref) for ref in piece_refs], trace_ref, FULL, cross_ref, before_ref)
    turn_blocks(cross_ref, FULL, flat_ref)


def far_kernel(mq, place_ref, counts_ref, listed_ref, flat_ref, after_ref, picked_ref):
    listed = listed_ref[cross_full(listed_ref)[2] :].astype(jnp.float32)
    listing = listed.shape[0] // 2
    listed = listed[(mq % 2) * listing : (mq % 2 + 1) * listing]
    pick(place_ref, counts_ref, listed, flat_ref, FULL, mq, picked_ref)


def near_kernel(
    place_ref, counts_ref, own_pairs_ref, near_pairs_ref, part_ref, full_ref, part_0, full_0, full_1, *part_1
):
    listed = listing_of(near_pairs_ref, LANES)
    pick(place_ref, counts_ref, listed, part_ref, PART, 1, *part_1)
    pick(place_ref, counts_ref, listed, full_ref, FULL, 1, full_1)
    listed = listing_of(own_pairs_ref, LANES)
    pick(place_ref, counts_ref, listed, part_ref, PART, 0, part_0)
    pick(place_ref, counts_ref, listed, full_ref, FULL, 0, full_0)


def both_rounds(rows, sign):
    row = lax.broadcasted_iota(jnp.int32, rows.shape, 0)
    rows = rows * jnp.where(row < rows.shape[0] // 2, 1.0, sign)
    empty = jnp.zeros_like(rows)
    return jnp.concatenate(
        [jnp.concatenate([rows, empty], axis=1), jnp.concatenate([empty, rows], axis=1)]
    )


def halves(table):
    high = table.astype(jnp.bfloat16)
    return high, (table - high.astype(jnp.float32)).astype(jnp.bfloat16)


def first_lags_kernel(groups, place_ref, inverse_ref, *refs):
    part_0, part_2, part_3, full_0, full_1, *part_1, lags_ref, table_ref = refs
    count, held = part_0.shape[0], full_0.shape[0]
    part_1 = jnp.concatenate([ref[...] for ref in part_1])
    parts = [part_0[...], part_2[...], part_1, part_3[...]]
    full_refs = [full_0, full_1]
    samples = inverse_ref.shape[1]
    quarter, _ = place_of(place_ref, groups)
    low = quarter % 2
    sign = jnp.where(quarter // 2 == low, 1.0, -1.0)

    def part_table(which):
        start = pl.multiple_of((low ^ which) * 2 * PART, 2 * PART)
        return both_rounds(inverse_ref[pl.ds(start, 2 * PART), :], sign)

    def full_table(mq):
        start = pl.multiple_of(samples // 2 + (quarter ^ mq) * 2 * FULL, 2 * FULL)
        return both_rounds(inverse_ref[pl.ds(start, 2 * FULL), :], sign)

    near, other = halves(part_table(0)), halves(part_table(1))
    picked = jnp.concatenate(parts, axis=1)
    lags = 0.0
    for which in range(2):
        table = jnp.concatenate([near[which], near[which], other[which], other[which]])
        lags += jnp.dot(picked, table, preferred_element_type=jnp.float32)
    packs = count // held
    here = [halves(full_table(m)) for m in (0, 1)]
    away = [halves(full_table(m)) for m in (2, 3)]
    picked = jnp.concatenate([ref[...] for ref in full_refs], axis=1)
    for pack in range(packs):
        more = 0.0
        for which in range(2):
            def placed(table):
                empty = jnp.zeros_like(table)
                return jnp.concatenate([table if at == pack else empty for at in range(packs)])

            more += jnp.dot(
                picked,
                jnp.concatenate([placed(table[which]) for table in here]),
                preferred_element_type=jnp.float32,
            )
            table_ref[pack, which] = jnp.concatenate([placed(table[which]) for table in away])
        total = lags[pack * held : (pack + 1) * held] + more
        for step_round in range(2):
            lags_ref[step_round, pack * held : (pack + 1) * held] = total[
                :, step_round * samples : (step_round + 1) * samples
            ]


def lag_kernel(first_ref, table_ref, *refs):
    picked_refs, lags_ref = refs[:-1], refs[-1]
    samples = lags_ref.shape[2]
    held = picked_refs[0].shape[0]
    picked = jnp.concatenate([ref[...] for ref in picked_refs], axis=1)
    for pack in range(table_ref.shape[0]):
        more = jnp.dot(picked, table_ref[pack, 0], preferred_element_type=jnp.float32)
        more += jnp.dot(picked, table_ref[pack, 1], preferred_element_type=jnp.float32)
        for step_round in range(2):
            lags_ref[step_round, pack * held : (pack + 1) * held] = (
                first_ref[step_round, pack * held : (pack + 1) * held]
                + more[:, step_round * samples : (step_round + 1) * samples]
            )


def on_device(windows, counts, pairs):
    comps, _, events, samples = windows.shape
    cells = lax.axis_size("cell")
    half, groups = cells // 2, cells // 4
    count = pairs.shape[2]
    inverse = jnp.asarray(inverse_table(samples, cells))
    place = lax.axis_index("cell").astype(jnp.int32).reshape(1)

    def swap(x, mask):
        return lax.ppermute(x, "cell", [(i, i ^ mask) for i in range(cells)])

    def shape(*dims, dtype=jnp.bfloat16):
        return jax.ShapeDtypeStruct(dims, dtype)

    vmem = pl.BlockSpec(memory_space=pltpu.VMEM)
    smem = pl.BlockSpec(memory_space=pltpu.SMEM)
    params = pltpu.CompilerParams(vmem_limit_bytes=VMEM_LIMIT)

    def cost(microseconds):
        return pl.CostEstimate(
            flops=int(microseconds * 1e9), bytes_accessed=2**20, transcendentals=0
        )

    windows = windows.reshape(comps, 2, groups, 2 * SLOTS, samples)
    near_windows, near_pairs = swap(windows, 1), swap(pairs, 1)
    part_rows, full_rows = comps * 2 * PART, comps * 2 * FULL
    part_spectra, full_spectra, table = pl.pallas_call(
        own_kernel,
        out_shape=[
            shape(groups, part_rows, LANES),
            shape(2 * groups, full_rows, LANES),
            shape(2 * PART + 4 * FULL, samples),
        ],
        in_specs=[smem, vmem],
        out_specs=[vmem] * 3,
        compiler_params=params,
        cost_estimate=cost(1),
        name="own_spectra",
    )(place, windows)
    listing = 2 * pairs.size // LANES
    pieces = pl.pallas_call(
        near_spectra_kernel,
        out_shape=[shape(2 * (part_rows + full_rows), LANES)] * groups
        + [shape(2 * full_rows + listing * (mg == 0), LANES) for mg in range(groups)],
        in_specs=[smem] + [vmem] * 6,
        out_specs=[vmem] * (2 * groups),
        compiler_params=params,
        cost_estimate=cost(1),
        name="near_spectra",
    )(place, pairs, near_pairs, table, part_spectra, full_spectra, near_windows)
    arrived = [pieces[0]] + [swap(pieces[m], 2 * m) for m in range(1, 2 * groups)]
    sides, far = arrived[:groups], arrived[groups:]

    part_flat, part_2, part_3 = pl.pallas_call(
        part_kernel,
        out_shape=[shape(2, 2, SLOTS * SLOTS * PART // LANES, 2 * LANES)] + [shape(count, 4 * PART)] * 2,
        in_specs=[smem, smem] + [vmem] * (1 + groups),
        out_specs=[vmem] * 3,
        scratch_shapes=[
            pltpu.VMEM((padded(groups * 2 * comps) * 2 * PART, LANES), jnp.float32),
            pltpu.VMEM((2 * SLOTS * 2 * PART, LANES), jnp.float32),
        ],
        compiler_params=params,
        cost_estimate=cost(4),
        name="part",
    )(place, counts, far[0], *sides)
    part_2, part_3 = swap(part_2, half), swap(part_3, half + 1)
    packed = count * 4 * FULL // LANES
    early, late = far[: groups - 2], far[groups - 2 :]
    sums = pl.pallas_call(
        functools.partial(early_kernel, groups),
        out_shape=shape(2 * SLOTS * 2 * FULL, LANES, dtype=jnp.float32),
        in_specs=[pl.BlockSpec(memory_space=pl.ANY)] + [vmem] * (groups + len(early)),
        out_specs=vmem,
        scratch_shapes=[
            pltpu.VMEM((padded((groups + len(early)) * 2 * comps) * 2 * FULL, LANES), jnp.float32)
        ],
        compiler_params=params,
        cost_estimate=cost(0.001),
        name="early",
    )(part_flat, *sides, *early)
    full_flat = pl.pallas_call(
        full_kernel,
        out_shape=shape(2, 2, SLOTS * SLOTS * FULL // LANES, 2 * LANES),
        in_specs=[vmem] * (1 + len(late)),
        out_specs=vmem,
        scratch_shapes=[
            pltpu.VMEM((padded(len(late) * 2 * comps) * 2 * FULL, LANES), jnp.float32),
            pltpu.VMEM((2 * SLOTS * 2 * FULL, LANES), jnp.float32),
        ],
        compiler_params=params,
        cost_estimate=cost(10),
        name="full",
    )(sums, *late)
    part_0, full_0, *near = pl.pallas_call(
        near_kernel,
        out_shape=[shape(count, LANES)] + [shape(packed, LANES)] * 2 + [shape(count // 2, LANES)] * 2,
        in_specs=[smem, smem] + [vmem] * 4,
        out_specs=[vmem] * 5,
        compiler_params=params,
        cost_estimate=cost(0.001),
        name="near",
    )(place, counts, pairs, near_pairs, part_flat, full_flat)
    near = [swap(x, 1) for x in near]

    def far_full(mq, after):
        picked = pl.pallas_call(
            functools.partial(far_kernel, mq),
            out_shape=shape(packed, LANES),
            in_specs=[smem, smem, vmem, vmem, pl.BlockSpec(memory_space=pl.ANY)],
            out_specs=vmem,
            compiler_params=params,
            cost_estimate=cost(0.001),
            name=f"far_{mq}",
        )(place, counts, far[0], full_flat, after)
        return swap(picked, half + mq % 2)

    full_2, full_3 = far_full(2, part_2), far_full(3, part_3)

    first, tables = pl.pallas_call(
        functools.partial(first_lags_kernel, groups),
        out_shape=[
            shape(2, count, samples, dtype=jnp.float32),
            shape(count // packed, 2, 2 * LANES, 2 * samples),
        ],
        in_specs=[smem] + [vmem] * 8,
        out_specs=[vmem] * 2,
        compiler_params=params,
        cost_estimate=cost(0.001),
        name="first_lags",
    )(place, inverse, part_0, part_2, part_3, full_0, *near)
    return pl.pallas_call(
        lag_kernel,
        out_shape=shape(2, count, samples, dtype=jnp.float32),
        in_specs=[vmem] * 4,
        out_specs=vmem,
        compiler_params=params,
        cost_estimate=cost(1),
        name="lags",
    )(first, tables, full_2, full_3)


def solution(mesh):
    in_specs = (P(None, "cell", "grp", None), P("grp"), P(None, None, ("grp", "cell")))
    out_specs = P(None, ("grp", "cell"), None)
    return jax.shard_map(
        on_device, mesh=mesh, in_specs=in_specs, out_specs=out_specs, check_vma=False
    )
```

time: 49.5 us -> 45.2 us (0.913)
  waiting for transfers between devices: 19.8 us -> 12 us
  Pallas kernels: 9.6 us -> 14.7 us
  starting transfers between devices: 18.7 us -> 17 us
    ppermute x15 -> x16, waiting for transfers between devices: 19.8 us -> 12 us  [swap(): return lax.ppermute(x, 'cell', [(i, i ^ mask) for i in range(cells)])]
    pallas_call x6 -> x10, Pallas kernels: 9.6 us -> 14.7 us  [the longest x1 3.86 us: on_device(): pl.pallas_call(part_kernel, out_shape=[shape(2, 2, SLOTS * SLOTS * PART /...]
    ppermute x15 -> x16, starting transfers between devices: 18.7 us -> 17 us  [swap(): return lax.ppermute(x, 'cell', [(i, i ^ mask) for i in range(cells)])]
  transfers between devices with their start and end apart: 15 -> 16, of which waited for: 8 -> 6; matrix products, arithmetic and copies ran while one was open for 0% -> 0% of each run, Pallas kernels for 8% -> 28%
where the time goes in v7:
time: 45.2 us; the launch traced here: 45 us
  starting transfers between devices  17 us (38%)
  Pallas kernels  14.7 us (33%)
  waiting for transfers between devices  12 us (27%)
  local copies, waits for them, and re-layouts  1.15 us (3%)
    ppermute x16, starting transfers between devices, swap(): return lax.ppermute(x, 'cell', [(i, i ^ mask) for i in range(cells)])  17 us
    ppermute x16, waiting for transfers between devices, swap(): return lax.ppermute(x, 'cell', [(i, i ^ mask) for i in range(cells)])  12 us
    pallas_call x1, Pallas kernels, on_device(): pl.pallas_call(part_kernel, out_shape=[shape(2, 2, SLOTS * SLOTS * PART /...  3.86 us
    pallas_call x2, Pallas kernels, far_full(): pl.pallas_call(functools.partial(far_kernel, mq), out_shape=shape(packed,...  2.55 us
    pallas_call x1, Pallas kernels, on_device(): pl.pallas_call(near_kernel, out_shape=[shape(count, LANES)] + [shape(pack...  2.5 us
    pallas_call x1, Pallas kernels, on_device(): pl.pallas_call(lag_kernel, out_shape=shape(2, count, samples, dtype=jnp.f...  1.41 us
    unnamed x8, local copies, waits for them, and re-layouts  1.15 us
    pallas_call x1, Pallas kernels, on_device(): pl.pallas_call(functools.partial(first_lags_kernel, groups), out_shape=[s...  1.01 us
  transfers between devices with their start and end apart: 16, of which 6 were waited for; matrix products, arithmetic and copies ran while one was open for 0% of the time, Pallas kernels for 28%

profile of v7, /device:TPU:0, one launch (start us, length us, event | category | flops | bytes accessed | tf_op | source)
XLA Modules:
  0.0 45.0 jit_solution(4156991492112843775)
XLA Ops:
  0.0 0.5 %collective-permute-start.1 = (bf16[3,2,4,64,256]{4,3,2,1,0:T(8,128)(2,1)}, bf16[3,2,4,64,256]{4,3,2,1,0:T(8,128)(2,1)S(1)}, u32[]{:S(2)}, u32[]{:S(2)}) collective-permute-start(bf16[3,2,4,64,256]{4,3,2,1,0:T(8,128)(2,1)} %bitcast.2), channel_id=1, source_target_pairs={{0,1},{1,0},{2,3},{3,2},{4,5},{5,4},{6,7},{7,6},{8,9},{9,8},{10,11... | collective-permute-start | bytes 2359304 | tf_op jit(solution)/shard_map/ppermute | solution.py:392
  0.5 0.1 collective-permute-start
  0.5 0.0 copy-start.3
  0.5 1.1 %copy-done.3 = bf16[3,1,512,256]{3,2,1,0:T(8,128)(2,1)S(1)} copy-done((bf16[3,1,512,256]{3,2,1,0:T(8,128)(2,1)S(1)}, bf16[3,1,512,256]{3,2,1,0:T(8,128)(2,1)}, u32[]{:S(2)}) %copy-start.3) | copy-done | bytes 786456
  1.6 0.9 %own_spectra.1 = (bf16[4,192,128]{2,1,0:T(8,128)(2,1)S(1)}, bf16[8,96,128]{2,1,0:T(8,128)(2,1)S(1)}, bf16[128,256]{1,0:T(8,128)(2,1)S(1)}) custom-call(s32[1]{0:T(128)} %bitcast.place_ref, bf16[3,2,4,64,256]{4,3,2,1,0:T(8,128)(2,1)S(1)} %bitcast.3), custom_call_target="tpu_custom_call" | custom-call | flops 1000000000 | bytes 1048576 | tf_op jit(solution)/shard_map/own_spectra/pallas_call | solution.py:409
  2.5 0.1 collective-permute-done.near_pairs_ref
  2.6 0.0 collective-permute-done.1.windows_ref
  2.6 0.0 copy-done.1
  2.6 0.8 %near_spectra.1 = (bf16[576,128]{1,0:T(8,128)(2,1)S(1)}, bf16[576,128]{1,0:T(8,128)(2,1)S(1)}, bf16[576,128]{1,0:T(8,128)(2,1)S(1)}, bf16[576,128]{1,0:T(8,128)(...) custom-call(s32[1]{0:T(128)} %bitcast.place_ref, ...), custom_call_target="tpu_custom_call" | custom-call | flops 1000000000 | bytes 1048576 | tf_op jit(solution)/shard_map/near_spectra/pallas_call | solution.py:423
  3.4 3.0 %collective-permute-start.3 = (bf16[576,128]{1,0:T(8,128)(2,1)S(1)}, bf16[576,128]{1,0:T(8,128)(2,1)S(1)}, u32[]{:S(2)}, u32[]{:S(2)}) collective-permute-start(bf16[576,128]{1,0:T(8,128)(2,1)S(1)} %get-tuple-element.31), channel_id=1, source_target_pairs={{0,2},{1,3},{2,0},{3,1},{4,6},{5,7},{6,4},{7,5},{8,10},{9,11},{10,... | collective-permute-start | bytes 442376 | tf_op jit(solution)/shard_map/ppermute | solution.py:392
  6.4 1.6 %collective-permute-start.4 = (bf16[576,128]{1,0:T(8,128)(2,1)S(1)}, bf16[576,128]{1,0:T(8,128)(2,1)S(1)}, u32[]{:S(2)}, u32[]{:S(2)}) collective-permute-start(bf16[576,128]{1,0:T(8,128)(2,1)S(1)} %get-tuple-element.32), channel_id=1, source_target_pairs={{0,4},{1,5},{2,6},{3,7},{4,0},{5,1},{6,2},{7,3},{8,12},{9,13},{10,... | collective-permute-start | bytes 442376 | tf_op jit(solution)/shard_map/ppermute | solution.py:392
  8.0 0.0 collective-permute-start.5
  8.0 3.0 %collective-permute-start.2 = (bf16[224,128]{1,0:T(8,128)(2,1)S(1)}, bf16[224,128]{1,0:T(8,128)(2,1)S(1)}, u32[]{:S(2)}, u32[]{:S(2)}) collective-permute-start(bf16[224,128]{1,0:T(8,128)(2,1)S(1)} %get-tuple-element.29), channel_id=1, source_target_pairs={{0,8},{1,9},{2,10},{3,11},{4,12},{5,13},{6,14},{7,15},{8,0},{9,1},... | collective-permute-start | bytes 172040 | tf_op jit(solution)/shard_map/ppermute | solution.py:392
  11.0 1.3 %collective-permute-start.6 = (bf16[192,128]{1,0:T(8,128)(2,1)S(1)}, bf16[192,128]{1,0:T(8,128)(2,1)S(1)}, u32[]{:S(2)}, u32[]{:S(2)}) collective-permute-start(bf16[192,128]{1,0:T(8,128)(2,1)S(1)} %get-tuple-element.35), channel_id=1, source_target_pairs={{0,10},{1,11},{2,8},{3,9},{4,14},{5,15},{6,12},{7,13},{8,2},{9,3},... | collective-permute-start | bytes 147464 | tf_op jit(solution)/shard_map/ppermute | solution.py:392
  12.3 3.7 %collective-permute-done.2.listed_ref.refs_4_ = bf16[224,128]{1,0:T(8,128)(2,1)S(1)} collective-permute-done((bf16[224,128]{1,0:T(8,128)(2,1)S(1)}, bf16[224,128]{1,0:T(8,128)(2,1)S(1)}, u32[]{:S(2)}, u32[]{:S(2)}) %collective-permute-start.2) | collective-permute-done | bytes 57376 | tf_op jit(solution)/shard_map/ppermute | solution.py:392
  16.0 2.6 %collective-permute-start.7 = (bf16[192,128]{1,0:T(8,128)(2,1)S(1)}, bf16[192,128]{1,0:T(8,128)(2,1)S(1)}, u32[]{:S(2)}, u32[]{:S(2)}) collective-permute-start(bf16[192,128]{1,0:T(8,128)(2,1)S(1)} %get-tuple-element.36), channel_id=1, source_target_pairs={{0,12},{1,13},{2,14},{3,15},{4,8},{5,9},{6,10},{7,11},{8,4},{9,5},... | collective-permute-start | bytes 147464 | tf_op jit(solution)/shard_map/ppermute | solution.py:392
  18.6 0.0 collective-permute-done.3.refs_1_
  18.6 1.2 %collective-permute-start.8 = (bf16[192,128]{1,0:T(8,128)(2,1)S(1)}, bf16[192,128]{1,0:T(8,128)(2,1)S(1)}, u32[]{:S(2)}, u32[]{:S(2)}) collective-permute-start(bf16[192,128]{1,0:T(8,128)(2,1)S(1)} %get-tuple-element.37), channel_id=1, source_target_pairs={{0,14},{1,15},{2,12},{3,13},{4,10},{5,11},{6,8},{7,9},{8,6},{9,7},... | collective-permute-start | bytes 147464 | tf_op jit(solution)/shard_map/ppermute | solution.py:392
  19.8 0.0 collective-permute-done.4.refs_2_
  19.8 0.0 collective-permute-done.5.refs_3_
  19.8 0.0 copy-done.2
  19.8 3.9 %part.1 = (bf16[2,2,256,256]{3,2,1,0:T(8,128)(2,1)S(1)}, bf16[512,128]{1,0:T(8,128)(2,1)S(1)}, bf16[512,128]{1,0:T(8,128)(2,1)S(1)}) custom-call(s32[1]{0:T(128)} %bitcast.place_ref, s32[16]{0:T(128)S(1)} %copy-done.2, bf16[224,128]{1,0:T(8,128)(2,1)S(1)} %collective-permute-done.2.listed_ref.refs_4_, bf16[576,128]{1,0:T(8,128)(2,1)S(1)} %get-tuple-element.30.refs_0_, ...), custom_call_target="tpu_custom_call" | custom-call | flops 4000000000 | bytes 1048576 | tf_op jit(solution)/shard_map/part/pallas_call | solution.py:436
  23.6 2.0 %collective-permute-start.9 = (bf16[512,128]{1,0:T(8,128)(2,1)S(1)}, bf16[512,128]{1,0:T(8,128)(2,1)S(1)}, u32[]{:S(2)}, u32[]{:S(2)}) collective-permute-start(bf16[512,128]{1,0:T(8,128)(2,1)S(1)} %get-tuple-element.39), channel_id=1, source_target_pairs={{0,8},{1,9},{2,10},{3,11},{4,12},{5,13},{6,14},{7,15},{8,0},{9,1},... | collective-permute-start | bytes 393224 | tf_op jit(solution)/shard_map/ppermute | solution.py:392
  25.6 0.0 collective-permute-start.10
  25.6 0.0 collective-permute-done.6.refs_5_
  25.6 0.7 %early.1.before_ref = f32[2048,128]{1,0:T(8,128)S(1)} custom-call(bf16[2,2,256,256]{3,2,1,0:T(8,128)(2,1)S(1)} %get-tuple-element.34.after_ref.part_ref, bf16[576,128]{1,0:T(8,128)(2,1)S(1)} %get-tuple-element.30.refs_0_, bf16[576,128]{1,0:T(8,128)(2,1)S(1)} %collective-permute-done.3.refs_1_, bf16[576,128]{1,0:T(8,128)(2,1)S(1)} %collective-permute-done.4.refs_2_, ...), custom_call_target="tpu_custom_call" | custom-call | flops 1000000 | bytes 1048576 | tf_op jit(solution)/shard_map/early/pallas_call | solution.py:452
  26.3 0.0 collective-permute-done.7.refs_0_
  26.3 0.0 collective-permute-done.8.refs_1_
  26.4 1.0 %full.1.full_ref.flat_ref = bf16[2,2,128,256]{3,2,1,0:T(8,128)(2,1)S(1)} custom-call(f32[2048,128]{1,0:T(8,128)S(1)} %early.1.before_ref, bf16[192,128]{1,0:T(8,128)(2,1)S(1)} %collective-permute-done.7.refs_0_, bf16[192,128]{1,0:T(8,128)(2,1)S(1)} %collective-permute-done.8.refs_1_), custom_call_target="tpu_custom_call" | custom-call | flops 10000000000 | bytes 1048576 | tf_op jit(solution)/shard_map/full/pallas_call | solution.py:464
  27.3 2.5 %near.1 = (bf16[512,128]{1,0:T(8,128)(2,1)S(1)}, bf16[256,128]{1,0:T(8,128)(2,1)S(1)}, bf16[256,128]{1,0:T(8,128)(2,1)S(1)}, bf16[256,128]{1,0:T(8,128)(2,1)S(1)}, bf16[256,128]{1,0:T(8,128)(2,1)S(1)}) custom-call(s32[1]{0:T(128)} %bitcast.place_ref, s32[16]{0:T(128)S(1)} %copy-done.2, s32[2,2,512]{2,1,0:T(2,128)S(1)} %copy-done.1, ...), custom_call_target="tpu_custom_call" | custom-call | flops 1000000 | bytes 1048576 | tf_op jit(solution)/shard_map/near/pallas_call | solution.py:477
  29.9 1.2 %collective-permute-start.11 = (bf16[256,128]{1,0:T(8,128)(2,1)S(1)}, bf16[256,128]{1,0:T(8,128)(2,1)S(1)}, u32[]{:S(2)}, u32[]{:S(2)}) collective-permute-start(bf16[256,128]{1,0:T(8,128)(2,1)S(1)} %get-tuple-element.42), channel_id=1, source_target_pairs={{0,1},{1,0},{2,3},{3,2},{4,5},{5,4},{6,7},{7,6},{8,9},{9,8},{10,11... | collective-permute-start | bytes 196616 | tf_op jit(solution)/shard_map/ppermute | solution.py:392
  31.1 0.1 collective-permute-start.12
  31.1 0.4 collective-permute-start.13
  31.6 2.3 %collective-permute-done.9.refs_1_.after_ref = bf16[512,128]{1,0:T(8,128)(2,1)S(1)} collective-permute-done((bf16[512,128]{1,0:T(8,128)(2,1)S(1)}, bf16[512,128]{1,0:T(8,128)(2,1)S(1)}, u32[]{:S(2)}, u32[]{:S(2)}) %collective-permute-start.9) | collective-permute-done | bytes 131104 | tf_op jit(solution)/shard_map/ppermute | solution.py:392
  33.8 1.3 %far_2.1 = bf16[256,128]{1,0:T(8,128)(2,1)S(1)} custom-call(s32[1]{0:T(128)} %bitcast.place_ref, s32[16]{0:T(128)S(1)} %copy-done.2, bf16[224,128]{1,0:T(8,128)(2,1)S(1)} %collective-permute-done.2.listed_ref.refs_4_, bf16[2,2,128,256]{3,2,1,0:T(8,128)(2,1)S(1)} %full.1.full_ref.flat_ref, bf16[512,128]{1,0:T(8,128)(2,1)S(1)} %collective-permute-done.9.refs_1_.after_ref), custom_call_target="tpu_custom_call" | custom-call | flops 1000000 | bytes 1048576 | tf_op jit(solution)/shard_map/far_2/pallas_call | solution.py:489
  35.1 0.0 copy-start
  35.1 0.1 collective-permute-start.14
  35.2 1.3 %collective-permute-done.10.refs_2_.after_ref = bf16[512,128]{1,0:T(8,128)(2,1)S(1)} collective-permute-done((bf16[512,128]{1,0:T(8,128)(2,1)S(1)}, bf16[512,128]{1,0:T(8,128)(2,1)S(1)}, u32[]{:S(2)}, u32[]{:S(2)}) %collective-permute-start.10) | collective-permute-done | bytes 131104 | tf_op jit(solution)/shard_map/ppermute | solution.py:392
  36.5 1.3 %far_3.1 = bf16[256,128]{1,0:T(8,128)(2,1)S(1)} custom-call(s32[1]{0:T(128)} %bitcast.place_ref, s32[16]{0:T(128)S(1)} %copy-done.2, bf16[224,128]{1,0:T(8,128)(2,1)S(1)} %collective-permute-done.2.listed_ref.refs_4_, bf16[2,2,128,256]{3,2,1,0:T(8,128)(2,1)S(1)} %full.1.full_ref.flat_ref, bf16[512,128]{1,0:T(8,128)(2,1)S(1)} %collective-permute-done.10.refs_2_.after_ref), custom_call_target="tpu_custom_call" | custom-call | flops 1000000 | bytes 1048576 | tf_op jit(solution)/shard_map/far_3/pallas_call | solution.py:489
  37.8 0.1 collective-permute-start.15
  37.9 0.0 collective-permute-done.11.refs_4_
  37.9 0.0 collective-permute-done.12.refs_5_
  37.9 0.0 collective-permute-done.13.refs_6_
  37.9 0.0 copy-done
  38.0 1.0 %first_lags.1 = (f32[2,512,256]{2,1,0:T(8,128)S(1)}, bf16[2,2,256,512]{3,2,1,0:T(8,128)(2,1)S(1)}) custom-call(s32[1]{0:T(128)} %bitcast.place_ref, f32[256,256]{1,0:T(8,128)S(1)} %copy-done, bf16[512,128]{1,0:T(8,128)(2,1)S(1)} %get-tuple-element.38.refs_0_, bf16[512,128]{1,0:T(8,128)(2,1)S(1)} %collective-permute-done.9.refs_1_.after_ref, ...), custom_call_target="tpu_custom_call" | custom-call | flops 1000000 | bytes 1048576 | tf_op jit(solution)/shard_map/first_lags/pallas_call | solution.py:502
  39.0 1.4 %collective-permute-done.14.refs_0_ = bf16[256,128]{1,0:T(8,128)(2,1)S(1)} collective-permute-done((bf16[256,128]{1,0:T(8,128)(2,1)S(1)}, bf16[256,128]{1,0:T(8,128)(2,1)S(1)}, u32[]{:S(2)}, u32[]{:S(2)}) %collective-permute-start.14) | collective-permute-done | bytes 65568 | tf_op jit(solution)/shard_map/ppermute | solution.py:392
  40.4 3.2 %collective-permute-done.15.refs_1_ = bf16[256,128]{1,0:T(8,128)(2,1)S(1)} collective-permute-done((bf16[256,128]{1,0:T(8,128)(2,1)S(1)}, bf16[256,128]{1,0:T(8,128)(2,1)S(1)}, u32[]{:S(2)}, u32[]{:S(2)}) %collective-permute-start.15) | collective-permute-done | bytes 65568 | tf_op jit(solution)/shard_map/ppermute | solution.py:392
  43.6 1.4 %lags.1 = f32[2,512,256]{2,1,0:T(8,128)} custom-call(f32[2,512,256]{2,1,0:T(8,128)S(1)} %get-tuple-element.45.first_ref, bf16[2,2,256,512]{3,2,1,0:T(8,128)(2,1)S(1)} %get-tuple-element.46.table_ref, bf16[256,128]{1,0:T(8,128)(2,1)S(1)} %collective-permute-done.14.refs_0_, bf16[256,128]{1,0:T(8,128)(2,1)S(1)} %collective-permute-done.15.refs_1_), custom_call_target="tpu_custom_call" | custom-call | flops 1000000000 | bytes 1048576 | tf_op jit(solution)/shard_map/lags/pallas_call | solution.py:514
  (2 shorter events, 0.0 us)
Async XLA Ops:
  0.0 2.6 %collective-permute-start.1 = (bf16[3,2,4,64,256]{4,3,2,1,0:T(8,128)(2,1)}, bf16[3,2,4,64,256]{4,3,2,1,0:T(8,128)(2,1)S(1)}, u32[]{:S(2)}, u32[]{:S(2)}) collective-permute-start(bf16[3,2,4,64,256]{4,3,2,1,0:T(8,128)(2,1)} %bitcast.2), channel_id=1, source_target_pairs={{0,1},{1,0},{2,3},{3,2},{4,5},{5,4},{6,7},{7,6},{8,9},{9,8},{10,11... | collective-permute-start | bytes 2359304 | tf_op jit(solution)/shard_map/ppermute | solution.py:392
  0.5 2.1 %collective-permute-start = (s32[2,2,512]{2,1,0:T(2,128)}, s32[2,2,512]{2,1,0:T(2,128)S(1)}, u32[]{:S(2)}, u32[]{:S(2)}) collective-permute-start(s32[2,2,512]{2,1,0:T(2,128)} %own_pairs_ref.3), channel_id=1, source_target_pairs={{0,1},{1,0},{2,3},{3,2},{4,5},{5,4},{6,7},{7,6},{8,9},{9,8},{10,11... | collective-permute-start | bytes 24584 | tf_op jit(solution)/shard_map/ppermute | solution.py:392
  0.5 1.1 %copy-start.3 = (bf16[3,1,512,256]{3,2,1,0:T(8,128)(2,1)S(1)}, bf16[3,1,512,256]{3,2,1,0:T(8,128)(2,1)}, u32[]{:S(2)}) copy-start(bf16[3,1,512,256]{3,2,1,0:T(8,128)(2,1)} %param.4) | copy-start | bytes 2359300
  1.6 0.9 %copy-start.1 = (s32[2,2,512]{2,1,0:T(2,128)S(1)}, s32[2,2,512]{2,1,0:T(2,128)}, u32[]{:S(2)}) copy-start(s32[2,2,512]{2,1,0:T(2,128)} %own_pairs_ref.3) | copy-start | bytes 24580
  3.4 15.1 %collective-permute-start.3 = (bf16[576,128]{1,0:T(8,128)(2,1)S(1)}, bf16[576,128]{1,0:T(8,128)(2,1)S(1)}, u32[]{:S(2)}, u32[]{:S(2)}) collective-permute-start(bf16[576,128]{1,0:T(8,128)(2,1)S(1)} %get-tuple-element.31), channel_id=1, source_target_pairs={{0,2},{1,3},{2,0},{3,1},{4,6},{5,7},{6,4},{7,5},{8,10},{9,11},{10,... | collective-permute-start | bytes 442376 | tf_op jit(solution)/shard_map/ppermute | solution.py:392
  6.4 13.3 %collective-permute-start.4 = (bf16[576,128]{1,0:T(8,128)(2,1)S(1)}, bf16[576,128]{1,0:T(8,128)(2,1)S(1)}, u32[]{:S(2)}, u32[]{:S(2)}) collective-permute-start(bf16[576,128]{1,0:T(8,128)(2,1)S(1)} %get-tuple-element.32), channel_id=1, source_target_pairs={{0,4},{1,5},{2,6},{3,7},{4,0},{5,1},{6,2},{7,3},{8,12},{9,13},{10,... | collective-permute-start | bytes 442376 | tf_op jit(solution)/shard_map/ppermute | solution.py:392
  8.0 11.8 %collective-permute-start.5 = (bf16[576,128]{1,0:T(8,128)(2,1)S(1)}, bf16[576,128]{1,0:T(8,128)(2,1)S(1)}, u32[]{:S(2)}, u32[]{:S(2)}) collective-permute-start(bf16[576,128]{1,0:T(8,128)(2,1)S(1)} %get-tuple-element.33), channel_id=1, source_target_pairs={{0,6},{1,7},{2,4},{3,5},{4,2},{5,3},{6,0},{7,1},{8,14},{9,15},{10,... | collective-permute-start | bytes 442376 | tf_op jit(solution)/shard_map/ppermute | solution.py:392
  8.0 8.0 %collective-permute-start.2 = (bf16[224,128]{1,0:T(8,128)(2,1)S(1)}, bf16[224,128]{1,0:T(8,128)(2,1)S(1)}, u32[]{:S(2)}, u32[]{:S(2)}) collective-permute-start(bf16[224,128]{1,0:T(8,128)(2,1)S(1)} %get-tuple-element.29), channel_id=1, source_target_pairs={{0,8},{1,9},{2,10},{3,11},{4,12},{5,13},{6,14},{7,15},{8,0},{9,1},... | collective-permute-start | bytes 172040 | tf_op jit(solution)/shard_map/ppermute | solution.py:392
  11.0 14.6 %collective-permute-start.6 = (bf16[192,128]{1,0:T(8,128)(2,1)S(1)}, bf16[192,128]{1,0:T(8,128)(2,1)S(1)}, u32[]{:S(2)}, u32[]{:S(2)}) collective-permute-start(bf16[192,128]{1,0:T(8,128)(2,1)S(1)} %get-tuple-element.35), channel_id=1, source_target_pairs={{0,10},{1,11},{2,8},{3,9},{4,14},{5,15},{6,12},{7,13},{8,2},{9,3},... | collective-permute-start | bytes 147464 | tf_op jit(solution)/shard_map/ppermute | solution.py:392
  16.0 10.3 %collective-permute-start.7 = (bf16[192,128]{1,0:T(8,128)(2,1)S(1)}, bf16[192,128]{1,0:T(8,128)(2,1)S(1)}, u32[]{:S(2)}, u32[]{:S(2)}) collective-permute-start(bf16[192,128]{1,0:T(8,128)(2,1)S(1)} %get-tuple-element.36), channel_id=1, source_target_pairs={{0,12},{1,13},{2,14},{3,15},{4,8},{5,9},{6,10},{7,11},{8,4},{9,5},... | collective-permute-start | bytes 147464 | tf_op jit(solution)/shard_map/ppermute | solution.py:392
  18.6 1.2 %copy-start.2 = (s32[16]{0:T(128)S(1)}, s32[16]{0:T(128)}, u32[]{:S(2)}) copy-start(s32[16]{0:T(128)} %counts_ref.7) | copy-start | bytes 196
  18.6 7.8 %collective-permute-start.8 = (bf16[192,128]{1,0:T(8,128)(2,1)S(1)}, bf16[192,128]{1,0:T(8,128)(2,1)S(1)}, u32[]{:S(2)}, u32[]{:S(2)}) collective-permute-start(bf16[192,128]{1,0:T(8,128)(2,1)S(1)} %get-tuple-element.37), channel_id=1, source_target_pairs={{0,14},{1,15},{2,12},{3,13},{4,10},{5,11},{6,8},{7,9},{8,6},{9,7},... | collective-permute-start | bytes 147464 | tf_op jit(solution)/shard_map/ppermute | solution.py:392
  23.6 10.2 %collective-permute-start.9 = (bf16[512,128]{1,0:T(8,128)(2,1)S(1)}, bf16[512,128]{1,0:T(8,128)(2,1)S(1)}, u32[]{:S(2)}, u32[]{:S(2)}) collective-permute-start(bf16[512,128]{1,0:T(8,128)(2,1)S(1)} %get-tuple-element.39), channel_id=1, source_target_pairs={{0,8},{1,9},{2,10},{3,11},{4,12},{5,13},{6,14},{7,15},{8,0},{9,1},... | collective-permute-start | bytes 393224 | tf_op jit(solution)/shard_map/ppermute | solution.py:392
  25.6 10.9 %collective-permute-start.10 = (bf16[512,128]{1,0:T(8,128)(2,1)S(1)}, bf16[512,128]{1,0:T(8,128)(2,1)S(1)}, u32[]{:S(2)}, u32[]{:S(2)}) collective-permute-start(bf16[512,128]{1,0:T(8,128)(2,1)S(1)} %get-tuple-element.40), channel_id=1, source_target_pairs={{0,9},{1,8},{2,11},{3,10},{4,13},{5,12},{6,15},{7,14},{8,1},{9,0},... | collective-permute-start | bytes 393224 | tf_op jit(solution)/shard_map/ppermute | solution.py:392
  29.9 8.1 %collective-permute-start.11 = (bf16[256,128]{1,0:T(8,128)(2,1)S(1)}, bf16[256,128]{1,0:T(8,128)(2,1)S(1)}, u32[]{:S(2)}, u32[]{:S(2)}) collective-permute-start(bf16[256,128]{1,0:T(8,128)(2,1)S(1)} %get-tuple-element.42), channel_id=1, source_target_pairs={{0,1},{1,0},{2,3},{3,2},{4,5},{5,4},{6,7},{7,6},{8,9},{9,8},{10,11... | collective-permute-start | bytes 196616 | tf_op jit(solution)/shard_map/ppermute | solution.py:392
  31.1 6.9 %collective-permute-start.12 = (bf16[256,128]{1,0:T(8,128)(2,1)S(1)}, bf16[256,128]{1,0:T(8,128)(2,1)S(1)}, u32[]{:S(2)}, u32[]{:S(2)}) collective-permute-start(bf16[256,128]{1,0:T(8,128)(2,1)S(1)} %get-tuple-element.43), channel_id=1, source_target_pairs={{0,1},{1,0},{2,3},{3,2},{4,5},{5,4},{6,7},{7,6},{8,9},{9,8},{10,11... | collective-permute-start | bytes 196616 | tf_op jit(solution)/shard_map/ppermute | solution.py:392
  31.1 6.8 %collective-permute-start.13 = (bf16[256,128]{1,0:T(8,128)(2,1)S(1)}, bf16[256,128]{1,0:T(8,128)(2,1)S(1)}, u32[]{:S(2)}, u32[]{:S(2)}) collective-permute-start(bf16[256,128]{1,0:T(8,128)(2,1)S(1)} %get-tuple-element.44), channel_id=1, source_target_pairs={{0,1},{1,0},{2,3},{3,2},{4,5},{5,4},{6,7},{7,6},{8,9},{9,8},{10,11... | collective-permute-start | bytes 196616 | tf_op jit(solution)/shard_map/ppermute | solution.py:392
  35.1 2.8 %copy-start = (f32[256,256]{1,0:T(8,128)S(1)}, f32[256,256]{1,0:T(8,128)}, u32[]{:S(2)}) copy-start(f32[256,256]{1,0:T(8,128)} %constant.6.clone.inverse_ref) | copy-start | bytes 786436
  35.1 5.2 %collective-permute-start.14 = (bf16[256,128]{1,0:T(8,128)(2,1)S(1)}, bf16[256,128]{1,0:T(8,128)(2,1)S(1)}, u32[]{:S(2)}, u32[]{:S(2)}) collective-permute-start(bf16[256,128]{1,0:T(8,128)(2,1)S(1)} %far_2.1), channel_id=1, source_target_pairs={{0,8},{1,9},{2,10},{3,11},{4,12},{5,13},{6,14},{7,15},{8,0},{9,1},... | collective-permute-start | bytes 196616 | tf_op jit(solution)/shard_map/ppermute | solution.py:392
  37.8 5.8 %collective-permute-start.15 = (bf16[256,128]{1,0:T(8,128)(2,1)S(1)}, bf16[256,128]{1,0:T(8,128)(2,1)S(1)}, u32[]{:S(2)}, u32[]{:S(2)}) collective-permute-start(bf16[256,128]{1,0:T(8,128)(2,1)S(1)} %far_3.1), channel_id=1, source_target_pairs={{0,9},{1,8},{2,11},{3,10},{4,13},{5,12},{6,15},{7,14},{8,1},{9,0},... | collective-permute-start | bytes 196616 | tf_op jit(solution)/shard_map/ppermute | solution.py:392

commit v8 on v7

--- a/solution.py
+++ b/solution.py
@@ -48,7 +48,8 @@
 def forward_rows(bins, samples):
     count = bins.shape[0]
     sample = lax.broadcasted_iota(jnp.int32, (2 * count, samples), 1)
-    turn = jnp.concatenate([bins * sample[:count], bins * sample[:count] + samples // 4]) % samples
+    turn = jnp.concatenate([bins * sample[:count], bins * sample[:count] + samples // 4])
+    turn &= samples - 1
     x = jnp.where(turn > samples // 2, turn - samples, turn).astype(jnp.float32) * (2.0 / samples)
     square = x * x
     value = jnp.full(square.shape, COSINE[-1], jnp.float32)
@@ -144,15 +145,16 @@
     cell = high * (cells // 2) + group * 2 + low
     count = listed.shape[0] // 2
     runs = LANES // bins
+    run_bits, bin_bits, lane_bits = (n.bit_length() - 1 for n in (runs, bins, LANES))
     first, second = listed[:count].astype(jnp.int32), listed[count:].astype(jnp.int32)
     far_counts = [counts_ref[cell ^ 1], counts_ref[cell ^ (cells // 2)]]
-    odd = lax.broadcasted_iota(jnp.int32, (count, LANES), 0) % 2
+    odd = lax.broadcasted_iota(jnp.int32, (count, LANES), 0) & 1
     live = (first < counts_ref[cell]) & (second < jnp.where(odd == 1, far_counts[1], far_counts[0]))
     left, right = jnp.where(high == low, first, second), jnp.where(high == low, second, first)
-    spot = jnp.where(live, (left // runs) * SLOTS + right, -1)
-    turned = jnp.concatenate([spot, left % runs]).T
+    spot = jnp.where(live, (left >> run_bits) * SLOTS + right, -1)
+    turned = jnp.concatenate([spot, left & (runs - 1)]).T
     lane = lax.broadcasted_iota(jnp.int32, (LANES, LANES), 1)
-    run = lane // bins
+    run = lane >> bin_bits
     spread = lax.broadcasted_iota(jnp.int32, (2 * LANES, LANES), 0)
     kept = lax.broadcasted_iota(jnp.int32, (2 * LANES, LANES), 1)
     sides = ((high, high), (low, 1 - low))
@@ -193,7 +195,7 @@
     for pack in range(packs):
         folds = []
         for step_round in range(2):
-            place = (pack * 4 + step_round * 2 + spread // LANES) * bins + spread % bins
+            place = (pack * 4 + step_round * 2 + (spread >> lane_bits)) * bins + (spread & (bins - 1))
             folds.append(jnp.where(kept == place, 1.0, 0.0).astype(jnp.bfloat16))
         picked += jnp.dot(
             found[pack * held : (pack + 1) * held],
@@ -278,17 +280,14 @@
     add_cross(pieces, trace_ref, FULL, sums_ref)
 
 
-def full_kernel(before_ref, *refs):
-    piece_refs, (flat_ref, trace_ref, cross_ref) = refs[:-3], refs[-3:]
+def full_kernel(place_ref, counts_ref, listed_ref, before_ref, *refs):
+    piece_refs, (flat_ref, picked_0, picked_1, trace_ref, cross_ref) = refs[:-5], refs[-5:]
     add_cross([cross_full(ref) for ref in piece_refs], trace_ref, FULL, cross_ref, before_ref)
     turn_blocks(cross_ref, FULL, flat_ref)
-
-
-def far_kernel(mq, place_ref, counts_ref, listed_ref, flat_ref, after_ref, picked_ref):
     listed = listed_ref[cross_full(listed_ref)[2] :].astype(jnp.float32)
     listing = listed.shape[0] // 2
-    listed = listed[(mq % 2) * listing : (mq % 2 + 1) * listing]
-    pick(place_ref, counts_ref, listed, flat_ref, FULL, mq, picked_ref)
+    pick(place_ref, counts_ref, listed[:listing], flat_ref, FULL, 2, picked_0)
+    pick(place_ref, counts_ref, listed[listing:], flat_ref, FULL, 3, picked_1)
 
 
 def near_kernel(
@@ -461,11 +460,11 @@
         cost_estimate=cost(0.001),
         name="early",
     )(part_flat, *sides, *early)
-    full_flat = pl.pallas_call(
+    full_flat, full_2, full_3 = pl.pallas_call(
         full_kernel,
-        out_shape=shape(2, 2, SLOTS * SLOTS * FULL // LANES, 2 * LANES),
-        in_specs=[vmem] * (1 + len(late)),
-        out_specs=vmem,
+        out_shape=[shape(2, 2, SLOTS * SLOTS * FULL // LANES, 2 * LANES)] + [shape(packed, LANES)] * 2,
+        in_specs=[smem, smem] + [vmem] * (2 + len(late)),
+        out_specs=[vmem] * 3,
         scratch_shapes=[
             pltpu.VMEM((padded(len(late) * 2 * comps) * 2 * FULL, LANES), jnp.float32),
             pltpu.VMEM((2 * SLOTS * 2 * FULL, LANES), jnp.float32),
@@ -473,31 +472,18 @@
         compiler_params=params,
         cost_estimate=cost(10),
         name="full",
-    )(sums, *late)
+    )(place, counts, far[0], sums, *late)
+    full_2, full_3 = swap(full_2, half), swap(full_3, half + 1)
     part_0, full_0, *near = pl.pallas_call(
         near_kernel,
         out_shape=[shape(count, LANES)] + [shape(packed, LANES)] * 2 + [shape(count // 2, LANES)] * 2,
         in_specs=[smem, smem] + [vmem] * 4,
         out_specs=[vmem] * 5,
         compiler_params=params,
-        cost_estimate=cost(0.001),
+        cost_estimate=cost(0.5),
         name="near",
     )(place, counts, pairs, near_pairs, part_flat, full_flat)
     near = [swap(x, 1) for x in near]
-
-    def far_full(mq, after):
-        picked = pl.pallas_call(
-            functools.partial(far_kernel, mq),
-            out_shape=shape(packed, LANES),
-            in_specs=[smem, smem, vmem, vmem, pl.BlockSpec(memory_space=pl.ANY)],
-            out_specs=vmem,
-            compiler_params=params,
-            cost_estimate=cost(0.001),
-            name=f"far_{mq}",
-        )(place, counts, far[0], full_flat, after)
-        return swap(picked, half + mq % 2)
-
-    full_2, full_3 = far_full(2, part_2), far_full(3, part_3)
 
     first, tables = pl.pallas_call(
         functools.partial(first_lags_kernel, groups),

time: 45.2 us -> 44.3 us (0.980)
  starting transfers between devices: 17 us -> 19.4 us
  waiting for transfers between devices: 12 us -> 10 us
  Pallas kernels: 14.7 us -> 13.6 us
    ppermute x16, starting transfers between devices: 17 us -> 19.4 us  [swap(): return lax.ppermute(x, 'cell', [(i, i ^ mask) for i in range(cells)])]
    ppermute x16, waiting for transfers between devices: 12 us -> 10 us  [swap(): return lax.ppermute(x, 'cell', [(i, i ^ mask) for i in range(cells)])]
    pallas_call x3 -> x1, Pallas kernels: 3.54 us -> 2.48 us  [on_device(): pl.pallas_call(full_kernel, out_shape=[shape(2, 2, SLOTS * SLOTS * FULL /...]
  transfers between devices with their start and end apart: 16 -> 16, of which waited for: 6 -> 6; matrix products, arithmetic and copies ran while one was open for 0% -> 0% of each run, Pallas kernels for 28% -> 26%
where the time goes in v8:
time: 44.3 us; the launch traced here: 44.2 us
  starting transfers between devices  19.4 us (44%)
  Pallas kernels  13.6 us (31%)
  waiting for transfers between devices  10 us (23%)
  local copies, waits for them, and re-layouts  1.15 us (3%)
    ppermute x16, starting transfers between devices, swap(): return lax.ppermute(x, 'cell', [(i, i ^ mask) for i in range(cells)])  19.4 us
    ppermute x16, waiting for transfers between devices, swap(): return lax.ppermute(x, 'cell', [(i, i ^ mask) for i in range(cells)])  10 us
    pallas_call x1, Pallas kernels, on_device(): pl.pallas_call(part_kernel, out_shape=[shape(2, 2, SLOTS * SLOTS * PART /...  3.84 us
    pallas_call x1, Pallas kernels, on_device(): pl.pallas_call(near_kernel, out_shape=[shape(count, LANES)] + [shape(pack...  2.49 us
    pallas_call x1, Pallas kernels, on_device(): pl.pallas_call(full_kernel, out_shape=[shape(2, 2, SLOTS * SLOTS * FULL /...  2.48 us
    pallas_call x1, Pallas kernels, on_device(): pl.pallas_call(lag_kernel, out_shape=shape(2, count, samples, dtype=jnp.f...  1.41 us
    unnamed x8, local copies, waits for them, and re-layouts  1.15 us
    pallas_call x1, Pallas kernels, on_device(): pl.pallas_call(functools.partial(first_lags_kernel, groups), out_shape=[s...  1 us
  transfers between devices with their start and end apart: 16, of which 6 were waited for; matrix products, arithmetic and copies ran while one was open for 0% of the time, Pallas kernels for 26%

profile of v8, /device:TPU:0, one launch (start us, length us, event | category | flops | bytes accessed | tf_op | source)
XLA Modules:
  0.0 44.2 jit_solution(9416141191113504175)
XLA Ops:
  0.0 0.5 %collective-permute-start.1 = (bf16[3,2,4,64,256]{4,3,2,1,0:T(8,128)(2,1)}, bf16[3,2,4,64,256]{4,3,2,1,0:T(8,128)(2,1)S(1)}, u32[]{:S(2)}, u32[]{:S(2)}) collective-permute-start(bf16[3,2,4,64,256]{4,3,2,1,0:T(8,128)(2,1)} %bitcast.2), channel_id=1, source_target_pairs={{0,1},{1,0},{2,3},{3,2},{4,5},{5,4},{6,7},{7,6},{8,9},{9,8},{10,11... | collective-permute-start | bytes 2359304 | tf_op jit(solution)/shard_map/ppermute | solution.py:391
  0.5 0.1 collective-permute-start
  0.5 0.0 copy-start.1
  0.5 1.1 %copy-done.1 = bf16[3,1,512,256]{3,2,1,0:T(8,128)(2,1)S(1)} copy-done((bf16[3,1,512,256]{3,2,1,0:T(8,128)(2,1)S(1)}, bf16[3,1,512,256]{3,2,1,0:T(8,128)(2,1)}, u32[]{:S(2)}) %copy-start.1) | copy-done | bytes 786456
  1.6 0.0 copy-start.2
  1.6 0.8 %own_spectra.1 = (bf16[4,192,128]{2,1,0:T(8,128)(2,1)S(1)}, bf16[8,96,128]{2,1,0:T(8,128)(2,1)S(1)}, bf16[128,256]{1,0:T(8,128)(2,1)S(1)}) custom-call(s32[1]{0:T(128)} %bitcast.place_ref, bf16[3,2,4,64,256]{4,3,2,1,0:T(8,128)(2,1)S(1)} %bitcast.3), custom_call_target="tpu_custom_call" | custom-call | flops 1000000000 | bytes 1048576 | tf_op jit(solution)/shard_map/own_spectra/pallas_call | solution.py:408
  2.5 0.1 collective-permute-done.near_pairs_ref
  2.6 0.0 collective-permute-done.1.windows_ref
  2.6 0.0 copy-done.2
  2.6 0.8 %near_spectra.1 = (bf16[576,128]{1,0:T(8,128)(2,1)S(1)}, bf16[576,128]{1,0:T(8,128)(2,1)S(1)}, bf16[576,128]{1,0:T(8,128)(2,1)S(1)}, bf16[576,128]{1,0:T(8,128)(...) custom-call(s32[1]{0:T(128)} %bitcast.place_ref, ...), custom_call_target="tpu_custom_call" | custom-call | flops 1000000000 | bytes 1048576 | tf_op jit(solution)/shard_map/near_spectra/pallas_call | solution.py:422
  3.4 3.0 %collective-permute-start.3 = (bf16[576,128]{1,0:T(8,128)(2,1)S(1)}, bf16[576,128]{1,0:T(8,128)(2,1)S(1)}, u32[]{:S(2)}, u32[]{:S(2)}) collective-permute-start(bf16[576,128]{1,0:T(8,128)(2,1)S(1)} %get-tuple-element.34), channel_id=1, source_target_pairs={{0,2},{1,3},{2,0},{3,1},{4,6},{5,7},{6,4},{7,5},{8,10},{9,11},{10,... | collective-permute-start | bytes 442376 | tf_op jit(solution)/shard_map/ppermute | solution.py:391
  6.4 1.6 %collective-permute-start.4 = (bf16[576,128]{1,0:T(8,128)(2,1)S(1)}, bf16[576,128]{1,0:T(8,128)(2,1)S(1)}, u32[]{:S(2)}, u32[]{:S(2)}) collective-permute-start(bf16[576,128]{1,0:T(8,128)(2,1)S(1)} %get-tuple-element.35), channel_id=1, source_target_pairs={{0,4},{1,5},{2,6},{3,7},{4,0},{5,1},{6,2},{7,3},{8,12},{9,13},{10,... | collective-permute-start | bytes 442376 | tf_op jit(solution)/shard_map/ppermute | solution.py:391
  8.0 0.0 collective-permute-start.5
  8.0 3.0 %collective-permute-start.2 = (bf16[224,128]{1,0:T(8,128)(2,1)S(1)}, bf16[224,128]{1,0:T(8,128)(2,1)S(1)}, u32[]{:S(2)}, u32[]{:S(2)}) collective-permute-start(bf16[224,128]{1,0:T(8,128)(2,1)S(1)} %get-tuple-element.32), channel_id=1, source_target_pairs={{0,8},{1,9},{2,10},{3,11},{4,12},{5,13},{6,14},{7,15},{8,0},{9,1},... | collective-permute-start | bytes 172040 | tf_op jit(solution)/shard_map/ppermute | solution.py:391
  11.0 1.3 %collective-permute-start.6 = (bf16[192,128]{1,0:T(8,128)(2,1)S(1)}, bf16[192,128]{1,0:T(8,128)(2,1)S(1)}, u32[]{:S(2)}, u32[]{:S(2)}) collective-permute-start(bf16[192,128]{1,0:T(8,128)(2,1)S(1)} %get-tuple-element.38), channel_id=1, source_target_pairs={{0,10},{1,11},{2,8},{3,9},{4,14},{5,15},{6,12},{7,13},{8,2},{9,3},... | collective-permute-start | bytes 147464 | tf_op jit(solution)/shard_map/ppermute | solution.py:391
  12.3 3.7 %collective-permute-done.2.listed_ref.refs_4_ = bf16[224,128]{1,0:T(8,128)(2,1)S(1)} collective-permute-done((bf16[224,128]{1,0:T(8,128)(2,1)S(1)}, bf16[224,128]{1,0:T(8,128)(2,1)S(1)}, u32[]{:S(2)}, u32[]{:S(2)}) %collective-permute-start.2) | collective-permute-done | bytes 57376 | tf_op jit(solution)/shard_map/ppermute | solution.py:391
  16.0 2.5 %collective-permute-start.7 = (bf16[192,128]{1,0:T(8,128)(2,1)S(1)}, bf16[192,128]{1,0:T(8,128)(2,1)S(1)}, u32[]{:S(2)}, u32[]{:S(2)}) collective-permute-start(bf16[192,128]{1,0:T(8,128)(2,1)S(1)} %get-tuple-element.39), channel_id=1, source_target_pairs={{0,12},{1,13},{2,14},{3,15},{4,8},{5,9},{6,10},{7,11},{8,4},{9,5},... | collective-permute-start | bytes 147464 | tf_op jit(solution)/shard_map/ppermute | solution.py:391
  18.5 0.0 collective-permute-done.3.refs_1_
  18.5 0.0 copy-start.3
  18.5 1.3 %collective-permute-start.8 = (bf16[192,128]{1,0:T(8,128)(2,1)S(1)}, bf16[192,128]{1,0:T(8,128)(2,1)S(1)}, u32[]{:S(2)}, u32[]{:S(2)}) collective-permute-start(bf16[192,128]{1,0:T(8,128)(2,1)S(1)} %get-tuple-element.40), channel_id=1, source_target_pairs={{0,14},{1,15},{2,12},{3,13},{4,10},{5,11},{6,8},{7,9},{8,6},{9,7},... | collective-permute-start | bytes 147464 | tf_op jit(solution)/shard_map/ppermute | solution.py:391
  19.8 0.0 collective-permute-done.4.refs_2_
  19.8 0.0 collective-permute-done.5.refs_3_
  19.8 0.0 copy-done.3
  19.8 3.8 %part.1 = (bf16[2,2,256,256]{3,2,1,0:T(8,128)(2,1)S(1)}, bf16[512,128]{1,0:T(8,128)(2,1)S(1)}, bf16[512,128]{1,0:T(8,128)(2,1)S(1)}) custom-call(s32[1]{0:T(128)} %bitcast.place_ref, s32[16]{0:T(128)S(1)} %copy-done.3, bf16[224,128]{1,0:T(8,128)(2,1)S(1)} %collective-permute-done.2.listed_ref.refs_4_, bf16[576,128]{1,0:T(8,128)(2,1)S(1)} %get-tuple-element.33.refs_0_, ...), custom_call_target="tpu_custom_call" | custom-call | flops 4000000000 | bytes 1048576 | tf_op jit(solution)/shard_map/part/pallas_call | solution.py:435
  23.6 1.9 %collective-permute-start.9 = (bf16[512,128]{1,0:T(8,128)(2,1)S(1)}, bf16[512,128]{1,0:T(8,128)(2,1)S(1)}, u32[]{:S(2)}, u32[]{:S(2)}) collective-permute-start(bf16[512,128]{1,0:T(8,128)(2,1)S(1)} %get-tuple-element.43), channel_id=1, source_target_pairs={{0,8},{1,9},{2,10},{3,11},{4,12},{5,13},{6,14},{7,15},{8,0},{9,1},... | collective-permute-start | bytes 393224 | tf_op jit(solution)/shard_map/ppermute | solution.py:391
  25.6 0.0 collective-permute-start.10
  25.6 0.0 collective-permute-done.6.refs_5_
  25.6 0.7 %early.1.before_ref = f32[2048,128]{1,0:T(8,128)S(1)} custom-call(bf16[2,2,256,256]{3,2,1,0:T(8,128)(2,1)S(1)} %get-tuple-element.37.after_ref.part_ref, bf16[576,128]{1,0:T(8,128)(2,1)S(1)} %get-tuple-element.33.refs_0_, bf16[576,128]{1,0:T(8,128)(2,1)S(1)} %collective-permute-done.3.refs_1_, bf16[576,128]{1,0:T(8,128)(2,1)S(1)} %collective-permute-done.4.refs_2_, ...), custom_call_target="tpu_custom_call" | custom-call | flops 1000000 | bytes 1048576 | tf_op jit(solution)/shard_map/early/pallas_call | solution.py:451
  26.3 0.0 collective-permute-done.7.refs_0_
  26.3 0.0 collective-permute-done.8.refs_1_
  26.3 2.5 %full.1 = (bf16[2,2,128,256]{3,2,1,0:T(8,128)(2,1)S(1)}, bf16[256,128]{1,0:T(8,128)(2,1)S(1)}, bf16[256,128]{1,0:T(8,128)(2,1)S(1)}) custom-call(s32[1]{0:T(128)} %bitcast.place_ref, s32[16]{0:T(128)S(1)} %copy-done.3, bf16[224,128]{1,0:T(8,128)(2,1)S(1)} %collective-permute-done.2.listed_ref.refs_4_, f32[2048,128]{1,0:T(8,128)S(1)} %early.1.before_ref, ...), custom_call_target="tpu_custom_call" | custom-call | flops 10000000000 | bytes 1048576 | tf_op jit(solution)/shard_map/full/pallas_call | solution.py:463
  28.8 0.0 copy-start
  28.8 2.5 %near.1 = (bf16[512,128]{1,0:T(8,128)(2,1)S(1)}, bf16[256,128]{1,0:T(8,128)(2,1)S(1)}, bf16[256,128]{1,0:T(8,128)(2,1)S(1)}, bf16[256,128]{1,0:T(8,128)(2,1)S(1)}, bf16[256,128]{1,0:T(8,128)(2,1)S(1)}) custom-call(s32[1]{0:T(128)} %bitcast.place_ref, s32[16]{0:T(128)S(1)} %copy-done.3, s32[2,2,512]{2,1,0:T(2,128)S(1)} %copy-done.2, ...), custom_call_target="tpu_custom_call" | custom-call | flops 500000000 | bytes 1048576 | tf_op jit(solution)/shard_map/near/pallas_call | solution.py:477
  31.3 1.2 %collective-permute-start.11 = (bf16[256,128]{1,0:T(8,128)(2,1)S(1)}, bf16[256,128]{1,0:T(8,128)(2,1)S(1)}, u32[]{:S(2)}, u32[]{:S(2)}) collective-permute-start(bf16[256,128]{1,0:T(8,128)(2,1)S(1)} %get-tuple-element.46), channel_id=1, source_target_pairs={{0,1},{1,0},{2,3},{3,2},{4,5},{5,4},{6,7},{7,6},{8,9},{9,8},{10,11... | collective-permute-start | bytes 196616 | tf_op jit(solution)/shard_map/ppermute | solution.py:391
  32.5 0.1 collective-permute-start.12
  32.6 0.4 collective-permute-start.13
  33.0 0.4 collective-permute-done.11.refs_4_
  33.4 1.9 %collective-permute-start.14 = (bf16[256,128]{1,0:T(8,128)(2,1)S(1)}, bf16[256,128]{1,0:T(8,128)(2,1)S(1)}, u32[]{:S(2)}, u32[]{:S(2)}) collective-permute-start(bf16[256,128]{1,0:T(8,128)(2,1)S(1)} %get-tuple-element.51), channel_id=1, source_target_pairs={{0,8},{1,9},{2,10},{3,11},{4,12},{5,13},{6,14},{7,15},{8,0},{9,1},... | collective-permute-start | bytes 196616 | tf_op jit(solution)/shard_map/ppermute | solution.py:391
  35.3 0.0 collective-permute-done.12.refs_5_
  35.3 0.7 %collective-permute-start.15 = (bf16[256,128]{1,0:T(8,128)(2,1)S(1)}, bf16[256,128]{1,0:T(8,128)(2,1)S(1)}, u32[]{:S(2)}, u32[]{:S(2)}) collective-permute-start(bf16[256,128]{1,0:T(8,128)(2,1)S(1)} %get-tuple-element.52), channel_id=1, source_target_pairs={{0,9},{1,8},{2,11},{3,10},{4,13},{5,12},{6,15},{7,14},{8,1},{9,0},... | collective-permute-start | bytes 196616 | tf_op jit(solution)/shard_map/ppermute | solution.py:391
  36.0 0.0 collective-permute-done.13.refs_6_
  36.0 0.0 collective-permute-done.9.refs_1_
  36.0 0.5 %collective-permute-done.10.refs_2_ = bf16[512,128]{1,0:T(8,128)(2,1)S(1)} collective-permute-done((bf16[512,128]{1,0:T(8,128)(2,1)S(1)}, bf16[512,128]{1,0:T(8,128)(2,1)S(1)}, u32[]{:S(2)}, u32[]{:S(2)}) %collective-permute-start.10) | collective-permute-done | bytes 131104 | tf_op jit(solution)/shard_map/ppermute | solution.py:391
  36.5 0.0 copy-done
  36.5 1.0 %first_lags.1 = (f32[2,512,256]{2,1,0:T(8,128)S(1)}, bf16[2,2,256,512]{3,2,1,0:T(8,128)(2,1)S(1)}) custom-call(s32[1]{0:T(128)} %bitcast.place_ref, f32[256,256]{1,0:T(8,128)S(1)} %copy-done, bf16[512,128]{1,0:T(8,128)(2,1)S(1)} %get-tuple-element.42.refs_0_, bf16[512,128]{1,0:T(8,128)(2,1)S(1)} %collective-permute-done.9.refs_1_, ...), custom_call_target="tpu_custom_call" | custom-call | flops 1000000 | bytes 1048576 | tf_op jit(solution)/shard_map/first_lags/pallas_call | solution.py:488
  37.5 4.1 %collective-permute-done.14.refs_0_ = bf16[256,128]{1,0:T(8,128)(2,1)S(1)} collective-permute-done((bf16[256,128]{1,0:T(8,128)(2,1)S(1)}, bf16[256,128]{1,0:T(8,128)(2,1)S(1)}, u32[]{:S(2)}, u32[]{:S(2)}) %collective-permute-start.14) | collective-permute-done | bytes 65568 | tf_op jit(solution)/shard_map/ppermute | solution.py:391
  41.6 1.2 %collective-permute-done.15.refs_1_ = bf16[256,128]{1,0:T(8,128)(2,1)S(1)} collective-permute-done((bf16[256,128]{1,0:T(8,128)(2,1)S(1)}, bf16[256,128]{1,0:T(8,128)(2,1)S(1)}, u32[]{:S(2)}, u32[]{:S(2)}) %collective-permute-start.15) | collective-permute-done | bytes 65568 | tf_op jit(solution)/shard_map/ppermute | solution.py:391
  42.8 1.4 %lags.1 = f32[2,512,256]{2,1,0:T(8,128)} custom-call(f32[2,512,256]{2,1,0:T(8,128)S(1)} %get-tuple-element.49.first_ref, bf16[2,2,256,512]{3,2,1,0:T(8,128)(2,1)S(1)} %get-tuple-element.50.table_ref, bf16[256,128]{1,0:T(8,128)(2,1)S(1)} %collective-permute-done.14.refs_0_, bf16[256,128]{1,0:T(8,128)(2,1)S(1)} %collective-permute-done.15.refs_1_), custom_call_target="tpu_custom_call" | custom-call | flops 1000000000 | bytes 1048576 | tf_op jit(solution)/shard_map/lags/pallas_call | solution.py:500
Async XLA Ops:
  0.0 2.6 %collective-permute-start.1 = (bf16[3,2,4,64,256]{4,3,2,1,0:T(8,128)(2,1)}, bf16[3,2,4,64,256]{4,3,2,1,0:T(8,128)(2,1)S(1)}, u32[]{:S(2)}, u32[]{:S(2)}) collective-permute-start(bf16[3,2,4,64,256]{4,3,2,1,0:T(8,128)(2,1)} %bitcast.2), channel_id=1, source_target_pairs={{0,1},{1,0},{2,3},{3,2},{4,5},{5,4},{6,7},{7,6},{8,9},{9,8},{10,11... | collective-permute-start | bytes 2359304 | tf_op jit(solution)/shard_map/ppermute | solution.py:391
  0.5 2.1 %collective-permute-start = (s32[2,2,512]{2,1,0:T(2,128)}, s32[2,2,512]{2,1,0:T(2,128)S(1)}, u32[]{:S(2)}, u32[]{:S(2)}) collective-permute-start(s32[2,2,512]{2,1,0:T(2,128)} %own_pairs_ref.3), channel_id=1, source_target_pairs={{0,1},{1,0},{2,3},{3,2},{4,5},{5,4},{6,7},{7,6},{8,9},{9,8},{10,11... | collective-permute-start | bytes 24584 | tf_op jit(solution)/shard_map/ppermute | solution.py:391
  0.5 1.1 %copy-start.1 = (bf16[3,1,512,256]{3,2,1,0:T(8,128)(2,1)S(1)}, bf16[3,1,512,256]{3,2,1,0:T(8,128)(2,1)}, u32[]{:S(2)}) copy-start(bf16[3,1,512,256]{3,2,1,0:T(8,128)(2,1)} %param.4) | copy-start | bytes 2359300
  1.6 0.9 %copy-start.2 = (s32[2,2,512]{2,1,0:T(2,128)S(1)}, s32[2,2,512]{2,1,0:T(2,128)}, u32[]{:S(2)}) copy-start(s32[2,2,512]{2,1,0:T(2,128)} %own_pairs_ref.3) | copy-start | bytes 24580
  3.4 15.1 %collective-permute-start.3 = (bf16[576,128]{1,0:T(8,128)(2,1)S(1)}, bf16[576,128]{1,0:T(8,128)(2,1)S(1)}, u32[]{:S(2)}, u32[]{:S(2)}) collective-permute-start(bf16[576,128]{1,0:T(8,128)(2,1)S(1)} %get-tuple-element.34), channel_id=1, source_target_pairs={{0,2},{1,3},{2,0},{3,1},{4,6},{5,7},{6,4},{7,5},{8,10},{9,11},{10,... | collective-permute-start | bytes 442376 | tf_op jit(solution)/shard_map/ppermute | solution.py:391
  6.4 13.4 %collective-permute-start.4 = (bf16[576,128]{1,0:T(8,128)(2,1)S(1)}, bf16[576,128]{1,0:T(8,128)(2,1)S(1)}, u32[]{:S(2)}, u32[]{:S(2)}) collective-permute-start(bf16[576,128]{1,0:T(8,128)(2,1)S(1)} %get-tuple-element.35), channel_id=1, source_target_pairs={{0,4},{1,5},{2,6},{3,7},{4,0},{5,1},{6,2},{7,3},{8,12},{9,13},{10,... | collective-permute-start | bytes 442376 | tf_op jit(solution)/shard_map/ppermute | solution.py:391
  8.0 11.8 %collective-permute-start.5 = (bf16[576,128]{1,0:T(8,128)(2,1)S(1)}, bf16[576,128]{1,0:T(8,128)(2,1)S(1)}, u32[]{:S(2)}, u32[]{:S(2)}) collective-permute-start(bf16[576,128]{1,0:T(8,128)(2,1)S(1)} %get-tuple-element.36), channel_id=1, source_target_pairs={{0,6},{1,7},{2,4},{3,5},{4,2},{5,3},{6,0},{7,1},{8,14},{9,15},{10,... | collective-permute-start | bytes 442376 | tf_op jit(solution)/shard_map/ppermute | solution.py:391
  8.0 8.0 %collective-permute-start.2 = (bf16[224,128]{1,0:T(8,128)(2,1)S(1)}, bf16[224,128]{1,0:T(8,128)(2,1)S(1)}, u32[]{:S(2)}, u32[]{:S(2)}) collective-permute-start(bf16[224,128]{1,0:T(8,128)(2,1)S(1)} %get-tuple-element.32), channel_id=1, source_target_pairs={{0,8},{1,9},{2,10},{3,11},{4,12},{5,13},{6,14},{7,15},{8,0},{9,1},... | collective-permute-start | bytes 172040 | tf_op jit(solution)/shard_map/ppermute | solution.py:391
  11.0 14.6 %collective-permute-start.6 = (bf16[192,128]{1,0:T(8,128)(2,1)S(1)}, bf16[192,128]{1,0:T(8,128)(2,1)S(1)}, u32[]{:S(2)}, u32[]{:S(2)}) collective-permute-start(bf16[192,128]{1,0:T(8,128)(2,1)S(1)} %get-tuple-element.38), channel_id=1, source_target_pairs={{0,10},{1,11},{2,8},{3,9},{4,14},{5,15},{6,12},{7,13},{8,2},{9,3},... | collective-permute-start | bytes 147464 | tf_op jit(solution)/shard_map/ppermute | solution.py:391
  16.0 10.3 %collective-permute-start.7 = (bf16[192,128]{1,0:T(8,128)(2,1)S(1)}, bf16[192,128]{1,0:T(8,128)(2,1)S(1)}, u32[]{:S(2)}, u32[]{:S(2)}) collective-permute-start(bf16[192,128]{1,0:T(8,128)(2,1)S(1)} %get-tuple-element.39), channel_id=1, source_target_pairs={{0,12},{1,13},{2,14},{3,15},{4,8},{5,9},{6,10},{7,11},{8,4},{9,5},... | collective-permute-start | bytes 147464 | tf_op jit(solution)/shard_map/ppermute | solution.py:391
  18.5 1.3 %copy-start.3 = (s32[16]{0:T(128)S(1)}, s32[16]{0:T(128)}, u32[]{:S(2)}) copy-start(s32[16]{0:T(128)} %counts_ref.5) | copy-start | bytes 196
  18.5 7.8 %collective-permute-start.8 = (bf16[192,128]{1,0:T(8,128)(2,1)S(1)}, bf16[192,128]{1,0:T(8,128)(2,1)S(1)}, u32[]{:S(2)}, u32[]{:S(2)}) collective-permute-start(bf16[192,128]{1,0:T(8,128)(2,1)S(1)} %get-tuple-element.40), channel_id=1, source_target_pairs={{0,14},{1,15},{2,12},{3,13},{4,10},{5,11},{6,8},{7,9},{8,6},{9,7},... | collective-permute-start | bytes 147464 | tf_op jit(solution)/shard_map/ppermute | solution.py:391
  23.6 12.4 %collective-permute-start.9 = (bf16[512,128]{1,0:T(8,128)(2,1)S(1)}, bf16[512,128]{1,0:T(8,128)(2,1)S(1)}, u32[]{:S(2)}, u32[]{:S(2)}) collective-permute-start(bf16[512,128]{1,0:T(8,128)(2,1)S(1)} %get-tuple-element.43), channel_id=1, source_target_pairs={{0,8},{1,9},{2,10},{3,11},{4,12},{5,13},{6,14},{7,15},{8,0},{9,1},... | collective-permute-start | bytes 393224 | tf_op jit(solution)/shard_map/ppermute | solution.py:391
  25.6 10.9 %collective-permute-start.10 = (bf16[512,128]{1,0:T(8,128)(2,1)S(1)}, bf16[512,128]{1,0:T(8,128)(2,1)S(1)}, u32[]{:S(2)}, u32[]{:S(2)}) collective-permute-start(bf16[512,128]{1,0:T(8,128)(2,1)S(1)} %get-tuple-element.44), channel_id=1, source_target_pairs={{0,9},{1,8},{2,11},{3,10},{4,13},{5,12},{6,15},{7,14},{8,1},{9,0},... | collective-permute-start | bytes 393224 | tf_op jit(solution)/shard_map/ppermute | solution.py:391
  28.8 7.7 %copy-start = (f32[256,256]{1,0:T(8,128)S(1)}, f32[256,256]{1,0:T(8,128)}, u32[]{:S(2)}) copy-start(f32[256,256]{1,0:T(8,128)} %constant.6.clone.inverse_ref) | copy-start | bytes 786436
  31.3 2.1 %collective-permute-start.11 = (bf16[256,128]{1,0:T(8,128)(2,1)S(1)}, bf16[256,128]{1,0:T(8,128)(2,1)S(1)}, u32[]{:S(2)}, u32[]{:S(2)}) collective-permute-start(bf16[256,128]{1,0:T(8,128)(2,1)S(1)} %get-tuple-element.46), channel_id=1, source_target_pairs={{0,1},{1,0},{2,3},{3,2},{4,5},{5,4},{6,7},{7,6},{8,9},{9,8},{10,11... | collective-permute-start | bytes 196616 | tf_op jit(solution)/shard_map/ppermute | solution.py:391
  32.5 2.8 %collective-permute-start.12 = (bf16[256,128]{1,0:T(8,128)(2,1)S(1)}, bf16[256,128]{1,0:T(8,128)(2,1)S(1)}, u32[]{:S(2)}, u32[]{:S(2)}) collective-permute-start(bf16[256,128]{1,0:T(8,128)(2,1)S(1)} %get-tuple-element.47), channel_id=1, source_target_pairs={{0,1},{1,0},{2,3},{3,2},{4,5},{5,4},{6,7},{7,6},{8,9},{9,8},{10,11... | collective-permute-start | bytes 196616 | tf_op jit(solution)/shard_map/ppermute | solution.py:391
  32.6 3.4 %collective-permute-start.13 = (bf16[256,128]{1,0:T(8,128)(2,1)S(1)}, bf16[256,128]{1,0:T(8,128)(2,1)S(1)}, u32[]{:S(2)}, u32[]{:S(2)}) collective-permute-start(bf16[256,128]{1,0:T(8,128)(2,1)S(1)} %get-tuple-element.48), channel_id=1, source_target_pairs={{0,1},{1,0},{2,3},{3,2},{4,5},{5,4},{6,7},{7,6},{8,9},{9,8},{10,11... | collective-permute-start | bytes 196616 | tf_op jit(solution)/shard_map/ppermute | solution.py:391
  33.4 8.1 %collective-permute-start.14 = (bf16[256,128]{1,0:T(8,128)(2,1)S(1)}, bf16[256,128]{1,0:T(8,128)(2,1)S(1)}, u32[]{:S(2)}, u32[]{:S(2)}) collective-permute-start(bf16[256,128]{1,0:T(8,128)(2,1)S(1)} %get-tuple-element.51), channel_id=1, source_target_pairs={{0,8},{1,9},{2,10},{3,11},{4,12},{5,13},{6,14},{7,15},{8,0},{9,1},... | collective-permute-start | bytes 196616 | tf_op jit(solution)/shard_map/ppermute | solution.py:391
  35.3 7.5 %collective-permute-start.15 = (bf16[256,128]{1,0:T(8,128)(2,1)S(1)}, bf16[256,128]{1,0:T(8,128)(2,1)S(1)}, u32[]{:S(2)}, u32[]{:S(2)}) collective-permute-start(bf16[256,128]{1,0:T(8,128)(2,1)S(1)} %get-tuple-element.52), channel_id=1, source_target_pairs={{0,9},{1,8},{2,11},{3,10},{4,13},{5,12},{6,15},{7,14},{8,1},{9,0},... | collective-permute-start | bytes 196616 | tf_op jit(solution)/shard_map/ppermute | solution.py:391

commit v9 on v8

--- a/solution.py
+++ b/solution.py
@@ -28,8 +28,8 @@
 TN = (((0,), (0,)), ((), ()))
 VMEM_LIMIT = 40 * 1024 * 1024
 
-PART = 32
-FULL = 16
+PART = 16
+FULL = 24
 
 
 def inverse_table(samples, stations):
@@ -39,8 +39,8 @@
     weight = np.where(np.arange(bins) == 0, 1.0, 2.0)[:, None] / samples
     weight = weight * math.sqrt(samples / (3.0 * stations))
     real, imag = weight * np.cos(angle), -weight * np.sin(angle)
-    runs = [(at, PART) for at in range(0, bins // 2, PART)]
-    runs += [(at, FULL) for at in range(bins // 2, bins, FULL)]
+    runs = [(at, PART) for at in range(0, 2 * PART, PART)]
+    runs += [(at, FULL) for at in range(2 * PART, bins, FULL)]
     rows = [part[at : at + run] for at, run in runs for part in (real, imag)]
     return np.concatenate(rows).astype(np.float32)
 
@@ -96,7 +96,7 @@
     bins = lax.broadcasted_iota(jnp.int32, (PART, samples), 0) + (quarter % 2) * PART
     table_ref[: 2 * PART] = forward_rows(bins, samples)
     for far in range(2):
-        start = samples // 4 + (quarter ^ (2 * far)) * FULL
+        start = 2 * PART + (quarter ^ (2 * far)) * FULL
         bins = lax.broadcasted_iota(jnp.int32, (FULL, samples), 0) + start
         at = 2 * PART + 2 * FULL * far
         table_ref[at : at + 2 * FULL] = forward_rows(bins, samples)
@@ -137,6 +137,38 @@
             cross[at : at + 2 * FULL] = lanes[2 * PART + 2 * FULL :]
 
 
+def width(bins):
+    return 1 << (bins - 1).bit_length()
+
+
+def packing(count, bins):
+    used = 4 * bins
+    spare = LANES - used
+    if not spare:
+        return count, [[(0, 0, 0, used)]]
+    runs = used // spare
+    rows = count // (runs + 1)
+    return rows, [
+        [(at * rows, 0, 0, used), (runs * rows, used, at * spare, (at + 1) * spare)] for at in range(runs)
+    ]
+
+
+def packed_rows(count, bins):
+    rows, parts = packing(count, bins)
+    return rows * len(parts)
+
+
+def unpack(picked, bins):
+    used = 4 * bins
+    spare = LANES - used
+    if not spare:
+        return picked
+    runs = used // spare
+    rows = picked.shape[0] // runs
+    rest = [picked[at * rows : (at + 1) * rows, used:] for at in range(runs)]
+    return jnp.concatenate([picked[:, :used], jnp.concatenate(rest, axis=1)])
+
+
 def pick(place_ref, counts_ref, listed, flat_ref, bins, mq, *picked_refs):
     cells = counts_ref.shape[0]
     quarter, group = place_of(place_ref, cells // 4)
@@ -144,25 +176,25 @@
     high, low = own // 2, own % 2
     cell = high * (cells // 2) + group * 2 + low
     count = listed.shape[0] // 2
-    runs = LANES // bins
-    run_bits, bin_bits, lane_bits = (n.bit_length() - 1 for n in (runs, bins, LANES))
+    runs = LANES // width(bins)
+    run_bits, bin_bits, lane_bits = (n.bit_length() - 1 for n in (runs, width(bins), LANES))
     first, second = listed[:count].astype(jnp.int32), listed[count:].astype(jnp.int32)
     far_counts = [counts_ref[cell ^ 1], counts_ref[cell ^ (cells // 2)]]
     odd = lax.broadcasted_iota(jnp.int32, (count, LANES), 0) & 1
     live = (first < counts_ref[cell]) & (second < jnp.where(odd == 1, far_counts[1], far_counts[0]))
     left, right = jnp.where(high == low, first, second), jnp.where(high == low, second, first)
     spot = jnp.where(live, (left >> run_bits) * SLOTS + right, -1)
-    turned = jnp.concatenate([spot, left & (runs - 1)]).T
+    turned = (spot * runs + (left & (runs - 1))).T
     lane = lax.broadcasted_iota(jnp.int32, (LANES, LANES), 1)
     run = lane >> bin_bits
-    spread = lax.broadcasted_iota(jnp.int32, (2 * LANES, LANES), 0)
-    kept = lax.broadcasted_iota(jnp.int32, (2 * LANES, LANES), 1)
     sides = ((high, high), (low, 1 - low))
     found = []
     for step_round in range(2):
-        hot = []
+        hot, here = [], []
         for at in range(step_round, count, 2):
-            offset = turned[:, at : at + 1] - lane
+            both = jnp.broadcast_to(turned[:, at : at + 1], (LANES, LANES))
+            here.append((both & (runs - 1)) == run)
+            offset = (both >> run_bits) - lane
             hot.append(
                 jnp.concatenate(
                     [
@@ -175,35 +207,37 @@
         block = flat_ref[sides[step_round][0], sides[step_round][1]]
         wide = jnp.dot(jnp.concatenate(hot), block, preferred_element_type=jnp.float32)
         masked = []
-        for chunk, at in enumerate(range(step_round, count, 2)):
-            here = run == turned[:, count + at : count + at + 1]
+        for chunk, mask in enumerate(here):
             part = wide[chunk * LANES : (chunk + 1) * LANES]
             masked.append(
                 jnp.concatenate(
                     [
-                        jnp.where(here, part[:, :LANES], 0.0).astype(jnp.bfloat16),
-                        jnp.where(here, part[:, LANES:], 0.0).astype(jnp.bfloat16),
+                        jnp.where(mask, part[:, :LANES], 0.0).astype(jnp.bfloat16),
+                        jnp.where(mask, part[:, LANES:], 0.0).astype(jnp.bfloat16),
                     ],
                     axis=1,
                 )
             )
         found.append(jnp.concatenate(masked))
     found = jnp.concatenate(found, axis=1)
-    packs = LANES // (4 * bins)
-    held = found.shape[0] // packs
-    picked = 0.0
-    for pack in range(packs):
-        folds = []
-        for step_round in range(2):
-            place = (pack * 4 + step_round * 2 + (spread >> lane_bits)) * bins + (spread & (bins - 1))
-            folds.append(jnp.where(kept == place, 1.0, 0.0).astype(jnp.bfloat16))
-        picked += jnp.dot(
-            found[pack * held : (pack + 1) * held],
-            jnp.concatenate(folds),
-            preferred_element_type=jnp.float32,
-        )
-    picked = picked.astype(jnp.bfloat16)
-    each = held // len(picked_refs)
+    spread = lax.broadcasted_iota(jnp.int32, (4 * LANES, LANES), 0)
+    kept = lax.broadcasted_iota(jnp.int32, (4 * LANES, LANES), 1)
+    bin_of = spread & (width(bins) - 1)
+    value = jnp.where(bin_of < bins, (spread >> lane_bits) * bins + bin_of, -1)
+    rows, parts = packing(found.shape[0], bins)
+    picked = []
+    for entries in parts:
+        total = 0.0
+        for start, at, least, end in entries:
+            fold = (value >= least) & (value < end) & (kept == value + (at - least))
+            total += jnp.dot(
+                found[start : start + rows],
+                jnp.where(fold, 1.0, 0.0).astype(jnp.bfloat16),
+                preferred_element_type=jnp.float32,
+            )
+        picked.append(total.astype(jnp.bfloat16))
+    picked = jnp.concatenate(picked)
+    each = picked.shape[0] // len(picked_refs)
     for at, ref in enumerate(picked_refs):
         ref[...] = picked[at * each : (at + 1) * each]
 
@@ -238,14 +272,17 @@
 
 
 def turn_blocks(cross_ref, bins, flat_ref):
-    slots, runs = 2 * SLOTS, LANES // bins
+    slots, runs = 2 * SLOTS, LANES // width(bins)
+    empty = jnp.zeros((width(bins) - bins, LANES), jnp.float32)
     for own in range(2):
         for at in range(SLOTS // runs):
             for part in range(2):
                 first = part * bins * slots + own * SLOTS + at * runs
-                block = jnp.concatenate(
-                    [cross_ref[pl.ds(first + i, bins, stride=slots), :] for i in range(runs)]
-                ).T.astype(jnp.bfloat16)
+                block = []
+                for i in range(runs):
+                    block.append(cross_ref[pl.ds(first + i, bins, stride=slots), :])
+                    block += [empty] * (bins < width(bins))
+                block = jnp.concatenate(block).T.astype(jnp.bfloat16)
                 for far in range(2):
                     flat_ref[
                         own, far, at * SLOTS : (at + 1) * SLOTS, part * LANES : (part + 1) * LANES
@@ -264,14 +301,17 @@
     return (ref, 0, 2 * COMPS * 2 * FULL)
 
 
-def part_kernel(place_ref, counts_ref, listed_ref, *refs):
-    piece_refs, (flat_ref, picked_0, picked_1, trace_ref, cross_ref) = refs[:-5], refs[-5:]
+def part_kernel(*refs):
+    piece_refs, (flat_ref, trace_ref, cross_ref) = refs[:-3], refs[-3:]
     add_cross([side_part(ref) for ref in piece_refs], trace_ref, PART, cross_ref)
     turn_blocks(cross_ref, PART, flat_ref)
+
+
+def far_kernel(bins, place_ref, counts_ref, listed_ref, flat_ref, picked_0, picked_1):
     listed = listed_ref[cross_full(listed_ref)[2] :].astype(jnp.float32)
     listing = listed.shape[0] // 2
-    pick(place_ref, counts_ref, listed[:listing], flat_ref, PART, 2, picked_0)
-    pick(place_ref, counts_ref, listed[listing:], flat_ref, PART, 3, picked_1)
+    pick(place_ref, counts_ref, listed[:listing], flat_ref, bins, 2, picked_0)
+    pick(place_ref, counts_ref, listed[listing:], flat_ref, bins, 3, picked_1)
 
 
 def early_kernel(sides, after_ref, *refs):
@@ -291,11 +331,22 @@
 
 
 def near_kernel(
-    place_ref, counts_ref, own_pairs_ref, near_pairs_ref, part_ref, full_ref, part_0, full_0, full_1, *part_1
+    place_ref,
+    counts_ref,
+    own_pairs_ref,
+    near_pairs_ref,
+    part_ref,
+    full_ref,
+    after_2,
+    after_3,
+    part_0,
+    full_0,
+    part_1,
+    *full_1,
 ):
     listed = listing_of(near_pairs_ref, LANES)
-    pick(place_ref, counts_ref, listed, part_ref, PART, 1, *part_1)
-    pick(place_ref, counts_ref, listed, full_ref, FULL, 1, full_1)
+    pick(place_ref, counts_ref, listed, part_ref, PART, 1, part_1)
+    pick(place_ref, counts_ref, listed, full_ref, FULL, 1, *full_1)
     listed = listing_of(own_pairs_ref, LANES)
     pick(place_ref, counts_ref, listed, part_ref, PART, 0, part_0)
     pick(place_ref, counts_ref, listed, full_ref, FULL, 0, full_0)
@@ -316,11 +367,7 @@
 
 
 def first_lags_kernel(groups, place_ref, inverse_ref, *refs):
-    part_0, part_2, part_3, full_0, full_1, *part_1, lags_ref, table_ref = refs
-    count, held = part_0.shape[0], full_0.shape[0]
-    part_1 = jnp.concatenate([ref[...] for ref in part_1])
-    parts = [part_0[...], part_2[...], part_1, part_3[...]]
-    full_refs = [full_0, full_1]
+    part_0, part_2, part_3, full_0, part_1, *full_1, lags_ref, table_ref = refs
     samples = inverse_ref.shape[1]
     quarter, _ = place_of(place_ref, groups)
     low = quarter % 2
@@ -328,55 +375,45 @@
 
     def part_table(which):
         start = pl.multiple_of((low ^ which) * 2 * PART, 2 * PART)
-        return both_rounds(inverse_ref[pl.ds(start, 2 * PART), :], sign)
+        return halves(both_rounds(inverse_ref[pl.ds(start, 2 * PART), :], sign))
 
     def full_table(mq):
-        start = pl.multiple_of(samples // 2 + (quarter ^ mq) * 2 * FULL, 2 * FULL)
-        return both_rounds(inverse_ref[pl.ds(start, 2 * FULL), :], sign)
-
-    near, other = halves(part_table(0)), halves(part_table(1))
-    picked = jnp.concatenate(parts, axis=1)
+        start = pl.multiple_of(4 * PART + (quarter ^ mq) * 2 * FULL, 2 * FULL)
+        return halves(both_rounds(inverse_ref[pl.ds(start, 2 * FULL), :], sign))
+
+    near, other = part_table(0), part_table(1)
     lags = 0.0
-    for which in range(2):
-        table = jnp.concatenate([near[which], near[which], other[which], other[which]])
-        lags += jnp.dot(picked, table, preferred_element_type=jnp.float32)
-    packs = count // held
-    here = [halves(full_table(m)) for m in (0, 1)]
-    away = [halves(full_table(m)) for m in (2, 3)]
-    picked = jnp.concatenate([ref[...] for ref in full_refs], axis=1)
-    for pack in range(packs):
-        more = 0.0
-        for which in range(2):
-            def placed(table):
-                empty = jnp.zeros_like(table)
-                return jnp.concatenate([table if at == pack else empty for at in range(packs)])
-
-            more += jnp.dot(
-                picked,
-                jnp.concatenate([placed(table[which]) for table in here]),
-                preferred_element_type=jnp.float32,
-            )
-            table_ref[pack, which] = jnp.concatenate([placed(table[which]) for table in away])
-        total = lags[pack * held : (pack + 1) * held] + more
-        for step_round in range(2):
-            lags_ref[step_round, pack * held : (pack + 1) * held] = total[
-                :, step_round * samples : (step_round + 1) * samples
-            ]
+    full_1 = jnp.concatenate([ref[...] for ref in full_1])
+    for picked, bins, table in (
+        (part_0[...], PART, near),
+        (part_2[...], PART, near),
+        (part_1[...], PART, other),
+        (part_3[...], PART, other),
+        (full_0[...], FULL, full_table(0)),
+        (full_1, FULL, full_table(1)),
+    ):
+        picked = unpack(picked, bins)
+        for half in table:
+            lags += jnp.dot(picked, half, preferred_element_type=jnp.float32)
+    for step_round in range(2):
+        lags_ref[step_round] = lags[:, step_round * samples : (step_round + 1) * samples]
+    for at in range(2):
+        for which, half in enumerate(full_table(2 + at)):
+            table_ref[at, which] = half
 
 
 def lag_kernel(first_ref, table_ref, *refs):
     picked_refs, lags_ref = refs[:-1], refs[-1]
     samples = lags_ref.shape[2]
-    held = picked_refs[0].shape[0]
-    picked = jnp.concatenate([ref[...] for ref in picked_refs], axis=1)
-    for pack in range(table_ref.shape[0]):
-        more = jnp.dot(picked, table_ref[pack, 0], preferred_element_type=jnp.float32)
-        more += jnp.dot(picked, table_ref[pack, 1], preferred_element_type=jnp.float32)
-        for step_round in range(2):
-            lags_ref[step_round, pack * held : (pack + 1) * held] = (
-                first_ref[step_round, pack * held : (pack + 1) * held]
-                + more[:, step_round * samples : (step_round + 1) * samples]
-            )
+    more = 0.0
+    for at, ref in enumerate(picked_refs):
+        picked = unpack(ref[...], FULL)
+        for which in range(2):
+            more += jnp.dot(picked, table_ref[at, which], preferred_element_type=jnp.float32)
+    for step_round in range(2):
+        lags_ref[step_round] = (
+            first_ref[step_round] + more[:, step_round * samples : (step_round + 1) * samples]
+        )
 
 
 def on_device(windows, counts, pairs):
@@ -432,21 +469,34 @@
     arrived = [pieces[0]] + [swap(pieces[m], 2 * m) for m in range(1, 2 * groups)]
     sides, far = arrived[:groups], arrived[groups:]
 
-    part_flat, part_2, part_3 = pl.pallas_call(
+    part_packed = shape(packed_rows(count, PART), LANES)
+    full_packed = shape(packed_rows(count, FULL), LANES)
+    half_packed = shape(packed_rows(count, FULL) // 2, LANES)
+    part_blocks = shape(2, 2, SLOTS * SLOTS * width(PART) // LANES, 2 * LANES)
+    full_blocks = shape(2, 2, SLOTS * SLOTS * width(FULL) // LANES, 2 * LANES)
+    part_flat = pl.pallas_call(
         part_kernel,
-        out_shape=[shape(2, 2, SLOTS * SLOTS * PART // LANES, 2 * LANES)] + [shape(count, 4 * PART)] * 2,
-        in_specs=[smem, smem] + [vmem] * (1 + groups),
-        out_specs=[vmem] * 3,
+        out_shape=part_blocks,
+        in_specs=[vmem] * groups,
+        out_specs=vmem,
         scratch_shapes=[
             pltpu.VMEM((padded(groups * 2 * comps) * 2 * PART, LANES), jnp.float32),
             pltpu.VMEM((2 * SLOTS * 2 * PART, LANES), jnp.float32),
         ],
         compiler_params=params,
-        cost_estimate=cost(4),
+        cost_estimate=cost(2),
         name="part",
-    )(place, counts, far[0], *sides)
+    )(*sides)
+    part_2, part_3 = pl.pallas_call(
+        functools.partial(far_kernel, PART),
+        out_shape=[part_packed, part_packed],
+        in_specs=[smem, smem, vmem, vmem],
+        out_specs=[vmem, vmem],
+        compiler_params=params,
+        cost_estimate=cost(1),
+        name="part_far",
+    )(place, counts, far[0], part_flat)
     part_2, part_3 = swap(part_2, half), swap(part_3, half + 1)
-    packed = count * 4 * FULL // LANES
     early, late = far[: groups - 2], far[groups - 2 :]
     sums = pl.pallas_call(
         functools.partial(early_kernel, groups),
@@ -462,7 +512,7 @@
     )(part_flat, *sides, *early)
     full_flat, full_2, full_3 = pl.pallas_call(
         full_kernel,
-        out_shape=[shape(2, 2, SLOTS * SLOTS * FULL // LANES, 2 * LANES)] + [shape(packed, LANES)] * 2,
+        out_shape=[full_blocks, full_packed, full_packed],
         in_specs=[smem, smem] + [vmem] * (2 + len(late)),
         out_specs=[vmem] * 3,
         scratch_shapes=[
@@ -476,20 +526,20 @@
     full_2, full_3 = swap(full_2, half), swap(full_3, half + 1)
     part_0, full_0, *near = pl.pallas_call(
         near_kernel,
-        out_shape=[shape(count, LANES)] + [shape(packed, LANES)] * 2 + [shape(count // 2, LANES)] * 2,
-        in_specs=[smem, smem] + [vmem] * 4,
+        out_shape=[part_packed, full_packed, part_packed] + [half_packed] * 2,
+        in_specs=[smem, smem] + [vmem] * 4 + [pl.BlockSpec(memory_space=pl.ANY)] * 2,
         out_specs=[vmem] * 5,
         compiler_params=params,
         cost_estimate=cost(0.5),
         name="near",
-    )(place, counts, pairs, near_pairs, part_flat, full_flat)
+    )(place, counts, pairs, near_pairs, part_flat, full_flat, part_2, part_3)
     near = [swap(x, 1) for x in near]
 
     first, tables = pl.pallas_call(
         functools.partial(first_lags_kernel, groups),
         out_shape=[
             shape(2, count, samples, dtype=jnp.float32),
-            shape(count // packed, 2, 2 * LANES, 2 * samples),
+            shape(2, 2, 4 * FULL, 2 * samples),
         ],
         in_specs=[smem] + [vmem] * 8,
         out_specs=[vmem] * 2,

time: 44.3 us -> 43.2 us (0.975)
  waiting for transfers between devices: 10 us -> 3.54 us
  starting transfers between devices: 19.4 us -> 23.4 us
  Pallas kernels: 13.6 us -> 14.8 us
    ppermute x16, waiting for transfers between devices: 10 us -> 3.54 us  [swap(): return lax.ppermute(x, 'cell', [(i, i ^ mask) for i in range(cells)])]
    ppermute x16, starting transfers between devices: 19.4 us -> 23.4 us  [swap(): return lax.ppermute(x, 'cell', [(i, i ^ mask) for i in range(cells)])]
    pallas_call x1, Pallas kernels: 1 us -> 1.78 us  [on_device(): pl.pallas_call(functools.partial(first_lags_kernel, groups), out_shape=[s...]
    pallas_call x3 -> x4, Pallas kernels: 8.81 us -> 8.97 us  [the longest x1 3.31 us: on_device(): pl.pallas_call(full_kernel, out_shape=[full_blocks, full_packed, full_pac...]
  transfers between devices with their start and end apart: 16 -> 16, of which waited for: 6 -> 4; matrix products, arithmetic and copies ran while one was open for 0% -> 0% of each run, Pallas kernels for 26% -> 29%
where the time goes in v9:
time: 43.2 us; the launch traced here: 43.1 us
  starting transfers between devices  23.4 us (54%)
  Pallas kernels  14.8 us (34%)
  waiting for transfers between devices  3.54 us (8%)
  local copies, waits for them, and re-layouts  1.15 us (3%)
    ppermute x16, starting transfers between devices, swap(): return lax.ppermute(x, 'cell', [(i, i ^ mask) for i in range(cells)])  23.4 us
    ppermute x16, waiting for transfers between devices, swap(): return lax.ppermute(x, 'cell', [(i, i ^ mask) for i in range(cells)])  3.54 us
    pallas_call x1, Pallas kernels, on_device(): pl.pallas_call(full_kernel, out_shape=[full_blocks, full_packed, full_pac...  3.31 us
    pallas_call x1, Pallas kernels, on_device(): pl.pallas_call(near_kernel, out_shape=[part_packed, full_packed, part_pac...  2.82 us
    pallas_call x1, Pallas kernels, on_device(): pl.pallas_call(functools.partial(first_lags_kernel, groups), out_shape=[s...  1.78 us
    pallas_call x1, Pallas kernels, on_device(): pl.pallas_call(functools.partial(far_kernel, PART), out_shape=[part_packe...  1.68 us
    pallas_call x1, Pallas kernels, on_device(): pl.pallas_call(lag_kernel, out_shape=shape(2, count, samples, dtype=jnp.f...  1.66 us
    pallas_call x1, Pallas kernels, on_device(): pl.pallas_call(part_kernel, out_shape=part_blocks, in_specs=[vmem] * grou...  1.16 us
  transfers between devices with their start and end apart: 16, of which 4 were waited for; matrix products, arithmetic and copies ran while one was open for 0% of the time, Pallas kernels for 29%

profile of v9, /device:TPU:0, one launch (start us, length us, event | category | flops | bytes accessed | tf_op | source)
XLA Modules:
  0.0 43.1 jit_solution(10097399842768934589)
XLA Ops:
  0.0 0.5 %collective-permute-start.1 = (bf16[3,2,4,64,256]{4,3,2,1,0:T(8,128)(2,1)}, bf16[3,2,4,64,256]{4,3,2,1,0:T(8,128)(2,1)S(1)}, u32[]{:S(2)}, u32[]{:S(2)}) collective-permute-start(bf16[3,2,4,64,256]{4,3,2,1,0:T(8,128)(2,1)} %bitcast.2), channel_id=1, source_target_pairs={{0,1},{1,0},{2,3},{3,2},{4,5},{5,4},{6,7},{7,6},{8,9},{9,8},{10,11... | collective-permute-start | bytes 2359304 | tf_op jit(solution)/shard_map/ppermute | solution.py:428
  0.5 0.1 collective-permute-start
  0.5 0.0 copy-start.1
  0.5 1.1 %copy-done.1 = bf16[3,1,512,256]{3,2,1,0:T(8,128)(2,1)S(1)} copy-done((bf16[3,1,512,256]{3,2,1,0:T(8,128)(2,1)S(1)}, bf16[3,1,512,256]{3,2,1,0:T(8,128)(2,1)}, u32[]{:S(2)}) %copy-start.1) | copy-done | bytes 786456
  1.6 0.0 copy-start.2
  1.6 0.8 %own_spectra.1 = (bf16[4,96,128]{2,1,0:T(8,128)(2,1)S(1)}, bf16[8,144,128]{2,1,0:T(8,128)(2,1)S(1)}, bf16[128,256]{1,0:T(8,128)(2,1)S(1)}) custom-call(s32[1]{0:T(128)} %bitcast.place_ref, bf16[3,2,4,64,256]{4,3,2,1,0:T(8,128)(2,1)S(1)} %bitcast.3), custom_call_target="tpu_custom_call" | custom-call | flops 1000000000 | bytes 1048576 | tf_op jit(solution)/shard_map/own_spectra/pallas_call | solution.py:445
  2.5 0.1 collective-permute-done.near_pairs_ref
  2.6 0.0 collective-permute-done.1.windows_ref
  2.6 0.0 copy-done.2
  2.6 0.8 %near_spectra.1 = (bf16[480,128]{1,0:T(8,128)(2,1)S(1)}, bf16[480,128]{1,0:T(8,128)(2,1)S(1)}, bf16[480,128]{1,0:T(8,128)(2,1)S(1)}, bf16[480,128]{1,0:T(8,128)(...) custom-call(s32[1]{0:T(128)} %bitcast.place_ref, ...), custom_call_target="tpu_custom_call" | custom-call | flops 1000000000 | bytes 1048576 | tf_op jit(solution)/shard_map/near_spectra/pallas_call | solution.py:459
  3.4 3.0 %collective-permute-start.2 = (bf16[480,128]{1,0:T(8,128)(2,1)S(1)}, bf16[480,128]{1,0:T(8,128)(2,1)S(1)}, u32[]{:S(2)}, u32[]{:S(2)}) collective-permute-start(bf16[480,128]{1,0:T(8,128)(2,1)S(1)} %get-tuple-element.32), channel_id=1, source_target_pairs={{0,2},{1,3},{2,0},{3,1},{4,6},{5,7},{6,4},{7,5},{8,10},{9,11},{10,... | collective-permute-start | bytes 368648 | tf_op jit(solution)/shard_map/ppermute | solution.py:428
  6.4 1.6 %collective-permute-start.3 = (bf16[480,128]{1,0:T(8,128)(2,1)S(1)}, bf16[480,128]{1,0:T(8,128)(2,1)S(1)}, u32[]{:S(2)}, u32[]{:S(2)}) collective-permute-start(bf16[480,128]{1,0:T(8,128)(2,1)S(1)} %get-tuple-element.33), channel_id=1, source_target_pairs={{0,4},{1,5},{2,6},{3,7},{4,0},{5,1},{6,2},{7,3},{8,12},{9,13},{10,... | collective-permute-start | bytes 368648 | tf_op jit(solution)/shard_map/ppermute | solution.py:428
  8.0 0.0 collective-permute-start.4
  8.0 3.0 %collective-permute-start.5 = (bf16[320,128]{1,0:T(8,128)(2,1)S(1)}, bf16[320,128]{1,0:T(8,128)(2,1)S(1)}, u32[]{:S(2)}, u32[]{:S(2)}) collective-permute-start(bf16[320,128]{1,0:T(8,128)(2,1)S(1)} %get-tuple-element.35), channel_id=1, source_target_pairs={{0,8},{1,9},{2,10},{3,11},{4,12},{5,13},{6,14},{7,15},{8,0},{9,1},... | collective-permute-start | bytes 245768 | tf_op jit(solution)/shard_map/ppermute | solution.py:428
  11.0 1.3 %collective-permute-start.6 = (bf16[288,128]{1,0:T(8,128)(2,1)S(1)}, bf16[288,128]{1,0:T(8,128)(2,1)S(1)}, u32[]{:S(2)}, u32[]{:S(2)}) collective-permute-start(bf16[288,128]{1,0:T(8,128)(2,1)S(1)} %get-tuple-element.36), channel_id=1, source_target_pairs={{0,10},{1,11},{2,8},{3,9},{4,14},{5,15},{6,12},{7,13},{8,2},{9,3},... | collective-permute-start | bytes 221192 | tf_op jit(solution)/shard_map/ppermute | solution.py:428
  12.3 0.0 collective-permute-done.2.refs_1_
  12.3 3.6 %collective-permute-start.7 = (bf16[288,128]{1,0:T(8,128)(2,1)S(1)}, bf16[288,128]{1,0:T(8,128)(2,1)S(1)}, u32[]{:S(2)}, u32[]{:S(2)}) collective-permute-start(bf16[288,128]{1,0:T(8,128)(2,1)S(1)} %get-tuple-element.37), channel_id=1, source_target_pairs={{0,12},{1,13},{2,14},{3,15},{4,8},{5,9},{6,10},{7,11},{8,4},{9,5},... | collective-permute-start | bytes 221192 | tf_op jit(solution)/shard_map/ppermute | solution.py:428
  15.9 0.0 collective-permute-done.3.refs_2_
  15.9 1.3 %collective-permute-start.8 = (bf16[288,128]{1,0:T(8,128)(2,1)S(1)}, bf16[288,128]{1,0:T(8,128)(2,1)S(1)}, u32[]{:S(2)}, u32[]{:S(2)}) collective-permute-start(bf16[288,128]{1,0:T(8,128)(2,1)S(1)} %get-tuple-element.38), channel_id=1, source_target_pairs={{0,14},{1,15},{2,12},{3,13},{4,10},{5,11},{6,8},{7,9},{8,6},{9,7},... | collective-permute-start | bytes 221192 | tf_op jit(solution)/shard_map/ppermute | solution.py:428
  17.2 0.0 collective-permute-done.4.refs_3_
  17.2 1.2 %part.1.after_ref.flat_ref.part_ref = bf16[2,2,128,256]{3,2,1,0:T(8,128)(2,1)S(1)} custom-call(bf16[480,128]{1,0:T(8,128)(2,1)S(1)} %get-tuple-element.31.refs_0_, bf16[480,128]{1,0:T(8,128)(2,1)S(1)} %collective-permute-done.2.refs_1_, bf16[480,128]{1,0:T(8,128)(2,1)S(1)} %collective-permute-done.3.refs_2_, bf16[480,128]{1,0:T(8,128)(2,1)S(1)} %collective-permute-done.4.refs_3_), custom_call_target="tpu_custom_call" | custom-call | flops 2000000000 | bytes 1048576 | tf_op jit(solution)/shard_map/part/pallas_call | solution.py:477
  18.4 0.0 collective-permute-done.5.refs_4_.listed_ref
  18.4 0.0 copy-done.3
  18.4 1.7 %part_far.1 = (bf16[256,128]{1,0:T(8,128)(2,1)S(1)}, bf16[256,128]{1,0:T(8,128)(2,1)S(1)}) custom-call(s32[1]{0:T(128)} %bitcast.place_ref, s32[16]{0:T(128)S(1)} %copy-done.3, bf16[320,128]{1,0:T(8,128)(2,1)S(1)} %collective-permute-done.5.refs_4_.listed_ref, bf16[2,2,128,256]{3,2,1,0:T(8,128)(2,1)S(1)} %part.1.after_ref.flat_ref.part_ref), custom_call_target="tpu_custom_call" | custom-call | flops 1000000000 | bytes 1048576 | tf_op jit(solution)/shard_map/part_far/pallas_call | solution.py:490
  20.1 0.1 collective-permute-start.10
  20.1 1.3 %collective-permute-start.9 = (bf16[256,128]{1,0:T(8,128)(2,1)S(1)}, bf16[256,128]{1,0:T(8,128)(2,1)S(1)}, u32[]{:S(2)}, u32[]{:S(2)}) collective-permute-start(bf16[256,128]{1,0:T(8,128)(2,1)S(1)} %get-tuple-element.40), channel_id=1, source_target_pairs={{0,8},{1,9},{2,10},{3,11},{4,12},{5,13},{6,14},{7,15},{8,0},{9,1},... | collective-permute-start | bytes 196616 | tf_op jit(solution)/shard_map/ppermute | solution.py:428
  21.4 2.4 %collective-permute-done.6.refs_5_ = bf16[288,128]{1,0:T(8,128)(2,1)S(1)} collective-permute-done((bf16[288,128]{1,0:T(8,128)(2,1)S(1)}, bf16[288,128]{1,0:T(8,128)(2,1)S(1)}, u32[]{:S(2)}, u32[]{:S(2)}) %collective-permute-start.6) | collective-permute-done | bytes 73760 | tf_op jit(solution)/shard_map/ppermute | solution.py:428
  23.8 0.7 %early.1.before_ref = f32[3072,128]{1,0:T(8,128)S(1)} custom-call(bf16[2,2,128,256]{3,2,1,0:T(8,128)(2,1)S(1)} %part.1.after_ref.flat_ref.part_ref, bf16[480,128]{1,0:T(8,128)(2,1)S(1)} %get-tuple-element.31.refs_0_, bf16[480,128]{1,0:T(8,128)(2,1)S(1)} %collective-permute-done.2.refs_1_, bf16[480,128]{1,0:T(8,128)(2,1)S(1)} %collective-permute-done.3.refs_2_, ...), custom_call_target="tpu_custom_call" | custom-call | flops 1000000 | bytes 1048576 | tf_op jit(solution)/shard_map/early/pallas_call | solution.py:501
  24.5 0.0 collective-permute-done.7.refs_0_
  24.5 0.0 collective-permute-done.8.refs_1_
  24.5 3.3 %full.1 = (bf16[2,2,256,256]{3,2,1,0:T(8,128)(2,1)S(1)}, bf16[384,128]{1,0:T(8,128)(2,1)S(1)}, bf16[384,128]{1,0:T(8,128)(2,1)S(1)}) custom-call(s32[1]{0:T(128)} %bitcast.place_ref, s32[16]{0:T(128)S(1)} %copy-done.3, bf16[320,128]{1,0:T(8,128)(2,1)S(1)} %collective-permute-done.5.refs_4_.listed_ref, f32[3072,128]{1,0:T(8,128)S(1)} %early.1.before_ref, ...), custom_call_target="tpu_custom_call" | custom-call | flops 10000000000 | bytes 1048576 | tf_op jit(solution)/shard_map/full/pallas_call | solution.py:513
  27.9 0.0 copy-start
  27.9 7.1 %collective-permute-start.14 = (bf16[384,128]{1,0:T(8,128)(2,1)S(1)}, bf16[384,128]{1,0:T(8,128)(2,1)S(1)}, u32[]{:S(2)}, u32[]{:S(2)}) collective-permute-start(bf16[384,128]{1,0:T(8,128)(2,1)S(1)} %get-tuple-element.49), channel_id=1, source_target_pairs={{0,8},{1,9},{2,10},{3,11},{4,12},{5,13},{6,14},{7,15},{8,0},{9,1},... | collective-permute-start | bytes 294920 | tf_op jit(solution)/shard_map/ppermute | solution.py:428
  34.9 0.0 collective-permute-start.15
  34.9 0.0 collective-permute-done.10.after_3.refs_2_
  34.9 0.0 collective-permute-done.9.after_2.refs_1_
  34.9 2.8 %near.1 = (bf16[256,128]{1,0:T(8,128)(2,1)S(1)}, bf16[384,128]{1,0:T(8,128)(2,1)S(1)}, bf16[256,128]{1,0:T(8,128)(2,1)S(1)}, bf16[192,128]{1,0:T(8,128)(2,1)S(1)}, bf16[192,128]{1,0:T(8,128)(2,1)S(1)}) custom-call(s32[1]{0:T(128)} %bitcast.place_ref, s32[16]{0:T(128)S(1)} %copy-done.3, s32[2,2,512]{2,1,0:T(2,128)S(1)} %copy-done.2, ...), custom_call_target="tpu_custom_call" | custom-call | flops 500000000 | bytes 1048576 | tf_op jit(solution)/shard_map/near/pallas_call | solution.py:527
  37.8 0.3 collective-permute-start.11
  38.0 0.3 collective-permute-start.12
  38.4 0.2 collective-permute-start.13
  38.5 0.7 %collective-permute-done.12.refs_5_ = bf16[192,128]{1,0:T(8,128)(2,1)S(1)} collective-permute-done((bf16[192,128]{1,0:T(8,128)(2,1)S(1)}, bf16[192,128]{1,0:T(8,128)(2,1)S(1)}, u32[]{:S(2)}, u32[]{:S(2)}) %collective-permute-start.12) | collective-permute-done | bytes 49184 | tf_op jit(solution)/shard_map/ppermute | solution.py:428
  39.3 0.3 collective-permute-done.13.refs_6_
  39.6 0.0 collective-permute-done.11.refs_4_
  39.6 0.0 copy-done
  39.6 1.8 %first_lags.1 = (f32[2,512,256]{2,1,0:T(8,128)S(1)}, bf16[2,2,96,512]{3,2,1,0:T(8,128)(2,1)S(1)}) custom-call(s32[1]{0:T(128)} %bitcast.place_ref, f32[256,256]{1,0:T(8,128)S(1)} %copy-done, bf16[256,128]{1,0:T(8,128)(2,1)S(1)} %get-tuple-element.42.refs_0_, bf16[256,128]{1,0:T(8,128)(2,1)S(1)} %collective-permute-done.9.after_2.refs_1_, ...), custom_call_target="tpu_custom_call" | custom-call | flops 1000000 | bytes 1048576 | tf_op jit(solution)/shard_map/first_lags/pallas_call | solution.py:538
  41.4 0.0 collective-permute-done.14.refs_0_
  41.4 0.0 collective-permute-done.15.refs_1_
  41.4 1.7 %lags.1 = f32[2,512,256]{2,1,0:T(8,128)} custom-call(f32[2,512,256]{2,1,0:T(8,128)S(1)} %get-tuple-element.47.first_ref, bf16[2,2,96,512]{3,2,1,0:T(8,128)(2,1)S(1)} %get-tuple-element.48.table_ref, bf16[384,128]{1,0:T(8,128)(2,1)S(1)} %collective-permute-done.14.refs_0_, bf16[384,128]{1,0:T(8,128)(2,1)S(1)} %collective-permute-done.15.refs_1_), custom_call_target="tpu_custom_call" | custom-call | flops 1000000000 | bytes 1048576 | tf_op jit(solution)/shard_map/lags/pallas_call | solution.py:550
  (1 shorter events, 0.0 us)
Async XLA Ops:
  0.0 2.6 %collective-permute-start.1 = (bf16[3,2,4,64,256]{4,3,2,1,0:T(8,128)(2,1)}, bf16[3,2,4,64,256]{4,3,2,1,0:T(8,128)(2,1)S(1)}, u32[]{:S(2)}, u32[]{:S(2)}) collective-permute-start(bf16[3,2,4,64,256]{4,3,2,1,0:T(8,128)(2,1)} %bitcast.2), channel_id=1, source_target_pairs={{0,1},{1,0},{2,3},{3,2},{4,5},{5,4},{6,7},{7,6},{8,9},{9,8},{10,11... | collective-permute-start | bytes 2359304 | tf_op jit(solution)/shard_map/ppermute | solution.py:428
  0.5 2.1 %collective-permute-start = (s32[2,2,512]{2,1,0:T(2,128)}, s32[2,2,512]{2,1,0:T(2,128)S(1)}, u32[]{:S(2)}, u32[]{:S(2)}) collective-permute-start(s32[2,2,512]{2,1,0:T(2,128)} %own_pairs_ref.3), channel_id=1, source_target_pairs={{0,1},{1,0},{2,3},{3,2},{4,5},{5,4},{6,7},{7,6},{8,9},{9,8},{10,11... | collective-permute-start | bytes 24584 | tf_op jit(solution)/shard_map/ppermute | solution.py:428
  0.5 1.1 %copy-start.1 = (bf16[3,1,512,256]{3,2,1,0:T(8,128)(2,1)S(1)}, bf16[3,1,512,256]{3,2,1,0:T(8,128)(2,1)}, u32[]{:S(2)}) copy-start(bf16[3,1,512,256]{3,2,1,0:T(8,128)(2,1)} %param.4) | copy-start | bytes 2359300
  1.6 0.9 %copy-start.2 = (s32[2,2,512]{2,1,0:T(2,128)S(1)}, s32[2,2,512]{2,1,0:T(2,128)}, u32[]{:S(2)}) copy-start(s32[2,2,512]{2,1,0:T(2,128)} %own_pairs_ref.3) | copy-start | bytes 24580
  3.4 8.8 %collective-permute-start.2 = (bf16[480,128]{1,0:T(8,128)(2,1)S(1)}, bf16[480,128]{1,0:T(8,128)(2,1)S(1)}, u32[]{:S(2)}, u32[]{:S(2)}) collective-permute-start(bf16[480,128]{1,0:T(8,128)(2,1)S(1)} %get-tuple-element.32), channel_id=1, source_target_pairs={{0,2},{1,3},{2,0},{3,1},{4,6},{5,7},{6,4},{7,5},{8,10},{9,11},{10,... | collective-permute-start | bytes 368648 | tf_op jit(solution)/shard_map/ppermute | solution.py:428
  6.4 9.5 %collective-permute-start.3 = (bf16[480,128]{1,0:T(8,128)(2,1)S(1)}, bf16[480,128]{1,0:T(8,128)(2,1)S(1)}, u32[]{:S(2)}, u32[]{:S(2)}) collective-permute-start(bf16[480,128]{1,0:T(8,128)(2,1)S(1)} %get-tuple-element.33), channel_id=1, source_target_pairs={{0,4},{1,5},{2,6},{3,7},{4,0},{5,1},{6,2},{7,3},{8,12},{9,13},{10,... | collective-permute-start | bytes 368648 | tf_op jit(solution)/shard_map/ppermute | solution.py:428
  8.0 9.2 %collective-permute-start.4 = (bf16[480,128]{1,0:T(8,128)(2,1)S(1)}, bf16[480,128]{1,0:T(8,128)(2,1)S(1)}, u32[]{:S(2)}, u32[]{:S(2)}) collective-permute-start(bf16[480,128]{1,0:T(8,128)(2,1)S(1)} %get-tuple-element.34), channel_id=1, source_target_pairs={{0,6},{1,7},{2,4},{3,5},{4,2},{5,3},{6,0},{7,1},{8,14},{9,15},{10,... | collective-permute-start | bytes 368648 | tf_op jit(solution)/shard_map/ppermute | solution.py:428
  8.0 10.4 %collective-permute-start.5 = (bf16[320,128]{1,0:T(8,128)(2,1)S(1)}, bf16[320,128]{1,0:T(8,128)(2,1)S(1)}, u32[]{:S(2)}, u32[]{:S(2)}) collective-permute-start(bf16[320,128]{1,0:T(8,128)(2,1)S(1)} %get-tuple-element.35), channel_id=1, source_target_pairs={{0,8},{1,9},{2,10},{3,11},{4,12},{5,13},{6,14},{7,15},{8,0},{9,1},... | collective-permute-start | bytes 245768 | tf_op jit(solution)/shard_map/ppermute | solution.py:428
  11.0 12.8 %collective-permute-start.6 = (bf16[288,128]{1,0:T(8,128)(2,1)S(1)}, bf16[288,128]{1,0:T(8,128)(2,1)S(1)}, u32[]{:S(2)}, u32[]{:S(2)}) collective-permute-start(bf16[288,128]{1,0:T(8,128)(2,1)S(1)} %get-tuple-element.36), channel_id=1, source_target_pairs={{0,10},{1,11},{2,8},{3,9},{4,14},{5,15},{6,12},{7,13},{8,2},{9,3},... | collective-permute-start | bytes 221192 | tf_op jit(solution)/shard_map/ppermute | solution.py:428
  12.3 12.3 %collective-permute-start.7 = (bf16[288,128]{1,0:T(8,128)(2,1)S(1)}, bf16[288,128]{1,0:T(8,128)(2,1)S(1)}, u32[]{:S(2)}, u32[]{:S(2)}) collective-permute-start(bf16[288,128]{1,0:T(8,128)(2,1)S(1)} %get-tuple-element.37), channel_id=1, source_target_pairs={{0,12},{1,13},{2,14},{3,15},{4,8},{5,9},{6,10},{7,11},{8,4},{9,5},... | collective-permute-start | bytes 221192 | tf_op jit(solution)/shard_map/ppermute | solution.py:428
  15.9 8.7 %collective-permute-start.8 = (bf16[288,128]{1,0:T(8,128)(2,1)S(1)}, bf16[288,128]{1,0:T(8,128)(2,1)S(1)}, u32[]{:S(2)}, u32[]{:S(2)}) collective-permute-start(bf16[288,128]{1,0:T(8,128)(2,1)S(1)} %get-tuple-element.38), channel_id=1, source_target_pairs={{0,14},{1,15},{2,12},{3,13},{4,10},{5,11},{6,8},{7,9},{8,6},{9,7},... | collective-permute-start | bytes 221192 | tf_op jit(solution)/shard_map/ppermute | solution.py:428
  17.2 1.2 %copy-start.3 = (s32[16]{0:T(128)S(1)}, s32[16]{0:T(128)}, u32[]{:S(2)}) copy-start(s32[16]{0:T(128)} %counts_ref.5) | copy-start | bytes 196
  20.1 14.9 %collective-permute-start.10 = (bf16[256,128]{1,0:T(8,128)(2,1)S(1)}, bf16[256,128]{1,0:T(8,128)(2,1)S(1)}, u32[]{:S(2)}, u32[]{:S(2)}) collective-permute-start(bf16[256,128]{1,0:T(8,128)(2,1)S(1)} %get-tuple-element.41), channel_id=1, source_target_pairs={{0,9},{1,8},{2,11},{3,10},{4,13},{5,12},{6,15},{7,14},{8,1},{9,0},... | collective-permute-start | bytes 196616 | tf_op jit(solution)/shard_map/ppermute | solution.py:428
  20.1 14.8 %collective-permute-start.9 = (bf16[256,128]{1,0:T(8,128)(2,1)S(1)}, bf16[256,128]{1,0:T(8,128)(2,1)S(1)}, u32[]{:S(2)}, u32[]{:S(2)}) collective-permute-start(bf16[256,128]{1,0:T(8,128)(2,1)S(1)} %get-tuple-element.40), channel_id=1, source_target_pairs={{0,8},{1,9},{2,10},{3,11},{4,12},{5,13},{6,14},{7,15},{8,0},{9,1},... | collective-permute-start | bytes 196616 | tf_op jit(solution)/shard_map/ppermute | solution.py:428
  27.9 11.7 %copy-start = (f32[256,256]{1,0:T(8,128)S(1)}, f32[256,256]{1,0:T(8,128)}, u32[]{:S(2)}) copy-start(f32[256,256]{1,0:T(8,128)} %constant.6.clone.inverse_ref) | copy-start | bytes 786436
  27.9 13.5 %collective-permute-start.14 = (bf16[384,128]{1,0:T(8,128)(2,1)S(1)}, bf16[384,128]{1,0:T(8,128)(2,1)S(1)}, u32[]{:S(2)}, u32[]{:S(2)}) collective-permute-start(bf16[384,128]{1,0:T(8,128)(2,1)S(1)} %get-tuple-element.49), channel_id=1, source_target_pairs={{0,8},{1,9},{2,10},{3,11},{4,12},{5,13},{6,14},{7,15},{8,0},{9,1},... | collective-permute-start | bytes 294920 | tf_op jit(solution)/shard_map/ppermute | solution.py:428
  34.9 6.5 %collective-permute-start.15 = (bf16[384,128]{1,0:T(8,128)(2,1)S(1)}, bf16[384,128]{1,0:T(8,128)(2,1)S(1)}, u32[]{:S(2)}, u32[]{:S(2)}) collective-permute-start(bf16[384,128]{1,0:T(8,128)(2,1)S(1)} %get-tuple-element.50), channel_id=1, source_target_pairs={{0,9},{1,8},{2,11},{3,10},{4,13},{5,12},{6,15},{7,14},{8,1},{9,0},... | collective-permute-start | bytes 294920 | tf_op jit(solution)/shard_map/ppermute | solution.py:428
  37.8 1.8 %collective-permute-start.11 = (bf16[256,128]{1,0:T(8,128)(2,1)S(1)}, bf16[256,128]{1,0:T(8,128)(2,1)S(1)}, u32[]{:S(2)}, u32[]{:S(2)}) collective-permute-start(bf16[256,128]{1,0:T(8,128)(2,1)S(1)} %get-tuple-element.44), channel_id=1, source_target_pairs={{0,1},{1,0},{2,3},{3,2},{4,5},{5,4},{6,7},{7,6},{8,9},{9,8},{10,11... | collective-permute-start | bytes 196616 | tf_op jit(solution)/shard_map/ppermute | solution.py:428
  38.0 1.2 %collective-permute-start.12 = (bf16[192,128]{1,0:T(8,128)(2,1)S(1)}, bf16[192,128]{1,0:T(8,128)(2,1)S(1)}, u32[]{:S(2)}, u32[]{:S(2)}) collective-permute-start(bf16[192,128]{1,0:T(8,128)(2,1)S(1)} %get-tuple-element.45), channel_id=1, source_target_pairs={{0,1},{1,0},{2,3},{3,2},{4,5},{5,4},{6,7},{7,6},{8,9},{9,8},{10,11... | collective-permute-start | bytes 147464 | tf_op jit(solution)/shard_map/ppermute | solution.py:428
  38.4 1.2 %collective-permute-start.13 = (bf16[192,128]{1,0:T(8,128)(2,1)S(1)}, bf16[192,128]{1,0:T(8,128)(2,1)S(1)}, u32[]{:S(2)}, u32[]{:S(2)}) collective-permute-start(bf16[192,128]{1,0:T(8,128)(2,1)S(1)} %get-tuple-element.46), channel_id=1, source_target_pairs={{0,1},{1,0},{2,3},{3,2},{4,5},{5,4},{6,7},{7,6},{8,9},{9,8},{10,11... | collective-permute-start | bytes 147464 | tf_op jit(solution)/shard_map/ppermute | solution.py:428

commit v10 on v9

--- a/solution.py
+++ b/solution.py
@@ -307,7 +307,7 @@
     turn_blocks(cross_ref, PART, flat_ref)
 
 
-def far_kernel(bins, place_ref, counts_ref, listed_ref, flat_ref, picked_0, picked_1):
+def far_kernel(bins, place_ref, counts_ref, listed_ref, flat_ref, after_ref, picked_0, picked_1):
     listed = listed_ref[cross_full(listed_ref)[2] :].astype(jnp.float32)
     listing = listed.shape[0] // 2
     pick(place_ref, counts_ref, listed[:listing], flat_ref, bins, 2, picked_0)
@@ -320,7 +320,7 @@
     add_cross(pieces, trace_ref, FULL, sums_ref)
 
 
-def full_kernel(place_ref, counts_ref, listed_ref, before_ref, *refs):
+def full_kernel(place_ref, counts_ref, listed_ref, after_0, after_2, before_ref, *refs):
     piece_refs, (flat_ref, picked_0, picked_1, trace_ref, cross_ref) = refs[:-5], refs[-5:]
     add_cross([cross_full(ref) for ref in piece_refs], trace_ref, FULL, cross_ref, before_ref)
     turn_blocks(cross_ref, FULL, flat_ref)
@@ -330,26 +330,10 @@
     pick(place_ref, counts_ref, listed[listing:], flat_ref, FULL, 3, picked_1)
 
 
-def near_kernel(
-    place_ref,
-    counts_ref,
-    own_pairs_ref,
-    near_pairs_ref,
-    part_ref,
-    full_ref,
-    after_2,
-    after_3,
-    part_0,
-    full_0,
-    part_1,
-    *full_1,
-):
-    listed = listing_of(near_pairs_ref, LANES)
-    pick(place_ref, counts_ref, listed, part_ref, PART, 1, part_1)
-    pick(place_ref, counts_ref, listed, full_ref, FULL, 1, *full_1)
-    listed = listing_of(own_pairs_ref, LANES)
-    pick(place_ref, counts_ref, listed, part_ref, PART, 0, part_0)
-    pick(place_ref, counts_ref, listed, full_ref, FULL, 0, full_0)
+def near_kernel(bins, sent, place_ref, counts_ref, own_pairs_ref, near_pairs_ref, flat_ref, *refs):
+    picked_0, *picked_1 = refs[-1 - sent :]
+    pick(place_ref, counts_ref, listing_of(near_pairs_ref, LANES), flat_ref, bins, 1, *picked_1)
+    pick(place_ref, counts_ref, listing_of(own_pairs_ref, LANES), flat_ref, bins, 0, picked_0)
 
 
 def both_rounds(rows, sign):
@@ -469,6 +453,7 @@
     arrived = [pieces[0]] + [swap(pieces[m], 2 * m) for m in range(1, 2 * groups)]
     sides, far = arrived[:groups], arrived[groups:]
 
+    early, late = far[: groups - 2], far[groups - 2 :]
     part_packed = shape(packed_rows(count, PART), LANES)
     full_packed = shape(packed_rows(count, FULL), LANES)
     half_packed = shape(packed_rows(count, FULL) // 2, LANES)
@@ -490,14 +475,23 @@
     part_2, part_3 = pl.pallas_call(
         functools.partial(far_kernel, PART),
         out_shape=[part_packed, part_packed],
-        in_specs=[smem, smem, vmem, vmem],
+        in_specs=[smem, smem, vmem, vmem, pl.BlockSpec(memory_space=pl.ANY)],
         out_specs=[vmem, vmem],
         compiler_params=params,
         cost_estimate=cost(1),
         name="part_far",
-    )(place, counts, far[0], part_flat)
-    part_2, part_3 = swap(part_2, half), swap(part_3, half + 1)
-    early, late = far[: groups - 2], far[groups - 2 :]
+    )(place, counts, far[0], part_flat, late[0])
+    sent, part_2, part_3 = part_2, swap(part_2, half), swap(part_3, half + 1)
+    part_0, part_1 = pl.pallas_call(
+        functools.partial(near_kernel, PART, 1),
+        out_shape=[part_packed, part_packed],
+        in_specs=[smem, smem] + [vmem] * 3,
+        out_specs=[vmem] * 2,
+        compiler_params=params,
+        cost_estimate=cost(1),
+        name="part_near",
+    )(place, counts, pairs, near_pairs, part_flat)
+    part_1 = swap(part_1, 1)
     sums = pl.pallas_call(
         functools.partial(early_kernel, groups),
         out_shape=shape(2 * SLOTS * 2 * FULL, LANES, dtype=jnp.float32),
@@ -513,7 +507,7 @@
     full_flat, full_2, full_3 = pl.pallas_call(
         full_kernel,
         out_shape=[full_blocks, full_packed, full_packed],
-        in_specs=[smem, smem] + [vmem] * (2 + len(late)),
+        in_specs=[smem, smem, vmem] + [pl.BlockSpec(memory_space=pl.ANY)] * 2 + [vmem] * (1 + len(late)),
         out_specs=[vmem] * 3,
         scratch_shapes=[
             pltpu.VMEM((padded(len(late) * 2 * comps) * 2 * FULL, LANES), jnp.float32),
@@ -522,18 +516,18 @@
         compiler_params=params,
         cost_estimate=cost(10),
         name="full",
-    )(place, counts, far[0], sums, *late)
+    )(place, counts, far[0], part_0, sent, sums, *late)
     full_2, full_3 = swap(full_2, half), swap(full_3, half + 1)
-    part_0, full_0, *near = pl.pallas_call(
-        near_kernel,
-        out_shape=[part_packed, full_packed, part_packed] + [half_packed] * 2,
-        in_specs=[smem, smem] + [vmem] * 4 + [pl.BlockSpec(memory_space=pl.ANY)] * 2,
-        out_specs=[vmem] * 5,
+    full_0, *full_1 = pl.pallas_call(
+        functools.partial(near_kernel, FULL, 2),
+        out_shape=[full_packed, half_packed, half_packed],
+        in_specs=[smem, smem] + [vmem] * 3 + [pl.BlockSpec(memory_space=pl.ANY)] * 3,
+        out_specs=[vmem] * 3,
         compiler_params=params,
         cost_estimate=cost(0.5),
-        name="near",
-    )(place, counts, pairs, near_pairs, part_flat, full_flat, part_2, part_3)
-    near = [swap(x, 1) for x in near]
+        name="full_near",
+    )(place, counts, pairs, near_pairs, full_flat, part_1, part_2, part_3)
+    full_1 = [swap(x, 1) for x in full_1]
 
     first, tables = pl.pallas_call(
         functools.partial(first_lags_kernel, groups),
@@ -546,7 +540,7 @@
         compiler_params=params,
         cost_estimate=cost(0.001),
         name="first_lags",
-    )(place, inverse, part_0, part_2, part_3, full_0, *near)
+    )(place, inverse, part_0, part_2, part_3, full_0, part_1, *full_1)
     return pl.pallas_call(
         lag_kernel,
         out_shape=shape(2, count, samples, dtype=jnp.float32),

time: 43.2 us -> 47.4 us (1.097)
  waiting for transfers between devices: 3.54 us -> 8.08 us
  starting transfers between devices: 23.4 us -> 22.3 us
  Pallas kernels: 14.8 us -> 15.6 us
    ppermute x16, waiting for transfers between devices: 3.54 us -> 8.08 us  [swap(): return lax.ppermute(x, 'cell', [(i, i ^ mask) for i in range(cells)])]
    ppermute x16, starting transfers between devices: 23.4 us -> 22.3 us  [swap(): return lax.ppermute(x, 'cell', [(i, i ^ mask) for i in range(cells)])]
    pallas_call x1 -> x2, Pallas kernels: 2.82 us -> 3.66 us  [the longest x1 2 us: on_device(): pl.pallas_call(functools.partial(near_kernel, FULL, 2), out_shape=[full_p...]
  transfers between devices with their start and end apart: 16 -> 16, of which waited for: 4 -> 6; matrix products, arithmetic and copies ran while one was open for 0% -> 0% of each run, Pallas kernels for 29% -> 28%
where the time goes in v10:
time: 47.4 us; the launch traced here: 47.3 us
  starting transfers between devices  22.3 us (47%)
  Pallas kernels  15.6 us (33%)
  waiting for transfers between devices  8.08 us (17%)
  local copies, waits for them, and re-layouts  1.15 us (2%)
    ppermute x16, starting transfers between devices, swap(): return lax.ppermute(x, 'cell', [(i, i ^ mask) for i in range(cells)])  22.3 us
    ppermute x16, waiting for transfers between devices, swap(): return lax.ppermute(x, 'cell', [(i, i ^ mask) for i in range(cells)])  8.08 us
    pallas_call x1, Pallas kernels, on_device(): pl.pallas_call(full_kernel, out_shape=[full_blocks, full_packed, full_pac...  3.3 us
    pallas_call x1, Pallas kernels, on_device(): pl.pallas_call(functools.partial(near_kernel, FULL, 2), out_shape=[full_p...  2 us
    pallas_call x1, Pallas kernels, on_device(): pl.pallas_call(functools.partial(first_lags_kernel, groups), out_shape=[s...  1.78 us
    pallas_call x1, Pallas kernels, on_device(): pl.pallas_call(functools.partial(far_kernel, PART), out_shape=[part_packe...  1.68 us
    pallas_call x1, Pallas kernels, on_device(): pl.pallas_call(functools.partial(near_kernel, PART, 1), out_shape=[part_p...  1.67 us
    pallas_call x1, Pallas kernels, on_device(): pl.pallas_call(lag_kernel, out_shape=shape(2, count, samples, dtype=jnp.f...  1.66 us
  transfers between devices with their start and end apart: 16, of which 6 were waited for; matrix products, arithmetic and copies ran while one was open for 0% of the time, Pallas kernels for 28%

profile of v10, /device:TPU:0, one launch (start us, length us, event | category | flops | bytes accessed | tf_op | source)
XLA Modules:
  0.0 47.3 jit_solution(8521804066536995216)
XLA Ops:
  0.0 0.5 collective-permute-start.1
  0.5 0.1 collective-permute-start
  0.5 0.0 copy-start.1
  0.5 1.1 %copy-done.1 = bf16[3,1,512,256]{3,2,1,0:T(8,128)(2,1)S(1)} copy-done((bf16[3,1,512,256]{3,2,1,0:T(8,128)(2,1)S(1)}, bf16[3,1,512,256]{3,2,1,0:T(8,128)(2,1)}, u32[]{:S(2)}) %copy-start.1) | copy-done | bytes 786456
  1.6 0.8 %own_spectra.1 = (bf16[4,96,128]{2,1,0:T(8,128)(2,1)S(1)}, bf16[8,144,128]{2,1,0:T(8,128)(2,1)S(1)}, bf16[128,256]{1,0:T(8,128)(2,1)S(1)}) custom-call(s32[1]{0:T(128)} %bitcast.place_ref, bf16[3,2,4,64,256]{4,3,2,1,0:T(8,128)(2,1)S(1)} %bitcast.3), custom_call_target="tpu_custom_call" | custom-call | flops 1000000000 | bytes 1048576 | tf_op jit(solution)/shard_map/own_spectra/pallas_call | solution.py:429
  2.5 0.1 collective-permute-done.near_pairs_ref
  2.6 0.0 collective-permute-done.1.windows_ref
  2.6 0.0 copy-done.2
  2.6 0.8 %near_spectra.1 = (bf16[480,128]{1,0:T(8,128)(2,1)S(1)}, bf16[480,128]{1,0:T(8,128)(2,1)S(1)}, bf16[480,128]{1,0:T(8,128)(2,1)S(1)}, bf16[480,128]{1,0:T(8,128)(...) custom-call(s32[1]{0:T(128)} %bitcast.place_ref, ...), custom_call_target="tpu_custom_call" | custom-call | flops 1000000000 | bytes 1048576 | tf_op jit(solution)/shard_map/near_spectra/pallas_call | solution.py:443
  3.4 3.0 %collective-permute-start.2 = (bf16[480,128]{1,0:T(8,128)(2,1)S(1)}, bf16[480,128]{1,0:T(8,128)(2,1)S(1)}, u32[]{:S(2)}, u32[]{:S(2)}) collective-permute-start(bf16[480,128]{1,0:T(8,128)(2,1)S(1)} %get-tuple-element.32), channel_id=1, source_target_pairs={{0,2},{1,3},{2,0},{3,1},{4,6},{5,7},{6,4},{7,5},{8,10},{9,11},{10,... | collective-permute-start | bytes 368648 | tf_op jit(solution)/shard_map/ppermute | solution.py:412
  6.4 1.6 %collective-permute-start.3 = (bf16[480,128]{1,0:T(8,128)(2,1)S(1)}, bf16[480,128]{1,0:T(8,128)(2,1)S(1)}, u32[]{:S(2)}, u32[]{:S(2)}) collective-permute-start(bf16[480,128]{1,0:T(8,128)(2,1)S(1)} %get-tuple-element.33), channel_id=1, source_target_pairs={{0,4},{1,5},{2,6},{3,7},{4,0},{5,1},{6,2},{7,3},{8,12},{9,13},{10,... | collective-permute-start | bytes 368648 | tf_op jit(solution)/shard_map/ppermute | solution.py:412
  8.0 0.0 collective-permute-start.4
  8.0 3.0 %collective-permute-start.5 = (bf16[320,128]{1,0:T(8,128)(2,1)S(1)}, bf16[320,128]{1,0:T(8,128)(2,1)S(1)}, u32[]{:S(2)}, u32[]{:S(2)}) collective-permute-start(bf16[320,128]{1,0:T(8,128)(2,1)S(1)} %get-tuple-element.36), channel_id=1, source_target_pairs={{0,8},{1,9},{2,10},{3,11},{4,12},{5,13},{6,14},{7,15},{8,0},{9,1},... | collective-permute-start | bytes 245768 | tf_op jit(solution)/shard_map/ppermute | solution.py:412
  11.0 1.3 %collective-permute-start.9 = (bf16[288,128]{1,0:T(8,128)(2,1)S(1)}, bf16[288,128]{1,0:T(8,128)(2,1)S(1)}, u32[]{:S(2)}, u32[]{:S(2)}) collective-permute-start(bf16[288,128]{1,0:T(8,128)(2,1)S(1)} %get-tuple-element.40), channel_id=1, source_target_pairs={{0,10},{1,11},{2,8},{3,9},{4,14},{5,15},{6,12},{7,13},{8,2},{9,3},... | collective-permute-start | bytes 221192 | tf_op jit(solution)/shard_map/ppermute | solution.py:412
  12.2 0.0 collective-permute-done.2.refs_1_
  12.3 3.6 %collective-permute-start.6 = (bf16[288,128]{1,0:T(8,128)(2,1)S(1)}, bf16[288,128]{1,0:T(8,128)(2,1)S(1)}, u32[]{:S(2)}, u32[]{:S(2)}) collective-permute-start(bf16[288,128]{1,0:T(8,128)(2,1)S(1)} %get-tuple-element.37), channel_id=1, source_target_pairs={{0,12},{1,13},{2,14},{3,15},{4,8},{5,9},{6,10},{7,11},{8,4},{9,5},... | collective-permute-start | bytes 221192 | tf_op jit(solution)/shard_map/ppermute | solution.py:412
  15.9 0.0 collective-permute-done.3.refs_2_
  15.9 1.3 %collective-permute-start.10 = (bf16[288,128]{1,0:T(8,128)(2,1)S(1)}, bf16[288,128]{1,0:T(8,128)(2,1)S(1)}, u32[]{:S(2)}, u32[]{:S(2)}) collective-permute-start(bf16[288,128]{1,0:T(8,128)(2,1)S(1)} %get-tuple-element.41), channel_id=1, source_target_pairs={{0,14},{1,15},{2,12},{3,13},{4,10},{5,11},{6,8},{7,9},{8,6},{9,7},... | collective-permute-start | bytes 221192 | tf_op jit(solution)/shard_map/ppermute | solution.py:412
  17.2 0.0 collective-permute-done.4.refs_3_
  17.2 1.2 %part.1.flat_ref.after_ref = bf16[2,2,128,256]{3,2,1,0:T(8,128)(2,1)S(1)} custom-call(bf16[480,128]{1,0:T(8,128)(2,1)S(1)} %get-tuple-element.31.refs_0_, bf16[480,128]{1,0:T(8,128)(2,1)S(1)} %collective-permute-done.2.refs_1_, bf16[480,128]{1,0:T(8,128)(2,1)S(1)} %collective-permute-done.3.refs_2_, bf16[480,128]{1,0:T(8,128)(2,1)S(1)} %collective-permute-done.4.refs_3_), custom_call_target="tpu_custom_call" | custom-call | flops 2000000000 | bytes 1048576 | tf_op jit(solution)/shard_map/part/pallas_call | solution.py:462
  18.3 3.6 %collective-permute-done.6.after_ref.refs_0_ = bf16[288,128]{1,0:T(8,128)(2,1)S(1)} collective-permute-done((bf16[288,128]{1,0:T(8,128)(2,1)S(1)}, bf16[288,128]{1,0:T(8,128)(2,1)S(1)}, u32[]{:S(2)}, u32[]{:S(2)}) %collective-permute-start.6) | collective-permute-done | bytes 73760 | tf_op jit(solution)/shard_map/ppermute | solution.py:412
  21.9 0.0 collective-permute-done.5.listed_ref.refs_4_
  21.9 0.0 copy-done.3
  21.9 1.7 %part_far.1 = (bf16[256,128]{1,0:T(8,128)(2,1)S(1)}, bf16[256,128]{1,0:T(8,128)(2,1)S(1)}) custom-call(s32[1]{0:T(128)} %bitcast.place_ref, s32[16]{0:T(128)S(1)} %copy-done.3, bf16[320,128]{1,0:T(8,128)(2,1)S(1)} %collective-permute-done.5.listed_ref.refs_4_, bf16[2,2,128,256]{3,2,1,0:T(8,128)(2,1)S(1)} %part.1.flat_ref.after_ref, ...), custom_call_target="tpu_custom_call" | custom-call | flops 1000000000 | bytes 1048576 | tf_op jit(solution)/shard_map/part_far/pallas_call | solution.py:475
  23.6 4.3 %collective-permute-start.7 = (bf16[256,128]{1,0:T(8,128)(2,1)S(1)}, bf16[256,128]{1,0:T(8,128)(2,1)S(1)}, u32[]{:S(2)}, u32[]{:S(2)}) collective-permute-start(bf16[256,128]{1,0:T(8,128)(2,1)S(1)} %get-tuple-element.38.after_2), channel_id=1, source_target_pairs={{0,8},{1,9},{2,10},{3,11},{4,12},{5,13},{6,14},{7,15},{8,0},{9,1},... | collective-permute-start | bytes 196616 | tf_op jit(solution)/shard_map/ppermute | solution.py:412
  27.9 0.0 collective-permute-start.8
  27.9 1.7 %part_near.1 = (bf16[256,128]{1,0:T(8,128)(2,1)S(1)}, bf16[256,128]{1,0:T(8,128)(2,1)S(1)}) custom-call(s32[1]{0:T(128)} %bitcast.place_ref, s32[16]{0:T(128)S(1)} %copy-done.3, s32[2,2,512]{2,1,0:T(2,128)S(1)} %copy-done.2, s32[2,2,512]{2,1,0:T(2,128)S(1)} %collective-permute-done.near_pairs_ref, bf16[2,2,128,256]{3,2,1,0:T(8,128)(2,1)S(1)} %part.1.flat_ref.after_ref), custom_call_target="tpu_custom_call" | custom-call | flops 1000000000 | bytes 1048576 | tf_op jit(solution)/shard_map/part_near/pallas_call | solution.py:485
  29.6 0.3 collective-permute-start.11
  29.9 0.0 collective-permute-done.9.refs_5_
  29.9 0.7 %early.1.before_ref = f32[3072,128]{1,0:T(8,128)S(1)} custom-call(bf16[2,2,128,256]{3,2,1,0:T(8,128)(2,1)S(1)} %part.1.flat_ref.after_ref, bf16[480,128]{1,0:T(8,128)(2,1)S(1)} %get-tuple-element.31.refs_0_, bf16[480,128]{1,0:T(8,128)(2,1)S(1)} %collective-permute-done.2.refs_1_, bf16[480,128]{1,0:T(8,128)(2,1)S(1)} %collective-permute-done.3.refs_2_, ...), custom_call_target="tpu_custom_call" | custom-call | flops 1000000 | bytes 1048576 | tf_op jit(solution)/shard_map/early/pallas_call | solution.py:495
  30.6 0.0 collective-permute-done.10.refs_1_
  30.6 3.3 %full.1 = (bf16[2,2,256,256]{3,2,1,0:T(8,128)(2,1)S(1)}, bf16[384,128]{1,0:T(8,128)(2,1)S(1)}, bf16[384,128]{1,0:T(8,128)(2,1)S(1)}) custom-call(s32[1]{0:T(128)} %bitcast.place_ref, s32[16]{0:T(128)S(1)} %copy-done.3, bf16[320,128]{1,0:T(8,128)(2,1)S(1)} %collective-permute-done.5.listed_ref.refs_4_, ...), custom_call_target="tpu_custom_call" | custom-call | flops 10000000000 | bytes 1048576 | tf_op jit(solution)/shard_map/full/pallas_call | solution.py:507
  33.9 0.0 copy-start
  34.0 2.9 %collective-permute-start.14 = (bf16[384,128]{1,0:T(8,128)(2,1)S(1)}, bf16[384,128]{1,0:T(8,128)(2,1)S(1)}, u32[]{:S(2)}, u32[]{:S(2)}) collective-permute-start(bf16[384,128]{1,0:T(8,128)(2,1)S(1)} %get-tuple-element.49), channel_id=1, source_target_pairs={{0,8},{1,9},{2,10},{3,11},{4,12},{5,13},{6,14},{7,15},{8,0},{9,1},... | collective-permute-start | bytes 294920 | tf_op jit(solution)/shard_map/ppermute | solution.py:412
  36.9 0.0 collective-permute-start.15
  36.9 0.0 collective-permute-done.7.refs_1_
  36.9 0.0 collective-permute-done.8.refs_2_
  36.9 0.0 collective-permute-done.11.refs_0_.refs_4_
  36.9 2.0 %full_near.1 = (bf16[384,128]{1,0:T(8,128)(2,1)S(1)}, bf16[192,128]{1,0:T(8,128)(2,1)S(1)}, bf16[192,128]{1,0:T(8,128)(2,1)S(1)}) custom-call(s32[1]{0:T(128)} %bitcast.place_ref, s32[16]{0:T(128)S(1)} %copy-done.3, s32[2,2,512]{2,1,0:T(2,128)S(1)} %copy-done.2, s32[2,2,512]{2,1,0:T(2,128)S(1)} %collective-permute-done.near_pairs_ref, ...), custom_call_target="tpu_custom_call" | custom-call | flops 500000000 | bytes 1048576 | tf_op jit(solution)/shard_map/full_near/pallas_call | solution.py:521
  38.9 0.3 collective-permute-start.12
  39.1 0.3 collective-permute-start.13
  39.5 0.7 %collective-permute-done.12.refs_5_ = bf16[192,128]{1,0:T(8,128)(2,1)S(1)} collective-permute-done((bf16[192,128]{1,0:T(8,128)(2,1)S(1)}, bf16[192,128]{1,0:T(8,128)(2,1)S(1)}, u32[]{:S(2)}, u32[]{:S(2)}) %collective-permute-start.12) | collective-permute-done | bytes 49184 | tf_op jit(solution)/shard_map/ppermute | solution.py:412
  40.2 0.2 collective-permute-done.13.refs_6_
  40.4 0.0 copy-done
  40.4 1.8 %first_lags.1 = (f32[2,512,256]{2,1,0:T(8,128)S(1)}, bf16[2,2,96,512]{3,2,1,0:T(8,128)(2,1)S(1)}) custom-call(s32[1]{0:T(128)} %bitcast.place_ref, f32[256,256]{1,0:T(8,128)S(1)} %copy-done, bf16[256,128]{1,0:T(8,128)(2,1)S(1)} %get-tuple-element.35.after_0.refs_0_, bf16[256,128]{1,0:T(8,128)(2,1)S(1)} %collective-permute-done.7.refs_1_, ...), custom_call_target="tpu_custom_call" | custom-call | flops 1000000 | bytes 1048576 | tf_op jit(solution)/shard_map/first_lags/pallas_call | solution.py:532
  42.2 2.6 %collective-permute-done.14.refs_0_ = bf16[384,128]{1,0:T(8,128)(2,1)S(1)} collective-permute-done((bf16[384,128]{1,0:T(8,128)(2,1)S(1)}, bf16[384,128]{1,0:T(8,128)(2,1)S(1)}, u32[]{:S(2)}, u32[]{:S(2)}) %collective-permute-start.14) | collective-permute-done | bytes 98336 | tf_op jit(solution)/shard_map/ppermute | solution.py:412
  44.7 0.9 %collective-permute-done.15.refs_1_ = bf16[384,128]{1,0:T(8,128)(2,1)S(1)} collective-permute-done((bf16[384,128]{1,0:T(8,128)(2,1)S(1)}, bf16[384,128]{1,0:T(8,128)(2,1)S(1)}, u32[]{:S(2)}, u32[]{:S(2)}) %collective-permute-start.15) | collective-permute-done | bytes 98336 | tf_op jit(solution)/shard_map/ppermute | solution.py:412
  45.6 1.7 %lags.1 = f32[2,512,256]{2,1,0:T(8,128)} custom-call(f32[2,512,256]{2,1,0:T(8,128)S(1)} %get-tuple-element.47.first_ref, bf16[2,2,96,512]{3,2,1,0:T(8,128)(2,1)S(1)} %get-tuple-element.48.table_ref, bf16[384,128]{1,0:T(8,128)(2,1)S(1)} %collective-permute-done.14.refs_0_, bf16[384,128]{1,0:T(8,128)(2,1)S(1)} %collective-permute-done.15.refs_1_), custom_call_target="tpu_custom_call" | custom-call | flops 1000000000 | bytes 1048576 | tf_op jit(solution)/shard_map/lags/pallas_call | solution.py:544
  (2 shorter events, 0.0 us)
Async XLA Ops:
  0.0 2.6 %collective-permute-start.1 = (bf16[3,2,4,64,256]{4,3,2,1,0:T(8,128)(2,1)}, bf16[3,2,4,64,256]{4,3,2,1,0:T(8,128)(2,1)S(1)}, u32[]{:S(2)}, u32[]{:S(2)}) collective-permute-start(bf16[3,2,4,64,256]{4,3,2,1,0:T(8,128)(2,1)} %bitcast.2), channel_id=1, source_target_pairs={{0,1},{1,0},{2,3},{3,2},{4,5},{5,4},{6,7},{7,6},{8,9},{9,8},{10,11... | collective-permute-start | bytes 2359304 | tf_op jit(solution)/shard_map/ppermute | solution.py:412
  0.5 2.1 %collective-permute-start = (s32[2,2,512]{2,1,0:T(2,128)}, s32[2,2,512]{2,1,0:T(2,128)S(1)}, u32[]{:S(2)}, u32[]{:S(2)}) collective-permute-start(s32[2,2,512]{2,1,0:T(2,128)} %own_pairs_ref.5), channel_id=1, source_target_pairs={{0,1},{1,0},{2,3},{3,2},{4,5},{5,4},{6,7},{7,6},{8,9},{9,8},{10,11... | collective-permute-start | bytes 24584 | tf_op jit(solution)/shard_map/ppermute | solution.py:412
  0.5 1.1 %copy-start.1 = (bf16[3,1,512,256]{3,2,1,0:T(8,128)(2,1)S(1)}, bf16[3,1,512,256]{3,2,1,0:T(8,128)(2,1)}, u32[]{:S(2)}) copy-start(bf16[3,1,512,256]{3,2,1,0:T(8,128)(2,1)} %param.4) | copy-start | bytes 2359300
  1.6 0.9 %copy-start.2 = (s32[2,2,512]{2,1,0:T(2,128)S(1)}, s32[2,2,512]{2,1,0:T(2,128)}, u32[]{:S(2)}) copy-start(s32[2,2,512]{2,1,0:T(2,128)} %own_pairs_ref.5) | copy-start | bytes 24580
  3.4 8.8 %collective-permute-start.2 = (bf16[480,128]{1,0:T(8,128)(2,1)S(1)}, bf16[480,128]{1,0:T(8,128)(2,1)S(1)}, u32[]{:S(2)}, u32[]{:S(2)}) collective-permute-start(bf16[480,128]{1,0:T(8,128)(2,1)S(1)} %get-tuple-element.32), channel_id=1, source_target_pairs={{0,2},{1,3},{2,0},{3,1},{4,6},{5,7},{6,4},{7,5},{8,10},{9,11},{10,... | collective-permute-start | bytes 368648 | tf_op jit(solution)/shard_map/ppermute | solution.py:412
  6.4 9.5 %collective-permute-start.3 = (bf16[480,128]{1,0:T(8,128)(2,1)S(1)}, bf16[480,128]{1,0:T(8,128)(2,1)S(1)}, u32[]{:S(2)}, u32[]{:S(2)}) collective-permute-start(bf16[480,128]{1,0:T(8,128)(2,1)S(1)} %get-tuple-element.33), channel_id=1, source_target_pairs={{0,4},{1,5},{2,6},{3,7},{4,0},{5,1},{6,2},{7,3},{8,12},{9,13},{10,... | collective-permute-start | bytes 368648 | tf_op jit(solution)/shard_map/ppermute | solution.py:412
  8.0 9.2 %collective-permute-start.4 = (bf16[480,128]{1,0:T(8,128)(2,1)S(1)}, bf16[480,128]{1,0:T(8,128)(2,1)S(1)}, u32[]{:S(2)}, u32[]{:S(2)}) collective-permute-start(bf16[480,128]{1,0:T(8,128)(2,1)S(1)} %get-tuple-element.34), channel_id=1, source_target_pairs={{0,6},{1,7},{2,4},{3,5},{4,2},{5,3},{6,0},{7,1},{8,14},{9,15},{10,... | collective-permute-start | bytes 368648 | tf_op jit(solution)/shard_map/ppermute | solution.py:412
  8.0 13.9 %collective-permute-start.5 = (bf16[320,128]{1,0:T(8,128)(2,1)S(1)}, bf16[320,128]{1,0:T(8,128)(2,1)S(1)}, u32[]{:S(2)}, u32[]{:S(2)}) collective-permute-start(bf16[320,128]{1,0:T(8,128)(2,1)S(1)} %get-tuple-element.36), channel_id=1, source_target_pairs={{0,8},{1,9},{2,10},{3,11},{4,12},{5,13},{6,14},{7,15},{8,0},{9,1},... | collective-permute-start | bytes 245768 | tf_op jit(solution)/shard_map/ppermute | solution.py:412
  11.0 18.9 %collective-permute-start.9 = (bf16[288,128]{1,0:T(8,128)(2,1)S(1)}, bf16[288,128]{1,0:T(8,128)(2,1)S(1)}, u32[]{:S(2)}, u32[]{:S(2)}) collective-permute-start(bf16[288,128]{1,0:T(8,128)(2,1)S(1)} %get-tuple-element.40), channel_id=1, source_target_pairs={{0,10},{1,11},{2,8},{3,9},{4,14},{5,15},{6,12},{7,13},{8,2},{9,3},... | collective-permute-start | bytes 221192 | tf_op jit(solution)/shard_map/ppermute | solution.py:412
  12.3 9.7 %collective-permute-start.6 = (bf16[288,128]{1,0:T(8,128)(2,1)S(1)}, bf16[288,128]{1,0:T(8,128)(2,1)S(1)}, u32[]{:S(2)}, u32[]{:S(2)}) collective-permute-start(bf16[288,128]{1,0:T(8,128)(2,1)S(1)} %get-tuple-element.37), channel_id=1, source_target_pairs={{0,12},{1,13},{2,14},{3,15},{4,8},{5,9},{6,10},{7,11},{8,4},{9,5},... | collective-permute-start | bytes 221192 | tf_op jit(solution)/shard_map/ppermute | solution.py:412
  15.9 14.8 %collective-permute-start.10 = (bf16[288,128]{1,0:T(8,128)(2,1)S(1)}, bf16[288,128]{1,0:T(8,128)(2,1)S(1)}, u32[]{:S(2)}, u32[]{:S(2)}) collective-permute-start(bf16[288,128]{1,0:T(8,128)(2,1)S(1)} %get-tuple-element.41), channel_id=1, source_target_pairs={{0,14},{1,15},{2,12},{3,13},{4,10},{5,11},{6,8},{7,9},{8,6},{9,7},... | collective-permute-start | bytes 221192 | tf_op jit(solution)/shard_map/ppermute | solution.py:412
  17.2 4.8 %copy-start.3 = (s32[16]{0:T(128)S(1)}, s32[16]{0:T(128)}, u32[]{:S(2)}) copy-start(s32[16]{0:T(128)} %counts_ref.7) | copy-start | bytes 196
  23.6 13.3 %collective-permute-start.7 = (bf16[256,128]{1,0:T(8,128)(2,1)S(1)}, bf16[256,128]{1,0:T(8,128)(2,1)S(1)}, u32[]{:S(2)}, u32[]{:S(2)}) collective-permute-start(bf16[256,128]{1,0:T(8,128)(2,1)S(1)} %get-tuple-element.38.after_2), channel_id=1, source_target_pairs={{0,8},{1,9},{2,10},{3,11},{4,12},{5,13},{6,14},{7,15},{8,0},{9,1},... | collective-permute-start | bytes 196616 | tf_op jit(solution)/shard_map/ppermute | solution.py:412
  27.9 9.0 %collective-permute-start.8 = (bf16[256,128]{1,0:T(8,128)(2,1)S(1)}, bf16[256,128]{1,0:T(8,128)(2,1)S(1)}, u32[]{:S(2)}, u32[]{:S(2)}) collective-permute-start(bf16[256,128]{1,0:T(8,128)(2,1)S(1)} %get-tuple-element.39), channel_id=1, source_target_pairs={{0,9},{1,8},{2,11},{3,10},{4,13},{5,12},{6,15},{7,14},{8,1},{9,0},... | collective-permute-start | bytes 196616 | tf_op jit(solution)/shard_map/ppermute | solution.py:412
  29.6 7.3 %collective-permute-start.11 = (bf16[256,128]{1,0:T(8,128)(2,1)S(1)}, bf16[256,128]{1,0:T(8,128)(2,1)S(1)}, u32[]{:S(2)}, u32[]{:S(2)}) collective-permute-start(bf16[256,128]{1,0:T(8,128)(2,1)S(1)} %get-tuple-element.43), channel_id=1, source_target_pairs={{0,1},{1,0},{2,3},{3,2},{4,5},{5,4},{6,7},{7,6},{8,9},{9,8},{10,11... | collective-permute-start | bytes 196616 | tf_op jit(solution)/shard_map/ppermute | solution.py:412
  33.9 6.4 %copy-start = (f32[256,256]{1,0:T(8,128)S(1)}, f32[256,256]{1,0:T(8,128)}, u32[]{:S(2)}) copy-start(f32[256,256]{1,0:T(8,128)} %constant.6.clone.inverse_ref) | copy-start | bytes 786436
  34.0 10.8 %collective-permute-start.14 = (bf16[384,128]{1,0:T(8,128)(2,1)S(1)}, bf16[384,128]{1,0:T(8,128)(2,1)S(1)}, u32[]{:S(2)}, u32[]{:S(2)}) collective-permute-start(bf16[384,128]{1,0:T(8,128)(2,1)S(1)} %get-tuple-element.49), channel_id=1, source_target_pairs={{0,8},{1,9},{2,10},{3,11},{4,12},{5,13},{6,14},{7,15},{8,0},{9,1},... | collective-permute-start | bytes 294920 | tf_op jit(solution)/shard_map/ppermute | solution.py:412
  36.9 8.8 %collective-permute-start.15 = (bf16[384,128]{1,0:T(8,128)(2,1)S(1)}, bf16[384,128]{1,0:T(8,128)(2,1)S(1)}, u32[]{:S(2)}, u32[]{:S(2)}) collective-permute-start(bf16[384,128]{1,0:T(8,128)(2,1)S(1)} %get-tuple-element.50), channel_id=1, source_target_pairs={{0,9},{1,8},{2,11},{3,10},{4,13},{5,12},{6,15},{7,14},{8,1},{9,0},... | collective-permute-start | bytes 294920 | tf_op jit(solution)/shard_map/ppermute | solution.py:412
  38.9 1.3 %collective-permute-start.12 = (bf16[192,128]{1,0:T(8,128)(2,1)S(1)}, bf16[192,128]{1,0:T(8,128)(2,1)S(1)}, u32[]{:S(2)}, u32[]{:S(2)}) collective-permute-start(bf16[192,128]{1,0:T(8,128)(2,1)S(1)} %get-tuple-element.45), channel_id=1, source_target_pairs={{0,1},{1,0},{2,3},{3,2},{4,5},{5,4},{6,7},{7,6},{8,9},{9,8},{10,11... | collective-permute-start | bytes 147464 | tf_op jit(solution)/shard_map/ppermute | solution.py:412
  39.1 1.2 %collective-permute-start.13 = (bf16[192,128]{1,0:T(8,128)(2,1)S(1)}, bf16[192,128]{1,0:T(8,128)(2,1)S(1)}, u32[]{:S(2)}, u32[]{:S(2)}) collective-permute-start(bf16[192,128]{1,0:T(8,128)(2,1)S(1)} %get-tuple-element.46), channel_id=1, source_target_pairs={{0,1},{1,0},{2,3},{3,2},{4,5},{5,4},{6,7},{7,6},{8,9},{9,8},{10,11... | collective-permute-start | bytes 147464 | tf_op jit(solution)/shard_map/ppermute | solution.py:412

commit v11 on v10

--- a/solution.py
+++ b/solution.py
@@ -307,11 +307,16 @@
     turn_blocks(cross_ref, PART, flat_ref)
 
 
-def far_kernel(bins, place_ref, counts_ref, listed_ref, flat_ref, after_ref, picked_0, picked_1):
+def far_kernel(bins, place_ref, counts_ref, listed_ref, flat_ref, picked_0, picked_1):
     listed = listed_ref[cross_full(listed_ref)[2] :].astype(jnp.float32)
     listing = listed.shape[0] // 2
     pick(place_ref, counts_ref, listed[:listing], flat_ref, bins, 2, picked_0)
     pick(place_ref, counts_ref, listed[listing:], flat_ref, bins, 3, picked_1)
+
+
+def hold_kernel(picked_0, picked_1, after_0, after_1, after_2, held_0, held_1):
+    held_0[...] = picked_0[...]
+    held_1[...] = picked_1[...]
 
 
 def early_kernel(sides, after_ref, *refs):
@@ -475,13 +480,12 @@
     part_2, part_3 = pl.pallas_call(
         functools.partial(far_kernel, PART),
         out_shape=[part_packed, part_packed],
-        in_specs=[smem, smem, vmem, vmem, pl.BlockSpec(memory_space=pl.ANY)],
+        in_specs=[smem, smem, vmem, vmem],
         out_specs=[vmem, vmem],
         compiler_params=params,
         cost_estimate=cost(1),
         name="part_far",
-    )(place, counts, far[0], part_flat, late[0])
-    sent, part_2, part_3 = part_2, swap(part_2, half), swap(part_3, half + 1)
+    )(place, counts, far[0], part_flat)
     part_0, part_1 = pl.pallas_call(
         functools.partial(near_kernel, PART, 1),
         out_shape=[part_packed, part_packed],
@@ -504,6 +508,16 @@
         cost_estimate=cost(0.001),
         name="early",
     )(part_flat, *sides, *early)
+    sent, part_3 = pl.pallas_call(
+        hold_kernel,
+        out_shape=[part_packed, part_packed],
+        in_specs=[vmem] * 2 + [pl.BlockSpec(memory_space=pl.ANY)] * 3,
+        out_specs=[vmem] * 2,
+        compiler_params=params,
+        cost_estimate=cost(0.1),
+        name="hold",
+    )(part_2, part_3, part_0, sums, late[0])
+    part_2, part_3 = swap(sent, half), swap(part_3, half + 1)
     full_flat, full_2, full_3 = pl.pallas_call(
         full_kernel,
         out_shape=[full_blocks, full_packed, full_packed],
@@ -521,12 +535,12 @@
     full_0, *full_1 = pl.pallas_call(
         functools.partial(near_kernel, FULL, 2),
         out_shape=[full_packed, half_packed, half_packed],
-        in_specs=[smem, smem] + [vmem] * 3 + [pl.BlockSpec(memory_space=pl.ANY)] * 3,
+        in_specs=[smem, smem] + [vmem] * 3 + [pl.BlockSpec(memory_space=pl.ANY)] * 2,
         out_specs=[vmem] * 3,
         compiler_params=params,
         cost_estimate=cost(0.5),
         name="full_near",
-    )(place, counts, pairs, near_pairs, full_flat, part_1, part_2, part_3)
+    )(place, counts, pairs, near_pairs, full_flat, part_2, part_3)
     full_1 = [swap(x, 1) for x in full_1]
 
     first, tables = pl.pallas_call(

time: 47.4 us -> 47.1 us (level)
  starting transfers between devices: 22.3 us -> 20.3 us
  waiting for transfers between devices: 8.08 us -> 9.69 us
    ppermute x16, starting transfers between devices: 22.3 us -> 20.3 us  [swap(): return lax.ppermute(x, 'cell', [(i, i ^ mask) for i in range(cells)])]
    ppermute x16, waiting for transfers between devices: 8.08 us -> 9.69 us  [swap(): return lax.ppermute(x, 'cell', [(i, i ^ mask) for i in range(cells)])]
  transfers between devices with their start and end apart: 16 -> 16, of which waited for: 6 -> 5; matrix products, arithmetic and copies ran while one was open for 0% -> 0% of each run, Pallas kernels for 28% -> 28%
where the time goes in v11:
time: 47.1 us; the launch traced here: 46.9 us
  starting transfers between devices  20.3 us (43%)
  Pallas kernels  15.7 us (33%)
  waiting for transfers between devices  9.69 us (21%)
  local copies, waits for them, and re-layouts  1.15 us (2%)
    ppermute x16, starting transfers between devices, swap(): return lax.ppermute(x, 'cell', [(i, i ^ mask) for i in range(cells)])  20.3 us
    ppermute x16, waiting for transfers between devices, swap(): return lax.ppermute(x, 'cell', [(i, i ^ mask) for i in range(cells)])  9.69 us
    pallas_call x1, Pallas kernels, on_device(): pl.pallas_call(full_kernel, out_shape=[full_blocks, full_packed, full_pac...  3.31 us
    pallas_call x1, Pallas kernels, on_device(): pl.pallas_call(functools.partial(near_kernel, FULL, 2), out_shape=[full_p...  2 us
    pallas_call x1, Pallas kernels, on_device(): pl.pallas_call(functools.partial(first_lags_kernel, groups), out_shape=[s...  1.78 us
    pallas_call x1, Pallas kernels, on_device(): pl.pallas_call(functools.partial(near_kernel, PART, 1), out_shape=[part_p...  1.68 us
    pallas_call x1, Pallas kernels, on_device(): pl.pallas_call(functools.partial(far_kernel, PART), out_shape=[part_packe...  1.67 us
    pallas_call x1, Pallas kernels, on_device(): pl.pallas_call(lag_kernel, out_shape=shape(2, count, samples, dtype=jnp.f...  1.65 us
  transfers between devices with their start and end apart: 16, of which 5 were waited for; matrix products, arithmetic and copies ran while one was open for 0% of the time, Pallas kernels for 28%

profile of v11, /device:TPU:0, one launch (start us, length us, event | category | flops | bytes accessed | tf_op | source)
XLA Modules:
  0.0 46.9 jit_solution(6079349415210914429)
XLA Ops:
  0.0 0.5 collective-permute-start.1
  0.5 0.1 collective-permute-start
  0.5 1.1 %copy-done.1 = bf16[3,1,512,256]{3,2,1,0:T(8,128)(2,1)S(1)} copy-done((bf16[3,1,512,256]{3,2,1,0:T(8,128)(2,1)S(1)}, bf16[3,1,512,256]{3,2,1,0:T(8,128)(2,1)}, u32[]{:S(2)}) %copy-start.1) | copy-done | bytes 786456
  1.6 0.8 %own_spectra.1 = (bf16[4,96,128]{2,1,0:T(8,128)(2,1)S(1)}, bf16[8,144,128]{2,1,0:T(8,128)(2,1)S(1)}, bf16[128,256]{1,0:T(8,128)(2,1)S(1)}) custom-call(s32[1]{0:T(128)} %bitcast.place_ref, bf16[3,2,4,64,256]{4,3,2,1,0:T(8,128)(2,1)S(1)} %bitcast.3), custom_call_target="tpu_custom_call" | custom-call | flops 1000000000 | bytes 1048576 | tf_op jit(solution)/shard_map/own_spectra/pallas_call | solution.py:434
  2.5 0.1 collective-permute-done.near_pairs_ref
  2.6 0.0 collective-permute-done.1.windows_ref
  2.6 0.0 copy-done.2
  2.6 0.8 %near_spectra.1 = (bf16[480,128]{1,0:T(8,128)(2,1)S(1)}, bf16[480,128]{1,0:T(8,128)(2,1)S(1)}, bf16[480,128]{1,0:T(8,128)(2,1)S(1)}, bf16[480,128]{1,0:T(8,128)(...) custom-call(s32[1]{0:T(128)} %bitcast.place_ref, ...), custom_call_target="tpu_custom_call" | custom-call | flops 1000000000 | bytes 1048576 | tf_op jit(solution)/shard_map/near_spectra/pallas_call | solution.py:448
  3.4 3.0 %collective-permute-start.2 = (bf16[480,128]{1,0:T(8,128)(2,1)S(1)}, bf16[480,128]{1,0:T(8,128)(2,1)S(1)}, u32[]{:S(2)}, u32[]{:S(2)}) collective-permute-start(bf16[480,128]{1,0:T(8,128)(2,1)S(1)} %get-tuple-element.34), channel_id=1, source_target_pairs={{0,2},{1,3},{2,0},{3,1},{4,6},{5,7},{6,4},{7,5},{8,10},{9,11},{10,... | collective-permute-start | bytes 368648 | tf_op jit(solution)/shard_map/ppermute | solution.py:417
  6.4 1.6 %collective-permute-start.3 = (bf16[480,128]{1,0:T(8,128)(2,1)S(1)}, bf16[480,128]{1,0:T(8,128)(2,1)S(1)}, u32[]{:S(2)}, u32[]{:S(2)}) collective-permute-start(bf16[480,128]{1,0:T(8,128)(2,1)S(1)} %get-tuple-element.35), channel_id=1, source_target_pairs={{0,4},{1,5},{2,6},{3,7},{4,0},{5,1},{6,2},{7,3},{8,12},{9,13},{10,... | collective-permute-start | bytes 368648 | tf_op jit(solution)/shard_map/ppermute | solution.py:417
  8.0 0.0 collective-permute-start.4
  8.0 3.0 %collective-permute-start.5 = (bf16[320,128]{1,0:T(8,128)(2,1)S(1)}, bf16[320,128]{1,0:T(8,128)(2,1)S(1)}, u32[]{:S(2)}, u32[]{:S(2)}) collective-permute-start(bf16[320,128]{1,0:T(8,128)(2,1)S(1)} %get-tuple-element.38), channel_id=1, source_target_pairs={{0,8},{1,9},{2,10},{3,11},{4,12},{5,13},{6,14},{7,15},{8,0},{9,1},... | collective-permute-start | bytes 245768 | tf_op jit(solution)/shard_map/ppermute | solution.py:417
  11.0 1.3 %collective-permute-start.6 = (bf16[288,128]{1,0:T(8,128)(2,1)S(1)}, bf16[288,128]{1,0:T(8,128)(2,1)S(1)}, u32[]{:S(2)}, u32[]{:S(2)}) collective-permute-start(bf16[288,128]{1,0:T(8,128)(2,1)S(1)} %get-tuple-element.41), channel_id=1, source_target_pairs={{0,10},{1,11},{2,8},{3,9},{4,14},{5,15},{6,12},{7,13},{8,2},{9,3},... | collective-permute-start | bytes 221192 | tf_op jit(solution)/shard_map/ppermute | solution.py:417
  12.2 0.0 collective-permute-done.2.refs_1_
  12.3 3.6 %collective-permute-start.7 = (bf16[288,128]{1,0:T(8,128)(2,1)S(1)}, bf16[288,128]{1,0:T(8,128)(2,1)S(1)}, u32[]{:S(2)}, u32[]{:S(2)}) collective-permute-start(bf16[288,128]{1,0:T(8,128)(2,1)S(1)} %get-tuple-element.42), channel_id=1, source_target_pairs={{0,12},{1,13},{2,14},{3,15},{4,8},{5,9},{6,10},{7,11},{8,4},{9,5},... | collective-permute-start | bytes 221192 | tf_op jit(solution)/shard_map/ppermute | solution.py:417
  15.9 0.0 collective-permute-done.3.refs_2_
  15.9 1.3 %collective-permute-start.10 = (bf16[288,128]{1,0:T(8,128)(2,1)S(1)}, bf16[288,128]{1,0:T(8,128)(2,1)S(1)}, u32[]{:S(2)}, u32[]{:S(2)}) collective-permute-start(bf16[288,128]{1,0:T(8,128)(2,1)S(1)} %get-tuple-element.45), channel_id=1, source_target_pairs={{0,14},{1,15},{2,12},{3,13},{4,10},{5,11},{6,8},{7,9},{8,6},{9,7},... | collective-permute-start | bytes 221192 | tf_op jit(solution)/shard_map/ppermute | solution.py:417
  17.2 0.0 collective-permute-done.4.refs_3_
  17.2 1.2 %part.1.flat_ref.after_ref = bf16[2,2,128,256]{3,2,1,0:T(8,128)(2,1)S(1)} custom-call(bf16[480,128]{1,0:T(8,128)(2,1)S(1)} %get-tuple-element.33.refs_0_, bf16[480,128]{1,0:T(8,128)(2,1)S(1)} %collective-permute-done.2.refs_1_, bf16[480,128]{1,0:T(8,128)(2,1)S(1)} %collective-permute-done.3.refs_2_, bf16[480,128]{1,0:T(8,128)(2,1)S(1)} %collective-permute-done.4.refs_3_), custom_call_target="tpu_custom_call" | custom-call | flops 2000000000 | bytes 1048576 | tf_op jit(solution)/shard_map/part/pallas_call | solution.py:467
  18.3 0.0 copy-start.3
  18.4 5.4 %collective-permute-done.6.refs_5_ = bf16[288,128]{1,0:T(8,128)(2,1)S(1)} collective-permute-done((bf16[288,128]{1,0:T(8,128)(2,1)S(1)}, bf16[288,128]{1,0:T(8,128)(2,1)S(1)}, u32[]{:S(2)}, u32[]{:S(2)}) %collective-permute-start.6) | collective-permute-done | bytes 73760 | tf_op jit(solution)/shard_map/ppermute | solution.py:417
  23.8 0.0 collective-permute-done.5.listed_ref.refs_4_
  23.8 0.7 %early.1.after_1.before_ref = f32[3072,128]{1,0:T(8,128)S(1)} custom-call(bf16[2,2,128,256]{3,2,1,0:T(8,128)(2,1)S(1)} %part.1.flat_ref.after_ref, bf16[480,128]{1,0:T(8,128)(2,1)S(1)} %get-tuple-element.33.refs_0_, bf16[480,128]{1,0:T(8,128)(2,1)S(1)} %collective-permute-done.2.refs_1_, bf16[480,128]{1,0:T(8,128)(2,1)S(1)} %collective-permute-done.3.refs_2_, ...), custom_call_target="tpu_custom_call" | custom-call | flops 1000000 | bytes 1048576 | tf_op jit(solution)/shard_map/early/pallas_call | solution.py:499
  24.5 0.0 copy-done.3
  24.5 1.7 %part_far.1 = (bf16[256,128]{1,0:T(8,128)(2,1)S(1)}, bf16[256,128]{1,0:T(8,128)(2,1)S(1)}) custom-call(s32[1]{0:T(128)} %bitcast.place_ref, s32[16]{0:T(128)S(1)} %copy-done.3, bf16[320,128]{1,0:T(8,128)(2,1)S(1)} %collective-permute-done.5.listed_ref.refs_4_, bf16[2,2,128,256]{3,2,1,0:T(8,128)(2,1)S(1)} %part.1.flat_ref.after_ref), custom_call_target="tpu_custom_call" | custom-call | flops 1000000000 | bytes 1048576 | tf_op jit(solution)/shard_map/part_far/pallas_call | solution.py:480
  26.2 1.7 %part_near.1 = (bf16[256,128]{1,0:T(8,128)(2,1)S(1)}, bf16[256,128]{1,0:T(8,128)(2,1)S(1)}) custom-call(s32[1]{0:T(128)} %bitcast.place_ref, s32[16]{0:T(128)S(1)} %copy-done.3, s32[2,2,512]{2,1,0:T(2,128)S(1)} %copy-done.2, s32[2,2,512]{2,1,0:T(2,128)S(1)} %collective-permute-done.near_pairs_ref, bf16[2,2,128,256]{3,2,1,0:T(8,128)(2,1)S(1)} %part.1.flat_ref.after_ref), custom_call_target="tpu_custom_call" | custom-call | flops 1000000000 | bytes 1048576 | tf_op jit(solution)/shard_map/part_near/pallas_call | solution.py:489
  27.9 0.0 collective-permute-done.7.after_2.refs_0_
  27.9 0.1 collective-permute-start.8
  28.0 0.1 collective-permute-start.9
  28.1 0.0 collective-permute-done.10.refs_1_
  28.1 3.3 %full.1 = (bf16[2,2,256,256]{3,2,1,0:T(8,128)(2,1)S(1)}, bf16[384,128]{1,0:T(8,128)(2,1)S(1)}, bf16[384,128]{1,0:T(8,128)(2,1)S(1)}) custom-call(s32[1]{0:T(128)} %bitcast.place_ref, s32[16]{0:T(128)S(1)} %copy-done.3, bf16[320,128]{1,0:T(8,128)(2,1)S(1)} %collective-permute-done.5.listed_ref.refs_4_, ...), custom_call_target="tpu_custom_call" | custom-call | flops 10000000000 | bytes 1048576 | tf_op jit(solution)/shard_map/full/pallas_call | solution.py:521
  31.4 0.0 copy-start
  31.4 2.9 %collective-permute-start.14 = (bf16[384,128]{1,0:T(8,128)(2,1)S(1)}, bf16[384,128]{1,0:T(8,128)(2,1)S(1)}, u32[]{:S(2)}, u32[]{:S(2)}) collective-permute-start(bf16[384,128]{1,0:T(8,128)(2,1)S(1)} %get-tuple-element.53), channel_id=1, source_target_pairs={{0,8},{1,9},{2,10},{3,11},{4,12},{5,13},{6,14},{7,15},{8,0},{9,1},... | collective-permute-start | bytes 294920 | tf_op jit(solution)/shard_map/ppermute | solution.py:417
  34.3 2.4 %collective-permute-start.15 = (bf16[384,128]{1,0:T(8,128)(2,1)S(1)}, bf16[384,128]{1,0:T(8,128)(2,1)S(1)}, u32[]{:S(2)}, u32[]{:S(2)}) collective-permute-start(bf16[384,128]{1,0:T(8,128)(2,1)S(1)} %get-tuple-element.54), channel_id=1, source_target_pairs={{0,9},{1,8},{2,11},{3,10},{4,13},{5,12},{6,15},{7,14},{8,1},{9,0},... | collective-permute-start | bytes 294920 | tf_op jit(solution)/shard_map/ppermute | solution.py:417
  36.7 0.0 collective-permute-start.11
  36.7 0.0 collective-permute-done.8.refs_0_.refs_1_
  36.7 0.0 collective-permute-done.9.refs_1_.refs_2_
  36.7 2.0 %full_near.1 = (bf16[384,128]{1,0:T(8,128)(2,1)S(1)}, bf16[192,128]{1,0:T(8,128)(2,1)S(1)}, bf16[192,128]{1,0:T(8,128)(2,1)S(1)}) custom-call(s32[1]{0:T(128)} %bitcast.place_ref, s32[16]{0:T(128)S(1)} %copy-done.3, s32[2,2,512]{2,1,0:T(2,128)S(1)} %copy-done.2, s32[2,2,512]{2,1,0:T(2,128)S(1)} %collective-permute-done.near_pairs_ref, ...), custom_call_target="tpu_custom_call" | custom-call | flops 500000000 | bytes 1048576 | tf_op jit(solution)/shard_map/full_near/pallas_call | solution.py:535
  38.7 0.6 %collective-permute-start.12 = (bf16[192,128]{1,0:T(8,128)(2,1)S(1)}, bf16[192,128]{1,0:T(8,128)(2,1)S(1)}, u32[]{:S(2)}, u32[]{:S(2)}) collective-permute-start(bf16[192,128]{1,0:T(8,128)(2,1)S(1)} %get-tuple-element.49), channel_id=1, source_target_pairs={{0,1},{1,0},{2,3},{3,2},{4,5},{5,4},{6,7},{7,6},{8,9},{9,8},{10,11... | collective-permute-start | bytes 147464 | tf_op jit(solution)/shard_map/ppermute | solution.py:417
  39.3 0.1 collective-permute-start.13
  39.4 0.0 collective-permute-done.11.refs_4_
  39.4 0.8 %collective-permute-done.12.refs_5_ = bf16[192,128]{1,0:T(8,128)(2,1)S(1)} collective-permute-done((bf16[192,128]{1,0:T(8,128)(2,1)S(1)}, bf16[192,128]{1,0:T(8,128)(2,1)S(1)}, u32[]{:S(2)}, u32[]{:S(2)}) %collective-permute-start.12) | collective-permute-done | bytes 49184 | tf_op jit(solution)/shard_map/ppermute | solution.py:417
  40.2 0.3 collective-permute-done.13.refs_6_
  40.5 0.0 copy-done
  40.5 1.8 %first_lags.1 = (f32[2,512,256]{2,1,0:T(8,128)S(1)}, bf16[2,2,96,512]{3,2,1,0:T(8,128)(2,1)S(1)}) custom-call(s32[1]{0:T(128)} %bitcast.place_ref, f32[256,256]{1,0:T(8,128)S(1)} %copy-done, bf16[256,128]{1,0:T(8,128)(2,1)S(1)} %get-tuple-element.37.after_0.refs_0_, bf16[256,128]{1,0:T(8,128)(2,1)S(1)} %collective-permute-done.8.refs_0_.refs_1_, ...), custom_call_target="tpu_custom_call" | custom-call | flops 1000000 | bytes 1048576 | tf_op jit(solution)/shard_map/first_lags/pallas_call | solution.py:546
  42.3 0.0 collective-permute-done.14.refs_0_
  42.3 3.0 %collective-permute-done.15.refs_1_ = bf16[384,128]{1,0:T(8,128)(2,1)S(1)} collective-permute-done((bf16[384,128]{1,0:T(8,128)(2,1)S(1)}, bf16[384,128]{1,0:T(8,128)(2,1)S(1)}, u32[]{:S(2)}, u32[]{:S(2)}) %collective-permute-start.15) | collective-permute-done | bytes 98336 | tf_op jit(solution)/shard_map/ppermute | solution.py:417
  45.3 1.7 %lags.1 = f32[2,512,256]{2,1,0:T(8,128)} custom-call(f32[2,512,256]{2,1,0:T(8,128)S(1)} %get-tuple-element.51.first_ref, bf16[2,2,96,512]{3,2,1,0:T(8,128)(2,1)S(1)} %get-tuple-element.52.table_ref, bf16[384,128]{1,0:T(8,128)(2,1)S(1)} %collective-permute-done.14.refs_0_, bf16[384,128]{1,0:T(8,128)(2,1)S(1)} %collective-permute-done.15.refs_1_), custom_call_target="tpu_custom_call" | custom-call | flops 1000000000 | bytes 1048576 | tf_op jit(solution)/shard_map/lags/pallas_call | solution.py:558
  (3 shorter events, 0.0 us)
Async XLA Ops:
  0.0 2.6 %collective-permute-start.1 = (bf16[3,2,4,64,256]{4,3,2,1,0:T(8,128)(2,1)}, bf16[3,2,4,64,256]{4,3,2,1,0:T(8,128)(2,1)S(1)}, u32[]{:S(2)}, u32[]{:S(2)}) collective-permute-start(bf16[3,2,4,64,256]{4,3,2,1,0:T(8,128)(2,1)} %bitcast.2), channel_id=1, source_target_pairs={{0,1},{1,0},{2,3},{3,2},{4,5},{5,4},{6,7},{7,6},{8,9},{9,8},{10,11... | collective-permute-start | bytes 2359304 | tf_op jit(solution)/shard_map/ppermute | solution.py:417
  0.5 2.1 %collective-permute-start = (s32[2,2,512]{2,1,0:T(2,128)}, s32[2,2,512]{2,1,0:T(2,128)S(1)}, u32[]{:S(2)}, u32[]{:S(2)}) collective-permute-start(s32[2,2,512]{2,1,0:T(2,128)} %own_pairs_ref.5), channel_id=1, source_target_pairs={{0,1},{1,0},{2,3},{3,2},{4,5},{5,4},{6,7},{7,6},{8,9},{9,8},{10,11... | collective-permute-start | bytes 24584 | tf_op jit(solution)/shard_map/ppermute | solution.py:417
  0.5 1.1 %copy-start.1 = (bf16[3,1,512,256]{3,2,1,0:T(8,128)(2,1)S(1)}, bf16[3,1,512,256]{3,2,1,0:T(8,128)(2,1)}, u32[]{:S(2)}) copy-start(bf16[3,1,512,256]{3,2,1,0:T(8,128)(2,1)} %param.4) | copy-start | bytes 2359300
  1.6 0.9 %copy-start.2 = (s32[2,2,512]{2,1,0:T(2,128)S(1)}, s32[2,2,512]{2,1,0:T(2,128)}, u32[]{:S(2)}) copy-start(s32[2,2,512]{2,1,0:T(2,128)} %own_pairs_ref.5) | copy-start | bytes 24580
  3.4 8.8 %collective-permute-start.2 = (bf16[480,128]{1,0:T(8,128)(2,1)S(1)}, bf16[480,128]{1,0:T(8,128)(2,1)S(1)}, u32[]{:S(2)}, u32[]{:S(2)}) collective-permute-start(bf16[480,128]{1,0:T(8,128)(2,1)S(1)} %get-tuple-element.34), channel_id=1, source_target_pairs={{0,2},{1,3},{2,0},{3,1},{4,6},{5,7},{6,4},{7,5},{8,10},{9,11},{10,... | collective-permute-start | bytes 368648 | tf_op jit(solution)/shard_map/ppermute | solution.py:417
  6.4 9.5 %collective-permute-start.3 = (bf16[480,128]{1,0:T(8,128)(2,1)S(1)}, bf16[480,128]{1,0:T(8,128)(2,1)S(1)}, u32[]{:S(2)}, u32[]{:S(2)}) collective-permute-start(bf16[480,128]{1,0:T(8,128)(2,1)S(1)} %get-tuple-element.35), channel_id=1, source_target_pairs={{0,4},{1,5},{2,6},{3,7},{4,0},{5,1},{6,2},{7,3},{8,12},{9,13},{10,... | collective-permute-start | bytes 368648 | tf_op jit(solution)/shard_map/ppermute | solution.py:417
  8.0 9.2 %collective-permute-start.4 = (bf16[480,128]{1,0:T(8,128)(2,1)S(1)}, bf16[480,128]{1,0:T(8,128)(2,1)S(1)}, u32[]{:S(2)}, u32[]{:S(2)}) collective-permute-start(bf16[480,128]{1,0:T(8,128)(2,1)S(1)} %get-tuple-element.36), channel_id=1, source_target_pairs={{0,6},{1,7},{2,4},{3,5},{4,2},{5,3},{6,0},{7,1},{8,14},{9,15},{10,... | collective-permute-start | bytes 368648 | tf_op jit(solution)/shard_map/ppermute | solution.py:417
  8.0 15.8 %collective-permute-start.5 = (bf16[320,128]{1,0:T(8,128)(2,1)S(1)}, bf16[320,128]{1,0:T(8,128)(2,1)S(1)}, u32[]{:S(2)}, u32[]{:S(2)}) collective-permute-start(bf16[320,128]{1,0:T(8,128)(2,1)S(1)} %get-tuple-element.38), channel_id=1, source_target_pairs={{0,8},{1,9},{2,10},{3,11},{4,12},{5,13},{6,14},{7,15},{8,0},{9,1},... | collective-permute-start | bytes 245768 | tf_op jit(solution)/shard_map/ppermute | solution.py:417
  11.0 12.8 %collective-permute-start.6 = (bf16[288,128]{1,0:T(8,128)(2,1)S(1)}, bf16[288,128]{1,0:T(8,128)(2,1)S(1)}, u32[]{:S(2)}, u32[]{:S(2)}) collective-permute-start(bf16[288,128]{1,0:T(8,128)(2,1)S(1)} %get-tuple-element.41), channel_id=1, source_target_pairs={{0,10},{1,11},{2,8},{3,9},{4,14},{5,15},{6,12},{7,13},{8,2},{9,3},... | collective-permute-start | bytes 221192 | tf_op jit(solution)/shard_map/ppermute | solution.py:417
  12.3 15.7 %collective-permute-start.7 = (bf16[288,128]{1,0:T(8,128)(2,1)S(1)}, bf16[288,128]{1,0:T(8,128)(2,1)S(1)}, u32[]{:S(2)}, u32[]{:S(2)}) collective-permute-start(bf16[288,128]{1,0:T(8,128)(2,1)S(1)} %get-tuple-element.42), channel_id=1, source_target_pairs={{0,12},{1,13},{2,14},{3,15},{4,8},{5,9},{6,10},{7,11},{8,4},{9,5},... | collective-permute-start | bytes 221192 | tf_op jit(solution)/shard_map/ppermute | solution.py:417
  15.9 12.2 %collective-permute-start.10 = (bf16[288,128]{1,0:T(8,128)(2,1)S(1)}, bf16[288,128]{1,0:T(8,128)(2,1)S(1)}, u32[]{:S(2)}, u32[]{:S(2)}) collective-permute-start(bf16[288,128]{1,0:T(8,128)(2,1)S(1)} %get-tuple-element.45), channel_id=1, source_target_pairs={{0,14},{1,15},{2,12},{3,13},{4,10},{5,11},{6,8},{7,9},{8,6},{9,7},... | collective-permute-start | bytes 221192 | tf_op jit(solution)/shard_map/ppermute | solution.py:417
  18.3 6.2 %copy-start.3 = (s32[16]{0:T(128)S(1)}, s32[16]{0:T(128)}, u32[]{:S(2)}) copy-start(s32[16]{0:T(128)} %counts_ref.7) | copy-start | bytes 196
  27.9 8.8 %collective-permute-start.8 = (bf16[256,128]{1,0:T(8,128)(2,1)S(1)}, bf16[256,128]{1,0:T(8,128)(2,1)S(1)}, u32[]{:S(2)}, u32[]{:S(2)}) collective-permute-start(bf16[256,128]{1,0:T(8,128)(2,1)S(1)} %get-tuple-element.43.after_2), channel_id=1, source_target_pairs={{0,8},{1,9},{2,10},{3,11},{4,12},{5,13},{6,14},{7,15},{8,0},{9,1},... | collective-permute-start | bytes 196616 | tf_op jit(solution)/shard_map/ppermute | solution.py:417
  28.0 8.7 %collective-permute-start.9 = (bf16[256,128]{1,0:T(8,128)(2,1)S(1)}, bf16[256,128]{1,0:T(8,128)(2,1)S(1)}, u32[]{:S(2)}, u32[]{:S(2)}) collective-permute-start(bf16[256,128]{1,0:T(8,128)(2,1)S(1)} %get-tuple-element.44), channel_id=1, source_target_pairs={{0,9},{1,8},{2,11},{3,10},{4,13},{5,12},{6,15},{7,14},{8,1},{9,0},... | collective-permute-start | bytes 196616 | tf_op jit(solution)/shard_map/ppermute | solution.py:417
  31.4 9.1 %copy-start = (f32[256,256]{1,0:T(8,128)S(1)}, f32[256,256]{1,0:T(8,128)}, u32[]{:S(2)}) copy-start(f32[256,256]{1,0:T(8,128)} %constant.6.clone.inverse_ref) | copy-start | bytes 786436
  31.4 10.9 %collective-permute-start.14 = (bf16[384,128]{1,0:T(8,128)(2,1)S(1)}, bf16[384,128]{1,0:T(8,128)(2,1)S(1)}, u32[]{:S(2)}, u32[]{:S(2)}) collective-permute-start(bf16[384,128]{1,0:T(8,128)(2,1)S(1)} %get-tuple-element.53), channel_id=1, source_target_pairs={{0,8},{1,9},{2,10},{3,11},{4,12},{5,13},{6,14},{7,15},{8,0},{9,1},... | collective-permute-start | bytes 294920 | tf_op jit(solution)/shard_map/ppermute | solution.py:417
  34.3 11.0 %collective-permute-start.15 = (bf16[384,128]{1,0:T(8,128)(2,1)S(1)}, bf16[384,128]{1,0:T(8,128)(2,1)S(1)}, u32[]{:S(2)}, u32[]{:S(2)}) collective-permute-start(bf16[384,128]{1,0:T(8,128)(2,1)S(1)} %get-tuple-element.54), channel_id=1, source_target_pairs={{0,9},{1,8},{2,11},{3,10},{4,13},{5,12},{6,15},{7,14},{8,1},{9,0},... | collective-permute-start | bytes 294920 | tf_op jit(solution)/shard_map/ppermute | solution.py:417
  36.7 2.7 %collective-permute-start.11 = (bf16[256,128]{1,0:T(8,128)(2,1)S(1)}, bf16[256,128]{1,0:T(8,128)(2,1)S(1)}, u32[]{:S(2)}, u32[]{:S(2)}) collective-permute-start(bf16[256,128]{1,0:T(8,128)(2,1)S(1)} %get-tuple-element.48), channel_id=1, source_target_pairs={{0,1},{1,0},{2,3},{3,2},{4,5},{5,4},{6,7},{7,6},{8,9},{9,8},{10,11... | collective-permute-start | bytes 196616 | tf_op jit(solution)/shard_map/ppermute | solution.py:417
  38.7 1.5 %collective-permute-start.12 = (bf16[192,128]{1,0:T(8,128)(2,1)S(1)}, bf16[192,128]{1,0:T(8,128)(2,1)S(1)}, u32[]{:S(2)}, u32[]{:S(2)}) collective-permute-start(bf16[192,128]{1,0:T(8,128)(2,1)S(1)} %get-tuple-element.49), channel_id=1, source_target_pairs={{0,1},{1,0},{2,3},{3,2},{4,5},{5,4},{6,7},{7,6},{8,9},{9,8},{10,11... | collective-permute-start | bytes 147464 | tf_op jit(solution)/shard_map/ppermute | solution.py:417
  39.3 1.2 %collective-permute-start.13 = (bf16[192,128]{1,0:T(8,128)(2,1)S(1)}, bf16[192,128]{1,0:T(8,128)(2,1)S(1)}, u32[]{:S(2)}, u32[]{:S(2)}) collective-permute-start(bf16[192,128]{1,0:T(8,128)(2,1)S(1)} %get-tuple-element.50), channel_id=1, source_target_pairs={{0,1},{1,0},{2,3},{3,2},{4,5},{5,4},{6,7},{7,6},{8,9},{9,8},{10,11... | collective-permute-start | bytes 147464 | tf_op jit(solution)/shard_map/ppermute | solution.py:417

commit v12 on v11

--- a/solution.py
+++ b/solution.py
@@ -255,20 +255,21 @@
         start += size
     if start < traces * rows:
         trace_ref[start:] = jnp.zeros((traces * rows - start, LANES), jnp.float32)
+    lower = lax.broadcasted_iota(jnp.int32, (traces, LANES), 1) < slots
     for k in range(bins):
-        real = trace_ref[pl.ds(k, traces, stride=rows), :].astype(jnp.bfloat16)
-        imag = trace_ref[pl.ds(bins + k, traces, stride=rows), :].astype(jnp.bfloat16)
-        left = jnp.concatenate([real, imag], axis=0)[:, :slots]
+        real = trace_ref[pl.ds(k, traces, stride=rows), :]
+        imag = trace_ref[pl.ds(bins + k, traces, stride=rows), :]
+        left = jnp.concatenate([real, imag]).astype(jnp.bfloat16)[:, :slots]
         right = jnp.concatenate(
-            [jnp.concatenate([real, imag], axis=1), jnp.concatenate([imag, -real], axis=1)], axis=0
-        )
+            [
+                jnp.where(lower, pltpu.roll(real, slots, 1), imag),
+                jnp.where(lower, pltpu.roll(imag, slots, 1), -real),
+            ]
+        ).astype(jnp.bfloat16)
         cross = lax.dot_general(left, right, TN, preferred_element_type=jnp.float32)
-        for part in range(2):
-            at = (part * bins + k) * slots
-            value = cross[:, part * LANES : (part + 1) * LANES]
-            if before_ref is not None:
-                value += before_ref[at : at + slots]
-            sums_ref[at : at + slots] = value
+        if before_ref is not None:
+            cross += before_ref[k * slots : (k + 1) * slots]
+        sums_ref[k * slots : (k + 1) * slots] = cross
 
 
 def turn_blocks(cross_ref, bins, flat_ref):
@@ -276,17 +277,17 @@
     empty = jnp.zeros((width(bins) - bins, LANES), jnp.float32)
     for own in range(2):
         for at in range(SLOTS // runs):
+            block = []
+            for i in range(runs):
+                block.append(cross_ref[pl.ds(own * SLOTS + at * runs + i, bins, stride=slots), :])
+                block += [empty] * (bins < width(bins))
+            block = jnp.concatenate(block).T.astype(jnp.bfloat16)
             for part in range(2):
-                first = part * bins * slots + own * SLOTS + at * runs
-                block = []
-                for i in range(runs):
-                    block.append(cross_ref[pl.ds(first + i, bins, stride=slots), :])
-                    block += [empty] * (bins < width(bins))
-                block = jnp.concatenate(block).T.astype(jnp.bfloat16)
                 for far in range(2):
+                    start = (part * 2 + far) * SLOTS
                     flat_ref[
                         own, far, at * SLOTS : (at + 1) * SLOTS, part * LANES : (part + 1) * LANES
-                    ] = block[slots + far * SLOTS : slots + (far + 1) * SLOTS]
+                    ] = block[start : start + SLOTS]
 
 
 def side_part(ref):
@@ -314,12 +315,11 @@
     pick(place_ref, counts_ref, listed[listing:], flat_ref, bins, 3, picked_1)
 
 
-def hold_kernel(picked_0, picked_1, after_0, after_1, after_2, held_0, held_1):
-    held_0[...] = picked_0[...]
-    held_1[...] = picked_1[...]
-
-
-def early_kernel(sides, after_ref, *refs):
+def hold_kernel(picked_ref, after_0, after_1, held_ref):
+    held_ref[...] = picked_ref[...]
+
+
+def early_kernel(sides, after_0, after_1, *refs):
     piece_refs, (sums_ref, trace_ref) = refs[:-2], refs[-2:]
     pieces = [side_full(ref) for ref in piece_refs[:sides]] + [cross_full(ref) for ref in piece_refs[sides:]]
     add_cross(pieces, trace_ref, FULL, sums_ref)
@@ -387,8 +387,7 @@
     for step_round in range(2):
         lags_ref[step_round] = lags[:, step_round * samples : (step_round + 1) * samples]
     for at in range(2):
-        for which, half in enumerate(full_table(2 + at)):
-            table_ref[at, which] = half
+        table_ref[at] = full_table(2 + at)[0]
 
 
 def lag_kernel(first_ref, table_ref, *refs):
@@ -396,9 +395,7 @@
     samples = lags_ref.shape[2]
     more = 0.0
     for at, ref in enumerate(picked_refs):
-        picked = unpack(ref[...], FULL)
-        for which in range(2):
-            more += jnp.dot(picked, table_ref[at, which], preferred_element_type=jnp.float32)
+        more += jnp.dot(unpack(ref[...], FULL), table_ref[at], preferred_element_type=jnp.float32)
     for step_round in range(2):
         lags_ref[step_round] = (
             first_ref[step_round] + more[:, step_round * samples : (step_round + 1) * samples]
@@ -471,10 +468,10 @@
         out_specs=vmem,
         scratch_shapes=[
             pltpu.VMEM((padded(groups * 2 * comps) * 2 * PART, LANES), jnp.float32),
-            pltpu.VMEM((2 * SLOTS * 2 * PART, LANES), jnp.float32),
+            pltpu.VMEM((2 * SLOTS * PART, LANES), jnp.float32),
         ],
         compiler_params=params,
-        cost_estimate=cost(2),
+        cost_estimate=cost(0.001),
         name="part",
     )(*sides)
     part_2, part_3 = pl.pallas_call(
@@ -492,14 +489,14 @@
         in_specs=[smem, smem] + [vmem] * 3,
         out_specs=[vmem] * 2,
         compiler_params=params,
-        cost_estimate=cost(1),
+        cost_estimate=cost(0.001),
         name="part_near",
     )(place, counts, pairs, near_pairs, part_flat)
     part_1 = swap(part_1, 1)
     sums = pl.pallas_call(
         functools.partial(early_kernel, groups),
-        out_shape=shape(2 * SLOTS * 2 * FULL, LANES, dtype=jnp.float32),
-        in_specs=[pl.BlockSpec(memory_space=pl.ANY)] + [vmem] * (groups + len(early)),
+        out_shape=shape(2 * SLOTS * FULL, LANES, dtype=jnp.float32),
+        in_specs=[pl.BlockSpec(memory_space=pl.ANY)] * 2 + [vmem] * (groups + len(early)),
         out_specs=vmem,
         scratch_shapes=[
             pltpu.VMEM((padded((groups + len(early)) * 2 * comps) * 2 * FULL, LANES), jnp.float32)
@@ -507,17 +504,17 @@
         compiler_params=params,
         cost_estimate=cost(0.001),
         name="early",
-    )(part_flat, *sides, *early)
-    sent, part_3 = pl.pallas_call(
+    )(part_0, part_2, *sides, *early)
+    held = pl.pallas_call(
         hold_kernel,
-        out_shape=[part_packed, part_packed],
-        in_specs=[vmem] * 2 + [pl.BlockSpec(memory_space=pl.ANY)] * 3,
-        out_specs=[vmem] * 2,
+        out_shape=part_packed,
+        in_specs=[vmem] + [pl.BlockSpec(memory_space=pl.ANY)] * 2,
+        out_specs=vmem,
         compiler_params=params,
         cost_estimate=cost(0.1),
         name="hold",
-    )(part_2, part_3, part_0, sums, late[0])
-    part_2, part_3 = swap(sent, half), swap(part_3, half + 1)
+    )(part_3, sums, late[0])
+    part_2, part_3 = swap(part_2, half), swap(held, half + 1)
     full_flat, full_2, full_3 = pl.pallas_call(
         full_kernel,
         out_shape=[full_blocks, full_packed, full_packed],
@@ -525,12 +522,12 @@
         out_specs=[vmem] * 3,
         scratch_shapes=[
             pltpu.VMEM((padded(len(late) * 2 * comps) * 2 * FULL, LANES), jnp.float32),
-            pltpu.VMEM((2 * SLOTS * 2 * FULL, LANES), jnp.float32),
+            pltpu.VMEM((2 * SLOTS * FULL, LANES), jnp.float32),
         ],
         compiler_params=params,
         cost_estimate=cost(10),
         name="full",
-    )(place, counts, far[0], part_0, sent, sums, *late)
+    )(place, counts, far[0], part_0, held, sums, *late)
     full_2, full_3 = swap(full_2, half), swap(full_3, half + 1)
     full_0, *full_1 = pl.pallas_call(
         functools.partial(near_kernel, FULL, 2),
@@ -547,7 +544,7 @@
         functools.partial(first_lags_kernel, groups),
         out_shape=[
             shape(2, count, samples, dtype=jnp.float32),
-            shape(2, 2, 4 * FULL, 2 * samples),
+            shape(2, 4 * FULL, 2 * samples),
         ],
         in_specs=[smem] + [vmem] * 8,
         out_specs=[vmem] * 2,

time: 47.1 us -> 44.3 us (0.941)
  waiting for transfers between devices: 9.69 us -> 6.38 us
  starting transfers between devices: 20.3 us -> 21.8 us
  Pallas kernels: 15.7 us -> 14.7 us
    ppermute x16, waiting for transfers between devices: 9.69 us -> 6.38 us  [swap(): return lax.ppermute(x, 'cell', [(i, i ^ mask) for i in range(cells)])]
    ppermute x16, starting transfers between devices: 20.3 us -> 21.8 us  [swap(): return lax.ppermute(x, 'cell', [(i, i ^ mask) for i in range(cells)])]
    pallas_call x1, Pallas kernels: 3.31 us -> 2.81 us  [on_device(): pl.pallas_call(full_kernel, out_shape=[full_blocks, full_packed, full_pac...]
where the time goes in v12:
time: 44.3 us; the launch traced here: 44.1 us
  starting transfers between devices  21.8 us (49%)
  Pallas kernels  14.7 us (33%)
  waiting for transfers between devices  6.38 us (14%)
  local copies, waits for them, and re-layouts  1.15 us (3%)
    ppermute x16, starting transfers between devices, swap(): return lax.ppermute(x, 'cell', [(i, i ^ mask) for i in range(cells)])  21.8 us
    ppermute x16, waiting for transfers between devices, swap(): return lax.ppermute(x, 'cell', [(i, i ^ mask) for i in range(cells)])  6.38 us
    pallas_call x1, Pallas kernels, on_device(): pl.pallas_call(full_kernel, out_shape=[full_blocks, full_packed, full_pac...  2.81 us
    pallas_call x1, Pallas kernels, on_device(): pl.pallas_call(functools.partial(near_kernel, FULL, 2), out_shape=[full_p...  2 us
    pallas_call x1, Pallas kernels, on_device(): pl.pallas_call(functools.partial(first_lags_kernel, groups), out_shape=[s...  1.77 us
    pallas_call x1, Pallas kernels, on_device(): pl.pallas_call(functools.partial(near_kernel, PART, 1), out_shape=[part_p...  1.68 us
    pallas_call x1, Pallas kernels, on_device(): pl.pallas_call(functools.partial(far_kernel, PART), out_shape=[part_packe...  1.67 us
    pallas_call x1, Pallas kernels, on_device(): pl.pallas_call(lag_kernel, out_shape=shape(2, count, samples, dtype=jnp.f...  1.39 us
  transfers between devices with their start and end apart: 16, of which 5 were waited for; matrix products, arithmetic and copies ran while one was open for 0% of the time, Pallas kernels for 28%

profile of v12, /device:TPU:0, one launch (start us, length us, event | category | flops | bytes accessed | tf_op | source)
XLA Modules:
  0.0 44.1 jit_solution(10093317594777928270)
XLA Ops:
  0.0 0.5 %collective-permute-start.1 = (bf16[3,2,4,64,256]{4,3,2,1,0:T(8,128)(2,1)}, bf16[3,2,4,64,256]{4,3,2,1,0:T(8,128)(2,1)S(1)}, u32[]{:S(2)}, u32[]{:S(2)}) collective-permute-start(bf16[3,2,4,64,256]{4,3,2,1,0:T(8,128)(2,1)} %bitcast.2), channel_id=1, source_target_pairs={{0,1},{1,0},{2,3},{3,2},{4,5},{5,4},{6,7},{7,6},{8,9},{9,8},{10,11... | collective-permute-start | bytes 2359304 | tf_op jit(solution)/shard_map/ppermute | solution.py:414
  0.5 0.1 collective-permute-start
  0.5 0.0 copy-start.3
  0.5 1.1 %copy-done.3 = bf16[3,1,512,256]{3,2,1,0:T(8,128)(2,1)S(1)} copy-done((bf16[3,1,512,256]{3,2,1,0:T(8,128)(2,1)S(1)}, bf16[3,1,512,256]{3,2,1,0:T(8,128)(2,1)}, u32[]{:S(2)}) %copy-start.3) | copy-done | bytes 786456
  1.6 0.8 %own_spectra.1 = (bf16[4,96,128]{2,1,0:T(8,128)(2,1)S(1)}, bf16[8,144,128]{2,1,0:T(8,128)(2,1)S(1)}, bf16[128,256]{1,0:T(8,128)(2,1)S(1)}) custom-call(s32[1]{0:T(128)} %bitcast.place_ref, bf16[3,2,4,64,256]{4,3,2,1,0:T(8,128)(2,1)S(1)} %bitcast.3), custom_call_target="tpu_custom_call" | custom-call | flops 1000000000 | bytes 1048576 | tf_op jit(solution)/shard_map/own_spectra/pallas_call | solution.py:431
  2.5 0.1 collective-permute-done.near_pairs_ref
  2.6 0.0 collective-permute-done.1.windows_ref
  2.6 0.0 copy-done.1
  2.6 0.8 %near_spectra.1 = (bf16[480,128]{1,0:T(8,128)(2,1)S(1)}, bf16[480,128]{1,0:T(8,128)(2,1)S(1)}, bf16[480,128]{1,0:T(8,128)(2,1)S(1)}, bf16[480,128]{1,0:T(8,128)(...) custom-call(s32[1]{0:T(128)} %bitcast.place_ref, ...), custom_call_target="tpu_custom_call" | custom-call | flops 1000000000 | bytes 1048576 | tf_op jit(solution)/shard_map/near_spectra/pallas_call | solution.py:445
  3.4 3.0 %collective-permute-start.2 = (bf16[480,128]{1,0:T(8,128)(2,1)S(1)}, bf16[480,128]{1,0:T(8,128)(2,1)S(1)}, u32[]{:S(2)}, u32[]{:S(2)}) collective-permute-start(bf16[480,128]{1,0:T(8,128)(2,1)S(1)} %get-tuple-element.32), channel_id=1, source_target_pairs={{0,2},{1,3},{2,0},{3,1},{4,6},{5,7},{6,4},{7,5},{8,10},{9,11},{10,... | collective-permute-start | bytes 368648 | tf_op jit(solution)/shard_map/ppermute | solution.py:414
  6.4 1.6 %collective-permute-start.3 = (bf16[480,128]{1,0:T(8,128)(2,1)S(1)}, bf16[480,128]{1,0:T(8,128)(2,1)S(1)}, u32[]{:S(2)}, u32[]{:S(2)}) collective-permute-start(bf16[480,128]{1,0:T(8,128)(2,1)S(1)} %get-tuple-element.33), channel_id=1, source_target_pairs={{0,4},{1,5},{2,6},{3,7},{4,0},{5,1},{6,2},{7,3},{8,12},{9,13},{10,... | collective-permute-start | bytes 368648 | tf_op jit(solution)/shard_map/ppermute | solution.py:414
  8.0 0.0 collective-permute-start.4
  8.0 3.0 %collective-permute-start.5 = (bf16[320,128]{1,0:T(8,128)(2,1)S(1)}, bf16[320,128]{1,0:T(8,128)(2,1)S(1)}, u32[]{:S(2)}, u32[]{:S(2)}) collective-permute-start(bf16[320,128]{1,0:T(8,128)(2,1)S(1)} %get-tuple-element.36), channel_id=1, source_target_pairs={{0,8},{1,9},{2,10},{3,11},{4,12},{5,13},{6,14},{7,15},{8,0},{9,1},... | collective-permute-start | bytes 245768 | tf_op jit(solution)/shard_map/ppermute | solution.py:414
  11.0 1.3 %collective-permute-start.7 = (bf16[288,128]{1,0:T(8,128)(2,1)S(1)}, bf16[288,128]{1,0:T(8,128)(2,1)S(1)}, u32[]{:S(2)}, u32[]{:S(2)}) collective-permute-start(bf16[288,128]{1,0:T(8,128)(2,1)S(1)} %get-tuple-element.39), channel_id=1, source_target_pairs={{0,10},{1,11},{2,8},{3,9},{4,14},{5,15},{6,12},{7,13},{8,2},{9,3},... | collective-permute-start | bytes 221192 | tf_op jit(solution)/shard_map/ppermute | solution.py:414
  12.3 0.0 collective-permute-done.2.refs_1_
  12.3 3.6 %collective-permute-start.8 = (bf16[288,128]{1,0:T(8,128)(2,1)S(1)}, bf16[288,128]{1,0:T(8,128)(2,1)S(1)}, u32[]{:S(2)}, u32[]{:S(2)}) collective-permute-start(bf16[288,128]{1,0:T(8,128)(2,1)S(1)} %get-tuple-element.40), channel_id=1, source_target_pairs={{0,12},{1,13},{2,14},{3,15},{4,8},{5,9},{6,10},{7,11},{8,4},{9,5},... | collective-permute-start | bytes 221192 | tf_op jit(solution)/shard_map/ppermute | solution.py:414
  15.9 0.0 collective-permute-done.3.refs_2_
  15.9 1.3 %collective-permute-start.10 = (bf16[288,128]{1,0:T(8,128)(2,1)S(1)}, bf16[288,128]{1,0:T(8,128)(2,1)S(1)}, u32[]{:S(2)}, u32[]{:S(2)}) collective-permute-start(bf16[288,128]{1,0:T(8,128)(2,1)S(1)} %get-tuple-element.41), channel_id=1, source_target_pairs={{0,14},{1,15},{2,12},{3,13},{4,10},{5,11},{6,8},{7,9},{8,6},{9,7},... | collective-permute-start | bytes 221192 | tf_op jit(solution)/shard_map/ppermute | solution.py:414
  17.2 0.0 collective-permute-done.4.refs_3_
  17.2 0.9 %part.1.flat_ref = bf16[2,2,128,256]{3,2,1,0:T(8,128)(2,1)S(1)} custom-call(bf16[480,128]{1,0:T(8,128)(2,1)S(1)} %get-tuple-element.31.refs_0_, bf16[480,128]{1,0:T(8,128)(2,1)S(1)} %collective-permute-done.2.refs_1_, bf16[480,128]{1,0:T(8,128)(2,1)S(1)} %collective-permute-done.3.refs_2_, bf16[480,128]{1,0:T(8,128)(2,1)S(1)} %collective-permute-done.4.refs_3_), custom_call_target="tpu_custom_call" | custom-call | flops 1000000 | bytes 1048576 | tf_op jit(solution)/shard_map/part/pallas_call | solution.py:464
  18.1 0.0 collective-permute-done.5.listed_ref.refs_4_
  18.1 0.0 copy-done.2
  18.1 1.7 %part_far.1 = (bf16[256,128]{1,0:T(8,128)(2,1)S(1)}, bf16[256,128]{1,0:T(8,128)(2,1)S(1)}) custom-call(s32[1]{0:T(128)} %bitcast.place_ref, s32[16]{0:T(128)S(1)} %copy-done.2, bf16[320,128]{1,0:T(8,128)(2,1)S(1)} %collective-permute-done.5.listed_ref.refs_4_, bf16[2,2,128,256]{3,2,1,0:T(8,128)(2,1)S(1)} %part.1.flat_ref), custom_call_target="tpu_custom_call" | custom-call | flops 1000000000 | bytes 1048576 | tf_op jit(solution)/shard_map/part_far/pallas_call | solution.py:477
  19.8 1.5 %collective-permute-start.6 = (bf16[256,128]{1,0:T(8,128)(2,1)S(1)}, bf16[256,128]{1,0:T(8,128)(2,1)S(1)}, u32[]{:S(2)}, u32[]{:S(2)}) collective-permute-start(bf16[256,128]{1,0:T(8,128)(2,1)S(1)} %get-tuple-element.37.after_1), channel_id=1, source_target_pairs={{0,8},{1,9},{2,10},{3,11},{4,12},{5,13},{6,14},{7,15},{8,0},{9,1},... | collective-permute-start | bytes 196616 | tf_op jit(solution)/shard_map/ppermute | solution.py:414
  21.3 1.7 %part_near.1 = (bf16[256,128]{1,0:T(8,128)(2,1)S(1)}, bf16[256,128]{1,0:T(8,128)(2,1)S(1)}) custom-call(s32[1]{0:T(128)} %bitcast.place_ref, s32[16]{0:T(128)S(1)} %copy-done.2, s32[2,2,512]{2,1,0:T(2,128)S(1)} %copy-done.1, s32[2,2,512]{2,1,0:T(2,128)S(1)} %collective-permute-done.near_pairs_ref, bf16[2,2,128,256]{3,2,1,0:T(8,128)(2,1)S(1)} %part.1.flat_ref), custom_call_target="tpu_custom_call" | custom-call | flops 1000000 | bytes 1048576 | tf_op jit(solution)/shard_map/part_near/pallas_call | solution.py:486
  23.0 1.5 %collective-permute-done.7.refs_5_ = bf16[288,128]{1,0:T(8,128)(2,1)S(1)} collective-permute-done((bf16[288,128]{1,0:T(8,128)(2,1)S(1)}, bf16[288,128]{1,0:T(8,128)(2,1)S(1)}, u32[]{:S(2)}, u32[]{:S(2)}) %collective-permute-start.7) | collective-permute-done | bytes 73760 | tf_op jit(solution)/shard_map/ppermute | solution.py:414
  24.5 0.8 %early.1.after_0.before_ref = f32[1536,128]{1,0:T(8,128)S(1)} custom-call(bf16[256,128]{1,0:T(8,128)(2,1)S(1)} %get-tuple-element.35.after_0.refs_0_, bf16[256,128]{1,0:T(8,128)(2,1)S(1)} %get-tuple-element.37.after_1, bf16[480,128]{1,0:T(8,128)(2,1)S(1)} %get-tuple-element.31.refs_0_, bf16[480,128]{1,0:T(8,128)(2,1)S(1)} %collective-permute-done.2.refs_1_, ...), custom_call_target="tpu_custom_call" | custom-call | flops 1000000 | bytes 1048576 | tf_op jit(solution)/shard_map/early/pallas_call | solution.py:496
  25.3 0.0 collective-permute-done.8.after_1.refs_0_
  25.3 0.1 collective-permute-start.9
  25.4 0.0 collective-permute-done.10.refs_1_
  25.4 2.8 %full.1 = (bf16[2,2,256,256]{3,2,1,0:T(8,128)(2,1)S(1)}, bf16[384,128]{1,0:T(8,128)(2,1)S(1)}, bf16[384,128]{1,0:T(8,128)(2,1)S(1)}) custom-call(s32[1]{0:T(128)} %bitcast.place_ref, s32[16]{0:T(128)S(1)} %copy-done.2, bf16[320,128]{1,0:T(8,128)(2,1)S(1)} %collective-permute-done.5.listed_ref.refs_4_, ...), custom_call_target="tpu_custom_call" | custom-call | flops 10000000000 | bytes 1048576 | tf_op jit(solution)/shard_map/full/pallas_call | solution.py:518
  28.2 4.5 %collective-permute-start.14 = (bf16[384,128]{1,0:T(8,128)(2,1)S(1)}, bf16[384,128]{1,0:T(8,128)(2,1)S(1)}, u32[]{:S(2)}, u32[]{:S(2)}) collective-permute-start(bf16[384,128]{1,0:T(8,128)(2,1)S(1)} %get-tuple-element.49), channel_id=1, source_target_pairs={{0,8},{1,9},{2,10},{3,11},{4,12},{5,13},{6,14},{7,15},{8,0},{9,1},... | collective-permute-start | bytes 294920 | tf_op jit(solution)/shard_map/ppermute | solution.py:414
  32.8 0.7 %collective-permute-start.15 = (bf16[384,128]{1,0:T(8,128)(2,1)S(1)}, bf16[384,128]{1,0:T(8,128)(2,1)S(1)}, u32[]{:S(2)}, u32[]{:S(2)}) collective-permute-start(bf16[384,128]{1,0:T(8,128)(2,1)S(1)} %get-tuple-element.50), channel_id=1, source_target_pairs={{0,9},{1,8},{2,11},{3,10},{4,13},{5,12},{6,15},{7,14},{8,1},{9,0},... | collective-permute-start | bytes 294920 | tf_op jit(solution)/shard_map/ppermute | solution.py:414
  33.5 0.0 collective-permute-start.11
  33.5 0.0 collective-permute-done.6.refs_0_.refs_1_
  33.5 0.0 collective-permute-done.9.refs_1_.refs_2_
  33.5 0.0 copy-start
  33.5 2.0 %full_near.1 = (bf16[384,128]{1,0:T(8,128)(2,1)S(1)}, bf16[192,128]{1,0:T(8,128)(2,1)S(1)}, bf16[192,128]{1,0:T(8,128)(2,1)S(1)}) custom-call(s32[1]{0:T(128)} %bitcast.place_ref, s32[16]{0:T(128)S(1)} %copy-done.2, s32[2,2,512]{2,1,0:T(2,128)S(1)} %copy-done.1, s32[2,2,512]{2,1,0:T(2,128)S(1)} %collective-permute-done.near_pairs_ref, ...), custom_call_target="tpu_custom_call" | custom-call | flops 500000000 | bytes 1048576 | tf_op jit(solution)/shard_map/full_near/pallas_call | solution.py:532
  35.5 0.6 %collective-permute-start.12 = (bf16[192,128]{1,0:T(8,128)(2,1)S(1)}, bf16[192,128]{1,0:T(8,128)(2,1)S(1)}, u32[]{:S(2)}, u32[]{:S(2)}) collective-permute-start(bf16[192,128]{1,0:T(8,128)(2,1)S(1)} %get-tuple-element.45), channel_id=1, source_target_pairs={{0,1},{1,0},{2,3},{3,2},{4,5},{5,4},{6,7},{7,6},{8,9},{9,8},{10,11... | collective-permute-start | bytes 147464 | tf_op jit(solution)/shard_map/ppermute | solution.py:414
  36.1 0.1 collective-permute-start.13
  36.2 0.0 collective-permute-done.11.refs_4_
  36.2 0.8 %collective-permute-done.12.refs_5_ = bf16[192,128]{1,0:T(8,128)(2,1)S(1)} collective-permute-done((bf16[192,128]{1,0:T(8,128)(2,1)S(1)}, bf16[192,128]{1,0:T(8,128)(2,1)S(1)}, u32[]{:S(2)}, u32[]{:S(2)}) %collective-permute-start.12) | collective-permute-done | bytes 49184 | tf_op jit(solution)/shard_map/ppermute | solution.py:414
  37.0 0.3 collective-permute-done.13.refs_6_
  37.3 0.0 copy-done
  37.3 1.8 %first_lags.1 = (f32[2,512,256]{2,1,0:T(8,128)S(1)}, bf16[2,96,512]{2,1,0:T(8,128)(2,1)S(1)}) custom-call(s32[1]{0:T(128)} %bitcast.place_ref, f32[256,256]{1,0:T(8,128)S(1)} %copy-done, bf16[256,128]{1,0:T(8,128)(2,1)S(1)} %get-tuple-element.35.after_0.refs_0_, bf16[256,128]{1,0:T(8,128)(2,1)S(1)} %collective-permute-done.6.refs_0_.refs_1_, ...), custom_call_target="tpu_custom_call" | custom-call | flops 1000000 | bytes 1048576 | tf_op jit(solution)/shard_map/first_lags/pallas_call | solution.py:543
  39.1 0.0 collective-permute-done.14.refs_0_
  39.1 3.6 %collective-permute-done.15.refs_1_ = bf16[384,128]{1,0:T(8,128)(2,1)S(1)} collective-permute-done((bf16[384,128]{1,0:T(8,128)(2,1)S(1)}, bf16[384,128]{1,0:T(8,128)(2,1)S(1)}, u32[]{:S(2)}, u32[]{:S(2)}) %collective-permute-start.15) | collective-permute-done | bytes 98336 | tf_op jit(solution)/shard_map/ppermute | solution.py:414
  42.7 1.4 %lags.1 = f32[2,512,256]{2,1,0:T(8,128)} custom-call(f32[2,512,256]{2,1,0:T(8,128)S(1)} %get-tuple-element.47.first_ref, bf16[2,96,512]{2,1,0:T(8,128)(2,1)S(1)} %get-tuple-element.48.table_ref, bf16[384,128]{1,0:T(8,128)(2,1)S(1)} %collective-permute-done.14.refs_0_, bf16[384,128]{1,0:T(8,128)(2,1)S(1)} %collective-permute-done.15.refs_1_), custom_call_target="tpu_custom_call" | custom-call | flops 1000000000 | bytes 1048576 | tf_op jit(solution)/shard_map/lags/pallas_call | solution.py:555
  (3 shorter events, 0.0 us)
Async XLA Ops:
  0.0 2.6 %collective-permute-start.1 = (bf16[3,2,4,64,256]{4,3,2,1,0:T(8,128)(2,1)}, bf16[3,2,4,64,256]{4,3,2,1,0:T(8,128)(2,1)S(1)}, u32[]{:S(2)}, u32[]{:S(2)}) collective-permute-start(bf16[3,2,4,64,256]{4,3,2,1,0:T(8,128)(2,1)} %bitcast.2), channel_id=1, source_target_pairs={{0,1},{1,0},{2,3},{3,2},{4,5},{5,4},{6,7},{7,6},{8,9},{9,8},{10,11... | collective-permute-start | bytes 2359304 | tf_op jit(solution)/shard_map/ppermute | solution.py:414
  0.5 2.1 %collective-permute-start = (s32[2,2,512]{2,1,0:T(2,128)}, s32[2,2,512]{2,1,0:T(2,128)S(1)}, u32[]{:S(2)}, u32[]{:S(2)}) collective-permute-start(s32[2,2,512]{2,1,0:T(2,128)} %own_pairs_ref.5), channel_id=1, source_target_pairs={{0,1},{1,0},{2,3},{3,2},{4,5},{5,4},{6,7},{7,6},{8,9},{9,8},{10,11... | collective-permute-start | bytes 24584 | tf_op jit(solution)/shard_map/ppermute | solution.py:414
  0.5 1.1 %copy-start.3 = (bf16[3,1,512,256]{3,2,1,0:T(8,128)(2,1)S(1)}, bf16[3,1,512,256]{3,2,1,0:T(8,128)(2,1)}, u32[]{:S(2)}) copy-start(bf16[3,1,512,256]{3,2,1,0:T(8,128)(2,1)} %param.4) | copy-start | bytes 2359300
  1.6 0.9 %copy-start.1 = (s32[2,2,512]{2,1,0:T(2,128)S(1)}, s32[2,2,512]{2,1,0:T(2,128)}, u32[]{:S(2)}) copy-start(s32[2,2,512]{2,1,0:T(2,128)} %own_pairs_ref.5) | copy-start | bytes 24580
  3.4 8.8 %collective-permute-start.2 = (bf16[480,128]{1,0:T(8,128)(2,1)S(1)}, bf16[480,128]{1,0:T(8,128)(2,1)S(1)}, u32[]{:S(2)}, u32[]{:S(2)}) collective-permute-start(bf16[480,128]{1,0:T(8,128)(2,1)S(1)} %get-tuple-element.32), channel_id=1, source_target_pairs={{0,2},{1,3},{2,0},{3,1},{4,6},{5,7},{6,4},{7,5},{8,10},{9,11},{10,... | collective-permute-start | bytes 368648 | tf_op jit(solution)/shard_map/ppermute | solution.py:414
  6.4 9.5 %collective-permute-start.3 = (bf16[480,128]{1,0:T(8,128)(2,1)S(1)}, bf16[480,128]{1,0:T(8,128)(2,1)S(1)}, u32[]{:S(2)}, u32[]{:S(2)}) collective-permute-start(bf16[480,128]{1,0:T(8,128)(2,1)S(1)} %get-tuple-element.33), channel_id=1, source_target_pairs={{0,4},{1,5},{2,6},{3,7},{4,0},{5,1},{6,2},{7,3},{8,12},{9,13},{10,... | collective-permute-start | bytes 368648 | tf_op jit(solution)/shard_map/ppermute | solution.py:414
  8.0 9.2 %collective-permute-start.4 = (bf16[480,128]{1,0:T(8,128)(2,1)S(1)}, bf16[480,128]{1,0:T(8,128)(2,1)S(1)}, u32[]{:S(2)}, u32[]{:S(2)}) collective-permute-start(bf16[480,128]{1,0:T(8,128)(2,1)S(1)} %get-tuple-element.34), channel_id=1, source_target_pairs={{0,6},{1,7},{2,4},{3,5},{4,2},{5,3},{6,0},{7,1},{8,14},{9,15},{10,... | collective-permute-start | bytes 368648 | tf_op jit(solution)/shard_map/ppermute | solution.py:414
  8.0 10.1 %collective-permute-start.5 = (bf16[320,128]{1,0:T(8,128)(2,1)S(1)}, bf16[320,128]{1,0:T(8,128)(2,1)S(1)}, u32[]{:S(2)}, u32[]{:S(2)}) collective-permute-start(bf16[320,128]{1,0:T(8,128)(2,1)S(1)} %get-tuple-element.36), channel_id=1, source_target_pairs={{0,8},{1,9},{2,10},{3,11},{4,12},{5,13},{6,14},{7,15},{8,0},{9,1},... | collective-permute-start | bytes 245768 | tf_op jit(solution)/shard_map/ppermute | solution.py:414
  11.0 13.5 %collective-permute-start.7 = (bf16[288,128]{1,0:T(8,128)(2,1)S(1)}, bf16[288,128]{1,0:T(8,128)(2,1)S(1)}, u32[]{:S(2)}, u32[]{:S(2)}) collective-permute-start(bf16[288,128]{1,0:T(8,128)(2,1)S(1)} %get-tuple-element.39), channel_id=1, source_target_pairs={{0,10},{1,11},{2,8},{3,9},{4,14},{5,15},{6,12},{7,13},{8,2},{9,3},... | collective-permute-start | bytes 221192 | tf_op jit(solution)/shard_map/ppermute | solution.py:414
  12.3 13.0 %collective-permute-start.8 = (bf16[288,128]{1,0:T(8,128)(2,1)S(1)}, bf16[288,128]{1,0:T(8,128)(2,1)S(1)}, u32[]{:S(2)}, u32[]{:S(2)}) collective-permute-start(bf16[288,128]{1,0:T(8,128)(2,1)S(1)} %get-tuple-element.40), channel_id=1, source_target_pairs={{0,12},{1,13},{2,14},{3,15},{4,8},{5,9},{6,10},{7,11},{8,4},{9,5},... | collective-permute-start | bytes 221192 | tf_op jit(solution)/shard_map/ppermute | solution.py:414
  15.9 9.5 %collective-permute-start.10 = (bf16[288,128]{1,0:T(8,128)(2,1)S(1)}, bf16[288,128]{1,0:T(8,128)(2,1)S(1)}, u32[]{:S(2)}, u32[]{:S(2)}) collective-permute-start(bf16[288,128]{1,0:T(8,128)(2,1)S(1)} %get-tuple-element.41), channel_id=1, source_target_pairs={{0,14},{1,15},{2,12},{3,13},{4,10},{5,11},{6,8},{7,9},{8,6},{9,7},... | collective-permute-start | bytes 221192 | tf_op jit(solution)/shard_map/ppermute | solution.py:414
  17.2 0.9 %copy-start.2 = (s32[16]{0:T(128)S(1)}, s32[16]{0:T(128)}, u32[]{:S(2)}) copy-start(s32[16]{0:T(128)} %counts_ref.7) | copy-start | bytes 196
  19.8 13.7 %collective-permute-start.6 = (bf16[256,128]{1,0:T(8,128)(2,1)S(1)}, bf16[256,128]{1,0:T(8,128)(2,1)S(1)}, u32[]{:S(2)}, u32[]{:S(2)}) collective-permute-start(bf16[256,128]{1,0:T(8,128)(2,1)S(1)} %get-tuple-element.37.after_1), channel_id=1, source_target_pairs={{0,8},{1,9},{2,10},{3,11},{4,12},{5,13},{6,14},{7,15},{8,0},{9,1},... | collective-permute-start | bytes 196616 | tf_op jit(solution)/shard_map/ppermute | solution.py:414
  25.3 8.2 %collective-permute-start.9 = (bf16[256,128]{1,0:T(8,128)(2,1)S(1)}, bf16[256,128]{1,0:T(8,128)(2,1)S(1)}, u32[]{:S(2)}, u32[]{:S(2)}) collective-permute-start(bf16[256,128]{1,0:T(8,128)(2,1)S(1)} %hold.1.after_2), channel_id=1, source_target_pairs={{0,9},{1,8},{2,11},{3,10},{4,13},{5,12},{6,15},{7,14},{8,1},{9,0},... | collective-permute-start | bytes 196616 | tf_op jit(solution)/shard_map/ppermute | solution.py:414
  28.2 10.9 %collective-permute-start.14 = (bf16[384,128]{1,0:T(8,128)(2,1)S(1)}, bf16[384,128]{1,0:T(8,128)(2,1)S(1)}, u32[]{:S(2)}, u32[]{:S(2)}) collective-permute-start(bf16[384,128]{1,0:T(8,128)(2,1)S(1)} %get-tuple-element.49), channel_id=1, source_target_pairs={{0,8},{1,9},{2,10},{3,11},{4,12},{5,13},{6,14},{7,15},{8,0},{9,1},... | collective-permute-start | bytes 294920 | tf_op jit(solution)/shard_map/ppermute | solution.py:414
  32.8 10.0 %collective-permute-start.15 = (bf16[384,128]{1,0:T(8,128)(2,1)S(1)}, bf16[384,128]{1,0:T(8,128)(2,1)S(1)}, u32[]{:S(2)}, u32[]{:S(2)}) collective-permute-start(bf16[384,128]{1,0:T(8,128)(2,1)S(1)} %get-tuple-element.50), channel_id=1, source_target_pairs={{0,9},{1,8},{2,11},{3,10},{4,13},{5,12},{6,15},{7,14},{8,1},{9,0},... | collective-permute-start | bytes 294920 | tf_op jit(solution)/shard_map/ppermute | solution.py:414
  33.5 2.7 %collective-permute-start.11 = (bf16[256,128]{1,0:T(8,128)(2,1)S(1)}, bf16[256,128]{1,0:T(8,128)(2,1)S(1)}, u32[]{:S(2)}, u32[]{:S(2)}) collective-permute-start(bf16[256,128]{1,0:T(8,128)(2,1)S(1)} %get-tuple-element.44), channel_id=1, source_target_pairs={{0,1},{1,0},{2,3},{3,2},{4,5},{5,4},{6,7},{7,6},{8,9},{9,8},{10,11... | collective-permute-start | bytes 196616 | tf_op jit(solution)/shard_map/ppermute | solution.py:414
  33.5 3.8 %copy-start = (f32[256,256]{1,0:T(8,128)S(1)}, f32[256,256]{1,0:T(8,128)}, u32[]{:S(2)}) copy-start(f32[256,256]{1,0:T(8,128)} %constant.6.clone.inverse_ref) | copy-start | bytes 786436
  35.5 1.4 %collective-permute-start.12 = (bf16[192,128]{1,0:T(8,128)(2,1)S(1)}, bf16[192,128]{1,0:T(8,128)(2,1)S(1)}, u32[]{:S(2)}, u32[]{:S(2)}) collective-permute-start(bf16[192,128]{1,0:T(8,128)(2,1)S(1)} %get-tuple-element.45), channel_id=1, source_target_pairs={{0,1},{1,0},{2,3},{3,2},{4,5},{5,4},{6,7},{7,6},{8,9},{9,8},{10,11... | collective-permute-start | bytes 147464 | tf_op jit(solution)/shard_map/ppermute | solution.py:414
  36.1 1.2 %collective-permute-start.13 = (bf16[192,128]{1,0:T(8,128)(2,1)S(1)}, bf16[192,128]{1,0:T(8,128)(2,1)S(1)}, u32[]{:S(2)}, u32[]{:S(2)}) collective-permute-start(bf16[192,128]{1,0:T(8,128)(2,1)S(1)} %get-tuple-element.46), channel_id=1, source_target_pairs={{0,1},{1,0},{2,3},{3,2},{4,5},{5,4},{6,7},{7,6},{8,9},{9,8},{10,11... | collective-permute-start | bytes 147464 | tf_op jit(solution)/shard_map/ppermute | solution.py:414

commit v13 on v12

--- a/solution.py
+++ b/solution.py
@@ -308,15 +308,11 @@
     turn_blocks(cross_ref, PART, flat_ref)
 
 
-def far_kernel(bins, place_ref, counts_ref, listed_ref, flat_ref, picked_0, picked_1):
+def far_kernel(bins, place_ref, counts_ref, listed_ref, flat_ref, after_ref, picked_0, picked_1):
     listed = listed_ref[cross_full(listed_ref)[2] :].astype(jnp.float32)
     listing = listed.shape[0] // 2
     pick(place_ref, counts_ref, listed[:listing], flat_ref, bins, 2, picked_0)
     pick(place_ref, counts_ref, listed[listing:], flat_ref, bins, 3, picked_1)
-
-
-def hold_kernel(picked_ref, after_0, after_1, held_ref):
-    held_ref[...] = picked_ref[...]
 
 
 def early_kernel(sides, after_0, after_1, *refs):
@@ -474,15 +470,6 @@
         cost_estimate=cost(0.001),
         name="part",
     )(*sides)
-    part_2, part_3 = pl.pallas_call(
-        functools.partial(far_kernel, PART),
-        out_shape=[part_packed, part_packed],
-        in_specs=[smem, smem, vmem, vmem],
-        out_specs=[vmem, vmem],
-        compiler_params=params,
-        cost_estimate=cost(1),
-        name="part_far",
-    )(place, counts, far[0], part_flat)
     part_0, part_1 = pl.pallas_call(
         functools.partial(near_kernel, PART, 1),
         out_shape=[part_packed, part_packed],
@@ -492,6 +479,15 @@
         cost_estimate=cost(0.001),
         name="part_near",
     )(place, counts, pairs, near_pairs, part_flat)
+    part_2, part_3 = pl.pallas_call(
+        functools.partial(far_kernel, PART),
+        out_shape=[part_packed, part_packed],
+        in_specs=[smem, smem, vmem, vmem, pl.BlockSpec(memory_space=pl.ANY)],
+        out_specs=[vmem, vmem],
+        compiler_params=params,
+        cost_estimate=cost(1),
+        name="part_far",
+    )(place, counts, far[0], part_flat, part_0)
     part_1 = swap(part_1, 1)
     sums = pl.pallas_call(
         functools.partial(early_kernel, groups),
@@ -505,16 +501,7 @@
         cost_estimate=cost(0.001),
         name="early",
     )(part_0, part_2, *sides, *early)
-    held = pl.pallas_call(
-        hold_kernel,
-        out_shape=part_packed,
-        in_specs=[vmem] + [pl.BlockSpec(memory_space=pl.ANY)] * 2,
-        out_specs=vmem,
-        compiler_params=params,
-        cost_estimate=cost(0.1),
-        name="hold",
-    )(part_3, sums, late[0])
-    part_2, part_3 = swap(part_2, half), swap(held, half + 1)
+    sent, part_2, part_3 = part_2, swap(part_2, half), swap(part_3, half + 1)
     full_flat, full_2, full_3 = pl.pallas_call(
         full_kernel,
         out_shape=[full_blocks, full_packed, full_packed],
@@ -527,7 +514,7 @@
         compiler_params=params,
         cost_estimate=cost(10),
         name="full",
-    )(place, counts, far[0], part_0, held, sums, *late)
+    )(place, counts, far[0], part_0, sent, sums, *late)
     full_2, full_3 = swap(full_2, half), swap(full_3, half + 1)
     full_0, *full_1 = pl.pallas_call(
         functools.partial(near_kernel, FULL, 2),

time: 44.3 us -> 41.9 us (0.946)
  waiting for transfers between devices: 6.38 us -> 3.75 us
    ppermute x16, waiting for transfers between devices: 6.38 us -> 3.75 us  [swap(): return lax.ppermute(x, 'cell', [(i, i ^ mask) for i in range(cells)])]
  transfers between devices with their start and end apart: 16 -> 16, of which waited for: 5 -> 6; matrix products, arithmetic and copies ran while one was open for 0% -> 0% of each run, Pallas kernels for 28% -> 30%
where the time goes in v13:
time: 41.9 us; the launch traced here: 41.5 us
  starting transfers between devices  21.7 us (52%)
  Pallas kernels  14.7 us (35%)
  waiting for transfers between devices  3.75 us (9%)
  local copies, waits for them, and re-layouts  1.14 us (3%)
    ppermute x16, starting transfers between devices, swap(): return lax.ppermute(x, 'cell', [(i, i ^ mask) for i in range(cells)])  21.7 us
    ppermute x16, waiting for transfers between devices, swap(): return lax.ppermute(x, 'cell', [(i, i ^ mask) for i in range(cells)])  3.75 us
    pallas_call x1, Pallas kernels, on_device(): pl.pallas_call(full_kernel, out_shape=[full_blocks, full_packed, full_pac...  2.81 us
    pallas_call x1, Pallas kernels, on_device(): pl.pallas_call(functools.partial(near_kernel, FULL, 2), out_shape=[full_p...  2 us
    pallas_call x1, Pallas kernels, on_device(): pl.pallas_call(functools.partial(first_lags_kernel, groups), out_shape=[s...  1.77 us
    pallas_call x1, Pallas kernels, on_device(): pl.pallas_call(functools.partial(near_kernel, PART, 1), out_shape=[part_p...  1.68 us
    pallas_call x1, Pallas kernels, on_device(): pl.pallas_call(functools.partial(far_kernel, PART), out_shape=[part_packe...  1.68 us
    pallas_call x1, Pallas kernels, on_device(): pl.pallas_call(lag_kernel, out_shape=shape(2, count, samples, dtype=jnp.f...  1.39 us
  transfers between devices with their start and end apart: 16, of which 6 were waited for; matrix products, arithmetic and copies ran while one was open for 0% of the time, Pallas kernels for 30%

profile of v13, /device:TPU:0, one launch (start us, length us, event | category | flops | bytes accessed | tf_op | source)
XLA Modules:
  0.0 41.5 jit_solution(1620603674082346264)
XLA Ops:
  0.0 0.5 %collective-permute-start.1 = (bf16[3,2,4,64,256]{4,3,2,1,0:T(8,128)(2,1)}, bf16[3,2,4,64,256]{4,3,2,1,0:T(8,128)(2,1)S(1)}, u32[]{:S(2)}, u32[]{:S(2)}) collective-permute-start(bf16[3,2,4,64,256]{4,3,2,1,0:T(8,128)(2,1)} %bitcast.2), channel_id=1, source_target_pairs={{0,1},{1,0},{2,3},{3,2},{4,5},{5,4},{6,7},{7,6},{8,9},{9,8},{10,11... | collective-permute-start | bytes 2359304 | tf_op jit(solution)/shard_map/ppermute | solution.py:410
  0.5 0.1 collective-permute-start
  0.5 0.0 copy-start.3
  0.5 1.1 %copy-done.3 = bf16[3,1,512,256]{3,2,1,0:T(8,128)(2,1)S(1)} copy-done((bf16[3,1,512,256]{3,2,1,0:T(8,128)(2,1)S(1)}, bf16[3,1,512,256]{3,2,1,0:T(8,128)(2,1)}, u32[]{:S(2)}) %copy-start.3) | copy-done | bytes 786456
  1.6 0.0 copy-start.1
  1.6 0.8 %own_spectra.1 = (bf16[4,96,128]{2,1,0:T(8,128)(2,1)S(1)}, bf16[8,144,128]{2,1,0:T(8,128)(2,1)S(1)}, bf16[128,256]{1,0:T(8,128)(2,1)S(1)}) custom-call(s32[1]{0:T(128)} %bitcast.place_ref, bf16[3,2,4,64,256]{4,3,2,1,0:T(8,128)(2,1)S(1)} %bitcast.3), custom_call_target="tpu_custom_call" | custom-call | flops 1000000000 | bytes 1048576 | tf_op jit(solution)/shard_map/own_spectra/pallas_call | solution.py:427
  2.5 0.1 collective-permute-done.near_pairs_ref
  2.6 0.0 collective-permute-done.1.windows_ref
  2.6 0.0 copy-done.1
  2.6 0.8 %near_spectra.1 = (bf16[480,128]{1,0:T(8,128)(2,1)S(1)}, bf16[480,128]{1,0:T(8,128)(2,1)S(1)}, bf16[480,128]{1,0:T(8,128)(2,1)S(1)}, bf16[480,128]{1,0:T(8,128)(...) custom-call(s32[1]{0:T(128)} %bitcast.place_ref, ...), custom_call_target="tpu_custom_call" | custom-call | flops 1000000000 | bytes 1048576 | tf_op jit(solution)/shard_map/near_spectra/pallas_call | solution.py:441
  3.4 3.0 %collective-permute-start.2 = (bf16[480,128]{1,0:T(8,128)(2,1)S(1)}, bf16[480,128]{1,0:T(8,128)(2,1)S(1)}, u32[]{:S(2)}, u32[]{:S(2)}) collective-permute-start(bf16[480,128]{1,0:T(8,128)(2,1)S(1)} %get-tuple-element.32), channel_id=1, source_target_pairs={{0,2},{1,3},{2,0},{3,1},{4,6},{5,7},{6,4},{7,5},{8,10},{9,11},{10,... | collective-permute-start | bytes 368648 | tf_op jit(solution)/shard_map/ppermute | solution.py:410
  6.4 1.6 %collective-permute-start.3 = (bf16[480,128]{1,0:T(8,128)(2,1)S(1)}, bf16[480,128]{1,0:T(8,128)(2,1)S(1)}, u32[]{:S(2)}, u32[]{:S(2)}) collective-permute-start(bf16[480,128]{1,0:T(8,128)(2,1)S(1)} %get-tuple-element.33), channel_id=1, source_target_pairs={{0,4},{1,5},{2,6},{3,7},{4,0},{5,1},{6,2},{7,3},{8,12},{9,13},{10,... | collective-permute-start | bytes 368648 | tf_op jit(solution)/shard_map/ppermute | solution.py:410
  8.0 0.0 collective-permute-start.4
  8.0 3.0 %collective-permute-start.5 = (bf16[320,128]{1,0:T(8,128)(2,1)S(1)}, bf16[320,128]{1,0:T(8,128)(2,1)S(1)}, u32[]{:S(2)}, u32[]{:S(2)}) collective-permute-start(bf16[320,128]{1,0:T(8,128)(2,1)S(1)} %get-tuple-element.36), channel_id=1, source_target_pairs={{0,8},{1,9},{2,10},{3,11},{4,12},{5,13},{6,14},{7,15},{8,0},{9,1},... | collective-permute-start | bytes 245768 | tf_op jit(solution)/shard_map/ppermute | solution.py:410
  11.0 1.3 %collective-permute-start.8 = (bf16[288,128]{1,0:T(8,128)(2,1)S(1)}, bf16[288,128]{1,0:T(8,128)(2,1)S(1)}, u32[]{:S(2)}, u32[]{:S(2)}) collective-permute-start(bf16[288,128]{1,0:T(8,128)(2,1)S(1)} %get-tuple-element.39), channel_id=1, source_target_pairs={{0,10},{1,11},{2,8},{3,9},{4,14},{5,15},{6,12},{7,13},{8,2},{9,3},... | collective-permute-start | bytes 221192 | tf_op jit(solution)/shard_map/ppermute | solution.py:410
  12.3 0.0 collective-permute-done.2.refs_1_
  12.3 3.6 %collective-permute-start.9 = (bf16[288,128]{1,0:T(8,128)(2,1)S(1)}, bf16[288,128]{1,0:T(8,128)(2,1)S(1)}, u32[]{:S(2)}, u32[]{:S(2)}) collective-permute-start(bf16[288,128]{1,0:T(8,128)(2,1)S(1)} %get-tuple-element.40), channel_id=1, source_target_pairs={{0,12},{1,13},{2,14},{3,15},{4,8},{5,9},{6,10},{7,11},{8,4},{9,5},... | collective-permute-start | bytes 221192 | tf_op jit(solution)/shard_map/ppermute | solution.py:410
  15.9 0.0 collective-permute-done.3.refs_2_
  15.9 1.3 %collective-permute-start.10 = (bf16[288,128]{1,0:T(8,128)(2,1)S(1)}, bf16[288,128]{1,0:T(8,128)(2,1)S(1)}, u32[]{:S(2)}, u32[]{:S(2)}) collective-permute-start(bf16[288,128]{1,0:T(8,128)(2,1)S(1)} %get-tuple-element.41), channel_id=1, source_target_pairs={{0,14},{1,15},{2,12},{3,13},{4,10},{5,11},{6,8},{7,9},{8,6},{9,7},... | collective-permute-start | bytes 221192 | tf_op jit(solution)/shard_map/ppermute | solution.py:410
  17.2 0.0 collective-permute-done.4.refs_3_
  17.2 0.9 %part.1.flat_ref = bf16[2,2,128,256]{3,2,1,0:T(8,128)(2,1)S(1)} custom-call(bf16[480,128]{1,0:T(8,128)(2,1)S(1)} %get-tuple-element.31.refs_0_, bf16[480,128]{1,0:T(8,128)(2,1)S(1)} %collective-permute-done.2.refs_1_, bf16[480,128]{1,0:T(8,128)(2,1)S(1)} %collective-permute-done.3.refs_2_, bf16[480,128]{1,0:T(8,128)(2,1)S(1)} %collective-permute-done.4.refs_3_), custom_call_target="tpu_custom_call" | custom-call | flops 1000000 | bytes 1048576 | tf_op jit(solution)/shard_map/part/pallas_call | solution.py:460
  18.1 0.0 copy-done.2
  18.1 1.7 %part_near.1 = (bf16[256,128]{1,0:T(8,128)(2,1)S(1)}, bf16[256,128]{1,0:T(8,128)(2,1)S(1)}) custom-call(s32[1]{0:T(128)} %bitcast.place_ref, s32[16]{0:T(128)S(1)} %copy-done.2, s32[2,2,512]{2,1,0:T(2,128)S(1)} %copy-done.1, s32[2,2,512]{2,1,0:T(2,128)S(1)} %collective-permute-done.near_pairs_ref, bf16[2,2,128,256]{3,2,1,0:T(8,128)(2,1)S(1)} %part.1.flat_ref), custom_call_target="tpu_custom_call" | custom-call | flops 1000000 | bytes 1048576 | tf_op jit(solution)/shard_map/part_near/pallas_call | solution.py:473
  19.8 0.0 collective-permute-done.5.listed_ref.refs_4_
  19.8 1.7 %part_far.1 = (bf16[256,128]{1,0:T(8,128)(2,1)S(1)}, bf16[256,128]{1,0:T(8,128)(2,1)S(1)}) custom-call(s32[1]{0:T(128)} %bitcast.place_ref, s32[16]{0:T(128)S(1)} %copy-done.2, bf16[320,128]{1,0:T(8,128)(2,1)S(1)} %collective-permute-done.5.listed_ref.refs_4_, bf16[2,2,128,256]{3,2,1,0:T(8,128)(2,1)S(1)} %part.1.flat_ref, ...), custom_call_target="tpu_custom_call" | custom-call | flops 1000000000 | bytes 1048576 | tf_op jit(solution)/shard_map/part_far/pallas_call | solution.py:482
  21.5 0.1 collective-permute-start.7
  21.6 1.0 %collective-permute-start.6 = (bf16[256,128]{1,0:T(8,128)(2,1)S(1)}, bf16[256,128]{1,0:T(8,128)(2,1)S(1)}, u32[]{:S(2)}, u32[]{:S(2)}) collective-permute-start(bf16[256,128]{1,0:T(8,128)(2,1)S(1)} %get-tuple-element.37.after_1.after_2), channel_id=1, source_target_pairs={{0,8},{1,9},{2,10},{3,11},{4,12},{5,13},{6,14},{7,15},{8,0},{9,1},... | collective-permute-start | bytes 196616 | tf_op jit(solution)/shard_map/ppermute | solution.py:410
  22.6 1.2 %collective-permute-done.8.refs_5_ = bf16[288,128]{1,0:T(8,128)(2,1)S(1)} collective-permute-done((bf16[288,128]{1,0:T(8,128)(2,1)S(1)}, bf16[288,128]{1,0:T(8,128)(2,1)S(1)}, u32[]{:S(2)}, u32[]{:S(2)}) %collective-permute-start.8) | collective-permute-done | bytes 73760 | tf_op jit(solution)/shard_map/ppermute | solution.py:410
  23.8 0.8 %early.1.before_ref = f32[1536,128]{1,0:T(8,128)S(1)} custom-call(bf16[256,128]{1,0:T(8,128)(2,1)S(1)} %get-tuple-element.35.after_ref.after_0.refs_0_, bf16[256,128]{1,0:T(8,128)(2,1)S(1)} %get-tuple-element.37.after_1.after_2, bf16[480,128]{1,0:T(8,128)(2,1)S(1)} %get-tuple-element.31.refs_0_, bf16[480,128]{1,0:T(8,128)(2,1)S(1)} %collective-permute-done.2.refs_1_, ...), custom_call_target="tpu_custom_call" | custom-call | flops 1000000 | bytes 1048576 | tf_op jit(solution)/shard_map/early/pallas_call | solution.py:492
  24.6 0.0 collective-permute-done.9.refs_0_
  24.6 0.0 collective-permute-done.10.refs_1_
  24.6 2.8 %full.1 = (bf16[2,2,256,256]{3,2,1,0:T(8,128)(2,1)S(1)}, bf16[384,128]{1,0:T(8,128)(2,1)S(1)}, bf16[384,128]{1,0:T(8,128)(2,1)S(1)}) custom-call(s32[1]{0:T(128)} %bitcast.place_ref, s32[16]{0:T(128)S(1)} %copy-done.2, bf16[320,128]{1,0:T(8,128)(2,1)S(1)} %collective-permute-done.5.listed_ref.refs_4_, ...), custom_call_target="tpu_custom_call" | custom-call | flops 10000000000 | bytes 1048576 | tf_op jit(solution)/shard_map/full/pallas_call | solution.py:505
  27.4 5.6 %collective-permute-start.14 = (bf16[384,128]{1,0:T(8,128)(2,1)S(1)}, bf16[384,128]{1,0:T(8,128)(2,1)S(1)}, u32[]{:S(2)}, u32[]{:S(2)}) collective-permute-start(bf16[384,128]{1,0:T(8,128)(2,1)S(1)} %get-tuple-element.49), channel_id=1, source_target_pairs={{0,8},{1,9},{2,10},{3,11},{4,12},{5,13},{6,14},{7,15},{8,0},{9,1},... | collective-permute-start | bytes 294920 | tf_op jit(solution)/shard_map/ppermute | solution.py:410
  33.1 0.0 collective-permute-start.15
  33.1 0.2 collective-permute-start.11
  33.2 0.0 collective-permute-done.7.refs_1_.refs_2_
  33.2 0.0 collective-permute-done.6.refs_0_.refs_1_
  33.3 2.0 %full_near.1 = (bf16[384,128]{1,0:T(8,128)(2,1)S(1)}, bf16[192,128]{1,0:T(8,128)(2,1)S(1)}, bf16[192,128]{1,0:T(8,128)(2,1)S(1)}) custom-call(s32[1]{0:T(128)} %bitcast.place_ref, s32[16]{0:T(128)S(1)} %copy-done.2, s32[2,2,512]{2,1,0:T(2,128)S(1)} %copy-done.1, s32[2,2,512]{2,1,0:T(2,128)S(1)} %collective-permute-done.near_pairs_ref, ...), custom_call_target="tpu_custom_call" | custom-call | flops 500000000 | bytes 1048576 | tf_op jit(solution)/shard_map/full_near/pallas_call | solution.py:519
  35.3 0.4 collective-permute-start.12
  35.6 0.2 collective-permute-start.13
  35.8 0.0 collective-permute-done.11.refs_4_
  35.8 0.7 %collective-permute-done.12.refs_5_ = bf16[192,128]{1,0:T(8,128)(2,1)S(1)} collective-permute-done((bf16[192,128]{1,0:T(8,128)(2,1)S(1)}, bf16[192,128]{1,0:T(8,128)(2,1)S(1)}, u32[]{:S(2)}, u32[]{:S(2)}) %collective-permute-start.12) | collective-permute-done | bytes 49184 | tf_op jit(solution)/shard_map/ppermute | solution.py:410
  36.6 0.3 collective-permute-done.13.refs_6_
  36.9 0.0 copy-done
  36.9 1.8 %first_lags.1 = (f32[2,512,256]{2,1,0:T(8,128)S(1)}, bf16[2,96,512]{2,1,0:T(8,128)(2,1)S(1)}) custom-call(s32[1]{0:T(128)} %bitcast.place_ref, f32[256,256]{1,0:T(8,128)S(1)} %copy-done, bf16[256,128]{1,0:T(8,128)(2,1)S(1)} %get-tuple-element.35.after_ref.after_0.refs_0_, bf16[256,128]{1,0:T(8,128)(2,1)S(1)} %collective-permute-done.6.refs_0_.refs_1_, ...), custom_call_target="tpu_custom_call" | custom-call | flops 1000000 | bytes 1048576 | tf_op jit(solution)/shard_map/first_lags/pallas_call | solution.py:530
  38.7 1.2 %collective-permute-done.14.refs_0_ = bf16[384,128]{1,0:T(8,128)(2,1)S(1)} collective-permute-done((bf16[384,128]{1,0:T(8,128)(2,1)S(1)}, bf16[384,128]{1,0:T(8,128)(2,1)S(1)}, u32[]{:S(2)}, u32[]{:S(2)}) %collective-permute-start.14) | collective-permute-done | bytes 98336 | tf_op jit(solution)/shard_map/ppermute | solution.py:410
  39.9 0.2 collective-permute-done.15.refs_1_
  40.1 1.4 %lags.1 = f32[2,512,256]{2,1,0:T(8,128)} custom-call(f32[2,512,256]{2,1,0:T(8,128)S(1)} %get-tuple-element.47.first_ref, bf16[2,96,512]{2,1,0:T(8,128)(2,1)S(1)} %get-tuple-element.48.table_ref, bf16[384,128]{1,0:T(8,128)(2,1)S(1)} %collective-permute-done.14.refs_0_, bf16[384,128]{1,0:T(8,128)(2,1)S(1)} %collective-permute-done.15.refs_1_), custom_call_target="tpu_custom_call" | custom-call | flops 1000000000 | bytes 1048576 | tf_op jit(solution)/shard_map/lags/pallas_call | solution.py:542
  (2 shorter events, 0.0 us)
Async XLA Ops:
  0.0 2.6 %collective-permute-start.1 = (bf16[3,2,4,64,256]{4,3,2,1,0:T(8,128)(2,1)}, bf16[3,2,4,64,256]{4,3,2,1,0:T(8,128)(2,1)S(1)}, u32[]{:S(2)}, u32[]{:S(2)}) collective-permute-start(bf16[3,2,4,64,256]{4,3,2,1,0:T(8,128)(2,1)} %bitcast.2), channel_id=1, source_target_pairs={{0,1},{1,0},{2,3},{3,2},{4,5},{5,4},{6,7},{7,6},{8,9},{9,8},{10,11... | collective-permute-start | bytes 2359304 | tf_op jit(solution)/shard_map/ppermute | solution.py:410
  0.5 2.1 %collective-permute-start = (s32[2,2,512]{2,1,0:T(2,128)}, s32[2,2,512]{2,1,0:T(2,128)S(1)}, u32[]{:S(2)}, u32[]{:S(2)}) collective-permute-start(s32[2,2,512]{2,1,0:T(2,128)} %own_pairs_ref.5), channel_id=1, source_target_pairs={{0,1},{1,0},{2,3},{3,2},{4,5},{5,4},{6,7},{7,6},{8,9},{9,8},{10,11... | collective-permute-start | bytes 24584 | tf_op jit(solution)/shard_map/ppermute | solution.py:410
  0.5 1.1 %copy-start.3 = (bf16[3,1,512,256]{3,2,1,0:T(8,128)(2,1)S(1)}, bf16[3,1,512,256]{3,2,1,0:T(8,128)(2,1)}, u32[]{:S(2)}) copy-start(bf16[3,1,512,256]{3,2,1,0:T(8,128)(2,1)} %param.4) | copy-start | bytes 2359300
  1.6 0.9 %copy-start.1 = (s32[2,2,512]{2,1,0:T(2,128)S(1)}, s32[2,2,512]{2,1,0:T(2,128)}, u32[]{:S(2)}) copy-start(s32[2,2,512]{2,1,0:T(2,128)} %own_pairs_ref.5) | copy-start | bytes 24580
  3.4 8.8 %collective-permute-start.2 = (bf16[480,128]{1,0:T(8,128)(2,1)S(1)}, bf16[480,128]{1,0:T(8,128)(2,1)S(1)}, u32[]{:S(2)}, u32[]{:S(2)}) collective-permute-start(bf16[480,128]{1,0:T(8,128)(2,1)S(1)} %get-tuple-element.32), channel_id=1, source_target_pairs={{0,2},{1,3},{2,0},{3,1},{4,6},{5,7},{6,4},{7,5},{8,10},{9,11},{10,... | collective-permute-start | bytes 368648 | tf_op jit(solution)/shard_map/ppermute | solution.py:410
  6.4 9.5 %collective-permute-start.3 = (bf16[480,128]{1,0:T(8,128)(2,1)S(1)}, bf16[480,128]{1,0:T(8,128)(2,1)S(1)}, u32[]{:S(2)}, u32[]{:S(2)}) collective-permute-start(bf16[480,128]{1,0:T(8,128)(2,1)S(1)} %get-tuple-element.33), channel_id=1, source_target_pairs={{0,4},{1,5},{2,6},{3,7},{4,0},{5,1},{6,2},{7,3},{8,12},{9,13},{10,... | collective-permute-start | bytes 368648 | tf_op jit(solution)/shard_map/ppermute | solution.py:410
  8.0 9.2 %collective-permute-start.4 = (bf16[480,128]{1,0:T(8,128)(2,1)S(1)}, bf16[480,128]{1,0:T(8,128)(2,1)S(1)}, u32[]{:S(2)}, u32[]{:S(2)}) collective-permute-start(bf16[480,128]{1,0:T(8,128)(2,1)S(1)} %get-tuple-element.34), channel_id=1, source_target_pairs={{0,6},{1,7},{2,4},{3,5},{4,2},{5,3},{6,0},{7,1},{8,14},{9,15},{10,... | collective-permute-start | bytes 368648 | tf_op jit(solution)/shard_map/ppermute | solution.py:410
  8.0 11.8 %collective-permute-start.5 = (bf16[320,128]{1,0:T(8,128)(2,1)S(1)}, bf16[320,128]{1,0:T(8,128)(2,1)S(1)}, u32[]{:S(2)}, u32[]{:S(2)}) collective-permute-start(bf16[320,128]{1,0:T(8,128)(2,1)S(1)} %get-tuple-element.36), channel_id=1, source_target_pairs={{0,8},{1,9},{2,10},{3,11},{4,12},{5,13},{6,14},{7,15},{8,0},{9,1},... | collective-permute-start | bytes 245768 | tf_op jit(solution)/shard_map/ppermute | solution.py:410
  11.0 12.8 %collective-permute-start.8 = (bf16[288,128]{1,0:T(8,128)(2,1)S(1)}, bf16[288,128]{1,0:T(8,128)(2,1)S(1)}, u32[]{:S(2)}, u32[]{:S(2)}) collective-permute-start(bf16[288,128]{1,0:T(8,128)(2,1)S(1)} %get-tuple-element.39), channel_id=1, source_target_pairs={{0,10},{1,11},{2,8},{3,9},{4,14},{5,15},{6,12},{7,13},{8,2},{9,3},... | collective-permute-start | bytes 221192 | tf_op jit(solution)/shard_map/ppermute | solution.py:410
  12.3 12.3 %collective-permute-start.9 = (bf16[288,128]{1,0:T(8,128)(2,1)S(1)}, bf16[288,128]{1,0:T(8,128)(2,1)S(1)}, u32[]{:S(2)}, u32[]{:S(2)}) collective-permute-start(bf16[288,128]{1,0:T(8,128)(2,1)S(1)} %get-tuple-element.40), channel_id=1, source_target_pairs={{0,12},{1,13},{2,14},{3,15},{4,8},{5,9},{6,10},{7,11},{8,4},{9,5},... | collective-permute-start | bytes 221192 | tf_op jit(solution)/shard_map/ppermute | solution.py:410
  15.9 8.7 %collective-permute-start.10 = (bf16[288,128]{1,0:T(8,128)(2,1)S(1)}, bf16[288,128]{1,0:T(8,128)(2,1)S(1)}, u32[]{:S(2)}, u32[]{:S(2)}) collective-permute-start(bf16[288,128]{1,0:T(8,128)(2,1)S(1)} %get-tuple-element.41), channel_id=1, source_target_pairs={{0,14},{1,15},{2,12},{3,13},{4,10},{5,11},{6,8},{7,9},{8,6},{9,7},... | collective-permute-start | bytes 221192 | tf_op jit(solution)/shard_map/ppermute | solution.py:410
  17.2 0.9 %copy-start.2 = (s32[16]{0:T(128)S(1)}, s32[16]{0:T(128)}, u32[]{:S(2)}) copy-start(s32[16]{0:T(128)} %counts_ref.7) | copy-start | bytes 196
  21.5 11.8 %collective-permute-start.7 = (bf16[256,128]{1,0:T(8,128)(2,1)S(1)}, bf16[256,128]{1,0:T(8,128)(2,1)S(1)}, u32[]{:S(2)}, u32[]{:S(2)}) collective-permute-start(bf16[256,128]{1,0:T(8,128)(2,1)S(1)} %get-tuple-element.38), channel_id=1, source_target_pairs={{0,9},{1,8},{2,11},{3,10},{4,13},{5,12},{6,15},{7,14},{8,1},{9,0},... | collective-permute-start | bytes 196616 | tf_op jit(solution)/shard_map/ppermute | solution.py:410
  21.6 11.7 %collective-permute-start.6 = (bf16[256,128]{1,0:T(8,128)(2,1)S(1)}, bf16[256,128]{1,0:T(8,128)(2,1)S(1)}, u32[]{:S(2)}, u32[]{:S(2)}) collective-permute-start(bf16[256,128]{1,0:T(8,128)(2,1)S(1)} %get-tuple-element.37.after_1.after_2), channel_id=1, source_target_pairs={{0,8},{1,9},{2,10},{3,11},{4,12},{5,13},{6,14},{7,15},{8,0},{9,1},... | collective-permute-start | bytes 196616 | tf_op jit(solution)/shard_map/ppermute | solution.py:410
  27.4 12.4 %collective-permute-start.14 = (bf16[384,128]{1,0:T(8,128)(2,1)S(1)}, bf16[384,128]{1,0:T(8,128)(2,1)S(1)}, u32[]{:S(2)}, u32[]{:S(2)}) collective-permute-start(bf16[384,128]{1,0:T(8,128)(2,1)S(1)} %get-tuple-element.49), channel_id=1, source_target_pairs={{0,8},{1,9},{2,10},{3,11},{4,12},{5,13},{6,14},{7,15},{8,0},{9,1},... | collective-permute-start | bytes 294920 | tf_op jit(solution)/shard_map/ppermute | solution.py:410
  33.1 7.0 %collective-permute-start.15 = (bf16[384,128]{1,0:T(8,128)(2,1)S(1)}, bf16[384,128]{1,0:T(8,128)(2,1)S(1)}, u32[]{:S(2)}, u32[]{:S(2)}) collective-permute-start(bf16[384,128]{1,0:T(8,128)(2,1)S(1)} %get-tuple-element.50), channel_id=1, source_target_pairs={{0,9},{1,8},{2,11},{3,10},{4,13},{5,12},{6,15},{7,14},{8,1},{9,0},... | collective-permute-start | bytes 294920 | tf_op jit(solution)/shard_map/ppermute | solution.py:410
  33.1 2.8 %collective-permute-start.11 = (bf16[256,128]{1,0:T(8,128)(2,1)S(1)}, bf16[256,128]{1,0:T(8,128)(2,1)S(1)}, u32[]{:S(2)}, u32[]{:S(2)}) collective-permute-start(bf16[256,128]{1,0:T(8,128)(2,1)S(1)} %get-tuple-element.44), channel_id=1, source_target_pairs={{0,1},{1,0},{2,3},{3,2},{4,5},{5,4},{6,7},{7,6},{8,9},{9,8},{10,11... | collective-permute-start | bytes 196616 | tf_op jit(solution)/shard_map/ppermute | solution.py:410
  33.3 3.6 %copy-start = (f32[256,256]{1,0:T(8,128)S(1)}, f32[256,256]{1,0:T(8,128)}, u32[]{:S(2)}) copy-start(f32[256,256]{1,0:T(8,128)} %constant.6.clone.inverse_ref) | copy-start | bytes 786436
  35.3 1.3 %collective-permute-start.12 = (bf16[192,128]{1,0:T(8,128)(2,1)S(1)}, bf16[192,128]{1,0:T(8,128)(2,1)S(1)}, u32[]{:S(2)}, u32[]{:S(2)}) collective-permute-start(bf16[192,128]{1,0:T(8,128)(2,1)S(1)} %get-tuple-element.45), channel_id=1, source_target_pairs={{0,1},{1,0},{2,3},{3,2},{4,5},{5,4},{6,7},{7,6},{8,9},{9,8},{10,11... | collective-permute-start | bytes 147464 | tf_op jit(solution)/shard_map/ppermute | solution.py:410
  35.6 1.2 %collective-permute-start.13 = (bf16[192,128]{1,0:T(8,128)(2,1)S(1)}, bf16[192,128]{1,0:T(8,128)(2,1)S(1)}, u32[]{:S(2)}, u32[]{:S(2)}) collective-permute-start(bf16[192,128]{1,0:T(8,128)(2,1)S(1)} %get-tuple-element.46), channel_id=1, source_target_pairs={{0,1},{1,0},{2,3},{3,2},{4,5},{5,4},{6,7},{7,6},{8,9},{9,8},{10,11... | collective-permute-start | bytes 147464 | tf_op jit(solution)/shard_map/ppermute | solution.py:410

commit v14 on v13

--- a/solution.py
+++ b/solution.py
@@ -112,29 +112,29 @@
 
 
 def near_spectra_kernel(
-    place_ref, own_pairs_ref, near_pairs_ref, table_ref, part_ref, full_ref, windows_ref, *piece_refs
+    place_ref, own_pairs_ref, near_pairs_ref, table_ref, part_ref, full_ref, windows_ref, *refs
 ):
     groups = windows_ref.shape[2]
+    side_refs, full_refs = refs[:groups], refs[groups:]
     _, group = place_of(place_ref, groups)
     table = table_ref[...]
     part_rows, full_rows = COMPS * 2 * PART, COMPS * 2 * FULL
-    piece_refs[groups][2 * full_rows :] = jnp.concatenate(
+    full_refs[groups][2 * full_rows :] = jnp.concatenate(
         [listing_of(own_pairs_ref, LANES), listing_of(near_pairs_ref, LANES)]
     ).astype(jnp.bfloat16)
     for mg in range(groups):
         spectra = station_spectra(windows_ref, group ^ mg, table)
-        side, cross = piece_refs[mg], piece_refs[groups + mg]
-        side[:part_rows] = part_ref[mg]
-        side[2 * part_rows : 2 * part_rows + full_rows] = full_ref[mg]
-        cross[:full_rows] = full_ref[groups + mg]
+        side_refs[mg][:part_rows] = part_ref[mg]
+        for far in range(2):
+            full_refs[far * groups + mg][:full_rows] = full_ref[far * groups + mg]
         for comp in range(COMPS):
             lanes = spectra[:, comp * LANES : (comp + 1) * LANES]
             at = part_rows + comp * 2 * PART
-            side[at : at + 2 * PART] = lanes[: 2 * PART]
-            at = 2 * part_rows + full_rows + comp * 2 * FULL
-            side[at : at + 2 * FULL] = lanes[2 * PART : 2 * PART + 2 * FULL]
-            at = full_rows + comp * 2 * FULL
-            cross[at : at + 2 * FULL] = lanes[2 * PART + 2 * FULL :]
+            side_refs[mg][at : at + 2 * PART] = lanes[: 2 * PART]
+            for far in range(2):
+                at = full_rows + comp * 2 * FULL
+                start = 2 * PART + 2 * FULL * far
+                full_refs[far * groups + mg][at : at + 2 * FULL] = lanes[start : start + 2 * FULL]
 
 
 def width(bins):
@@ -290,42 +290,33 @@
                     ] = block[start : start + SLOTS]
 
 
-def side_part(ref):
-    return (ref, 0, 2 * COMPS * 2 * PART)
-
-
-def side_full(ref):
-    return (ref, 2 * COMPS * 2 * PART, 2 * COMPS * 2 * FULL)
-
-
-def cross_full(ref):
+def full_part(ref):
     return (ref, 0, 2 * COMPS * 2 * FULL)
 
 
 def part_kernel(*refs):
     piece_refs, (flat_ref, trace_ref, cross_ref) = refs[:-3], refs[-3:]
-    add_cross([side_part(ref) for ref in piece_refs], trace_ref, PART, cross_ref)
+    add_cross([(ref, 0, ref.shape[0]) for ref in piece_refs], trace_ref, PART, cross_ref)
     turn_blocks(cross_ref, PART, flat_ref)
 
 
 def far_kernel(bins, place_ref, counts_ref, listed_ref, flat_ref, after_ref, picked_0, picked_1):
-    listed = listed_ref[cross_full(listed_ref)[2] :].astype(jnp.float32)
+    listed = listed_ref[full_part(listed_ref)[2] :].astype(jnp.float32)
     listing = listed.shape[0] // 2
     pick(place_ref, counts_ref, listed[:listing], flat_ref, bins, 2, picked_0)
     pick(place_ref, counts_ref, listed[listing:], flat_ref, bins, 3, picked_1)
 
 
-def early_kernel(sides, after_0, after_1, *refs):
+def early_kernel(after_0, after_1, *refs):
     piece_refs, (sums_ref, trace_ref) = refs[:-2], refs[-2:]
-    pieces = [side_full(ref) for ref in piece_refs[:sides]] + [cross_full(ref) for ref in piece_refs[sides:]]
-    add_cross(pieces, trace_ref, FULL, sums_ref)
+    add_cross([full_part(ref) for ref in piece_refs], trace_ref, FULL, sums_ref)
 
 
 def full_kernel(place_ref, counts_ref, listed_ref, after_0, after_2, before_ref, *refs):
     piece_refs, (flat_ref, picked_0, picked_1, trace_ref, cross_ref) = refs[:-5], refs[-5:]
-    add_cross([cross_full(ref) for ref in piece_refs], trace_ref, FULL, cross_ref, before_ref)
+    add_cross([full_part(ref) for ref in piece_refs], trace_ref, FULL, cross_ref, before_ref)
     turn_blocks(cross_ref, FULL, flat_ref)
-    listed = listed_ref[cross_full(listed_ref)[2] :].astype(jnp.float32)
+    listed = listed_ref[full_part(listed_ref)[2] :].astype(jnp.float32)
     listing = listed.shape[0] // 2
     pick(place_ref, counts_ref, listed[:listing], flat_ref, FULL, 2, picked_0)
     pick(place_ref, counts_ref, listed[listing:], flat_ref, FULL, 3, picked_1)
@@ -440,18 +431,20 @@
     listing = 2 * pairs.size // LANES
     pieces = pl.pallas_call(
         near_spectra_kernel,
-        out_shape=[shape(2 * (part_rows + full_rows), LANES)] * groups
-        + [shape(2 * full_rows + listing * (mg == 0), LANES) for mg in range(groups)],
+        out_shape=[shape(2 * part_rows, LANES)] * groups
+        + [shape(2 * full_rows + listing * (m == groups), LANES) for m in range(2 * groups)],
         in_specs=[smem] + [vmem] * 6,
-        out_specs=[vmem] * (2 * groups),
+        out_specs=[vmem] * (3 * groups),
         compiler_params=params,
         cost_estimate=cost(1),
         name="near_spectra",
     )(place, pairs, near_pairs, table, part_spectra, full_spectra, near_windows)
-    arrived = [pieces[0]] + [swap(pieces[m], 2 * m) for m in range(1, 2 * groups)]
-    sides, far = arrived[:groups], arrived[groups:]
-
-    early, late = far[: groups - 2], far[groups - 2 :]
+    parts, fulls = pieces[:groups], pieces[groups:]
+    parts = [parts[0]] + [swap(parts[m], 2 * m) for m in range(1, groups)]
+    fulls = [fulls[0]] + [swap(fulls[m], 2 * m) for m in range(1, 2 * groups)]
+    sides, far = fulls[:groups], fulls[groups:]
+
+    early, late = [sides[0], *far[: groups - 2]], [*far[groups - 2 :], *sides[1:]]
     part_packed = shape(packed_rows(count, PART), LANES)
     full_packed = shape(packed_rows(count, FULL), LANES)
     half_packed = shape(packed_rows(count, FULL) // 2, LANES)
@@ -469,7 +462,7 @@
         compiler_params=params,
         cost_estimate=cost(0.001),
         name="part",
-    )(*sides)
+    )(*parts)
     part_0, part_1 = pl.pallas_call(
         functools.partial(near_kernel, PART, 1),
         out_shape=[part_packed, part_packed],
@@ -490,17 +483,17 @@
     )(place, counts, far[0], part_flat, part_0)
     part_1 = swap(part_1, 1)
     sums = pl.pallas_call(
-        functools.partial(early_kernel, groups),
+        early_kernel,
         out_shape=shape(2 * SLOTS * FULL, LANES, dtype=jnp.float32),
-        in_specs=[pl.BlockSpec(memory_space=pl.ANY)] * 2 + [vmem] * (groups + len(early)),
+        in_specs=[pl.BlockSpec(memory_space=pl.ANY)] * 2 + [vmem] * len(early),
         out_specs=vmem,
         scratch_shapes=[
-            pltpu.VMEM((padded((groups + len(early)) * 2 * comps) * 2 * FULL, LANES), jnp.float32)
+            pltpu.VMEM((padded(len(early) * 2 * comps) * 2 * FULL, LANES), jnp.float32)
         ],
         compiler_params=params,
         cost_estimate=cost(0.001),
         name="early",
-    )(part_0, part_2, *sides, *early)
+    )(part_0, part_2, *early)
     sent, part_2, part_3 = part_2, swap(part_2, half), swap(part_3, half + 1)
     full_flat, full_2, full_3 = pl.pallas_call(
         full_kernel,

time: 41.9 us -> 48 us (1.15)
  starting transfers between devices: 21.7 us -> 27.2 us
  waiting for transfers between devices: 3.75 us -> 4.8 us
    ppermute x16 -> x19, starting transfers between devices: 21.7 us -> 27.2 us  [swap(): return lax.ppermute(x, 'cell', [(i, i ^ mask) for i in range(cells)])]
    ppermute x16 -> x19, waiting for transfers between devices: 3.75 us -> 4.8 us  [swap(): return lax.ppermute(x, 'cell', [(i, i ^ mask) for i in range(cells)])]
  transfers between devices with their start and end apart: 16 -> 19, of which waited for: 6 -> 5; matrix products, arithmetic and copies ran while one was open for 0% -> 0% of each run, Pallas kernels for 30% -> 26%
where the time goes in v14:
time: 48 us; the launch traced here: 47.9 us
  starting transfers between devices  27.2 us (57%)
  Pallas kernels  14.6 us (30%)
  waiting for transfers between devices  4.8 us (10%)
  local copies, waits for them, and re-layouts  1.15 us (2%)
    ppermute x19, starting transfers between devices, swap(): return lax.ppermute(x, 'cell', [(i, i ^ mask) for i in range(cells)])  27.2 us
    ppermute x19, waiting for transfers between devices, swap(): return lax.ppermute(x, 'cell', [(i, i ^ mask) for i in range(cells)])  4.8 us
    pallas_call x1, Pallas kernels, on_device(): pl.pallas_call(full_kernel, out_shape=[full_blocks, full_packed, full_pac...  2.95 us
    pallas_call x1, Pallas kernels, on_device(): pl.pallas_call(functools.partial(near_kernel, FULL, 2), out_shape=[full_p...  1.99 us
    pallas_call x1, Pallas kernels, on_device(): pl.pallas_call(functools.partial(first_lags_kernel, groups), out_shape=[s...  1.77 us
    pallas_call x1, Pallas kernels, on_device(): pl.pallas_call(functools.partial(near_kernel, PART, 1), out_shape=[part_p...  1.68 us
    pallas_call x1, Pallas kernels, on_device(): pl.pallas_call(functools.partial(far_kernel, PART), out_shape=[part_packe...  1.68 us
    pallas_call x1, Pallas kernels, on_device(): pl.pallas_call(lag_kernel, out_shape=shape(2, count, samples, dtype=jnp.f...  1.39 us
  transfers between devices with their start and end apart: 19, of which 5 were waited for; matrix products, arithmetic and copies ran while one was open for 0% of the time, Pallas kernels for 26%

profile of v14, /device:TPU:0, one launch (start us, length us, event | category | flops | bytes accessed | tf_op | source)
XLA Modules:
  0.0 47.9 jit_solution(14496283213197038101)
XLA Ops:
  0.0 0.5 collective-permute-start.1
  0.5 0.1 collective-permute-start
  0.5 1.1 %copy-done.3 = bf16[3,1,512,256]{3,2,1,0:T(8,128)(2,1)S(1)} copy-done((bf16[3,1,512,256]{3,2,1,0:T(8,128)(2,1)S(1)}, bf16[3,1,512,256]{3,2,1,0:T(8,128)(2,1)}, u32[]{:S(2)}) %copy-start.3) | copy-done | bytes 786456
  1.6 0.8 %own_spectra.1 = (bf16[4,96,128]{2,1,0:T(8,128)(2,1)S(1)}, bf16[8,144,128]{2,1,0:T(8,128)(2,1)S(1)}, bf16[128,256]{1,0:T(8,128)(2,1)S(1)}) custom-call(s32[1]{0:T(128)} %bitcast.place_ref, bf16[3,2,4,64,256]{4,3,2,1,0:T(8,128)(2,1)S(1)} %bitcast.3), custom_call_target="tpu_custom_call" | custom-call | flops 1000000000 | bytes 1048576 | tf_op jit(solution)/shard_map/own_spectra/pallas_call | solution.py:418
  2.5 0.1 collective-permute-done.near_pairs_ref
  2.6 0.0 collective-permute-done.1.windows_ref
  2.6 0.8 %near_spectra.1 = (bf16[192,128]{1,0:T(8,128)(2,1)S(1)}, bf16[192,128]{1,0:T(8,128)(2,1)S(1)}, bf16[192,128]{1,0:T(8,128)(2,1)S(1)}, bf16[192,128]{1,0:T(8,128)(...) custom-call(s32[1]{0:T(128)} %bitcast.place_ref, ...), custom_call_target="tpu_custom_call" | custom-call | flops 1000000000 | bytes 1048576 | tf_op jit(solution)/shard_map/near_spectra/pallas_call | solution.py:432
  3.4 4.1 %collective-permute-start.5 = (bf16[320,128]{1,0:T(8,128)(2,1)S(1)}, bf16[320,128]{1,0:T(8,128)(2,1)S(1)}, u32[]{:S(2)}, u32[]{:S(2)}) collective-permute-start(bf16[320,128]{1,0:T(8,128)(2,1)S(1)} %get-tuple-element.40), channel_id=1, source_target_pairs={{0,8},{1,9},{2,10},{3,11},{4,12},{5,13},{6,14},{7,15},{8,0},{9,1},... | collective-permute-start | bytes 245768 | tf_op jit(solution)/shard_map/ppermute | solution.py:401
  7.5 1.3 %collective-permute-start.8 = (bf16[288,128]{1,0:T(8,128)(2,1)S(1)}, bf16[288,128]{1,0:T(8,128)(2,1)S(1)}, u32[]{:S(2)}, u32[]{:S(2)}) collective-permute-start(bf16[288,128]{1,0:T(8,128)(2,1)S(1)} %get-tuple-element.44), channel_id=1, source_target_pairs={{0,10},{1,11},{2,8},{3,9},{4,14},{5,15},{6,12},{7,13},{8,2},{9,3},... | collective-permute-start | bytes 221192 | tf_op jit(solution)/shard_map/ppermute | solution.py:401
  8.8 0.2 collective-permute-start.2
  9.0 1.8 %collective-permute-start.3 = (bf16[192,128]{1,0:T(8,128)(2,1)S(1)}, bf16[192,128]{1,0:T(8,128)(2,1)S(1)}, u32[]{:S(2)}, u32[]{:S(2)}) collective-permute-start(bf16[192,128]{1,0:T(8,128)(2,1)S(1)} %get-tuple-element.37), channel_id=1, source_target_pairs={{0,4},{1,5},{2,6},{3,7},{4,0},{5,1},{6,2},{7,3},{8,12},{9,13},{10,... | collective-permute-start | bytes 147464 | tf_op jit(solution)/shard_map/ppermute | solution.py:401
  10.8 1.4 %collective-permute-start.4 = (bf16[192,128]{1,0:T(8,128)(2,1)S(1)}, bf16[192,128]{1,0:T(8,128)(2,1)S(1)}, u32[]{:S(2)}, u32[]{:S(2)}) collective-permute-start(bf16[192,128]{1,0:T(8,128)(2,1)S(1)} %get-tuple-element.38), channel_id=1, source_target_pairs={{0,6},{1,7},{2,4},{3,5},{4,2},{5,3},{6,0},{7,1},{8,14},{9,15},{10,... | collective-permute-start | bytes 147464 | tf_op jit(solution)/shard_map/ppermute | solution.py:401
  12.3 0.8 %collective-permute-done.2.refs_1_ = bf16[192,128]{1,0:T(8,128)(2,1)S(1)} collective-permute-done((bf16[192,128]{1,0:T(8,128)(2,1)S(1)}, bf16[192,128]{1,0:T(8,128)(2,1)S(1)}, u32[]{:S(2)}, u32[]{:S(2)}) %collective-permute-start.2) | collective-permute-done | bytes 49184 | tf_op jit(solution)/shard_map/ppermute | solution.py:401
  13.1 3.4 %collective-permute-start.9 = (bf16[288,128]{1,0:T(8,128)(2,1)S(1)}, bf16[288,128]{1,0:T(8,128)(2,1)S(1)}, u32[]{:S(2)}, u32[]{:S(2)}) collective-permute-start(bf16[288,128]{1,0:T(8,128)(2,1)S(1)} %get-tuple-element.45), channel_id=1, source_target_pairs={{0,12},{1,13},{2,14},{3,15},{4,8},{5,9},{6,10},{7,11},{8,4},{9,5},... | collective-permute-start | bytes 221192 | tf_op jit(solution)/shard_map/ppermute | solution.py:401
  16.5 0.0 collective-permute-done.3.refs_2_
  16.5 4.8 %collective-permute-start.10 = (bf16[288,128]{1,0:T(8,128)(2,1)S(1)}, bf16[288,128]{1,0:T(8,128)(2,1)S(1)}, u32[]{:S(2)}, u32[]{:S(2)}) collective-permute-start(bf16[288,128]{1,0:T(8,128)(2,1)S(1)} %get-tuple-element.46), channel_id=1, source_target_pairs={{0,14},{1,15},{2,12},{3,13},{4,10},{5,11},{6,8},{7,9},{8,6},{9,7},... | collective-permute-start | bytes 221192 | tf_op jit(solution)/shard_map/ppermute | solution.py:401
  21.3 0.0 collective-permute-done.4.refs_3_
  21.3 0.0 collective-permute-start.11
  21.3 0.9 %part.1.flat_ref = bf16[2,2,128,256]{3,2,1,0:T(8,128)(2,1)S(1)} custom-call(bf16[192,128]{1,0:T(8,128)(2,1)S(1)} %get-tuple-element.35.refs_0_, bf16[192,128]{1,0:T(8,128)(2,1)S(1)} %collective-permute-done.2.refs_1_, bf16[192,128]{1,0:T(8,128)(2,1)S(1)} %collective-permute-done.3.refs_2_, bf16[192,128]{1,0:T(8,128)(2,1)S(1)} %collective-permute-done.4.refs_3_), custom_call_target="tpu_custom_call" | custom-call | flops 1000000 | bytes 1048576 | tf_op jit(solution)/shard_map/part/pallas_call | solution.py:453
  22.2 1.7 %part_near.1 = (bf16[256,128]{1,0:T(8,128)(2,1)S(1)}, bf16[256,128]{1,0:T(8,128)(2,1)S(1)}) custom-call(s32[1]{0:T(128)} %bitcast.place_ref, s32[16]{0:T(128)S(1)} %copy-done.2, s32[2,2,512]{2,1,0:T(2,128)S(1)} %copy-done.1, s32[2,2,512]{2,1,0:T(2,128)S(1)} %collective-permute-done.near_pairs_ref, bf16[2,2,128,256]{3,2,1,0:T(8,128)(2,1)S(1)} %part.1.flat_ref), custom_call_target="tpu_custom_call" | custom-call | flops 1000000 | bytes 1048576 | tf_op jit(solution)/shard_map/part_near/pallas_call | solution.py:466
  23.9 0.0 collective-permute-done.8.refs_2_
  23.9 0.1 collective-permute-start.12
  24.0 0.0 collective-permute-done.5.listed_ref.refs_1_
  24.0 3.5 %collective-permute-start.13 = (bf16[288,128]{1,0:T(8,128)(2,1)S(1)}, bf16[288,128]{1,0:T(8,128)(2,1)S(1)}, u32[]{:S(2)}, u32[]{:S(2)}) collective-permute-start(bf16[288,128]{1,0:T(8,128)(2,1)S(1)} %get-tuple-element.49), channel_id=1, source_target_pairs={{0,6},{1,7},{2,4},{3,5},{4,2},{5,3},{6,0},{7,1},{8,14},{9,15},{10,... | collective-permute-start | bytes 221192 | tf_op jit(solution)/shard_map/ppermute | solution.py:401
  27.5 1.7 %part_far.1 = (bf16[256,128]{1,0:T(8,128)(2,1)S(1)}, bf16[256,128]{1,0:T(8,128)(2,1)S(1)}) custom-call(s32[1]{0:T(128)} %bitcast.place_ref, s32[16]{0:T(128)S(1)} %copy-done.2, bf16[320,128]{1,0:T(8,128)(2,1)S(1)} %collective-permute-done.5.listed_ref.refs_1_, bf16[2,2,128,256]{3,2,1,0:T(8,128)(2,1)S(1)} %part.1.flat_ref, ...), custom_call_target="tpu_custom_call" | custom-call | flops 1000000000 | bytes 1048576 | tf_op jit(solution)/shard_map/part_far/pallas_call | solution.py:475
  29.2 0.6 %early.1.before_ref = f32[1536,128]{1,0:T(8,128)S(1)} custom-call(bf16[256,128]{1,0:T(8,128)(2,1)S(1)} %get-tuple-element.39.after_ref.after_0.refs_0_, bf16[256,128]{1,0:T(8,128)(2,1)S(1)} %get-tuple-element.41.after_1.after_2, bf16[288,128]{1,0:T(8,128)(2,1)S(1)} %get-tuple-element.43.refs_0_, ...), custom_call_target="tpu_custom_call" | custom-call | flops 1000000 | bytes 1048576 | tf_op jit(solution)/shard_map/early/pallas_call | solution.py:485
  29.8 0.0 collective-permute-done.9.refs_0_
  29.8 0.8 %collective-permute-start.6 = (bf16[256,128]{1,0:T(8,128)(2,1)S(1)}, bf16[256,128]{1,0:T(8,128)(2,1)S(1)}, u32[]{:S(2)}, u32[]{:S(2)}) collective-permute-start(bf16[256,128]{1,0:T(8,128)(2,1)S(1)} %get-tuple-element.41.after_1.after_2), channel_id=1, source_target_pairs={{0,8},{1,9},{2,10},{3,11},{4,12},{5,13},{6,14},{7,15},{8,0},{9,1},... | collective-permute-start | bytes 196616 | tf_op jit(solution)/shard_map/ppermute | solution.py:401
  30.6 0.0 collective-permute-done.10.refs_1_
  30.6 0.0 collective-permute-start.7
  30.6 0.0 collective-permute-done.11.refs_2_
  30.6 0.0 collective-permute-done.12.refs_3_
  30.6 0.0 collective-permute-done.13.refs_4_
  30.6 3.0 %full.1 = (bf16[2,2,256,256]{3,2,1,0:T(8,128)(2,1)S(1)}, bf16[384,128]{1,0:T(8,128)(2,1)S(1)}, bf16[384,128]{1,0:T(8,128)(2,1)S(1)}) custom-call(s32[1]{0:T(128)} %bitcast.place_ref, s32[16]{0:T(128)S(1)} %copy-done.2, bf16[320,128]{1,0:T(8,128)(2,1)S(1)} %collective-permute-done.5.listed_ref.refs_1_, ...), custom_call_target="tpu_custom_call" | custom-call | flops 10000000000 | bytes 1048576 | tf_op jit(solution)/shard_map/full/pallas_call | solution.py:498
  33.5 2.3 %collective-permute-start.17 = (bf16[384,128]{1,0:T(8,128)(2,1)S(1)}, bf16[384,128]{1,0:T(8,128)(2,1)S(1)}, u32[]{:S(2)}, u32[]{:S(2)}) collective-permute-start(bf16[384,128]{1,0:T(8,128)(2,1)S(1)} %get-tuple-element.57), channel_id=1, source_target_pairs={{0,8},{1,9},{2,10},{3,11},{4,12},{5,13},{6,14},{7,15},{8,0},{9,1},... | collective-permute-start | bytes 294920 | tf_op jit(solution)/shard_map/ppermute | solution.py:401
  35.8 2.3 %collective-permute-start.18 = (bf16[384,128]{1,0:T(8,128)(2,1)S(1)}, bf16[384,128]{1,0:T(8,128)(2,1)S(1)}, u32[]{:S(2)}, u32[]{:S(2)}) collective-permute-start(bf16[384,128]{1,0:T(8,128)(2,1)S(1)} %get-tuple-element.58), channel_id=1, source_target_pairs={{0,9},{1,8},{2,11},{3,10},{4,13},{5,12},{6,15},{7,14},{8,1},{9,0},... | collective-permute-start | bytes 294920 | tf_op jit(solution)/shard_map/ppermute | solution.py:401
  38.2 0.0 collective-permute-start.14
  38.2 0.0 collective-permute-done.7.refs_1_.refs_2_
  38.2 0.0 copy-start
  38.2 2.0 %full_near.1 = (bf16[384,128]{1,0:T(8,128)(2,1)S(1)}, bf16[192,128]{1,0:T(8,128)(2,1)S(1)}, bf16[192,128]{1,0:T(8,128)(2,1)S(1)}) custom-call(s32[1]{0:T(128)} %bitcast.place_ref, s32[16]{0:T(128)S(1)} %copy-done.2, s32[2,2,512]{2,1,0:T(2,128)S(1)} %copy-done.1, s32[2,2,512]{2,1,0:T(2,128)S(1)} %collective-permute-done.near_pairs_ref, ...), custom_call_target="tpu_custom_call" | custom-call | flops 500000000 | bytes 1048576 | tf_op jit(solution)/shard_map/full_near/pallas_call | solution.py:512
  40.2 0.6 %collective-permute-start.15 = (bf16[192,128]{1,0:T(8,128)(2,1)S(1)}, bf16[192,128]{1,0:T(8,128)(2,1)S(1)}, u32[]{:S(2)}, u32[]{:S(2)}) collective-permute-start(bf16[192,128]{1,0:T(8,128)(2,1)S(1)} %get-tuple-element.53), channel_id=1, source_target_pairs={{0,1},{1,0},{2,3},{3,2},{4,5},{5,4},{6,7},{7,6},{8,9},{9,8},{10,11... | collective-permute-start | bytes 147464 | tf_op jit(solution)/shard_map/ppermute | solution.py:401
  40.8 0.1 collective-permute-start.16
  40.8 0.0 collective-permute-done.14.refs_4_
  40.8 0.8 %collective-permute-done.15.refs_5_ = bf16[192,128]{1,0:T(8,128)(2,1)S(1)} collective-permute-done((bf16[192,128]{1,0:T(8,128)(2,1)S(1)}, bf16[192,128]{1,0:T(8,128)(2,1)S(1)}, u32[]{:S(2)}, u32[]{:S(2)}) %collective-permute-start.15) | collective-permute-done | bytes 49184 | tf_op jit(solution)/shard_map/ppermute | solution.py:401
  41.6 0.3 collective-permute-done.16.refs_6_
  42.0 1.8 %first_lags.1 = (f32[2,512,256]{2,1,0:T(8,128)S(1)}, bf16[2,96,512]{2,1,0:T(8,128)(2,1)S(1)}) custom-call(s32[1]{0:T(128)} %bitcast.place_ref, f32[256,256]{1,0:T(8,128)S(1)} %copy-done, bf16[256,128]{1,0:T(8,128)(2,1)S(1)} %get-tuple-element.39.after_ref.after_0.refs_0_, bf16[256,128]{1,0:T(8,128)(2,1)S(1)} %collective-permute-done.6.refs_0_.refs_1_, ...), custom_call_target="tpu_custom_call" | custom-call | flops 1000000 | bytes 1048576 | tf_op jit(solution)/shard_map/first_lags/pallas_call | solution.py:523
  43.8 2.7 %collective-permute-done.18.refs_1_ = bf16[384,128]{1,0:T(8,128)(2,1)S(1)} collective-permute-done((bf16[384,128]{1,0:T(8,128)(2,1)S(1)}, bf16[384,128]{1,0:T(8,128)(2,1)S(1)}, u32[]{:S(2)}, u32[]{:S(2)}) %collective-permute-start.18) | collective-permute-done | bytes 98336 | tf_op jit(solution)/shard_map/ppermute | solution.py:401
  46.5 1.4 %lags.1 = f32[2,512,256]{2,1,0:T(8,128)} custom-call(f32[2,512,256]{2,1,0:T(8,128)S(1)} %get-tuple-element.55.first_ref, bf16[2,96,512]{2,1,0:T(8,128)(2,1)S(1)} %get-tuple-element.56.table_ref, bf16[384,128]{1,0:T(8,128)(2,1)S(1)} %collective-permute-done.17.refs_0_, bf16[384,128]{1,0:T(8,128)(2,1)S(1)} %collective-permute-done.18.refs_1_), custom_call_target="tpu_custom_call" | custom-call | flops 1000000000 | bytes 1048576 | tf_op jit(solution)/shard_map/lags/pallas_call | solution.py:535
  (8 shorter events, 0.0 us)
Async XLA Ops:
  0.0 2.6 %collective-permute-start.1 = (bf16[3,2,4,64,256]{4,3,2,1,0:T(8,128)(2,1)}, bf16[3,2,4,64,256]{4,3,2,1,0:T(8,128)(2,1)S(1)}, u32[]{:S(2)}, u32[]{:S(2)}) collective-permute-start(bf16[3,2,4,64,256]{4,3,2,1,0:T(8,128)(2,1)} %bitcast.2), channel_id=1, source_target_pairs={{0,1},{1,0},{2,3},{3,2},{4,5},{5,4},{6,7},{7,6},{8,9},{9,8},{10,11... | collective-permute-start | bytes 2359304 | tf_op jit(solution)/shard_map/ppermute | solution.py:401
  0.5 2.1 %collective-permute-start = (s32[2,2,512]{2,1,0:T(2,128)}, s32[2,2,512]{2,1,0:T(2,128)S(1)}, u32[]{:S(2)}, u32[]{:S(2)}) collective-permute-start(s32[2,2,512]{2,1,0:T(2,128)} %own_pairs_ref.5), channel_id=1, source_target_pairs={{0,1},{1,0},{2,3},{3,2},{4,5},{5,4},{6,7},{7,6},{8,9},{9,8},{10,11... | collective-permute-start | bytes 24584 | tf_op jit(solution)/shard_map/ppermute | solution.py:401
  0.5 1.1 %copy-start.3 = (bf16[3,1,512,256]{3,2,1,0:T(8,128)(2,1)S(1)}, bf16[3,1,512,256]{3,2,1,0:T(8,128)(2,1)}, u32[]{:S(2)}) copy-start(bf16[3,1,512,256]{3,2,1,0:T(8,128)(2,1)} %param.4) | copy-start | bytes 2359300
  1.6 0.9 %copy-start.1 = (s32[2,2,512]{2,1,0:T(2,128)S(1)}, s32[2,2,512]{2,1,0:T(2,128)}, u32[]{:S(2)}) copy-start(s32[2,2,512]{2,1,0:T(2,128)} %own_pairs_ref.5) | copy-start | bytes 24580
  3.4 20.6 %collective-permute-start.5 = (bf16[320,128]{1,0:T(8,128)(2,1)S(1)}, bf16[320,128]{1,0:T(8,128)(2,1)S(1)}, u32[]{:S(2)}, u32[]{:S(2)}) collective-permute-start(bf16[320,128]{1,0:T(8,128)(2,1)S(1)} %get-tuple-element.40), channel_id=1, source_target_pairs={{0,8},{1,9},{2,10},{3,11},{4,12},{5,13},{6,14},{7,15},{8,0},{9,1},... | collective-permute-start | bytes 245768 | tf_op jit(solution)/shard_map/ppermute | solution.py:401
  7.5 16.4 %collective-permute-start.8 = (bf16[288,128]{1,0:T(8,128)(2,1)S(1)}, bf16[288,128]{1,0:T(8,128)(2,1)S(1)}, u32[]{:S(2)}, u32[]{:S(2)}) collective-permute-start(bf16[288,128]{1,0:T(8,128)(2,1)S(1)} %get-tuple-element.44), channel_id=1, source_target_pairs={{0,10},{1,11},{2,8},{3,9},{4,14},{5,15},{6,12},{7,13},{8,2},{9,3},... | collective-permute-start | bytes 221192 | tf_op jit(solution)/shard_map/ppermute | solution.py:401
  8.8 4.3 %collective-permute-start.2 = (bf16[192,128]{1,0:T(8,128)(2,1)S(1)}, bf16[192,128]{1,0:T(8,128)(2,1)S(1)}, u32[]{:S(2)}, u32[]{:S(2)}) collective-permute-start(bf16[192,128]{1,0:T(8,128)(2,1)S(1)} %get-tuple-element.36), channel_id=1, source_target_pairs={{0,2},{1,3},{2,0},{3,1},{4,6},{5,7},{6,4},{7,5},{8,10},{9,11},{10,... | collective-permute-start | bytes 147464 | tf_op jit(solution)/shard_map/ppermute | solution.py:401
  9.0 7.4 %collective-permute-start.3 = (bf16[192,128]{1,0:T(8,128)(2,1)S(1)}, bf16[192,128]{1,0:T(8,128)(2,1)S(1)}, u32[]{:S(2)}, u32[]{:S(2)}) collective-permute-start(bf16[192,128]{1,0:T(8,128)(2,1)S(1)} %get-tuple-element.37), channel_id=1, source_target_pairs={{0,4},{1,5},{2,6},{3,7},{4,0},{5,1},{6,2},{7,3},{8,12},{9,13},{10,... | collective-permute-start | bytes 147464 | tf_op jit(solution)/shard_map/ppermute | solution.py:401
  10.8 10.4 %collective-permute-start.4 = (bf16[192,128]{1,0:T(8,128)(2,1)S(1)}, bf16[192,128]{1,0:T(8,128)(2,1)S(1)}, u32[]{:S(2)}, u32[]{:S(2)}) collective-permute-start(bf16[192,128]{1,0:T(8,128)(2,1)S(1)} %get-tuple-element.38), channel_id=1, source_target_pairs={{0,6},{1,7},{2,4},{3,5},{4,2},{5,3},{6,0},{7,1},{8,14},{9,15},{10,... | collective-permute-start | bytes 147464 | tf_op jit(solution)/shard_map/ppermute | solution.py:401
  13.1 16.7 %collective-permute-start.9 = (bf16[288,128]{1,0:T(8,128)(2,1)S(1)}, bf16[288,128]{1,0:T(8,128)(2,1)S(1)}, u32[]{:S(2)}, u32[]{:S(2)}) collective-permute-start(bf16[288,128]{1,0:T(8,128)(2,1)S(1)} %get-tuple-element.45), channel_id=1, source_target_pairs={{0,12},{1,13},{2,14},{3,15},{4,8},{5,9},{6,10},{7,11},{8,4},{9,5},... | collective-permute-start | bytes 221192 | tf_op jit(solution)/shard_map/ppermute | solution.py:401
  16.5 14.1 %collective-permute-start.10 = (bf16[288,128]{1,0:T(8,128)(2,1)S(1)}, bf16[288,128]{1,0:T(8,128)(2,1)S(1)}, u32[]{:S(2)}, u32[]{:S(2)}) collective-permute-start(bf16[288,128]{1,0:T(8,128)(2,1)S(1)} %get-tuple-element.46), channel_id=1, source_target_pairs={{0,14},{1,15},{2,12},{3,13},{4,10},{5,11},{6,8},{7,9},{8,6},{9,7},... | collective-permute-start | bytes 221192 | tf_op jit(solution)/shard_map/ppermute | solution.py:401
  21.3 9.3 %collective-permute-start.11 = (bf16[288,128]{1,0:T(8,128)(2,1)S(1)}, bf16[288,128]{1,0:T(8,128)(2,1)S(1)}, u32[]{:S(2)}, u32[]{:S(2)}) collective-permute-start(bf16[288,128]{1,0:T(8,128)(2,1)S(1)} %get-tuple-element.47), channel_id=1, source_target_pairs={{0,2},{1,3},{2,0},{3,1},{4,6},{5,7},{6,4},{7,5},{8,10},{9,11},{10,... | collective-permute-start | bytes 221192 | tf_op jit(solution)/shard_map/ppermute | solution.py:401
  21.3 0.9 %copy-start.2 = (s32[16]{0:T(128)S(1)}, s32[16]{0:T(128)}, u32[]{:S(2)}) copy-start(s32[16]{0:T(128)} %counts_ref.7) | copy-start | bytes 196
  23.9 6.6 %collective-permute-start.12 = (bf16[288,128]{1,0:T(8,128)(2,1)S(1)}, bf16[288,128]{1,0:T(8,128)(2,1)S(1)}, u32[]{:S(2)}, u32[]{:S(2)}) collective-permute-start(bf16[288,128]{1,0:T(8,128)(2,1)S(1)} %get-tuple-element.48), channel_id=1, source_target_pairs={{0,4},{1,5},{2,6},{3,7},{4,0},{5,1},{6,2},{7,3},{8,12},{9,13},{10,... | collective-permute-start | bytes 221192 | tf_op jit(solution)/shard_map/ppermute | solution.py:401
  24.0 6.6 %collective-permute-start.13 = (bf16[288,128]{1,0:T(8,128)(2,1)S(1)}, bf16[288,128]{1,0:T(8,128)(2,1)S(1)}, u32[]{:S(2)}, u32[]{:S(2)}) collective-permute-start(bf16[288,128]{1,0:T(8,128)(2,1)S(1)} %get-tuple-element.49), channel_id=1, source_target_pairs={{0,6},{1,7},{2,4},{3,5},{4,2},{5,3},{6,0},{7,1},{8,14},{9,15},{10,... | collective-permute-start | bytes 221192 | tf_op jit(solution)/shard_map/ppermute | solution.py:401
  29.8 8.4 %collective-permute-start.6 = (bf16[256,128]{1,0:T(8,128)(2,1)S(1)}, bf16[256,128]{1,0:T(8,128)(2,1)S(1)}, u32[]{:S(2)}, u32[]{:S(2)}) collective-permute-start(bf16[256,128]{1,0:T(8,128)(2,1)S(1)} %get-tuple-element.41.after_1.after_2), channel_id=1, source_target_pairs={{0,8},{1,9},{2,10},{3,11},{4,12},{5,13},{6,14},{7,15},{8,0},{9,1},... | collective-permute-start | bytes 196616 | tf_op jit(solution)/shard_map/ppermute | solution.py:401
  30.6 7.6 %collective-permute-start.7 = (bf16[256,128]{1,0:T(8,128)(2,1)S(1)}, bf16[256,128]{1,0:T(8,128)(2,1)S(1)}, u32[]{:S(2)}, u32[]{:S(2)}) collective-permute-start(bf16[256,128]{1,0:T(8,128)(2,1)S(1)} %get-tuple-element.42), channel_id=1, source_target_pairs={{0,9},{1,8},{2,11},{3,10},{4,13},{5,12},{6,15},{7,14},{8,1},{9,0},... | collective-permute-start | bytes 196616 | tf_op jit(solution)/shard_map/ppermute | solution.py:401
  33.5 10.2 %collective-permute-start.17 = (bf16[384,128]{1,0:T(8,128)(2,1)S(1)}, bf16[384,128]{1,0:T(8,128)(2,1)S(1)}, u32[]{:S(2)}, u32[]{:S(2)}) collective-permute-start(bf16[384,128]{1,0:T(8,128)(2,1)S(1)} %get-tuple-element.57), channel_id=1, source_target_pairs={{0,8},{1,9},{2,10},{3,11},{4,12},{5,13},{6,14},{7,15},{8,0},{9,1},... | collective-permute-start | bytes 294920 | tf_op jit(solution)/shard_map/ppermute | solution.py:401
  35.8 10.7 %collective-permute-start.18 = (bf16[384,128]{1,0:T(8,128)(2,1)S(1)}, bf16[384,128]{1,0:T(8,128)(2,1)S(1)}, u32[]{:S(2)}, u32[]{:S(2)}) collective-permute-start(bf16[384,128]{1,0:T(8,128)(2,1)S(1)} %get-tuple-element.58), channel_id=1, source_target_pairs={{0,9},{1,8},{2,11},{3,10},{4,13},{5,12},{6,15},{7,14},{8,1},{9,0},... | collective-permute-start | bytes 294920 | tf_op jit(solution)/shard_map/ppermute | solution.py:401
  38.2 2.7 %collective-permute-start.14 = (bf16[256,128]{1,0:T(8,128)(2,1)S(1)}, bf16[256,128]{1,0:T(8,128)(2,1)S(1)}, u32[]{:S(2)}, u32[]{:S(2)}) collective-permute-start(bf16[256,128]{1,0:T(8,128)(2,1)S(1)} %get-tuple-element.52), channel_id=1, source_target_pairs={{0,1},{1,0},{2,3},{3,2},{4,5},{5,4},{6,7},{7,6},{8,9},{9,8},{10,11... | collective-permute-start | bytes 196616 | tf_op jit(solution)/shard_map/ppermute | solution.py:401
  38.2 3.8 %copy-start = (f32[256,256]{1,0:T(8,128)S(1)}, f32[256,256]{1,0:T(8,128)}, u32[]{:S(2)}) copy-start(f32[256,256]{1,0:T(8,128)} %constant.6.clone.inverse_ref) | copy-start | bytes 786436
  40.2 1.4 %collective-permute-start.15 = (bf16[192,128]{1,0:T(8,128)(2,1)S(1)}, bf16[192,128]{1,0:T(8,128)(2,1)S(1)}, u32[]{:S(2)}, u32[]{:S(2)}) collective-permute-start(bf16[192,128]{1,0:T(8,128)(2,1)S(1)} %get-tuple-element.53), channel_id=1, source_target_pairs={{0,1},{1,0},{2,3},{3,2},{4,5},{5,4},{6,7},{7,6},{8,9},{9,8},{10,11... | collective-permute-start | bytes 147464 | tf_op jit(solution)/shard_map/ppermute | solution.py:401
  40.8 1.2 %collective-permute-start.16 = (bf16[192,128]{1,0:T(8,128)(2,1)S(1)}, bf16[192,128]{1,0:T(8,128)(2,1)S(1)}, u32[]{:S(2)}, u32[]{:S(2)}) collective-permute-start(bf16[192,128]{1,0:T(8,128)(2,1)S(1)} %get-tuple-element.54), channel_id=1, source_target_pairs={{0,1},{1,0},{2,3},{3,2},{4,5},{5,4},{6,7},{7,6},{8,9},{9,8},{10,11... | collective-permute-start | bytes 147464 | tf_op jit(solution)/shard_map/ppermute | solution.py:401

commit v15 on v13

--- a/solution.py
+++ b/solution.py
@@ -28,8 +28,8 @@
 TN = (((0,), (0,)), ((), ()))
 VMEM_LIMIT = 40 * 1024 * 1024
 
-PART = 16
-FULL = 24
+PART = 32
+FULL = 16
 
 
 def inverse_table(samples, stations):

time: 41.9 us -> 46.5 us (1.11)
  waiting for transfers between devices: 3.75 us -> 10 us
  starting transfers between devices: 21.7 us -> 20.8 us
  Pallas kernels: 14.7 us -> 14.2 us
    ppermute x16, waiting for transfers between devices: 3.75 us -> 10 us  [swap(): return lax.ppermute(x, 'cell', [(i, i ^ mask) for i in range(cells)])]
    ppermute x16, starting transfers between devices: 21.7 us -> 20.8 us  [swap(): return lax.ppermute(x, 'cell', [(i, i ^ mask) for i in range(cells)])]
    pallas_call x1, Pallas kernels: 0.91 us -> 1.69 us  [on_device(): pl.pallas_call(part_kernel, out_shape=part_blocks, in_specs=[vmem] * grou...]
    pallas_call x1, Pallas kernels: 2.81 us -> 2.22 us  [on_device(): pl.pallas_call(full_kernel, out_shape=[full_blocks, full_packed, full_pac...]
  transfers between devices with their start and end apart: 16 -> 16, of which waited for: 6 -> 5; matrix products, arithmetic and copies ran while one was open for 0% -> 0% of each run, Pallas kernels for 30% -> 26%
where the time goes in v15:
time: 46.5 us; the launch traced here: 46.3 us
  starting transfers between devices  20.8 us (45%)
  Pallas kernels  14.2 us (31%)
  waiting for transfers between devices  10 us (22%)
  local copies, waits for them, and re-layouts  1.14 us (2%)
    ppermute x16, starting transfers between devices, swap(): return lax.ppermute(x, 'cell', [(i, i ^ mask) for i in range(cells)])  20.8 us
    ppermute x16, waiting for transfers between devices, swap(): return lax.ppermute(x, 'cell', [(i, i ^ mask) for i in range(cells)])  10 us
    pallas_call x1, Pallas kernels, on_device(): pl.pallas_call(full_kernel, out_shape=[full_blocks, full_packed, full_pac...  2.22 us
    pallas_call x1, Pallas kernels, on_device(): pl.pallas_call(functools.partial(first_lags_kernel, groups), out_shape=[s...  1.78 us
    pallas_call x1, Pallas kernels, on_device(): pl.pallas_call(part_kernel, out_shape=part_blocks, in_specs=[vmem] * grou...  1.69 us
    pallas_call x1, Pallas kernels, on_device(): pl.pallas_call(functools.partial(near_kernel, FULL, 2), out_shape=[full_p...  1.68 us
    pallas_call x1, Pallas kernels, on_device(): pl.pallas_call(functools.partial(far_kernel, PART), out_shape=[part_packe...  1.54 us
    pallas_call x1, Pallas kernels, on_device(): pl.pallas_call(functools.partial(near_kernel, PART, 1), out_shape=[part_p...  1.54 us
  transfers between devices with their start and end apart: 16, of which 5 were waited for; matrix products, arithmetic and copies ran while one was open for 0% of the time, Pallas kernels for 26%

profile of v15, /device:TPU:0, one launch (start us, length us, event | category | flops | bytes accessed | tf_op | source)
XLA Modules:
  0.0 46.3 jit_solution(9608791368128466860)
XLA Ops:
  0.0 0.5 collective-permute-start.1
  0.5 0.1 collective-permute-start
  0.5 0.0 copy-start.3
  0.5 1.1 %copy-done.3 = bf16[3,1,512,256]{3,2,1,0:T(8,128)(2,1)S(1)} copy-done((bf16[3,1,512,256]{3,2,1,0:T(8,128)(2,1)S(1)}, bf16[3,1,512,256]{3,2,1,0:T(8,128)(2,1)}, u32[]{:S(2)}) %copy-start.3) | copy-done | bytes 786456
  1.6 0.0 copy-start.1
  1.6 0.8 %own_spectra.1 = (bf16[4,192,128]{2,1,0:T(8,128)(2,1)S(1)}, bf16[8,96,128]{2,1,0:T(8,128)(2,1)S(1)}, bf16[128,256]{1,0:T(8,128)(2,1)S(1)}) custom-call(s32[1]{0:T(128)} %bitcast.place_ref, bf16[3,2,4,64,256]{4,3,2,1,0:T(8,128)(2,1)S(1)} %bitcast.3), custom_call_target="tpu_custom_call" | custom-call | flops 1000000000 | bytes 1048576 | tf_op jit(solution)/shard_map/own_spectra/pallas_call | solution.py:427
  2.5 0.1 collective-permute-done.near_pairs_ref
  2.6 0.0 collective-permute-done.1.windows_ref
  2.6 0.0 copy-done.1
  2.6 0.8 %near_spectra.1 = (bf16[576,128]{1,0:T(8,128)(2,1)S(1)}, bf16[576,128]{1,0:T(8,128)(2,1)S(1)}, bf16[576,128]{1,0:T(8,128)(2,1)S(1)}, bf16[576,128]{1,0:T(8,128)(...) custom-call(s32[1]{0:T(128)} %bitcast.place_ref, ...), custom_call_target="tpu_custom_call" | custom-call | flops 1000000000 | bytes 1048576 | tf_op jit(solution)/shard_map/near_spectra/pallas_call | solution.py:441
  3.4 3.0 %collective-permute-start.2 = (bf16[576,128]{1,0:T(8,128)(2,1)S(1)}, bf16[576,128]{1,0:T(8,128)(2,1)S(1)}, u32[]{:S(2)}, u32[]{:S(2)}) collective-permute-start(bf16[576,128]{1,0:T(8,128)(2,1)S(1)} %get-tuple-element.32), channel_id=1, source_target_pairs={{0,2},{1,3},{2,0},{3,1},{4,6},{5,7},{6,4},{7,5},{8,10},{9,11},{10,... | collective-permute-start | bytes 442376 | tf_op jit(solution)/shard_map/ppermute | solution.py:410
  6.4 1.6 %collective-permute-start.3 = (bf16[576,128]{1,0:T(8,128)(2,1)S(1)}, bf16[576,128]{1,0:T(8,128)(2,1)S(1)}, u32[]{:S(2)}, u32[]{:S(2)}) collective-permute-start(bf16[576,128]{1,0:T(8,128)(2,1)S(1)} %get-tuple-element.33), channel_id=1, source_target_pairs={{0,4},{1,5},{2,6},{3,7},{4,0},{5,1},{6,2},{7,3},{8,12},{9,13},{10,... | collective-permute-start | bytes 442376 | tf_op jit(solution)/shard_map/ppermute | solution.py:410
  8.0 0.0 collective-permute-start.4
  8.0 3.0 %collective-permute-start.5 = (bf16[224,128]{1,0:T(8,128)(2,1)S(1)}, bf16[224,128]{1,0:T(8,128)(2,1)S(1)}, u32[]{:S(2)}, u32[]{:S(2)}) collective-permute-start(bf16[224,128]{1,0:T(8,128)(2,1)S(1)} %get-tuple-element.36), channel_id=1, source_target_pairs={{0,8},{1,9},{2,10},{3,11},{4,12},{5,13},{6,14},{7,15},{8,0},{9,1},... | collective-permute-start | bytes 172040 | tf_op jit(solution)/shard_map/ppermute | solution.py:410
  11.0 1.3 %collective-permute-start.8 = (bf16[192,128]{1,0:T(8,128)(2,1)S(1)}, bf16[192,128]{1,0:T(8,128)(2,1)S(1)}, u32[]{:S(2)}, u32[]{:S(2)}) collective-permute-start(bf16[192,128]{1,0:T(8,128)(2,1)S(1)} %get-tuple-element.39), channel_id=1, source_target_pairs={{0,10},{1,11},{2,8},{3,9},{4,14},{5,15},{6,12},{7,13},{8,2},{9,3},... | collective-permute-start | bytes 147464 | tf_op jit(solution)/shard_map/ppermute | solution.py:410
  12.3 0.0 collective-permute-done.2.refs_1_
  12.3 3.6 %collective-permute-start.9 = (bf16[192,128]{1,0:T(8,128)(2,1)S(1)}, bf16[192,128]{1,0:T(8,128)(2,1)S(1)}, u32[]{:S(2)}, u32[]{:S(2)}) collective-permute-start(bf16[192,128]{1,0:T(8,128)(2,1)S(1)} %get-tuple-element.40), channel_id=1, source_target_pairs={{0,12},{1,13},{2,14},{3,15},{4,8},{5,9},{6,10},{7,11},{8,4},{9,5},... | collective-permute-start | bytes 147464 | tf_op jit(solution)/shard_map/ppermute | solution.py:410
  15.9 0.0 collective-permute-done.3.refs_2_
  15.9 2.1 %collective-permute-start.10 = (bf16[192,128]{1,0:T(8,128)(2,1)S(1)}, bf16[192,128]{1,0:T(8,128)(2,1)S(1)}, u32[]{:S(2)}, u32[]{:S(2)}) collective-permute-start(bf16[192,128]{1,0:T(8,128)(2,1)S(1)} %get-tuple-element.41), channel_id=1, source_target_pairs={{0,14},{1,15},{2,12},{3,13},{4,10},{5,11},{6,8},{7,9},{8,6},{9,7},... | collective-permute-start | bytes 147464 | tf_op jit(solution)/shard_map/ppermute | solution.py:410
  18.0 0.0 collective-permute-done.4.refs_3_
  18.0 1.7 %part.1.flat_ref = bf16[2,2,256,256]{3,2,1,0:T(8,128)(2,1)S(1)} custom-call(bf16[576,128]{1,0:T(8,128)(2,1)S(1)} %get-tuple-element.31.refs_0_, bf16[576,128]{1,0:T(8,128)(2,1)S(1)} %collective-permute-done.2.refs_1_, bf16[576,128]{1,0:T(8,128)(2,1)S(1)} %collective-permute-done.3.refs_2_, bf16[576,128]{1,0:T(8,128)(2,1)S(1)} %collective-permute-done.4.refs_3_), custom_call_target="tpu_custom_call" | custom-call | flops 1000000 | bytes 1048576 | tf_op jit(solution)/shard_map/part/pallas_call | solution.py:460
  19.7 0.0 copy-done.2
  19.7 1.5 %part_near.1 = (bf16[512,128]{1,0:T(8,128)(2,1)S(1)}, bf16[512,128]{1,0:T(8,128)(2,1)S(1)}) custom-call(s32[1]{0:T(128)} %bitcast.place_ref, s32[16]{0:T(128)S(1)} %copy-done.2, s32[2,2,512]{2,1,0:T(2,128)S(1)} %copy-done.1, s32[2,2,512]{2,1,0:T(2,128)S(1)} %collective-permute-done.near_pairs_ref, bf16[2,2,256,256]{3,2,1,0:T(8,128)(2,1)S(1)} %part.1.flat_ref), custom_call_target="tpu_custom_call" | custom-call | flops 1000000 | bytes 1048576 | tf_op jit(solution)/shard_map/part_near/pallas_call | solution.py:473
  21.2 0.0 collective-permute-done.5.listed_ref.refs_4_
  21.2 1.5 %part_far.1 = (bf16[512,128]{1,0:T(8,128)(2,1)S(1)}, bf16[512,128]{1,0:T(8,128)(2,1)S(1)}) custom-call(s32[1]{0:T(128)} %bitcast.place_ref, s32[16]{0:T(128)S(1)} %copy-done.2, bf16[224,128]{1,0:T(8,128)(2,1)S(1)} %collective-permute-done.5.listed_ref.refs_4_, bf16[2,2,256,256]{3,2,1,0:T(8,128)(2,1)S(1)} %part.1.flat_ref, ...), custom_call_target="tpu_custom_call" | custom-call | flops 1000000000 | bytes 1048576 | tf_op jit(solution)/shard_map/part_far/pallas_call | solution.py:482
  22.8 0.1 collective-permute-start.7
  22.9 2.3 %collective-permute-start.6 = (bf16[512,128]{1,0:T(8,128)(2,1)S(1)}, bf16[512,128]{1,0:T(8,128)(2,1)S(1)}, u32[]{:S(2)}, u32[]{:S(2)}) collective-permute-start(bf16[512,128]{1,0:T(8,128)(2,1)S(1)} %get-tuple-element.37.after_1.after_2), channel_id=1, source_target_pairs={{0,8},{1,9},{2,10},{3,11},{4,12},{5,13},{6,14},{7,15},{8,0},{9,1},... | collective-permute-start | bytes 393224 | tf_op jit(solution)/shard_map/ppermute | solution.py:410
  25.1 0.0 collective-permute-done.8.refs_5_
  25.1 0.5 collective-permute-start.11
  25.6 0.8 %early.1.before_ref = f32[1024,128]{1,0:T(8,128)S(1)} custom-call(bf16[512,128]{1,0:T(8,128)(2,1)S(1)} %get-tuple-element.35.after_ref.after_0.refs_0_, bf16[512,128]{1,0:T(8,128)(2,1)S(1)} %get-tuple-element.37.after_1.after_2, bf16[576,128]{1,0:T(8,128)(2,1)S(1)} %get-tuple-element.31.refs_0_, bf16[576,128]{1,0:T(8,128)(2,1)S(1)} %collective-permute-done.2.refs_1_, ...), custom_call_target="tpu_custom_call" | custom-call | flops 1000000 | bytes 1048576 | tf_op jit(solution)/shard_map/early/pallas_call | solution.py:492
  26.4 0.0 collective-permute-done.9.refs_0_
  26.4 0.0 collective-permute-done.10.refs_1_
  26.4 2.2 %full.1 = (bf16[2,2,128,256]{3,2,1,0:T(8,128)(2,1)S(1)}, bf16[256,128]{1,0:T(8,128)(2,1)S(1)}, bf16[256,128]{1,0:T(8,128)(2,1)S(1)}) custom-call(s32[1]{0:T(128)} %bitcast.place_ref, s32[16]{0:T(128)S(1)} %copy-done.2, bf16[224,128]{1,0:T(8,128)(2,1)S(1)} %collective-permute-done.5.listed_ref.refs_4_, ...), custom_call_target="tpu_custom_call" | custom-call | flops 10000000000 | bytes 1048576 | tf_op jit(solution)/shard_map/full/pallas_call | solution.py:505
  28.6 2.3 %collective-permute-start.14 = (bf16[256,128]{1,0:T(8,128)(2,1)S(1)}, bf16[256,128]{1,0:T(8,128)(2,1)S(1)}, u32[]{:S(2)}, u32[]{:S(2)}) collective-permute-start(bf16[256,128]{1,0:T(8,128)(2,1)S(1)} %get-tuple-element.49), channel_id=1, source_target_pairs={{0,8},{1,9},{2,10},{3,11},{4,12},{5,13},{6,14},{7,15},{8,0},{9,1},... | collective-permute-start | bytes 196616 | tf_op jit(solution)/shard_map/ppermute | solution.py:410
  30.9 0.1 collective-permute-start.15
  31.0 6.3 %collective-permute-done.7.refs_1_.refs_2_ = bf16[512,128]{1,0:T(8,128)(2,1)S(1)} collective-permute-done((bf16[512,128]{1,0:T(8,128)(2,1)S(1)}, bf16[512,128]{1,0:T(8,128)(2,1)S(1)}, u32[]{:S(2)}, u32[]{:S(2)}) %collective-permute-start.7) | collective-permute-done | bytes 131104 | tf_op jit(solution)/shard_map/ppermute | solution.py:410
  37.3 2.8 %collective-permute-done.6.refs_0_.refs_1_ = bf16[512,128]{1,0:T(8,128)(2,1)S(1)} collective-permute-done((bf16[512,128]{1,0:T(8,128)(2,1)S(1)}, bf16[512,128]{1,0:T(8,128)(2,1)S(1)}, u32[]{:S(2)}, u32[]{:S(2)}) %collective-permute-start.6) | collective-permute-done | bytes 131104 | tf_op jit(solution)/shard_map/ppermute | solution.py:410
  40.0 1.7 %full_near.1 = (bf16[256,128]{1,0:T(8,128)(2,1)S(1)}, bf16[128,128]{1,0:T(8,128)(2,1)S(1)}, bf16[128,128]{1,0:T(8,128)(2,1)S(1)}) custom-call(s32[1]{0:T(128)} %bitcast.place_ref, s32[16]{0:T(128)S(1)} %copy-done.2, s32[2,2,512]{2,1,0:T(2,128)S(1)} %copy-done.1, s32[2,2,512]{2,1,0:T(2,128)S(1)} %collective-permute-done.near_pairs_ref, ...), custom_call_target="tpu_custom_call" | custom-call | flops 500000000 | bytes 1048576 | tf_op jit(solution)/shard_map/full_near/pallas_call | solution.py:519
  41.7 0.2 collective-permute-start.12
  41.9 0.4 collective-permute-start.13
  42.3 0.0 collective-permute-done.11.refs_4_
  42.3 0.7 %collective-permute-done.12.refs_5_ = bf16[128,128]{1,0:T(8,128)(2,1)S(1)} collective-permute-done((bf16[128,128]{1,0:T(8,128)(2,1)S(1)}, bf16[128,128]{1,0:T(8,128)(2,1)S(1)}, u32[]{:S(2)}, u32[]{:S(2)}) %collective-permute-start.12) | collective-permute-done | bytes 32800 | tf_op jit(solution)/shard_map/ppermute | solution.py:410
  43.0 0.2 collective-permute-done.13.refs_6_
  43.2 0.0 copy-done
  43.2 1.8 %first_lags.1 = (f32[2,512,256]{2,1,0:T(8,128)S(1)}, bf16[2,64,512]{2,1,0:T(8,128)(2,1)S(1)}) custom-call(s32[1]{0:T(128)} %bitcast.place_ref, f32[256,256]{1,0:T(8,128)S(1)} %copy-done, bf16[512,128]{1,0:T(8,128)(2,1)S(1)} %get-tuple-element.35.after_ref.after_0.refs_0_, bf16[512,128]{1,0:T(8,128)(2,1)S(1)} %collective-permute-done.6.refs_0_.refs_1_, ...), custom_call_target="tpu_custom_call" | custom-call | flops 1000000 | bytes 1048576 | tf_op jit(solution)/shard_map/first_lags/pallas_call | solution.py:530
  45.0 0.0 collective-permute-done.14.refs_0_
  45.0 0.0 collective-permute-done.15.refs_1_
  45.0 1.4 %lags.1 = f32[2,512,256]{2,1,0:T(8,128)} custom-call(f32[2,512,256]{2,1,0:T(8,128)S(1)} %get-tuple-element.47.first_ref, bf16[2,64,512]{2,1,0:T(8,128)(2,1)S(1)} %get-tuple-element.48.table_ref, bf16[256,128]{1,0:T(8,128)(2,1)S(1)} %collective-permute-done.14.refs_0_, bf16[256,128]{1,0:T(8,128)(2,1)S(1)} %collective-permute-done.15.refs_1_), custom_call_target="tpu_custom_call" | custom-call | flops 1000000000 | bytes 1048576 | tf_op jit(solution)/shard_map/lags/pallas_call | solution.py:542
  (2 shorter events, 0.0 us)
Async XLA Ops:
  0.0 2.6 %collective-permute-start.1 = (bf16[3,2,4,64,256]{4,3,2,1,0:T(8,128)(2,1)}, bf16[3,2,4,64,256]{4,3,2,1,0:T(8,128)(2,1)S(1)}, u32[]{:S(2)}, u32[]{:S(2)}) collective-permute-start(bf16[3,2,4,64,256]{4,3,2,1,0:T(8,128)(2,1)} %bitcast.2), channel_id=1, source_target_pairs={{0,1},{1,0},{2,3},{3,2},{4,5},{5,4},{6,7},{7,6},{8,9},{9,8},{10,11... | collective-permute-start | bytes 2359304 | tf_op jit(solution)/shard_map/ppermute | solution.py:410
  0.5 2.1 %collective-permute-start = (s32[2,2,512]{2,1,0:T(2,128)}, s32[2,2,512]{2,1,0:T(2,128)S(1)}, u32[]{:S(2)}, u32[]{:S(2)}) collective-permute-start(s32[2,2,512]{2,1,0:T(2,128)} %own_pairs_ref.5), channel_id=1, source_target_pairs={{0,1},{1,0},{2,3},{3,2},{4,5},{5,4},{6,7},{7,6},{8,9},{9,8},{10,11... | collective-permute-start | bytes 24584 | tf_op jit(solution)/shard_map/ppermute | solution.py:410
  0.5 1.1 %copy-start.3 = (bf16[3,1,512,256]{3,2,1,0:T(8,128)(2,1)S(1)}, bf16[3,1,512,256]{3,2,1,0:T(8,128)(2,1)}, u32[]{:S(2)}) copy-start(bf16[3,1,512,256]{3,2,1,0:T(8,128)(2,1)} %param.4) | copy-start | bytes 2359300
  1.6 0.9 %copy-start.1 = (s32[2,2,512]{2,1,0:T(2,128)S(1)}, s32[2,2,512]{2,1,0:T(2,128)}, u32[]{:S(2)}) copy-start(s32[2,2,512]{2,1,0:T(2,128)} %own_pairs_ref.5) | copy-start | bytes 24580
  3.4 8.8 %collective-permute-start.2 = (bf16[576,128]{1,0:T(8,128)(2,1)S(1)}, bf16[576,128]{1,0:T(8,128)(2,1)S(1)}, u32[]{:S(2)}, u32[]{:S(2)}) collective-permute-start(bf16[576,128]{1,0:T(8,128)(2,1)S(1)} %get-tuple-element.32), channel_id=1, source_target_pairs={{0,2},{1,3},{2,0},{3,1},{4,6},{5,7},{6,4},{7,5},{8,10},{9,11},{10,... | collective-permute-start | bytes 442376 | tf_op jit(solution)/shard_map/ppermute | solution.py:410
  6.4 9.5 %collective-permute-start.3 = (bf16[576,128]{1,0:T(8,128)(2,1)S(1)}, bf16[576,128]{1,0:T(8,128)(2,1)S(1)}, u32[]{:S(2)}, u32[]{:S(2)}) collective-permute-start(bf16[576,128]{1,0:T(8,128)(2,1)S(1)} %get-tuple-element.33), channel_id=1, source_target_pairs={{0,4},{1,5},{2,6},{3,7},{4,0},{5,1},{6,2},{7,3},{8,12},{9,13},{10,... | collective-permute-start | bytes 442376 | tf_op jit(solution)/shard_map/ppermute | solution.py:410
  8.0 10.0 %collective-permute-start.4 = (bf16[576,128]{1,0:T(8,128)(2,1)S(1)}, bf16[576,128]{1,0:T(8,128)(2,1)S(1)}, u32[]{:S(2)}, u32[]{:S(2)}) collective-permute-start(bf16[576,128]{1,0:T(8,128)(2,1)S(1)} %get-tuple-element.34), channel_id=1, source_target_pairs={{0,6},{1,7},{2,4},{3,5},{4,2},{5,3},{6,0},{7,1},{8,14},{9,15},{10,... | collective-permute-start | bytes 442376 | tf_op jit(solution)/shard_map/ppermute | solution.py:410
  8.0 13.2 %collective-permute-start.5 = (bf16[224,128]{1,0:T(8,128)(2,1)S(1)}, bf16[224,128]{1,0:T(8,128)(2,1)S(1)}, u32[]{:S(2)}, u32[]{:S(2)}) collective-permute-start(bf16[224,128]{1,0:T(8,128)(2,1)S(1)} %get-tuple-element.36), channel_id=1, source_target_pairs={{0,8},{1,9},{2,10},{3,11},{4,12},{5,13},{6,14},{7,15},{8,0},{9,1},... | collective-permute-start | bytes 172040 | tf_op jit(solution)/shard_map/ppermute | solution.py:410
  11.0 14.2 %collective-permute-start.8 = (bf16[192,128]{1,0:T(8,128)(2,1)S(1)}, bf16[192,128]{1,0:T(8,128)(2,1)S(1)}, u32[]{:S(2)}, u32[]{:S(2)}) collective-permute-start(bf16[192,128]{1,0:T(8,128)(2,1)S(1)} %get-tuple-element.39), channel_id=1, source_target_pairs={{0,10},{1,11},{2,8},{3,9},{4,14},{5,15},{6,12},{7,13},{8,2},{9,3},... | collective-permute-start | bytes 147464 | tf_op jit(solution)/shard_map/ppermute | solution.py:410
  12.3 14.1 %collective-permute-start.9 = (bf16[192,128]{1,0:T(8,128)(2,1)S(1)}, bf16[192,128]{1,0:T(8,128)(2,1)S(1)}, u32[]{:S(2)}, u32[]{:S(2)}) collective-permute-start(bf16[192,128]{1,0:T(8,128)(2,1)S(1)} %get-tuple-element.40), channel_id=1, source_target_pairs={{0,12},{1,13},{2,14},{3,15},{4,8},{5,9},{6,10},{7,11},{8,4},{9,5},... | collective-permute-start | bytes 147464 | tf_op jit(solution)/shard_map/ppermute | solution.py:410
  15.9 10.5 %collective-permute-start.10 = (bf16[192,128]{1,0:T(8,128)(2,1)S(1)}, bf16[192,128]{1,0:T(8,128)(2,1)S(1)}, u32[]{:S(2)}, u32[]{:S(2)}) collective-permute-start(bf16[192,128]{1,0:T(8,128)(2,1)S(1)} %get-tuple-element.41), channel_id=1, source_target_pairs={{0,14},{1,15},{2,12},{3,13},{4,10},{5,11},{6,8},{7,9},{8,6},{9,7},... | collective-permute-start | bytes 147464 | tf_op jit(solution)/shard_map/ppermute | solution.py:410
  18.0 1.7 %copy-start.2 = (s32[16]{0:T(128)S(1)}, s32[16]{0:T(128)}, u32[]{:S(2)}) copy-start(s32[16]{0:T(128)} %counts_ref.7) | copy-start | bytes 196
  22.8 14.5 %collective-permute-start.7 = (bf16[512,128]{1,0:T(8,128)(2,1)S(1)}, bf16[512,128]{1,0:T(8,128)(2,1)S(1)}, u32[]{:S(2)}, u32[]{:S(2)}) collective-permute-start(bf16[512,128]{1,0:T(8,128)(2,1)S(1)} %get-tuple-element.38), channel_id=1, source_target_pairs={{0,9},{1,8},{2,11},{3,10},{4,13},{5,12},{6,15},{7,14},{8,1},{9,0},... | collective-permute-start | bytes 393224 | tf_op jit(solution)/shard_map/ppermute | solution.py:410
  22.9 17.2 %collective-permute-start.6 = (bf16[512,128]{1,0:T(8,128)(2,1)S(1)}, bf16[512,128]{1,0:T(8,128)(2,1)S(1)}, u32[]{:S(2)}, u32[]{:S(2)}) collective-permute-start(bf16[512,128]{1,0:T(8,128)(2,1)S(1)} %get-tuple-element.37.after_1.after_2), channel_id=1, source_target_pairs={{0,8},{1,9},{2,10},{3,11},{4,12},{5,13},{6,14},{7,15},{8,0},{9,1},... | collective-permute-start | bytes 393224 | tf_op jit(solution)/shard_map/ppermute | solution.py:410
  25.1 17.2 %collective-permute-start.11 = (bf16[512,128]{1,0:T(8,128)(2,1)S(1)}, bf16[512,128]{1,0:T(8,128)(2,1)S(1)}, u32[]{:S(2)}, u32[]{:S(2)}) collective-permute-start(bf16[512,128]{1,0:T(8,128)(2,1)S(1)} %get-tuple-element.44), channel_id=1, source_target_pairs={{0,1},{1,0},{2,3},{3,2},{4,5},{5,4},{6,7},{7,6},{8,9},{9,8},{10,11... | collective-permute-start | bytes 393224 | tf_op jit(solution)/shard_map/ppermute | solution.py:410
  28.6 16.3 %collective-permute-start.14 = (bf16[256,128]{1,0:T(8,128)(2,1)S(1)}, bf16[256,128]{1,0:T(8,128)(2,1)S(1)}, u32[]{:S(2)}, u32[]{:S(2)}) collective-permute-start(bf16[256,128]{1,0:T(8,128)(2,1)S(1)} %get-tuple-element.49), channel_id=1, source_target_pairs={{0,8},{1,9},{2,10},{3,11},{4,12},{5,13},{6,14},{7,15},{8,0},{9,1},... | collective-permute-start | bytes 196616 | tf_op jit(solution)/shard_map/ppermute | solution.py:410
  30.9 14.1 %collective-permute-start.15 = (bf16[256,128]{1,0:T(8,128)(2,1)S(1)}, bf16[256,128]{1,0:T(8,128)(2,1)S(1)}, u32[]{:S(2)}, u32[]{:S(2)}) collective-permute-start(bf16[256,128]{1,0:T(8,128)(2,1)S(1)} %get-tuple-element.50), channel_id=1, source_target_pairs={{0,9},{1,8},{2,11},{3,10},{4,13},{5,12},{6,15},{7,14},{8,1},{9,0},... | collective-permute-start | bytes 196616 | tf_op jit(solution)/shard_map/ppermute | solution.py:410
  40.0 3.1 %copy-start = (f32[256,256]{1,0:T(8,128)S(1)}, f32[256,256]{1,0:T(8,128)}, u32[]{:S(2)}) copy-start(f32[256,256]{1,0:T(8,128)} %constant.6.clone.inverse_ref) | copy-start | bytes 786436
  41.7 1.3 %collective-permute-start.12 = (bf16[128,128]{1,0:T(8,128)(2,1)S(1)}, bf16[128,128]{1,0:T(8,128)(2,1)S(1)}, u32[]{:S(2)}, u32[]{:S(2)}) collective-permute-start(bf16[128,128]{1,0:T(8,128)(2,1)S(1)} %get-tuple-element.45), channel_id=1, source_target_pairs={{0,1},{1,0},{2,3},{3,2},{4,5},{5,4},{6,7},{7,6},{8,9},{9,8},{10,11... | collective-permute-start | bytes 98312 | tf_op jit(solution)/shard_map/ppermute | solution.py:410
  41.9 1.2 %collective-permute-start.13 = (bf16[128,128]{1,0:T(8,128)(2,1)S(1)}, bf16[128,128]{1,0:T(8,128)(2,1)S(1)}, u32[]{:S(2)}, u32[]{:S(2)}) collective-permute-start(bf16[128,128]{1,0:T(8,128)(2,1)S(1)} %get-tuple-element.46), channel_id=1, source_target_pairs={{0,1},{1,0},{2,3},{3,2},{4,5},{5,4},{6,7},{7,6},{8,9},{9,8},{10,11... | collective-permute-start | bytes 98312 | tf_op jit(solution)/shard_map/ppermute | solution.py:410

commit v16 on v13

--- a/solution.py
+++ b/solution.py
@@ -118,9 +118,9 @@
     _, group = place_of(place_ref, groups)
     table = table_ref[...]
     part_rows, full_rows = COMPS * 2 * PART, COMPS * 2 * FULL
-    piece_refs[groups][2 * full_rows :] = jnp.concatenate(
-        [listing_of(own_pairs_ref, LANES), listing_of(near_pairs_ref, LANES)]
-    ).astype(jnp.bfloat16)
+    listed = jnp.concatenate([listing_of(own_pairs_ref, LANES), listing_of(near_pairs_ref, LANES)])
+    for m in (groups, groups + 1):
+        piece_refs[m][2 * full_rows :] = listed.astype(jnp.bfloat16)
     for mg in range(groups):
         spectra = station_spectra(windows_ref, group ^ mg, table)
         side, cross = piece_refs[mg], piece_refs[groups + mg]
@@ -302,7 +302,7 @@
     return (ref, 0, 2 * COMPS * 2 * FULL)
 
 
-def part_kernel(*refs):
+def part_kernel(after_ref, *refs):
     piece_refs, (flat_ref, trace_ref, cross_ref) = refs[:-3], refs[-3:]
     add_cross([side_part(ref) for ref in piece_refs], trace_ref, PART, cross_ref)
     turn_blocks(cross_ref, PART, flat_ref)
@@ -315,10 +315,14 @@
     pick(place_ref, counts_ref, listed[listing:], flat_ref, bins, 3, picked_1)
 
 
-def early_kernel(sides, after_0, after_1, *refs):
+def early_kernel(own_ref, *refs):
     piece_refs, (sums_ref, trace_ref) = refs[:-2], refs[-2:]
-    pieces = [side_full(ref) for ref in piece_refs[:sides]] + [cross_full(ref) for ref in piece_refs[sides:]]
-    add_cross(pieces, trace_ref, FULL, sums_ref)
+    add_cross([side_full(own_ref)] + [cross_full(ref) for ref in piece_refs], trace_ref, FULL, sums_ref)
+
+
+def side_kernel(after_0, after_1, before_ref, *refs):
+    piece_refs, (sums_ref, trace_ref) = refs[:-2], refs[-2:]
+    add_cross([side_full(ref) for ref in piece_refs], trace_ref, FULL, sums_ref, before_ref)
 
 
 def full_kernel(place_ref, counts_ref, listed_ref, after_0, after_2, before_ref, *refs):
@@ -441,7 +445,7 @@
     pieces = pl.pallas_call(
         near_spectra_kernel,
         out_shape=[shape(2 * (part_rows + full_rows), LANES)] * groups
-        + [shape(2 * full_rows + listing * (mg == 0), LANES) for mg in range(groups)],
+        + [shape(2 * full_rows + listing * (mg < 2), LANES) for mg in range(groups)],
         in_specs=[smem] + [vmem] * 6,
         out_specs=[vmem] * (2 * groups),
         compiler_params=params,
@@ -457,10 +461,22 @@
     half_packed = shape(packed_rows(count, FULL) // 2, LANES)
     part_blocks = shape(2, 2, SLOTS * SLOTS * width(PART) // LANES, 2 * LANES)
     full_blocks = shape(2, 2, SLOTS * SLOTS * width(FULL) // LANES, 2 * LANES)
+    sums = pl.pallas_call(
+        early_kernel,
+        out_shape=shape(2 * SLOTS * FULL, LANES, dtype=jnp.float32),
+        in_specs=[vmem] * (1 + len(early)),
+        out_specs=vmem,
+        scratch_shapes=[
+            pltpu.VMEM((padded((1 + len(early)) * 2 * comps) * 2 * FULL, LANES), jnp.float32)
+        ],
+        compiler_params=params,
+        cost_estimate=cost(0.7),
+        name="early",
+    )(sides[0], *early)
     part_flat = pl.pallas_call(
         part_kernel,
         out_shape=part_blocks,
-        in_specs=[vmem] * groups,
+        in_specs=[pl.BlockSpec(memory_space=pl.ANY)] + [vmem] * groups,
         out_specs=vmem,
         scratch_shapes=[
             pltpu.VMEM((padded(groups * 2 * comps) * 2 * PART, LANES), jnp.float32),
@@ -469,7 +485,7 @@
         compiler_params=params,
         cost_estimate=cost(0.001),
         name="part",
-    )(*sides)
+    )(sums, *sides)
     part_0, part_1 = pl.pallas_call(
         functools.partial(near_kernel, PART, 1),
         out_shape=[part_packed, part_packed],
@@ -490,17 +506,17 @@
     )(place, counts, far[0], part_flat, part_0)
     part_1 = swap(part_1, 1)
     sums = pl.pallas_call(
-        functools.partial(early_kernel, groups),
+        side_kernel,
         out_shape=shape(2 * SLOTS * FULL, LANES, dtype=jnp.float32),
-        in_specs=[pl.BlockSpec(memory_space=pl.ANY)] * 2 + [vmem] * (groups + len(early)),
+        in_specs=[pl.BlockSpec(memory_space=pl.ANY)] * 2 + [vmem] * groups,
         out_specs=vmem,
         scratch_shapes=[
-            pltpu.VMEM((padded((groups + len(early)) * 2 * comps) * 2 * FULL, LANES), jnp.float32)
+            pltpu.VMEM((padded((groups - 1) * 2 * comps) * 2 * FULL, LANES), jnp.float32)
         ],
         compiler_params=params,
         cost_estimate=cost(0.001),
-        name="early",
-    )(part_0, part_2, *sides, *early)
+        name="side",
+    )(part_0, part_2, sums, *sides[1:])
     sent, part_2, part_3 = part_2, swap(part_2, half), swap(part_3, half + 1)
     full_flat, full_2, full_3 = pl.pallas_call(
         full_kernel,

time: 41.9 us -> 45.5 us (1.086)
  starting transfers between devices: 21.7 us -> 24.9 us
    ppermute x16, starting transfers between devices: 21.7 us -> 24.9 us  [swap(): return lax.ppermute(x, 'cell', [(i, i ^ mask) for i in range(cells)])]
    pallas_call x2 -> x3, Pallas kernels: 1.71 us -> 2.09 us  [the longest x1 0.9 us: on_device(): pl.pallas_call(part_kernel, out_shape=part_blocks, in_specs=[pl.BlockSpec...]
  transfers between devices with their start and end apart: 16 -> 16, of which waited for: 6 -> 5; matrix products, arithmetic and copies ran while one was open for 0% -> 0% of each run, Pallas kernels for 30% -> 29%
where the time goes in v16:
time: 45.5 us; the launch traced here: 45.1 us
  starting transfers between devices  24.9 us (55%)
  Pallas kernels  15.1 us (33%)
  waiting for transfers between devices  3.82 us (8%)
  local copies, waits for them, and re-layouts  1.15 us (3%)
    ppermute x16, starting transfers between devices, swap(): return lax.ppermute(x, 'cell', [(i, i ^ mask) for i in range(cells)])  24.9 us
    ppermute x16, waiting for transfers between devices, swap(): return lax.ppermute(x, 'cell', [(i, i ^ mask) for i in range(cells)])  3.82 us
    pallas_call x1, Pallas kernels, on_device(): pl.pallas_call(full_kernel, out_shape=[full_blocks, full_packed, full_pac...  2.81 us
    pallas_call x1, Pallas kernels, on_device(): pl.pallas_call(functools.partial(near_kernel, FULL, 2), out_shape=[full_p...  1.99 us
    pallas_call x1, Pallas kernels, on_device(): pl.pallas_call(functools.partial(first_lags_kernel, groups), out_shape=[s...  1.77 us
    pallas_call x1, Pallas kernels, on_device(): pl.pallas_call(functools.partial(near_kernel, PART, 1), out_shape=[part_p...  1.69 us
    pallas_call x1, Pallas kernels, on_device(): pl.pallas_call(functools.partial(far_kernel, PART), out_shape=[part_packe...  1.68 us
    pallas_call x1, Pallas kernels, on_device(): pl.pallas_call(lag_kernel, out_shape=shape(2, count, samples, dtype=jnp.f...  1.39 us
  transfers between devices with their start and end apart: 16, of which 5 were waited for; matrix products, arithmetic and copies ran while one was open for 0% of the time, Pallas kernels for 29%

profile of v16, /device:TPU:0, one launch (start us, length us, event | category | flops | bytes accessed | tf_op | source)
XLA Modules:
  0.0 45.1 jit_solution(1239037363991464802)
XLA Ops:
  0.0 0.5 %collective-permute-start.1 = (bf16[3,2,4,64,256]{4,3,2,1,0:T(8,128)(2,1)}, bf16[3,2,4,64,256]{4,3,2,1,0:T(8,128)(2,1)S(1)}, u32[]{:S(2)}, u32[]{:S(2)}) collective-permute-start(bf16[3,2,4,64,256]{4,3,2,1,0:T(8,128)(2,1)} %bitcast.2), channel_id=1, source_target_pairs={{0,1},{1,0},{2,3},{3,2},{4,5},{5,4},{6,7},{7,6},{8,9},{9,8},{10,11... | collective-permute-start | bytes 2359304 | tf_op jit(solution)/shard_map/ppermute | solution.py:414
  0.5 0.1 collective-permute-start
  0.5 1.1 %copy-done.3 = bf16[3,1,512,256]{3,2,1,0:T(8,128)(2,1)S(1)} copy-done((bf16[3,1,512,256]{3,2,1,0:T(8,128)(2,1)S(1)}, bf16[3,1,512,256]{3,2,1,0:T(8,128)(2,1)}, u32[]{:S(2)}) %copy-start.3) | copy-done | bytes 786456
  1.6 0.8 %own_spectra.1 = (bf16[4,96,128]{2,1,0:T(8,128)(2,1)S(1)}, bf16[8,144,128]{2,1,0:T(8,128)(2,1)S(1)}, bf16[128,256]{1,0:T(8,128)(2,1)S(1)}) custom-call(s32[1]{0:T(128)} %bitcast.place_ref, bf16[3,2,4,64,256]{4,3,2,1,0:T(8,128)(2,1)S(1)} %bitcast.3), custom_call_target="tpu_custom_call" | custom-call | flops 1000000000 | bytes 1048576 | tf_op jit(solution)/shard_map/own_spectra/pallas_call | solution.py:431
  2.5 0.1 collective-permute-done.near_pairs_ref
  2.6 0.0 collective-permute-done.1.windows_ref
  2.6 0.0 copy-done.1
  2.6 0.8 %near_spectra.1 = (bf16[480,128]{1,0:T(8,128)(2,1)S(1)}, bf16[480,128]{1,0:T(8,128)(2,1)S(1)}, bf16[480,128]{1,0:T(8,128)(2,1)S(1)}, bf16[480,128]{1,0:T(8,128)(...) custom-call(s32[1]{0:T(128)} %bitcast.place_ref, ...), custom_call_target="tpu_custom_call" | custom-call | flops 1000000000 | bytes 1048576 | tf_op jit(solution)/shard_map/near_spectra/pallas_call | solution.py:445
  3.4 4.0 %collective-permute-start.2 = (bf16[320,128]{1,0:T(8,128)(2,1)S(1)}, bf16[320,128]{1,0:T(8,128)(2,1)S(1)}, u32[]{:S(2)}, u32[]{:S(2)}) collective-permute-start(bf16[320,128]{1,0:T(8,128)(2,1)S(1)} %get-tuple-element.32), channel_id=1, source_target_pairs={{0,8},{1,9},{2,10},{3,11},{4,12},{5,13},{6,14},{7,15},{8,0},{9,1},... | collective-permute-start | bytes 245768 | tf_op jit(solution)/shard_map/ppermute | solution.py:414
  7.5 1.3 %collective-permute-start.3 = (bf16[320,128]{1,0:T(8,128)(2,1)S(1)}, bf16[320,128]{1,0:T(8,128)(2,1)S(1)}, u32[]{:S(2)}, u32[]{:S(2)}) collective-permute-start(bf16[320,128]{1,0:T(8,128)(2,1)S(1)} %get-tuple-element.33), channel_id=1, source_target_pairs={{0,10},{1,11},{2,8},{3,9},{4,14},{5,15},{6,12},{7,13},{8,2},{9,3},... | collective-permute-start | bytes 245768 | tf_op jit(solution)/shard_map/ppermute | solution.py:414
  8.8 0.2 collective-permute-start.4
  9.0 1.8 %collective-permute-start.5 = (bf16[480,128]{1,0:T(8,128)(2,1)S(1)}, bf16[480,128]{1,0:T(8,128)(2,1)S(1)}, u32[]{:S(2)}, u32[]{:S(2)}) collective-permute-start(bf16[480,128]{1,0:T(8,128)(2,1)S(1)} %get-tuple-element.35), channel_id=1, source_target_pairs={{0,4},{1,5},{2,6},{3,7},{4,0},{5,1},{6,2},{7,3},{8,12},{9,13},{10,... | collective-permute-start | bytes 368648 | tf_op jit(solution)/shard_map/ppermute | solution.py:414
  10.8 1.4 %collective-permute-start.6 = (bf16[480,128]{1,0:T(8,128)(2,1)S(1)}, bf16[480,128]{1,0:T(8,128)(2,1)S(1)}, u32[]{:S(2)}, u32[]{:S(2)}) collective-permute-start(bf16[480,128]{1,0:T(8,128)(2,1)S(1)} %get-tuple-element.36), channel_id=1, source_target_pairs={{0,6},{1,7},{2,4},{3,5},{4,2},{5,3},{6,0},{7,1},{8,14},{9,15},{10,... | collective-permute-start | bytes 368648 | tf_op jit(solution)/shard_map/ppermute | solution.py:414
  12.2 0.0 collective-permute-done.2.refs_0_.listed_ref
  12.3 5.2 %collective-permute-start.9 = (bf16[288,128]{1,0:T(8,128)(2,1)S(1)}, bf16[288,128]{1,0:T(8,128)(2,1)S(1)}, u32[]{:S(2)}, u32[]{:S(2)}) collective-permute-start(bf16[288,128]{1,0:T(8,128)(2,1)S(1)} %get-tuple-element.40), channel_id=1, source_target_pairs={{0,12},{1,13},{2,14},{3,15},{4,8},{5,9},{6,10},{7,11},{8,4},{9,5},... | collective-permute-start | bytes 221192 | tf_op jit(solution)/shard_map/ppermute | solution.py:414
  17.4 0.0 collective-permute-done.3.refs_1_
  17.4 2.6 %collective-permute-start.10 = (bf16[288,128]{1,0:T(8,128)(2,1)S(1)}, bf16[288,128]{1,0:T(8,128)(2,1)S(1)}, u32[]{:S(2)}, u32[]{:S(2)}) collective-permute-start(bf16[288,128]{1,0:T(8,128)(2,1)S(1)} %get-tuple-element.41), channel_id=1, source_target_pairs={{0,14},{1,15},{2,12},{3,13},{4,10},{5,11},{6,8},{7,9},{8,6},{9,7},... | collective-permute-start | bytes 221192 | tf_op jit(solution)/shard_map/ppermute | solution.py:414
  20.0 0.6 %early.1.after_ref.before_ref = f32[1536,128]{1,0:T(8,128)S(1)} custom-call(bf16[480,128]{1,0:T(8,128)(2,1)S(1)} %get-tuple-element.31.own_ref.refs_0_, bf16[320,128]{1,0:T(8,128)(2,1)S(1)} %collective-permute-done.2.refs_0_.listed_ref, bf16[320,128]{1,0:T(8,128)(2,1)S(1)} %collective-permute-done.3.refs_1_), custom_call_target="tpu_custom_call" | custom-call | flops 700000000 | bytes 1048576 | tf_op jit(solution)/shard_map/early/pallas_call | solution.py:464
  20.6 0.0 copy-start.2
  20.6 0.0 collective-permute-done.4.refs_1_.refs_0_
  20.6 0.0 collective-permute-done.5.refs_2_.refs_1_
  20.6 0.0 collective-permute-done.6.refs_3_.refs_2_
  20.7 0.9 %part.1.flat_ref = bf16[2,2,128,256]{3,2,1,0:T(8,128)(2,1)S(1)} custom-call(f32[1536,128]{1,0:T(8,128)S(1)} %early.1.after_ref.before_ref, bf16[480,128]{1,0:T(8,128)(2,1)S(1)} %get-tuple-element.31.own_ref.refs_0_, bf16[480,128]{1,0:T(8,128)(2,1)S(1)} %collective-permute-done.4.refs_1_.refs_0_, bf16[480,128]{1,0:T(8,128)(2,1)S(1)} %collective-permute-done.5.refs_2_.refs_1_, ...), custom_call_target="tpu_custom_call" | custom-call | flops 1000000 | bytes 1048576 | tf_op jit(solution)/shard_map/part/pallas_call | solution.py:476
  21.6 0.0 copy-done.2
  21.6 1.7 %part_near.1 = (bf16[256,128]{1,0:T(8,128)(2,1)S(1)}, bf16[256,128]{1,0:T(8,128)(2,1)S(1)}) custom-call(s32[1]{0:T(128)} %bitcast.place_ref, s32[16]{0:T(128)S(1)} %copy-done.2, s32[2,2,512]{2,1,0:T(2,128)S(1)} %copy-done.1, s32[2,2,512]{2,1,0:T(2,128)S(1)} %collective-permute-done.near_pairs_ref, bf16[2,2,128,256]{3,2,1,0:T(8,128)(2,1)S(1)} %part.1.flat_ref), custom_call_target="tpu_custom_call" | custom-call | flops 1000000 | bytes 1048576 | tf_op jit(solution)/shard_map/part_near/pallas_call | solution.py:489
  23.3 1.7 %part_far.1 = (bf16[256,128]{1,0:T(8,128)(2,1)S(1)}, bf16[256,128]{1,0:T(8,128)(2,1)S(1)}) custom-call(s32[1]{0:T(128)} %bitcast.place_ref, s32[16]{0:T(128)S(1)} %copy-done.2, bf16[320,128]{1,0:T(8,128)(2,1)S(1)} %collective-permute-done.2.refs_0_.listed_ref, bf16[2,2,128,256]{3,2,1,0:T(8,128)(2,1)S(1)} %part.1.flat_ref, ...), custom_call_target="tpu_custom_call" | custom-call | flops 1000000000 | bytes 1048576 | tf_op jit(solution)/shard_map/part_far/pallas_call | solution.py:498
  25.0 1.0 %collective-permute-start.8 = (bf16[256,128]{1,0:T(8,128)(2,1)S(1)}, bf16[256,128]{1,0:T(8,128)(2,1)S(1)}, u32[]{:S(2)}, u32[]{:S(2)}) collective-permute-start(bf16[256,128]{1,0:T(8,128)(2,1)S(1)} %get-tuple-element.39), channel_id=1, source_target_pairs={{0,9},{1,8},{2,11},{3,10},{4,13},{5,12},{6,15},{7,14},{8,1},{9,0},... | collective-permute-start | bytes 196616 | tf_op jit(solution)/shard_map/ppermute | solution.py:414
  26.0 3.1 %collective-permute-start.7 = (bf16[256,128]{1,0:T(8,128)(2,1)S(1)}, bf16[256,128]{1,0:T(8,128)(2,1)S(1)}, u32[]{:S(2)}, u32[]{:S(2)}) collective-permute-start(bf16[256,128]{1,0:T(8,128)(2,1)S(1)} %get-tuple-element.38.after_1.after_2), channel_id=1, source_target_pairs={{0,8},{1,9},{2,10},{3,11},{4,12},{5,13},{6,14},{7,15},{8,0},{9,1},... | collective-permute-start | bytes 196616 | tf_op jit(solution)/shard_map/ppermute | solution.py:414
  29.1 0.6 %side.1.before_ref = f32[1536,128]{1,0:T(8,128)S(1)} custom-call(bf16[256,128]{1,0:T(8,128)(2,1)S(1)} %get-tuple-element.37.after_ref.after_0.refs_0_, bf16[256,128]{1,0:T(8,128)(2,1)S(1)} %get-tuple-element.38.after_1.after_2, f32[1536,128]{1,0:T(8,128)S(1)} %early.1.after_ref.before_ref, bf16[480,128]{1,0:T(8,128)(2,1)S(1)} %collective-permute-done.4.refs_1_.refs_0_, ...), custom_call_target="tpu_custom_call" | custom-call | flops 1000000 | bytes 1048576 | tf_op jit(solution)/shard_map/side/pallas_call | solution.py:508
  29.7 0.0 collective-permute-done.9.refs_0_
  29.7 0.0 collective-permute-done.10.refs_1_
  29.7 2.8 %full.1 = (bf16[2,2,256,256]{3,2,1,0:T(8,128)(2,1)S(1)}, bf16[384,128]{1,0:T(8,128)(2,1)S(1)}, bf16[384,128]{1,0:T(8,128)(2,1)S(1)}) custom-call(s32[1]{0:T(128)} %bitcast.place_ref, s32[16]{0:T(128)S(1)} %copy-done.2, bf16[320,128]{1,0:T(8,128)(2,1)S(1)} %collective-permute-done.2.refs_0_.listed_ref, ...), custom_call_target="tpu_custom_call" | custom-call | flops 10000000000 | bytes 1048576 | tf_op jit(solution)/shard_map/full/pallas_call | solution.py:521
  32.6 0.1 collective-permute-start.14
  32.6 2.3 %collective-permute-start.15 = (bf16[384,128]{1,0:T(8,128)(2,1)S(1)}, bf16[384,128]{1,0:T(8,128)(2,1)S(1)}, u32[]{:S(2)}, u32[]{:S(2)}) collective-permute-start(bf16[384,128]{1,0:T(8,128)(2,1)S(1)} %get-tuple-element.50), channel_id=1, source_target_pairs={{0,9},{1,8},{2,11},{3,10},{4,13},{5,12},{6,15},{7,14},{8,1},{9,0},... | collective-permute-start | bytes 294920 | tf_op jit(solution)/shard_map/ppermute | solution.py:414
  35.0 0.7 %collective-permute-start.11 = (bf16[256,128]{1,0:T(8,128)(2,1)S(1)}, bf16[256,128]{1,0:T(8,128)(2,1)S(1)}, u32[]{:S(2)}, u32[]{:S(2)}) collective-permute-start(bf16[256,128]{1,0:T(8,128)(2,1)S(1)} %get-tuple-element.44), channel_id=1, source_target_pairs={{0,1},{1,0},{2,3},{3,2},{4,5},{5,4},{6,7},{7,6},{8,9},{9,8},{10,11... | collective-permute-start | bytes 196616 | tf_op jit(solution)/shard_map/ppermute | solution.py:414
  35.7 0.0 collective-permute-done.8.refs_1_.refs_2_
  35.7 0.0 collective-permute-done.7.refs_0_.refs_1_
  35.7 2.0 %full_near.1 = (bf16[384,128]{1,0:T(8,128)(2,1)S(1)}, bf16[192,128]{1,0:T(8,128)(2,1)S(1)}, bf16[192,128]{1,0:T(8,128)(2,1)S(1)}) custom-call(s32[1]{0:T(128)} %bitcast.place_ref, s32[16]{0:T(128)S(1)} %copy-done.2, s32[2,2,512]{2,1,0:T(2,128)S(1)} %copy-done.1, s32[2,2,512]{2,1,0:T(2,128)S(1)} %collective-permute-done.near_pairs_ref, ...), custom_call_target="tpu_custom_call" | custom-call | flops 500000000 | bytes 1048576 | tf_op jit(solution)/shard_map/full_near/pallas_call | solution.py:535
  37.7 0.1 collective-permute-start.12
  37.7 0.5 %collective-permute-start.13 = (bf16[192,128]{1,0:T(8,128)(2,1)S(1)}, bf16[192,128]{1,0:T(8,128)(2,1)S(1)}, u32[]{:S(2)}, u32[]{:S(2)}) collective-permute-start(bf16[192,128]{1,0:T(8,128)(2,1)S(1)} %get-tuple-element.46), channel_id=1, source_target_pairs={{0,1},{1,0},{2,3},{3,2},{4,5},{5,4},{6,7},{7,6},{8,9},{9,8},{10,11... | collective-permute-start | bytes 147464 | tf_op jit(solution)/shard_map/ppermute | solution.py:414
  38.2 0.0 collective-permute-done.11.refs_4_
  38.2 0.7 %collective-permute-done.12.refs_5_ = bf16[192,128]{1,0:T(8,128)(2,1)S(1)} collective-permute-done((bf16[192,128]{1,0:T(8,128)(2,1)S(1)}, bf16[192,128]{1,0:T(8,128)(2,1)S(1)}, u32[]{:S(2)}, u32[]{:S(2)}) %collective-permute-start.12) | collective-permute-done | bytes 49184 | tf_op jit(solution)/shard_map/ppermute | solution.py:414
  39.0 0.2 collective-permute-done.13.refs_6_
  39.1 0.0 copy-done
  39.1 1.8 %first_lags.1 = (f32[2,512,256]{2,1,0:T(8,128)S(1)}, bf16[2,96,512]{2,1,0:T(8,128)(2,1)S(1)}) custom-call(s32[1]{0:T(128)} %bitcast.place_ref, f32[256,256]{1,0:T(8,128)S(1)} %copy-done, bf16[256,128]{1,0:T(8,128)(2,1)S(1)} %get-tuple-element.37.after_ref.after_0.refs_0_, bf16[256,128]{1,0:T(8,128)(2,1)S(1)} %collective-permute-done.7.refs_0_.refs_1_, ...), custom_call_target="tpu_custom_call" | custom-call | flops 1000000 | bytes 1048576 | tf_op jit(solution)/shard_map/first_lags/pallas_call | solution.py:546
  40.9 2.5 %collective-permute-done.14.refs_0_ = bf16[384,128]{1,0:T(8,128)(2,1)S(1)} collective-permute-done((bf16[384,128]{1,0:T(8,128)(2,1)S(1)}, bf16[384,128]{1,0:T(8,128)(2,1)S(1)}, u32[]{:S(2)}, u32[]{:S(2)}) %collective-permute-start.14) | collective-permute-done | bytes 98336 | tf_op jit(solution)/shard_map/ppermute | solution.py:414
  43.4 0.3 collective-permute-done.15.refs_1_
  43.7 1.4 %lags.1 = f32[2,512,256]{2,1,0:T(8,128)} custom-call(f32[2,512,256]{2,1,0:T(8,128)S(1)} %get-tuple-element.47.first_ref, bf16[2,96,512]{2,1,0:T(8,128)(2,1)S(1)} %get-tuple-element.48.table_ref, bf16[384,128]{1,0:T(8,128)(2,1)S(1)} %collective-permute-done.14.refs_0_, bf16[384,128]{1,0:T(8,128)(2,1)S(1)} %collective-permute-done.15.refs_1_), custom_call_target="tpu_custom_call" | custom-call | flops 1000000000 | bytes 1048576 | tf_op jit(solution)/shard_map/lags/pallas_call | solution.py:558
  (3 shorter events, 0.0 us)
Async XLA Ops:
  0.0 2.6 %collective-permute-start.1 = (bf16[3,2,4,64,256]{4,3,2,1,0:T(8,128)(2,1)}, bf16[3,2,4,64,256]{4,3,2,1,0:T(8,128)(2,1)S(1)}, u32[]{:S(2)}, u32[]{:S(2)}) collective-permute-start(bf16[3,2,4,64,256]{4,3,2,1,0:T(8,128)(2,1)} %bitcast.2), channel_id=1, source_target_pairs={{0,1},{1,0},{2,3},{3,2},{4,5},{5,4},{6,7},{7,6},{8,9},{9,8},{10,11... | collective-permute-start | bytes 2359304 | tf_op jit(solution)/shard_map/ppermute | solution.py:414
  0.5 2.1 %collective-permute-start = (s32[2,2,512]{2,1,0:T(2,128)}, s32[2,2,512]{2,1,0:T(2,128)S(1)}, u32[]{:S(2)}, u32[]{:S(2)}) collective-permute-start(s32[2,2,512]{2,1,0:T(2,128)} %own_pairs_ref.5), channel_id=1, source_target_pairs={{0,1},{1,0},{2,3},{3,2},{4,5},{5,4},{6,7},{7,6},{8,9},{9,8},{10,11... | collective-permute-start | bytes 24584 | tf_op jit(solution)/shard_map/ppermute | solution.py:414
  0.5 1.1 %copy-start.3 = (bf16[3,1,512,256]{3,2,1,0:T(8,128)(2,1)S(1)}, bf16[3,1,512,256]{3,2,1,0:T(8,128)(2,1)}, u32[]{:S(2)}) copy-start(bf16[3,1,512,256]{3,2,1,0:T(8,128)(2,1)} %param.4) | copy-start | bytes 2359300
  1.6 0.9 %copy-start.1 = (s32[2,2,512]{2,1,0:T(2,128)S(1)}, s32[2,2,512]{2,1,0:T(2,128)}, u32[]{:S(2)}) copy-start(s32[2,2,512]{2,1,0:T(2,128)} %own_pairs_ref.5) | copy-start | bytes 24580
  3.4 8.8 %collective-permute-start.2 = (bf16[320,128]{1,0:T(8,128)(2,1)S(1)}, bf16[320,128]{1,0:T(8,128)(2,1)S(1)}, u32[]{:S(2)}, u32[]{:S(2)}) collective-permute-start(bf16[320,128]{1,0:T(8,128)(2,1)S(1)} %get-tuple-element.32), channel_id=1, source_target_pairs={{0,8},{1,9},{2,10},{3,11},{4,12},{5,13},{6,14},{7,15},{8,0},{9,1},... | collective-permute-start | bytes 245768 | tf_op jit(solution)/shard_map/ppermute | solution.py:414
  7.5 10.0 %collective-permute-start.3 = (bf16[320,128]{1,0:T(8,128)(2,1)S(1)}, bf16[320,128]{1,0:T(8,128)(2,1)S(1)}, u32[]{:S(2)}, u32[]{:S(2)}) collective-permute-start(bf16[320,128]{1,0:T(8,128)(2,1)S(1)} %get-tuple-element.33), channel_id=1, source_target_pairs={{0,10},{1,11},{2,8},{3,9},{4,14},{5,15},{6,12},{7,13},{8,2},{9,3},... | collective-permute-start | bytes 245768 | tf_op jit(solution)/shard_map/ppermute | solution.py:414
  8.8 11.9 %collective-permute-start.4 = (bf16[480,128]{1,0:T(8,128)(2,1)S(1)}, bf16[480,128]{1,0:T(8,128)(2,1)S(1)}, u32[]{:S(2)}, u32[]{:S(2)}) collective-permute-start(bf16[480,128]{1,0:T(8,128)(2,1)S(1)} %get-tuple-element.34), channel_id=1, source_target_pairs={{0,2},{1,3},{2,0},{3,1},{4,6},{5,7},{6,4},{7,5},{8,10},{9,11},{10,... | collective-permute-start | bytes 368648 | tf_op jit(solution)/shard_map/ppermute | solution.py:414
  9.0 11.6 %collective-permute-start.5 = (bf16[480,128]{1,0:T(8,128)(2,1)S(1)}, bf16[480,128]{1,0:T(8,128)(2,1)S(1)}, u32[]{:S(2)}, u32[]{:S(2)}) collective-permute-start(bf16[480,128]{1,0:T(8,128)(2,1)S(1)} %get-tuple-element.35), channel_id=1, source_target_pairs={{0,4},{1,5},{2,6},{3,7},{4,0},{5,1},{6,2},{7,3},{8,12},{9,13},{10,... | collective-permute-start | bytes 368648 | tf_op jit(solution)/shard_map/ppermute | solution.py:414
  10.8 9.8 %collective-permute-start.6 = (bf16[480,128]{1,0:T(8,128)(2,1)S(1)}, bf16[480,128]{1,0:T(8,128)(2,1)S(1)}, u32[]{:S(2)}, u32[]{:S(2)}) collective-permute-start(bf16[480,128]{1,0:T(8,128)(2,1)S(1)} %get-tuple-element.36), channel_id=1, source_target_pairs={{0,6},{1,7},{2,4},{3,5},{4,2},{5,3},{6,0},{7,1},{8,14},{9,15},{10,... | collective-permute-start | bytes 368648 | tf_op jit(solution)/shard_map/ppermute | solution.py:414
  12.3 17.5 %collective-permute-start.9 = (bf16[288,128]{1,0:T(8,128)(2,1)S(1)}, bf16[288,128]{1,0:T(8,128)(2,1)S(1)}, u32[]{:S(2)}, u32[]{:S(2)}) collective-permute-start(bf16[288,128]{1,0:T(8,128)(2,1)S(1)} %get-tuple-element.40), channel_id=1, source_target_pairs={{0,12},{1,13},{2,14},{3,15},{4,8},{5,9},{6,10},{7,11},{8,4},{9,5},... | collective-permute-start | bytes 221192 | tf_op jit(solution)/shard_map/ppermute | solution.py:414
  17.4 12.3 %collective-permute-start.10 = (bf16[288,128]{1,0:T(8,128)(2,1)S(1)}, bf16[288,128]{1,0:T(8,128)(2,1)S(1)}, u32[]{:S(2)}, u32[]{:S(2)}) collective-permute-start(bf16[288,128]{1,0:T(8,128)(2,1)S(1)} %get-tuple-element.41), channel_id=1, source_target_pairs={{0,14},{1,15},{2,12},{3,13},{4,10},{5,11},{6,8},{7,9},{8,6},{9,7},... | collective-permute-start | bytes 221192 | tf_op jit(solution)/shard_map/ppermute | solution.py:414
  20.6 1.0 %copy-start.2 = (s32[16]{0:T(128)S(1)}, s32[16]{0:T(128)}, u32[]{:S(2)}) copy-start(s32[16]{0:T(128)} %counts_ref.7) | copy-start | bytes 196
  25.0 10.7 %collective-permute-start.8 = (bf16[256,128]{1,0:T(8,128)(2,1)S(1)}, bf16[256,128]{1,0:T(8,128)(2,1)S(1)}, u32[]{:S(2)}, u32[]{:S(2)}) collective-permute-start(bf16[256,128]{1,0:T(8,128)(2,1)S(1)} %get-tuple-element.39), channel_id=1, source_target_pairs={{0,9},{1,8},{2,11},{3,10},{4,13},{5,12},{6,15},{7,14},{8,1},{9,0},... | collective-permute-start | bytes 196616 | tf_op jit(solution)/shard_map/ppermute | solution.py:414
  26.0 9.7 %collective-permute-start.7 = (bf16[256,128]{1,0:T(8,128)(2,1)S(1)}, bf16[256,128]{1,0:T(8,128)(2,1)S(1)}, u32[]{:S(2)}, u32[]{:S(2)}) collective-permute-start(bf16[256,128]{1,0:T(8,128)(2,1)S(1)} %get-tuple-element.38.after_1.after_2), channel_id=1, source_target_pairs={{0,8},{1,9},{2,10},{3,11},{4,12},{5,13},{6,14},{7,15},{8,0},{9,1},... | collective-permute-start | bytes 196616 | tf_op jit(solution)/shard_map/ppermute | solution.py:414
  32.6 10.8 %collective-permute-start.14 = (bf16[384,128]{1,0:T(8,128)(2,1)S(1)}, bf16[384,128]{1,0:T(8,128)(2,1)S(1)}, u32[]{:S(2)}, u32[]{:S(2)}) collective-permute-start(bf16[384,128]{1,0:T(8,128)(2,1)S(1)} %get-tuple-element.49), channel_id=1, source_target_pairs={{0,8},{1,9},{2,10},{3,11},{4,12},{5,13},{6,14},{7,15},{8,0},{9,1},... | collective-permute-start | bytes 294920 | tf_op jit(solution)/shard_map/ppermute | solution.py:414
  32.6 11.1 %collective-permute-start.15 = (bf16[384,128]{1,0:T(8,128)(2,1)S(1)}, bf16[384,128]{1,0:T(8,128)(2,1)S(1)}, u32[]{:S(2)}, u32[]{:S(2)}) collective-permute-start(bf16[384,128]{1,0:T(8,128)(2,1)S(1)} %get-tuple-element.50), channel_id=1, source_target_pairs={{0,9},{1,8},{2,11},{3,10},{4,13},{5,12},{6,15},{7,14},{8,1},{9,0},... | collective-permute-start | bytes 294920 | tf_op jit(solution)/shard_map/ppermute | solution.py:414
  35.0 3.3 %collective-permute-start.11 = (bf16[256,128]{1,0:T(8,128)(2,1)S(1)}, bf16[256,128]{1,0:T(8,128)(2,1)S(1)}, u32[]{:S(2)}, u32[]{:S(2)}) collective-permute-start(bf16[256,128]{1,0:T(8,128)(2,1)S(1)} %get-tuple-element.44), channel_id=1, source_target_pairs={{0,1},{1,0},{2,3},{3,2},{4,5},{5,4},{6,7},{7,6},{8,9},{9,8},{10,11... | collective-permute-start | bytes 196616 | tf_op jit(solution)/shard_map/ppermute | solution.py:414
  35.7 3.5 %copy-start = (f32[256,256]{1,0:T(8,128)S(1)}, f32[256,256]{1,0:T(8,128)}, u32[]{:S(2)}) copy-start(f32[256,256]{1,0:T(8,128)} %constant.6.clone.inverse_ref) | copy-start | bytes 786436
  37.7 1.3 %collective-permute-start.12 = (bf16[192,128]{1,0:T(8,128)(2,1)S(1)}, bf16[192,128]{1,0:T(8,128)(2,1)S(1)}, u32[]{:S(2)}, u32[]{:S(2)}) collective-permute-start(bf16[192,128]{1,0:T(8,128)(2,1)S(1)} %get-tuple-element.45), channel_id=1, source_target_pairs={{0,1},{1,0},{2,3},{3,2},{4,5},{5,4},{6,7},{7,6},{8,9},{9,8},{10,11... | collective-permute-start | bytes 147464 | tf_op jit(solution)/shard_map/ppermute | solution.py:414
  37.7 1.4 %collective-permute-start.13 = (bf16[192,128]{1,0:T(8,128)(2,1)S(1)}, bf16[192,128]{1,0:T(8,128)(2,1)S(1)}, u32[]{:S(2)}, u32[]{:S(2)}) collective-permute-start(bf16[192,128]{1,0:T(8,128)(2,1)S(1)} %get-tuple-element.46), channel_id=1, source_target_pairs={{0,1},{1,0},{2,3},{3,2},{4,5},{5,4},{6,7},{7,6},{8,9},{9,8},{10,11... | collective-permute-start | bytes 147464 | tf_op jit(solution)/shard_map/ppermute | solution.py:414

commit v17 on v13

--- a/solution.py
+++ b/solution.py
@@ -281,7 +281,7 @@
             for i in range(runs):
                 block.append(cross_ref[pl.ds(own * SLOTS + at * runs + i, bins, stride=slots), :])
                 block += [empty] * (bins < width(bins))
-            block = jnp.concatenate(block).T.astype(jnp.bfloat16)
+            block = jnp.concatenate(block).astype(jnp.bfloat16).T
             for part in range(2):
                 for far in range(2):
                     start = (part * 2 + far) * SLOTS
@@ -387,15 +387,27 @@
 
 
 def lag_kernel(first_ref, table_ref, *refs):
-    picked_refs, lags_ref = refs[:-1], refs[-1]
+    picked_refs, (lags_ref, held_ref, sems) = refs[:-3], refs[-3:]
     samples = lags_ref.shape[2]
-    more = 0.0
-    for at, ref in enumerate(picked_refs):
-        more += jnp.dot(unpack(ref[...], FULL), table_ref[at], preferred_element_type=jnp.float32)
-    for step_round in range(2):
-        lags_ref[step_round] = (
-            first_ref[step_round] + more[:, step_round * samples : (step_round + 1) * samples]
+    runs = sems.shape[0]
+    held = held_ref.shape[1] // runs
+    picked = [unpack(ref[...], FULL) for ref in picked_refs]
+    copies = []
+    for run in range(runs):
+        rows = slice(run * held, (run + 1) * held)
+        more = 0.0
+        for at, values in enumerate(picked):
+            more += jnp.dot(values[rows], table_ref[at], preferred_element_type=jnp.float32)
+        for step_round in range(2):
+            held_ref[step_round, rows] = (
+                first_ref[step_round, rows] + more[:, step_round * samples : (step_round + 1) * samples]
+            )
+        copies.append(
+            pltpu.make_async_copy(held_ref.at[:, rows], lags_ref.at[:, rows], sems.at[run])
         )
+        copies[-1].start()
+    for copy in copies:
+        copy.wait()
 
 
 def on_device(windows, counts, pairs):
@@ -543,7 +555,11 @@
         lag_kernel,
         out_shape=shape(2, count, samples, dtype=jnp.float32),
         in_specs=[vmem] * 4,
-        out_specs=vmem,
+        out_specs=pl.BlockSpec(memory_space=pl.ANY),
+        scratch_shapes=[
+            pltpu.VMEM((2, count, samples), jnp.float32),
+            pltpu.SemaphoreType.DMA((4,)),
+        ],
         compiler_params=params,
         cost_estimate=cost(1),
         name="lags",

time: 41.9 us -> 41.8 us (level)
  no operation moved by 1% of the time
where the time goes in v17:
time: 41.8 us; the launch traced here: 41.3 us
  starting transfers between devices  21.8 us (52%)
  Pallas kernels  14.5 us (35%)
  waiting for transfers between devices  3.75 us (9%)
  local copies, waits for them, and re-layouts  1.14 us (3%)
    ppermute x16, starting transfers between devices, swap(): return lax.ppermute(x, 'cell', [(i, i ^ mask) for i in range(cells)])  21.8 us
    ppermute x16, waiting for transfers between devices, swap(): return lax.ppermute(x, 'cell', [(i, i ^ mask) for i in range(cells)])  3.75 us
    pallas_call x1, Pallas kernels, on_device(): pl.pallas_call(full_kernel, out_shape=[full_blocks, full_packed, full_pac...  2.81 us
    pallas_call x1, Pallas kernels, on_device(): pl.pallas_call(functools.partial(near_kernel, FULL, 2), out_shape=[full_p...  2 us
    pallas_call x1, Pallas kernels, on_device(): pl.pallas_call(functools.partial(first_lags_kernel, groups), out_shape=[s...  1.78 us
    pallas_call x1, Pallas kernels, on_device(): pl.pallas_call(functools.partial(near_kernel, PART, 1), out_shape=[part_p...  1.68 us
    pallas_call x1, Pallas kernels, on_device(): pl.pallas_call(functools.partial(far_kernel, PART), out_shape=[part_packe...  1.68 us
    pallas_call x1, Pallas kernels, on_device(): pl.pallas_call(lag_kernel, out_shape=shape(2, count, samples, dtype=jnp.f...  1.22 us
  transfers between devices with their start and end apart: 16, of which 6 were waited for; matrix products, arithmetic and copies ran while one was open for 0% of the time, Pallas kernels for 30%

profile of v17, /device:TPU:0, one launch (start us, length us, event | category | flops | bytes accessed | tf_op | source)
XLA Modules:
  0.0 41.3 jit_solution(11249826708975597538)
XLA Ops:
  0.0 0.5 %collective-permute-start.1 = (bf16[3,2,4,64,256]{4,3,2,1,0:T(8,128)(2,1)}, bf16[3,2,4,64,256]{4,3,2,1,0:T(8,128)(2,1)S(1)}, u32[]{:S(2)}, u32[]{:S(2)}) collective-permute-start(bf16[3,2,4,64,256]{4,3,2,1,0:T(8,128)(2,1)} %bitcast.2), channel_id=1, source_target_pairs={{0,1},{1,0},{2,3},{3,2},{4,5},{5,4},{6,7},{7,6},{8,9},{9,8},{10,11... | collective-permute-start | bytes 2359304 | tf_op jit(solution)/shard_map/ppermute | solution.py:422
  0.5 0.1 collective-permute-start
  0.5 0.0 copy-start.3
  0.5 1.1 %copy-done.3 = bf16[3,1,512,256]{3,2,1,0:T(8,128)(2,1)S(1)} copy-done((bf16[3,1,512,256]{3,2,1,0:T(8,128)(2,1)S(1)}, bf16[3,1,512,256]{3,2,1,0:T(8,128)(2,1)}, u32[]{:S(2)}) %copy-start.3) | copy-done | bytes 786456
  1.6 0.0 copy-start.1
  1.6 0.8 %own_spectra.1 = (bf16[4,96,128]{2,1,0:T(8,128)(2,1)S(1)}, bf16[8,144,128]{2,1,0:T(8,128)(2,1)S(1)}, bf16[128,256]{1,0:T(8,128)(2,1)S(1)}) custom-call(s32[1]{0:T(128)} %bitcast.place_ref, bf16[3,2,4,64,256]{4,3,2,1,0:T(8,128)(2,1)S(1)} %bitcast.3), custom_call_target="tpu_custom_call" | custom-call | flops 1000000000 | bytes 1048576 | tf_op jit(solution)/shard_map/own_spectra/pallas_call | solution.py:439
  2.5 0.1 collective-permute-done.near_pairs_ref
  2.6 0.0 collective-permute-done.1.windows_ref
  2.6 0.0 copy-done.1
  2.6 0.8 %near_spectra.1 = (bf16[480,128]{1,0:T(8,128)(2,1)S(1)}, bf16[480,128]{1,0:T(8,128)(2,1)S(1)}, bf16[480,128]{1,0:T(8,128)(2,1)S(1)}, bf16[480,128]{1,0:T(8,128)(...) custom-call(s32[1]{0:T(128)} %bitcast.place_ref, ...), custom_call_target="tpu_custom_call" | custom-call | flops 1000000000 | bytes 1048576 | tf_op jit(solution)/shard_map/near_spectra/pallas_call | solution.py:453
  3.4 3.0 %collective-permute-start.2 = (bf16[480,128]{1,0:T(8,128)(2,1)S(1)}, bf16[480,128]{1,0:T(8,128)(2,1)S(1)}, u32[]{:S(2)}, u32[]{:S(2)}) collective-permute-start(bf16[480,128]{1,0:T(8,128)(2,1)S(1)} %get-tuple-element.32), channel_id=1, source_target_pairs={{0,2},{1,3},{2,0},{3,1},{4,6},{5,7},{6,4},{7,5},{8,10},{9,11},{10,... | collective-permute-start | bytes 368648 | tf_op jit(solution)/shard_map/ppermute | solution.py:422
  6.4 1.6 %collective-permute-start.3 = (bf16[480,128]{1,0:T(8,128)(2,1)S(1)}, bf16[480,128]{1,0:T(8,128)(2,1)S(1)}, u32[]{:S(2)}, u32[]{:S(2)}) collective-permute-start(bf16[480,128]{1,0:T(8,128)(2,1)S(1)} %get-tuple-element.33), channel_id=1, source_target_pairs={{0,4},{1,5},{2,6},{3,7},{4,0},{5,1},{6,2},{7,3},{8,12},{9,13},{10,... | collective-permute-start | bytes 368648 | tf_op jit(solution)/shard_map/ppermute | solution.py:422
  8.0 0.0 collective-permute-start.4
  8.0 3.0 %collective-permute-start.5 = (bf16[320,128]{1,0:T(8,128)(2,1)S(1)}, bf16[320,128]{1,0:T(8,128)(2,1)S(1)}, u32[]{:S(2)}, u32[]{:S(2)}) collective-permute-start(bf16[320,128]{1,0:T(8,128)(2,1)S(1)} %get-tuple-element.36), channel_id=1, source_target_pairs={{0,8},{1,9},{2,10},{3,11},{4,12},{5,13},{6,14},{7,15},{8,0},{9,1},... | collective-permute-start | bytes 245768 | tf_op jit(solution)/shard_map/ppermute | solution.py:422
  11.0 1.3 %collective-permute-start.8 = (bf16[288,128]{1,0:T(8,128)(2,1)S(1)}, bf16[288,128]{1,0:T(8,128)(2,1)S(1)}, u32[]{:S(2)}, u32[]{:S(2)}) collective-permute-start(bf16[288,128]{1,0:T(8,128)(2,1)S(1)} %get-tuple-element.39), channel_id=1, source_target_pairs={{0,10},{1,11},{2,8},{3,9},{4,14},{5,15},{6,12},{7,13},{8,2},{9,3},... | collective-permute-start | bytes 221192 | tf_op jit(solution)/shard_map/ppermute | solution.py:422
  12.3 0.0 collective-permute-done.2.refs_1_
  12.3 3.6 %collective-permute-start.9 = (bf16[288,128]{1,0:T(8,128)(2,1)S(1)}, bf16[288,128]{1,0:T(8,128)(2,1)S(1)}, u32[]{:S(2)}, u32[]{:S(2)}) collective-permute-start(bf16[288,128]{1,0:T(8,128)(2,1)S(1)} %get-tuple-element.40), channel_id=1, source_target_pairs={{0,12},{1,13},{2,14},{3,15},{4,8},{5,9},{6,10},{7,11},{8,4},{9,5},... | collective-permute-start | bytes 221192 | tf_op jit(solution)/shard_map/ppermute | solution.py:422
  15.9 0.0 collective-permute-done.3.refs_2_
  15.9 1.3 %collective-permute-start.10 = (bf16[288,128]{1,0:T(8,128)(2,1)S(1)}, bf16[288,128]{1,0:T(8,128)(2,1)S(1)}, u32[]{:S(2)}, u32[]{:S(2)}) collective-permute-start(bf16[288,128]{1,0:T(8,128)(2,1)S(1)} %get-tuple-element.41), channel_id=1, source_target_pairs={{0,14},{1,15},{2,12},{3,13},{4,10},{5,11},{6,8},{7,9},{8,6},{9,7},... | collective-permute-start | bytes 221192 | tf_op jit(solution)/shard_map/ppermute | solution.py:422
  17.2 0.0 collective-permute-done.4.refs_3_
  17.2 0.9 %part.1.flat_ref = bf16[2,2,128,256]{3,2,1,0:T(8,128)(2,1)S(1)} custom-call(bf16[480,128]{1,0:T(8,128)(2,1)S(1)} %get-tuple-element.31.refs_0_, bf16[480,128]{1,0:T(8,128)(2,1)S(1)} %collective-permute-done.2.refs_1_, bf16[480,128]{1,0:T(8,128)(2,1)S(1)} %collective-permute-done.3.refs_2_, bf16[480,128]{1,0:T(8,128)(2,1)S(1)} %collective-permute-done.4.refs_3_), custom_call_target="tpu_custom_call" | custom-call | flops 1000000 | bytes 1048576 | tf_op jit(solution)/shard_map/part/pallas_call | solution.py:472
  18.1 0.0 copy-done.2
  18.1 1.7 %part_near.1 = (bf16[256,128]{1,0:T(8,128)(2,1)S(1)}, bf16[256,128]{1,0:T(8,128)(2,1)S(1)}) custom-call(s32[1]{0:T(128)} %bitcast.place_ref, s32[16]{0:T(128)S(1)} %copy-done.2, s32[2,2,512]{2,1,0:T(2,128)S(1)} %copy-done.1, s32[2,2,512]{2,1,0:T(2,128)S(1)} %collective-permute-done.near_pairs_ref, bf16[2,2,128,256]{3,2,1,0:T(8,128)(2,1)S(1)} %part.1.flat_ref), custom_call_target="tpu_custom_call" | custom-call | flops 1000000 | bytes 1048576 | tf_op jit(solution)/shard_map/part_near/pallas_call | solution.py:485
  19.8 0.0 collective-permute-done.5.listed_ref.refs_4_
  19.8 1.7 %part_far.1 = (bf16[256,128]{1,0:T(8,128)(2,1)S(1)}, bf16[256,128]{1,0:T(8,128)(2,1)S(1)}) custom-call(s32[1]{0:T(128)} %bitcast.place_ref, s32[16]{0:T(128)S(1)} %copy-done.2, bf16[320,128]{1,0:T(8,128)(2,1)S(1)} %collective-permute-done.5.listed_ref.refs_4_, bf16[2,2,128,256]{3,2,1,0:T(8,128)(2,1)S(1)} %part.1.flat_ref, ...), custom_call_target="tpu_custom_call" | custom-call | flops 1000000000 | bytes 1048576 | tf_op jit(solution)/shard_map/part_far/pallas_call | solution.py:494
  21.5 0.1 collective-permute-start.7
  21.6 1.0 %collective-permute-start.6 = (bf16[256,128]{1,0:T(8,128)(2,1)S(1)}, bf16[256,128]{1,0:T(8,128)(2,1)S(1)}, u32[]{:S(2)}, u32[]{:S(2)}) collective-permute-start(bf16[256,128]{1,0:T(8,128)(2,1)S(1)} %get-tuple-element.37.after_1.after_2), channel_id=1, source_target_pairs={{0,8},{1,9},{2,10},{3,11},{4,12},{5,13},{6,14},{7,15},{8,0},{9,1},... | collective-permute-start | bytes 196616 | tf_op jit(solution)/shard_map/ppermute | solution.py:422
  22.6 1.2 %collective-permute-done.8.refs_5_ = bf16[288,128]{1,0:T(8,128)(2,1)S(1)} collective-permute-done((bf16[288,128]{1,0:T(8,128)(2,1)S(1)}, bf16[288,128]{1,0:T(8,128)(2,1)S(1)}, u32[]{:S(2)}, u32[]{:S(2)}) %collective-permute-start.8) | collective-permute-done | bytes 73760 | tf_op jit(solution)/shard_map/ppermute | solution.py:422
  23.8 0.8 %early.1.before_ref = f32[1536,128]{1,0:T(8,128)S(1)} custom-call(bf16[256,128]{1,0:T(8,128)(2,1)S(1)} %get-tuple-element.35.after_ref.after_0.refs_0_, bf16[256,128]{1,0:T(8,128)(2,1)S(1)} %get-tuple-element.37.after_1.after_2, bf16[480,128]{1,0:T(8,128)(2,1)S(1)} %get-tuple-element.31.refs_0_, bf16[480,128]{1,0:T(8,128)(2,1)S(1)} %collective-permute-done.2.refs_1_, ...), custom_call_target="tpu_custom_call" | custom-call | flops 1000000 | bytes 1048576 | tf_op jit(solution)/shard_map/early/pallas_call | solution.py:504
  24.6 0.0 collective-permute-done.9.refs_0_
  24.6 0.0 collective-permute-done.10.refs_1_
  24.6 2.8 %full.1 = (bf16[2,2,256,256]{3,2,1,0:T(8,128)(2,1)S(1)}, bf16[384,128]{1,0:T(8,128)(2,1)S(1)}, bf16[384,128]{1,0:T(8,128)(2,1)S(1)}) custom-call(s32[1]{0:T(128)} %bitcast.place_ref, s32[16]{0:T(128)S(1)} %copy-done.2, bf16[320,128]{1,0:T(8,128)(2,1)S(1)} %collective-permute-done.5.listed_ref.refs_4_, ...), custom_call_target="tpu_custom_call" | custom-call | flops 10000000000 | bytes 1048576 | tf_op jit(solution)/shard_map/full/pallas_call | solution.py:517
  27.4 5.6 %collective-permute-start.14 = (bf16[384,128]{1,0:T(8,128)(2,1)S(1)}, bf16[384,128]{1,0:T(8,128)(2,1)S(1)}, u32[]{:S(2)}, u32[]{:S(2)}) collective-permute-start(bf16[384,128]{1,0:T(8,128)(2,1)S(1)} %get-tuple-element.49), channel_id=1, source_target_pairs={{0,8},{1,9},{2,10},{3,11},{4,12},{5,13},{6,14},{7,15},{8,0},{9,1},... | collective-permute-start | bytes 294920 | tf_op jit(solution)/shard_map/ppermute | solution.py:422
  33.1 0.0 collective-permute-start.15
  33.1 0.2 collective-permute-start.11
  33.3 0.0 collective-permute-done.7.refs_1_.refs_2_
  33.3 0.0 collective-permute-done.6.refs_0_.refs_1_
  33.3 2.0 %full_near.1 = (bf16[384,128]{1,0:T(8,128)(2,1)S(1)}, bf16[192,128]{1,0:T(8,128)(2,1)S(1)}, bf16[192,128]{1,0:T(8,128)(2,1)S(1)}) custom-call(s32[1]{0:T(128)} %bitcast.place_ref, s32[16]{0:T(128)S(1)} %copy-done.2, s32[2,2,512]{2,1,0:T(2,128)S(1)} %copy-done.1, s32[2,2,512]{2,1,0:T(2,128)S(1)} %collective-permute-done.near_pairs_ref, ...), custom_call_target="tpu_custom_call" | custom-call | flops 500000000 | bytes 1048576 | tf_op jit(solution)/shard_map/full_near/pallas_call | solution.py:531
  35.3 0.4 collective-permute-start.12
  35.7 0.2 collective-permute-start.13
  35.8 0.0 collective-permute-done.11.refs_4_
  35.9 0.7 %collective-permute-done.12.refs_5_ = bf16[192,128]{1,0:T(8,128)(2,1)S(1)} collective-permute-done((bf16[192,128]{1,0:T(8,128)(2,1)S(1)}, bf16[192,128]{1,0:T(8,128)(2,1)S(1)}, u32[]{:S(2)}, u32[]{:S(2)}) %collective-permute-start.12) | collective-permute-done | bytes 49184 | tf_op jit(solution)/shard_map/ppermute | solution.py:422
  36.6 0.3 collective-permute-done.13.refs_6_
  36.9 0.0 copy-done
  36.9 1.8 %first_lags.1 = (f32[2,512,256]{2,1,0:T(8,128)S(1)}, bf16[2,96,512]{2,1,0:T(8,128)(2,1)S(1)}) custom-call(s32[1]{0:T(128)} %bitcast.place_ref, f32[256,256]{1,0:T(8,128)S(1)} %copy-done, bf16[256,128]{1,0:T(8,128)(2,1)S(1)} %get-tuple-element.35.after_ref.after_0.refs_0_, bf16[256,128]{1,0:T(8,128)(2,1)S(1)} %collective-permute-done.6.refs_0_.refs_1_, ...), custom_call_target="tpu_custom_call" | custom-call | flops 1000000 | bytes 1048576 | tf_op jit(solution)/shard_map/first_lags/pallas_call | solution.py:542
  38.7 1.2 %collective-permute-done.14.refs_0_ = bf16[384,128]{1,0:T(8,128)(2,1)S(1)} collective-permute-done((bf16[384,128]{1,0:T(8,128)(2,1)S(1)}, bf16[384,128]{1,0:T(8,128)(2,1)S(1)}, u32[]{:S(2)}, u32[]{:S(2)}) %collective-permute-start.14) | collective-permute-done | bytes 98336 | tf_op jit(solution)/shard_map/ppermute | solution.py:422
  39.9 0.2 collective-permute-done.15.refs_1_
  40.1 1.2 %lags.1 = f32[2,512,256]{2,1,0:T(8,128)} custom-call(f32[2,512,256]{2,1,0:T(8,128)S(1)} %get-tuple-element.47.first_ref, bf16[2,96,512]{2,1,0:T(8,128)(2,1)S(1)} %get-tuple-element.48.table_ref, bf16[384,128]{1,0:T(8,128)(2,1)S(1)} %collective-permute-done.14.refs_0_, bf16[384,128]{1,0:T(8,128)(2,1)S(1)} %collective-permute-done.15.refs_1_), custom_call_target="tpu_custom_call" | custom-call | flops 1000000000 | bytes 1048576 | tf_op jit(solution)/shard_map/lags/pallas_call | solution.py:554
  (2 shorter events, 0.0 us)
Async XLA Ops:
  0.0 2.6 %collective-permute-start.1 = (bf16[3,2,4,64,256]{4,3,2,1,0:T(8,128)(2,1)}, bf16[3,2,4,64,256]{4,3,2,1,0:T(8,128)(2,1)S(1)}, u32[]{:S(2)}, u32[]{:S(2)}) collective-permute-start(bf16[3,2,4,64,256]{4,3,2,1,0:T(8,128)(2,1)} %bitcast.2), channel_id=1, source_target_pairs={{0,1},{1,0},{2,3},{3,2},{4,5},{5,4},{6,7},{7,6},{8,9},{9,8},{10,11... | collective-permute-start | bytes 2359304 | tf_op jit(solution)/shard_map/ppermute | solution.py:422
  0.5 2.1 %collective-permute-start = (s32[2,2,512]{2,1,0:T(2,128)}, s32[2,2,512]{2,1,0:T(2,128)S(1)}, u32[]{:S(2)}, u32[]{:S(2)}) collective-permute-start(s32[2,2,512]{2,1,0:T(2,128)} %own_pairs_ref.5), channel_id=1, source_target_pairs={{0,1},{1,0},{2,3},{3,2},{4,5},{5,4},{6,7},{7,6},{8,9},{9,8},{10,11... | collective-permute-start | bytes 24584 | tf_op jit(solution)/shard_map/ppermute | solution.py:422
  0.5 1.1 %copy-start.3 = (bf16[3,1,512,256]{3,2,1,0:T(8,128)(2,1)S(1)}, bf16[3,1,512,256]{3,2,1,0:T(8,128)(2,1)}, u32[]{:S(2)}) copy-start(bf16[3,1,512,256]{3,2,1,0:T(8,128)(2,1)} %param.4) | copy-start | bytes 2359300
  1.6 0.9 %copy-start.1 = (s32[2,2,512]{2,1,0:T(2,128)S(1)}, s32[2,2,512]{2,1,0:T(2,128)}, u32[]{:S(2)}) copy-start(s32[2,2,512]{2,1,0:T(2,128)} %own_pairs_ref.5) | copy-start | bytes 24580
  3.4 8.8 %collective-permute-start.2 = (bf16[480,128]{1,0:T(8,128)(2,1)S(1)}, bf16[480,128]{1,0:T(8,128)(2,1)S(1)}, u32[]{:S(2)}, u32[]{:S(2)}) collective-permute-start(bf16[480,128]{1,0:T(8,128)(2,1)S(1)} %get-tuple-element.32), channel_id=1, source_target_pairs={{0,2},{1,3},{2,0},{3,1},{4,6},{5,7},{6,4},{7,5},{8,10},{9,11},{10,... | collective-permute-start | bytes 368648 | tf_op jit(solution)/shard_map/ppermute | solution.py:422
  6.4 9.5 %collective-permute-start.3 = (bf16[480,128]{1,0:T(8,128)(2,1)S(1)}, bf16[480,128]{1,0:T(8,128)(2,1)S(1)}, u32[]{:S(2)}, u32[]{:S(2)}) collective-permute-start(bf16[480,128]{1,0:T(8,128)(2,1)S(1)} %get-tuple-element.33), channel_id=1, source_target_pairs={{0,4},{1,5},{2,6},{3,7},{4,0},{5,1},{6,2},{7,3},{8,12},{9,13},{10,... | collective-permute-start | bytes 368648 | tf_op jit(solution)/shard_map/ppermute | solution.py:422
  8.0 9.2 %collective-permute-start.4 = (bf16[480,128]{1,0:T(8,128)(2,1)S(1)}, bf16[480,128]{1,0:T(8,128)(2,1)S(1)}, u32[]{:S(2)}, u32[]{:S(2)}) collective-permute-start(bf16[480,128]{1,0:T(8,128)(2,1)S(1)} %get-tuple-element.34), channel_id=1, source_target_pairs={{0,6},{1,7},{2,4},{3,5},{4,2},{5,3},{6,0},{7,1},{8,14},{9,15},{10,... | collective-permute-start | bytes 368648 | tf_op jit(solution)/shard_map/ppermute | solution.py:422
  8.0 11.8 %collective-permute-start.5 = (bf16[320,128]{1,0:T(8,128)(2,1)S(1)}, bf16[320,128]{1,0:T(8,128)(2,1)S(1)}, u32[]{:S(2)}, u32[]{:S(2)}) collective-permute-start(bf16[320,128]{1,0:T(8,128)(2,1)S(1)} %get-tuple-element.36), channel_id=1, source_target_pairs={{0,8},{1,9},{2,10},{3,11},{4,12},{5,13},{6,14},{7,15},{8,0},{9,1},... | collective-permute-start | bytes 245768 | tf_op jit(solution)/shard_map/ppermute | solution.py:422
  11.0 12.8 %collective-permute-start.8 = (bf16[288,128]{1,0:T(8,128)(2,1)S(1)}, bf16[288,128]{1,0:T(8,128)(2,1)S(1)}, u32[]{:S(2)}, u32[]{:S(2)}) collective-permute-start(bf16[288,128]{1,0:T(8,128)(2,1)S(1)} %get-tuple-element.39), channel_id=1, source_target_pairs={{0,10},{1,11},{2,8},{3,9},{4,14},{5,15},{6,12},{7,13},{8,2},{9,3},... | collective-permute-start | bytes 221192 | tf_op jit(solution)/shard_map/ppermute | solution.py:422
  12.3 12.3 %collective-permute-start.9 = (bf16[288,128]{1,0:T(8,128)(2,1)S(1)}, bf16[288,128]{1,0:T(8,128)(2,1)S(1)}, u32[]{:S(2)}, u32[]{:S(2)}) collective-permute-start(bf16[288,128]{1,0:T(8,128)(2,1)S(1)} %get-tuple-element.40), channel_id=1, source_target_pairs={{0,12},{1,13},{2,14},{3,15},{4,8},{5,9},{6,10},{7,11},{8,4},{9,5},... | collective-permute-start | bytes 221192 | tf_op jit(solution)/shard_map/ppermute | solution.py:422
  15.9 8.7 %collective-permute-start.10 = (bf16[288,128]{1,0:T(8,128)(2,1)S(1)}, bf16[288,128]{1,0:T(8,128)(2,1)S(1)}, u32[]{:S(2)}, u32[]{:S(2)}) collective-permute-start(bf16[288,128]{1,0:T(8,128)(2,1)S(1)} %get-tuple-element.41), channel_id=1, source_target_pairs={{0,14},{1,15},{2,12},{3,13},{4,10},{5,11},{6,8},{7,9},{8,6},{9,7},... | collective-permute-start | bytes 221192 | tf_op jit(solution)/shard_map/ppermute | solution.py:422
  17.2 0.9 %copy-start.2 = (s32[16]{0:T(128)S(1)}, s32[16]{0:T(128)}, u32[]{:S(2)}) copy-start(s32[16]{0:T(128)} %counts_ref.7) | copy-start | bytes 196
  21.5 11.8 %collective-permute-start.7 = (bf16[256,128]{1,0:T(8,128)(2,1)S(1)}, bf16[256,128]{1,0:T(8,128)(2,1)S(1)}, u32[]{:S(2)}, u32[]{:S(2)}) collective-permute-start(bf16[256,128]{1,0:T(8,128)(2,1)S(1)} %get-tuple-element.38), channel_id=1, source_target_pairs={{0,9},{1,8},{2,11},{3,10},{4,13},{5,12},{6,15},{7,14},{8,1},{9,0},... | collective-permute-start | bytes 196616 | tf_op jit(solution)/shard_map/ppermute | solution.py:422
  21.6 11.7 %collective-permute-start.6 = (bf16[256,128]{1,0:T(8,128)(2,1)S(1)}, bf16[256,128]{1,0:T(8,128)(2,1)S(1)}, u32[]{:S(2)}, u32[]{:S(2)}) collective-permute-start(bf16[256,128]{1,0:T(8,128)(2,1)S(1)} %get-tuple-element.37.after_1.after_2), channel_id=1, source_target_pairs={{0,8},{1,9},{2,10},{3,11},{4,12},{5,13},{6,14},{7,15},{8,0},{9,1},... | collective-permute-start | bytes 196616 | tf_op jit(solution)/shard_map/ppermute | solution.py:422
  27.4 12.4 %collective-permute-start.14 = (bf16[384,128]{1,0:T(8,128)(2,1)S(1)}, bf16[384,128]{1,0:T(8,128)(2,1)S(1)}, u32[]{:S(2)}, u32[]{:S(2)}) collective-permute-start(bf16[384,128]{1,0:T(8,128)(2,1)S(1)} %get-tuple-element.49), channel_id=1, source_target_pairs={{0,8},{1,9},{2,10},{3,11},{4,12},{5,13},{6,14},{7,15},{8,0},{9,1},... | collective-permute-start | bytes 294920 | tf_op jit(solution)/shard_map/ppermute | solution.py:422
  33.1 7.0 %collective-permute-start.15 = (bf16[384,128]{1,0:T(8,128)(2,1)S(1)}, bf16[384,128]{1,0:T(8,128)(2,1)S(1)}, u32[]{:S(2)}, u32[]{:S(2)}) collective-permute-start(bf16[384,128]{1,0:T(8,128)(2,1)S(1)} %get-tuple-element.50), channel_id=1, source_target_pairs={{0,9},{1,8},{2,11},{3,10},{4,13},{5,12},{6,15},{7,14},{8,1},{9,0},... | collective-permute-start | bytes 294920 | tf_op jit(solution)/shard_map/ppermute | solution.py:422
  33.1 2.8 %collective-permute-start.11 = (bf16[256,128]{1,0:T(8,128)(2,1)S(1)}, bf16[256,128]{1,0:T(8,128)(2,1)S(1)}, u32[]{:S(2)}, u32[]{:S(2)}) collective-permute-start(bf16[256,128]{1,0:T(8,128)(2,1)S(1)} %get-tuple-element.44), channel_id=1, source_target_pairs={{0,1},{1,0},{2,3},{3,2},{4,5},{5,4},{6,7},{7,6},{8,9},{9,8},{10,11... | collective-permute-start | bytes 196616 | tf_op jit(solution)/shard_map/ppermute | solution.py:422
  33.3 3.6 %copy-start = (f32[256,256]{1,0:T(8,128)S(1)}, f32[256,256]{1,0:T(8,128)}, u32[]{:S(2)}) copy-start(f32[256,256]{1,0:T(8,128)} %constant.6.clone.inverse_ref) | copy-start | bytes 786436
  35.3 1.3 %collective-permute-start.12 = (bf16[192,128]{1,0:T(8,128)(2,1)S(1)}, bf16[192,128]{1,0:T(8,128)(2,1)S(1)}, u32[]{:S(2)}, u32[]{:S(2)}) collective-permute-start(bf16[192,128]{1,0:T(8,128)(2,1)S(1)} %get-tuple-element.45), channel_id=1, source_target_pairs={{0,1},{1,0},{2,3},{3,2},{4,5},{5,4},{6,7},{7,6},{8,9},{9,8},{10,11... | collective-permute-start | bytes 147464 | tf_op jit(solution)/shard_map/ppermute | solution.py:422
  35.7 1.2 %collective-permute-start.13 = (bf16[192,128]{1,0:T(8,128)(2,1)S(1)}, bf16[192,128]{1,0:T(8,128)(2,1)S(1)}, u32[]{:S(2)}, u32[]{:S(2)}) collective-permute-start(bf16[192,128]{1,0:T(8,128)(2,1)S(1)} %get-tuple-element.46), channel_id=1, source_target_pairs={{0,1},{1,0},{2,3},{3,2},{4,5},{5,4},{6,7},{7,6},{8,9},{9,8},{10,11... | collective-permute-start | bytes 147464 | tf_op jit(solution)/shard_map/ppermute | solution.py:422

commit v18 on v17

--- a/solution.py
+++ b/solution.py
@@ -74,20 +74,15 @@
 
 def station_spectra(windows_ref, at, table):
     parts = []
-    for comp in range(windows_ref.shape[0]):
+    for comp in range(COMPS):
         low = windows_ref[comp, 0, at]
         high = windows_ref[comp, 1, at]
         parts += [low[:SLOTS], high[SLOTS:], low[SLOTS:], high[:SLOTS]]
     traces = jnp.concatenate(parts)
-    square = jnp.square(traces.astype(jnp.float32))
-    square_hi = square.astype(jnp.bfloat16)
-    square_lo = (square - square_hi.astype(jnp.float32)).astype(jnp.bfloat16)
-    ones = jnp.ones((16, traces.shape[1]), jnp.bfloat16)
-    energy = lax.dot_general(ones, square_hi, NT, preferred_element_type=jnp.float32)
-    energy += lax.dot_general(ones, square_lo, NT, preferred_element_type=jnp.float32)
-    scale = lax.rsqrt(energy[:1] + EPSILON)
-    raw = lax.dot_general(table, traces, NT, preferred_element_type=jnp.float32)
-    return (raw * scale).astype(jnp.bfloat16)
+    energy = jnp.sum(jnp.square(traces.astype(jnp.float32)), axis=1, keepdims=True)
+    raw = lax.dot_general(traces, table, NT, preferred_element_type=jnp.float32)
+    spectra = (raw * lax.rsqrt(energy + EPSILON)).astype(jnp.bfloat16)
+    return [spectra[comp * LANES : (comp + 1) * LANES].T for comp in range(COMPS)]
 
 
 def own_kernel(place_ref, windows_ref, part_ref, full_ref, table_ref):
@@ -104,7 +99,7 @@
     for mg in range(groups):
         spectra = station_spectra(windows_ref, group ^ mg, table)
         for comp in range(COMPS):
-            lanes = spectra[:, comp * LANES : (comp + 1) * LANES]
+            lanes = spectra[comp]
             part_ref[mg, comp * 2 * PART : (comp + 1) * 2 * PART] = lanes[: 2 * PART]
             for far in range(2):
                 at = 2 * PART + 2 * FULL * far
@@ -128,7 +123,7 @@
         side[2 * part_rows : 2 * part_rows + full_rows] = full_ref[mg]
         cross[:full_rows] = full_ref[groups + mg]
         for comp in range(COMPS):
-            lanes = spectra[:, comp * LANES : (comp + 1) * LANES]
+            lanes = spectra[comp]
             at = part_rows + comp * 2 * PART
             side[at : at + 2 * PART] = lanes[: 2 * PART]
             at = 2 * part_rows + full_rows + comp * 2 * FULL
@@ -169,15 +164,19 @@
     return jnp.concatenate([picked[:, :used], jnp.concatenate(rest, axis=1)])
 
 
-def pick(place_ref, counts_ref, listed, flat_ref, bins, mq, *picked_refs):
-    cells = counts_ref.shape[0]
+def sides_of(place_ref, cells, mq):
     quarter, group = place_of(place_ref, cells // 4)
     own = quarter ^ mq
     high, low = own // 2, own % 2
-    cell = high * (cells // 2) + group * 2 + low
+    return high * (cells // 2) + group * 2 + low, high, low, ((high, high), (low, 1 - low))
+
+
+def hots(place_ref, counts_ref, listed, rows, bins, mq):
+    cells = counts_ref.shape[0]
+    cell, high, low, _ = sides_of(place_ref, cells, mq)
     count = listed.shape[0] // 2
     runs = LANES // width(bins)
-    run_bits, bin_bits, lane_bits = (n.bit_length() - 1 for n in (runs, width(bins), LANES))
+    run_bits, bin_bits = (n.bit_length() - 1 for n in (runs, width(bins)))
     first, second = listed[:count].astype(jnp.int32), listed[count:].astype(jnp.int32)
     far_counts = [counts_ref[cell ^ 1], counts_ref[cell ^ (cells // 2)]]
     odd = lax.broadcasted_iota(jnp.int32, (count, LANES), 0) & 1
@@ -187,56 +186,68 @@
     turned = (spot * runs + (left & (runs - 1))).T
     lane = lax.broadcasted_iota(jnp.int32, (LANES, LANES), 1)
     run = lane >> bin_bits
-    sides = ((high, high), (low, 1 - low))
     found = []
     for step_round in range(2):
         hot, here = [], []
         for at in range(step_round, count, 2):
             both = jnp.broadcast_to(turned[:, at : at + 1], (LANES, LANES))
-            here.append((both & (runs - 1)) == run)
+            here.append(jnp.where((both & (runs - 1)) == run, 1.0, 0.0).astype(jnp.bfloat16))
             offset = (both >> run_bits) - lane
             hot.append(
                 jnp.concatenate(
                     [
                         jnp.where(offset == start, 1.0, 0.0).astype(jnp.bfloat16)
-                        for start in range(0, flat_ref.shape[2], LANES)
+                        for start in range(0, rows, LANES)
                     ],
                     axis=1,
                 )
             )
-        block = flat_ref[sides[step_round][0], sides[step_round][1]]
-        wide = jnp.dot(jnp.concatenate(hot), block, preferred_element_type=jnp.float32)
-        masked = []
-        for chunk, mask in enumerate(here):
-            part = wide[chunk * LANES : (chunk + 1) * LANES]
-            masked.append(
-                jnp.concatenate(
-                    [
-                        jnp.where(mask, part[:, :LANES], 0.0).astype(jnp.bfloat16),
-                        jnp.where(mask, part[:, LANES:], 0.0).astype(jnp.bfloat16),
-                    ],
-                    axis=1,
-                )
-            )
-        found.append(jnp.concatenate(masked))
-    found = jnp.concatenate(found, axis=1)
+        found.append((jnp.concatenate(hot), jnp.concatenate(here)))
+    return found
+
+
+def folds_of(count, bins):
+    return sorted({entry[1:] for entries in packing(count, bins)[1] for entry in entries})
+
+
+def folds(count, bins):
     spread = lax.broadcasted_iota(jnp.int32, (4 * LANES, LANES), 0)
     kept = lax.broadcasted_iota(jnp.int32, (4 * LANES, LANES), 1)
     bin_of = spread & (width(bins) - 1)
-    value = jnp.where(bin_of < bins, (spread >> lane_bits) * bins + bin_of, -1)
-    rows, parts = packing(found.shape[0], bins)
+    value = jnp.where(bin_of < bins, (spread >> (LANES.bit_length() - 1)) * bins + bin_of, -1)
+    kinds = folds_of(count, bins)
+    matrices = []
+    for at, least, end in kinds:
+        fold = (value >= least) & (value < end) & (kept == value + (at - least))
+        matrices.append(jnp.where(fold, 1.0, 0.0).astype(jnp.bfloat16))
+    return kinds, matrices
+
+
+def picks(place_ref, cells, hot, kinds, matrices, flat_ref, bins, mq):
+    _, _, _, sides = sides_of(place_ref, cells, mq)
+    found = []
+    for (rows, lanes), (own, far) in zip(hot, sides):
+        wide = jnp.dot(rows, flat_ref[own, far], preferred_element_type=jnp.float32).astype(jnp.bfloat16)
+        found += [wide[:, :LANES] * lanes, wide[:, LANES:] * lanes]
+    found = jnp.concatenate(found, axis=1)
+    held, parts = packing(found.shape[0], bins)
     picked = []
     for entries in parts:
         total = 0.0
-        for start, at, least, end in entries:
-            fold = (value >= least) & (value < end) & (kept == value + (at - least))
+        for start, *kind in entries:
             total += jnp.dot(
-                found[start : start + rows],
-                jnp.where(fold, 1.0, 0.0).astype(jnp.bfloat16),
+                found[start : start + held],
+                matrices[kinds.index(tuple(kind))],
                 preferred_element_type=jnp.float32,
             )
         picked.append(total.astype(jnp.bfloat16))
-    picked = jnp.concatenate(picked)
+    return jnp.concatenate(picked)
+
+
+def pick(place_ref, counts_ref, listed, flat_ref, bins, mq, *picked_refs):
+    hot = hots(place_ref, counts_ref, listed, flat_ref.shape[2], bins, mq)
+    kinds, matrices = folds(listed.shape[0] // 4 * LANES, bins)
+    picked = picks(place_ref, counts_ref.shape[0], hot, kinds, matrices, flat_ref, bins, mq)
     each = picked.shape[0] // len(picked_refs)
     for at, ref in enumerate(picked_refs):
         ref[...] = picked[at * each : (at + 1) * each]
@@ -321,14 +332,30 @@
     add_cross(pieces, trace_ref, FULL, sums_ref)
 
 
-def full_kernel(place_ref, counts_ref, listed_ref, after_0, after_2, before_ref, *refs):
+def ready_kernel(place_ref, counts_ref, listed_ref, after_ref, hot_ref, here_ref, fold_ref):
+    listed = listed_ref[cross_full(listed_ref)[2] :].astype(jnp.float32)
+    listing = listed.shape[0] // 2
+    for at in range(2):
+        part = listed[at * listing : (at + 1) * listing]
+        for step_round, (hot, here) in enumerate(
+            hots(place_ref, counts_ref, part, hot_ref.shape[3], FULL, 2 + at)
+        ):
+            hot_ref[at, step_round] = hot
+            here_ref[at, step_round] = here
+    for at, matrix in enumerate(folds(hot_ref.shape[2], FULL)[1]):
+        fold_ref[at] = matrix
+
+
+def full_kernel(cells, place_ref, hot_ref, here_ref, fold_ref, after_0, before_ref, *refs):
     piece_refs, (flat_ref, picked_0, picked_1, trace_ref, cross_ref) = refs[:-5], refs[-5:]
     add_cross([cross_full(ref) for ref in piece_refs], trace_ref, FULL, cross_ref, before_ref)
     turn_blocks(cross_ref, FULL, flat_ref)
-    listed = listed_ref[cross_full(listed_ref)[2] :].astype(jnp.float32)
-    listing = listed.shape[0] // 2
-    pick(place_ref, counts_ref, listed[:listing], flat_ref, FULL, 2, picked_0)
-    pick(place_ref, counts_ref, listed[listing:], flat_ref, FULL, 3, picked_1)
+    count = hot_ref.shape[2]
+    kinds = folds_of(count, FULL)
+    matrices = [fold_ref[at] for at in range(len(kinds))]
+    for at, ref in enumerate((picked_0, picked_1)):
+        hot = [(hot_ref[at, step_round], here_ref[at, step_round]) for step_round in range(2)]
+        ref[...] = picks(place_ref, cells, hot, kinds, matrices, flat_ref, FULL, 2 + at)
 
 
 def near_kernel(bins, sent, place_ref, counts_ref, own_pairs_ref, near_pairs_ref, flat_ref, *refs):
@@ -513,11 +540,24 @@
         cost_estimate=cost(0.001),
         name="early",
     )(part_0, part_2, *sides, *early)
-    sent, part_2, part_3 = part_2, swap(part_2, half), swap(part_3, half + 1)
+    part_2, part_3 = swap(part_2, half), swap(part_3, half + 1)
+    ready = pl.pallas_call(
+        ready_kernel,
+        out_shape=[
+            shape(2, 2, count, full_blocks.shape[2]),
+            shape(2, 2, count, LANES),
+            shape(len(folds_of(count, FULL)), 4 * LANES, LANES),
+        ],
+        in_specs=[smem, smem, vmem, pl.BlockSpec(memory_space=pl.ANY)],
+        out_specs=[vmem] * 3,
+        compiler_params=params,
+        cost_estimate=cost(0.001),
+        name="ready",
+    )(place, counts, far[0], sums)
     full_flat, full_2, full_3 = pl.pallas_call(
-        full_kernel,
+        functools.partial(full_kernel, cells),
         out_shape=[full_blocks, full_packed, full_packed],
-        in_specs=[smem, smem, vmem] + [pl.BlockSpec(memory_space=pl.ANY)] * 2 + [vmem] * (1 + len(late)),
+        in_specs=[smem] + [vmem] * 3 + [pl.BlockSpec(memory_space=pl.ANY)] + [vmem] * (1 + len(late)),
         out_specs=[vmem] * 3,
         scratch_shapes=[
             pltpu.VMEM((padded(len(late) * 2 * comps) * 2 * FULL, LANES), jnp.float32),
@@ -526,7 +566,7 @@
         compiler_params=params,
         cost_estimate=cost(10),
         name="full",
-    )(place, counts, far[0], part_0, sent, sums, *late)
+    )(place, *ready, part_0, sums, *late)
     full_2, full_3 = swap(full_2, half), swap(full_3, half + 1)
     full_0, *full_1 = pl.pallas_call(
         functools.partial(near_kernel, FULL, 2),

time: 41.8 us -> 41.7 us (level)
  waiting for transfers between devices: 3.75 us -> 5.5 us
  starting transfers between devices: 21.8 us -> 20.4 us
    ppermute x16, waiting for transfers between devices: 3.75 us -> 5.5 us  [swap(): return lax.ppermute(x, 'cell', [(i, i ^ mask) for i in range(cells)])]
    ppermute x16, starting transfers between devices: 21.8 us -> 20.4 us  [swap(): return lax.ppermute(x, 'cell', [(i, i ^ mask) for i in range(cells)])]
    pallas_call x1 -> x2, Pallas kernels: 2.81 us -> 3.33 us  [the longest x1 2.01 us: on_device(): pl.pallas_call(functools.partial(full_kernel, cells), out_shape=[full_blo...]
  transfers between devices with their start and end apart: 16 -> 16, of which waited for: 6 -> 6; matrix products, arithmetic and copies ran while one was open for 0% -> 0% of each run, Pallas kernels for 30% -> 31%
where the time goes in v18:
time: 41.7 us; the launch traced here: 41.5 us
  starting transfers between devices  20.4 us (49%)
  Pallas kernels  14.4 us (35%)
  waiting for transfers between devices  5.5 us (13%)
  local copies, waits for them, and re-layouts  1.14 us (3%)
    ppermute x16, starting transfers between devices, swap(): return lax.ppermute(x, 'cell', [(i, i ^ mask) for i in range(cells)])  20.4 us
    ppermute x16, waiting for transfers between devices, swap(): return lax.ppermute(x, 'cell', [(i, i ^ mask) for i in range(cells)])  5.5 us
    pallas_call x1, Pallas kernels, on_device(): pl.pallas_call(functools.partial(full_kernel, cells), out_shape=[full_blo...  2.01 us
    pallas_call x1, Pallas kernels, on_device(): pl.pallas_call(functools.partial(near_kernel, FULL, 2), out_shape=[full_p...  1.95 us
    pallas_call x1, Pallas kernels, on_device(): pl.pallas_call(functools.partial(first_lags_kernel, groups), out_shape=[s...  1.77 us
    pallas_call x1, Pallas kernels, on_device(): pl.pallas_call(functools.partial(near_kernel, PART, 1), out_shape=[part_p...  1.69 us
    pallas_call x1, Pallas kernels, on_device(): pl.pallas_call(functools.partial(far_kernel, PART), out_shape=[part_packe...  1.68 us
    pallas_call x1, Pallas kernels, on_device(): pl.pallas_call(ready_kernel, out_shape=[shape(2, 2, count, full_blocks.sh...  1.32 us
  transfers between devices with their start and end apart: 16, of which 6 were waited for; matrix products, arithmetic and copies ran while one was open for 0% of the time, Pallas kernels for 31%

profile of v18, /device:TPU:0, one launch (start us, length us, event | category | flops | bytes accessed | tf_op | source)
XLA Modules:
  0.0 41.5 jit_solution(18200883755034622992)
XLA Ops:
  0.0 0.5 %collective-permute-start.1 = (bf16[3,2,4,64,256]{4,3,2,1,0:T(8,128)(2,1)}, bf16[3,2,4,64,256]{4,3,2,1,0:T(8,128)(2,1)S(1)}, u32[]{:S(2)}, u32[]{:S(2)}) collective-permute-start(bf16[3,2,4,64,256]{4,3,2,1,0:T(8,128)(2,1)} %bitcast.2), channel_id=1, source_target_pairs={{0,1},{1,0},{2,3},{3,2},{4,5},{5,4},{6,7},{7,6},{8,9},{9,8},{10,11... | collective-permute-start | bytes 2359304 | tf_op jit(solution)/shard_map/ppermute | solution.py:449
  0.5 0.1 collective-permute-start
  0.5 0.0 copy-start.3
  0.5 1.1 %copy-done.3 = bf16[3,1,512,256]{3,2,1,0:T(8,128)(2,1)S(1)} copy-done((bf16[3,1,512,256]{3,2,1,0:T(8,128)(2,1)S(1)}, bf16[3,1,512,256]{3,2,1,0:T(8,128)(2,1)}, u32[]{:S(2)}) %copy-start.3) | copy-done | bytes 786456
  1.6 0.6 %own_spectra.1 = (bf16[4,96,128]{2,1,0:T(8,128)(2,1)S(1)}, bf16[8,144,128]{2,1,0:T(8,128)(2,1)S(1)}, bf16[128,256]{1,0:T(8,128)(2,1)S(1)}) custom-call(s32[1]{0:T(128)} %bitcast.place_ref, bf16[3,2,4,64,256]{4,3,2,1,0:T(8,128)(2,1)S(1)} %bitcast.3), custom_call_target="tpu_custom_call" | custom-call | flops 1000000000 | bytes 1048576 | tf_op jit(solution)/shard_map/own_spectra/pallas_call | solution.py:466
  2.2 0.4 collective-permute-done.near_pairs_ref
  2.6 0.0 collective-permute-done.1.windows_ref
  2.6 0.0 copy-done.1
  2.6 0.5 %near_spectra.1 = (bf16[480,128]{1,0:T(8,128)(2,1)S(1)}, bf16[480,128]{1,0:T(8,128)(2,1)S(1)}, bf16[480,128]{1,0:T(8,128)(2,1)S(1)}, bf16[480,128]{1,0:T(8,128)(...) custom-call(s32[1]{0:T(128)} %bitcast.place_ref, ...), custom_call_target="tpu_custom_call" | custom-call | flops 1000000000 | bytes 1048576 | tf_op jit(solution)/shard_map/near_spectra/pallas_call | solution.py:480
  3.1 3.0 %collective-permute-start.2 = (bf16[480,128]{1,0:T(8,128)(2,1)S(1)}, bf16[480,128]{1,0:T(8,128)(2,1)S(1)}, u32[]{:S(2)}, u32[]{:S(2)}) collective-permute-start(bf16[480,128]{1,0:T(8,128)(2,1)S(1)} %get-tuple-element.35), channel_id=1, source_target_pairs={{0,2},{1,3},{2,0},{3,1},{4,6},{5,7},{6,4},{7,5},{8,10},{9,11},{10,... | collective-permute-start | bytes 368648 | tf_op jit(solution)/shard_map/ppermute | solution.py:449
  6.0 1.6 %collective-permute-start.3 = (bf16[480,128]{1,0:T(8,128)(2,1)S(1)}, bf16[480,128]{1,0:T(8,128)(2,1)S(1)}, u32[]{:S(2)}, u32[]{:S(2)}) collective-permute-start(bf16[480,128]{1,0:T(8,128)(2,1)S(1)} %get-tuple-element.36), channel_id=1, source_target_pairs={{0,4},{1,5},{2,6},{3,7},{4,0},{5,1},{6,2},{7,3},{8,12},{9,13},{10,... | collective-permute-start | bytes 368648 | tf_op jit(solution)/shard_map/ppermute | solution.py:449
  7.6 0.0 collective-permute-start.4
  7.6 3.0 %collective-permute-start.5 = (bf16[320,128]{1,0:T(8,128)(2,1)S(1)}, bf16[320,128]{1,0:T(8,128)(2,1)S(1)}, u32[]{:S(2)}, u32[]{:S(2)}) collective-permute-start(bf16[320,128]{1,0:T(8,128)(2,1)S(1)} %get-tuple-element.39), channel_id=1, source_target_pairs={{0,8},{1,9},{2,10},{3,11},{4,12},{5,13},{6,14},{7,15},{8,0},{9,1},... | collective-permute-start | bytes 245768 | tf_op jit(solution)/shard_map/ppermute | solution.py:449
  10.6 1.3 %collective-permute-start.8 = (bf16[288,128]{1,0:T(8,128)(2,1)S(1)}, bf16[288,128]{1,0:T(8,128)(2,1)S(1)}, u32[]{:S(2)}, u32[]{:S(2)}) collective-permute-start(bf16[288,128]{1,0:T(8,128)(2,1)S(1)} %get-tuple-element.42), channel_id=1, source_target_pairs={{0,10},{1,11},{2,8},{3,9},{4,14},{5,15},{6,12},{7,13},{8,2},{9,3},... | collective-permute-start | bytes 221192 | tf_op jit(solution)/shard_map/ppermute | solution.py:449
  11.9 0.0 collective-permute-done.2.refs_1_
  11.9 3.6 %collective-permute-start.9 = (bf16[288,128]{1,0:T(8,128)(2,1)S(1)}, bf16[288,128]{1,0:T(8,128)(2,1)S(1)}, u32[]{:S(2)}, u32[]{:S(2)}) collective-permute-start(bf16[288,128]{1,0:T(8,128)(2,1)S(1)} %get-tuple-element.46), channel_id=1, source_target_pairs={{0,12},{1,13},{2,14},{3,15},{4,8},{5,9},{6,10},{7,11},{8,4},{9,5},... | collective-permute-start | bytes 221192 | tf_op jit(solution)/shard_map/ppermute | solution.py:449
  15.5 0.0 collective-permute-done.3.refs_2_
  15.5 1.3 %collective-permute-start.10 = (bf16[288,128]{1,0:T(8,128)(2,1)S(1)}, bf16[288,128]{1,0:T(8,128)(2,1)S(1)}, u32[]{:S(2)}, u32[]{:S(2)}) collective-permute-start(bf16[288,128]{1,0:T(8,128)(2,1)S(1)} %get-tuple-element.47), channel_id=1, source_target_pairs={{0,14},{1,15},{2,12},{3,13},{4,10},{5,11},{6,8},{7,9},{8,6},{9,7},... | collective-permute-start | bytes 221192 | tf_op jit(solution)/shard_map/ppermute | solution.py:449
  16.8 0.0 collective-permute-done.4.refs_3_
  16.8 0.9 %part.1.flat_ref = bf16[2,2,128,256]{3,2,1,0:T(8,128)(2,1)S(1)} custom-call(bf16[480,128]{1,0:T(8,128)(2,1)S(1)} %get-tuple-element.34.refs_0_, bf16[480,128]{1,0:T(8,128)(2,1)S(1)} %collective-permute-done.2.refs_1_, bf16[480,128]{1,0:T(8,128)(2,1)S(1)} %collective-permute-done.3.refs_2_, bf16[480,128]{1,0:T(8,128)(2,1)S(1)} %collective-permute-done.4.refs_3_), custom_call_target="tpu_custom_call" | custom-call | flops 1000000 | bytes 1048576 | tf_op jit(solution)/shard_map/part/pallas_call | solution.py:499
  17.7 0.0 copy-done.2
  17.7 1.7 %part_near.1 = (bf16[256,128]{1,0:T(8,128)(2,1)S(1)}, bf16[256,128]{1,0:T(8,128)(2,1)S(1)}) custom-call(s32[1]{0:T(128)} %bitcast.place_ref, s32[16]{0:T(128)S(1)} %copy-done.2, s32[2,2,512]{2,1,0:T(2,128)S(1)} %copy-done.1, s32[2,2,512]{2,1,0:T(2,128)S(1)} %collective-permute-done.near_pairs_ref, bf16[2,2,128,256]{3,2,1,0:T(8,128)(2,1)S(1)} %part.1.flat_ref), custom_call_target="tpu_custom_call" | custom-call | flops 1000000 | bytes 1048576 | tf_op jit(solution)/shard_map/part_near/pallas_call | solution.py:512
  19.4 0.0 collective-permute-done.5.listed_ref.refs_4_
  19.4 1.7 %part_far.1 = (bf16[256,128]{1,0:T(8,128)(2,1)S(1)}, bf16[256,128]{1,0:T(8,128)(2,1)S(1)}) custom-call(s32[1]{0:T(128)} %bitcast.place_ref, s32[16]{0:T(128)S(1)} %copy-done.2, bf16[320,128]{1,0:T(8,128)(2,1)S(1)} %collective-permute-done.5.listed_ref.refs_4_, bf16[2,2,128,256]{3,2,1,0:T(8,128)(2,1)S(1)} %part.1.flat_ref, ...), custom_call_target="tpu_custom_call" | custom-call | flops 1000000000 | bytes 1048576 | tf_op jit(solution)/shard_map/part_far/pallas_call | solution.py:521
  21.1 0.1 collective-permute-start.7
  21.2 1.0 %collective-permute-start.6 = (bf16[256,128]{1,0:T(8,128)(2,1)S(1)}, bf16[256,128]{1,0:T(8,128)(2,1)S(1)}, u32[]{:S(2)}, u32[]{:S(2)}) collective-permute-start(bf16[256,128]{1,0:T(8,128)(2,1)S(1)} %get-tuple-element.40.after_1), channel_id=1, source_target_pairs={{0,8},{1,9},{2,10},{3,11},{4,12},{5,13},{6,14},{7,15},{8,0},{9,1},... | collective-permute-start | bytes 196616 | tf_op jit(solution)/shard_map/ppermute | solution.py:449
  22.2 1.2 %collective-permute-done.8.refs_5_ = bf16[288,128]{1,0:T(8,128)(2,1)S(1)} collective-permute-done((bf16[288,128]{1,0:T(8,128)(2,1)S(1)}, bf16[288,128]{1,0:T(8,128)(2,1)S(1)}, u32[]{:S(2)}, u32[]{:S(2)}) %collective-permute-start.8) | collective-permute-done | bytes 73760 | tf_op jit(solution)/shard_map/ppermute | solution.py:449
  23.4 0.8 %early.1.after_ref.before_ref = f32[1536,128]{1,0:T(8,128)S(1)} custom-call(bf16[256,128]{1,0:T(8,128)(2,1)S(1)} %get-tuple-element.38.after_ref.after_0.refs_0_, bf16[256,128]{1,0:T(8,128)(2,1)S(1)} %get-tuple-element.40.after_1, bf16[480,128]{1,0:T(8,128)(2,1)S(1)} %get-tuple-element.34.refs_0_, bf16[480,128]{1,0:T(8,128)(2,1)S(1)} %collective-permute-done.2.refs_1_, ...), custom_call_target="tpu_custom_call" | custom-call | flops 1000000 | bytes 1048576 | tf_op jit(solution)/shard_map/early/pallas_call | solution.py:531
  24.3 1.3 %ready.1 = (bf16[2,2,512,256]{3,2,1,0:T(8,128)(2,1)S(1)}, bf16[2,2,512,128]{3,2,1,0:T(8,128)(2,1)S(1)}, bf16[4,512,128]{2,1,0:T(8,128)(2,1)S(1)}) custom-call(s32[1]{0:T(128)} %bitcast.place_ref, s32[16]{0:T(128)S(1)} %copy-done.2, bf16[320,128]{1,0:T(8,128)(2,1)S(1)} %collective-permute-done.5.listed_ref.refs_4_, f32[1536,128]{1,0:T(8,128)S(1)} %early.1.after_ref.before_ref), custom_call_target="tpu_custom_call" | custom-call | flops 1000000 | bytes 1048576 | tf_op jit(solution)/shard_map/ready/pallas_call | solution.py:544
  25.6 0.0 collective-permute-done.9.refs_0_
  25.6 0.0 collective-permute-done.10.refs_1_
  25.6 2.0 %full.1 = (bf16[2,2,256,256]{3,2,1,0:T(8,128)(2,1)S(1)}, bf16[384,128]{1,0:T(8,128)(2,1)S(1)}, bf16[384,128]{1,0:T(8,128)(2,1)S(1)}) custom-call(s32[1]{0:T(128)} %bitcast.place_ref, bf16[2,2,512,256]{3,2,1,0:T(8,128)(2,1)S(1)} %get-tuple-element.43.hot_ref, bf16[2,2,512,128]{3,2,1,0:T(8,128)(2,1)S(1)} %get-tuple-element.44.here_ref, ...), custom_call_target="tpu_custom_call" | custom-call | flops 10000000000 | bytes 1048576 | tf_op jit(solution)/shard_map/full/pallas_call | solution.py:557
  27.6 4.3 %collective-permute-start.14 = (bf16[384,128]{1,0:T(8,128)(2,1)S(1)}, bf16[384,128]{1,0:T(8,128)(2,1)S(1)}, u32[]{:S(2)}, u32[]{:S(2)}) collective-permute-start(bf16[384,128]{1,0:T(8,128)(2,1)S(1)} %get-tuple-element.55), channel_id=1, source_target_pairs={{0,8},{1,9},{2,10},{3,11},{4,12},{5,13},{6,14},{7,15},{8,0},{9,1},... | collective-permute-start | bytes 294920 | tf_op jit(solution)/shard_map/ppermute | solution.py:449
  31.9 0.0 collective-permute-start.15
  31.9 0.2 collective-permute-start.11
  32.1 0.0 collective-permute-done.7.refs_1_.refs_2_
  32.1 0.0 collective-permute-done.6.refs_0_.refs_1_
  32.1 1.9 %full_near.1 = (bf16[384,128]{1,0:T(8,128)(2,1)S(1)}, bf16[192,128]{1,0:T(8,128)(2,1)S(1)}, bf16[192,128]{1,0:T(8,128)(2,1)S(1)}) custom-call(s32[1]{0:T(128)} %bitcast.place_ref, s32[16]{0:T(128)S(1)} %copy-done.2, s32[2,2,512]{2,1,0:T(2,128)S(1)} %copy-done.1, s32[2,2,512]{2,1,0:T(2,128)S(1)} %collective-permute-done.near_pairs_ref, ...), custom_call_target="tpu_custom_call" | custom-call | flops 500000000 | bytes 1048576 | tf_op jit(solution)/shard_map/full_near/pallas_call | solution.py:571
  34.1 0.4 collective-permute-start.12
  34.5 0.2 collective-permute-start.13
  34.7 0.0 collective-permute-done.11.refs_4_
  34.7 0.7 %collective-permute-done.12.refs_5_ = bf16[192,128]{1,0:T(8,128)(2,1)S(1)} collective-permute-done((bf16[192,128]{1,0:T(8,128)(2,1)S(1)}, bf16[192,128]{1,0:T(8,128)(2,1)S(1)}, u32[]{:S(2)}, u32[]{:S(2)}) %collective-permute-start.12) | collective-permute-done | bytes 49184 | tf_op jit(solution)/shard_map/ppermute | solution.py:449
  35.4 0.3 collective-permute-done.13.refs_6_
  35.7 0.0 copy-done
  35.7 1.8 %first_lags.1 = (f32[2,512,256]{2,1,0:T(8,128)S(1)}, bf16[2,96,512]{2,1,0:T(8,128)(2,1)S(1)}) custom-call(s32[1]{0:T(128)} %bitcast.place_ref, f32[256,256]{1,0:T(8,128)S(1)} %copy-done, bf16[256,128]{1,0:T(8,128)(2,1)S(1)} %get-tuple-element.38.after_ref.after_0.refs_0_, bf16[256,128]{1,0:T(8,128)(2,1)S(1)} %collective-permute-done.6.refs_0_.refs_1_, ...), custom_call_target="tpu_custom_call" | custom-call | flops 1000000 | bytes 1048576 | tf_op jit(solution)/shard_map/first_lags/pallas_call | solution.py:582
  37.5 1.8 %collective-permute-done.14.refs_0_ = bf16[384,128]{1,0:T(8,128)(2,1)S(1)} collective-permute-done((bf16[384,128]{1,0:T(8,128)(2,1)S(1)}, bf16[384,128]{1,0:T(8,128)(2,1)S(1)}, u32[]{:S(2)}, u32[]{:S(2)}) %collective-permute-start.14) | collective-permute-done | bytes 98336 | tf_op jit(solution)/shard_map/ppermute | solution.py:449
  39.2 1.1 %collective-permute-done.15.refs_1_ = bf16[384,128]{1,0:T(8,128)(2,1)S(1)} collective-permute-done((bf16[384,128]{1,0:T(8,128)(2,1)S(1)}, bf16[384,128]{1,0:T(8,128)(2,1)S(1)}, u32[]{:S(2)}, u32[]{:S(2)}) %collective-permute-start.15) | collective-permute-done | bytes 98336 | tf_op jit(solution)/shard_map/ppermute | solution.py:449
  40.3 1.2 %lags.1 = f32[2,512,256]{2,1,0:T(8,128)} custom-call(f32[2,512,256]{2,1,0:T(8,128)S(1)} %get-tuple-element.53.first_ref, bf16[2,96,512]{2,1,0:T(8,128)(2,1)S(1)} %get-tuple-element.54.table_ref, bf16[384,128]{1,0:T(8,128)(2,1)S(1)} %collective-permute-done.14.refs_0_, bf16[384,128]{1,0:T(8,128)(2,1)S(1)} %collective-permute-done.15.refs_1_), custom_call_target="tpu_custom_call" | custom-call | flops 1000000000 | bytes 1048576 | tf_op jit(solution)/shard_map/lags/pallas_call | solution.py:594
  (3 shorter events, 0.0 us)
Async XLA Ops:
  0.0 2.6 %collective-permute-start.1 = (bf16[3,2,4,64,256]{4,3,2,1,0:T(8,128)(2,1)}, bf16[3,2,4,64,256]{4,3,2,1,0:T(8,128)(2,1)S(1)}, u32[]{:S(2)}, u32[]{:S(2)}) collective-permute-start(bf16[3,2,4,64,256]{4,3,2,1,0:T(8,128)(2,1)} %bitcast.2), channel_id=1, source_target_pairs={{0,1},{1,0},{2,3},{3,2},{4,5},{5,4},{6,7},{7,6},{8,9},{9,8},{10,11... | collective-permute-start | bytes 2359304 | tf_op jit(solution)/shard_map/ppermute | solution.py:449
  0.5 2.1 %collective-permute-start = (s32[2,2,512]{2,1,0:T(2,128)}, s32[2,2,512]{2,1,0:T(2,128)S(1)}, u32[]{:S(2)}, u32[]{:S(2)}) collective-permute-start(s32[2,2,512]{2,1,0:T(2,128)} %own_pairs_ref.5), channel_id=1, source_target_pairs={{0,1},{1,0},{2,3},{3,2},{4,5},{5,4},{6,7},{7,6},{8,9},{9,8},{10,11... | collective-permute-start | bytes 24584 | tf_op jit(solution)/shard_map/ppermute | solution.py:449
  0.5 1.1 %copy-start.3 = (bf16[3,1,512,256]{3,2,1,0:T(8,128)(2,1)S(1)}, bf16[3,1,512,256]{3,2,1,0:T(8,128)(2,1)}, u32[]{:S(2)}) copy-start(bf16[3,1,512,256]{3,2,1,0:T(8,128)(2,1)} %param.4) | copy-start | bytes 2359300
  1.6 0.9 %copy-start.1 = (s32[2,2,512]{2,1,0:T(2,128)S(1)}, s32[2,2,512]{2,1,0:T(2,128)}, u32[]{:S(2)}) copy-start(s32[2,2,512]{2,1,0:T(2,128)} %own_pairs_ref.5) | copy-start | bytes 24580
  3.1 8.8 %collective-permute-start.2 = (bf16[480,128]{1,0:T(8,128)(2,1)S(1)}, bf16[480,128]{1,0:T(8,128)(2,1)S(1)}, u32[]{:S(2)}, u32[]{:S(2)}) collective-permute-start(bf16[480,128]{1,0:T(8,128)(2,1)S(1)} %get-tuple-element.35), channel_id=1, source_target_pairs={{0,2},{1,3},{2,0},{3,1},{4,6},{5,7},{6,4},{7,5},{8,10},{9,11},{10,... | collective-permute-start | bytes 368648 | tf_op jit(solution)/shard_map/ppermute | solution.py:449
  6.0 9.5 %collective-permute-start.3 = (bf16[480,128]{1,0:T(8,128)(2,1)S(1)}, bf16[480,128]{1,0:T(8,128)(2,1)S(1)}, u32[]{:S(2)}, u32[]{:S(2)}) collective-permute-start(bf16[480,128]{1,0:T(8,128)(2,1)S(1)} %get-tuple-element.36), channel_id=1, source_target_pairs={{0,4},{1,5},{2,6},{3,7},{4,0},{5,1},{6,2},{7,3},{8,12},{9,13},{10,... | collective-permute-start | bytes 368648 | tf_op jit(solution)/shard_map/ppermute | solution.py:449
  7.6 9.2 %collective-permute-start.4 = (bf16[480,128]{1,0:T(8,128)(2,1)S(1)}, bf16[480,128]{1,0:T(8,128)(2,1)S(1)}, u32[]{:S(2)}, u32[]{:S(2)}) collective-permute-start(bf16[480,128]{1,0:T(8,128)(2,1)S(1)} %get-tuple-element.37), channel_id=1, source_target_pairs={{0,6},{1,7},{2,4},{3,5},{4,2},{5,3},{6,0},{7,1},{8,14},{9,15},{10,... | collective-permute-start | bytes 368648 | tf_op jit(solution)/shard_map/ppermute | solution.py:449
  7.6 11.8 %collective-permute-start.5 = (bf16[320,128]{1,0:T(8,128)(2,1)S(1)}, bf16[320,128]{1,0:T(8,128)(2,1)S(1)}, u32[]{:S(2)}, u32[]{:S(2)}) collective-permute-start(bf16[320,128]{1,0:T(8,128)(2,1)S(1)} %get-tuple-element.39), channel_id=1, source_target_pairs={{0,8},{1,9},{2,10},{3,11},{4,12},{5,13},{6,14},{7,15},{8,0},{9,1},... | collective-permute-start | bytes 245768 | tf_op jit(solution)/shard_map/ppermute | solution.py:449
  10.6 12.8 %collective-permute-start.8 = (bf16[288,128]{1,0:T(8,128)(2,1)S(1)}, bf16[288,128]{1,0:T(8,128)(2,1)S(1)}, u32[]{:S(2)}, u32[]{:S(2)}) collective-permute-start(bf16[288,128]{1,0:T(8,128)(2,1)S(1)} %get-tuple-element.42), channel_id=1, source_target_pairs={{0,10},{1,11},{2,8},{3,9},{4,14},{5,15},{6,12},{7,13},{8,2},{9,3},... | collective-permute-start | bytes 221192 | tf_op jit(solution)/shard_map/ppermute | solution.py:449
  11.9 13.7 %collective-permute-start.9 = (bf16[288,128]{1,0:T(8,128)(2,1)S(1)}, bf16[288,128]{1,0:T(8,128)(2,1)S(1)}, u32[]{:S(2)}, u32[]{:S(2)}) collective-permute-start(bf16[288,128]{1,0:T(8,128)(2,1)S(1)} %get-tuple-element.46), channel_id=1, source_target_pairs={{0,12},{1,13},{2,14},{3,15},{4,8},{5,9},{6,10},{7,11},{8,4},{9,5},... | collective-permute-start | bytes 221192 | tf_op jit(solution)/shard_map/ppermute | solution.py:449
  15.5 10.1 %collective-permute-start.10 = (bf16[288,128]{1,0:T(8,128)(2,1)S(1)}, bf16[288,128]{1,0:T(8,128)(2,1)S(1)}, u32[]{:S(2)}, u32[]{:S(2)}) collective-permute-start(bf16[288,128]{1,0:T(8,128)(2,1)S(1)} %get-tuple-element.47), channel_id=1, source_target_pairs={{0,14},{1,15},{2,12},{3,13},{4,10},{5,11},{6,8},{7,9},{8,6},{9,7},... | collective-permute-start | bytes 221192 | tf_op jit(solution)/shard_map/ppermute | solution.py:449
  16.8 0.9 %copy-start.2 = (s32[16]{0:T(128)S(1)}, s32[16]{0:T(128)}, u32[]{:S(2)}) copy-start(s32[16]{0:T(128)} %counts_ref.7) | copy-start | bytes 196
  21.1 11.0 %collective-permute-start.7 = (bf16[256,128]{1,0:T(8,128)(2,1)S(1)}, bf16[256,128]{1,0:T(8,128)(2,1)S(1)}, u32[]{:S(2)}, u32[]{:S(2)}) collective-permute-start(bf16[256,128]{1,0:T(8,128)(2,1)S(1)} %get-tuple-element.41), channel_id=1, source_target_pairs={{0,9},{1,8},{2,11},{3,10},{4,13},{5,12},{6,15},{7,14},{8,1},{9,0},... | collective-permute-start | bytes 196616 | tf_op jit(solution)/shard_map/ppermute | solution.py:449
  21.2 10.9 %collective-permute-start.6 = (bf16[256,128]{1,0:T(8,128)(2,1)S(1)}, bf16[256,128]{1,0:T(8,128)(2,1)S(1)}, u32[]{:S(2)}, u32[]{:S(2)}) collective-permute-start(bf16[256,128]{1,0:T(8,128)(2,1)S(1)} %get-tuple-element.40.after_1), channel_id=1, source_target_pairs={{0,8},{1,9},{2,10},{3,11},{4,12},{5,13},{6,14},{7,15},{8,0},{9,1},... | collective-permute-start | bytes 196616 | tf_op jit(solution)/shard_map/ppermute | solution.py:449
  27.6 11.6 %collective-permute-start.14 = (bf16[384,128]{1,0:T(8,128)(2,1)S(1)}, bf16[384,128]{1,0:T(8,128)(2,1)S(1)}, u32[]{:S(2)}, u32[]{:S(2)}) collective-permute-start(bf16[384,128]{1,0:T(8,128)(2,1)S(1)} %get-tuple-element.55), channel_id=1, source_target_pairs={{0,8},{1,9},{2,10},{3,11},{4,12},{5,13},{6,14},{7,15},{8,0},{9,1},... | collective-permute-start | bytes 294920 | tf_op jit(solution)/shard_map/ppermute | solution.py:449
  31.9 8.4 %collective-permute-start.15 = (bf16[384,128]{1,0:T(8,128)(2,1)S(1)}, bf16[384,128]{1,0:T(8,128)(2,1)S(1)}, u32[]{:S(2)}, u32[]{:S(2)}) collective-permute-start(bf16[384,128]{1,0:T(8,128)(2,1)S(1)} %get-tuple-element.56), channel_id=1, source_target_pairs={{0,9},{1,8},{2,11},{3,10},{4,13},{5,12},{6,15},{7,14},{8,1},{9,0},... | collective-permute-start | bytes 294920 | tf_op jit(solution)/shard_map/ppermute | solution.py:449
  31.9 2.7 %collective-permute-start.11 = (bf16[256,128]{1,0:T(8,128)(2,1)S(1)}, bf16[256,128]{1,0:T(8,128)(2,1)S(1)}, u32[]{:S(2)}, u32[]{:S(2)}) collective-permute-start(bf16[256,128]{1,0:T(8,128)(2,1)S(1)} %get-tuple-element.50), channel_id=1, source_target_pairs={{0,1},{1,0},{2,3},{3,2},{4,5},{5,4},{6,7},{7,6},{8,9},{9,8},{10,11... | collective-permute-start | bytes 196616 | tf_op jit(solution)/shard_map/ppermute | solution.py:449
  32.1 3.6 %copy-start = (f32[256,256]{1,0:T(8,128)S(1)}, f32[256,256]{1,0:T(8,128)}, u32[]{:S(2)}) copy-start(f32[256,256]{1,0:T(8,128)} %constant.6.clone.inverse_ref) | copy-start | bytes 786436
  34.1 1.3 %collective-permute-start.12 = (bf16[192,128]{1,0:T(8,128)(2,1)S(1)}, bf16[192,128]{1,0:T(8,128)(2,1)S(1)}, u32[]{:S(2)}, u32[]{:S(2)}) collective-permute-start(bf16[192,128]{1,0:T(8,128)(2,1)S(1)} %get-tuple-element.51), channel_id=1, source_target_pairs={{0,1},{1,0},{2,3},{3,2},{4,5},{5,4},{6,7},{7,6},{8,9},{9,8},{10,11... | collective-permute-start | bytes 147464 | tf_op jit(solution)/shard_map/ppermute | solution.py:449
  34.5 1.2 %collective-permute-start.13 = (bf16[192,128]{1,0:T(8,128)(2,1)S(1)}, bf16[192,128]{1,0:T(8,128)(2,1)S(1)}, u32[]{:S(2)}, u32[]{:S(2)}) collective-permute-start(bf16[192,128]{1,0:T(8,128)(2,1)S(1)} %get-tuple-element.52), channel_id=1, source_target_pairs={{0,1},{1,0},{2,3},{3,2},{4,5},{5,4},{6,7},{7,6},{8,9},{9,8},{10,11... | collective-permute-start | bytes 147464 | tf_op jit(solution)/shard_map/ppermute | solution.py:449

commit v19 on v18

--- a/solution.py
+++ b/solution.py
@@ -119,15 +119,16 @@
     for mg in range(groups):
         spectra = station_spectra(windows_ref, group ^ mg, table)
         side, cross = piece_refs[mg], piece_refs[groups + mg]
+        full, start = (side, 2 * part_rows) if mg < groups - 1 else (piece_refs[2 * groups], 0)
         side[:part_rows] = part_ref[mg]
-        side[2 * part_rows : 2 * part_rows + full_rows] = full_ref[mg]
+        full[start : start + full_rows] = full_ref[mg]
         cross[:full_rows] = full_ref[groups + mg]
         for comp in range(COMPS):
             lanes = spectra[comp]
             at = part_rows + comp * 2 * PART
             side[at : at + 2 * PART] = lanes[: 2 * PART]
-            at = 2 * part_rows + full_rows + comp * 2 * FULL
-            side[at : at + 2 * FULL] = lanes[2 * PART : 2 * PART + 2 * FULL]
+            at = start + full_rows + comp * 2 * FULL
+            full[at : at + 2 * FULL] = lanes[2 * PART : 2 * PART + 2 * FULL]
             at = full_rows + comp * 2 * FULL
             cross[at : at + 2 * FULL] = lanes[2 * PART + 2 * FULL :]
 
@@ -479,16 +480,19 @@
     listing = 2 * pairs.size // LANES
     pieces = pl.pallas_call(
         near_spectra_kernel,
-        out_shape=[shape(2 * (part_rows + full_rows), LANES)] * groups
-        + [shape(2 * full_rows + listing * (mg == 0), LANES) for mg in range(groups)],
+        out_shape=[shape(2 * (part_rows + full_rows), LANES)] * (groups - 1)
+        + [shape(2 * part_rows, LANES)]
+        + [shape(2 * full_rows + listing * (mg == 0), LANES) for mg in range(groups)]
+        + [shape(2 * full_rows, LANES)],
         in_specs=[smem] + [vmem] * 6,
-        out_specs=[vmem] * (2 * groups),
+        out_specs=[vmem] * (2 * groups + 1),
         compiler_params=params,
         cost_estimate=cost(1),
         name="near_spectra",
     )(place, pairs, near_pairs, table, part_spectra, full_spectra, near_windows)
     arrived = [pieces[0]] + [swap(pieces[m], 2 * m) for m in range(1, 2 * groups)]
     sides, far = arrived[:groups], arrived[groups:]
+    side_rest = swap(pieces[2 * groups], 2 * (groups - 1))
 
     early, late = far[: groups - 2], far[groups - 2 :]
     part_packed = shape(packed_rows(count, PART), LANES)
@@ -529,7 +533,7 @@
     )(place, counts, far[0], part_flat, part_0)
     part_1 = swap(part_1, 1)
     sums = pl.pallas_call(
-        functools.partial(early_kernel, groups),
+        functools.partial(early_kernel, groups - 1),
         out_shape=shape(2 * SLOTS * FULL, LANES, dtype=jnp.float32),
         in_specs=[pl.BlockSpec(memory_space=pl.ANY)] * 2 + [vmem] * (groups + len(early)),
         out_specs=vmem,
@@ -539,7 +543,7 @@
         compiler_params=params,
         cost_estimate=cost(0.001),
         name="early",
-    )(part_0, part_2, *sides, *early)
+    )(part_0, part_2, *sides[:-1], *early, side_rest)
     part_2, part_3 = swap(part_2, half), swap(part_3, half + 1)
     ready = pl.pallas_call(
         ready_kernel,

time: 41.7 us -> 44.5 us (1.067)
  waiting for transfers between devices: 5.5 us -> 7.75 us
  starting transfers between devices: 20.4 us -> 20.9 us
    ppermute x16 -> x17, waiting for transfers between devices: 5.5 us -> 7.75 us  [swap(): return lax.ppermute(x, 'cell', [(i, i ^ mask) for i in range(cells)])]
    ppermute x16 -> x17, starting transfers between devices: 20.4 us -> 20.9 us  [swap(): return lax.ppermute(x, 'cell', [(i, i ^ mask) for i in range(cells)])]
  transfers between devices with their start and end apart: 16 -> 17, of which waited for: 6 -> 5; matrix products, arithmetic and copies ran while one was open for 0% -> 0% of each run, Pallas kernels for 31% -> 29%
where the time goes in v19:
time: 44.5 us; the launch traced here: 44.3 us
  starting transfers between devices  20.9 us (47%)
  Pallas kernels  14.4 us (32%)
  waiting for transfers between devices  7.75 us (17%)
  local copies, waits for them, and re-layouts  1.15 us (3%)
    ppermute x17, starting transfers between devices, swap(): return lax.ppermute(x, 'cell', [(i, i ^ mask) for i in range(cells)])  20.9 us
    ppermute x17, waiting for transfers between devices, swap(): return lax.ppermute(x, 'cell', [(i, i ^ mask) for i in range(cells)])  7.75 us
    pallas_call x1, Pallas kernels, on_device(): pl.pallas_call(functools.partial(full_kernel, cells), out_shape=[full_blo...  2.01 us
    pallas_call x1, Pallas kernels, on_device(): pl.pallas_call(functools.partial(near_kernel, FULL, 2), out_shape=[full_p...  1.95 us
    pallas_call x1, Pallas kernels, on_device(): pl.pallas_call(functools.partial(first_lags_kernel, groups), out_shape=[s...  1.77 us
    pallas_call x1, Pallas kernels, on_device(): pl.pallas_call(functools.partial(far_kernel, PART), out_shape=[part_packe...  1.69 us
    pallas_call x1, Pallas kernels, on_device(): pl.pallas_call(functools.partial(near_kernel, PART, 1), out_shape=[part_p...  1.69 us
    pallas_call x1, Pallas kernels, on_device(): pl.pallas_call(ready_kernel, out_shape=[shape(2, 2, count, full_blocks.sh...  1.32 us
  transfers between devices with their start and end apart: 17, of which 5 were waited for; matrix products, arithmetic and copies ran while one was open for 0% of the time, Pallas kernels for 29%

profile of v19, /device:TPU:0, one launch (start us, length us, event | category | flops | bytes accessed | tf_op | source)
XLA Modules:
  0.0 44.3 jit_solution(7600547811916278781)
XLA Ops:
  0.0 0.5 %collective-permute-start.1 = (bf16[3,2,4,64,256]{4,3,2,1,0:T(8,128)(2,1)}, bf16[3,2,4,64,256]{4,3,2,1,0:T(8,128)(2,1)S(1)}, u32[]{:S(2)}, u32[]{:S(2)}) collective-permute-start(bf16[3,2,4,64,256]{4,3,2,1,0:T(8,128)(2,1)} %bitcast.2), channel_id=1, source_target_pairs={{0,1},{1,0},{2,3},{3,2},{4,5},{5,4},{6,7},{7,6},{8,9},{9,8},{10,11... | collective-permute-start | bytes 2359304 | tf_op jit(solution)/shard_map/ppermute | solution.py:450
  0.5 0.1 collective-permute-start
  0.5 1.1 %copy-done.3 = bf16[3,1,512,256]{3,2,1,0:T(8,128)(2,1)S(1)} copy-done((bf16[3,1,512,256]{3,2,1,0:T(8,128)(2,1)S(1)}, bf16[3,1,512,256]{3,2,1,0:T(8,128)(2,1)}, u32[]{:S(2)}) %copy-start.3) | copy-done | bytes 786456
  1.6 0.6 %own_spectra.1 = (bf16[4,96,128]{2,1,0:T(8,128)(2,1)S(1)}, bf16[8,144,128]{2,1,0:T(8,128)(2,1)S(1)}, bf16[128,256]{1,0:T(8,128)(2,1)S(1)}) custom-call(s32[1]{0:T(128)} %bitcast.place_ref, bf16[3,2,4,64,256]{4,3,2,1,0:T(8,128)(2,1)S(1)} %bitcast.3), custom_call_target="tpu_custom_call" | custom-call | flops 1000000000 | bytes 1048576 | tf_op jit(solution)/shard_map/own_spectra/pallas_call | solution.py:467
  2.2 0.4 collective-permute-done.near_pairs_ref
  2.6 0.0 collective-permute-done.1.windows_ref
  2.6 0.5 %near_spectra.1 = (bf16[480,128]{1,0:T(8,128)(2,1)S(1)}, bf16[480,128]{1,0:T(8,128)(2,1)S(1)}, bf16[480,128]{1,0:T(8,128)(2,1)S(1)}, bf16[192,128]{1,0:T(8,128)(...) custom-call(s32[1]{0:T(128)} %bitcast.place_ref, ...), custom_call_target="tpu_custom_call" | custom-call | flops 1000000000 | bytes 1048576 | tf_op jit(solution)/shard_map/near_spectra/pallas_call | solution.py:481
  3.1 3.0 %collective-permute-start.2 = (bf16[480,128]{1,0:T(8,128)(2,1)S(1)}, bf16[480,128]{1,0:T(8,128)(2,1)S(1)}, u32[]{:S(2)}, u32[]{:S(2)}) collective-permute-start(bf16[480,128]{1,0:T(8,128)(2,1)S(1)} %get-tuple-element.36), channel_id=1, source_target_pairs={{0,2},{1,3},{2,0},{3,1},{4,6},{5,7},{6,4},{7,5},{8,10},{9,11},{10,... | collective-permute-start | bytes 368648 | tf_op jit(solution)/shard_map/ppermute | solution.py:450
  6.0 1.6 %collective-permute-start.3 = (bf16[480,128]{1,0:T(8,128)(2,1)S(1)}, bf16[480,128]{1,0:T(8,128)(2,1)S(1)}, u32[]{:S(2)}, u32[]{:S(2)}) collective-permute-start(bf16[480,128]{1,0:T(8,128)(2,1)S(1)} %get-tuple-element.37), channel_id=1, source_target_pairs={{0,4},{1,5},{2,6},{3,7},{4,0},{5,1},{6,2},{7,3},{8,12},{9,13},{10,... | collective-permute-start | bytes 368648 | tf_op jit(solution)/shard_map/ppermute | solution.py:450
  7.6 2.6 %collective-permute-start.5 = (bf16[320,128]{1,0:T(8,128)(2,1)S(1)}, bf16[320,128]{1,0:T(8,128)(2,1)S(1)}, u32[]{:S(2)}, u32[]{:S(2)}) collective-permute-start(bf16[320,128]{1,0:T(8,128)(2,1)S(1)} %get-tuple-element.40), channel_id=1, source_target_pairs={{0,8},{1,9},{2,10},{3,11},{4,12},{5,13},{6,14},{7,15},{8,0},{9,1},... | collective-permute-start | bytes 245768 | tf_op jit(solution)/shard_map/ppermute | solution.py:450
  10.2 0.4 collective-permute-start.4
  10.6 1.3 %collective-permute-start.8 = (bf16[288,128]{1,0:T(8,128)(2,1)S(1)}, bf16[288,128]{1,0:T(8,128)(2,1)S(1)}, u32[]{:S(2)}, u32[]{:S(2)}) collective-permute-start(bf16[288,128]{1,0:T(8,128)(2,1)S(1)} %get-tuple-element.43), channel_id=1, source_target_pairs={{0,10},{1,11},{2,8},{3,9},{4,14},{5,15},{6,12},{7,13},{8,2},{9,3},... | collective-permute-start | bytes 221192 | tf_op jit(solution)/shard_map/ppermute | solution.py:450
  11.9 3.5 %collective-permute-done.4.refs_3_ = bf16[192,128]{1,0:T(8,128)(2,1)S(1)} collective-permute-done((bf16[192,128]{1,0:T(8,128)(2,1)S(1)}, bf16[192,128]{1,0:T(8,128)(2,1)S(1)}, u32[]{:S(2)}, u32[]{:S(2)}) %collective-permute-start.4) | collective-permute-done | bytes 49184 | tf_op jit(solution)/shard_map/ppermute | solution.py:450
  15.3 2.0 %collective-permute-start.9 = (bf16[288,128]{1,0:T(8,128)(2,1)S(1)}, bf16[288,128]{1,0:T(8,128)(2,1)S(1)}, u32[]{:S(2)}, u32[]{:S(2)}) collective-permute-start(bf16[288,128]{1,0:T(8,128)(2,1)S(1)} %get-tuple-element.44), channel_id=1, source_target_pairs={{0,6},{1,7},{2,4},{3,5},{4,2},{5,3},{6,0},{7,1},{8,14},{9,15},{10,... | collective-permute-start | bytes 221192 | tf_op jit(solution)/shard_map/ppermute | solution.py:450
  17.4 0.0 collective-permute-done.2.refs_1_
  17.4 2.4 %collective-permute-start.10 = (bf16[288,128]{1,0:T(8,128)(2,1)S(1)}, bf16[288,128]{1,0:T(8,128)(2,1)S(1)}, u32[]{:S(2)}, u32[]{:S(2)}) collective-permute-start(bf16[288,128]{1,0:T(8,128)(2,1)S(1)} %get-tuple-element.48), channel_id=1, source_target_pairs={{0,12},{1,13},{2,14},{3,15},{4,8},{5,9},{6,10},{7,11},{8,4},{9,5},... | collective-permute-start | bytes 221192 | tf_op jit(solution)/shard_map/ppermute | solution.py:450
  19.7 0.0 collective-permute-done.3.refs_2_
  19.7 1.4 %collective-permute-start.11 = (bf16[288,128]{1,0:T(8,128)(2,1)S(1)}, bf16[288,128]{1,0:T(8,128)(2,1)S(1)}, u32[]{:S(2)}, u32[]{:S(2)}) collective-permute-start(bf16[288,128]{1,0:T(8,128)(2,1)S(1)} %get-tuple-element.49), channel_id=1, source_target_pairs={{0,14},{1,15},{2,12},{3,13},{4,10},{5,11},{6,8},{7,9},{8,6},{9,7},... | collective-permute-start | bytes 221192 | tf_op jit(solution)/shard_map/ppermute | solution.py:450
  21.2 0.9 %part.1.flat_ref = bf16[2,2,128,256]{3,2,1,0:T(8,128)(2,1)S(1)} custom-call(bf16[480,128]{1,0:T(8,128)(2,1)S(1)} %get-tuple-element.35.refs_0_, bf16[480,128]{1,0:T(8,128)(2,1)S(1)} %collective-permute-done.2.refs_1_, bf16[480,128]{1,0:T(8,128)(2,1)S(1)} %collective-permute-done.3.refs_2_, bf16[192,128]{1,0:T(8,128)(2,1)S(1)} %collective-permute-done.4.refs_3_), custom_call_target="tpu_custom_call" | custom-call | flops 1000000 | bytes 1048576 | tf_op jit(solution)/shard_map/part/pallas_call | solution.py:503
  22.1 1.7 %part_near.1 = (bf16[256,128]{1,0:T(8,128)(2,1)S(1)}, bf16[256,128]{1,0:T(8,128)(2,1)S(1)}) custom-call(s32[1]{0:T(128)} %bitcast.place_ref, s32[16]{0:T(128)S(1)} %copy-done.2, s32[2,2,512]{2,1,0:T(2,128)S(1)} %copy-done.1, s32[2,2,512]{2,1,0:T(2,128)S(1)} %collective-permute-done.near_pairs_ref, bf16[2,2,128,256]{3,2,1,0:T(8,128)(2,1)S(1)} %part.1.flat_ref), custom_call_target="tpu_custom_call" | custom-call | flops 1000000 | bytes 1048576 | tf_op jit(solution)/shard_map/part_near/pallas_call | solution.py:516
  23.8 0.0 collective-permute-done.5.listed_ref.refs_3_
  23.8 1.7 %part_far.1 = (bf16[256,128]{1,0:T(8,128)(2,1)S(1)}, bf16[256,128]{1,0:T(8,128)(2,1)S(1)}) custom-call(s32[1]{0:T(128)} %bitcast.place_ref, s32[16]{0:T(128)S(1)} %copy-done.2, bf16[320,128]{1,0:T(8,128)(2,1)S(1)} %collective-permute-done.5.listed_ref.refs_3_, bf16[2,2,128,256]{3,2,1,0:T(8,128)(2,1)S(1)} %part.1.flat_ref, ...), custom_call_target="tpu_custom_call" | custom-call | flops 1000000000 | bytes 1048576 | tf_op jit(solution)/shard_map/part_far/pallas_call | solution.py:525
  25.5 0.1 collective-permute-start.7
  25.5 0.0 collective-permute-done.8.refs_4_
  25.6 0.1 collective-permute-start.6
  25.6 0.0 collective-permute-done.9.refs_5_
  25.6 0.8 %early.1.after_ref.before_ref = f32[1536,128]{1,0:T(8,128)S(1)} custom-call(bf16[256,128]{1,0:T(8,128)(2,1)S(1)} %get-tuple-element.39.after_ref.after_0.refs_0_, bf16[256,128]{1,0:T(8,128)(2,1)S(1)} %get-tuple-element.41.after_1, bf16[480,128]{1,0:T(8,128)(2,1)S(1)} %get-tuple-element.35.refs_0_, bf16[480,128]{1,0:T(8,128)(2,1)S(1)} %collective-permute-done.2.refs_1_, ...), custom_call_target="tpu_custom_call" | custom-call | flops 1000000 | bytes 1048576 | tf_op jit(solution)/shard_map/early/pallas_call | solution.py:535
  26.5 1.3 %ready.1 = (bf16[2,2,512,256]{3,2,1,0:T(8,128)(2,1)S(1)}, bf16[2,2,512,128]{3,2,1,0:T(8,128)(2,1)S(1)}, bf16[4,512,128]{2,1,0:T(8,128)(2,1)S(1)}) custom-call(s32[1]{0:T(128)} %bitcast.place_ref, s32[16]{0:T(128)S(1)} %copy-done.2, bf16[320,128]{1,0:T(8,128)(2,1)S(1)} %collective-permute-done.5.listed_ref.refs_3_, f32[1536,128]{1,0:T(8,128)S(1)} %early.1.after_ref.before_ref), custom_call_target="tpu_custom_call" | custom-call | flops 1000000 | bytes 1048576 | tf_op jit(solution)/shard_map/ready/pallas_call | solution.py:548
  27.8 0.0 collective-permute-done.10.refs_0_
  27.8 0.0 collective-permute-done.11.refs_1_
  27.8 2.0 %full.1 = (bf16[2,2,256,256]{3,2,1,0:T(8,128)(2,1)S(1)}, bf16[384,128]{1,0:T(8,128)(2,1)S(1)}, bf16[384,128]{1,0:T(8,128)(2,1)S(1)}) custom-call(s32[1]{0:T(128)} %bitcast.place_ref, bf16[2,2,512,256]{3,2,1,0:T(8,128)(2,1)S(1)} %get-tuple-element.45.hot_ref, bf16[2,2,512,128]{3,2,1,0:T(8,128)(2,1)S(1)} %get-tuple-element.46.here_ref, ...), custom_call_target="tpu_custom_call" | custom-call | flops 10000000000 | bytes 1048576 | tf_op jit(solution)/shard_map/full/pallas_call | solution.py:561
  29.8 3.0 %collective-permute-start.15 = (bf16[384,128]{1,0:T(8,128)(2,1)S(1)}, bf16[384,128]{1,0:T(8,128)(2,1)S(1)}, u32[]{:S(2)}, u32[]{:S(2)}) collective-permute-start(bf16[384,128]{1,0:T(8,128)(2,1)S(1)} %get-tuple-element.57), channel_id=1, source_target_pairs={{0,8},{1,9},{2,10},{3,11},{4,12},{5,13},{6,14},{7,15},{8,0},{9,1},... | collective-permute-start | bytes 294920 | tf_op jit(solution)/shard_map/ppermute | solution.py:450
  32.8 2.0 %collective-permute-start.16 = (bf16[384,128]{1,0:T(8,128)(2,1)S(1)}, bf16[384,128]{1,0:T(8,128)(2,1)S(1)}, u32[]{:S(2)}, u32[]{:S(2)}) collective-permute-start(bf16[384,128]{1,0:T(8,128)(2,1)S(1)} %get-tuple-element.58), channel_id=1, source_target_pairs={{0,9},{1,8},{2,11},{3,10},{4,13},{5,12},{6,15},{7,14},{8,1},{9,0},... | collective-permute-start | bytes 294920 | tf_op jit(solution)/shard_map/ppermute | solution.py:450
  34.8 0.0 collective-permute-start.12
  34.8 0.0 collective-permute-done.7.refs_1_.refs_2_
  34.8 0.0 collective-permute-done.6.refs_0_.refs_1_
  34.8 0.0 copy-start
  34.8 1.9 %full_near.1 = (bf16[384,128]{1,0:T(8,128)(2,1)S(1)}, bf16[192,128]{1,0:T(8,128)(2,1)S(1)}, bf16[192,128]{1,0:T(8,128)(2,1)S(1)}) custom-call(s32[1]{0:T(128)} %bitcast.place_ref, s32[16]{0:T(128)S(1)} %copy-done.2, s32[2,2,512]{2,1,0:T(2,128)S(1)} %copy-done.1, s32[2,2,512]{2,1,0:T(2,128)S(1)} %collective-permute-done.near_pairs_ref, ...), custom_call_target="tpu_custom_call" | custom-call | flops 500000000 | bytes 1048576 | tf_op jit(solution)/shard_map/full_near/pallas_call | solution.py:575
  36.8 0.6 %collective-permute-start.13 = (bf16[192,128]{1,0:T(8,128)(2,1)S(1)}, bf16[192,128]{1,0:T(8,128)(2,1)S(1)}, u32[]{:S(2)}, u32[]{:S(2)}) collective-permute-start(bf16[192,128]{1,0:T(8,128)(2,1)S(1)} %get-tuple-element.53), channel_id=1, source_target_pairs={{0,1},{1,0},{2,3},{3,2},{4,5},{5,4},{6,7},{7,6},{8,9},{9,8},{10,11... | collective-permute-start | bytes 147464 | tf_op jit(solution)/shard_map/ppermute | solution.py:450
  37.3 0.1 collective-permute-start.14
  37.4 0.0 collective-permute-done.12.refs_4_
  37.4 0.8 %collective-permute-done.13.refs_5_ = bf16[192,128]{1,0:T(8,128)(2,1)S(1)} collective-permute-done((bf16[192,128]{1,0:T(8,128)(2,1)S(1)}, bf16[192,128]{1,0:T(8,128)(2,1)S(1)}, u32[]{:S(2)}, u32[]{:S(2)}) %collective-permute-start.13) | collective-permute-done | bytes 49184 | tf_op jit(solution)/shard_map/ppermute | solution.py:450
  38.2 0.3 collective-permute-done.14.refs_6_
  38.6 0.0 copy-done
  38.6 1.8 %first_lags.1 = (f32[2,512,256]{2,1,0:T(8,128)S(1)}, bf16[2,96,512]{2,1,0:T(8,128)(2,1)S(1)}) custom-call(s32[1]{0:T(128)} %bitcast.place_ref, f32[256,256]{1,0:T(8,128)S(1)} %copy-done, bf16[256,128]{1,0:T(8,128)(2,1)S(1)} %get-tuple-element.39.after_ref.after_0.refs_0_, bf16[256,128]{1,0:T(8,128)(2,1)S(1)} %collective-permute-done.6.refs_0_.refs_1_, ...), custom_call_target="tpu_custom_call" | custom-call | flops 1000000 | bytes 1048576 | tf_op jit(solution)/shard_map/first_lags/pallas_call | solution.py:586
  40.3 0.0 collective-permute-done.15.refs_0_
  40.3 2.8 %collective-permute-done.16.refs_1_ = bf16[384,128]{1,0:T(8,128)(2,1)S(1)} collective-permute-done((bf16[384,128]{1,0:T(8,128)(2,1)S(1)}, bf16[384,128]{1,0:T(8,128)(2,1)S(1)}, u32[]{:S(2)}, u32[]{:S(2)}) %collective-permute-start.16) | collective-permute-done | bytes 98336 | tf_op jit(solution)/shard_map/ppermute | solution.py:450
  43.1 1.2 %lags.1 = f32[2,512,256]{2,1,0:T(8,128)} custom-call(f32[2,512,256]{2,1,0:T(8,128)S(1)} %get-tuple-element.55.first_ref, bf16[2,96,512]{2,1,0:T(8,128)(2,1)S(1)} %get-tuple-element.56.table_ref, bf16[384,128]{1,0:T(8,128)(2,1)S(1)} %collective-permute-done.15.refs_0_, bf16[384,128]{1,0:T(8,128)(2,1)S(1)} %collective-permute-done.16.refs_1_), custom_call_target="tpu_custom_call" | custom-call | flops 1000000000 | bytes 1048576 | tf_op jit(solution)/shard_map/lags/pallas_call | solution.py:598
  (5 shorter events, 0.0 us)
Async XLA Ops:
  0.0 2.6 %collective-permute-start.1 = (bf16[3,2,4,64,256]{4,3,2,1,0:T(8,128)(2,1)}, bf16[3,2,4,64,256]{4,3,2,1,0:T(8,128)(2,1)S(1)}, u32[]{:S(2)}, u32[]{:S(2)}) collective-permute-start(bf16[3,2,4,64,256]{4,3,2,1,0:T(8,128)(2,1)} %bitcast.2), channel_id=1, source_target_pairs={{0,1},{1,0},{2,3},{3,2},{4,5},{5,4},{6,7},{7,6},{8,9},{9,8},{10,11... | collective-permute-start | bytes 2359304 | tf_op jit(solution)/shard_map/ppermute | solution.py:450
  0.5 2.1 %collective-permute-start = (s32[2,2,512]{2,1,0:T(2,128)}, s32[2,2,512]{2,1,0:T(2,128)S(1)}, u32[]{:S(2)}, u32[]{:S(2)}) collective-permute-start(s32[2,2,512]{2,1,0:T(2,128)} %own_pairs_ref.5), channel_id=1, source_target_pairs={{0,1},{1,0},{2,3},{3,2},{4,5},{5,4},{6,7},{7,6},{8,9},{9,8},{10,11... | collective-permute-start | bytes 24584 | tf_op jit(solution)/shard_map/ppermute | solution.py:450
  0.5 1.1 %copy-start.3 = (bf16[3,1,512,256]{3,2,1,0:T(8,128)(2,1)S(1)}, bf16[3,1,512,256]{3,2,1,0:T(8,128)(2,1)}, u32[]{:S(2)}) copy-start(bf16[3,1,512,256]{3,2,1,0:T(8,128)(2,1)} %param.4) | copy-start | bytes 2359300
  1.6 0.9 %copy-start.1 = (s32[2,2,512]{2,1,0:T(2,128)S(1)}, s32[2,2,512]{2,1,0:T(2,128)}, u32[]{:S(2)}) copy-start(s32[2,2,512]{2,1,0:T(2,128)} %own_pairs_ref.5) | copy-start | bytes 24580
  3.1 14.3 %collective-permute-start.2 = (bf16[480,128]{1,0:T(8,128)(2,1)S(1)}, bf16[480,128]{1,0:T(8,128)(2,1)S(1)}, u32[]{:S(2)}, u32[]{:S(2)}) collective-permute-start(bf16[480,128]{1,0:T(8,128)(2,1)S(1)} %get-tuple-element.36), channel_id=1, source_target_pairs={{0,2},{1,3},{2,0},{3,1},{4,6},{5,7},{6,4},{7,5},{8,10},{9,11},{10,... | collective-permute-start | bytes 368648 | tf_op jit(solution)/shard_map/ppermute | solution.py:450
  6.0 13.7 %collective-permute-start.3 = (bf16[480,128]{1,0:T(8,128)(2,1)S(1)}, bf16[480,128]{1,0:T(8,128)(2,1)S(1)}, u32[]{:S(2)}, u32[]{:S(2)}) collective-permute-start(bf16[480,128]{1,0:T(8,128)(2,1)S(1)} %get-tuple-element.37), channel_id=1, source_target_pairs={{0,4},{1,5},{2,6},{3,7},{4,0},{5,1},{6,2},{7,3},{8,12},{9,13},{10,... | collective-permute-start | bytes 368648 | tf_op jit(solution)/shard_map/ppermute | solution.py:450
  7.6 16.2 %collective-permute-start.5 = (bf16[320,128]{1,0:T(8,128)(2,1)S(1)}, bf16[320,128]{1,0:T(8,128)(2,1)S(1)}, u32[]{:S(2)}, u32[]{:S(2)}) collective-permute-start(bf16[320,128]{1,0:T(8,128)(2,1)S(1)} %get-tuple-element.40), channel_id=1, source_target_pairs={{0,8},{1,9},{2,10},{3,11},{4,12},{5,13},{6,14},{7,15},{8,0},{9,1},... | collective-permute-start | bytes 245768 | tf_op jit(solution)/shard_map/ppermute | solution.py:450
  10.2 5.1 %collective-permute-start.4 = (bf16[192,128]{1,0:T(8,128)(2,1)S(1)}, bf16[192,128]{1,0:T(8,128)(2,1)S(1)}, u32[]{:S(2)}, u32[]{:S(2)}) collective-permute-start(bf16[192,128]{1,0:T(8,128)(2,1)S(1)} %get-tuple-element.38), channel_id=1, source_target_pairs={{0,6},{1,7},{2,4},{3,5},{4,2},{5,3},{6,0},{7,1},{8,14},{9,15},{10,... | collective-permute-start | bytes 147464 | tf_op jit(solution)/shard_map/ppermute | solution.py:450
  10.6 15.0 %collective-permute-start.8 = (bf16[288,128]{1,0:T(8,128)(2,1)S(1)}, bf16[288,128]{1,0:T(8,128)(2,1)S(1)}, u32[]{:S(2)}, u32[]{:S(2)}) collective-permute-start(bf16[288,128]{1,0:T(8,128)(2,1)S(1)} %get-tuple-element.43), channel_id=1, source_target_pairs={{0,10},{1,11},{2,8},{3,9},{4,14},{5,15},{6,12},{7,13},{8,2},{9,3},... | collective-permute-start | bytes 221192 | tf_op jit(solution)/shard_map/ppermute | solution.py:450
  15.3 10.3 %collective-permute-start.9 = (bf16[288,128]{1,0:T(8,128)(2,1)S(1)}, bf16[288,128]{1,0:T(8,128)(2,1)S(1)}, u32[]{:S(2)}, u32[]{:S(2)}) collective-permute-start(bf16[288,128]{1,0:T(8,128)(2,1)S(1)} %get-tuple-element.44), channel_id=1, source_target_pairs={{0,6},{1,7},{2,4},{3,5},{4,2},{5,3},{6,0},{7,1},{8,14},{9,15},{10,... | collective-permute-start | bytes 221192 | tf_op jit(solution)/shard_map/ppermute | solution.py:450
  17.4 10.4 %collective-permute-start.10 = (bf16[288,128]{1,0:T(8,128)(2,1)S(1)}, bf16[288,128]{1,0:T(8,128)(2,1)S(1)}, u32[]{:S(2)}, u32[]{:S(2)}) collective-permute-start(bf16[288,128]{1,0:T(8,128)(2,1)S(1)} %get-tuple-element.48), channel_id=1, source_target_pairs={{0,12},{1,13},{2,14},{3,15},{4,8},{5,9},{6,10},{7,11},{8,4},{9,5},... | collective-permute-start | bytes 221192 | tf_op jit(solution)/shard_map/ppermute | solution.py:450
  19.7 8.1 %collective-permute-start.11 = (bf16[288,128]{1,0:T(8,128)(2,1)S(1)}, bf16[288,128]{1,0:T(8,128)(2,1)S(1)}, u32[]{:S(2)}, u32[]{:S(2)}) collective-permute-start(bf16[288,128]{1,0:T(8,128)(2,1)S(1)} %get-tuple-element.49), channel_id=1, source_target_pairs={{0,14},{1,15},{2,12},{3,13},{4,10},{5,11},{6,8},{7,9},{8,6},{9,7},... | collective-permute-start | bytes 221192 | tf_op jit(solution)/shard_map/ppermute | solution.py:450
  21.2 0.9 %copy-start.2 = (s32[16]{0:T(128)S(1)}, s32[16]{0:T(128)}, u32[]{:S(2)}) copy-start(s32[16]{0:T(128)} %counts_ref.7) | copy-start | bytes 196
  25.5 9.3 %collective-permute-start.7 = (bf16[256,128]{1,0:T(8,128)(2,1)S(1)}, bf16[256,128]{1,0:T(8,128)(2,1)S(1)}, u32[]{:S(2)}, u32[]{:S(2)}) collective-permute-start(bf16[256,128]{1,0:T(8,128)(2,1)S(1)} %get-tuple-element.42), channel_id=1, source_target_pairs={{0,9},{1,8},{2,11},{3,10},{4,13},{5,12},{6,15},{7,14},{8,1},{9,0},... | collective-permute-start | bytes 196616 | tf_op jit(solution)/shard_map/ppermute | solution.py:450
  25.6 9.2 %collective-permute-start.6 = (bf16[256,128]{1,0:T(8,128)(2,1)S(1)}, bf16[256,128]{1,0:T(8,128)(2,1)S(1)}, u32[]{:S(2)}, u32[]{:S(2)}) collective-permute-start(bf16[256,128]{1,0:T(8,128)(2,1)S(1)} %get-tuple-element.41.after_1), channel_id=1, source_target_pairs={{0,8},{1,9},{2,10},{3,11},{4,12},{5,13},{6,14},{7,15},{8,0},{9,1},... | collective-permute-start | bytes 196616 | tf_op jit(solution)/shard_map/ppermute | solution.py:450
  29.8 10.5 %collective-permute-start.15 = (bf16[384,128]{1,0:T(8,128)(2,1)S(1)}, bf16[384,128]{1,0:T(8,128)(2,1)S(1)}, u32[]{:S(2)}, u32[]{:S(2)}) collective-permute-start(bf16[384,128]{1,0:T(8,128)(2,1)S(1)} %get-tuple-element.57), channel_id=1, source_target_pairs={{0,8},{1,9},{2,10},{3,11},{4,12},{5,13},{6,14},{7,15},{8,0},{9,1},... | collective-permute-start | bytes 294920 | tf_op jit(solution)/shard_map/ppermute | solution.py:450
  32.8 10.3 %collective-permute-start.16 = (bf16[384,128]{1,0:T(8,128)(2,1)S(1)}, bf16[384,128]{1,0:T(8,128)(2,1)S(1)}, u32[]{:S(2)}, u32[]{:S(2)}) collective-permute-start(bf16[384,128]{1,0:T(8,128)(2,1)S(1)} %get-tuple-element.58), channel_id=1, source_target_pairs={{0,9},{1,8},{2,11},{3,10},{4,13},{5,12},{6,15},{7,14},{8,1},{9,0},... | collective-permute-start | bytes 294920 | tf_op jit(solution)/shard_map/ppermute | solution.py:450
  34.8 2.6 %collective-permute-start.12 = (bf16[256,128]{1,0:T(8,128)(2,1)S(1)}, bf16[256,128]{1,0:T(8,128)(2,1)S(1)}, u32[]{:S(2)}, u32[]{:S(2)}) collective-permute-start(bf16[256,128]{1,0:T(8,128)(2,1)S(1)} %get-tuple-element.52), channel_id=1, source_target_pairs={{0,1},{1,0},{2,3},{3,2},{4,5},{5,4},{6,7},{7,6},{8,9},{9,8},{10,11... | collective-permute-start | bytes 196616 | tf_op jit(solution)/shard_map/ppermute | solution.py:450
  34.8 3.8 %copy-start = (f32[256,256]{1,0:T(8,128)S(1)}, f32[256,256]{1,0:T(8,128)}, u32[]{:S(2)}) copy-start(f32[256,256]{1,0:T(8,128)} %constant.6.clone.inverse_ref) | copy-start | bytes 786436
  36.8 1.4 %collective-permute-start.13 = (bf16[192,128]{1,0:T(8,128)(2,1)S(1)}, bf16[192,128]{1,0:T(8,128)(2,1)S(1)}, u32[]{:S(2)}, u32[]{:S(2)}) collective-permute-start(bf16[192,128]{1,0:T(8,128)(2,1)S(1)} %get-tuple-element.53), channel_id=1, source_target_pairs={{0,1},{1,0},{2,3},{3,2},{4,5},{5,4},{6,7},{7,6},{8,9},{9,8},{10,11... | collective-permute-start | bytes 147464 | tf_op jit(solution)/shard_map/ppermute | solution.py:450
  37.3 1.2 %collective-permute-start.14 = (bf16[192,128]{1,0:T(8,128)(2,1)S(1)}, bf16[192,128]{1,0:T(8,128)(2,1)S(1)}, u32[]{:S(2)}, u32[]{:S(2)}) collective-permute-start(bf16[192,128]{1,0:T(8,128)(2,1)S(1)} %get-tuple-element.54), channel_id=1, source_target_pairs={{0,1},{1,0},{2,3},{3,2},{4,5},{5,4},{6,7},{7,6},{8,9},{9,8},{10,11... | collective-permute-start | bytes 147464 | tf_op jit(solution)/shard_map/ppermute | solution.py:450

commit v20 on v18

--- a/solution.py
+++ b/solution.py
@@ -28,8 +28,8 @@
 TN = (((0,), (0,)), ((), ()))
 VMEM_LIMIT = 40 * 1024 * 1024
 
-PART = 16
-FULL = 24
+PART = 24
+FULL = 20
 
 
 def inverse_table(samples, stations):
@@ -45,17 +45,18 @@
     return np.concatenate(rows).astype(np.float32)
 
 
-def forward_rows(bins, samples):
-    count = bins.shape[0]
+def forward_rows(start, count, samples):
+    row = lax.broadcasted_iota(jnp.int32, (2 * count, samples), 0)
     sample = lax.broadcasted_iota(jnp.int32, (2 * count, samples), 1)
-    turn = jnp.concatenate([bins * sample[:count], bins * sample[:count] + samples // 4])
+    imag = row >= count
+    turn = (row + start - jnp.where(imag, count, 0)) * sample + jnp.where(imag, samples // 4, 0)
     turn &= samples - 1
     x = jnp.where(turn > samples // 2, turn - samples, turn).astype(jnp.float32) * (2.0 / samples)
     square = x * x
     value = jnp.full(square.shape, COSINE[-1], jnp.float32)
     for factor in COSINE[-2::-1]:
         value = value * square + factor
-    return value.astype(jnp.bfloat16)
+    return value
 
 
 def place_of(place_ref, groups):
@@ -81,29 +82,31 @@
     traces = jnp.concatenate(parts)
     energy = jnp.sum(jnp.square(traces.astype(jnp.float32)), axis=1, keepdims=True)
     raw = lax.dot_general(traces, table, NT, preferred_element_type=jnp.float32)
-    spectra = (raw * lax.rsqrt(energy + EPSILON)).astype(jnp.bfloat16)
+    spectra = raw * lax.rsqrt(energy + EPSILON)
     return [spectra[comp * LANES : (comp + 1) * LANES].T for comp in range(COMPS)]
+
+
+def rows_of(spectra, start, count):
+    return jnp.concatenate([lanes[start : start + count] for lanes in spectra])
 
 
 def own_kernel(place_ref, windows_ref, part_ref, full_ref, table_ref):
     groups, samples = windows_ref.shape[2], windows_ref.shape[4]
     quarter, group = place_of(place_ref, groups)
-    bins = lax.broadcasted_iota(jnp.int32, (PART, samples), 0) + (quarter % 2) * PART
-    table_ref[: 2 * PART] = forward_rows(bins, samples)
+    table = [forward_rows((quarter % 2) * PART, PART, samples)]
     for far in range(2):
-        start = 2 * PART + (quarter ^ (2 * far)) * FULL
-        bins = lax.broadcasted_iota(jnp.int32, (FULL, samples), 0) + start
-        at = 2 * PART + 2 * FULL * far
-        table_ref[at : at + 2 * FULL] = forward_rows(bins, samples)
-    table = table_ref[...]
+        table.append(forward_rows(2 * PART + (quarter ^ (2 * far)) * FULL, FULL, samples))
+    table = jnp.concatenate(table).astype(jnp.bfloat16)
+    table_ref[...] = table
+    held = full_ref.shape[1] - COMPS * 2 * FULL
     for mg in range(groups):
         spectra = station_spectra(windows_ref, group ^ mg, table)
-        for comp in range(COMPS):
-            lanes = spectra[comp]
-            part_ref[mg, comp * 2 * PART : (comp + 1) * 2 * PART] = lanes[: 2 * PART]
-            for far in range(2):
-                at = 2 * PART + 2 * FULL * far
-                full_ref[far * groups + mg, comp * 2 * FULL : (comp + 1) * 2 * FULL] = lanes[at : at + 2 * FULL]
+        part_ref[mg] = rows_of(spectra, 0, 2 * PART).astype(jnp.bfloat16)
+        for far in range(2):
+            rows = rows_of(spectra, 2 * PART + 2 * FULL * far, 2 * FULL)
+            if held:
+                rows = jnp.concatenate([rows, jnp.zeros((held, LANES), jnp.float32)])
+            full_ref[far * groups + mg] = rows.astype(jnp.bfloat16)
 
 
 def near_spectra_kernel(
@@ -118,18 +121,13 @@
     ).astype(jnp.bfloat16)
     for mg in range(groups):
         spectra = station_spectra(windows_ref, group ^ mg, table)
-        side, cross = piece_refs[mg], piece_refs[groups + mg]
+        side = piece_refs[mg]
         side[:part_rows] = part_ref[mg]
-        side[2 * part_rows : 2 * part_rows + full_rows] = full_ref[mg]
-        cross[:full_rows] = full_ref[groups + mg]
-        for comp in range(COMPS):
-            lanes = spectra[comp]
-            at = part_rows + comp * 2 * PART
-            side[at : at + 2 * PART] = lanes[: 2 * PART]
-            at = 2 * part_rows + full_rows + comp * 2 * FULL
-            side[at : at + 2 * FULL] = lanes[2 * PART : 2 * PART + 2 * FULL]
-            at = full_rows + comp * 2 * FULL
-            cross[at : at + 2 * FULL] = lanes[2 * PART + 2 * FULL :]
+        side[part_rows : 2 * part_rows] = rows_of(spectra, 0, 2 * PART).astype(jnp.bfloat16)
+        for far, (piece, start) in enumerate(((side, 2 * part_rows), (piece_refs[groups + mg], 0))):
+            own = full_ref[far * groups + mg].astype(jnp.float32)[:full_rows]
+            near = rows_of(spectra, 2 * PART + 2 * FULL * far, 2 * FULL)
+            piece[start : start + 2 * full_rows] = jnp.concatenate([own, near]).astype(jnp.bfloat16)
 
 
 def width(bins):
@@ -139,13 +137,17 @@
 def packing(count, bins):
     used = 4 * bins
     spare = LANES - used
-    if not spare:
-        return count, [[(0, 0, 0, used)]]
-    runs = used // spare
-    rows = count // (runs + 1)
-    return rows, [
-        [(at * rows, 0, 0, used), (runs * rows, used, at * spare, (at + 1) * spare)] for at in range(runs)
-    ]
+    runs, rest = used // math.gcd(used, LANES), spare // math.gcd(used, LANES)
+    rows = count // (runs + rest)
+    parts = []
+    for run in range(runs):
+        parts.append([(run * rows, 0, 0, used)])
+        for extra in range(rest):
+            start, end = max(run * spare, extra * used), min((run + 1) * spare, (extra + 1) * used)
+            if start < end:
+                lane = used + start - run * spare
+                parts[-1].append(((runs + extra) * rows, lane, start - extra * used, end - extra * used))
+    return rows, parts
 
 
 def packed_rows(count, bins):
@@ -155,13 +157,14 @@
 
 def unpack(picked, bins):
     used = 4 * bins
-    spare = LANES - used
-    if not spare:
+    runs, rest = used // math.gcd(used, LANES), (LANES - used) // math.gcd(used, LANES)
+    rows = picked.shape[0] // runs
+    if not rest:
         return picked
-    runs = used // spare
-    rows = picked.shape[0] // runs
-    rest = [picked[at * rows : (at + 1) * rows, used:] for at in range(runs)]
-    return jnp.concatenate([picked[:, :used], jnp.concatenate(rest, axis=1)])
+    spare = jnp.concatenate([picked[run * rows : (run + 1) * rows, used:] for run in range(runs)], axis=1)
+    return jnp.concatenate(
+        [picked[:, :used]] + [spare[:, extra * used : (extra + 1) * used] for extra in range(rest)]
+    )
 
 
 def sides_of(place_ref, cells, mq):
@@ -253,8 +256,12 @@
         ref[...] = picked[at * each : (at + 1) * each]
 
 
+def whole(count, tile):
+    return -(-count // tile) * tile
+
+
 def padded(traces):
-    return -(-traces // 16) * 16
+    return whole(traces, 16)
 
 
 def add_cross(pieces, trace_ref, bins, sums_ref, before_ref=None):
@@ -285,13 +292,16 @@
 
 def turn_blocks(cross_ref, bins, flat_ref):
     slots, runs = 2 * SLOTS, LANES // width(bins)
-    empty = jnp.zeros((width(bins) - bins, LANES), jnp.float32)
+    held = cross_ref.shape[0] // slots
+    if held > bins:
+        cross_ref[bins * slots :] = jnp.zeros(((held - bins) * slots, LANES), jnp.float32)
+    empty = jnp.zeros((width(bins) - held, LANES), jnp.float32)
     for own in range(2):
         for at in range(SLOTS // runs):
             block = []
             for i in range(runs):
-                block.append(cross_ref[pl.ds(own * SLOTS + at * runs + i, bins, stride=slots), :])
-                block += [empty] * (bins < width(bins))
+                block.append(cross_ref[pl.ds(own * SLOTS + at * runs + i, held, stride=slots), :])
+                block += [empty] * (held < width(bins))
             block = jnp.concatenate(block).astype(jnp.bfloat16).T
             for part in range(2):
                 for far in range(2):
@@ -467,7 +477,7 @@
         own_kernel,
         out_shape=[
             shape(groups, part_rows, LANES),
-            shape(2 * groups, full_rows, LANES),
+            shape(2 * groups, whole(full_rows, 16), LANES),
             shape(2 * PART + 4 * FULL, samples),
         ],
         in_specs=[smem, vmem],
@@ -503,7 +513,7 @@
         out_specs=vmem,
         scratch_shapes=[
             pltpu.VMEM((padded(groups * 2 * comps) * 2 * PART, LANES), jnp.float32),
-            pltpu.VMEM((2 * SLOTS * PART, LANES), jnp.float32),
+            pltpu.VMEM((2 * SLOTS * whole(PART, 8), LANES), jnp.float32),
         ],
         compiler_params=params,
         cost_estimate=cost(0.001),
@@ -561,7 +571,7 @@
         out_specs=[vmem] * 3,
         scratch_shapes=[
             pltpu.VMEM((padded(len(late) * 2 * comps) * 2 * FULL, LANES), jnp.float32),
-            pltpu.VMEM((2 * SLOTS * FULL, LANES), jnp.float32),
+            pltpu.VMEM((2 * SLOTS * whole(FULL, 8), LANES), jnp.float32),
         ],
         compiler_params=params,
         cost_estimate=cost(10),

time: 41.7 us -> 42.4 us (1.017)
  Pallas kernels: 14.4 us -> 15.4 us
  waiting for transfers between devices: 5.5 us -> 4.88 us
    ppermute x16, waiting for transfers between devices: 5.5 us -> 4.88 us  [swap(): return lax.ppermute(x, 'cell', [(i, i ^ mask) for i in range(cells)])]
  transfers between devices with their start and end apart: 16 -> 16, of which waited for: 6 -> 4; matrix products, arithmetic and copies ran while one was open for 0% -> 0% of each run, Pallas kernels for 31% -> 32%
where the time goes in v20:
time: 42.4 us; the launch traced here: 42.3 us
  starting transfers between devices  20.7 us (49%)
  Pallas kernels  15.4 us (36%)
  waiting for transfers between devices  4.88 us (12%)
  local copies, waits for them, and re-layouts  1.14 us (3%)
    ppermute x16, starting transfers between devices, swap(): return lax.ppermute(x, 'cell', [(i, i ^ mask) for i in range(cells)])  20.7 us
    ppermute x16, waiting for transfers between devices, swap(): return lax.ppermute(x, 'cell', [(i, i ^ mask) for i in range(cells)])  4.88 us
    pallas_call x1, Pallas kernels, on_device(): pl.pallas_call(functools.partial(near_kernel, FULL, 2), out_shape=[full_p...  2.15 us
    pallas_call x1, Pallas kernels, on_device(): pl.pallas_call(functools.partial(full_kernel, cells), out_shape=[full_blo...  2.03 us
    pallas_call x1, Pallas kernels, on_device(): pl.pallas_call(functools.partial(near_kernel, PART, 1), out_shape=[part_p...  1.95 us
    pallas_call x1, Pallas kernels, on_device(): pl.pallas_call(functools.partial(far_kernel, PART), out_shape=[part_packe...  1.95 us
    pallas_call x1, Pallas kernels, on_device(): pl.pallas_call(functools.partial(first_lags_kernel, groups), out_shape=[s...  1.78 us
    pallas_call x1, Pallas kernels, on_device(): pl.pallas_call(ready_kernel, out_shape=[shape(2, 2, count, full_blocks.sh...  1.58 us
  transfers between devices with their start and end apart: 16, of which 4 were waited for; matrix products, arithmetic and copies ran while one was open for 0% of the time, Pallas kernels for 32%

profile of v20, /device:TPU:0, one launch (start us, length us, event | category | flops | bytes accessed | tf_op | source)
XLA Modules:
  0.0 42.3 jit_solution(5809392296637864487)
XLA Ops:
  0.0 0.5 %collective-permute-start.1 = (bf16[3,2,4,64,256]{4,3,2,1,0:T(8,128)(2,1)}, bf16[3,2,4,64,256]{4,3,2,1,0:T(8,128)(2,1)S(1)}, u32[]{:S(2)}, u32[]{:S(2)}) collective-permute-start(bf16[3,2,4,64,256]{4,3,2,1,0:T(8,128)(2,1)} %bitcast.2), channel_id=1, source_target_pairs={{0,1},{1,0},{2,3},{3,2},{4,5},{5,4},{6,7},{7,6},{8,9},{9,8},{10,11... | collective-permute-start | bytes 2359304 | tf_op jit(solution)/shard_map/ppermute | solution.py:459
  0.5 0.1 collective-permute-start
  0.5 0.0 copy-start.3
  0.5 1.1 %copy-done.3 = bf16[3,1,512,256]{3,2,1,0:T(8,128)(2,1)S(1)} copy-done((bf16[3,1,512,256]{3,2,1,0:T(8,128)(2,1)S(1)}, bf16[3,1,512,256]{3,2,1,0:T(8,128)(2,1)}, u32[]{:S(2)}) %copy-start.3) | copy-done | bytes 786456
  1.6 0.6 %own_spectra.1 = (bf16[4,144,128]{2,1,0:T(8,128)(2,1)S(1)}, bf16[8,128,128]{2,1,0:T(8,128)(2,1)S(1)}, bf16[128,256]{1,0:T(8,128)(2,1)S(1)}) custom-call(s32[1]{0:T(128)} %bitcast.place_ref, bf16[3,2,4,64,256]{4,3,2,1,0:T(8,128)(2,1)S(1)} %bitcast.3), custom_call_target="tpu_custom_call" | custom-call | flops 1000000000 | bytes 1048576 | tf_op jit(solution)/shard_map/own_spectra/pallas_call | solution.py:476
  2.3 0.3 collective-permute-done.near_pairs_ref
  2.6 0.0 collective-permute-done.1.windows_ref
  2.6 0.0 copy-done.1
  2.6 0.5 %near_spectra.1 = (bf16[528,128]{1,0:T(8,128)(2,1)S(1)}, bf16[528,128]{1,0:T(8,128)(2,1)S(1)}, bf16[528,128]{1,0:T(8,128)(2,1)S(1)}, bf16[528,128]{1,0:T(8,128)(...) custom-call(s32[1]{0:T(128)} %bitcast.place_ref, ...), custom_call_target="tpu_custom_call" | custom-call | flops 1000000000 | bytes 1048576 | tf_op jit(solution)/shard_map/near_spectra/pallas_call | solution.py:490
  3.1 3.0 %collective-permute-start.2 = (bf16[528,128]{1,0:T(8,128)(2,1)S(1)}, bf16[528,128]{1,0:T(8,128)(2,1)S(1)}, u32[]{:S(2)}, u32[]{:S(2)}) collective-permute-start(bf16[528,128]{1,0:T(8,128)(2,1)S(1)} %get-tuple-element.35), channel_id=1, source_target_pairs={{0,2},{1,3},{2,0},{3,1},{4,6},{5,7},{6,4},{7,5},{8,10},{9,11},{10,... | collective-permute-start | bytes 405512 | tf_op jit(solution)/shard_map/ppermute | solution.py:459
  6.0 1.6 %collective-permute-start.3 = (bf16[528,128]{1,0:T(8,128)(2,1)S(1)}, bf16[528,128]{1,0:T(8,128)(2,1)S(1)}, u32[]{:S(2)}, u32[]{:S(2)}) collective-permute-start(bf16[528,128]{1,0:T(8,128)(2,1)S(1)} %get-tuple-element.36), channel_id=1, source_target_pairs={{0,4},{1,5},{2,6},{3,7},{4,0},{5,1},{6,2},{7,3},{8,12},{9,13},{10,... | collective-permute-start | bytes 405512 | tf_op jit(solution)/shard_map/ppermute | solution.py:459
  7.6 0.0 collective-permute-start.4
  7.6 3.0 %collective-permute-start.5 = (bf16[272,128]{1,0:T(8,128)(2,1)S(1)}, bf16[272,128]{1,0:T(8,128)(2,1)S(1)}, u32[]{:S(2)}, u32[]{:S(2)}) collective-permute-start(bf16[272,128]{1,0:T(8,128)(2,1)S(1)} %get-tuple-element.39), channel_id=1, source_target_pairs={{0,8},{1,9},{2,10},{3,11},{4,12},{5,13},{6,14},{7,15},{8,0},{9,1},... | collective-permute-start | bytes 208904 | tf_op jit(solution)/shard_map/ppermute | solution.py:459
  10.6 1.3 %collective-permute-start.8 = (bf16[240,128]{1,0:T(8,128)(2,1)S(1)}, bf16[240,128]{1,0:T(8,128)(2,1)S(1)}, u32[]{:S(2)}, u32[]{:S(2)}) collective-permute-start(bf16[240,128]{1,0:T(8,128)(2,1)S(1)} %get-tuple-element.42), channel_id=1, source_target_pairs={{0,10},{1,11},{2,8},{3,9},{4,14},{5,15},{6,12},{7,13},{8,2},{9,3},... | collective-permute-start | bytes 184328 | tf_op jit(solution)/shard_map/ppermute | solution.py:459
  11.9 0.0 collective-permute-done.2.refs_1_
  11.9 3.6 %collective-permute-start.9 = (bf16[240,128]{1,0:T(8,128)(2,1)S(1)}, bf16[240,128]{1,0:T(8,128)(2,1)S(1)}, u32[]{:S(2)}, u32[]{:S(2)}) collective-permute-start(bf16[240,128]{1,0:T(8,128)(2,1)S(1)} %get-tuple-element.46), channel_id=1, source_target_pairs={{0,12},{1,13},{2,14},{3,15},{4,8},{5,9},{6,10},{7,11},{8,4},{9,5},... | collective-permute-start | bytes 184328 | tf_op jit(solution)/shard_map/ppermute | solution.py:459
  15.5 0.0 collective-permute-done.3.refs_2_
  15.5 2.1 %collective-permute-start.10 = (bf16[240,128]{1,0:T(8,128)(2,1)S(1)}, bf16[240,128]{1,0:T(8,128)(2,1)S(1)}, u32[]{:S(2)}, u32[]{:S(2)}) collective-permute-start(bf16[240,128]{1,0:T(8,128)(2,1)S(1)} %get-tuple-element.47), channel_id=1, source_target_pairs={{0,14},{1,15},{2,12},{3,13},{4,10},{5,11},{6,8},{7,9},{8,6},{9,7},... | collective-permute-start | bytes 184328 | tf_op jit(solution)/shard_map/ppermute | solution.py:459
  17.6 0.0 collective-permute-done.4.refs_3_
  17.6 1.1 %part.1.flat_ref = bf16[2,2,256,256]{3,2,1,0:T(8,128)(2,1)S(1)} custom-call(bf16[528,128]{1,0:T(8,128)(2,1)S(1)} %get-tuple-element.34.refs_0_, bf16[528,128]{1,0:T(8,128)(2,1)S(1)} %collective-permute-done.2.refs_1_, bf16[528,128]{1,0:T(8,128)(2,1)S(1)} %collective-permute-done.3.refs_2_, bf16[528,128]{1,0:T(8,128)(2,1)S(1)} %collective-permute-done.4.refs_3_), custom_call_target="tpu_custom_call" | custom-call | flops 1000000 | bytes 1048576 | tf_op jit(solution)/shard_map/part/pallas_call | solution.py:509
  18.7 0.0 copy-done.2
  18.7 1.9 %part_near.1 = (bf16[384,128]{1,0:T(8,128)(2,1)S(1)}, bf16[384,128]{1,0:T(8,128)(2,1)S(1)}) custom-call(s32[1]{0:T(128)} %bitcast.place_ref, s32[16]{0:T(128)S(1)} %copy-done.2, s32[2,2,512]{2,1,0:T(2,128)S(1)} %copy-done.1, s32[2,2,512]{2,1,0:T(2,128)S(1)} %collective-permute-done.near_pairs_ref, bf16[2,2,256,256]{3,2,1,0:T(8,128)(2,1)S(1)} %part.1.flat_ref), custom_call_target="tpu_custom_call" | custom-call | flops 1000000 | bytes 1048576 | tf_op jit(solution)/shard_map/part_near/pallas_call | solution.py:522
  20.6 0.0 collective-permute-done.5.listed_ref.refs_4_
  20.7 1.9 %part_far.1 = (bf16[384,128]{1,0:T(8,128)(2,1)S(1)}, bf16[384,128]{1,0:T(8,128)(2,1)S(1)}) custom-call(s32[1]{0:T(128)} %bitcast.place_ref, s32[16]{0:T(128)S(1)} %copy-done.2, bf16[272,128]{1,0:T(8,128)(2,1)S(1)} %collective-permute-done.5.listed_ref.refs_4_, bf16[2,2,256,256]{3,2,1,0:T(8,128)(2,1)S(1)} %part.1.flat_ref, ...), custom_call_target="tpu_custom_call" | custom-call | flops 1000000000 | bytes 1048576 | tf_op jit(solution)/shard_map/part_far/pallas_call | solution.py:531
  22.6 0.1 collective-permute-start.7
  22.7 1.7 %collective-permute-start.6 = (bf16[384,128]{1,0:T(8,128)(2,1)S(1)}, bf16[384,128]{1,0:T(8,128)(2,1)S(1)}, u32[]{:S(2)}, u32[]{:S(2)}) collective-permute-start(bf16[384,128]{1,0:T(8,128)(2,1)S(1)} %get-tuple-element.40.after_1), channel_id=1, source_target_pairs={{0,8},{1,9},{2,10},{3,11},{4,12},{5,13},{6,14},{7,15},{8,0},{9,1},... | collective-permute-start | bytes 294920 | tf_op jit(solution)/shard_map/ppermute | solution.py:459
  24.4 0.0 collective-permute-done.8.refs_5_
  24.4 1.0 %collective-permute-start.11 = (bf16[384,128]{1,0:T(8,128)(2,1)S(1)}, bf16[384,128]{1,0:T(8,128)(2,1)S(1)}, u32[]{:S(2)}, u32[]{:S(2)}) collective-permute-start(bf16[384,128]{1,0:T(8,128)(2,1)S(1)} %get-tuple-element.50), channel_id=1, source_target_pairs={{0,1},{1,0},{2,3},{3,2},{4,5},{5,4},{6,7},{7,6},{8,9},{9,8},{10,11... | collective-permute-start | bytes 294920 | tf_op jit(solution)/shard_map/ppermute | solution.py:459
  25.4 0.6 %early.1.after_ref.before_ref = f32[1280,128]{1,0:T(8,128)S(1)} custom-call(bf16[384,128]{1,0:T(8,128)(2,1)S(1)} %get-tuple-element.38.after_ref.after_0.refs_0_, bf16[384,128]{1,0:T(8,128)(2,1)S(1)} %get-tuple-element.40.after_1, bf16[528,128]{1,0:T(8,128)(2,1)S(1)} %get-tuple-element.34.refs_0_, bf16[528,128]{1,0:T(8,128)(2,1)S(1)} %collective-permute-done.2.refs_1_, ...), custom_call_target="tpu_custom_call" | custom-call | flops 1000000 | bytes 1048576 | tf_op jit(solution)/shard_map/early/pallas_call | solution.py:541
  26.0 1.6 %ready.1 = (bf16[2,2,512,256]{3,2,1,0:T(8,128)(2,1)S(1)}, bf16[2,2,512,128]{3,2,1,0:T(8,128)(2,1)S(1)}, bf16[8,512,128]{2,1,0:T(8,128)(2,1)S(1)}) custom-call(s32[1]{0:T(128)} %bitcast.place_ref, s32[16]{0:T(128)S(1)} %copy-done.2, bf16[272,128]{1,0:T(8,128)(2,1)S(1)} %collective-permute-done.5.listed_ref.refs_4_, f32[1280,128]{1,0:T(8,128)S(1)} %early.1.after_ref.before_ref), custom_call_target="tpu_custom_call" | custom-call | flops 1000000 | bytes 1048576 | tf_op jit(solution)/shard_map/ready/pallas_call | solution.py:554
  27.6 0.0 collective-permute-done.9.refs_0_
  27.6 0.0 collective-permute-done.10.refs_1_
  27.6 2.0 %full.1 = (bf16[2,2,256,256]{3,2,1,0:T(8,128)(2,1)S(1)}, bf16[320,128]{1,0:T(8,128)(2,1)S(1)}, bf16[320,128]{1,0:T(8,128)(2,1)S(1)}) custom-call(s32[1]{0:T(128)} %bitcast.place_ref, bf16[2,2,512,256]{3,2,1,0:T(8,128)(2,1)S(1)} %get-tuple-element.43.hot_ref, bf16[2,2,512,128]{3,2,1,0:T(8,128)(2,1)S(1)} %get-tuple-element.44.here_ref, ...), custom_call_target="tpu_custom_call" | custom-call | flops 10000000000 | bytes 1048576 | tf_op jit(solution)/shard_map/full/pallas_call | solution.py:567
  29.7 1.7 %collective-permute-start.14 = (bf16[320,128]{1,0:T(8,128)(2,1)S(1)}, bf16[320,128]{1,0:T(8,128)(2,1)S(1)}, u32[]{:S(2)}, u32[]{:S(2)}) collective-permute-start(bf16[320,128]{1,0:T(8,128)(2,1)S(1)} %get-tuple-element.55), channel_id=1, source_target_pairs={{0,8},{1,9},{2,10},{3,11},{4,12},{5,13},{6,14},{7,15},{8,0},{9,1},... | collective-permute-start | bytes 245768 | tf_op jit(solution)/shard_map/ppermute | solution.py:459
  31.4 0.6 %collective-permute-start.15 = (bf16[320,128]{1,0:T(8,128)(2,1)S(1)}, bf16[320,128]{1,0:T(8,128)(2,1)S(1)}, u32[]{:S(2)}, u32[]{:S(2)}) collective-permute-start(bf16[320,128]{1,0:T(8,128)(2,1)S(1)} %get-tuple-element.56), channel_id=1, source_target_pairs={{0,9},{1,8},{2,11},{3,10},{4,13},{5,12},{6,15},{7,14},{8,1},{9,0},... | collective-permute-start | bytes 245768 | tf_op jit(solution)/shard_map/ppermute | solution.py:459
  32.0 0.0 collective-permute-done.7.refs_1_.refs_2_
  32.0 3.4 %collective-permute-done.6.refs_0_.refs_1_ = bf16[384,128]{1,0:T(8,128)(2,1)S(1)} collective-permute-done((bf16[384,128]{1,0:T(8,128)(2,1)S(1)}, bf16[384,128]{1,0:T(8,128)(2,1)S(1)}, u32[]{:S(2)}, u32[]{:S(2)}) %collective-permute-start.6) | collective-permute-done | bytes 98336 | tf_op jit(solution)/shard_map/ppermute | solution.py:459
  35.4 2.2 %full_near.1 = (bf16[320,128]{1,0:T(8,128)(2,1)S(1)}, bf16[160,128]{1,0:T(8,128)(2,1)S(1)}, bf16[160,128]{1,0:T(8,128)(2,1)S(1)}) custom-call(s32[1]{0:T(128)} %bitcast.place_ref, s32[16]{0:T(128)S(1)} %copy-done.2, s32[2,2,512]{2,1,0:T(2,128)S(1)} %copy-done.1, s32[2,2,512]{2,1,0:T(2,128)S(1)} %collective-permute-done.near_pairs_ref, ...), custom_call_target="tpu_custom_call" | custom-call | flops 500000000 | bytes 1048576 | tf_op jit(solution)/shard_map/full_near/pallas_call | solution.py:581
  37.5 0.5 %collective-permute-start.12 = (bf16[160,128]{1,0:T(8,128)(2,1)S(1)}, bf16[160,128]{1,0:T(8,128)(2,1)S(1)}, u32[]{:S(2)}, u32[]{:S(2)}) collective-permute-start(bf16[160,128]{1,0:T(8,128)(2,1)S(1)} %get-tuple-element.51), channel_id=1, source_target_pairs={{0,1},{1,0},{2,3},{3,2},{4,5},{5,4},{6,7},{7,6},{8,9},{9,8},{10,11... | collective-permute-start | bytes 122888 | tf_op jit(solution)/shard_map/ppermute | solution.py:459
  38.0 0.1 collective-permute-start.13
  38.1 0.0 collective-permute-done.11.refs_4_
  38.1 0.8 %collective-permute-done.12.refs_5_ = bf16[160,128]{1,0:T(8,128)(2,1)S(1)} collective-permute-done((bf16[160,128]{1,0:T(8,128)(2,1)S(1)}, bf16[160,128]{1,0:T(8,128)(2,1)S(1)}, u32[]{:S(2)}, u32[]{:S(2)}) %collective-permute-start.12) | collective-permute-done | bytes 40992 | tf_op jit(solution)/shard_map/ppermute | solution.py:459
  38.9 0.3 collective-permute-done.13.refs_6_
  39.2 0.0 copy-done
  39.3 1.8 %first_lags.1 = (f32[2,512,256]{2,1,0:T(8,128)S(1)}, bf16[2,80,512]{2,1,0:T(8,128)(2,1)S(1)}) custom-call(s32[1]{0:T(128)} %bitcast.place_ref, f32[256,256]{1,0:T(8,128)S(1)} %copy-done, bf16[384,128]{1,0:T(8,128)(2,1)S(1)} %get-tuple-element.38.after_ref.after_0.refs_0_, bf16[384,128]{1,0:T(8,128)(2,1)S(1)} %collective-permute-done.6.refs_0_.refs_1_, ...), custom_call_target="tpu_custom_call" | custom-call | flops 1000000 | bytes 1048576 | tf_op jit(solution)/shard_map/first_lags/pallas_call | solution.py:592
  41.0 0.0 collective-permute-done.14.refs_0_
  41.1 0.0 collective-permute-done.15.refs_1_
  41.1 1.2 %lags.1 = f32[2,512,256]{2,1,0:T(8,128)} custom-call(f32[2,512,256]{2,1,0:T(8,128)S(1)} %get-tuple-element.53.first_ref, bf16[2,80,512]{2,1,0:T(8,128)(2,1)S(1)} %get-tuple-element.54.table_ref, bf16[320,128]{1,0:T(8,128)(2,1)S(1)} %collective-permute-done.14.refs_0_, bf16[320,128]{1,0:T(8,128)(2,1)S(1)} %collective-permute-done.15.refs_1_), custom_call_target="tpu_custom_call" | custom-call | flops 1000000000 | bytes 1048576 | tf_op jit(solution)/shard_map/lags/pallas_call | solution.py:604
  (3 shorter events, 0.0 us)
Async XLA Ops:
  0.0 2.6 %collective-permute-start.1 = (bf16[3,2,4,64,256]{4,3,2,1,0:T(8,128)(2,1)}, bf16[3,2,4,64,256]{4,3,2,1,0:T(8,128)(2,1)S(1)}, u32[]{:S(2)}, u32[]{:S(2)}) collective-permute-start(bf16[3,2,4,64,256]{4,3,2,1,0:T(8,128)(2,1)} %bitcast.2), channel_id=1, source_target_pairs={{0,1},{1,0},{2,3},{3,2},{4,5},{5,4},{6,7},{7,6},{8,9},{9,8},{10,11... | collective-permute-start | bytes 2359304 | tf_op jit(solution)/shard_map/ppermute | solution.py:459
  0.5 2.1 %collective-permute-start = (s32[2,2,512]{2,1,0:T(2,128)}, s32[2,2,512]{2,1,0:T(2,128)S(1)}, u32[]{:S(2)}, u32[]{:S(2)}) collective-permute-start(s32[2,2,512]{2,1,0:T(2,128)} %own_pairs_ref.5), channel_id=1, source_target_pairs={{0,1},{1,0},{2,3},{3,2},{4,5},{5,4},{6,7},{7,6},{8,9},{9,8},{10,11... | collective-permute-start | bytes 24584 | tf_op jit(solution)/shard_map/ppermute | solution.py:459
  0.5 1.1 %copy-start.3 = (bf16[3,1,512,256]{3,2,1,0:T(8,128)(2,1)S(1)}, bf16[3,1,512,256]{3,2,1,0:T(8,128)(2,1)}, u32[]{:S(2)}) copy-start(bf16[3,1,512,256]{3,2,1,0:T(8,128)(2,1)} %param.4) | copy-start | bytes 2359300
  1.6 0.9 %copy-start.1 = (s32[2,2,512]{2,1,0:T(2,128)S(1)}, s32[2,2,512]{2,1,0:T(2,128)}, u32[]{:S(2)}) copy-start(s32[2,2,512]{2,1,0:T(2,128)} %own_pairs_ref.5) | copy-start | bytes 24580
  3.1 8.8 %collective-permute-start.2 = (bf16[528,128]{1,0:T(8,128)(2,1)S(1)}, bf16[528,128]{1,0:T(8,128)(2,1)S(1)}, u32[]{:S(2)}, u32[]{:S(2)}) collective-permute-start(bf16[528,128]{1,0:T(8,128)(2,1)S(1)} %get-tuple-element.35), channel_id=1, source_target_pairs={{0,2},{1,3},{2,0},{3,1},{4,6},{5,7},{6,4},{7,5},{8,10},{9,11},{10,... | collective-permute-start | bytes 405512 | tf_op jit(solution)/shard_map/ppermute | solution.py:459
  6.0 9.5 %collective-permute-start.3 = (bf16[528,128]{1,0:T(8,128)(2,1)S(1)}, bf16[528,128]{1,0:T(8,128)(2,1)S(1)}, u32[]{:S(2)}, u32[]{:S(2)}) collective-permute-start(bf16[528,128]{1,0:T(8,128)(2,1)S(1)} %get-tuple-element.36), channel_id=1, source_target_pairs={{0,4},{1,5},{2,6},{3,7},{4,0},{5,1},{6,2},{7,3},{8,12},{9,13},{10,... | collective-permute-start | bytes 405512 | tf_op jit(solution)/shard_map/ppermute | solution.py:459
  7.6 10.0 %collective-permute-start.4 = (bf16[528,128]{1,0:T(8,128)(2,1)S(1)}, bf16[528,128]{1,0:T(8,128)(2,1)S(1)}, u32[]{:S(2)}, u32[]{:S(2)}) collective-permute-start(bf16[528,128]{1,0:T(8,128)(2,1)S(1)} %get-tuple-element.37), channel_id=1, source_target_pairs={{0,6},{1,7},{2,4},{3,5},{4,2},{5,3},{6,0},{7,1},{8,14},{9,15},{10,... | collective-permute-start | bytes 405512 | tf_op jit(solution)/shard_map/ppermute | solution.py:459
  7.6 13.0 %collective-permute-start.5 = (bf16[272,128]{1,0:T(8,128)(2,1)S(1)}, bf16[272,128]{1,0:T(8,128)(2,1)S(1)}, u32[]{:S(2)}, u32[]{:S(2)}) collective-permute-start(bf16[272,128]{1,0:T(8,128)(2,1)S(1)} %get-tuple-element.39), channel_id=1, source_target_pairs={{0,8},{1,9},{2,10},{3,11},{4,12},{5,13},{6,14},{7,15},{8,0},{9,1},... | collective-permute-start | bytes 208904 | tf_op jit(solution)/shard_map/ppermute | solution.py:459
  10.6 13.8 %collective-permute-start.8 = (bf16[240,128]{1,0:T(8,128)(2,1)S(1)}, bf16[240,128]{1,0:T(8,128)(2,1)S(1)}, u32[]{:S(2)}, u32[]{:S(2)}) collective-permute-start(bf16[240,128]{1,0:T(8,128)(2,1)S(1)} %get-tuple-element.42), channel_id=1, source_target_pairs={{0,10},{1,11},{2,8},{3,9},{4,14},{5,15},{6,12},{7,13},{8,2},{9,3},... | collective-permute-start | bytes 184328 | tf_op jit(solution)/shard_map/ppermute | solution.py:459
  11.9 15.7 %collective-permute-start.9 = (bf16[240,128]{1,0:T(8,128)(2,1)S(1)}, bf16[240,128]{1,0:T(8,128)(2,1)S(1)}, u32[]{:S(2)}, u32[]{:S(2)}) collective-permute-start(bf16[240,128]{1,0:T(8,128)(2,1)S(1)} %get-tuple-element.46), channel_id=1, source_target_pairs={{0,12},{1,13},{2,14},{3,15},{4,8},{5,9},{6,10},{7,11},{8,4},{9,5},... | collective-permute-start | bytes 184328 | tf_op jit(solution)/shard_map/ppermute | solution.py:459
  15.5 12.1 %collective-permute-start.10 = (bf16[240,128]{1,0:T(8,128)(2,1)S(1)}, bf16[240,128]{1,0:T(8,128)(2,1)S(1)}, u32[]{:S(2)}, u32[]{:S(2)}) collective-permute-start(bf16[240,128]{1,0:T(8,128)(2,1)S(1)} %get-tuple-element.47), channel_id=1, source_target_pairs={{0,14},{1,15},{2,12},{3,13},{4,10},{5,11},{6,8},{7,9},{8,6},{9,7},... | collective-permute-start | bytes 184328 | tf_op jit(solution)/shard_map/ppermute | solution.py:459
  17.6 1.1 %copy-start.2 = (s32[16]{0:T(128)S(1)}, s32[16]{0:T(128)}, u32[]{:S(2)}) copy-start(s32[16]{0:T(128)} %counts_ref.7) | copy-start | bytes 196
  22.6 9.4 %collective-permute-start.7 = (bf16[384,128]{1,0:T(8,128)(2,1)S(1)}, bf16[384,128]{1,0:T(8,128)(2,1)S(1)}, u32[]{:S(2)}, u32[]{:S(2)}) collective-permute-start(bf16[384,128]{1,0:T(8,128)(2,1)S(1)} %get-tuple-element.41), channel_id=1, source_target_pairs={{0,9},{1,8},{2,11},{3,10},{4,13},{5,12},{6,15},{7,14},{8,1},{9,0},... | collective-permute-start | bytes 294920 | tf_op jit(solution)/shard_map/ppermute | solution.py:459
  22.7 12.7 %collective-permute-start.6 = (bf16[384,128]{1,0:T(8,128)(2,1)S(1)}, bf16[384,128]{1,0:T(8,128)(2,1)S(1)}, u32[]{:S(2)}, u32[]{:S(2)}) collective-permute-start(bf16[384,128]{1,0:T(8,128)(2,1)S(1)} %get-tuple-element.40.after_1), channel_id=1, source_target_pairs={{0,8},{1,9},{2,10},{3,11},{4,12},{5,13},{6,14},{7,15},{8,0},{9,1},... | collective-permute-start | bytes 294920 | tf_op jit(solution)/shard_map/ppermute | solution.py:459
  24.4 13.7 %collective-permute-start.11 = (bf16[384,128]{1,0:T(8,128)(2,1)S(1)}, bf16[384,128]{1,0:T(8,128)(2,1)S(1)}, u32[]{:S(2)}, u32[]{:S(2)}) collective-permute-start(bf16[384,128]{1,0:T(8,128)(2,1)S(1)} %get-tuple-element.50), channel_id=1, source_target_pairs={{0,1},{1,0},{2,3},{3,2},{4,5},{5,4},{6,7},{7,6},{8,9},{9,8},{10,11... | collective-permute-start | bytes 294920 | tf_op jit(solution)/shard_map/ppermute | solution.py:459
  29.7 11.4 %collective-permute-start.14 = (bf16[320,128]{1,0:T(8,128)(2,1)S(1)}, bf16[320,128]{1,0:T(8,128)(2,1)S(1)}, u32[]{:S(2)}, u32[]{:S(2)}) collective-permute-start(bf16[320,128]{1,0:T(8,128)(2,1)S(1)} %get-tuple-element.55), channel_id=1, source_target_pairs={{0,8},{1,9},{2,10},{3,11},{4,12},{5,13},{6,14},{7,15},{8,0},{9,1},... | collective-permute-start | bytes 245768 | tf_op jit(solution)/shard_map/ppermute | solution.py:459
  31.4 9.7 %collective-permute-start.15 = (bf16[320,128]{1,0:T(8,128)(2,1)S(1)}, bf16[320,128]{1,0:T(8,128)(2,1)S(1)}, u32[]{:S(2)}, u32[]{:S(2)}) collective-permute-start(bf16[320,128]{1,0:T(8,128)(2,1)S(1)} %get-tuple-element.56), channel_id=1, source_target_pairs={{0,9},{1,8},{2,11},{3,10},{4,13},{5,12},{6,15},{7,14},{8,1},{9,0},... | collective-permute-start | bytes 245768 | tf_op jit(solution)/shard_map/ppermute | solution.py:459
  35.4 3.9 %copy-start = (f32[256,256]{1,0:T(8,128)S(1)}, f32[256,256]{1,0:T(8,128)}, u32[]{:S(2)}) copy-start(f32[256,256]{1,0:T(8,128)} %constant.6.clone.inverse_ref) | copy-start | bytes 786436
  37.5 1.4 %collective-permute-start.12 = (bf16[160,128]{1,0:T(8,128)(2,1)S(1)}, bf16[160,128]{1,0:T(8,128)(2,1)S(1)}, u32[]{:S(2)}, u32[]{:S(2)}) collective-permute-start(bf16[160,128]{1,0:T(8,128)(2,1)S(1)} %get-tuple-element.51), channel_id=1, source_target_pairs={{0,1},{1,0},{2,3},{3,2},{4,5},{5,4},{6,7},{7,6},{8,9},{9,8},{10,11... | collective-permute-start | bytes 122888 | tf_op jit(solution)/shard_map/ppermute | solution.py:459
  38.0 1.2 %collective-permute-start.13 = (bf16[160,128]{1,0:T(8,128)(2,1)S(1)}, bf16[160,128]{1,0:T(8,128)(2,1)S(1)}, u32[]{:S(2)}, u32[]{:S(2)}) collective-permute-start(bf16[160,128]{1,0:T(8,128)(2,1)S(1)} %get-tuple-element.52), channel_id=1, source_target_pairs={{0,1},{1,0},{2,3},{3,2},{4,5},{5,4},{6,7},{7,6},{8,9},{9,8},{10,11... | collective-permute-start | bytes 122888 | tf_op jit(solution)/shard_map/ppermute | solution.py:459

commit v21 on v20

--- a/solution.py
+++ b/solution.py
@@ -388,9 +388,7 @@
     return high, (table - high.astype(jnp.float32)).astype(jnp.bfloat16)
 
 
-def first_lags_kernel(groups, place_ref, inverse_ref, *refs):
-    part_0, part_2, part_3, full_0, part_1, *full_1, lags_ref, table_ref = refs
-    samples = inverse_ref.shape[1]
+def tables_of(groups, place_ref, inverse_ref):
     quarter, _ = place_of(place_ref, groups)
     low = quarter % 2
     sign = jnp.where(quarter // 2 == low, 1.0, -1.0)
@@ -403,22 +401,44 @@
         start = pl.multiple_of(4 * PART + (quarter ^ mq) * 2 * FULL, 2 * FULL)
         return halves(both_rounds(inverse_ref[pl.ds(start, 2 * FULL), :], sign))
 
-    near, other = part_table(0), part_table(1)
+    return part_table, full_table
+
+
+def sum_lags(terms):
     lags = 0.0
-    full_1 = jnp.concatenate([ref[...] for ref in full_1])
-    for picked, bins, table in (
-        (part_0[...], PART, near),
-        (part_2[...], PART, near),
-        (part_1[...], PART, other),
-        (part_3[...], PART, other),
-        (full_0[...], FULL, full_table(0)),
-        (full_1, FULL, full_table(1)),
-    ):
+    for picked, bins, table in terms:
         picked = unpack(picked, bins)
         for half in table:
             lags += jnp.dot(picked, half, preferred_element_type=jnp.float32)
+    return lags
+
+
+def part_lags_kernel(groups, place_ref, inverse_ref, part_0, part_2, part_3, part_1, lags_ref):
+    samples = inverse_ref.shape[1]
+    part_table, _ = tables_of(groups, place_ref, inverse_ref)
+    near, other = part_table(0), part_table(1)
+    lags = sum_lags(
+        [
+            (part_0[...], PART, near),
+            (part_2[...], PART, near),
+            (part_1[...], PART, other),
+            (part_3[...], PART, other),
+        ]
+    )
     for step_round in range(2):
         lags_ref[step_round] = lags[:, step_round * samples : (step_round + 1) * samples]
+
+
+def first_lags_kernel(groups, place_ref, inverse_ref, before_ref, full_0, *refs):
+    full_1, (lags_ref, table_ref) = refs[:-2], refs[-2:]
+    samples = inverse_ref.shape[1]
+    _, full_table = tables_of(groups, place_ref, inverse_ref)
+    full_1 = jnp.concatenate([ref[...] for ref in full_1])
+    lags = sum_lags([(full_0[...], FULL, full_table(0)), (full_1, FULL, full_table(1))])
+    for step_round in range(2):
+        lags_ref[step_round] = (
+            before_ref[step_round] + lags[:, step_round * samples : (step_round + 1) * samples]
+        )
     for at in range(2):
         table_ref[at] = full_table(2 + at)[0]
 
@@ -581,26 +601,35 @@
     full_0, *full_1 = pl.pallas_call(
         functools.partial(near_kernel, FULL, 2),
         out_shape=[full_packed, half_packed, half_packed],
-        in_specs=[smem, smem] + [vmem] * 3 + [pl.BlockSpec(memory_space=pl.ANY)] * 2,
+        in_specs=[smem, smem] + [vmem] * 3,
         out_specs=[vmem] * 3,
         compiler_params=params,
         cost_estimate=cost(0.5),
         name="full_near",
-    )(place, counts, pairs, near_pairs, full_flat, part_2, part_3)
+    )(place, counts, pairs, near_pairs, full_flat)
     full_1 = [swap(x, 1) for x in full_1]
 
+    part_lags = pl.pallas_call(
+        functools.partial(part_lags_kernel, groups),
+        out_shape=shape(2, count, samples, dtype=jnp.float32),
+        in_specs=[smem] + [vmem] * 5,
+        out_specs=vmem,
+        compiler_params=params,
+        cost_estimate=cost(0.001),
+        name="part_lags",
+    )(place, inverse, part_0, part_2, part_3, part_1)
     first, tables = pl.pallas_call(
         functools.partial(first_lags_kernel, groups),
         out_shape=[
             shape(2, count, samples, dtype=jnp.float32),
             shape(2, 4 * FULL, 2 * samples),
         ],
-        in_specs=[smem] + [vmem] * 8,
+        in_specs=[smem] + [vmem] * 5,
         out_specs=[vmem] * 2,
         compiler_params=params,
         cost_estimate=cost(0.001),
         name="first_lags",
-    )(place, inverse, part_0, part_2, part_3, full_0, part_1, *full_1)
+    )(place, inverse, part_lags, full_0, *full_1)
     return pl.pallas_call(
         lag_kernel,
         out_shape=shape(2, count, samples, dtype=jnp.float32),

time: 42.4 us -> 41.6 us (0.981)
  waiting for transfers between devices: 4.88 us -> 3.29 us
  starting transfers between devices: 20.7 us -> 21.3 us
    ppermute x16, waiting for transfers between devices: 4.88 us -> 3.29 us  [swap(): return lax.ppermute(x, 'cell', [(i, i ^ mask) for i in range(cells)])]
    pallas_call x0 -> x1, Pallas kernels: none -> 1.24 us  [on_device(): pl.pallas_call(functools.partial(part_lags_kernel, groups), out_shape=sha...]
    pallas_call x1, Pallas kernels: 1.78 us -> 0.71 us  [on_device(): pl.pallas_call(functools.partial(first_lags_kernel, groups), out_shape=[s...]
    ppermute x16, starting transfers between devices: 20.7 us -> 21.3 us  [swap(): return lax.ppermute(x, 'cell', [(i, i ^ mask) for i in range(cells)])]
  transfers between devices with their start and end apart: 16 -> 16, of which waited for: 4 -> 3; matrix products, arithmetic and copies ran while one was open for 0% -> 0% of each run, Pallas kernels for 32% -> 33%
where the time goes in v21:
time: 41.6 us; the launch traced here: 41.5 us
  starting transfers between devices  21.3 us (51%)
  Pallas kernels  15.6 us (38%)
  waiting for transfers between devices  3.29 us (8%)
  local copies, waits for them, and re-layouts  1.14 us (3%)
    ppermute x16, starting transfers between devices, swap(): return lax.ppermute(x, 'cell', [(i, i ^ mask) for i in range(cells)])  21.3 us
    ppermute x16, waiting for transfers between devices, swap(): return lax.ppermute(x, 'cell', [(i, i ^ mask) for i in range(cells)])  3.29 us
    pallas_call x1, Pallas kernels, on_device(): pl.pallas_call(functools.partial(near_kernel, FULL, 2), out_shape=[full_p...  2.13 us
    pallas_call x1, Pallas kernels, on_device(): pl.pallas_call(functools.partial(full_kernel, cells), out_shape=[full_blo...  2.03 us
    pallas_call x1, Pallas kernels, on_device(): pl.pallas_call(functools.partial(near_kernel, PART, 1), out_shape=[part_p...  1.95 us
    pallas_call x1, Pallas kernels, on_device(): pl.pallas_call(functools.partial(far_kernel, PART), out_shape=[part_packe...  1.95 us
    pallas_call x1, Pallas kernels, on_device(): pl.pallas_call(ready_kernel, out_shape=[shape(2, 2, count, full_blocks.sh...  1.58 us
    pallas_call x1, Pallas kernels, on_device(): pl.pallas_call(functools.partial(part_lags_kernel, groups), out_shape=sha...  1.24 us
  transfers between devices with their start and end apart: 16, of which 3 were waited for; matrix products, arithmetic and copies ran while one was open for 0% of the time, Pallas kernels for 33%

profile of v21, /device:TPU:0, one launch (start us, length us, event | category | flops | bytes accessed | tf_op | source)
XLA Modules:
  0.0 41.5 jit_solution(794434077897635706)
XLA Ops:
  0.0 0.5 %collective-permute-start.1 = (bf16[3,2,4,64,256]{4,3,2,1,0:T(8,128)(2,1)}, bf16[3,2,4,64,256]{4,3,2,1,0:T(8,128)(2,1)S(1)}, u32[]{:S(2)}, u32[]{:S(2)}) collective-permute-start(bf16[3,2,4,64,256]{4,3,2,1,0:T(8,128)(2,1)} %bitcast.2), channel_id=1, source_target_pairs={{0,1},{1,0},{2,3},{3,2},{4,5},{5,4},{6,7},{7,6},{8,9},{9,8},{10,11... | collective-permute-start | bytes 2359304 | tf_op jit(solution)/shard_map/ppermute | solution.py:479
  0.5 0.1 collective-permute-start
  0.5 1.1 %copy-done.3 = bf16[3,1,512,256]{3,2,1,0:T(8,128)(2,1)S(1)} copy-done((bf16[3,1,512,256]{3,2,1,0:T(8,128)(2,1)S(1)}, bf16[3,1,512,256]{3,2,1,0:T(8,128)(2,1)}, u32[]{:S(2)}) %copy-start.3) | copy-done | bytes 786456
  1.6 0.6 %own_spectra.1 = (bf16[4,144,128]{2,1,0:T(8,128)(2,1)S(1)}, bf16[8,128,128]{2,1,0:T(8,128)(2,1)S(1)}, bf16[128,256]{1,0:T(8,128)(2,1)S(1)}) custom-call(s32[1]{0:T(128)} %bitcast.place_ref, bf16[3,2,4,64,256]{4,3,2,1,0:T(8,128)(2,1)S(1)} %bitcast.3), custom_call_target="tpu_custom_call" | custom-call | flops 1000000000 | bytes 1048576 | tf_op jit(solution)/shard_map/own_spectra/pallas_call | solution.py:496
  2.3 0.3 collective-permute-done.near_pairs_ref
  2.6 0.0 collective-permute-done.1.windows_ref
  2.6 0.0 copy-done.1
  2.6 0.5 %near_spectra.1 = (bf16[528,128]{1,0:T(8,128)(2,1)S(1)}, bf16[528,128]{1,0:T(8,128)(2,1)S(1)}, bf16[528,128]{1,0:T(8,128)(2,1)S(1)}, bf16[528,128]{1,0:T(8,128)(...) custom-call(s32[1]{0:T(128)} %bitcast.place_ref, ...), custom_call_target="tpu_custom_call" | custom-call | flops 1000000000 | bytes 1048576 | tf_op jit(solution)/shard_map/near_spectra/pallas_call | solution.py:510
  3.1 3.0 %collective-permute-start.2 = (bf16[528,128]{1,0:T(8,128)(2,1)S(1)}, bf16[528,128]{1,0:T(8,128)(2,1)S(1)}, u32[]{:S(2)}, u32[]{:S(2)}) collective-permute-start(bf16[528,128]{1,0:T(8,128)(2,1)S(1)} %get-tuple-element.35), channel_id=1, source_target_pairs={{0,2},{1,3},{2,0},{3,1},{4,6},{5,7},{6,4},{7,5},{8,10},{9,11},{10,... | collective-permute-start | bytes 405512 | tf_op jit(solution)/shard_map/ppermute | solution.py:479
  6.0 1.6 %collective-permute-start.3 = (bf16[528,128]{1,0:T(8,128)(2,1)S(1)}, bf16[528,128]{1,0:T(8,128)(2,1)S(1)}, u32[]{:S(2)}, u32[]{:S(2)}) collective-permute-start(bf16[528,128]{1,0:T(8,128)(2,1)S(1)} %get-tuple-element.36), channel_id=1, source_target_pairs={{0,4},{1,5},{2,6},{3,7},{4,0},{5,1},{6,2},{7,3},{8,12},{9,13},{10,... | collective-permute-start | bytes 405512 | tf_op jit(solution)/shard_map/ppermute | solution.py:479
  7.6 0.0 collective-permute-start.4
  7.6 3.0 %collective-permute-start.5 = (bf16[272,128]{1,0:T(8,128)(2,1)S(1)}, bf16[272,128]{1,0:T(8,128)(2,1)S(1)}, u32[]{:S(2)}, u32[]{:S(2)}) collective-permute-start(bf16[272,128]{1,0:T(8,128)(2,1)S(1)} %get-tuple-element.39), channel_id=1, source_target_pairs={{0,8},{1,9},{2,10},{3,11},{4,12},{5,13},{6,14},{7,15},{8,0},{9,1},... | collective-permute-start | bytes 208904 | tf_op jit(solution)/shard_map/ppermute | solution.py:479
  10.6 1.3 %collective-permute-start.9 = (bf16[240,128]{1,0:T(8,128)(2,1)S(1)}, bf16[240,128]{1,0:T(8,128)(2,1)S(1)}, u32[]{:S(2)}, u32[]{:S(2)}) collective-permute-start(bf16[240,128]{1,0:T(8,128)(2,1)S(1)} %get-tuple-element.43), channel_id=1, source_target_pairs={{0,10},{1,11},{2,8},{3,9},{4,14},{5,15},{6,12},{7,13},{8,2},{9,3},... | collective-permute-start | bytes 184328 | tf_op jit(solution)/shard_map/ppermute | solution.py:479
  11.9 0.0 collective-permute-done.2.refs_1_
  11.9 3.6 %collective-permute-start.10 = (bf16[240,128]{1,0:T(8,128)(2,1)S(1)}, bf16[240,128]{1,0:T(8,128)(2,1)S(1)}, u32[]{:S(2)}, u32[]{:S(2)}) collective-permute-start(bf16[240,128]{1,0:T(8,128)(2,1)S(1)} %get-tuple-element.47), channel_id=1, source_target_pairs={{0,12},{1,13},{2,14},{3,15},{4,8},{5,9},{6,10},{7,11},{8,4},{9,5},... | collective-permute-start | bytes 184328 | tf_op jit(solution)/shard_map/ppermute | solution.py:479
  15.5 0.0 collective-permute-done.3.refs_2_
  15.5 2.1 %collective-permute-start.11 = (bf16[240,128]{1,0:T(8,128)(2,1)S(1)}, bf16[240,128]{1,0:T(8,128)(2,1)S(1)}, u32[]{:S(2)}, u32[]{:S(2)}) collective-permute-start(bf16[240,128]{1,0:T(8,128)(2,1)S(1)} %get-tuple-element.48), channel_id=1, source_target_pairs={{0,14},{1,15},{2,12},{3,13},{4,10},{5,11},{6,8},{7,9},{8,6},{9,7},... | collective-permute-start | bytes 184328 | tf_op jit(solution)/shard_map/ppermute | solution.py:479
  17.6 0.0 collective-permute-done.4.refs_3_
  17.6 1.1 %part.1.flat_ref = bf16[2,2,256,256]{3,2,1,0:T(8,128)(2,1)S(1)} custom-call(bf16[528,128]{1,0:T(8,128)(2,1)S(1)} %get-tuple-element.34.refs_0_, bf16[528,128]{1,0:T(8,128)(2,1)S(1)} %collective-permute-done.2.refs_1_, bf16[528,128]{1,0:T(8,128)(2,1)S(1)} %collective-permute-done.3.refs_2_, bf16[528,128]{1,0:T(8,128)(2,1)S(1)} %collective-permute-done.4.refs_3_), custom_call_target="tpu_custom_call" | custom-call | flops 1000000 | bytes 1048576 | tf_op jit(solution)/shard_map/part/pallas_call | solution.py:529
  18.7 0.0 copy-done.2
  18.7 1.9 %part_near.1 = (bf16[384,128]{1,0:T(8,128)(2,1)S(1)}, bf16[384,128]{1,0:T(8,128)(2,1)S(1)}) custom-call(s32[1]{0:T(128)} %bitcast.place_ref, s32[16]{0:T(128)S(1)} %copy-done.2, s32[2,2,512]{2,1,0:T(2,128)S(1)} %copy-done.1, s32[2,2,512]{2,1,0:T(2,128)S(1)} %collective-permute-done.near_pairs_ref, bf16[2,2,256,256]{3,2,1,0:T(8,128)(2,1)S(1)} %part.1.flat_ref), custom_call_target="tpu_custom_call" | custom-call | flops 1000000 | bytes 1048576 | tf_op jit(solution)/shard_map/part_near/pallas_call | solution.py:542
  20.6 0.0 collective-permute-done.5.listed_ref.refs_4_
  20.7 1.9 %part_far.1 = (bf16[384,128]{1,0:T(8,128)(2,1)S(1)}, bf16[384,128]{1,0:T(8,128)(2,1)S(1)}) custom-call(s32[1]{0:T(128)} %bitcast.place_ref, s32[16]{0:T(128)S(1)} %copy-done.2, bf16[272,128]{1,0:T(8,128)(2,1)S(1)} %collective-permute-done.5.listed_ref.refs_4_, bf16[2,2,256,256]{3,2,1,0:T(8,128)(2,1)S(1)} %part.1.flat_ref, ...), custom_call_target="tpu_custom_call" | custom-call | flops 1000000000 | bytes 1048576 | tf_op jit(solution)/shard_map/part_far/pallas_call | solution.py:551
  22.6 1.7 %collective-permute-start.6 = (bf16[384,128]{1,0:T(8,128)(2,1)S(1)}, bf16[384,128]{1,0:T(8,128)(2,1)S(1)}, u32[]{:S(2)}, u32[]{:S(2)}) collective-permute-start(bf16[384,128]{1,0:T(8,128)(2,1)S(1)} %get-tuple-element.40.after_1), channel_id=1, source_target_pairs={{0,8},{1,9},{2,10},{3,11},{4,12},{5,13},{6,14},{7,15},{8,0},{9,1},... | collective-permute-start | bytes 294920 | tf_op jit(solution)/shard_map/ppermute | solution.py:479
  24.4 0.0 collective-permute-start.7
  24.4 0.0 collective-permute-done.9.refs_5_
  24.4 1.4 %collective-permute-start.8 = (bf16[384,128]{1,0:T(8,128)(2,1)S(1)}, bf16[384,128]{1,0:T(8,128)(2,1)S(1)}, u32[]{:S(2)}, u32[]{:S(2)}) collective-permute-start(bf16[384,128]{1,0:T(8,128)(2,1)S(1)} %get-tuple-element.42), channel_id=1, source_target_pairs={{0,1},{1,0},{2,3},{3,2},{4,5},{5,4},{6,7},{7,6},{8,9},{9,8},{10,11... | collective-permute-start | bytes 294920 | tf_op jit(solution)/shard_map/ppermute | solution.py:479
  25.7 0.6 %early.1.after_ref.before_ref = f32[1280,128]{1,0:T(8,128)S(1)} custom-call(bf16[384,128]{1,0:T(8,128)(2,1)S(1)} %get-tuple-element.38.after_ref.part_0.after_0, bf16[384,128]{1,0:T(8,128)(2,1)S(1)} %get-tuple-element.40.after_1, bf16[528,128]{1,0:T(8,128)(2,1)S(1)} %get-tuple-element.34.refs_0_, bf16[528,128]{1,0:T(8,128)(2,1)S(1)} %collective-permute-done.2.refs_1_, ...), custom_call_target="tpu_custom_call" | custom-call | flops 1000000 | bytes 1048576 | tf_op jit(solution)/shard_map/early/pallas_call | solution.py:561
  26.3 1.6 %ready.1 = (bf16[2,2,512,256]{3,2,1,0:T(8,128)(2,1)S(1)}, bf16[2,2,512,128]{3,2,1,0:T(8,128)(2,1)S(1)}, bf16[8,512,128]{2,1,0:T(8,128)(2,1)S(1)}) custom-call(s32[1]{0:T(128)} %bitcast.place_ref, s32[16]{0:T(128)S(1)} %copy-done.2, bf16[272,128]{1,0:T(8,128)(2,1)S(1)} %collective-permute-done.5.listed_ref.refs_4_, f32[1280,128]{1,0:T(8,128)S(1)} %early.1.after_ref.before_ref), custom_call_target="tpu_custom_call" | custom-call | flops 1000000 | bytes 1048576 | tf_op jit(solution)/shard_map/ready/pallas_call | solution.py:574
  27.9 0.0 collective-permute-done.10.refs_0_
  27.9 0.0 collective-permute-done.11.refs_1_
  27.9 2.0 %full.1 = (bf16[2,2,256,256]{3,2,1,0:T(8,128)(2,1)S(1)}, bf16[320,128]{1,0:T(8,128)(2,1)S(1)}, bf16[320,128]{1,0:T(8,128)(2,1)S(1)}) custom-call(s32[1]{0:T(128)} %bitcast.place_ref, bf16[2,2,512,256]{3,2,1,0:T(8,128)(2,1)S(1)} %get-tuple-element.44.hot_ref, bf16[2,2,512,128]{3,2,1,0:T(8,128)(2,1)S(1)} %get-tuple-element.45.here_ref, ...), custom_call_target="tpu_custom_call" | custom-call | flops 10000000000 | bytes 1048576 | tf_op jit(solution)/shard_map/full/pallas_call | solution.py:587
  29.9 1.7 %collective-permute-start.14 = (bf16[320,128]{1,0:T(8,128)(2,1)S(1)}, bf16[320,128]{1,0:T(8,128)(2,1)S(1)}, u32[]{:S(2)}, u32[]{:S(2)}) collective-permute-start(bf16[320,128]{1,0:T(8,128)(2,1)S(1)} %get-tuple-element.55), channel_id=1, source_target_pairs={{0,8},{1,9},{2,10},{3,11},{4,12},{5,13},{6,14},{7,15},{8,0},{9,1},... | collective-permute-start | bytes 245768 | tf_op jit(solution)/shard_map/ppermute | solution.py:479
  31.7 0.6 %collective-permute-start.15 = (bf16[320,128]{1,0:T(8,128)(2,1)S(1)}, bf16[320,128]{1,0:T(8,128)(2,1)S(1)}, u32[]{:S(2)}, u32[]{:S(2)}) collective-permute-start(bf16[320,128]{1,0:T(8,128)(2,1)S(1)} %get-tuple-element.56), channel_id=1, source_target_pairs={{0,9},{1,8},{2,11},{3,10},{4,13},{5,12},{6,15},{7,14},{8,1},{9,0},... | collective-permute-start | bytes 245768 | tf_op jit(solution)/shard_map/ppermute | solution.py:479
  32.3 2.1 %full_near.1 = (bf16[320,128]{1,0:T(8,128)(2,1)S(1)}, bf16[160,128]{1,0:T(8,128)(2,1)S(1)}, bf16[160,128]{1,0:T(8,128)(2,1)S(1)}) custom-call(s32[1]{0:T(128)} %bitcast.place_ref, s32[16]{0:T(128)S(1)} %copy-done.2, s32[2,2,512]{2,1,0:T(2,128)S(1)} %copy-done.1, s32[2,2,512]{2,1,0:T(2,128)S(1)} %collective-permute-done.near_pairs_ref, ...), custom_call_target="tpu_custom_call" | custom-call | flops 500000000 | bytes 1048576 | tf_op jit(solution)/shard_map/full_near/pallas_call | solution.py:601
  34.4 0.0 collective-permute-done.6.part_2
  34.4 0.9 %collective-permute-start.12 = (bf16[160,128]{1,0:T(8,128)(2,1)S(1)}, bf16[160,128]{1,0:T(8,128)(2,1)S(1)}, u32[]{:S(2)}, u32[]{:S(2)}) collective-permute-start(bf16[160,128]{1,0:T(8,128)(2,1)S(1)} %get-tuple-element.51), channel_id=1, source_target_pairs={{0,1},{1,0},{2,3},{3,2},{4,5},{5,4},{6,7},{7,6},{8,9},{9,8},{10,11... | collective-permute-start | bytes 122888 | tf_op jit(solution)/shard_map/ppermute | solution.py:479
  35.3 0.0 collective-permute-done.7.part_3
  35.3 0.1 collective-permute-start.13
  35.3 0.0 collective-permute-done.8.part_1
  35.3 0.0 copy-done
  35.3 1.2 %part_lags.1.before_ref = f32[2,512,256]{2,1,0:T(8,128)S(1)} custom-call(s32[1]{0:T(128)} %bitcast.place_ref, f32[256,256]{1,0:T(8,128)S(1)} %copy-done, bf16[384,128]{1,0:T(8,128)(2,1)S(1)} %get-tuple-element.38.after_ref.part_0.after_0, bf16[384,128]{1,0:T(8,128)(2,1)S(1)} %collective-permute-done.6.part_2, ...), custom_call_target="tpu_custom_call" | custom-call | flops 1000000 | bytes 1048576 | tf_op jit(solution)/shard_map/part_lags/pallas_call | solution.py:612
  36.6 0.0 collective-permute-done.12.refs_0_
  36.6 0.0 collective-permute-done.13.refs_1_
  36.6 0.7 %first_lags.1 = (f32[2,512,256]{2,1,0:T(8,128)S(1)}, bf16[2,80,512]{2,1,0:T(8,128)(2,1)S(1)}) custom-call(s32[1]{0:T(128)} %bitcast.place_ref, f32[256,256]{1,0:T(8,128)S(1)} %copy-done, f32[2,512,256]{2,1,0:T(8,128)S(1)} %part_lags.1.before_ref, bf16[320,128]{1,0:T(8,128)(2,1)S(1)} %get-tuple-element.50.full_0, ...), custom_call_target="tpu_custom_call" | custom-call | flops 1000000 | bytes 1048576 | tf_op jit(solution)/shard_map/first_lags/pallas_call | solution.py:621
  37.3 1.4 %collective-permute-done.14.refs_0_ = bf16[320,128]{1,0:T(8,128)(2,1)S(1)} collective-permute-done((bf16[320,128]{1,0:T(8,128)(2,1)S(1)}, bf16[320,128]{1,0:T(8,128)(2,1)S(1)}, u32[]{:S(2)}, u32[]{:S(2)}) %collective-permute-start.14) | collective-permute-done | bytes 81952 | tf_op jit(solution)/shard_map/ppermute | solution.py:479
  38.7 1.6 %collective-permute-done.15.refs_1_ = bf16[320,128]{1,0:T(8,128)(2,1)S(1)} collective-permute-done((bf16[320,128]{1,0:T(8,128)(2,1)S(1)}, bf16[320,128]{1,0:T(8,128)(2,1)S(1)}, u32[]{:S(2)}, u32[]{:S(2)}) %collective-permute-start.15) | collective-permute-done | bytes 81952 | tf_op jit(solution)/shard_map/ppermute | solution.py:479
  40.3 1.2 %lags.1 = f32[2,512,256]{2,1,0:T(8,128)} custom-call(f32[2,512,256]{2,1,0:T(8,128)S(1)} %get-tuple-element.53.first_ref, bf16[2,80,512]{2,1,0:T(8,128)(2,1)S(1)} %get-tuple-element.54.table_ref, bf16[320,128]{1,0:T(8,128)(2,1)S(1)} %collective-permute-done.14.refs_0_, bf16[320,128]{1,0:T(8,128)(2,1)S(1)} %collective-permute-done.15.refs_1_), custom_call_target="tpu_custom_call" | custom-call | flops 1000000000 | bytes 1048576 | tf_op jit(solution)/shard_map/lags/pallas_call | solution.py:633
  (4 shorter events, 0.0 us)
Async XLA Ops:
  0.0 2.6 %collective-permute-start.1 = (bf16[3,2,4,64,256]{4,3,2,1,0:T(8,128)(2,1)}, bf16[3,2,4,64,256]{4,3,2,1,0:T(8,128)(2,1)S(1)}, u32[]{:S(2)}, u32[]{:S(2)}) collective-permute-start(bf16[3,2,4,64,256]{4,3,2,1,0:T(8,128)(2,1)} %bitcast.2), channel_id=1, source_target_pairs={{0,1},{1,0},{2,3},{3,2},{4,5},{5,4},{6,7},{7,6},{8,9},{9,8},{10,11... | collective-permute-start | bytes 2359304 | tf_op jit(solution)/shard_map/ppermute | solution.py:479
  0.5 2.1 %collective-permute-start = (s32[2,2,512]{2,1,0:T(2,128)}, s32[2,2,512]{2,1,0:T(2,128)S(1)}, u32[]{:S(2)}, u32[]{:S(2)}) collective-permute-start(s32[2,2,512]{2,1,0:T(2,128)} %own_pairs_ref.5), channel_id=1, source_target_pairs={{0,1},{1,0},{2,3},{3,2},{4,5},{5,4},{6,7},{7,6},{8,9},{9,8},{10,11... | collective-permute-start | bytes 24584 | tf_op jit(solution)/shard_map/ppermute | solution.py:479
  0.5 1.1 %copy-start.3 = (bf16[3,1,512,256]{3,2,1,0:T(8,128)(2,1)S(1)}, bf16[3,1,512,256]{3,2,1,0:T(8,128)(2,1)}, u32[]{:S(2)}) copy-start(bf16[3,1,512,256]{3,2,1,0:T(8,128)(2,1)} %param.4) | copy-start | bytes 2359300
  1.6 0.9 %copy-start.1 = (s32[2,2,512]{2,1,0:T(2,128)S(1)}, s32[2,2,512]{2,1,0:T(2,128)}, u32[]{:S(2)}) copy-start(s32[2,2,512]{2,1,0:T(2,128)} %own_pairs_ref.5) | copy-start | bytes 24580
  3.1 8.8 %collective-permute-start.2 = (bf16[528,128]{1,0:T(8,128)(2,1)S(1)}, bf16[528,128]{1,0:T(8,128)(2,1)S(1)}, u32[]{:S(2)}, u32[]{:S(2)}) collective-permute-start(bf16[528,128]{1,0:T(8,128)(2,1)S(1)} %get-tuple-element.35), channel_id=1, source_target_pairs={{0,2},{1,3},{2,0},{3,1},{4,6},{5,7},{6,4},{7,5},{8,10},{9,11},{10,... | collective-permute-start | bytes 405512 | tf_op jit(solution)/shard_map/ppermute | solution.py:479
  6.0 9.5 %collective-permute-start.3 = (bf16[528,128]{1,0:T(8,128)(2,1)S(1)}, bf16[528,128]{1,0:T(8,128)(2,1)S(1)}, u32[]{:S(2)}, u32[]{:S(2)}) collective-permute-start(bf16[528,128]{1,0:T(8,128)(2,1)S(1)} %get-tuple-element.36), channel_id=1, source_target_pairs={{0,4},{1,5},{2,6},{3,7},{4,0},{5,1},{6,2},{7,3},{8,12},{9,13},{10,... | collective-permute-start | bytes 405512 | tf_op jit(solution)/shard_map/ppermute | solution.py:479
  7.6 10.0 %collective-permute-start.4 = (bf16[528,128]{1,0:T(8,128)(2,1)S(1)}, bf16[528,128]{1,0:T(8,128)(2,1)S(1)}, u32[]{:S(2)}, u32[]{:S(2)}) collective-permute-start(bf16[528,128]{1,0:T(8,128)(2,1)S(1)} %get-tuple-element.37), channel_id=1, source_target_pairs={{0,6},{1,7},{2,4},{3,5},{4,2},{5,3},{6,0},{7,1},{8,14},{9,15},{10,... | collective-permute-start | bytes 405512 | tf_op jit(solution)/shard_map/ppermute | solution.py:479
  7.6 13.0 %collective-permute-start.5 = (bf16[272,128]{1,0:T(8,128)(2,1)S(1)}, bf16[272,128]{1,0:T(8,128)(2,1)S(1)}, u32[]{:S(2)}, u32[]{:S(2)}) collective-permute-start(bf16[272,128]{1,0:T(8,128)(2,1)S(1)} %get-tuple-element.39), channel_id=1, source_target_pairs={{0,8},{1,9},{2,10},{3,11},{4,12},{5,13},{6,14},{7,15},{8,0},{9,1},... | collective-permute-start | bytes 208904 | tf_op jit(solution)/shard_map/ppermute | solution.py:479
  10.6 13.8 %collective-permute-start.9 = (bf16[240,128]{1,0:T(8,128)(2,1)S(1)}, bf16[240,128]{1,0:T(8,128)(2,1)S(1)}, u32[]{:S(2)}, u32[]{:S(2)}) collective-permute-start(bf16[240,128]{1,0:T(8,128)(2,1)S(1)} %get-tuple-element.43), channel_id=1, source_target_pairs={{0,10},{1,11},{2,8},{3,9},{4,14},{5,15},{6,12},{7,13},{8,2},{9,3},... | collective-permute-start | bytes 184328 | tf_op jit(solution)/shard_map/ppermute | solution.py:479
  11.9 16.0 %collective-permute-start.10 = (bf16[240,128]{1,0:T(8,128)(2,1)S(1)}, bf16[240,128]{1,0:T(8,128)(2,1)S(1)}, u32[]{:S(2)}, u32[]{:S(2)}) collective-permute-start(bf16[240,128]{1,0:T(8,128)(2,1)S(1)} %get-tuple-element.47), channel_id=1, source_target_pairs={{0,12},{1,13},{2,14},{3,15},{4,8},{5,9},{6,10},{7,11},{8,4},{9,5},... | collective-permute-start | bytes 184328 | tf_op jit(solution)/shard_map/ppermute | solution.py:479
  15.5 12.4 %collective-permute-start.11 = (bf16[240,128]{1,0:T(8,128)(2,1)S(1)}, bf16[240,128]{1,0:T(8,128)(2,1)S(1)}, u32[]{:S(2)}, u32[]{:S(2)}) collective-permute-start(bf16[240,128]{1,0:T(8,128)(2,1)S(1)} %get-tuple-element.48), channel_id=1, source_target_pairs={{0,14},{1,15},{2,12},{3,13},{4,10},{5,11},{6,8},{7,9},{8,6},{9,7},... | collective-permute-start | bytes 184328 | tf_op jit(solution)/shard_map/ppermute | solution.py:479
  17.6 1.1 %copy-start.2 = (s32[16]{0:T(128)S(1)}, s32[16]{0:T(128)}, u32[]{:S(2)}) copy-start(s32[16]{0:T(128)} %counts_ref.7) | copy-start | bytes 196
  22.6 11.8 %collective-permute-start.6 = (bf16[384,128]{1,0:T(8,128)(2,1)S(1)}, bf16[384,128]{1,0:T(8,128)(2,1)S(1)}, u32[]{:S(2)}, u32[]{:S(2)}) collective-permute-start(bf16[384,128]{1,0:T(8,128)(2,1)S(1)} %get-tuple-element.40.after_1), channel_id=1, source_target_pairs={{0,8},{1,9},{2,10},{3,11},{4,12},{5,13},{6,14},{7,15},{8,0},{9,1},... | collective-permute-start | bytes 294920 | tf_op jit(solution)/shard_map/ppermute | solution.py:479
  24.4 10.9 %collective-permute-start.7 = (bf16[384,128]{1,0:T(8,128)(2,1)S(1)}, bf16[384,128]{1,0:T(8,128)(2,1)S(1)}, u32[]{:S(2)}, u32[]{:S(2)}) collective-permute-start(bf16[384,128]{1,0:T(8,128)(2,1)S(1)} %get-tuple-element.41), channel_id=1, source_target_pairs={{0,9},{1,8},{2,11},{3,10},{4,13},{5,12},{6,15},{7,14},{8,1},{9,0},... | collective-permute-start | bytes 294920 | tf_op jit(solution)/shard_map/ppermute | solution.py:479
  24.4 11.0 %collective-permute-start.8 = (bf16[384,128]{1,0:T(8,128)(2,1)S(1)}, bf16[384,128]{1,0:T(8,128)(2,1)S(1)}, u32[]{:S(2)}, u32[]{:S(2)}) collective-permute-start(bf16[384,128]{1,0:T(8,128)(2,1)S(1)} %get-tuple-element.42), channel_id=1, source_target_pairs={{0,1},{1,0},{2,3},{3,2},{4,5},{5,4},{6,7},{7,6},{8,9},{9,8},{10,11... | collective-permute-start | bytes 294920 | tf_op jit(solution)/shard_map/ppermute | solution.py:479
  29.9 8.8 %collective-permute-start.14 = (bf16[320,128]{1,0:T(8,128)(2,1)S(1)}, bf16[320,128]{1,0:T(8,128)(2,1)S(1)}, u32[]{:S(2)}, u32[]{:S(2)}) collective-permute-start(bf16[320,128]{1,0:T(8,128)(2,1)S(1)} %get-tuple-element.55), channel_id=1, source_target_pairs={{0,8},{1,9},{2,10},{3,11},{4,12},{5,13},{6,14},{7,15},{8,0},{9,1},... | collective-permute-start | bytes 245768 | tf_op jit(solution)/shard_map/ppermute | solution.py:479
  31.7 8.6 %collective-permute-start.15 = (bf16[320,128]{1,0:T(8,128)(2,1)S(1)}, bf16[320,128]{1,0:T(8,128)(2,1)S(1)}, u32[]{:S(2)}, u32[]{:S(2)}) collective-permute-start(bf16[320,128]{1,0:T(8,128)(2,1)S(1)} %get-tuple-element.56), channel_id=1, source_target_pairs={{0,9},{1,8},{2,11},{3,10},{4,13},{5,12},{6,15},{7,14},{8,1},{9,0},... | collective-permute-start | bytes 245768 | tf_op jit(solution)/shard_map/ppermute | solution.py:479
  32.3 3.1 %copy-start = (f32[256,256]{1,0:T(8,128)S(1)}, f32[256,256]{1,0:T(8,128)}, u32[]{:S(2)}) copy-start(f32[256,256]{1,0:T(8,128)} %constant.6.clone.inverse_ref) | copy-start | bytes 786436
  34.4 2.2 %collective-permute-start.12 = (bf16[160,128]{1,0:T(8,128)(2,1)S(1)}, bf16[160,128]{1,0:T(8,128)(2,1)S(1)}, u32[]{:S(2)}, u32[]{:S(2)}) collective-permute-start(bf16[160,128]{1,0:T(8,128)(2,1)S(1)} %get-tuple-element.51), channel_id=1, source_target_pairs={{0,1},{1,0},{2,3},{3,2},{4,5},{5,4},{6,7},{7,6},{8,9},{9,8},{10,11... | collective-permute-start | bytes 122888 | tf_op jit(solution)/shard_map/ppermute | solution.py:479
  35.3 1.4 %collective-permute-start.13 = (bf16[160,128]{1,0:T(8,128)(2,1)S(1)}, bf16[160,128]{1,0:T(8,128)(2,1)S(1)}, u32[]{:S(2)}, u32[]{:S(2)}) collective-permute-start(bf16[160,128]{1,0:T(8,128)(2,1)S(1)} %get-tuple-element.52), channel_id=1, source_target_pairs={{0,1},{1,0},{2,3},{3,2},{4,5},{5,4},{6,7},{7,6},{8,9},{9,8},{10,11... | collective-permute-start | bytes 122888 | tf_op jit(solution)/shard_map/ppermute | solution.py:479

commit v22 on v21

--- a/solution.py
+++ b/solution.py
@@ -329,7 +329,7 @@
     turn_blocks(cross_ref, PART, flat_ref)
 
 
-def far_kernel(bins, place_ref, counts_ref, listed_ref, flat_ref, after_ref, picked_0, picked_1):
+def far_kernel(bins, place_ref, counts_ref, listed_ref, flat_ref, picked_0, picked_1):
     listed = listed_ref[cross_full(listed_ref)[2] :].astype(jnp.float32)
     listing = listed.shape[0] // 2
     pick(place_ref, counts_ref, listed[:listing], flat_ref, bins, 2, picked_0)
@@ -342,30 +342,14 @@
     add_cross(pieces, trace_ref, FULL, sums_ref)
 
 
-def ready_kernel(place_ref, counts_ref, listed_ref, after_ref, hot_ref, here_ref, fold_ref):
-    listed = listed_ref[cross_full(listed_ref)[2] :].astype(jnp.float32)
-    listing = listed.shape[0] // 2
-    for at in range(2):
-        part = listed[at * listing : (at + 1) * listing]
-        for step_round, (hot, here) in enumerate(
-            hots(place_ref, counts_ref, part, hot_ref.shape[3], FULL, 2 + at)
-        ):
-            hot_ref[at, step_round] = hot
-            here_ref[at, step_round] = here
-    for at, matrix in enumerate(folds(hot_ref.shape[2], FULL)[1]):
-        fold_ref[at] = matrix
-
-
-def full_kernel(cells, place_ref, hot_ref, here_ref, fold_ref, after_0, before_ref, *refs):
+def full_kernel(place_ref, counts_ref, listed_ref, before_ref, *refs):
     piece_refs, (flat_ref, picked_0, picked_1, trace_ref, cross_ref) = refs[:-5], refs[-5:]
     add_cross([cross_full(ref) for ref in piece_refs], trace_ref, FULL, cross_ref, before_ref)
     turn_blocks(cross_ref, FULL, flat_ref)
-    count = hot_ref.shape[2]
-    kinds = folds_of(count, FULL)
-    matrices = [fold_ref[at] for at in range(len(kinds))]
-    for at, ref in enumerate((picked_0, picked_1)):
-        hot = [(hot_ref[at, step_round], here_ref[at, step_round]) for step_round in range(2)]
-        ref[...] = picks(place_ref, cells, hot, kinds, matrices, flat_ref, FULL, 2 + at)
+    listed = listed_ref[cross_full(listed_ref)[2] :].astype(jnp.float32)
+    listing = listed.shape[0] // 2
+    pick(place_ref, counts_ref, listed[:listing], flat_ref, FULL, 2, picked_0)
+    pick(place_ref, counts_ref, listed[listing:], flat_ref, FULL, 3, picked_1)
 
 
 def near_kernel(bins, sent, place_ref, counts_ref, own_pairs_ref, near_pairs_ref, flat_ref, *refs):
@@ -551,12 +535,12 @@
     part_2, part_3 = pl.pallas_call(
         functools.partial(far_kernel, PART),
         out_shape=[part_packed, part_packed],
-        in_specs=[smem, smem, vmem, vmem, pl.BlockSpec(memory_space=pl.ANY)],
+        in_specs=[smem, smem, vmem, vmem],
         out_specs=[vmem, vmem],
         compiler_params=params,
         cost_estimate=cost(1),
         name="part_far",
-    )(place, counts, far[0], part_flat, part_0)
+    )(place, counts, far[0], part_flat)
     part_1 = swap(part_1, 1)
     sums = pl.pallas_call(
         functools.partial(early_kernel, groups),
@@ -571,23 +555,10 @@
         name="early",
     )(part_0, part_2, *sides, *early)
     part_2, part_3 = swap(part_2, half), swap(part_3, half + 1)
-    ready = pl.pallas_call(
-        ready_kernel,
-        out_shape=[
-            shape(2, 2, count, full_blocks.shape[2]),
-            shape(2, 2, count, LANES),
-            shape(len(folds_of(count, FULL)), 4 * LANES, LANES),
-        ],
-        in_specs=[smem, smem, vmem, pl.BlockSpec(memory_space=pl.ANY)],
-        out_specs=[vmem] * 3,
-        compiler_params=params,
-        cost_estimate=cost(0.001),
-        name="ready",
-    )(place, counts, far[0], sums)
     full_flat, full_2, full_3 = pl.pallas_call(
-        functools.partial(full_kernel, cells),
+        full_kernel,
         out_shape=[full_blocks, full_packed, full_packed],
-        in_specs=[smem] + [vmem] * 3 + [pl.BlockSpec(memory_space=pl.ANY)] + [vmem] * (1 + len(late)),
+        in_specs=[smem, smem] + [vmem] * (2 + len(late)),
         out_specs=[vmem] * 3,
         scratch_shapes=[
             pltpu.VMEM((padded(len(late) * 2 * comps) * 2 * FULL, LANES), jnp.float32),
@@ -596,7 +567,7 @@
         compiler_params=params,
         cost_estimate=cost(10),
         name="full",
-    )(place, *ready, part_0, sums, *late)
+    )(place, counts, far[0], sums, *late)
     full_2, full_3 = swap(full_2, half), swap(full_3, half + 1)
     full_0, *full_1 = pl.pallas_call(
         functools.partial(near_kernel, FULL, 2),

time: 41.6 us -> 40.6 us (0.976)
  Pallas kernels: 15.6 us -> 15 us
    pallas_call x2 -> x1, Pallas kernels: 3.61 us -> 3 us  [on_device(): pl.pallas_call(full_kernel, out_shape=[full_blocks, full_packed, full_pac...]
where the time goes in v22:
time: 40.6 us; the launch traced here: 40.5 us
  starting transfers between devices  21.1 us (52%)
  Pallas kernels  15 us (37%)
  waiting for transfers between devices  3.13 us (8%)
  local copies, waits for them, and re-layouts  1.14 us (3%)
    ppermute x16, starting transfers between devices, swap(): return lax.ppermute(x, 'cell', [(i, i ^ mask) for i in range(cells)])  21.1 us
    ppermute x16, waiting for transfers between devices, swap(): return lax.ppermute(x, 'cell', [(i, i ^ mask) for i in range(cells)])  3.13 us
    pallas_call x1, Pallas kernels, on_device(): pl.pallas_call(full_kernel, out_shape=[full_blocks, full_packed, full_pac...  3 us
    pallas_call x1, Pallas kernels, on_device(): pl.pallas_call(functools.partial(near_kernel, FULL, 2), out_shape=[full_p...  2.13 us
    pallas_call x1, Pallas kernels, on_device(): pl.pallas_call(functools.partial(far_kernel, PART), out_shape=[part_packe...  1.94 us
    pallas_call x1, Pallas kernels, on_device(): pl.pallas_call(functools.partial(near_kernel, PART, 1), out_shape=[part_p...  1.94 us
    pallas_call x1, Pallas kernels, on_device(): pl.pallas_call(functools.partial(part_lags_kernel, groups), out_shape=sha...  1.24 us
    pallas_call x1, Pallas kernels, on_device(): pl.pallas_call(lag_kernel, out_shape=shape(2, count, samples, dtype=jnp.f...  1.21 us
  transfers between devices with their start and end apart: 16, of which 3 were waited for; matrix products, arithmetic and copies ran while one was open for 0% of the time, Pallas kernels for 33%

profile of v22, /device:TPU:0, one launch (start us, length us, event | category | flops | bytes accessed | tf_op | source)
XLA Modules:
  0.0 40.5 jit_solution(12218839425953025000)
XLA Ops:
  0.0 0.5 %collective-permute-start.1 = (bf16[3,2,4,64,256]{4,3,2,1,0:T(8,128)(2,1)}, bf16[3,2,4,64,256]{4,3,2,1,0:T(8,128)(2,1)S(1)}, u32[]{:S(2)}, u32[]{:S(2)}) collective-permute-start(bf16[3,2,4,64,256]{4,3,2,1,0:T(8,128)(2,1)} %bitcast.2), channel_id=1, source_target_pairs={{0,1},{1,0},{2,3},{3,2},{4,5},{5,4},{6,7},{7,6},{8,9},{9,8},{10,11... | collective-permute-start | bytes 2359304 | tf_op jit(solution)/shard_map/ppermute | solution.py:463
  0.5 0.1 collective-permute-start
  0.5 0.0 copy-start.3
  0.5 1.1 %copy-done.3 = bf16[3,1,512,256]{3,2,1,0:T(8,128)(2,1)S(1)} copy-done((bf16[3,1,512,256]{3,2,1,0:T(8,128)(2,1)S(1)}, bf16[3,1,512,256]{3,2,1,0:T(8,128)(2,1)}, u32[]{:S(2)}) %copy-start.3) | copy-done | bytes 786456
  1.6 0.6 %own_spectra.1 = (bf16[4,144,128]{2,1,0:T(8,128)(2,1)S(1)}, bf16[8,128,128]{2,1,0:T(8,128)(2,1)S(1)}, bf16[128,256]{1,0:T(8,128)(2,1)S(1)}) custom-call(s32[1]{0:T(128)} %bitcast.place_ref, bf16[3,2,4,64,256]{4,3,2,1,0:T(8,128)(2,1)S(1)} %bitcast.3), custom_call_target="tpu_custom_call" | custom-call | flops 1000000000 | bytes 1048576 | tf_op jit(solution)/shard_map/own_spectra/pallas_call | solution.py:480
  2.3 0.3 collective-permute-done.near_pairs_ref
  2.6 0.0 collective-permute-done.1.windows_ref
  2.6 0.0 copy-done.1
  2.6 0.5 %near_spectra.1 = (bf16[528,128]{1,0:T(8,128)(2,1)S(1)}, bf16[528,128]{1,0:T(8,128)(2,1)S(1)}, bf16[528,128]{1,0:T(8,128)(2,1)S(1)}, bf16[528,128]{1,0:T(8,128)(...) custom-call(s32[1]{0:T(128)} %bitcast.place_ref, ...), custom_call_target="tpu_custom_call" | custom-call | flops 1000000000 | bytes 1048576 | tf_op jit(solution)/shard_map/near_spectra/pallas_call | solution.py:494
  3.1 3.0 %collective-permute-start.2 = (bf16[528,128]{1,0:T(8,128)(2,1)S(1)}, bf16[528,128]{1,0:T(8,128)(2,1)S(1)}, u32[]{:S(2)}, u32[]{:S(2)}) collective-permute-start(bf16[528,128]{1,0:T(8,128)(2,1)S(1)} %get-tuple-element.32), channel_id=1, source_target_pairs={{0,2},{1,3},{2,0},{3,1},{4,6},{5,7},{6,4},{7,5},{8,10},{9,11},{10,... | collective-permute-start | bytes 405512 | tf_op jit(solution)/shard_map/ppermute | solution.py:463
  6.0 1.6 %collective-permute-start.3 = (bf16[528,128]{1,0:T(8,128)(2,1)S(1)}, bf16[528,128]{1,0:T(8,128)(2,1)S(1)}, u32[]{:S(2)}, u32[]{:S(2)}) collective-permute-start(bf16[528,128]{1,0:T(8,128)(2,1)S(1)} %get-tuple-element.33), channel_id=1, source_target_pairs={{0,4},{1,5},{2,6},{3,7},{4,0},{5,1},{6,2},{7,3},{8,12},{9,13},{10,... | collective-permute-start | bytes 405512 | tf_op jit(solution)/shard_map/ppermute | solution.py:463
  7.6 0.0 collective-permute-start.4
  7.6 3.0 %collective-permute-start.5 = (bf16[272,128]{1,0:T(8,128)(2,1)S(1)}, bf16[272,128]{1,0:T(8,128)(2,1)S(1)}, u32[]{:S(2)}, u32[]{:S(2)}) collective-permute-start(bf16[272,128]{1,0:T(8,128)(2,1)S(1)} %get-tuple-element.36), channel_id=1, source_target_pairs={{0,8},{1,9},{2,10},{3,11},{4,12},{5,13},{6,14},{7,15},{8,0},{9,1},... | collective-permute-start | bytes 208904 | tf_op jit(solution)/shard_map/ppermute | solution.py:463
  10.6 1.3 %collective-permute-start.9 = (bf16[240,128]{1,0:T(8,128)(2,1)S(1)}, bf16[240,128]{1,0:T(8,128)(2,1)S(1)}, u32[]{:S(2)}, u32[]{:S(2)}) collective-permute-start(bf16[240,128]{1,0:T(8,128)(2,1)S(1)} %get-tuple-element.40), channel_id=1, source_target_pairs={{0,10},{1,11},{2,8},{3,9},{4,14},{5,15},{6,12},{7,13},{8,2},{9,3},... | collective-permute-start | bytes 184328 | tf_op jit(solution)/shard_map/ppermute | solution.py:463
  11.9 0.0 collective-permute-done.2.refs_1_
  11.9 3.6 %collective-permute-start.10 = (bf16[240,128]{1,0:T(8,128)(2,1)S(1)}, bf16[240,128]{1,0:T(8,128)(2,1)S(1)}, u32[]{:S(2)}, u32[]{:S(2)}) collective-permute-start(bf16[240,128]{1,0:T(8,128)(2,1)S(1)} %get-tuple-element.41), channel_id=1, source_target_pairs={{0,12},{1,13},{2,14},{3,15},{4,8},{5,9},{6,10},{7,11},{8,4},{9,5},... | collective-permute-start | bytes 184328 | tf_op jit(solution)/shard_map/ppermute | solution.py:463
  15.5 0.0 collective-permute-done.3.refs_2_
  15.5 2.1 %collective-permute-start.11 = (bf16[240,128]{1,0:T(8,128)(2,1)S(1)}, bf16[240,128]{1,0:T(8,128)(2,1)S(1)}, u32[]{:S(2)}, u32[]{:S(2)}) collective-permute-start(bf16[240,128]{1,0:T(8,128)(2,1)S(1)} %get-tuple-element.42), channel_id=1, source_target_pairs={{0,14},{1,15},{2,12},{3,13},{4,10},{5,11},{6,8},{7,9},{8,6},{9,7},... | collective-permute-start | bytes 184328 | tf_op jit(solution)/shard_map/ppermute | solution.py:463
  17.6 0.0 collective-permute-done.4.refs_3_
  17.6 1.1 %part.1.flat_ref = bf16[2,2,256,256]{3,2,1,0:T(8,128)(2,1)S(1)} custom-call(bf16[528,128]{1,0:T(8,128)(2,1)S(1)} %get-tuple-element.31.refs_0_, bf16[528,128]{1,0:T(8,128)(2,1)S(1)} %collective-permute-done.2.refs_1_, bf16[528,128]{1,0:T(8,128)(2,1)S(1)} %collective-permute-done.3.refs_2_, bf16[528,128]{1,0:T(8,128)(2,1)S(1)} %collective-permute-done.4.refs_3_), custom_call_target="tpu_custom_call" | custom-call | flops 1000000 | bytes 1048576 | tf_op jit(solution)/shard_map/part/pallas_call | solution.py:513
  18.7 0.0 collective-permute-done.5.listed_ref.refs_4_
  18.7 0.0 copy-done.2
  18.7 1.9 %part_far.1 = (bf16[384,128]{1,0:T(8,128)(2,1)S(1)}, bf16[384,128]{1,0:T(8,128)(2,1)S(1)}) custom-call(s32[1]{0:T(128)} %bitcast.place_ref, s32[16]{0:T(128)S(1)} %copy-done.2, bf16[272,128]{1,0:T(8,128)(2,1)S(1)} %collective-permute-done.5.listed_ref.refs_4_, bf16[2,2,256,256]{3,2,1,0:T(8,128)(2,1)S(1)} %part.1.flat_ref), custom_call_target="tpu_custom_call" | custom-call | flops 1000000000 | bytes 1048576 | tf_op jit(solution)/shard_map/part_far/pallas_call | solution.py:535
  20.7 0.1 collective-permute-start.7
  20.7 1.7 %collective-permute-start.6 = (bf16[384,128]{1,0:T(8,128)(2,1)S(1)}, bf16[384,128]{1,0:T(8,128)(2,1)S(1)}, u32[]{:S(2)}, u32[]{:S(2)}) collective-permute-start(bf16[384,128]{1,0:T(8,128)(2,1)S(1)} %get-tuple-element.37.after_1), channel_id=1, source_target_pairs={{0,8},{1,9},{2,10},{3,11},{4,12},{5,13},{6,14},{7,15},{8,0},{9,1},... | collective-permute-start | bytes 294920 | tf_op jit(solution)/shard_map/ppermute | solution.py:463
  22.5 1.9 %part_near.1 = (bf16[384,128]{1,0:T(8,128)(2,1)S(1)}, bf16[384,128]{1,0:T(8,128)(2,1)S(1)}) custom-call(s32[1]{0:T(128)} %bitcast.place_ref, s32[16]{0:T(128)S(1)} %copy-done.2, s32[2,2,512]{2,1,0:T(2,128)S(1)} %copy-done.1, s32[2,2,512]{2,1,0:T(2,128)S(1)} %collective-permute-done.near_pairs_ref, bf16[2,2,256,256]{3,2,1,0:T(8,128)(2,1)S(1)} %part.1.flat_ref), custom_call_target="tpu_custom_call" | custom-call | flops 1000000 | bytes 1048576 | tf_op jit(solution)/shard_map/part_near/pallas_call | solution.py:526
  24.4 0.0 collective-permute-done.9.refs_5_
  24.4 1.1 %collective-permute-start.8 = (bf16[384,128]{1,0:T(8,128)(2,1)S(1)}, bf16[384,128]{1,0:T(8,128)(2,1)S(1)}, u32[]{:S(2)}, u32[]{:S(2)}) collective-permute-start(bf16[384,128]{1,0:T(8,128)(2,1)S(1)} %get-tuple-element.39), channel_id=1, source_target_pairs={{0,1},{1,0},{2,3},{3,2},{4,5},{5,4},{6,7},{7,6},{8,9},{9,8},{10,11... | collective-permute-start | bytes 294920 | tf_op jit(solution)/shard_map/ppermute | solution.py:463
  25.5 0.6 %early.1.before_ref = f32[1280,128]{1,0:T(8,128)S(1)} custom-call(bf16[384,128]{1,0:T(8,128)(2,1)S(1)} %get-tuple-element.35.part_0.after_0, bf16[384,128]{1,0:T(8,128)(2,1)S(1)} %get-tuple-element.37.after_1, bf16[528,128]{1,0:T(8,128)(2,1)S(1)} %get-tuple-element.31.refs_0_, bf16[528,128]{1,0:T(8,128)(2,1)S(1)} %collective-permute-done.2.refs_1_, ...), custom_call_target="tpu_custom_call" | custom-call | flops 1000000 | bytes 1048576 | tf_op jit(solution)/shard_map/early/pallas_call | solution.py:545
  26.1 0.0 collective-permute-done.10.refs_0_
  26.1 0.0 collective-permute-done.11.refs_1_
  26.1 3.0 %full.1 = (bf16[2,2,256,256]{3,2,1,0:T(8,128)(2,1)S(1)}, bf16[320,128]{1,0:T(8,128)(2,1)S(1)}, bf16[320,128]{1,0:T(8,128)(2,1)S(1)}) custom-call(s32[1]{0:T(128)} %bitcast.place_ref, s32[16]{0:T(128)S(1)} %copy-done.2, bf16[272,128]{1,0:T(8,128)(2,1)S(1)} %collective-permute-done.5.listed_ref.refs_4_, f32[1280,128]{1,0:T(8,128)S(1)} %early.1.before_ref, ...), custom_call_target="tpu_custom_call" | custom-call | flops 10000000000 | bytes 1048576 | tf_op jit(solution)/shard_map/full/pallas_call | solution.py:558
  29.1 1.7 %collective-permute-start.14 = (bf16[320,128]{1,0:T(8,128)(2,1)S(1)}, bf16[320,128]{1,0:T(8,128)(2,1)S(1)}, u32[]{:S(2)}, u32[]{:S(2)}) collective-permute-start(bf16[320,128]{1,0:T(8,128)(2,1)S(1)} %get-tuple-element.49), channel_id=1, source_target_pairs={{0,8},{1,9},{2,10},{3,11},{4,12},{5,13},{6,14},{7,15},{8,0},{9,1},... | collective-permute-start | bytes 245768 | tf_op jit(solution)/shard_map/ppermute | solution.py:463
  30.8 0.6 %collective-permute-start.15 = (bf16[320,128]{1,0:T(8,128)(2,1)S(1)}, bf16[320,128]{1,0:T(8,128)(2,1)S(1)}, u32[]{:S(2)}, u32[]{:S(2)}) collective-permute-start(bf16[320,128]{1,0:T(8,128)(2,1)S(1)} %get-tuple-element.50), channel_id=1, source_target_pairs={{0,9},{1,8},{2,11},{3,10},{4,13},{5,12},{6,15},{7,14},{8,1},{9,0},... | collective-permute-start | bytes 245768 | tf_op jit(solution)/shard_map/ppermute | solution.py:463
  31.4 2.1 %full_near.1 = (bf16[320,128]{1,0:T(8,128)(2,1)S(1)}, bf16[160,128]{1,0:T(8,128)(2,1)S(1)}, bf16[160,128]{1,0:T(8,128)(2,1)S(1)}) custom-call(s32[1]{0:T(128)} %bitcast.place_ref, s32[16]{0:T(128)S(1)} %copy-done.2, s32[2,2,512]{2,1,0:T(2,128)S(1)} %copy-done.1, s32[2,2,512]{2,1,0:T(2,128)S(1)} %collective-permute-done.near_pairs_ref, ...), custom_call_target="tpu_custom_call" | custom-call | flops 500000000 | bytes 1048576 | tf_op jit(solution)/shard_map/full_near/pallas_call | solution.py:572
  33.6 0.0 collective-permute-done.7.part_3
  33.6 0.8 %collective-permute-start.12 = (bf16[160,128]{1,0:T(8,128)(2,1)S(1)}, bf16[160,128]{1,0:T(8,128)(2,1)S(1)}, u32[]{:S(2)}, u32[]{:S(2)}) collective-permute-start(bf16[160,128]{1,0:T(8,128)(2,1)S(1)} %get-tuple-element.45), channel_id=1, source_target_pairs={{0,1},{1,0},{2,3},{3,2},{4,5},{5,4},{6,7},{7,6},{8,9},{9,8},{10,11... | collective-permute-start | bytes 122888 | tf_op jit(solution)/shard_map/ppermute | solution.py:463
  34.4 0.0 collective-permute-done.6.part_2
  34.4 0.1 collective-permute-start.13
  34.5 0.0 collective-permute-done.8.part_1
  34.5 0.0 copy-done
  34.5 1.2 %part_lags.1.before_ref = f32[2,512,256]{2,1,0:T(8,128)S(1)} custom-call(s32[1]{0:T(128)} %bitcast.place_ref, f32[256,256]{1,0:T(8,128)S(1)} %copy-done, bf16[384,128]{1,0:T(8,128)(2,1)S(1)} %get-tuple-element.35.part_0.after_0, bf16[384,128]{1,0:T(8,128)(2,1)S(1)} %collective-permute-done.6.part_2, bf16[384,128]{1,0:T(8,128)(2,1)S(1)} %collective-permute-done.7.part_3, ...), custom_call_target="tpu_custom_call" | custom-call | flops 1000000 | bytes 1048576 | tf_op jit(solution)/shard_map/part_lags/pallas_call | solution.py:583
  35.8 0.0 collective-permute-done.12.refs_0_
  35.8 0.0 collective-permute-done.13.refs_1_
  35.8 0.7 %first_lags.1 = (f32[2,512,256]{2,1,0:T(8,128)S(1)}, bf16[2,80,512]{2,1,0:T(8,128)(2,1)S(1)}) custom-call(s32[1]{0:T(128)} %bitcast.place_ref, f32[256,256]{1,0:T(8,128)S(1)} %copy-done, f32[2,512,256]{2,1,0:T(8,128)S(1)} %part_lags.1.before_ref, bf16[320,128]{1,0:T(8,128)(2,1)S(1)} %get-tuple-element.44.full_0, ...), custom_call_target="tpu_custom_call" | custom-call | flops 1000000 | bytes 1048576 | tf_op jit(solution)/shard_map/first_lags/pallas_call | solution.py:592
  36.5 1.8 %collective-permute-done.14.refs_0_ = bf16[320,128]{1,0:T(8,128)(2,1)S(1)} collective-permute-done((bf16[320,128]{1,0:T(8,128)(2,1)S(1)}, bf16[320,128]{1,0:T(8,128)(2,1)S(1)}, u32[]{:S(2)}, u32[]{:S(2)}) %collective-permute-start.14) | collective-permute-done | bytes 81952 | tf_op jit(solution)/shard_map/ppermute | solution.py:463
  38.3 0.9 %collective-permute-done.15.refs_1_ = bf16[320,128]{1,0:T(8,128)(2,1)S(1)} collective-permute-done((bf16[320,128]{1,0:T(8,128)(2,1)S(1)}, bf16[320,128]{1,0:T(8,128)(2,1)S(1)}, u32[]{:S(2)}, u32[]{:S(2)}) %collective-permute-start.15) | collective-permute-done | bytes 81952 | tf_op jit(solution)/shard_map/ppermute | solution.py:463
  39.3 1.2 %lags.1 = f32[2,512,256]{2,1,0:T(8,128)} custom-call(f32[2,512,256]{2,1,0:T(8,128)S(1)} %get-tuple-element.47.first_ref, bf16[2,80,512]{2,1,0:T(8,128)(2,1)S(1)} %get-tuple-element.48.table_ref, bf16[320,128]{1,0:T(8,128)(2,1)S(1)} %collective-permute-done.14.refs_0_, bf16[320,128]{1,0:T(8,128)(2,1)S(1)} %collective-permute-done.15.refs_1_), custom_call_target="tpu_custom_call" | custom-call | flops 1000000000 | bytes 1048576 | tf_op jit(solution)/shard_map/lags/pallas_call | solution.py:604
  (3 shorter events, 0.0 us)
Async XLA Ops:
  0.0 2.6 %collective-permute-start.1 = (bf16[3,2,4,64,256]{4,3,2,1,0:T(8,128)(2,1)}, bf16[3,2,4,64,256]{4,3,2,1,0:T(8,128)(2,1)S(1)}, u32[]{:S(2)}, u32[]{:S(2)}) collective-permute-start(bf16[3,2,4,64,256]{4,3,2,1,0:T(8,128)(2,1)} %bitcast.2), channel_id=1, source_target_pairs={{0,1},{1,0},{2,3},{3,2},{4,5},{5,4},{6,7},{7,6},{8,9},{9,8},{10,11... | collective-permute-start | bytes 2359304 | tf_op jit(solution)/shard_map/ppermute | solution.py:463
  0.5 2.1 %collective-permute-start = (s32[2,2,512]{2,1,0:T(2,128)}, s32[2,2,512]{2,1,0:T(2,128)S(1)}, u32[]{:S(2)}, u32[]{:S(2)}) collective-permute-start(s32[2,2,512]{2,1,0:T(2,128)} %own_pairs_ref.5), channel_id=1, source_target_pairs={{0,1},{1,0},{2,3},{3,2},{4,5},{5,4},{6,7},{7,6},{8,9},{9,8},{10,11... | collective-permute-start | bytes 24584 | tf_op jit(solution)/shard_map/ppermute | solution.py:463
  0.5 1.1 %copy-start.3 = (bf16[3,1,512,256]{3,2,1,0:T(8,128)(2,1)S(1)}, bf16[3,1,512,256]{3,2,1,0:T(8,128)(2,1)}, u32[]{:S(2)}) copy-start(bf16[3,1,512,256]{3,2,1,0:T(8,128)(2,1)} %param.4) | copy-start | bytes 2359300
  1.6 0.9 %copy-start.1 = (s32[2,2,512]{2,1,0:T(2,128)S(1)}, s32[2,2,512]{2,1,0:T(2,128)}, u32[]{:S(2)}) copy-start(s32[2,2,512]{2,1,0:T(2,128)} %own_pairs_ref.5) | copy-start | bytes 24580
  3.1 8.8 %collective-permute-start.2 = (bf16[528,128]{1,0:T(8,128)(2,1)S(1)}, bf16[528,128]{1,0:T(8,128)(2,1)S(1)}, u32[]{:S(2)}, u32[]{:S(2)}) collective-permute-start(bf16[528,128]{1,0:T(8,128)(2,1)S(1)} %get-tuple-element.32), channel_id=1, source_target_pairs={{0,2},{1,3},{2,0},{3,1},{4,6},{5,7},{6,4},{7,5},{8,10},{9,11},{10,... | collective-permute-start | bytes 405512 | tf_op jit(solution)/shard_map/ppermute | solution.py:463
  6.0 9.5 %collective-permute-start.3 = (bf16[528,128]{1,0:T(8,128)(2,1)S(1)}, bf16[528,128]{1,0:T(8,128)(2,1)S(1)}, u32[]{:S(2)}, u32[]{:S(2)}) collective-permute-start(bf16[528,128]{1,0:T(8,128)(2,1)S(1)} %get-tuple-element.33), channel_id=1, source_target_pairs={{0,4},{1,5},{2,6},{3,7},{4,0},{5,1},{6,2},{7,3},{8,12},{9,13},{10,... | collective-permute-start | bytes 405512 | tf_op jit(solution)/shard_map/ppermute | solution.py:463
  7.6 10.0 %collective-permute-start.4 = (bf16[528,128]{1,0:T(8,128)(2,1)S(1)}, bf16[528,128]{1,0:T(8,128)(2,1)S(1)}, u32[]{:S(2)}, u32[]{:S(2)}) collective-permute-start(bf16[528,128]{1,0:T(8,128)(2,1)S(1)} %get-tuple-element.34), channel_id=1, source_target_pairs={{0,6},{1,7},{2,4},{3,5},{4,2},{5,3},{6,0},{7,1},{8,14},{9,15},{10,... | collective-permute-start | bytes 405512 | tf_op jit(solution)/shard_map/ppermute | solution.py:463
  7.6 11.1 %collective-permute-start.5 = (bf16[272,128]{1,0:T(8,128)(2,1)S(1)}, bf16[272,128]{1,0:T(8,128)(2,1)S(1)}, u32[]{:S(2)}, u32[]{:S(2)}) collective-permute-start(bf16[272,128]{1,0:T(8,128)(2,1)S(1)} %get-tuple-element.36), channel_id=1, source_target_pairs={{0,8},{1,9},{2,10},{3,11},{4,12},{5,13},{6,14},{7,15},{8,0},{9,1},... | collective-permute-start | bytes 208904 | tf_op jit(solution)/shard_map/ppermute | solution.py:463
  10.6 13.8 %collective-permute-start.9 = (bf16[240,128]{1,0:T(8,128)(2,1)S(1)}, bf16[240,128]{1,0:T(8,128)(2,1)S(1)}, u32[]{:S(2)}, u32[]{:S(2)}) collective-permute-start(bf16[240,128]{1,0:T(8,128)(2,1)S(1)} %get-tuple-element.40), channel_id=1, source_target_pairs={{0,10},{1,11},{2,8},{3,9},{4,14},{5,15},{6,12},{7,13},{8,2},{9,3},... | collective-permute-start | bytes 184328 | tf_op jit(solution)/shard_map/ppermute | solution.py:463
  11.9 14.2 %collective-permute-start.10 = (bf16[240,128]{1,0:T(8,128)(2,1)S(1)}, bf16[240,128]{1,0:T(8,128)(2,1)S(1)}, u32[]{:S(2)}, u32[]{:S(2)}) collective-permute-start(bf16[240,128]{1,0:T(8,128)(2,1)S(1)} %get-tuple-element.41), channel_id=1, source_target_pairs={{0,12},{1,13},{2,14},{3,15},{4,8},{5,9},{6,10},{7,11},{8,4},{9,5},... | collective-permute-start | bytes 184328 | tf_op jit(solution)/shard_map/ppermute | solution.py:463
  15.5 10.6 %collective-permute-start.11 = (bf16[240,128]{1,0:T(8,128)(2,1)S(1)}, bf16[240,128]{1,0:T(8,128)(2,1)S(1)}, u32[]{:S(2)}, u32[]{:S(2)}) collective-permute-start(bf16[240,128]{1,0:T(8,128)(2,1)S(1)} %get-tuple-element.42), channel_id=1, source_target_pairs={{0,14},{1,15},{2,12},{3,13},{4,10},{5,11},{6,8},{7,9},{8,6},{9,7},... | collective-permute-start | bytes 184328 | tf_op jit(solution)/shard_map/ppermute | solution.py:463
  17.6 1.1 %copy-start.2 = (s32[16]{0:T(128)S(1)}, s32[16]{0:T(128)}, u32[]{:S(2)}) copy-start(s32[16]{0:T(128)} %counts_ref.7) | copy-start | bytes 196
  20.7 12.9 %collective-permute-start.7 = (bf16[384,128]{1,0:T(8,128)(2,1)S(1)}, bf16[384,128]{1,0:T(8,128)(2,1)S(1)}, u32[]{:S(2)}, u32[]{:S(2)}) collective-permute-start(bf16[384,128]{1,0:T(8,128)(2,1)S(1)} %get-tuple-element.38), channel_id=1, source_target_pairs={{0,9},{1,8},{2,11},{3,10},{4,13},{5,12},{6,15},{7,14},{8,1},{9,0},... | collective-permute-start | bytes 294920 | tf_op jit(solution)/shard_map/ppermute | solution.py:463
  20.7 13.7 %collective-permute-start.6 = (bf16[384,128]{1,0:T(8,128)(2,1)S(1)}, bf16[384,128]{1,0:T(8,128)(2,1)S(1)}, u32[]{:S(2)}, u32[]{:S(2)}) collective-permute-start(bf16[384,128]{1,0:T(8,128)(2,1)S(1)} %get-tuple-element.37.after_1), channel_id=1, source_target_pairs={{0,8},{1,9},{2,10},{3,11},{4,12},{5,13},{6,14},{7,15},{8,0},{9,1},... | collective-permute-start | bytes 294920 | tf_op jit(solution)/shard_map/ppermute | solution.py:463
  24.4 10.1 %collective-permute-start.8 = (bf16[384,128]{1,0:T(8,128)(2,1)S(1)}, bf16[384,128]{1,0:T(8,128)(2,1)S(1)}, u32[]{:S(2)}, u32[]{:S(2)}) collective-permute-start(bf16[384,128]{1,0:T(8,128)(2,1)S(1)} %get-tuple-element.39), channel_id=1, source_target_pairs={{0,1},{1,0},{2,3},{3,2},{4,5},{5,4},{6,7},{7,6},{8,9},{9,8},{10,11... | collective-permute-start | bytes 294920 | tf_op jit(solution)/shard_map/ppermute | solution.py:463
  29.1 9.2 %collective-permute-start.14 = (bf16[320,128]{1,0:T(8,128)(2,1)S(1)}, bf16[320,128]{1,0:T(8,128)(2,1)S(1)}, u32[]{:S(2)}, u32[]{:S(2)}) collective-permute-start(bf16[320,128]{1,0:T(8,128)(2,1)S(1)} %get-tuple-element.49), channel_id=1, source_target_pairs={{0,8},{1,9},{2,10},{3,11},{4,12},{5,13},{6,14},{7,15},{8,0},{9,1},... | collective-permute-start | bytes 245768 | tf_op jit(solution)/shard_map/ppermute | solution.py:463
  30.8 8.4 %collective-permute-start.15 = (bf16[320,128]{1,0:T(8,128)(2,1)S(1)}, bf16[320,128]{1,0:T(8,128)(2,1)S(1)}, u32[]{:S(2)}, u32[]{:S(2)}) collective-permute-start(bf16[320,128]{1,0:T(8,128)(2,1)S(1)} %get-tuple-element.50), channel_id=1, source_target_pairs={{0,9},{1,8},{2,11},{3,10},{4,13},{5,12},{6,15},{7,14},{8,1},{9,0},... | collective-permute-start | bytes 245768 | tf_op jit(solution)/shard_map/ppermute | solution.py:463
  31.4 3.1 %copy-start = (f32[256,256]{1,0:T(8,128)S(1)}, f32[256,256]{1,0:T(8,128)}, u32[]{:S(2)}) copy-start(f32[256,256]{1,0:T(8,128)} %constant.6.clone.inverse_ref) | copy-start | bytes 786436
  33.6 2.2 %collective-permute-start.12 = (bf16[160,128]{1,0:T(8,128)(2,1)S(1)}, bf16[160,128]{1,0:T(8,128)(2,1)S(1)}, u32[]{:S(2)}, u32[]{:S(2)}) collective-permute-start(bf16[160,128]{1,0:T(8,128)(2,1)S(1)} %get-tuple-element.45), channel_id=1, source_target_pairs={{0,1},{1,0},{2,3},{3,2},{4,5},{5,4},{6,7},{7,6},{8,9},{9,8},{10,11... | collective-permute-start | bytes 122888 | tf_op jit(solution)/shard_map/ppermute | solution.py:463
  34.4 1.4 %collective-permute-start.13 = (bf16[160,128]{1,0:T(8,128)(2,1)S(1)}, bf16[160,128]{1,0:T(8,128)(2,1)S(1)}, u32[]{:S(2)}, u32[]{:S(2)}) collective-permute-start(bf16[160,128]{1,0:T(8,128)(2,1)S(1)} %get-tuple-element.46), channel_id=1, source_target_pairs={{0,1},{1,0},{2,3},{3,2},{4,5},{5,4},{6,7},{7,6},{8,9},{9,8},{10,11... | collective-permute-start | bytes 122888 | tf_op jit(solution)/shard_map/ppermute | solution.py:463

commit v23 on v22

--- a/solution.py
+++ b/solution.py
@@ -90,7 +90,7 @@
     return jnp.concatenate([lanes[start : start + count] for lanes in spectra])
 
 
-def own_kernel(place_ref, windows_ref, part_ref, full_ref, table_ref):
+def own_kernel(place_ref, windows_ref, part_ref, full_ref, table_ref, *fold_refs):
     groups, samples = windows_ref.shape[2], windows_ref.shape[4]
     quarter, group = place_of(place_ref, groups)
     table = [forward_rows((quarter % 2) * PART, PART, samples)]
@@ -99,6 +99,9 @@
     table = jnp.concatenate(table).astype(jnp.bfloat16)
     table_ref[...] = table
     held = full_ref.shape[1] - COMPS * 2 * FULL
+    for fold_ref, bins in zip(fold_refs, (PART, FULL)):
+        for at, matrix in enumerate(folds(fold_ref.shape[1], bins)[1]):
+            fold_ref[at] = matrix
     for mg in range(groups):
         spectra = station_spectra(windows_ref, group ^ mg, table)
         part_ref[mg] = rows_of(spectra, 0, 2 * PART).astype(jnp.bfloat16)
@@ -247,9 +250,10 @@
     return jnp.concatenate(picked)
 
 
-def pick(place_ref, counts_ref, listed, flat_ref, bins, mq, *picked_refs):
+def pick(place_ref, counts_ref, listed, flat_ref, fold_ref, bins, mq, *picked_refs):
     hot = hots(place_ref, counts_ref, listed, flat_ref.shape[2], bins, mq)
-    kinds, matrices = folds(listed.shape[0] // 4 * LANES, bins)
+    kinds = folds_of(listed.shape[0] // 4 * LANES, bins)
+    matrices = [fold_ref[at] for at in range(len(kinds))]
     picked = picks(place_ref, counts_ref.shape[0], hot, kinds, matrices, flat_ref, bins, mq)
     each = picked.shape[0] // len(picked_refs)
     for at, ref in enumerate(picked_refs):
@@ -329,11 +333,11 @@
     turn_blocks(cross_ref, PART, flat_ref)
 
 
-def far_kernel(bins, place_ref, counts_ref, listed_ref, flat_ref, picked_0, picked_1):
+def far_kernel(bins, place_ref, counts_ref, listed_ref, flat_ref, fold_ref, picked_0, picked_1):
     listed = listed_ref[cross_full(listed_ref)[2] :].astype(jnp.float32)
     listing = listed.shape[0] // 2
-    pick(place_ref, counts_ref, listed[:listing], flat_ref, bins, 2, picked_0)
-    pick(place_ref, counts_ref, listed[listing:], flat_ref, bins, 3, picked_1)
+    pick(place_ref, counts_ref, listed[:listing], flat_ref, fold_ref, bins, 2, picked_0)
+    pick(place_ref, counts_ref, listed[listing:], flat_ref, fold_ref, bins, 3, picked_1)
 
 
 def early_kernel(sides, after_0, after_1, *refs):
@@ -342,20 +346,20 @@
     add_cross(pieces, trace_ref, FULL, sums_ref)
 
 
-def full_kernel(place_ref, counts_ref, listed_ref, before_ref, *refs):
+def full_kernel(place_ref, counts_ref, listed_ref, fold_ref, before_ref, *refs):
     piece_refs, (flat_ref, picked_0, picked_1, trace_ref, cross_ref) = refs[:-5], refs[-5:]
     add_cross([cross_full(ref) for ref in piece_refs], trace_ref, FULL, cross_ref, before_ref)
     turn_blocks(cross_ref, FULL, flat_ref)
     listed = listed_ref[cross_full(listed_ref)[2] :].astype(jnp.float32)
     listing = listed.shape[0] // 2
-    pick(place_ref, counts_ref, listed[:listing], flat_ref, FULL, 2, picked_0)
-    pick(place_ref, counts_ref, listed[listing:], flat_ref, FULL, 3, picked_1)
-
-
-def near_kernel(bins, sent, place_ref, counts_ref, own_pairs_ref, near_pairs_ref, flat_ref, *refs):
+    pick(place_ref, counts_ref, listed[:listing], flat_ref, fold_ref, FULL, 2, picked_0)
+    pick(place_ref, counts_ref, listed[listing:], flat_ref, fold_ref, FULL, 3, picked_1)
+
+
+def near_kernel(bins, sent, place_ref, counts_ref, own_pairs_ref, near_pairs_ref, flat_ref, fold_ref, *refs):
     picked_0, *picked_1 = refs[-1 - sent :]
-    pick(place_ref, counts_ref, listing_of(near_pairs_ref, LANES), flat_ref, bins, 1, *picked_1)
-    pick(place_ref, counts_ref, listing_of(own_pairs_ref, LANES), flat_ref, bins, 0, picked_0)
+    pick(place_ref, counts_ref, listing_of(near_pairs_ref, LANES), flat_ref, fold_ref, bins, 1, *picked_1)
+    pick(place_ref, counts_ref, listing_of(own_pairs_ref, LANES), flat_ref, fold_ref, bins, 0, picked_0)
 
 
 def both_rounds(rows, sign):
@@ -477,15 +481,17 @@
     windows = windows.reshape(comps, 2, groups, 2 * SLOTS, samples)
     near_windows, near_pairs = swap(windows, 1), swap(pairs, 1)
     part_rows, full_rows = comps * 2 * PART, comps * 2 * FULL
-    part_spectra, full_spectra, table = pl.pallas_call(
+    part_spectra, full_spectra, table, part_fold, full_fold = pl.pallas_call(
         own_kernel,
         out_shape=[
             shape(groups, part_rows, LANES),
             shape(2 * groups, whole(full_rows, 16), LANES),
             shape(2 * PART + 4 * FULL, samples),
+            shape(len(folds_of(count, PART)), 4 * LANES, LANES),
+            shape(len(folds_of(count, FULL)), 4 * LANES, LANES),
         ],
         in_specs=[smem, vmem],
-        out_specs=[vmem] * 3,
+        out_specs=[vmem] * 5,
         compiler_params=params,
         cost_estimate=cost(1),
         name="own_spectra",
@@ -526,21 +532,21 @@
     part_0, part_1 = pl.pallas_call(
         functools.partial(near_kernel, PART, 1),
         out_shape=[part_packed, part_packed],
-        in_specs=[smem, smem] + [vmem] * 3,
+        in_specs=[smem, smem] + [vmem] * 4,
         out_specs=[vmem] * 2,
         compiler_params=params,
         cost_estimate=cost(0.001),
         name="part_near",
-    )(place, counts, pairs, near_pairs, part_flat)
+    )(place, counts, pairs, near_pairs, part_flat, part_fold)
     part_2, part_3 = pl.pallas_call(
         functools.partial(far_kernel, PART),
         out_shape=[part_packed, part_packed],
-        in_specs=[smem, smem, vmem, vmem],
+        in_specs=[smem, smem, vmem, vmem, vmem],
         out_specs=[vmem, vmem],
         compiler_params=params,
         cost_estimate=cost(1),
         name="part_far",
-    )(place, counts, far[0], part_flat)
+    )(place, counts, far[0], part_flat, part_fold)
     part_1 = swap(part_1, 1)
     sums = pl.pallas_call(
         functools.partial(early_kernel, groups),
@@ -558,7 +564,7 @@
     full_flat, full_2, full_3 = pl.pallas_call(
         full_kernel,
         out_shape=[full_blocks, full_packed, full_packed],
-        in_specs=[smem, smem] + [vmem] * (2 + len(late)),
+        in_specs=[smem, smem] + [vmem] * (3 + len(late)),
         out_specs=[vmem] * 3,
         scratch_shapes=[
             pltpu.VMEM((padded(len(late) * 2 * comps) * 2 * FULL, LANES), jnp.float32),
@@ -567,17 +573,17 @@
         compiler_params=params,
         cost_estimate=cost(10),
         name="full",
-    )(place, counts, far[0], sums, *late)
+    )(place, counts, far[0], full_fold, sums, *late)
     full_2, full_3 = swap(full_2, half), swap(full_3, half + 1)
     full_0, *full_1 = pl.pallas_call(
         functools.partial(near_kernel, FULL, 2),
         out_shape=[full_packed, half_packed, half_packed],
-        in_specs=[smem, smem] + [vmem] * 3,
+        in_specs=[smem, smem] + [vmem] * 4,
         out_specs=[vmem] * 3,
         compiler_params=params,
         cost_estimate=cost(0.5),
         name="full_near",
-    )(place, counts, pairs, near_pairs, full_flat)
+    )(place, counts, pairs, near_pairs, full_flat, full_fold)
     full_1 = [swap(x, 1) for x in full_1]
 
     part_lags = pl.pallas_call(

time: 40.6 us -> 41.5 us (1.022)
  local copies, waits for them, and re-layouts: 1.14 us -> 1.78 us
    pallas_call x1, Pallas kernels: 0.62 us -> 1.39 us  [on_device(): pl.pallas_call(own_kernel, out_shape=[shape(groups, part_rows, LANES), sh...]
    unnamed x8, local copies, waits for them, and re-layouts: 1.14 us -> 1.78 us
  transfers between devices with their start and end apart: 16 -> 16, of which waited for: 3 -> 2; matrix products, arithmetic and copies ran while one was open for 0% -> 0% of each run, Pallas kernels for 33% -> 32%
where the time goes in v23:
time: 41.5 us; the launch traced here: 41.3 us
  starting transfers between devices  21.2 us (51%)
  Pallas kernels  15.1 us (36%)
  waiting for transfers between devices  3.12 us (8%)
  local copies, waits for them, and re-layouts  1.78 us (4%)
    ppermute x16, starting transfers between devices, swap(): return lax.ppermute(x, 'cell', [(i, i ^ mask) for i in range(cells)])  21.2 us
    ppermute x16, waiting for transfers between devices, swap(): return lax.ppermute(x, 'cell', [(i, i ^ mask) for i in range(cells)])  3.12 us
    pallas_call x1, Pallas kernels, on_device(): pl.pallas_call(full_kernel, out_shape=[full_blocks, full_packed, full_pac...  2.69 us
    pallas_call x1, Pallas kernels, on_device(): pl.pallas_call(functools.partial(near_kernel, FULL, 2), out_shape=[full_p...  1.89 us
    pallas_call x1, Pallas kernels, on_device(): pl.pallas_call(functools.partial(near_kernel, PART, 1), out_shape=[part_p...  1.88 us
    pallas_call x1, Pallas kernels, on_device(): pl.pallas_call(functools.partial(far_kernel, PART), out_shape=[part_packe...  1.88 us
    unnamed x8, local copies, waits for them, and re-layouts  1.78 us
    pallas_call x1, Pallas kernels, on_device(): pl.pallas_call(own_kernel, out_shape=[shape(groups, part_rows, LANES), sh...  1.39 us
  transfers between devices with their start and end apart: 16, of which 2 were waited for; matrix products, arithmetic and copies ran while one was open for 0% of the time, Pallas kernels for 32%

profile of v23, /device:TPU:0, one launch (start us, length us, event | category | flops | bytes accessed | tf_op | source)
XLA Modules:
  0.0 41.3 jit_solution(17942758355854567946)
XLA Ops:
  0.0 0.5 %collective-permute-start.1 = (bf16[3,2,4,64,256]{4,3,2,1,0:T(8,128)(2,1)}, bf16[3,2,4,64,256]{4,3,2,1,0:T(8,128)(2,1)S(1)}, u32[]{:S(2)}, u32[]{:S(2)}) collective-permute-start(bf16[3,2,4,64,256]{4,3,2,1,0:T(8,128)(2,1)} %bitcast.2), channel_id=1, source_target_pairs={{0,1},{1,0},{2,3},{3,2},{4,5},{5,4},{6,7},{7,6},{8,9},{9,8},{10,11... | collective-permute-start | bytes 2359304 | tf_op jit(solution)/shard_map/ppermute | solution.py:467
  0.5 0.1 collective-permute-start
  0.5 1.1 %copy-done.3 = bf16[3,1,512,256]{3,2,1,0:T(8,128)(2,1)S(1)} copy-done((bf16[3,1,512,256]{3,2,1,0:T(8,128)(2,1)S(1)}, bf16[3,1,512,256]{3,2,1,0:T(8,128)(2,1)}, u32[]{:S(2)}) %copy-start.3) | copy-done | bytes 786456
  1.6 1.4 %own_spectra.1 = (bf16[4,144,128]{2,1,0:T(8,128)(2,1)S(1)}, bf16[8,128,128]{2,1,0:T(8,128)(2,1)S(1)}, bf16[128,256]{1,0:T(8,128)(2,1)S(1)}, bf16[4,512,128]{2,1,0:T(8,128)(2,1)S(1)}, bf16[8,512,128]{2,1,0:T(8,128)(2,1)S(1)}) custom-call(s32[1]{0:T(128)} %bitcast.place_ref, bf16[3,2,4,64,256]{4,3,2,1,0:T(8,128)(2,1)S(1)} %bitcast.3), custom_call_target="tpu_custom_call" | custom-call | flops 1000000000 | bytes 1048576 | tf_op jit(solution)/shard_map/own_spectra/pallas_call | solution.py:484
  3.0 0.0 collective-permute-done.near_pairs_ref
  3.1 0.0 collective-permute-done.1.windows_ref
  3.1 0.0 copy-done.1
  3.1 0.5 %near_spectra.1 = (bf16[528,128]{1,0:T(8,128)(2,1)S(1)}, bf16[528,128]{1,0:T(8,128)(2,1)S(1)}, bf16[528,128]{1,0:T(8,128)(2,1)S(1)}, bf16[528,128]{1,0:T(8,128)(...) custom-call(s32[1]{0:T(128)} %bitcast.place_ref, ...), custom_call_target="tpu_custom_call" | custom-call | flops 1000000000 | bytes 1048576 | tf_op jit(solution)/shard_map/near_spectra/pallas_call | solution.py:500
  3.6 3.0 %collective-permute-start.2 = (bf16[528,128]{1,0:T(8,128)(2,1)S(1)}, bf16[528,128]{1,0:T(8,128)(2,1)S(1)}, u32[]{:S(2)}, u32[]{:S(2)}) collective-permute-start(bf16[528,128]{1,0:T(8,128)(2,1)S(1)} %get-tuple-element.34), channel_id=1, source_target_pairs={{0,2},{1,3},{2,0},{3,1},{4,6},{5,7},{6,4},{7,5},{8,10},{9,11},{10,... | collective-permute-start | bytes 405512 | tf_op jit(solution)/shard_map/ppermute | solution.py:467
  6.6 1.6 %collective-permute-start.3 = (bf16[528,128]{1,0:T(8,128)(2,1)S(1)}, bf16[528,128]{1,0:T(8,128)(2,1)S(1)}, u32[]{:S(2)}, u32[]{:S(2)}) collective-permute-start(bf16[528,128]{1,0:T(8,128)(2,1)S(1)} %get-tuple-element.35), channel_id=1, source_target_pairs={{0,4},{1,5},{2,6},{3,7},{4,0},{5,1},{6,2},{7,3},{8,12},{9,13},{10,... | collective-permute-start | bytes 405512 | tf_op jit(solution)/shard_map/ppermute | solution.py:467
  8.2 0.0 collective-permute-start.4
  8.2 3.0 %collective-permute-start.5 = (bf16[272,128]{1,0:T(8,128)(2,1)S(1)}, bf16[272,128]{1,0:T(8,128)(2,1)S(1)}, u32[]{:S(2)}, u32[]{:S(2)}) collective-permute-start(bf16[272,128]{1,0:T(8,128)(2,1)S(1)} %get-tuple-element.39), channel_id=1, source_target_pairs={{0,8},{1,9},{2,10},{3,11},{4,12},{5,13},{6,14},{7,15},{8,0},{9,1},... | collective-permute-start | bytes 208904 | tf_op jit(solution)/shard_map/ppermute | solution.py:467
  11.2 1.3 %collective-permute-start.9 = (bf16[240,128]{1,0:T(8,128)(2,1)S(1)}, bf16[240,128]{1,0:T(8,128)(2,1)S(1)}, u32[]{:S(2)}, u32[]{:S(2)}) collective-permute-start(bf16[240,128]{1,0:T(8,128)(2,1)S(1)} %get-tuple-element.44), channel_id=1, source_target_pairs={{0,10},{1,11},{2,8},{3,9},{4,14},{5,15},{6,12},{7,13},{8,2},{9,3},... | collective-permute-start | bytes 184328 | tf_op jit(solution)/shard_map/ppermute | solution.py:467
  12.5 0.0 collective-permute-done.2.refs_1_
  12.5 3.6 %collective-permute-start.10 = (bf16[240,128]{1,0:T(8,128)(2,1)S(1)}, bf16[240,128]{1,0:T(8,128)(2,1)S(1)}, u32[]{:S(2)}, u32[]{:S(2)}) collective-permute-start(bf16[240,128]{1,0:T(8,128)(2,1)S(1)} %get-tuple-element.45), channel_id=1, source_target_pairs={{0,12},{1,13},{2,14},{3,15},{4,8},{5,9},{6,10},{7,11},{8,4},{9,5},... | collective-permute-start | bytes 184328 | tf_op jit(solution)/shard_map/ppermute | solution.py:467
  16.1 0.0 collective-permute-done.3.refs_2_
  16.1 2.1 %collective-permute-start.11 = (bf16[240,128]{1,0:T(8,128)(2,1)S(1)}, bf16[240,128]{1,0:T(8,128)(2,1)S(1)}, u32[]{:S(2)}, u32[]{:S(2)}) collective-permute-start(bf16[240,128]{1,0:T(8,128)(2,1)S(1)} %get-tuple-element.46), channel_id=1, source_target_pairs={{0,14},{1,15},{2,12},{3,13},{4,10},{5,11},{6,8},{7,9},{8,6},{9,7},... | collective-permute-start | bytes 184328 | tf_op jit(solution)/shard_map/ppermute | solution.py:467
  18.1 0.0 collective-permute-done.4.refs_3_
  18.1 1.1 %part.1.flat_ref = bf16[2,2,256,256]{3,2,1,0:T(8,128)(2,1)S(1)} custom-call(bf16[528,128]{1,0:T(8,128)(2,1)S(1)} %get-tuple-element.33.refs_0_, bf16[528,128]{1,0:T(8,128)(2,1)S(1)} %collective-permute-done.2.refs_1_, bf16[528,128]{1,0:T(8,128)(2,1)S(1)} %collective-permute-done.3.refs_2_, bf16[528,128]{1,0:T(8,128)(2,1)S(1)} %collective-permute-done.4.refs_3_), custom_call_target="tpu_custom_call" | custom-call | flops 1000000 | bytes 1048576 | tf_op jit(solution)/shard_map/part/pallas_call | solution.py:519
  19.3 0.0 copy-start.2
  19.3 0.0 collective-permute-done.5.listed_ref.refs_4_
  19.3 0.6 %copy-done.2 = s32[16]{0:T(128)S(1)} copy-done((s32[16]{0:T(128)S(1)}, s32[16]{0:T(128)}, u32[]{:S(2)}) %copy-start.2) | copy-done | bytes 88
  19.9 1.9 %part_far.1 = (bf16[384,128]{1,0:T(8,128)(2,1)S(1)}, bf16[384,128]{1,0:T(8,128)(2,1)S(1)}) custom-call(s32[1]{0:T(128)} %bitcast.place_ref, s32[16]{0:T(128)S(1)} %copy-done.2, bf16[272,128]{1,0:T(8,128)(2,1)S(1)} %collective-permute-done.5.listed_ref.refs_4_, bf16[2,2,256,256]{3,2,1,0:T(8,128)(2,1)S(1)} %part.1.flat_ref, ...), custom_call_target="tpu_custom_call" | custom-call | flops 1000000000 | bytes 1048576 | tf_op jit(solution)/shard_map/part_far/pallas_call | solution.py:541
  21.8 0.1 collective-permute-start.7
  21.9 1.5 %collective-permute-start.6 = (bf16[384,128]{1,0:T(8,128)(2,1)S(1)}, bf16[384,128]{1,0:T(8,128)(2,1)S(1)}, u32[]{:S(2)}, u32[]{:S(2)}) collective-permute-start(bf16[384,128]{1,0:T(8,128)(2,1)S(1)} %get-tuple-element.40.after_1), channel_id=1, source_target_pairs={{0,8},{1,9},{2,10},{3,11},{4,12},{5,13},{6,14},{7,15},{8,0},{9,1},... | collective-permute-start | bytes 294920 | tf_op jit(solution)/shard_map/ppermute | solution.py:467
  23.3 1.9 %part_near.1 = (bf16[384,128]{1,0:T(8,128)(2,1)S(1)}, bf16[384,128]{1,0:T(8,128)(2,1)S(1)}) custom-call(s32[1]{0:T(128)} %bitcast.place_ref, s32[16]{0:T(128)S(1)} %copy-done.2, s32[2,2,512]{2,1,0:T(2,128)S(1)} %copy-done.1, s32[2,2,512]{2,1,0:T(2,128)S(1)} %collective-permute-done.near_pairs_ref, bf16[2,2,256,256]{3,2,1,0:T(8,128)(2,1)S(1)} %part.1.flat_ref, ...), custom_call_target="tpu_custom_call" | custom-call | flops 1000000 | bytes 1048576 | tf_op jit(solution)/shard_map/part_near/pallas_call | solution.py:532
  25.2 0.0 collective-permute-done.9.refs_5_
  25.2 1.3 %collective-permute-start.8 = (bf16[384,128]{1,0:T(8,128)(2,1)S(1)}, bf16[384,128]{1,0:T(8,128)(2,1)S(1)}, u32[]{:S(2)}, u32[]{:S(2)}) collective-permute-start(bf16[384,128]{1,0:T(8,128)(2,1)S(1)} %get-tuple-element.42), channel_id=1, source_target_pairs={{0,1},{1,0},{2,3},{3,2},{4,5},{5,4},{6,7},{7,6},{8,9},{9,8},{10,11... | collective-permute-start | bytes 294920 | tf_op jit(solution)/shard_map/ppermute | solution.py:467
  26.6 0.6 %early.1.before_ref = f32[1280,128]{1,0:T(8,128)S(1)} custom-call(bf16[384,128]{1,0:T(8,128)(2,1)S(1)} %get-tuple-element.38.part_0.after_0, bf16[384,128]{1,0:T(8,128)(2,1)S(1)} %get-tuple-element.40.after_1, bf16[528,128]{1,0:T(8,128)(2,1)S(1)} %get-tuple-element.33.refs_0_, bf16[528,128]{1,0:T(8,128)(2,1)S(1)} %collective-permute-done.2.refs_1_, ...), custom_call_target="tpu_custom_call" | custom-call | flops 1000000 | bytes 1048576 | tf_op jit(solution)/shard_map/early/pallas_call | solution.py:551
  27.2 0.0 collective-permute-done.10.refs_0_
  27.2 0.0 collective-permute-done.11.refs_1_
  27.2 2.7 %full.1 = (bf16[2,2,256,256]{3,2,1,0:T(8,128)(2,1)S(1)}, bf16[320,128]{1,0:T(8,128)(2,1)S(1)}, bf16[320,128]{1,0:T(8,128)(2,1)S(1)}) custom-call(s32[1]{0:T(128)} %bitcast.place_ref, s32[16]{0:T(128)S(1)} %copy-done.2, bf16[272,128]{1,0:T(8,128)(2,1)S(1)} %collective-permute-done.5.listed_ref.refs_4_, bf16[8,512,128]{2,1,0:T(8,128)(2,1)S(1)} %get-tuple-element.43.fold_ref, ...), custom_call_target="tpu_custom_call" | custom-call | flops 10000000000 | bytes 1048576 | tf_op jit(solution)/shard_map/full/pallas_call | solution.py:564
  29.9 1.5 %collective-permute-start.14 = (bf16[320,128]{1,0:T(8,128)(2,1)S(1)}, bf16[320,128]{1,0:T(8,128)(2,1)S(1)}, u32[]{:S(2)}, u32[]{:S(2)}) collective-permute-start(bf16[320,128]{1,0:T(8,128)(2,1)S(1)} %get-tuple-element.53), channel_id=1, source_target_pairs={{0,8},{1,9},{2,10},{3,11},{4,12},{5,13},{6,14},{7,15},{8,0},{9,1},... | collective-permute-start | bytes 245768 | tf_op jit(solution)/shard_map/ppermute | solution.py:467
  31.3 0.9 %collective-permute-start.15 = (bf16[320,128]{1,0:T(8,128)(2,1)S(1)}, bf16[320,128]{1,0:T(8,128)(2,1)S(1)}, u32[]{:S(2)}, u32[]{:S(2)}) collective-permute-start(bf16[320,128]{1,0:T(8,128)(2,1)S(1)} %get-tuple-element.54), channel_id=1, source_target_pairs={{0,9},{1,8},{2,11},{3,10},{4,13},{5,12},{6,15},{7,14},{8,1},{9,0},... | collective-permute-start | bytes 245768 | tf_op jit(solution)/shard_map/ppermute | solution.py:467
  32.2 1.9 %full_near.1 = (bf16[320,128]{1,0:T(8,128)(2,1)S(1)}, bf16[160,128]{1,0:T(8,128)(2,1)S(1)}, bf16[160,128]{1,0:T(8,128)(2,1)S(1)}) custom-call(s32[1]{0:T(128)} %bitcast.place_ref, s32[16]{0:T(128)S(1)} %copy-done.2, s32[2,2,512]{2,1,0:T(2,128)S(1)} %copy-done.1, s32[2,2,512]{2,1,0:T(2,128)S(1)} %collective-permute-done.near_pairs_ref, ...), custom_call_target="tpu_custom_call" | custom-call | flops 500000000 | bytes 1048576 | tf_op jit(solution)/shard_map/full_near/pallas_call | solution.py:578
  34.1 0.0 collective-permute-done.7.part_3
  34.1 0.8 %collective-permute-start.12 = (bf16[160,128]{1,0:T(8,128)(2,1)S(1)}, bf16[160,128]{1,0:T(8,128)(2,1)S(1)}, u32[]{:S(2)}, u32[]{:S(2)}) collective-permute-start(bf16[160,128]{1,0:T(8,128)(2,1)S(1)} %get-tuple-element.49), channel_id=1, source_target_pairs={{0,1},{1,0},{2,3},{3,2},{4,5},{5,4},{6,7},{7,6},{8,9},{9,8},{10,11... | collective-permute-start | bytes 122888 | tf_op jit(solution)/shard_map/ppermute | solution.py:467
  35.0 0.0 collective-permute-done.6.part_2
  35.0 0.1 collective-permute-start.13
  35.0 0.0 collective-permute-done.8.part_1
  35.0 0.0 copy-done
  35.0 1.2 %part_lags.1.before_ref = f32[2,512,256]{2,1,0:T(8,128)S(1)} custom-call(s32[1]{0:T(128)} %bitcast.place_ref, f32[256,256]{1,0:T(8,128)S(1)} %copy-done, bf16[384,128]{1,0:T(8,128)(2,1)S(1)} %get-tuple-element.38.part_0.after_0, bf16[384,128]{1,0:T(8,128)(2,1)S(1)} %collective-permute-done.6.part_2, bf16[384,128]{1,0:T(8,128)(2,1)S(1)} %collective-permute-done.7.part_3, ...), custom_call_target="tpu_custom_call" | custom-call | flops 1000000 | bytes 1048576 | tf_op jit(solution)/shard_map/part_lags/pallas_call | solution.py:589
  36.3 0.0 collective-permute-done.12.refs_0_
  36.3 0.0 collective-permute-done.13.refs_1_
  36.3 0.7 %first_lags.1 = (f32[2,512,256]{2,1,0:T(8,128)S(1)}, bf16[2,80,512]{2,1,0:T(8,128)(2,1)S(1)}) custom-call(s32[1]{0:T(128)} %bitcast.place_ref, f32[256,256]{1,0:T(8,128)S(1)} %copy-done, f32[2,512,256]{2,1,0:T(8,128)S(1)} %part_lags.1.before_ref, bf16[320,128]{1,0:T(8,128)(2,1)S(1)} %get-tuple-element.48.full_0, ...), custom_call_target="tpu_custom_call" | custom-call | flops 1000000 | bytes 1048576 | tf_op jit(solution)/shard_map/first_lags/pallas_call | solution.py:598
  37.0 2.0 %collective-permute-done.14.refs_0_ = bf16[320,128]{1,0:T(8,128)(2,1)S(1)} collective-permute-done((bf16[320,128]{1,0:T(8,128)(2,1)S(1)}, bf16[320,128]{1,0:T(8,128)(2,1)S(1)}, u32[]{:S(2)}, u32[]{:S(2)}) %collective-permute-start.14) | collective-permute-done | bytes 81952 | tf_op jit(solution)/shard_map/ppermute | solution.py:467
  39.1 1.1 %collective-permute-done.15.refs_1_ = bf16[320,128]{1,0:T(8,128)(2,1)S(1)} collective-permute-done((bf16[320,128]{1,0:T(8,128)(2,1)S(1)}, bf16[320,128]{1,0:T(8,128)(2,1)S(1)}, u32[]{:S(2)}, u32[]{:S(2)}) %collective-permute-start.15) | collective-permute-done | bytes 81952 | tf_op jit(solution)/shard_map/ppermute | solution.py:467
  40.1 1.2 %lags.1 = f32[2,512,256]{2,1,0:T(8,128)} custom-call(f32[2,512,256]{2,1,0:T(8,128)S(1)} %get-tuple-element.51.first_ref, bf16[2,80,512]{2,1,0:T(8,128)(2,1)S(1)} %get-tuple-element.52.table_ref, bf16[320,128]{1,0:T(8,128)(2,1)S(1)} %collective-permute-done.14.refs_0_, bf16[320,128]{1,0:T(8,128)(2,1)S(1)} %collective-permute-done.15.refs_1_), custom_call_target="tpu_custom_call" | custom-call | flops 1000000000 | bytes 1048576 | tf_op jit(solution)/shard_map/lags/pallas_call | solution.py:610
  (3 shorter events, 0.0 us)
Async XLA Ops:
  0.0 3.1 %collective-permute-start.1 = (bf16[3,2,4,64,256]{4,3,2,1,0:T(8,128)(2,1)}, bf16[3,2,4,64,256]{4,3,2,1,0:T(8,128)(2,1)S(1)}, u32[]{:S(2)}, u32[]{:S(2)}) collective-permute-start(bf16[3,2,4,64,256]{4,3,2,1,0:T(8,128)(2,1)} %bitcast.2), channel_id=1, source_target_pairs={{0,1},{1,0},{2,3},{3,2},{4,5},{5,4},{6,7},{7,6},{8,9},{9,8},{10,11... | collective-permute-start | bytes 2359304 | tf_op jit(solution)/shard_map/ppermute | solution.py:467
  0.5 2.6 %collective-permute-start = (s32[2,2,512]{2,1,0:T(2,128)}, s32[2,2,512]{2,1,0:T(2,128)S(1)}, u32[]{:S(2)}, u32[]{:S(2)}) collective-permute-start(s32[2,2,512]{2,1,0:T(2,128)} %own_pairs_ref.5), channel_id=1, source_target_pairs={{0,1},{1,0},{2,3},{3,2},{4,5},{5,4},{6,7},{7,6},{8,9},{9,8},{10,11... | collective-permute-start | bytes 24584 | tf_op jit(solution)/shard_map/ppermute | solution.py:467
  0.5 1.1 %copy-start.3 = (bf16[3,1,512,256]{3,2,1,0:T(8,128)(2,1)S(1)}, bf16[3,1,512,256]{3,2,1,0:T(8,128)(2,1)}, u32[]{:S(2)}) copy-start(bf16[3,1,512,256]{3,2,1,0:T(8,128)(2,1)} %param.4) | copy-start | bytes 2359300
  1.6 1.4 %copy-start.1 = (s32[2,2,512]{2,1,0:T(2,128)S(1)}, s32[2,2,512]{2,1,0:T(2,128)}, u32[]{:S(2)}) copy-start(s32[2,2,512]{2,1,0:T(2,128)} %own_pairs_ref.5) | copy-start | bytes 24580
  3.6 8.9 %collective-permute-start.2 = (bf16[528,128]{1,0:T(8,128)(2,1)S(1)}, bf16[528,128]{1,0:T(8,128)(2,1)S(1)}, u32[]{:S(2)}, u32[]{:S(2)}) collective-permute-start(bf16[528,128]{1,0:T(8,128)(2,1)S(1)} %get-tuple-element.34), channel_id=1, source_target_pairs={{0,2},{1,3},{2,0},{3,1},{4,6},{5,7},{6,4},{7,5},{8,10},{9,11},{10,... | collective-permute-start | bytes 405512 | tf_op jit(solution)/shard_map/ppermute | solution.py:467
  6.6 9.5 %collective-permute-start.3 = (bf16[528,128]{1,0:T(8,128)(2,1)S(1)}, bf16[528,128]{1,0:T(8,128)(2,1)S(1)}, u32[]{:S(2)}, u32[]{:S(2)}) collective-permute-start(bf16[528,128]{1,0:T(8,128)(2,1)S(1)} %get-tuple-element.35), channel_id=1, source_target_pairs={{0,4},{1,5},{2,6},{3,7},{4,0},{5,1},{6,2},{7,3},{8,12},{9,13},{10,... | collective-permute-start | bytes 405512 | tf_op jit(solution)/shard_map/ppermute | solution.py:467
  8.2 10.0 %collective-permute-start.4 = (bf16[528,128]{1,0:T(8,128)(2,1)S(1)}, bf16[528,128]{1,0:T(8,128)(2,1)S(1)}, u32[]{:S(2)}, u32[]{:S(2)}) collective-permute-start(bf16[528,128]{1,0:T(8,128)(2,1)S(1)} %get-tuple-element.36), channel_id=1, source_target_pairs={{0,6},{1,7},{2,4},{3,5},{4,2},{5,3},{6,0},{7,1},{8,14},{9,15},{10,... | collective-permute-start | bytes 405512 | tf_op jit(solution)/shard_map/ppermute | solution.py:467
  8.2 11.1 %collective-permute-start.5 = (bf16[272,128]{1,0:T(8,128)(2,1)S(1)}, bf16[272,128]{1,0:T(8,128)(2,1)S(1)}, u32[]{:S(2)}, u32[]{:S(2)}) collective-permute-start(bf16[272,128]{1,0:T(8,128)(2,1)S(1)} %get-tuple-element.39), channel_id=1, source_target_pairs={{0,8},{1,9},{2,10},{3,11},{4,12},{5,13},{6,14},{7,15},{8,0},{9,1},... | collective-permute-start | bytes 208904 | tf_op jit(solution)/shard_map/ppermute | solution.py:467
  11.2 14.1 %collective-permute-start.9 = (bf16[240,128]{1,0:T(8,128)(2,1)S(1)}, bf16[240,128]{1,0:T(8,128)(2,1)S(1)}, u32[]{:S(2)}, u32[]{:S(2)}) collective-permute-start(bf16[240,128]{1,0:T(8,128)(2,1)S(1)} %get-tuple-element.44), channel_id=1, source_target_pairs={{0,10},{1,11},{2,8},{3,9},{4,14},{5,15},{6,12},{7,13},{8,2},{9,3},... | collective-permute-start | bytes 184328 | tf_op jit(solution)/shard_map/ppermute | solution.py:467
  12.5 14.7 %collective-permute-start.10 = (bf16[240,128]{1,0:T(8,128)(2,1)S(1)}, bf16[240,128]{1,0:T(8,128)(2,1)S(1)}, u32[]{:S(2)}, u32[]{:S(2)}) collective-permute-start(bf16[240,128]{1,0:T(8,128)(2,1)S(1)} %get-tuple-element.45), channel_id=1, source_target_pairs={{0,12},{1,13},{2,14},{3,15},{4,8},{5,9},{6,10},{7,11},{8,4},{9,5},... | collective-permute-start | bytes 184328 | tf_op jit(solution)/shard_map/ppermute | solution.py:467
  16.1 11.1 %collective-permute-start.11 = (bf16[240,128]{1,0:T(8,128)(2,1)S(1)}, bf16[240,128]{1,0:T(8,128)(2,1)S(1)}, u32[]{:S(2)}, u32[]{:S(2)}) collective-permute-start(bf16[240,128]{1,0:T(8,128)(2,1)S(1)} %get-tuple-element.46), channel_id=1, source_target_pairs={{0,14},{1,15},{2,12},{3,13},{4,10},{5,11},{6,8},{7,9},{8,6},{9,7},... | collective-permute-start | bytes 184328 | tf_op jit(solution)/shard_map/ppermute | solution.py:467
  19.3 0.7 %copy-start.2 = (s32[16]{0:T(128)S(1)}, s32[16]{0:T(128)}, u32[]{:S(2)}) copy-start(s32[16]{0:T(128)} %counts_ref.7) | copy-start | bytes 196
  21.8 12.3 %collective-permute-start.7 = (bf16[384,128]{1,0:T(8,128)(2,1)S(1)}, bf16[384,128]{1,0:T(8,128)(2,1)S(1)}, u32[]{:S(2)}, u32[]{:S(2)}) collective-permute-start(bf16[384,128]{1,0:T(8,128)(2,1)S(1)} %get-tuple-element.41), channel_id=1, source_target_pairs={{0,9},{1,8},{2,11},{3,10},{4,13},{5,12},{6,15},{7,14},{8,1},{9,0},... | collective-permute-start | bytes 294920 | tf_op jit(solution)/shard_map/ppermute | solution.py:467
  21.9 13.1 %collective-permute-start.6 = (bf16[384,128]{1,0:T(8,128)(2,1)S(1)}, bf16[384,128]{1,0:T(8,128)(2,1)S(1)}, u32[]{:S(2)}, u32[]{:S(2)}) collective-permute-start(bf16[384,128]{1,0:T(8,128)(2,1)S(1)} %get-tuple-element.40.after_1), channel_id=1, source_target_pairs={{0,8},{1,9},{2,10},{3,11},{4,12},{5,13},{6,14},{7,15},{8,0},{9,1},... | collective-permute-start | bytes 294920 | tf_op jit(solution)/shard_map/ppermute | solution.py:467
  25.2 9.8 %collective-permute-start.8 = (bf16[384,128]{1,0:T(8,128)(2,1)S(1)}, bf16[384,128]{1,0:T(8,128)(2,1)S(1)}, u32[]{:S(2)}, u32[]{:S(2)}) collective-permute-start(bf16[384,128]{1,0:T(8,128)(2,1)S(1)} %get-tuple-element.42), channel_id=1, source_target_pairs={{0,1},{1,0},{2,3},{3,2},{4,5},{5,4},{6,7},{7,6},{8,9},{9,8},{10,11... | collective-permute-start | bytes 294920 | tf_op jit(solution)/shard_map/ppermute | solution.py:467
  29.9 9.2 %collective-permute-start.14 = (bf16[320,128]{1,0:T(8,128)(2,1)S(1)}, bf16[320,128]{1,0:T(8,128)(2,1)S(1)}, u32[]{:S(2)}, u32[]{:S(2)}) collective-permute-start(bf16[320,128]{1,0:T(8,128)(2,1)S(1)} %get-tuple-element.53), channel_id=1, source_target_pairs={{0,8},{1,9},{2,10},{3,11},{4,12},{5,13},{6,14},{7,15},{8,0},{9,1},... | collective-permute-start | bytes 245768 | tf_op jit(solution)/shard_map/ppermute | solution.py:467
  31.3 8.8 %collective-permute-start.15 = (bf16[320,128]{1,0:T(8,128)(2,1)S(1)}, bf16[320,128]{1,0:T(8,128)(2,1)S(1)}, u32[]{:S(2)}, u32[]{:S(2)}) collective-permute-start(bf16[320,128]{1,0:T(8,128)(2,1)S(1)} %get-tuple-element.54), channel_id=1, source_target_pairs={{0,9},{1,8},{2,11},{3,10},{4,13},{5,12},{6,15},{7,14},{8,1},{9,0},... | collective-permute-start | bytes 245768 | tf_op jit(solution)/shard_map/ppermute | solution.py:467
  32.2 2.8 %copy-start = (f32[256,256]{1,0:T(8,128)S(1)}, f32[256,256]{1,0:T(8,128)}, u32[]{:S(2)}) copy-start(f32[256,256]{1,0:T(8,128)} %constant.6.clone.inverse_ref) | copy-start | bytes 786436
  34.1 2.2 %collective-permute-start.12 = (bf16[160,128]{1,0:T(8,128)(2,1)S(1)}, bf16[160,128]{1,0:T(8,128)(2,1)S(1)}, u32[]{:S(2)}, u32[]{:S(2)}) collective-permute-start(bf16[160,128]{1,0:T(8,128)(2,1)S(1)} %get-tuple-element.49), channel_id=1, source_target_pairs={{0,1},{1,0},{2,3},{3,2},{4,5},{5,4},{6,7},{7,6},{8,9},{9,8},{10,11... | collective-permute-start | bytes 122888 | tf_op jit(solution)/shard_map/ppermute | solution.py:467
  35.0 1.4 %collective-permute-start.13 = (bf16[160,128]{1,0:T(8,128)(2,1)S(1)}, bf16[160,128]{1,0:T(8,128)(2,1)S(1)}, u32[]{:S(2)}, u32[]{:S(2)}) collective-permute-start(bf16[160,128]{1,0:T(8,128)(2,1)S(1)} %get-tuple-element.50), channel_id=1, source_target_pairs={{0,1},{1,0},{2,3},{3,2},{4,5},{5,4},{6,7},{7,6},{8,9},{9,8},{10,11... | collective-permute-start | bytes 122888 | tf_op jit(solution)/shard_map/ppermute | solution.py:467

commit v24 on v22

--- a/solution.py
+++ b/solution.py
@@ -336,15 +336,10 @@
     pick(place_ref, counts_ref, listed[listing:], flat_ref, bins, 3, picked_1)
 
 
-def early_kernel(sides, after_0, after_1, *refs):
-    piece_refs, (sums_ref, trace_ref) = refs[:-2], refs[-2:]
+def full_kernel(sides, place_ref, counts_ref, listed_ref, after_0, after_1, *refs):
+    piece_refs, (flat_ref, picked_0, picked_1, trace_ref, cross_ref) = refs[:-5], refs[-5:]
     pieces = [side_full(ref) for ref in piece_refs[:sides]] + [cross_full(ref) for ref in piece_refs[sides:]]
-    add_cross(pieces, trace_ref, FULL, sums_ref)
-
-
-def full_kernel(place_ref, counts_ref, listed_ref, before_ref, *refs):
-    piece_refs, (flat_ref, picked_0, picked_1, trace_ref, cross_ref) = refs[:-5], refs[-5:]
-    add_cross([cross_full(ref) for ref in piece_refs], trace_ref, FULL, cross_ref, before_ref)
+    add_cross(pieces, trace_ref, FULL, cross_ref)
     turn_blocks(cross_ref, FULL, flat_ref)
     listed = listed_ref[cross_full(listed_ref)[2] :].astype(jnp.float32)
     listing = listed.shape[0] // 2
@@ -504,7 +499,6 @@
     arrived = [pieces[0]] + [swap(pieces[m], 2 * m) for m in range(1, 2 * groups)]
     sides, far = arrived[:groups], arrived[groups:]
 
-    early, late = far[: groups - 2], far[groups - 2 :]
     part_packed = shape(packed_rows(count, PART), LANES)
     full_packed = shape(packed_rows(count, FULL), LANES)
     half_packed = shape(packed_rows(count, FULL) // 2, LANES)
@@ -542,32 +536,22 @@
         name="part_far",
     )(place, counts, far[0], part_flat)
     part_1 = swap(part_1, 1)
-    sums = pl.pallas_call(
-        functools.partial(early_kernel, groups),
-        out_shape=shape(2 * SLOTS * FULL, LANES, dtype=jnp.float32),
-        in_specs=[pl.BlockSpec(memory_space=pl.ANY)] * 2 + [vmem] * (groups + len(early)),
-        out_specs=vmem,
-        scratch_shapes=[
-            pltpu.VMEM((padded((groups + len(early)) * 2 * comps) * 2 * FULL, LANES), jnp.float32)
-        ],
-        compiler_params=params,
-        cost_estimate=cost(0.001),
-        name="early",
-    )(part_0, part_2, *sides, *early)
-    part_2, part_3 = swap(part_2, half), swap(part_3, half + 1)
+    sent, part_2, part_3 = part_2, swap(part_2, half), swap(part_3, half + 1)
     full_flat, full_2, full_3 = pl.pallas_call(
-        full_kernel,
+        functools.partial(full_kernel, groups),
         out_shape=[full_blocks, full_packed, full_packed],
-        in_specs=[smem, smem] + [vmem] * (2 + len(late)),
+        in_specs=[smem, smem, vmem]
+        + [pl.BlockSpec(memory_space=pl.ANY)] * 2
+        + [vmem] * (2 * groups),
         out_specs=[vmem] * 3,
         scratch_shapes=[
-            pltpu.VMEM((padded(len(late) * 2 * comps) * 2 * FULL, LANES), jnp.float32),
+            pltpu.VMEM((padded(2 * groups * 2 * comps) * 2 * FULL, LANES), jnp.float32),
             pltpu.VMEM((2 * SLOTS * whole(FULL, 8), LANES), jnp.float32),
         ],
         compiler_params=params,
         cost_estimate=cost(10),
         name="full",
-    )(place, counts, far[0], sums, *late)
+    )(place, counts, far[0], part_0, sent, *sides, *far)
     full_2, full_3 = swap(full_2, half), swap(full_3, half + 1)
     full_0, *full_1 = pl.pallas_call(
         functools.partial(near_kernel, FULL, 2),

time: 40.6 us -> 40.4 us (level)
    pallas_call x2 -> x1, Pallas kernels: 3.56 us -> 3.15 us  [on_device(): pl.pallas_call(functools.partial(full_kernel, groups), out_shape=[full_bl...]
  transfers between devices with their start and end apart: 16 -> 16, of which waited for: 3 -> 3; matrix products, arithmetic and copies ran while one was open for 0% -> 0% of each run, Pallas kernels for 33% -> 32%
where the time goes in v24:
time: 40.4 us; the launch traced here: 40.2 us
  starting transfers between devices  21.1 us (52%)
  Pallas kernels  14.6 us (36%)
  waiting for transfers between devices  3.28 us (8%)
  local copies, waits for them, and re-layouts  1.14 us (3%)
    ppermute x16, starting transfers between devices, swap(): return lax.ppermute(x, 'cell', [(i, i ^ mask) for i in range(cells)])  21.1 us
    ppermute x16, waiting for transfers between devices, swap(): return lax.ppermute(x, 'cell', [(i, i ^ mask) for i in range(cells)])  3.28 us
    pallas_call x1, Pallas kernels, on_device(): pl.pallas_call(functools.partial(full_kernel, groups), out_shape=[full_bl...  3.15 us
    pallas_call x1, Pallas kernels, on_device(): pl.pallas_call(functools.partial(near_kernel, FULL, 2), out_shape=[full_p...  2.15 us
    pallas_call x1, Pallas kernels, on_device(): pl.pallas_call(functools.partial(far_kernel, PART), out_shape=[part_packe...  1.94 us
    pallas_call x1, Pallas kernels, on_device(): pl.pallas_call(functools.partial(near_kernel, PART, 1), out_shape=[part_p...  1.94 us
    pallas_call x1, Pallas kernels, on_device(): pl.pallas_call(functools.partial(part_lags_kernel, groups), out_shape=sha...  1.24 us
    pallas_call x1, Pallas kernels, on_device(): pl.pallas_call(lag_kernel, out_shape=shape(2, count, samples, dtype=jnp.f...  1.22 us
  transfers between devices with their start and end apart: 16, of which 3 were waited for; matrix products, arithmetic and copies ran while one was open for 0% of the time, Pallas kernels for 32%

profile of v24, /device:TPU:0, one launch (start us, length us, event | category | flops | bytes accessed | tf_op | source)
XLA Modules:
  0.0 40.2 jit_solution(7558290837534578554)
XLA Ops:
  0.0 0.5 %collective-permute-start.1 = (bf16[3,2,4,64,256]{4,3,2,1,0:T(8,128)(2,1)}, bf16[3,2,4,64,256]{4,3,2,1,0:T(8,128)(2,1)S(1)}, u32[]{:S(2)}, u32[]{:S(2)}) collective-permute-start(bf16[3,2,4,64,256]{4,3,2,1,0:T(8,128)(2,1)} %bitcast.2), channel_id=1, source_target_pairs={{0,1},{1,0},{2,3},{3,2},{4,5},{5,4},{6,7},{7,6},{8,9},{9,8},{10,11... | collective-permute-start | bytes 2359304 | tf_op jit(solution)/shard_map/ppermute | solution.py:458
  0.5 0.1 collective-permute-start
  0.5 0.0 copy-start.3
  0.5 1.1 %copy-done.3 = bf16[3,1,512,256]{3,2,1,0:T(8,128)(2,1)S(1)} copy-done((bf16[3,1,512,256]{3,2,1,0:T(8,128)(2,1)S(1)}, bf16[3,1,512,256]{3,2,1,0:T(8,128)(2,1)}, u32[]{:S(2)}) %copy-start.3) | copy-done | bytes 786456
  1.6 0.0 copy-start.1
  1.6 0.6 %own_spectra.1 = (bf16[4,144,128]{2,1,0:T(8,128)(2,1)S(1)}, bf16[8,128,128]{2,1,0:T(8,128)(2,1)S(1)}, bf16[128,256]{1,0:T(8,128)(2,1)S(1)}) custom-call(s32[1]{0:T(128)} %bitcast.place_ref, bf16[3,2,4,64,256]{4,3,2,1,0:T(8,128)(2,1)S(1)} %bitcast.3), custom_call_target="tpu_custom_call" | custom-call | flops 1000000000 | bytes 1048576 | tf_op jit(solution)/shard_map/own_spectra/pallas_call | solution.py:475
  2.3 0.3 collective-permute-done.near_pairs_ref
  2.6 0.0 collective-permute-done.1.windows_ref
  2.6 0.0 copy-done.1
  2.6 0.5 %near_spectra.1 = (bf16[528,128]{1,0:T(8,128)(2,1)S(1)}, bf16[528,128]{1,0:T(8,128)(2,1)S(1)}, bf16[528,128]{1,0:T(8,128)(2,1)S(1)}, bf16[528,128]{1,0:T(8,128)(...) custom-call(s32[1]{0:T(128)} %bitcast.place_ref, ...), custom_call_target="tpu_custom_call" | custom-call | flops 1000000000 | bytes 1048576 | tf_op jit(solution)/shard_map/near_spectra/pallas_call | solution.py:489
  3.1 3.0 %collective-permute-start.2 = (bf16[528,128]{1,0:T(8,128)(2,1)S(1)}, bf16[528,128]{1,0:T(8,128)(2,1)S(1)}, u32[]{:S(2)}, u32[]{:S(2)}) collective-permute-start(bf16[528,128]{1,0:T(8,128)(2,1)S(1)} %get-tuple-element.32), channel_id=1, source_target_pairs={{0,2},{1,3},{2,0},{3,1},{4,6},{5,7},{6,4},{7,5},{8,10},{9,11},{10,... | collective-permute-start | bytes 405512 | tf_op jit(solution)/shard_map/ppermute | solution.py:458
  6.0 1.6 %collective-permute-start.3 = (bf16[528,128]{1,0:T(8,128)(2,1)S(1)}, bf16[528,128]{1,0:T(8,128)(2,1)S(1)}, u32[]{:S(2)}, u32[]{:S(2)}) collective-permute-start(bf16[528,128]{1,0:T(8,128)(2,1)S(1)} %get-tuple-element.33), channel_id=1, source_target_pairs={{0,4},{1,5},{2,6},{3,7},{4,0},{5,1},{6,2},{7,3},{8,12},{9,13},{10,... | collective-permute-start | bytes 405512 | tf_op jit(solution)/shard_map/ppermute | solution.py:458
  7.6 0.0 collective-permute-start.4
  7.6 3.0 %collective-permute-start.5 = (bf16[272,128]{1,0:T(8,128)(2,1)S(1)}, bf16[272,128]{1,0:T(8,128)(2,1)S(1)}, u32[]{:S(2)}, u32[]{:S(2)}) collective-permute-start(bf16[272,128]{1,0:T(8,128)(2,1)S(1)} %get-tuple-element.36), channel_id=1, source_target_pairs={{0,8},{1,9},{2,10},{3,11},{4,12},{5,13},{6,14},{7,15},{8,0},{9,1},... | collective-permute-start | bytes 208904 | tf_op jit(solution)/shard_map/ppermute | solution.py:458
  10.6 1.3 %collective-permute-start.9 = (bf16[240,128]{1,0:T(8,128)(2,1)S(1)}, bf16[240,128]{1,0:T(8,128)(2,1)S(1)}, u32[]{:S(2)}, u32[]{:S(2)}) collective-permute-start(bf16[240,128]{1,0:T(8,128)(2,1)S(1)} %get-tuple-element.40), channel_id=1, source_target_pairs={{0,10},{1,11},{2,8},{3,9},{4,14},{5,15},{6,12},{7,13},{8,2},{9,3},... | collective-permute-start | bytes 184328 | tf_op jit(solution)/shard_map/ppermute | solution.py:458
  11.9 0.0 collective-permute-done.2.refs_1_
  11.9 3.6 %collective-permute-start.10 = (bf16[240,128]{1,0:T(8,128)(2,1)S(1)}, bf16[240,128]{1,0:T(8,128)(2,1)S(1)}, u32[]{:S(2)}, u32[]{:S(2)}) collective-permute-start(bf16[240,128]{1,0:T(8,128)(2,1)S(1)} %get-tuple-element.41), channel_id=1, source_target_pairs={{0,12},{1,13},{2,14},{3,15},{4,8},{5,9},{6,10},{7,11},{8,4},{9,5},... | collective-permute-start | bytes 184328 | tf_op jit(solution)/shard_map/ppermute | solution.py:458
  15.5 0.0 collective-permute-done.3.refs_2_
  15.5 2.1 %collective-permute-start.11 = (bf16[240,128]{1,0:T(8,128)(2,1)S(1)}, bf16[240,128]{1,0:T(8,128)(2,1)S(1)}, u32[]{:S(2)}, u32[]{:S(2)}) collective-permute-start(bf16[240,128]{1,0:T(8,128)(2,1)S(1)} %get-tuple-element.42), channel_id=1, source_target_pairs={{0,14},{1,15},{2,12},{3,13},{4,10},{5,11},{6,8},{7,9},{8,6},{9,7},... | collective-permute-start | bytes 184328 | tf_op jit(solution)/shard_map/ppermute | solution.py:458
  17.6 0.0 collective-permute-done.4.refs_3_
  17.6 1.1 %part.1.flat_ref = bf16[2,2,256,256]{3,2,1,0:T(8,128)(2,1)S(1)} custom-call(bf16[528,128]{1,0:T(8,128)(2,1)S(1)} %get-tuple-element.31.refs_0_, bf16[528,128]{1,0:T(8,128)(2,1)S(1)} %collective-permute-done.2.refs_1_, bf16[528,128]{1,0:T(8,128)(2,1)S(1)} %collective-permute-done.3.refs_2_, bf16[528,128]{1,0:T(8,128)(2,1)S(1)} %collective-permute-done.4.refs_3_), custom_call_target="tpu_custom_call" | custom-call | flops 1000000 | bytes 1048576 | tf_op jit(solution)/shard_map/part/pallas_call | solution.py:507
  18.7 0.0 collective-permute-done.5.listed_ref.refs_4_
  18.7 0.0 copy-done.2
  18.7 1.9 %part_far.1 = (bf16[384,128]{1,0:T(8,128)(2,1)S(1)}, bf16[384,128]{1,0:T(8,128)(2,1)S(1)}) custom-call(s32[1]{0:T(128)} %bitcast.place_ref, s32[16]{0:T(128)S(1)} %copy-done.2, bf16[272,128]{1,0:T(8,128)(2,1)S(1)} %collective-permute-done.5.listed_ref.refs_4_, bf16[2,2,256,256]{3,2,1,0:T(8,128)(2,1)S(1)} %part.1.flat_ref), custom_call_target="tpu_custom_call" | custom-call | flops 1000000000 | bytes 1048576 | tf_op jit(solution)/shard_map/part_far/pallas_call | solution.py:529
  20.7 0.1 collective-permute-start.7
  20.7 1.7 %collective-permute-start.6 = (bf16[384,128]{1,0:T(8,128)(2,1)S(1)}, bf16[384,128]{1,0:T(8,128)(2,1)S(1)}, u32[]{:S(2)}, u32[]{:S(2)}) collective-permute-start(bf16[384,128]{1,0:T(8,128)(2,1)S(1)} %get-tuple-element.37.after_1), channel_id=1, source_target_pairs={{0,8},{1,9},{2,10},{3,11},{4,12},{5,13},{6,14},{7,15},{8,0},{9,1},... | collective-permute-start | bytes 294920 | tf_op jit(solution)/shard_map/ppermute | solution.py:458
  22.5 1.9 %part_near.1 = (bf16[384,128]{1,0:T(8,128)(2,1)S(1)}, bf16[384,128]{1,0:T(8,128)(2,1)S(1)}) custom-call(s32[1]{0:T(128)} %bitcast.place_ref, s32[16]{0:T(128)S(1)} %copy-done.2, s32[2,2,512]{2,1,0:T(2,128)S(1)} %copy-done.1, s32[2,2,512]{2,1,0:T(2,128)S(1)} %collective-permute-done.near_pairs_ref, bf16[2,2,256,256]{3,2,1,0:T(8,128)(2,1)S(1)} %part.1.flat_ref), custom_call_target="tpu_custom_call" | custom-call | flops 1000000 | bytes 1048576 | tf_op jit(solution)/shard_map/part_near/pallas_call | solution.py:520
  24.4 0.0 collective-permute-done.9.refs_5_
  24.4 1.1 %collective-permute-start.8 = (bf16[384,128]{1,0:T(8,128)(2,1)S(1)}, bf16[384,128]{1,0:T(8,128)(2,1)S(1)}, u32[]{:S(2)}, u32[]{:S(2)}) collective-permute-start(bf16[384,128]{1,0:T(8,128)(2,1)S(1)} %get-tuple-element.39), channel_id=1, source_target_pairs={{0,1},{1,0},{2,3},{3,2},{4,5},{5,4},{6,7},{7,6},{8,9},{9,8},{10,11... | collective-permute-start | bytes 294920 | tf_op jit(solution)/shard_map/ppermute | solution.py:458
  25.5 0.0 collective-permute-done.10.refs_6_
  25.5 0.0 collective-permute-done.11.refs_7_
  25.5 3.1 %full.1 = (bf16[2,2,256,256]{3,2,1,0:T(8,128)(2,1)S(1)}, bf16[320,128]{1,0:T(8,128)(2,1)S(1)}, bf16[320,128]{1,0:T(8,128)(2,1)S(1)}) custom-call(s32[1]{0:T(128)} %bitcast.place_ref, s32[16]{0:T(128)S(1)} %copy-done.2, bf16[272,128]{1,0:T(8,128)(2,1)S(1)} %collective-permute-done.5.listed_ref.refs_4_, bf16[384,128]{1,0:T(8,128)(2,1)S(1)} %get-tuple-element.35.part_0.after_0, ...), custom_call_target="tpu_custom_call" | custom-call | flops 10000000000 | bytes 1048576 | tf_op jit(solution)/shard_map/full/pallas_call | solution.py:540
  28.7 1.7 %collective-permute-start.14 = (bf16[320,128]{1,0:T(8,128)(2,1)S(1)}, bf16[320,128]{1,0:T(8,128)(2,1)S(1)}, u32[]{:S(2)}, u32[]{:S(2)}) collective-permute-start(bf16[320,128]{1,0:T(8,128)(2,1)S(1)} %get-tuple-element.49), channel_id=1, source_target_pairs={{0,8},{1,9},{2,10},{3,11},{4,12},{5,13},{6,14},{7,15},{8,0},{9,1},... | collective-permute-start | bytes 245768 | tf_op jit(solution)/shard_map/ppermute | solution.py:458
  30.4 0.6 %collective-permute-start.15 = (bf16[320,128]{1,0:T(8,128)(2,1)S(1)}, bf16[320,128]{1,0:T(8,128)(2,1)S(1)}, u32[]{:S(2)}, u32[]{:S(2)}) collective-permute-start(bf16[320,128]{1,0:T(8,128)(2,1)S(1)} %get-tuple-element.50), channel_id=1, source_target_pairs={{0,9},{1,8},{2,11},{3,10},{4,13},{5,12},{6,15},{7,14},{8,1},{9,0},... | collective-permute-start | bytes 245768 | tf_op jit(solution)/shard_map/ppermute | solution.py:458
  31.0 2.1 %full_near.1 = (bf16[320,128]{1,0:T(8,128)(2,1)S(1)}, bf16[160,128]{1,0:T(8,128)(2,1)S(1)}, bf16[160,128]{1,0:T(8,128)(2,1)S(1)}) custom-call(s32[1]{0:T(128)} %bitcast.place_ref, s32[16]{0:T(128)S(1)} %copy-done.2, s32[2,2,512]{2,1,0:T(2,128)S(1)} %copy-done.1, s32[2,2,512]{2,1,0:T(2,128)S(1)} %collective-permute-done.near_pairs_ref, ...), custom_call_target="tpu_custom_call" | custom-call | flops 500000000 | bytes 1048576 | tf_op jit(solution)/shard_map/full_near/pallas_call | solution.py:556
  33.2 0.0 collective-permute-done.7.part_3
  33.2 0.8 %collective-permute-start.12 = (bf16[160,128]{1,0:T(8,128)(2,1)S(1)}, bf16[160,128]{1,0:T(8,128)(2,1)S(1)}, u32[]{:S(2)}, u32[]{:S(2)}) collective-permute-start(bf16[160,128]{1,0:T(8,128)(2,1)S(1)} %get-tuple-element.45), channel_id=1, source_target_pairs={{0,1},{1,0},{2,3},{3,2},{4,5},{5,4},{6,7},{7,6},{8,9},{9,8},{10,11... | collective-permute-start | bytes 122888 | tf_op jit(solution)/shard_map/ppermute | solution.py:458
  34.0 0.0 collective-permute-done.6.part_2
  34.0 0.1 collective-permute-start.13
  34.1 0.0 collective-permute-done.8.part_1
  34.1 0.0 copy-done
  34.1 1.2 %part_lags.1.before_ref = f32[2,512,256]{2,1,0:T(8,128)S(1)} custom-call(s32[1]{0:T(128)} %bitcast.place_ref, f32[256,256]{1,0:T(8,128)S(1)} %copy-done, bf16[384,128]{1,0:T(8,128)(2,1)S(1)} %get-tuple-element.35.part_0.after_0, bf16[384,128]{1,0:T(8,128)(2,1)S(1)} %collective-permute-done.6.part_2, bf16[384,128]{1,0:T(8,128)(2,1)S(1)} %collective-permute-done.7.part_3, ...), custom_call_target="tpu_custom_call" | custom-call | flops 1000000 | bytes 1048576 | tf_op jit(solution)/shard_map/part_lags/pallas_call | solution.py:567
  35.3 0.0 collective-permute-done.12.refs_0_
  35.4 0.0 collective-permute-done.13.refs_1_
  35.4 0.7 %first_lags.1 = (f32[2,512,256]{2,1,0:T(8,128)S(1)}, bf16[2,80,512]{2,1,0:T(8,128)(2,1)S(1)}) custom-call(s32[1]{0:T(128)} %bitcast.place_ref, f32[256,256]{1,0:T(8,128)S(1)} %copy-done, f32[2,512,256]{2,1,0:T(8,128)S(1)} %part_lags.1.before_ref, bf16[320,128]{1,0:T(8,128)(2,1)S(1)} %get-tuple-element.44.full_0, ...), custom_call_target="tpu_custom_call" | custom-call | flops 1000000 | bytes 1048576 | tf_op jit(solution)/shard_map/first_lags/pallas_call | solution.py:576
  36.1 1.9 %collective-permute-done.14.refs_0_ = bf16[320,128]{1,0:T(8,128)(2,1)S(1)} collective-permute-done((bf16[320,128]{1,0:T(8,128)(2,1)S(1)}, bf16[320,128]{1,0:T(8,128)(2,1)S(1)}, u32[]{:S(2)}, u32[]{:S(2)}) %collective-permute-start.14) | collective-permute-done | bytes 81952 | tf_op jit(solution)/shard_map/ppermute | solution.py:458
  38.0 1.0 %collective-permute-done.15.refs_1_ = bf16[320,128]{1,0:T(8,128)(2,1)S(1)} collective-permute-done((bf16[320,128]{1,0:T(8,128)(2,1)S(1)}, bf16[320,128]{1,0:T(8,128)(2,1)S(1)}, u32[]{:S(2)}, u32[]{:S(2)}) %collective-permute-start.15) | collective-permute-done | bytes 81952 | tf_op jit(solution)/shard_map/ppermute | solution.py:458
  39.0 1.2 %lags.1 = f32[2,512,256]{2,1,0:T(8,128)} custom-call(f32[2,512,256]{2,1,0:T(8,128)S(1)} %get-tuple-element.47.first_ref, bf16[2,80,512]{2,1,0:T(8,128)(2,1)S(1)} %get-tuple-element.48.table_ref, bf16[320,128]{1,0:T(8,128)(2,1)S(1)} %collective-permute-done.14.refs_0_, bf16[320,128]{1,0:T(8,128)(2,1)S(1)} %collective-permute-done.15.refs_1_), custom_call_target="tpu_custom_call" | custom-call | flops 1000000000 | bytes 1048576 | tf_op jit(solution)/shard_map/lags/pallas_call | solution.py:588
  (2 shorter events, 0.0 us)
Async XLA Ops:
  0.0 2.6 %collective-permute-start.1 = (bf16[3,2,4,64,256]{4,3,2,1,0:T(8,128)(2,1)}, bf16[3,2,4,64,256]{4,3,2,1,0:T(8,128)(2,1)S(1)}, u32[]{:S(2)}, u32[]{:S(2)}) collective-permute-start(bf16[3,2,4,64,256]{4,3,2,1,0:T(8,128)(2,1)} %bitcast.2), channel_id=1, source_target_pairs={{0,1},{1,0},{2,3},{3,2},{4,5},{5,4},{6,7},{7,6},{8,9},{9,8},{10,11... | collective-permute-start | bytes 2359304 | tf_op jit(solution)/shard_map/ppermute | solution.py:458
  0.5 2.1 %collective-permute-start = (s32[2,2,512]{2,1,0:T(2,128)}, s32[2,2,512]{2,1,0:T(2,128)S(1)}, u32[]{:S(2)}, u32[]{:S(2)}) collective-permute-start(s32[2,2,512]{2,1,0:T(2,128)} %own_pairs_ref.5), channel_id=1, source_target_pairs={{0,1},{1,0},{2,3},{3,2},{4,5},{5,4},{6,7},{7,6},{8,9},{9,8},{10,11... | collective-permute-start | bytes 24584 | tf_op jit(solution)/shard_map/ppermute | solution.py:458
  0.5 1.1 %copy-start.3 = (bf16[3,1,512,256]{3,2,1,0:T(8,128)(2,1)S(1)}, bf16[3,1,512,256]{3,2,1,0:T(8,128)(2,1)}, u32[]{:S(2)}) copy-start(bf16[3,1,512,256]{3,2,1,0:T(8,128)(2,1)} %param.4) | copy-start | bytes 2359300
  1.6 0.9 %copy-start.1 = (s32[2,2,512]{2,1,0:T(2,128)S(1)}, s32[2,2,512]{2,1,0:T(2,128)}, u32[]{:S(2)}) copy-start(s32[2,2,512]{2,1,0:T(2,128)} %own_pairs_ref.5) | copy-start | bytes 24580
  3.1 8.8 %collective-permute-start.2 = (bf16[528,128]{1,0:T(8,128)(2,1)S(1)}, bf16[528,128]{1,0:T(8,128)(2,1)S(1)}, u32[]{:S(2)}, u32[]{:S(2)}) collective-permute-start(bf16[528,128]{1,0:T(8,128)(2,1)S(1)} %get-tuple-element.32), channel_id=1, source_target_pairs={{0,2},{1,3},{2,0},{3,1},{4,6},{5,7},{6,4},{7,5},{8,10},{9,11},{10,... | collective-permute-start | bytes 405512 | tf_op jit(solution)/shard_map/ppermute | solution.py:458
  6.0 9.5 %collective-permute-start.3 = (bf16[528,128]{1,0:T(8,128)(2,1)S(1)}, bf16[528,128]{1,0:T(8,128)(2,1)S(1)}, u32[]{:S(2)}, u32[]{:S(2)}) collective-permute-start(bf16[528,128]{1,0:T(8,128)(2,1)S(1)} %get-tuple-element.33), channel_id=1, source_target_pairs={{0,4},{1,5},{2,6},{3,7},{4,0},{5,1},{6,2},{7,3},{8,12},{9,13},{10,... | collective-permute-start | bytes 405512 | tf_op jit(solution)/shard_map/ppermute | solution.py:458
  7.6 10.0 %collective-permute-start.4 = (bf16[528,128]{1,0:T(8,128)(2,1)S(1)}, bf16[528,128]{1,0:T(8,128)(2,1)S(1)}, u32[]{:S(2)}, u32[]{:S(2)}) collective-permute-start(bf16[528,128]{1,0:T(8,128)(2,1)S(1)} %get-tuple-element.34), channel_id=1, source_target_pairs={{0,6},{1,7},{2,4},{3,5},{4,2},{5,3},{6,0},{7,1},{8,14},{9,15},{10,... | collective-permute-start | bytes 405512 | tf_op jit(solution)/shard_map/ppermute | solution.py:458
  7.6 11.1 %collective-permute-start.5 = (bf16[272,128]{1,0:T(8,128)(2,1)S(1)}, bf16[272,128]{1,0:T(8,128)(2,1)S(1)}, u32[]{:S(2)}, u32[]{:S(2)}) collective-permute-start(bf16[272,128]{1,0:T(8,128)(2,1)S(1)} %get-tuple-element.36), channel_id=1, source_target_pairs={{0,8},{1,9},{2,10},{3,11},{4,12},{5,13},{6,14},{7,15},{8,0},{9,1},... | collective-permute-start | bytes 208904 | tf_op jit(solution)/shard_map/ppermute | solution.py:458
  10.6 13.8 %collective-permute-start.9 = (bf16[240,128]{1,0:T(8,128)(2,1)S(1)}, bf16[240,128]{1,0:T(8,128)(2,1)S(1)}, u32[]{:S(2)}, u32[]{:S(2)}) collective-permute-start(bf16[240,128]{1,0:T(8,128)(2,1)S(1)} %get-tuple-element.40), channel_id=1, source_target_pairs={{0,10},{1,11},{2,8},{3,9},{4,14},{5,15},{6,12},{7,13},{8,2},{9,3},... | collective-permute-start | bytes 184328 | tf_op jit(solution)/shard_map/ppermute | solution.py:458
  11.9 13.6 %collective-permute-start.10 = (bf16[240,128]{1,0:T(8,128)(2,1)S(1)}, bf16[240,128]{1,0:T(8,128)(2,1)S(1)}, u32[]{:S(2)}, u32[]{:S(2)}) collective-permute-start(bf16[240,128]{1,0:T(8,128)(2,1)S(1)} %get-tuple-element.41), channel_id=1, source_target_pairs={{0,12},{1,13},{2,14},{3,15},{4,8},{5,9},{6,10},{7,11},{8,4},{9,5},... | collective-permute-start | bytes 184328 | tf_op jit(solution)/shard_map/ppermute | solution.py:458
  15.5 10.0 %collective-permute-start.11 = (bf16[240,128]{1,0:T(8,128)(2,1)S(1)}, bf16[240,128]{1,0:T(8,128)(2,1)S(1)}, u32[]{:S(2)}, u32[]{:S(2)}) collective-permute-start(bf16[240,128]{1,0:T(8,128)(2,1)S(1)} %get-tuple-element.42), channel_id=1, source_target_pairs={{0,14},{1,15},{2,12},{3,13},{4,10},{5,11},{6,8},{7,9},{8,6},{9,7},... | collective-permute-start | bytes 184328 | tf_op jit(solution)/shard_map/ppermute | solution.py:458
  17.6 1.1 %copy-start.2 = (s32[16]{0:T(128)S(1)}, s32[16]{0:T(128)}, u32[]{:S(2)}) copy-start(s32[16]{0:T(128)} %counts_ref.7) | copy-start | bytes 196
  20.7 12.5 %collective-permute-start.7 = (bf16[384,128]{1,0:T(8,128)(2,1)S(1)}, bf16[384,128]{1,0:T(8,128)(2,1)S(1)}, u32[]{:S(2)}, u32[]{:S(2)}) collective-permute-start(bf16[384,128]{1,0:T(8,128)(2,1)S(1)} %get-tuple-element.38), channel_id=1, source_target_pairs={{0,9},{1,8},{2,11},{3,10},{4,13},{5,12},{6,15},{7,14},{8,1},{9,0},... | collective-permute-start | bytes 294920 | tf_op jit(solution)/shard_map/ppermute | solution.py:458
  20.7 13.3 %collective-permute-start.6 = (bf16[384,128]{1,0:T(8,128)(2,1)S(1)}, bf16[384,128]{1,0:T(8,128)(2,1)S(1)}, u32[]{:S(2)}, u32[]{:S(2)}) collective-permute-start(bf16[384,128]{1,0:T(8,128)(2,1)S(1)} %get-tuple-element.37.after_1), channel_id=1, source_target_pairs={{0,8},{1,9},{2,10},{3,11},{4,12},{5,13},{6,14},{7,15},{8,0},{9,1},... | collective-permute-start | bytes 294920 | tf_op jit(solution)/shard_map/ppermute | solution.py:458
  24.4 9.7 %collective-permute-start.8 = (bf16[384,128]{1,0:T(8,128)(2,1)S(1)}, bf16[384,128]{1,0:T(8,128)(2,1)S(1)}, u32[]{:S(2)}, u32[]{:S(2)}) collective-permute-start(bf16[384,128]{1,0:T(8,128)(2,1)S(1)} %get-tuple-element.39), channel_id=1, source_target_pairs={{0,1},{1,0},{2,3},{3,2},{4,5},{5,4},{6,7},{7,6},{8,9},{9,8},{10,11... | collective-permute-start | bytes 294920 | tf_op jit(solution)/shard_map/ppermute | solution.py:458
  28.7 9.3 %collective-permute-start.14 = (bf16[320,128]{1,0:T(8,128)(2,1)S(1)}, bf16[320,128]{1,0:T(8,128)(2,1)S(1)}, u32[]{:S(2)}, u32[]{:S(2)}) collective-permute-start(bf16[320,128]{1,0:T(8,128)(2,1)S(1)} %get-tuple-element.49), channel_id=1, source_target_pairs={{0,8},{1,9},{2,10},{3,11},{4,12},{5,13},{6,14},{7,15},{8,0},{9,1},... | collective-permute-start | bytes 245768 | tf_op jit(solution)/shard_map/ppermute | solution.py:458
  30.4 8.6 %collective-permute-start.15 = (bf16[320,128]{1,0:T(8,128)(2,1)S(1)}, bf16[320,128]{1,0:T(8,128)(2,1)S(1)}, u32[]{:S(2)}, u32[]{:S(2)}) collective-permute-start(bf16[320,128]{1,0:T(8,128)(2,1)S(1)} %get-tuple-element.50), channel_id=1, source_target_pairs={{0,9},{1,8},{2,11},{3,10},{4,13},{5,12},{6,15},{7,14},{8,1},{9,0},... | collective-permute-start | bytes 245768 | tf_op jit(solution)/shard_map/ppermute | solution.py:458
  31.0 3.1 %copy-start = (f32[256,256]{1,0:T(8,128)S(1)}, f32[256,256]{1,0:T(8,128)}, u32[]{:S(2)}) copy-start(f32[256,256]{1,0:T(8,128)} %constant.6.clone.inverse_ref) | copy-start | bytes 786436
  33.2 2.2 %collective-permute-start.12 = (bf16[160,128]{1,0:T(8,128)(2,1)S(1)}, bf16[160,128]{1,0:T(8,128)(2,1)S(1)}, u32[]{:S(2)}, u32[]{:S(2)}) collective-permute-start(bf16[160,128]{1,0:T(8,128)(2,1)S(1)} %get-tuple-element.45), channel_id=1, source_target_pairs={{0,1},{1,0},{2,3},{3,2},{4,5},{5,4},{6,7},{7,6},{8,9},{9,8},{10,11... | collective-permute-start | bytes 122888 | tf_op jit(solution)/shard_map/ppermute | solution.py:458
  34.0 1.4 %collective-permute-start.13 = (bf16[160,128]{1,0:T(8,128)(2,1)S(1)}, bf16[160,128]{1,0:T(8,128)(2,1)S(1)}, u32[]{:S(2)}, u32[]{:S(2)}) collective-permute-start(bf16[160,128]{1,0:T(8,128)(2,1)S(1)} %get-tuple-element.46), channel_id=1, source_target_pairs={{0,1},{1,0},{2,3},{3,2},{4,5},{5,4},{6,7},{7,6},{8,9},{9,8},{10,11... | collective-permute-start | bytes 122888 | tf_op jit(solution)/shard_map/ppermute | solution.py:458

commit v25 on v24

--- a/solution.py
+++ b/solution.py
@@ -82,8 +82,9 @@
     traces = jnp.concatenate(parts)
     energy = jnp.sum(jnp.square(traces.astype(jnp.float32)), axis=1, keepdims=True)
     raw = lax.dot_general(traces, table, NT, preferred_element_type=jnp.float32)
-    spectra = raw * lax.rsqrt(energy + EPSILON)
-    return [spectra[comp * LANES : (comp + 1) * LANES].T for comp in range(COMPS)]
+    spectra = (raw * lax.rsqrt(energy + EPSILON)).astype(jnp.bfloat16)
+    turned = [spectra[comp * LANES : (comp + 1) * LANES].T for comp in range(COMPS)]
+    return [lanes.astype(jnp.float32) for lanes in turned]
 
 
 def rows_of(spectra, start, count):

time: 40.4 us -> 40.4 us (level)
  no operation moved by 1% of the time
where the time goes in v25:
time: 40.4 us; the launch traced here: 40.2 us
  starting transfers between devices  21.1 us (52%)
  Pallas kernels  14.6 us (36%)
  waiting for transfers between devices  3.3 us (8%)
  local copies, waits for them, and re-layouts  1.14 us (3%)
    ppermute x16, starting transfers between devices, swap(): return lax.ppermute(x, 'cell', [(i, i ^ mask) for i in range(cells)])  21.1 us
    ppermute x16, waiting for transfers between devices, swap(): return lax.ppermute(x, 'cell', [(i, i ^ mask) for i in range(cells)])  3.3 us
    pallas_call x1, Pallas kernels, on_device(): pl.pallas_call(functools.partial(full_kernel, groups), out_shape=[full_bl...  3.15 us
    pallas_call x1, Pallas kernels, on_device(): pl.pallas_call(functools.partial(near_kernel, FULL, 2), out_shape=[full_p...  2.15 us
    pallas_call x1, Pallas kernels, on_device(): pl.pallas_call(functools.partial(far_kernel, PART), out_shape=[part_packe...  1.94 us
    pallas_call x1, Pallas kernels, on_device(): pl.pallas_call(functools.partial(near_kernel, PART, 1), out_shape=[part_p...  1.94 us
    pallas_call x1, Pallas kernels, on_device(): pl.pallas_call(functools.partial(part_lags_kernel, groups), out_shape=sha...  1.24 us
    pallas_call x1, Pallas kernels, on_device(): pl.pallas_call(lag_kernel, out_shape=shape(2, count, samples, dtype=jnp.f...  1.22 us
  transfers between devices with their start and end apart: 16, of which 3 were waited for; matrix products, arithmetic and copies ran while one was open for 0% of the time, Pallas kernels for 32%

profile of v25, /device:TPU:0, one launch (start us, length us, event | category | flops | bytes accessed | tf_op | source)
XLA Modules:
  0.0 40.2 jit_solution(17188426430761654616)
XLA Ops:
  0.0 0.5 %collective-permute-start.1 = (bf16[3,2,4,64,256]{4,3,2,1,0:T(8,128)(2,1)}, bf16[3,2,4,64,256]{4,3,2,1,0:T(8,128)(2,1)S(1)}, u32[]{:S(2)}, u32[]{:S(2)}) collective-permute-start(bf16[3,2,4,64,256]{4,3,2,1,0:T(8,128)(2,1)} %bitcast.2), channel_id=1, source_target_pairs={{0,1},{1,0},{2,3},{3,2},{4,5},{5,4},{6,7},{7,6},{8,9},{9,8},{10,11... | collective-permute-start | bytes 2359304 | tf_op jit(solution)/shard_map/ppermute | solution.py:459
  0.5 0.1 collective-permute-start
  0.5 0.0 copy-start.3
  0.5 1.1 %copy-done.3 = bf16[3,1,512,256]{3,2,1,0:T(8,128)(2,1)S(1)} copy-done((bf16[3,1,512,256]{3,2,1,0:T(8,128)(2,1)S(1)}, bf16[3,1,512,256]{3,2,1,0:T(8,128)(2,1)}, u32[]{:S(2)}) %copy-start.3) | copy-done | bytes 786456
  1.6 0.0 copy-start.1
  1.6 0.6 %own_spectra.1 = (bf16[4,144,128]{2,1,0:T(8,128)(2,1)S(1)}, bf16[8,128,128]{2,1,0:T(8,128)(2,1)S(1)}, bf16[128,256]{1,0:T(8,128)(2,1)S(1)}) custom-call(s32[1]{0:T(128)} %bitcast.place_ref, bf16[3,2,4,64,256]{4,3,2,1,0:T(8,128)(2,1)S(1)} %bitcast.3), custom_call_target="tpu_custom_call" | custom-call | flops 1000000000 | bytes 1048576 | tf_op jit(solution)/shard_map/own_spectra/pallas_call | solution.py:476
  2.3 0.3 collective-permute-done.near_pairs_ref
  2.6 0.0 collective-permute-done.1.windows_ref
  2.6 0.0 copy-done.1
  2.6 0.5 %near_spectra.1 = (bf16[528,128]{1,0:T(8,128)(2,1)S(1)}, bf16[528,128]{1,0:T(8,128)(2,1)S(1)}, bf16[528,128]{1,0:T(8,128)(2,1)S(1)}, bf16[528,128]{1,0:T(8,128)(...) custom-call(s32[1]{0:T(128)} %bitcast.place_ref, ...), custom_call_target="tpu_custom_call" | custom-call | flops 1000000000 | bytes 1048576 | tf_op jit(solution)/shard_map/near_spectra/pallas_call | solution.py:490
  3.1 3.0 %collective-permute-start.2 = (bf16[528,128]{1,0:T(8,128)(2,1)S(1)}, bf16[528,128]{1,0:T(8,128)(2,1)S(1)}, u32[]{:S(2)}, u32[]{:S(2)}) collective-permute-start(bf16[528,128]{1,0:T(8,128)(2,1)S(1)} %get-tuple-element.32), channel_id=1, source_target_pairs={{0,2},{1,3},{2,0},{3,1},{4,6},{5,7},{6,4},{7,5},{8,10},{9,11},{10,... | collective-permute-start | bytes 405512 | tf_op jit(solution)/shard_map/ppermute | solution.py:459
  6.0 1.6 %collective-permute-start.3 = (bf16[528,128]{1,0:T(8,128)(2,1)S(1)}, bf16[528,128]{1,0:T(8,128)(2,1)S(1)}, u32[]{:S(2)}, u32[]{:S(2)}) collective-permute-start(bf16[528,128]{1,0:T(8,128)(2,1)S(1)} %get-tuple-element.33), channel_id=1, source_target_pairs={{0,4},{1,5},{2,6},{3,7},{4,0},{5,1},{6,2},{7,3},{8,12},{9,13},{10,... | collective-permute-start | bytes 405512 | tf_op jit(solution)/shard_map/ppermute | solution.py:459
  7.6 0.0 collective-permute-start.4
  7.6 3.0 %collective-permute-start.5 = (bf16[272,128]{1,0:T(8,128)(2,1)S(1)}, bf16[272,128]{1,0:T(8,128)(2,1)S(1)}, u32[]{:S(2)}, u32[]{:S(2)}) collective-permute-start(bf16[272,128]{1,0:T(8,128)(2,1)S(1)} %get-tuple-element.36), channel_id=1, source_target_pairs={{0,8},{1,9},{2,10},{3,11},{4,12},{5,13},{6,14},{7,15},{8,0},{9,1},... | collective-permute-start | bytes 208904 | tf_op jit(solution)/shard_map/ppermute | solution.py:459
  10.6 1.3 %collective-permute-start.9 = (bf16[240,128]{1,0:T(8,128)(2,1)S(1)}, bf16[240,128]{1,0:T(8,128)(2,1)S(1)}, u32[]{:S(2)}, u32[]{:S(2)}) collective-permute-start(bf16[240,128]{1,0:T(8,128)(2,1)S(1)} %get-tuple-element.40), channel_id=1, source_target_pairs={{0,10},{1,11},{2,8},{3,9},{4,14},{5,15},{6,12},{7,13},{8,2},{9,3},... | collective-permute-start | bytes 184328 | tf_op jit(solution)/shard_map/ppermute | solution.py:459
  11.9 0.0 collective-permute-done.2.refs_1_
  11.9 3.6 %collective-permute-start.10 = (bf16[240,128]{1,0:T(8,128)(2,1)S(1)}, bf16[240,128]{1,0:T(8,128)(2,1)S(1)}, u32[]{:S(2)}, u32[]{:S(2)}) collective-permute-start(bf16[240,128]{1,0:T(8,128)(2,1)S(1)} %get-tuple-element.41), channel_id=1, source_target_pairs={{0,12},{1,13},{2,14},{3,15},{4,8},{5,9},{6,10},{7,11},{8,4},{9,5},... | collective-permute-start | bytes 184328 | tf_op jit(solution)/shard_map/ppermute | solution.py:459
  15.5 0.0 collective-permute-done.3.refs_2_
  15.5 2.1 %collective-permute-start.11 = (bf16[240,128]{1,0:T(8,128)(2,1)S(1)}, bf16[240,128]{1,0:T(8,128)(2,1)S(1)}, u32[]{:S(2)}, u32[]{:S(2)}) collective-permute-start(bf16[240,128]{1,0:T(8,128)(2,1)S(1)} %get-tuple-element.42), channel_id=1, source_target_pairs={{0,14},{1,15},{2,12},{3,13},{4,10},{5,11},{6,8},{7,9},{8,6},{9,7},... | collective-permute-start | bytes 184328 | tf_op jit(solution)/shard_map/ppermute | solution.py:459
  17.6 0.0 collective-permute-done.4.refs_3_
  17.6 1.1 %part.1.flat_ref = bf16[2,2,256,256]{3,2,1,0:T(8,128)(2,1)S(1)} custom-call(bf16[528,128]{1,0:T(8,128)(2,1)S(1)} %get-tuple-element.31.refs_0_, bf16[528,128]{1,0:T(8,128)(2,1)S(1)} %collective-permute-done.2.refs_1_, bf16[528,128]{1,0:T(8,128)(2,1)S(1)} %collective-permute-done.3.refs_2_, bf16[528,128]{1,0:T(8,128)(2,1)S(1)} %collective-permute-done.4.refs_3_), custom_call_target="tpu_custom_call" | custom-call | flops 1000000 | bytes 1048576 | tf_op jit(solution)/shard_map/part/pallas_call | solution.py:508
  18.7 0.0 collective-permute-done.5.listed_ref.refs_4_
  18.7 0.0 copy-done.2
  18.7 1.9 %part_far.1 = (bf16[384,128]{1,0:T(8,128)(2,1)S(1)}, bf16[384,128]{1,0:T(8,128)(2,1)S(1)}) custom-call(s32[1]{0:T(128)} %bitcast.place_ref, s32[16]{0:T(128)S(1)} %copy-done.2, bf16[272,128]{1,0:T(8,128)(2,1)S(1)} %collective-permute-done.5.listed_ref.refs_4_, bf16[2,2,256,256]{3,2,1,0:T(8,128)(2,1)S(1)} %part.1.flat_ref), custom_call_target="tpu_custom_call" | custom-call | flops 1000000000 | bytes 1048576 | tf_op jit(solution)/shard_map/part_far/pallas_call | solution.py:530
  20.7 0.1 collective-permute-start.7
  20.7 1.7 %collective-permute-start.6 = (bf16[384,128]{1,0:T(8,128)(2,1)S(1)}, bf16[384,128]{1,0:T(8,128)(2,1)S(1)}, u32[]{:S(2)}, u32[]{:S(2)}) collective-permute-start(bf16[384,128]{1,0:T(8,128)(2,1)S(1)} %get-tuple-element.37.after_1), channel_id=1, source_target_pairs={{0,8},{1,9},{2,10},{3,11},{4,12},{5,13},{6,14},{7,15},{8,0},{9,1},... | collective-permute-start | bytes 294920 | tf_op jit(solution)/shard_map/ppermute | solution.py:459
  22.5 1.9 %part_near.1 = (bf16[384,128]{1,0:T(8,128)(2,1)S(1)}, bf16[384,128]{1,0:T(8,128)(2,1)S(1)}) custom-call(s32[1]{0:T(128)} %bitcast.place_ref, s32[16]{0:T(128)S(1)} %copy-done.2, s32[2,2,512]{2,1,0:T(2,128)S(1)} %copy-done.1, s32[2,2,512]{2,1,0:T(2,128)S(1)} %collective-permute-done.near_pairs_ref, bf16[2,2,256,256]{3,2,1,0:T(8,128)(2,1)S(1)} %part.1.flat_ref), custom_call_target="tpu_custom_call" | custom-call | flops 1000000 | bytes 1048576 | tf_op jit(solution)/shard_map/part_near/pallas_call | solution.py:521
  24.4 0.0 collective-permute-done.9.refs_5_
  24.4 1.1 %collective-permute-start.8 = (bf16[384,128]{1,0:T(8,128)(2,1)S(1)}, bf16[384,128]{1,0:T(8,128)(2,1)S(1)}, u32[]{:S(2)}, u32[]{:S(2)}) collective-permute-start(bf16[384,128]{1,0:T(8,128)(2,1)S(1)} %get-tuple-element.39), channel_id=1, source_target_pairs={{0,1},{1,0},{2,3},{3,2},{4,5},{5,4},{6,7},{7,6},{8,9},{9,8},{10,11... | collective-permute-start | bytes 294920 | tf_op jit(solution)/shard_map/ppermute | solution.py:459
  25.5 0.0 collective-permute-done.10.refs_6_
  25.5 0.0 collective-permute-done.11.refs_7_
  25.5 3.1 %full.1 = (bf16[2,2,256,256]{3,2,1,0:T(8,128)(2,1)S(1)}, bf16[320,128]{1,0:T(8,128)(2,1)S(1)}, bf16[320,128]{1,0:T(8,128)(2,1)S(1)}) custom-call(s32[1]{0:T(128)} %bitcast.place_ref, s32[16]{0:T(128)S(1)} %copy-done.2, bf16[272,128]{1,0:T(8,128)(2,1)S(1)} %collective-permute-done.5.listed_ref.refs_4_, bf16[384,128]{1,0:T(8,128)(2,1)S(1)} %get-tuple-element.35.part_0.after_0, ...), custom_call_target="tpu_custom_call" | custom-call | flops 10000000000 | bytes 1048576 | tf_op jit(solution)/shard_map/full/pallas_call | solution.py:541
  28.7 1.7 %collective-permute-start.14 = (bf16[320,128]{1,0:T(8,128)(2,1)S(1)}, bf16[320,128]{1,0:T(8,128)(2,1)S(1)}, u32[]{:S(2)}, u32[]{:S(2)}) collective-permute-start(bf16[320,128]{1,0:T(8,128)(2,1)S(1)} %get-tuple-element.49), channel_id=1, source_target_pairs={{0,8},{1,9},{2,10},{3,11},{4,12},{5,13},{6,14},{7,15},{8,0},{9,1},... | collective-permute-start | bytes 245768 | tf_op jit(solution)/shard_map/ppermute | solution.py:459
  30.4 0.6 %collective-permute-start.15 = (bf16[320,128]{1,0:T(8,128)(2,1)S(1)}, bf16[320,128]{1,0:T(8,128)(2,1)S(1)}, u32[]{:S(2)}, u32[]{:S(2)}) collective-permute-start(bf16[320,128]{1,0:T(8,128)(2,1)S(1)} %get-tuple-element.50), channel_id=1, source_target_pairs={{0,9},{1,8},{2,11},{3,10},{4,13},{5,12},{6,15},{7,14},{8,1},{9,0},... | collective-permute-start | bytes 245768 | tf_op jit(solution)/shard_map/ppermute | solution.py:459
  31.0 2.1 %full_near.1 = (bf16[320,128]{1,0:T(8,128)(2,1)S(1)}, bf16[160,128]{1,0:T(8,128)(2,1)S(1)}, bf16[160,128]{1,0:T(8,128)(2,1)S(1)}) custom-call(s32[1]{0:T(128)} %bitcast.place_ref, s32[16]{0:T(128)S(1)} %copy-done.2, s32[2,2,512]{2,1,0:T(2,128)S(1)} %copy-done.1, s32[2,2,512]{2,1,0:T(2,128)S(1)} %collective-permute-done.near_pairs_ref, ...), custom_call_target="tpu_custom_call" | custom-call | flops 500000000 | bytes 1048576 | tf_op jit(solution)/shard_map/full_near/pallas_call | solution.py:557
  33.2 0.0 collective-permute-done.7.part_3
  33.2 0.8 %collective-permute-start.12 = (bf16[160,128]{1,0:T(8,128)(2,1)S(1)}, bf16[160,128]{1,0:T(8,128)(2,1)S(1)}, u32[]{:S(2)}, u32[]{:S(2)}) collective-permute-start(bf16[160,128]{1,0:T(8,128)(2,1)S(1)} %get-tuple-element.45), channel_id=1, source_target_pairs={{0,1},{1,0},{2,3},{3,2},{4,5},{5,4},{6,7},{7,6},{8,9},{9,8},{10,11... | collective-permute-start | bytes 122888 | tf_op jit(solution)/shard_map/ppermute | solution.py:459
  34.0 0.0 collective-permute-done.6.part_2
  34.0 0.1 collective-permute-start.13
  34.1 0.0 collective-permute-done.8.part_1
  34.1 0.0 copy-done
  34.1 1.2 %part_lags.1.before_ref = f32[2,512,256]{2,1,0:T(8,128)S(1)} custom-call(s32[1]{0:T(128)} %bitcast.place_ref, f32[256,256]{1,0:T(8,128)S(1)} %copy-done, bf16[384,128]{1,0:T(8,128)(2,1)S(1)} %get-tuple-element.35.part_0.after_0, bf16[384,128]{1,0:T(8,128)(2,1)S(1)} %collective-permute-done.6.part_2, bf16[384,128]{1,0:T(8,128)(2,1)S(1)} %collective-permute-done.7.part_3, ...), custom_call_target="tpu_custom_call" | custom-call | flops 1000000 | bytes 1048576 | tf_op jit(solution)/shard_map/part_lags/pallas_call | solution.py:568
  35.3 0.0 collective-permute-done.12.refs_0_
  35.4 0.0 collective-permute-done.13.refs_1_
  35.4 0.7 %first_lags.1 = (f32[2,512,256]{2,1,0:T(8,128)S(1)}, bf16[2,80,512]{2,1,0:T(8,128)(2,1)S(1)}) custom-call(s32[1]{0:T(128)} %bitcast.place_ref, f32[256,256]{1,0:T(8,128)S(1)} %copy-done, f32[2,512,256]{2,1,0:T(8,128)S(1)} %part_lags.1.before_ref, bf16[320,128]{1,0:T(8,128)(2,1)S(1)} %get-tuple-element.44.full_0, ...), custom_call_target="tpu_custom_call" | custom-call | flops 1000000 | bytes 1048576 | tf_op jit(solution)/shard_map/first_lags/pallas_call | solution.py:577
  36.1 1.9 %collective-permute-done.14.refs_0_ = bf16[320,128]{1,0:T(8,128)(2,1)S(1)} collective-permute-done((bf16[320,128]{1,0:T(8,128)(2,1)S(1)}, bf16[320,128]{1,0:T(8,128)(2,1)S(1)}, u32[]{:S(2)}, u32[]{:S(2)}) %collective-permute-start.14) | collective-permute-done | bytes 81952 | tf_op jit(solution)/shard_map/ppermute | solution.py:459
  38.0 1.0 %collective-permute-done.15.refs_1_ = bf16[320,128]{1,0:T(8,128)(2,1)S(1)} collective-permute-done((bf16[320,128]{1,0:T(8,128)(2,1)S(1)}, bf16[320,128]{1,0:T(8,128)(2,1)S(1)}, u32[]{:S(2)}, u32[]{:S(2)}) %collective-permute-start.15) | collective-permute-done | bytes 81952 | tf_op jit(solution)/shard_map/ppermute | solution.py:459
  39.0 1.2 %lags.1 = f32[2,512,256]{2,1,0:T(8,128)} custom-call(f32[2,512,256]{2,1,0:T(8,128)S(1)} %get-tuple-element.47.first_ref, bf16[2,80,512]{2,1,0:T(8,128)(2,1)S(1)} %get-tuple-element.48.table_ref, bf16[320,128]{1,0:T(8,128)(2,1)S(1)} %collective-permute-done.14.refs_0_, bf16[320,128]{1,0:T(8,128)(2,1)S(1)} %collective-permute-done.15.refs_1_), custom_call_target="tpu_custom_call" | custom-call | flops 1000000000 | bytes 1048576 | tf_op jit(solution)/shard_map/lags/pallas_call | solution.py:589
  (2 shorter events, 0.0 us)
Async XLA Ops:
  0.0 2.6 %collective-permute-start.1 = (bf16[3,2,4,64,256]{4,3,2,1,0:T(8,128)(2,1)}, bf16[3,2,4,64,256]{4,3,2,1,0:T(8,128)(2,1)S(1)}, u32[]{:S(2)}, u32[]{:S(2)}) collective-permute-start(bf16[3,2,4,64,256]{4,3,2,1,0:T(8,128)(2,1)} %bitcast.2), channel_id=1, source_target_pairs={{0,1},{1,0},{2,3},{3,2},{4,5},{5,4},{6,7},{7,6},{8,9},{9,8},{10,11... | collective-permute-start | bytes 2359304 | tf_op jit(solution)/shard_map/ppermute | solution.py:459
  0.5 2.1 %collective-permute-start = (s32[2,2,512]{2,1,0:T(2,128)}, s32[2,2,512]{2,1,0:T(2,128)S(1)}, u32[]{:S(2)}, u32[]{:S(2)}) collective-permute-start(s32[2,2,512]{2,1,0:T(2,128)} %own_pairs_ref.5), channel_id=1, source_target_pairs={{0,1},{1,0},{2,3},{3,2},{4,5},{5,4},{6,7},{7,6},{8,9},{9,8},{10,11... | collective-permute-start | bytes 24584 | tf_op jit(solution)/shard_map/ppermute | solution.py:459
  0.5 1.1 %copy-start.3 = (bf16[3,1,512,256]{3,2,1,0:T(8,128)(2,1)S(1)}, bf16[3,1,512,256]{3,2,1,0:T(8,128)(2,1)}, u32[]{:S(2)}) copy-start(bf16[3,1,512,256]{3,2,1,0:T(8,128)(2,1)} %param.4) | copy-start | bytes 2359300
  1.6 0.9 %copy-start.1 = (s32[2,2,512]{2,1,0:T(2,128)S(1)}, s32[2,2,512]{2,1,0:T(2,128)}, u32[]{:S(2)}) copy-start(s32[2,2,512]{2,1,0:T(2,128)} %own_pairs_ref.5) | copy-start | bytes 24580
  3.1 8.8 %collective-permute-start.2 = (bf16[528,128]{1,0:T(8,128)(2,1)S(1)}, bf16[528,128]{1,0:T(8,128)(2,1)S(1)}, u32[]{:S(2)}, u32[]{:S(2)}) collective-permute-start(bf16[528,128]{1,0:T(8,128)(2,1)S(1)} %get-tuple-element.32), channel_id=1, source_target_pairs={{0,2},{1,3},{2,0},{3,1},{4,6},{5,7},{6,4},{7,5},{8,10},{9,11},{10,... | collective-permute-start | bytes 405512 | tf_op jit(solution)/shard_map/ppermute | solution.py:459
  6.0 9.5 %collective-permute-start.3 = (bf16[528,128]{1,0:T(8,128)(2,1)S(1)}, bf16[528,128]{1,0:T(8,128)(2,1)S(1)}, u32[]{:S(2)}, u32[]{:S(2)}) collective-permute-start(bf16[528,128]{1,0:T(8,128)(2,1)S(1)} %get-tuple-element.33), channel_id=1, source_target_pairs={{0,4},{1,5},{2,6},{3,7},{4,0},{5,1},{6,2},{7,3},{8,12},{9,13},{10,... | collective-permute-start | bytes 405512 | tf_op jit(solution)/shard_map/ppermute | solution.py:459
  7.6 9.9 %collective-permute-start.4 = (bf16[528,128]{1,0:T(8,128)(2,1)S(1)}, bf16[528,128]{1,0:T(8,128)(2,1)S(1)}, u32[]{:S(2)}, u32[]{:S(2)}) collective-permute-start(bf16[528,128]{1,0:T(8,128)(2,1)S(1)} %get-tuple-element.34), channel_id=1, source_target_pairs={{0,6},{1,7},{2,4},{3,5},{4,2},{5,3},{6,0},{7,1},{8,14},{9,15},{10,... | collective-permute-start | bytes 405512 | tf_op jit(solution)/shard_map/ppermute | solution.py:459
  7.6 11.1 %collective-permute-start.5 = (bf16[272,128]{1,0:T(8,128)(2,1)S(1)}, bf16[272,128]{1,0:T(8,128)(2,1)S(1)}, u32[]{:S(2)}, u32[]{:S(2)}) collective-permute-start(bf16[272,128]{1,0:T(8,128)(2,1)S(1)} %get-tuple-element.36), channel_id=1, source_target_pairs={{0,8},{1,9},{2,10},{3,11},{4,12},{5,13},{6,14},{7,15},{8,0},{9,1},... | collective-permute-start | bytes 208904 | tf_op jit(solution)/shard_map/ppermute | solution.py:459
  10.6 13.8 %collective-permute-start.9 = (bf16[240,128]{1,0:T(8,128)(2,1)S(1)}, bf16[240,128]{1,0:T(8,128)(2,1)S(1)}, u32[]{:S(2)}, u32[]{:S(2)}) collective-permute-start(bf16[240,128]{1,0:T(8,128)(2,1)S(1)} %get-tuple-element.40), channel_id=1, source_target_pairs={{0,10},{1,11},{2,8},{3,9},{4,14},{5,15},{6,12},{7,13},{8,2},{9,3},... | collective-permute-start | bytes 184328 | tf_op jit(solution)/shard_map/ppermute | solution.py:459
  11.9 13.6 %collective-permute-start.10 = (bf16[240,128]{1,0:T(8,128)(2,1)S(1)}, bf16[240,128]{1,0:T(8,128)(2,1)S(1)}, u32[]{:S(2)}, u32[]{:S(2)}) collective-permute-start(bf16[240,128]{1,0:T(8,128)(2,1)S(1)} %get-tuple-element.41), channel_id=1, source_target_pairs={{0,12},{1,13},{2,14},{3,15},{4,8},{5,9},{6,10},{7,11},{8,4},{9,5},... | collective-permute-start | bytes 184328 | tf_op jit(solution)/shard_map/ppermute | solution.py:459
  15.5 10.0 %collective-permute-start.11 = (bf16[240,128]{1,0:T(8,128)(2,1)S(1)}, bf16[240,128]{1,0:T(8,128)(2,1)S(1)}, u32[]{:S(2)}, u32[]{:S(2)}) collective-permute-start(bf16[240,128]{1,0:T(8,128)(2,1)S(1)} %get-tuple-element.42), channel_id=1, source_target_pairs={{0,14},{1,15},{2,12},{3,13},{4,10},{5,11},{6,8},{7,9},{8,6},{9,7},... | collective-permute-start | bytes 184328 | tf_op jit(solution)/shard_map/ppermute | solution.py:459
  17.6 1.1 %copy-start.2 = (s32[16]{0:T(128)S(1)}, s32[16]{0:T(128)}, u32[]{:S(2)}) copy-start(s32[16]{0:T(128)} %counts_ref.7) | copy-start | bytes 196
  20.7 12.5 %collective-permute-start.7 = (bf16[384,128]{1,0:T(8,128)(2,1)S(1)}, bf16[384,128]{1,0:T(8,128)(2,1)S(1)}, u32[]{:S(2)}, u32[]{:S(2)}) collective-permute-start(bf16[384,128]{1,0:T(8,128)(2,1)S(1)} %get-tuple-element.38), channel_id=1, source_target_pairs={{0,9},{1,8},{2,11},{3,10},{4,13},{5,12},{6,15},{7,14},{8,1},{9,0},... | collective-permute-start | bytes 294920 | tf_op jit(solution)/shard_map/ppermute | solution.py:459
  20.7 13.3 %collective-permute-start.6 = (bf16[384,128]{1,0:T(8,128)(2,1)S(1)}, bf16[384,128]{1,0:T(8,128)(2,1)S(1)}, u32[]{:S(2)}, u32[]{:S(2)}) collective-permute-start(bf16[384,128]{1,0:T(8,128)(2,1)S(1)} %get-tuple-element.37.after_1), channel_id=1, source_target_pairs={{0,8},{1,9},{2,10},{3,11},{4,12},{5,13},{6,14},{7,15},{8,0},{9,1},... | collective-permute-start | bytes 294920 | tf_op jit(solution)/shard_map/ppermute | solution.py:459
  24.4 9.7 %collective-permute-start.8 = (bf16[384,128]{1,0:T(8,128)(2,1)S(1)}, bf16[384,128]{1,0:T(8,128)(2,1)S(1)}, u32[]{:S(2)}, u32[]{:S(2)}) collective-permute-start(bf16[384,128]{1,0:T(8,128)(2,1)S(1)} %get-tuple-element.39), channel_id=1, source_target_pairs={{0,1},{1,0},{2,3},{3,2},{4,5},{5,4},{6,7},{7,6},{8,9},{9,8},{10,11... | collective-permute-start | bytes 294920 | tf_op jit(solution)/shard_map/ppermute | solution.py:459
  28.7 9.3 %collective-permute-start.14 = (bf16[320,128]{1,0:T(8,128)(2,1)S(1)}, bf16[320,128]{1,0:T(8,128)(2,1)S(1)}, u32[]{:S(2)}, u32[]{:S(2)}) collective-permute-start(bf16[320,128]{1,0:T(8,128)(2,1)S(1)} %get-tuple-element.49), channel_id=1, source_target_pairs={{0,8},{1,9},{2,10},{3,11},{4,12},{5,13},{6,14},{7,15},{8,0},{9,1},... | collective-permute-start | bytes 245768 | tf_op jit(solution)/shard_map/ppermute | solution.py:459
  30.4 8.6 %collective-permute-start.15 = (bf16[320,128]{1,0:T(8,128)(2,1)S(1)}, bf16[320,128]{1,0:T(8,128)(2,1)S(1)}, u32[]{:S(2)}, u32[]{:S(2)}) collective-permute-start(bf16[320,128]{1,0:T(8,128)(2,1)S(1)} %get-tuple-element.50), channel_id=1, source_target_pairs={{0,9},{1,8},{2,11},{3,10},{4,13},{5,12},{6,15},{7,14},{8,1},{9,0},... | collective-permute-start | bytes 245768 | tf_op jit(solution)/shard_map/ppermute | solution.py:459
  31.0 3.1 %copy-start = (f32[256,256]{1,0:T(8,128)S(1)}, f32[256,256]{1,0:T(8,128)}, u32[]{:S(2)}) copy-start(f32[256,256]{1,0:T(8,128)} %constant.6.clone.inverse_ref) | copy-start | bytes 786436
  33.2 2.2 %collective-permute-start.12 = (bf16[160,128]{1,0:T(8,128)(2,1)S(1)}, bf16[160,128]{1,0:T(8,128)(2,1)S(1)}, u32[]{:S(2)}, u32[]{:S(2)}) collective-permute-start(bf16[160,128]{1,0:T(8,128)(2,1)S(1)} %get-tuple-element.45), channel_id=1, source_target_pairs={{0,1},{1,0},{2,3},{3,2},{4,5},{5,4},{6,7},{7,6},{8,9},{9,8},{10,11... | collective-permute-start | bytes 122888 | tf_op jit(solution)/shard_map/ppermute | solution.py:459
  34.0 1.4 %collective-permute-start.13 = (bf16[160,128]{1,0:T(8,128)(2,1)S(1)}, bf16[160,128]{1,0:T(8,128)(2,1)S(1)}, u32[]{:S(2)}, u32[]{:S(2)}) collective-permute-start(bf16[160,128]{1,0:T(8,128)(2,1)S(1)} %get-tuple-element.46), channel_id=1, source_target_pairs={{0,1},{1,0},{2,3},{3,2},{4,5},{5,4},{6,7},{7,6},{8,9},{9,8},{10,11... | collective-permute-start | bytes 122888 | tf_op jit(solution)/shard_map/ppermute | solution.py:459
